TPU v7x, 32 devices: a whole 2x2x4 slice. The times are simulated.
32 devices in a mesh: dp: 8 (over z, y), mp: 4 (over x, core).
Axes of the slice: x: 2, y: 2, z: 4, core: 2. Of those that a mesh axis runs over, the one named last changes fastest.
Arguments:
- tokens: bfloat16 [4, 8, 1024, 1024], P(None, 'dp', 'mp'), may hold values from -6 to 6
- cotangent: bfloat16 [4, 8, 1024, 1024], P(None, 'dp', 'mp'), may hold values from -6 to 6
- qkv_weight: float32 [3, 1024, 1024], P(None, 'dp', 'mp'), may hold values from -0.1875 to 0.1875
- qkv_first: float32 [3, 1024, 1024], P(None, 'dp', 'mp'), may hold values from -32 to 32
- qkv_second: float32 [3, 1024, 1024], P(None, 'dp', 'mp'), may hold values from 2.94912 to 11.79648
- out_weight: float32 [1024, 1024], P('mp', 'dp'), may hold values from -0.75 to 0.75
- out_first: float32 [1024, 1024], P('mp', 'dp'), may hold values from -32 to 32
- out_second: float32 [1024, 1024], P('mp', 'dp'), may hold values from 2.94912 to 11.79648
- up_weight: float32 [1024, 4, 1024], P('dp', None, 'mp'), may hold values from -0.1875 to 0.1875
- up_first: float32 [1024, 4, 1024], P('dp', None, 'mp'), may hold values from -32 to 32
- up_second: float32 [1024, 4, 1024], P('dp', None, 'mp'), may hold values from 2.94912 to 11.79648
- down_weight: float32 [4, 1024, 1024], P(None, 'mp', 'dp'), may hold values from -0.09375 to 0.09375
- down_first: float32 [4, 1024, 1024], P(None, 'mp', 'dp'), may hold values from -64 to 64
- down_second: float32 [4, 1024, 1024], P(None, 'mp', 'dp'), may hold values from 11.79648 to 47.18592
- head_biases: float32 [6, 1024], P(None, ('mp', 'dp')), may hold values from -3 to 3
- bias_first: float32 [6, 1024], P(None, ('mp', 'dp')), may hold values from -32 to 32
- bias_second: float32 [6, 1024], P(None, ('mp', 'dp')), may hold values from 2.94912 to 11.79648
- vectors: float32 [8, 1024], P(None, 'dp'), may hold values from 0.25 to 1.75
- vector_first: float32 [8, 1024], P(None, 'dp'), may hold values from -128 to 128
- vector_second: float32 [8, 1024], P(None, 'dp'), may hold values from 32.768 to 131.072
Outputs:
- layer_output: bfloat16 [4, 8, 1024, 1024], P(None, 'dp', 'mp')
- input_grad: float32 [4, 8, 1024, 1024], P(None, 'dp', 'mp')
- qkv_weight_new: float32 [3, 1024, 1024], P(None, 'dp', 'mp')
- qkv_first_new: float32 [3, 1024, 1024], P(None, 'dp', 'mp')
- qkv_second_new: float32 [3, 1024, 1024], P(None, 'dp', 'mp')
- out_weight_new: float32 [1024, 1024], P('mp', 'dp')
- out_first_new: float32 [1024, 1024], P('mp', 'dp')
- out_second_new: float32 [1024, 1024], P('mp', 'dp')
- up_weight_new: float32 [1024, 4, 1024], P('dp', None, 'mp')
- up_first_new: float32 [1024, 4, 1024], P('dp', None, 'mp')
- up_second_new: float32 [1024, 4, 1024], P('dp', None, 'mp')
- down_weight_new: float32 [4, 1024, 1024], P(None, 'mp', 'dp')
- down_first_new: float32 [4, 1024, 1024], P(None, 'mp', 'dp')
- down_second_new: float32 [4, 1024, 1024], P(None, 'mp', 'dp')
- head_biases_new: float32 [6, 1024], P(None, ('mp', 'dp'))
- bias_first_new: float32 [6, 1024], P(None, ('mp', 'dp'))
- bias_second_new: float32 [6, 1024], P(None, ('mp', 'dp'))
- vectors_new: float32 [8, 1024], P(None, 'dp')
- vector_first_new: float32 [8, 1024], P(None, 'dp')
- vector_second_new: float32 [8, 1024], P(None, 'dp')
All inputs are finite; a program needn't handle non-finite values.
Results may differ from a plain program's by a relative error of at most 0.012.
The roundings to bfloat16 on the way count: a program that leaves them out, or rounds other values in their place, can miss the bound.
Values may be sent and summed in bfloat16 or wider, within the bound.
No kernel may reach another device: no remote copies, remote signals or barrier semaphores. Data moves between devices by JAX's collectives and lax.ppermute only.
A program may use at most 256 MiB of HBM per device.

v0:
```python
import jax
import jax.numpy as jnp
from jax import lax
from jax.sharding import PartitionSpec as P

DH = 64
MICRO = 4
STEP = 10


RATES = (0.05, 0.2, 0.05, 0.03, 0.5, 0.5)


def layer_norm(values, gain, shift):
    center = values - jnp.mean(values, -1, keepdims=True)
    spread = jnp.mean(center * center, -1, keepdims=True)
    return center * lax.rsqrt(spread + 1e-06) * gain + shift


def exact_gelu(values):
    return jax.nn.gelu(values, approximate=False)


def adam_update(weight, first, second, grad, rate):
    first_new = 0.9 * first + 0.1 * grad
    second_new = 0.999 * second + 0.001 * grad * grad
    corrected = first_new / (1.0 - 0.9**STEP)
    scaled = jnp.sqrt(second_new / (1.0 - 0.999**STEP))
    weight_new = weight - rate * (corrected / (scaled + 1e-08) + 0.05 * weight)
    return (weight_new, first_new, second_new)


def attend_forward(queries, key_rows, values, block_rows):
    images, seq_rows, head_count, head_width = queries.shape
    block_count = seq_rows // block_rows
    factor = head_width ** (-0.5)
    query_blocks = jnp.moveaxis(
        queries.reshape(images, block_count, block_rows, head_count, head_width), 1, 0
    )

    def one_block(query_part):
        scores = (
            jnp.einsum("iqhe,ikhe->ihqk", query_part, key_rows, preferred_element_type=jnp.float32)
            * factor
        )
        row_peak = jnp.max(scores, -1, keepdims=True)
        shifted = jnp.exp(scores - row_peak)
        row_total = jnp.sum(shifted, -1, keepdims=True)
        softmax_rows = (shifted / row_total).astype(jnp.bfloat16)
        blended = jnp.einsum(
            "ihqk,ikhe->iqhe", softmax_rows, values, preferred_element_type=jnp.float32
        )
        return (blended, row_peak[..., 0] + jnp.log(row_total[..., 0]))

    blended, log_total = lax.map(one_block, query_blocks)
    blended = jnp.moveaxis(blended, 0, 1).reshape(images, seq_rows, head_count * head_width)
    return (blended.astype(jnp.bfloat16), log_total)


def attend_backward(queries, key_rows, values, grad_blended, log_total, block_rows):
    images, seq_rows, head_count, head_width = queries.shape
    block_count = seq_rows // block_rows
    factor = head_width ** (-0.5)
    split_shape = (images, block_count, block_rows, head_count, head_width)
    query_blocks = jnp.moveaxis(queries.reshape(split_shape), 1, 0)
    grad_blocks = jnp.moveaxis(grad_blended.reshape(split_shape), 1, 0)

    def one_block(carry, inputs_part):
        query_part, grad_part, total_part = inputs_part
        grad_keys, grad_values = carry
        scores = (
            jnp.einsum("iqhe,ikhe->ihqk", query_part, key_rows, preferred_element_type=jnp.float32)
            * factor
        )
        softmax_rows = jnp.exp(scores - total_part[..., None])
        grad_values = grad_values + jnp.einsum(
            "ihqk,iqhe->ikhe",
            softmax_rows.astype(jnp.bfloat16),
            grad_part,
            preferred_element_type=jnp.float32,
        )
        grad_rows = jnp.einsum(
            "iqhe,ikhe->ihqk", grad_part, values, preferred_element_type=jnp.float32
        )
        grad_scores = softmax_rows * (
            grad_rows - jnp.sum(grad_rows * softmax_rows, -1, keepdims=True)
        )
        grad_scores = grad_scores.astype(jnp.bfloat16)
        grad_query = (
            jnp.einsum("ihqk,ikhe->iqhe", grad_scores, key_rows, preferred_element_type=jnp.float32)
            * factor
        )
        grad_keys = (
            grad_keys
            + jnp.einsum(
                "ihqk,iqhe->ikhe", grad_scores, query_part, preferred_element_type=jnp.float32
            )
            * factor
        )
        return ((grad_keys, grad_values), grad_query)

    zero_grad = jnp.zeros(queries.shape, jnp.float32)
    (grad_keys, grad_values), grad_query = lax.scan(
        one_block, (zero_grad, zero_grad), (query_blocks, grad_blocks, log_total)
    )
    flat_shape = (images, seq_rows, head_count * head_width)
    grad_query = jnp.moveaxis(grad_query, 0, 1).reshape(flat_shape)
    stacked = jnp.stack(
        [grad_query, grad_keys.reshape(flat_shape), grad_values.reshape(flat_shape)]
    )
    return stacked.astype(jnp.bfloat16)


def rows_forward(part):
    return lax.all_gather(part, "mp", axis=1, tiled=True)


def rows_sum_forward(part):
    return lax.psum_scatter(part, "mp", scatter_dimension=1, tiled=True)


def rows_backward(part):
    return lax.all_gather(part, "mp", axis=1, tiled=True)


def rows_sum_backward(part):
    return lax.psum_scatter(part, "mp", scatter_dimension=1, tiled=True)


def forward(inputs, params):
    qkv_full, out_full, up_full, down_full, bias_full, vector_full = params
    base = inputs.astype(jnp.float32)
    normed = layer_norm(base, vector_full[0], vector_full[1]).astype(jnp.bfloat16)
    normed_all = rows_forward(normed)
    images, seq_rows = (normed_all.shape[0], normed_all.shape[1])
    head_shape = (images, seq_rows, -1, DH)
    project = jnp.einsum("isd,tde->tise", normed_all, qkv_full, preferred_element_type=jnp.float32)
    queries = (project[0] + bias_full[0]).astype(jnp.bfloat16).reshape(head_shape)
    key_rows = project[1].astype(jnp.bfloat16).reshape(head_shape)
    values = (project[2] + bias_full[1]).astype(jnp.bfloat16).reshape(head_shape)
    blended, log_total = attend_forward(queries, key_rows, values, min(512, seq_rows))
    projected = rows_sum_forward(
        jnp.einsum("ise,ed->isd", blended, out_full, preferred_element_type=jnp.float32)
    )
    branch_one = projected + vector_full[2]
    hidden = base + vector_full[3] * branch_one
    normed_two = layer_norm(hidden, vector_full[4], vector_full[5]).astype(jnp.bfloat16)
    normed_two_all = rows_forward(normed_two)
    pre_act = jnp.einsum(
        "isd,df->isf", normed_two_all, up_full, preferred_element_type=jnp.float32
    ) + bias_full[2:].reshape(-1)
    activ = exact_gelu(pre_act).astype(jnp.bfloat16)
    branch_two = (
        rows_sum_forward(
            jnp.einsum("isf,fd->isd", activ, down_full, preferred_element_type=jnp.float32)
        )
        + vector_full[6]
    )
    output = hidden + vector_full[7] * branch_two
    saved = (
        base,
        hidden,
        branch_one,
        branch_two,
        normed_all,
        queries,
        key_rows,
        values,
        log_total,
        blended,
        normed_two_all,
        pre_act,
        activ,
    )
    return (output.astype(jnp.bfloat16), saved)


def backward(grad_output, saved, params):
    qkv_full, out_full, up_full, down_full, bias_full, vector_full = params
    (
        base,
        hidden,
        branch_one,
        branch_two,
        normed_all,
        queries,
        key_rows,
        values,
        log_total,
        blended,
        normed_two_all,
        pre_act,
        activ,
    ) = saved
    local_width = qkv_full.shape[2]
    grad_out = grad_output.astype(jnp.float32)
    grad_scale_two = jnp.sum(grad_out * branch_two, axis=(0, 1))
    grad_bias_two = jnp.sum(grad_out, axis=(0, 1)) * vector_full[7]
    grad_branch = rows_backward((grad_out * vector_full[7]).astype(jnp.bfloat16))
    grad_down = jnp.einsum("isf,isd->fd", activ, grad_branch, preferred_element_type=jnp.float32)
    grad_activ = jnp.einsum(
        "isd,fd->isf", grad_branch, down_full, preferred_element_type=jnp.float32
    )
    grad_pre = jax.vjp(exact_gelu, pre_act)[1](grad_activ)[0].astype(jnp.bfloat16)
    grad_up_bias = jnp.sum(grad_pre, axis=(0, 1), dtype=jnp.float32)
    grad_up = jnp.einsum(
        "isd,isf->df", normed_two_all, grad_pre, preferred_element_type=jnp.float32
    )
    grad_normed_two = rows_sum_backward(
        jnp.einsum("isf,df->isd", grad_pre, up_full, preferred_element_type=jnp.float32)
    )
    norm_back_two = jax.vjp(layer_norm, hidden, vector_full[4], vector_full[5])[1]
    grad_hidden, grad_gain_two, grad_shift_two = norm_back_two(grad_normed_two)
    grad_hidden = grad_out + grad_hidden
    grad_scale_one = jnp.sum(grad_hidden * branch_one, axis=(0, 1))
    grad_out_bias = jnp.sum(grad_hidden, axis=(0, 1)) * vector_full[3]
    grad_projected = rows_backward((grad_hidden * vector_full[3]).astype(jnp.bfloat16))
    grad_out_weight = jnp.einsum(
        "ise,isd->ed", blended, grad_projected, preferred_element_type=jnp.float32
    )
    grad_blended = jnp.einsum(
        "isd,ed->ise", grad_projected, out_full, preferred_element_type=jnp.float32
    ).astype(jnp.bfloat16)
    grad_project = attend_backward(
        queries, key_rows, values, grad_blended, log_total, min(512, queries.shape[1])
    )
    grad_query_bias = jnp.sum(grad_project[0], axis=(0, 1), dtype=jnp.float32)
    grad_value_bias = jnp.sum(grad_project[2], axis=(0, 1), dtype=jnp.float32)
    grad_qkv = jnp.einsum(
        "isd,tise->tde", normed_all, grad_project, preferred_element_type=jnp.float32
    )
    grad_normed = rows_sum_backward(
        jnp.einsum("tise,tde->isd", grad_project, qkv_full, preferred_element_type=jnp.float32)
    )
    norm_back_one = jax.vjp(layer_norm, base, vector_full[0], vector_full[1])[1]
    grad_input_part, grad_gain_one, grad_shift_one = norm_back_one(grad_normed)
    grad_input = grad_hidden + grad_input_part
    grad_vectors = jnp.stack(
        [
            grad_gain_one,
            grad_shift_one,
            grad_out_bias,
            grad_scale_one,
            grad_gain_two,
            grad_shift_two,
            grad_bias_two,
            grad_scale_two,
        ]
    )
    grad_biases = jnp.concatenate(
        [jnp.stack([grad_query_bias, grad_value_bias]), grad_up_bias.reshape(-1, local_width)], 0
    )
    return (grad_input, (grad_qkv, grad_out_weight, grad_up, grad_down, grad_biases, grad_vectors))


def local(
    tokens,
    cotangent,
    qkv_weight,
    qkv_first,
    qkv_second,
    out_weight,
    out_first,
    out_second,
    up_weight,
    up_first,
    up_second,
    down_weight,
    down_first,
    down_second,
    head_biases,
    bias_first,
    bias_second,
    vectors,
    vector_first,
    vector_second,
):

    def gather_params():
        gathered = (
            lax.all_gather(qkv_weight.astype(jnp.bfloat16), "dp", axis=1, tiled=True),
            lax.all_gather(out_weight.astype(jnp.bfloat16), "dp", axis=1, tiled=True),
            lax.all_gather(up_weight.astype(jnp.bfloat16), "dp", axis=0, tiled=True),
            lax.all_gather(down_weight.astype(jnp.bfloat16), "dp", axis=2, tiled=True),
            lax.all_gather(head_biases.astype(jnp.bfloat16), "dp", axis=1, tiled=True),
            lax.all_gather(vectors.astype(jnp.bfloat16), "dp", axis=1, tiled=True),
        )
        qkv_full, out_full, up_full, down_full, bias_full, vector_full = gathered
        return (
            qkv_full,
            out_full,
            up_full.reshape(up_full.shape[0], -1),
            down_full.reshape(-1, down_full.shape[2]),
            bias_full.astype(jnp.float32),
            vector_full.astype(jnp.float32),
        )

    grad_sums = None
    outputs = []
    input_grads = []
    for micro_step in range(MICRO):
        params_fwd = gather_params()
        output, saved = forward(tokens[micro_step], params_fwd)
        outputs.append(output)
        params_back = gather_params()
        grad_input, grads = backward(cotangent[micro_step], saved, params_back)
        input_grads.append(grad_input)
        if grad_sums is None:
            grad_sums = grads
        else:
            grad_sums = tuple((old_sum + new_part for old_sum, new_part in zip(grad_sums, grads)))
    grad_qkv, grad_out_weight, grad_up, grad_down, grad_biases, grad_vectors = grad_sums
    grad_up = grad_up.reshape(-1, up_weight.shape[1], up_weight.shape[2])
    grad_down = grad_down.reshape(down_weight.shape[0], down_weight.shape[1], -1)
    reduced = (
        lax.psum_scatter(grad_qkv, "dp", scatter_dimension=1, tiled=True),
        lax.psum_scatter(grad_out_weight, "dp", scatter_dimension=1, tiled=True),
        lax.psum_scatter(grad_up, "dp", scatter_dimension=0, tiled=True),
        lax.psum_scatter(grad_down, "dp", scatter_dimension=2, tiled=True),
        lax.psum_scatter(grad_biases, "dp", scatter_dimension=1, tiled=True),
        lax.psum_scatter(grad_vectors, "dp", scatter_dimension=1, tiled=True),
    )
    vector_grad = lax.psum(reduced[5], "mp")
    grads = (reduced[0], reduced[1], reduced[2], reduced[3], reduced[4], vector_grad)
    params = (qkv_weight, out_weight, up_weight, down_weight, head_biases, vectors)
    firsts = (qkv_first, out_first, up_first, down_first, bias_first, vector_first)
    seconds = (qkv_second, out_second, up_second, down_second, bias_second, vector_second)
    updated = [
        adam_update(params[slot], firsts[slot], seconds[slot], grads[slot], RATES[slot])
        for slot in range(6)
    ]
    return (
        jnp.stack(outputs),
        jnp.stack(input_grads),
        updated[0][0],
        updated[0][1],
        updated[0][2],
        updated[1][0],
        updated[1][1],
        updated[1][2],
        updated[2][0],
        updated[2][1],
        updated[2][2],
        updated[3][0],
        updated[3][1],
        updated[3][2],
        updated[4][0],
        updated[4][1],
        updated[4][2],
        updated[5][0],
        updated[5][1],
        updated[5][2],
    )


def solution(mesh):
    return jax.shard_map(
        local,
        mesh=mesh,
        in_specs=(
            P(None, "dp", "mp", None),
            P(None, "dp", "mp", None),
            P(None, "dp", "mp"),
            P(None, "dp", "mp"),
            P(None, "dp", "mp"),
            P("mp", "dp"),
            P("mp", "dp"),
            P("mp", "dp"),
            P("dp", None, "mp"),
            P("dp", None, "mp"),
            P("dp", None, "mp"),
            P(None, "mp", "dp"),
            P(None, "mp", "dp"),
            P(None, "mp", "dp"),
            P(None, ("mp", "dp")),
            P(None, ("mp", "dp")),
            P(None, ("mp", "dp")),
            P(None, "dp"),
            P(None, "dp"),
            P(None, "dp"),
        ),
        out_specs=(
            P(None, "dp", "mp", None),
            P(None, "dp", "mp", None),
            P(None, "dp", "mp"),
            P(None, "dp", "mp"),
            P(None, "dp", "mp"),
            P("mp", "dp"),
            P("mp", "dp"),
            P("mp", "dp"),
            P("dp", None, "mp"),
            P("dp", None, "mp"),
            P("dp", None, "mp"),
            P(None, "mp", "dp"),
            P(None, "mp", "dp"),
            P(None, "mp", "dp"),
            P(None, ("mp", "dp")),
            P(None, ("mp", "dp")),
            P(None, ("mp", "dp")),
            P(None, "dp"),
            P(None, "dp"),
            P(None, "dp"),
        ),
        check_vma=False,
    )
```

profile of v0, /device:TPU:0, one launch (start us, length us, event | category | flops | bytes accessed | tf_op | source)
XLA Modules:
  0.0 1930.0 jit_solution(6951657035486860750)
XLA Ops:
  10.1 27.8 %all_gather.44 = bf16[8,1024]{1,0:T(8,128)(2,1)S(1)} all-gather(bf16[8,128]{1,0:T(8,128)(2,1)S(1)} %convert_element_type.850), channel_id=1, replica_groups=mesh['dp'=8,'mp'=4] {'dp'}, dimensions={1}, use_global_device_ids=true | all-gather | bytes 18432 | tf_op jit(solution)/shard_map/all_gather | solution.py:286
  45.4 26.1 %all-gather = bf16[8,32,6]{1,2,0:T(8,128)(2,1)S(1)} all-gather(bf16[1,32,6]{1,2,0:T(8,128)(2,1)S(1)} %convert_bitcast_fusion.8), channel_id=1, replica_groups=mesh['dp'=8,'mp'=4] {'dp'}, dimensions={0}, use_global_device_ids=true | all-gather | bytes 3456 | tf_op jit(solution)/shard_map/all_gather | solution.py:285
  71.8 27.7 %all_gather.48 = bf16[256,1024]{1,0:T(8,128)(2,1)S(1)} all-gather(bf16[256,128]{1,0:T(8,128)(2,1)S(1)} %convert_element_type.861), channel_id=1, replica_groups=mesh['dp'=8,'mp'=4] {'dp'}, dimensions={1}, use_global_device_ids=true | all-gather | bytes 589824 | tf_op jit(solution)/shard_map/all_gather | solution.py:282
  113.2 18.0 all-gather.35.cloned.1.call-done
  149.9 12.5 while.109
  169.5 10.8 while.110
  186.7 11.2 while.111
  204.1 8.6 reduce-scatter.28.cloned.1.call-done
  212.7 47.1 %reduce-scatter.32.cloned.1.call-done = f32[1,256,1024]{2,1,0:T(8,128)} async-done(((f32[1,1024,1024]{2,1,0:T(8,128)}), f32[1,256,1024]{2,1,0:T(8,128)}) %reduce-scatter.32.cloned.1.call-update) | async-done | bytes 1048592 | tf_op jit(solution)/shard_map/reduce_scatter | solution.py:119
  259.8 47.1 %reduce-scatter.36.cloned.1.call-done = f32[1,256,1024]{2,1,0:T(8,128)} async-done(((f32[1,1024,1024]{2,1,0:T(8,128)}), f32[1,256,1024]{2,1,0:T(8,128)}) %reduce-scatter.36.cloned.1.call-update) | async-done | bytes 1048592 | tf_op jit(solution)/shard_map/reduce_scatter | solution.py:119
  317.5 41.6 %all-gather.27.cloned.1.call-done = bf16[1024,4,256]{2,1,0:T(4,128)(2,1)} async-done(((bf16[128,4,256]{2,1,0:T(4,128)(2,1)}), bf16[1024,4,256]{2,1,0:T(4,128)(2,1)}) %all-gather.27.cloned.1.call-update) | async-done | bytes 2097168 | tf_op jit(solution)/shard_map/all_gather | solution.py:283
  361.2 21.2 %all-gather.41.cloned.1.call-done = bf16[1,1024,1024]{2,1,0:T(8,128)(2,1)} async-done(((bf16[1,256,1024]{2,1,0:T(8,128)(2,1)}), bf16[1,1024,1024]{2,1,0:T(8,128)(2,1)}) %all-gather.41.cloned.1.call-update) | async-done | bytes 2097168 | tf_op jit(solution)/shard_map/all_gather | solution.py:115
  382.4 5.9 fusion.242
  388.4 18.7 all-gather.37.cloned.1.call-done
  407.1 6.0 fusion.250
  413.1 18.8 all-gather.33.cloned.1.call-done
  431.9 33.0 %multiply_convert_fusion.6 = (bf16[1024,1024]{1,0:T(8,128)(2,1)}, f32[1024,1024]{1,0:T(8,128)}, bf16[1024,1024]{1,0:T(8,128)(2,1)}, f32[1024,1024]{1,0:T(8,128)}...) fusion(f32[1024]{0:T(1024)S(1)} %bitcast.1148, f32[1024,1024]{1,0:T(8,128)} %fusion.242, ...), kind=kOutput, calls=%fused_computation.241 | convolution fusion | flops 2355101696 | bytes 35655680 | tf_op jit(solution)/shard_map/isd,df->isf/dot_general | solution.py:149
  465.0 45.0 %all-gather.29.cloned.1.call-done = bf16[4,256,1024]{2,1,0:T(8,128)(2,1)} async-done(((bf16[4,256,128]{2,1,0:T(8,128)(2,1)}), bf16[4,256,1024]{2,1,0:T(8,128)(2,1)}) %all-gather.29.cloned.1.call-update) | async-done | bytes 2097168 | tf_op jit(solution)/shard_map/all_gather | solution.py:284
  510.0 8.9 convert_reduce_fusion.2
  525.0 7.3 all-gather.51.cloned.1.call-done
  532.3 8.9 convert_reduce_fusion.1
  547.2 9.2 all-gather.55.cloned.1.call-done
  556.4 9.1 convert_reduce_fusion
  572.8 6.0 convolution_bitcast_fusion.12
  578.8 24.6 %reduce-scatter.44.cloned.1.call-done = f32[1,256,1024]{2,1,0:T(8,128)} async-done(((f32[1,1024,1024]{2,1,0:T(8,128)}), f32[1,256,1024]{2,1,0:T(8,128)}) %reduce-scatter.44.cloned.1.call-update) | async-done | bytes 1048592 | tf_op jit(solution)/shard_map/reduce_scatter | solution.py:127
  603.5 46.9 %reduce-scatter.48.cloned.1.call-done = f32[1,256,1024]{2,1,0:T(8,128)} async-done(((f32[1,1024,1024]{2,1,0:T(8,128)}), f32[1,256,1024]{2,1,0:T(8,128)}) %reduce-scatter.48.cloned.1.call-update) | async-done | bytes 1048592 | tf_op jit(solution)/shard_map/reduce_scatter | solution.py:127
  653.3 44.1 %reduce-scatter.52.cloned.1.call-done = f32[1,256,1024]{2,1,0:T(8,128)} async-done(((f32[1,1024,1024]{2,1,0:T(8,128)}), f32[1,256,1024]{2,1,0:T(8,128)}) %reduce-scatter.52.cloned.1.call-update) | async-done | bytes 1048592 | tf_op jit(solution)/shard_map/reduce_scatter | solution.py:127
  697.4 47.6 %reduce-scatter.30.cloned.1.call-done = f32[1,256,1024]{2,1,0:T(8,128)} async-done(((f32[1,1024,1024]{2,1,0:T(8,128)}), f32[1,256,1024]{2,1,0:T(8,128)}) %reduce-scatter.30.cloned.1.call-update) | async-done | bytes 1048592 | tf_op jit(solution)/shard_map/reduce_scatter | solution.py:119
  754.7 21.2 %all-gather.53.cloned.1.call-done = bf16[1,1024,1024]{2,1,0:T(8,128)(2,1)} async-done(((bf16[1,256,1024]{2,1,0:T(8,128)(2,1)}), bf16[1,1024,1024]{2,1,0:T(8,128)(2,1)}) %all-gather.53.cloned.1.call-update) | async-done | bytes 2097168 | tf_op jit(solution)/shard_map/all_gather | solution.py:123
  784.9 21.3 %while.114 = (s32[]{:T(128)}, f32[1,1024,4,64]{1,3,2,0:T(8,128)S(1)}, f32[1,1024,4,64]{1,3,2,0:T(8,128)S(1)}, bf16[2,1,512,4,64]{2,4,3,1,0:T(8,128)(2,1)}, bf16[...) while((s32[]{:T(128)}, ...), condition=%wide.region_63.64_spmd.clone, body=%wide.region_61.63_spmd.clone.sunk | while | flops 1368782848 | bytes 78700808 | solution.py:103
  810.0 5.7 convolution_bitcast_fusion.1
  825.2 21.3 %while.115 = (s32[]{:T(128)}, f32[1,1024,4,64]{1,3,2,0:T(8,128)S(1)}, f32[1,1024,4,64]{1,3,2,0:T(8,128)S(1)}, bf16[2,1,512,4,64]{2,4,3,1,0:T(8,128)(2,1)}, bf16[...) while((s32[]{:T(128)}, ...), condition=%wide.region_72.73_spmd.clone, body=%wide.region_70.72_spmd.clone.sunk | while | flops 1368782848 | bytes 78700808 | solution.py:103
  850.2 5.4 convolution_bitcast_fusion
  865.2 21.3 %while.113 = (s32[]{:T(128)}, f32[1,1024,4,64]{1,3,2,0:T(8,128)S(1)}, f32[1,1024,4,64]{1,3,2,0:T(8,128)S(1)}, bf16[2,1,512,4,64]{2,4,3,1,0:T(8,128)(2,1)}, bf16[...) while((s32[]{:T(128)}, ...), condition=%wide.region_54.55_spmd.clone, body=%wide.region_52.54_spmd.clone.sunk | while | flops 1368782848 | bytes 78700808 | solution.py:103
  896.9 22.7 %reduce-scatter.54.cloned.1.call-done = f32[1,256,1024]{2,1,0:T(8,128)} async-done(((f32[1,1024,1024]{2,1,0:T(8,128)}), f32[1,256,1024]{2,1,0:T(8,128)}) %reduce-scatter.54.cloned.1.call-update) | async-done | bytes 1048592 | tf_op jit(solution)/shard_map/reduce_scatter | solution.py:127
  919.7 47.8 %reduce-scatter.46.cloned.1.call-done = f32[1,256,1024]{2,1,0:T(8,128)} async-done(((f32[1,1024,1024]{2,1,0:T(8,128)}), f32[1,256,1024]{2,1,0:T(8,128)}) %reduce-scatter.46.cloned.1.call-update) | async-done | bytes 1048592 | tf_op jit(solution)/shard_map/reduce_scatter | solution.py:127
  972.4 22.3 %all-gather.21.cloned.1.call-done = bf16[1,1024,1024]{2,1,0:T(8,128)(2,1)} async-done(((bf16[1,256,1024]{2,1,0:T(8,128)(2,1)}), bf16[1,1024,1024]{2,1,0:T(8,128)(2,1)}) %all-gather.21.cloned.1.call-update) | async-done | bytes 2097168 | tf_op jit(solution)/shard_map/all_gather | solution.py:115
  1006.1 12.4 while.108
  1024.9 44.6 %reduce-scatter.24.cloned.1.call-done = f32[1,256,1024]{2,1,0:T(8,128)} async-done(((f32[1,1024,1024]{2,1,0:T(8,128)}), f32[1,256,1024]{2,1,0:T(8,128)}) %reduce-scatter.24.cloned.1.call-update) | async-done | bytes 1048592 | tf_op jit(solution)/shard_map/reduce_scatter | solution.py:119
  1074.0 21.8 %all-gather.25.cloned.1.call-done = bf16[1,1024,1024]{2,1,0:T(8,128)(2,1)} async-done(((bf16[1,256,1024]{2,1,0:T(8,128)(2,1)}), bf16[1,1024,1024]{2,1,0:T(8,128)(2,1)}) %all-gather.25.cloned.1.call-update) | async-done | bytes 2097168 | tf_op jit(solution)/shard_map/all_gather | solution.py:115
  1095.7 14.7 multiply_convert_fusion.7
  1110.4 9.6 all-gather.43.cloned.1.call-done
  1120.0 8.5 convert_reduce_fusion.3
  1134.4 6.0 convolution_bitcast_fusion.14
  1142.1 6.5 convolution_bitcast_fusion.8
  1148.6 6.0 convolution_bitcast_fusion.10
  1154.7 24.4 %reduce-scatter.40.cloned.1.call-done = f32[1,256,1024]{2,1,0:T(8,128)} async-done(((f32[1,1024,1024]{2,1,0:T(8,128)}), f32[1,256,1024]{2,1,0:T(8,128)}) %reduce-scatter.40.cloned.1.call-update) | async-done | bytes 1048592 | tf_op jit(solution)/shard_map/reduce_scatter | solution.py:127
  1181.6 44.6 %reduce-scatter.26.cloned.1.call-done = f32[1,256,1024]{2,1,0:T(8,128)} async-done(((f32[1,1024,1024]{2,1,0:T(8,128)}), f32[1,256,1024]{2,1,0:T(8,128)}) %reduce-scatter.26.cloned.1.call-update) | async-done | bytes 1048592 | tf_op jit(solution)/shard_map/reduce_scatter | solution.py:119
  1229.6 44.4 %reduce-scatter.38.cloned.1.call-done = f32[1,256,1024]{2,1,0:T(8,128)} async-done(((f32[1,1024,1024]{2,1,0:T(8,128)}), f32[1,256,1024]{2,1,0:T(8,128)}) %reduce-scatter.38.cloned.1.call-update) | async-done | bytes 1048592 | tf_op jit(solution)/shard_map/reduce_scatter | solution.py:119
  1273.9 46.9 %reduce-scatter.34.cloned.1.call-done = f32[1,256,1024]{2,1,0:T(8,128)} async-done(((f32[1,1024,1024]{2,1,0:T(8,128)}), f32[1,256,1024]{2,1,0:T(8,128)}) %reduce-scatter.34.cloned.1.call-update) | async-done | bytes 1048592 | tf_op jit(solution)/shard_map/reduce_scatter | solution.py:119
  1320.8 6.3 fusion.378
  1348.3 6.8 fusion.204
  1367.2 10.6 add_add_fusion
  1396.0 21.3 %while.112 = (s32[]{:T(128)}, f32[1,1024,4,64]{1,3,2,0:T(8,128)S(1)}, f32[1,1024,4,64]{1,3,2,0:T(8,128)S(1)}, bf16[2,1,512,4,64]{2,4,3,1,0:T(8,128)(2,1)}, bf16[...) while((s32[]{:T(128)}, ...), condition=%wide.region_45.46_spmd.clone, body=%wide.region_43.45_spmd.clone.sunk | while | flops 1368782848 | bytes 78700808 | solution.py:103
  1425.2 5.6 fusion.260
  1440.9 8.1 add_bitcast_fusion
  1461.5 48.8 %all-reduce.3.cloned.1.call-done = f32[1024,4,256]{2,1,0:T(4,128)} async-done(((f32[1024,4,256]{2,1,0:T(4,128)}), f32[1024,4,256]{2,1,0:T(4,128)}) %all-reduce.3.cloned.1.call-update) | async-done | bytes 4194320
  1518.3 83.4 %reduce-scatter.60.cloned.1.call-done = f32[4,256,128]{2,1,0:T(8,128)} async-done(((f32[4,256,1024]{2,1,0:T(8,128)}), f32[4,256,128]{2,1,0:T(8,128)}) %reduce-scatter.60.cloned.1.call-update) | async-done | bytes 524304 | tf_op jit(solution)/shard_map/reduce_scatter | solution.py:319
  1604.5 61.6 %reduce-scatter.64.cloned.1.call-done = f32[32,6]{1,0:T(8,128)} async-done(((f32[256,6]{1,0:T(8,128)}), f32[32,6]{1,0:T(8,128)}) %reduce-scatter.64.cloned.1.call-update) | async-done | bytes 784
  1668.3 64.3 %reduce-scatter.58.cloned.1.call-done = f32[256,128]{1,0:T(8,128)} async-done(((f32[256,1024]{1,0:T(8,128)}), f32[256,128]{1,0:T(8,128)}) %reduce-scatter.58.cloned.1.call-update) | async-done | bytes 131088 | tf_op jit(solution)/shard_map/reduce_scatter | solution.py:317
  1734.4 76.1 %reduce-scatter.56.cloned.1.call-done = f32[3,128,256]{1,2,0:T(8,128)} async-done(((f32[3,1024,256]{1,2,0:T(8,128)}), f32[3,128,256]{1,2,0:T(8,128)}) %reduce-scatter.56.cloned.1.call-update) | async-done | bytes 393232 | tf_op jit(solution)/shard_map/reduce_scatter | solution.py:316
  1818.9 38.6 %reduce-scatter.42.cloned.1.call-done = f32[1,256,1024]{2,1,0:T(8,128)} async-done(((f32[1,1024,1024]{2,1,0:T(8,128)}), f32[1,256,1024]{2,1,0:T(8,128)}) %reduce-scatter.42.cloned.1.call-update) | async-done | bytes 1048592 | tf_op jit(solution)/shard_map/reduce_scatter | solution.py:127
  1870.3 46.2 %reduce-scatter.62.cloned.1.call-done = f32[8,128]{1,0:T(8,128)} async-done(((f32[8,1024]{1,0:T(8,128)}), f32[8,128]{1,0:T(8,128)}) %reduce-scatter.62.cloned.1.call-update) | async-done | bytes 4112 | tf_op jit(solution)/shard_map/reduce_scatter | solution.py:321
  1916.5 5.8 psum.7
  (925 shorter events, 439.1 us)
Async XLA Ops:
  7.2 92.4 %all-gather.23.cloned.1.call-start = ((), (), s32[]{:S(2)}) async-start(), calls=%async_computation.22 | async-start | bytes 1769472 | tf_op jit(solution)/shard_map/all_gather | solution.py:281
  9.4 90.2 %all-gather.39.cloned.1.call-start = ((), (), s32[]{:S(2)}) async-start(), calls=%async_computation.36 | async-start | bytes 2621440 | tf_op jit(solution)/shard_map/all_gather | solution.py:115
  44.1 64.5 %all-gather.31.cloned.1.call-start = ((), (), s32[]{:S(2)}) async-start(), calls=%async_computation.28 | async-start | bytes 2621440 | tf_op jit(solution)/shard_map/all_gather | solution.py:115
  44.8 86.4 %all-gather.35.cloned.1.call-start = ((), (), s32[]{:S(2)}) async-start(), calls=%async_computation.32 | async-start | bytes 2621440 | tf_op jit(solution)/shard_map/all_gather | solution.py:115
  45.4 167.3 %reduce-scatter.28.cloned.1.call-start = ((), (), s32[]{:S(2)}) async-start(), calls=%async_computation.29 | async-start | bytes 5242880 | tf_op jit(solution)/shard_map/reduce_scatter | solution.py:119
  71.8 74.6 %copy-start.151 = (f32[4,64]{1,0:T(4,128)}, f32[4,64]{1,0:T(4,128)S(1)}, u32[]{:S(2)}) copy-start(f32[4,64]{1,0:T(4,128)S(1)} %add.755) | copy-start | bytes 3076
  99.6 98.9 %copy-start.40 = (bf16[256,1024]{1,0:T(8,128)(2,1)}, bf16[256,1024]{1,0:T(8,128)(2,1)S(1)}, u32[]{:S(2)}) copy-start(bf16[256,1024]{1,0:T(8,128)(2,1)S(1)} %all_gather.48) | copy-start | bytes 1572868
  168.1 91.7 %reduce-scatter.32.cloned.1.call-start = ((), (), s32[]{:S(2)}) async-start(), calls=%async_computation.33 | async-start | bytes 5242880 | tf_op jit(solution)/shard_map/reduce_scatter | solution.py:119
  185.2 121.7 %reduce-scatter.36.cloned.1.call-start = ((), (), s32[]{:S(2)}) async-start(), calls=%async_computation.37 | async-start | bytes 5242880 | tf_op jit(solution)/shard_map/reduce_scatter | solution.py:119
  199.4 107.5 %copy-start.7 = (bf16[4,1,256,1024]{3,2,1,0:T(8,128)(2,1)S(1)}, bf16[4,1,256,1024]{3,2,1,0:T(8,128)(2,1)}, u32[]{:S(2)}) copy-start(bf16[4,1,256,1024]{3,2,1,0:T(8,128)(2,1)} %param.36) | copy-start | bytes 6291460
  199.4 107.5 %copy-start.126 = (f32[1,1024]{1,0:T(1,128)S(1)}, f32[1,1024]{1,0:T(1,128)}, u32[]{:S(2)}) copy-start(f32[1,1024]{1,0:T(1,128)} %get-tuple-element.1005) | copy-start | bytes 12292
  199.4 107.5 %copy-start.129 = (f32[1,1024]{1,0:T(1,128)S(1)}, f32[1,1024]{1,0:T(1,128)}, u32[]{:S(2)}) copy-start(f32[1,1024]{1,0:T(1,128)} %get-tuple-element.1006) | copy-start | bytes 12292
  202.2 156.9 %all-gather.27.cloned.1.call-start = ((), (), s32[]{:S(2)}) async-start(), calls=%async_computation.25 | async-start | bytes 2359296 | tf_op jit(solution)/shard_map/all_gather | solution.py:283
  204.0 178.4 %all-gather.41.cloned.1.call-start = ((), (), s32[]{:S(2)}) async-start(), calls=%async_computation.38 | async-start | bytes 2621440 | tf_op jit(solution)/shard_map/all_gather | solution.py:115
  312.3 94.8 %all-gather.37.cloned.1.call-start = ((), (), s32[]{:S(2)}) async-start(), calls=%async_computation.34 | async-start | bytes 2621440 | tf_op jit(solution)/shard_map/all_gather | solution.py:115
  312.9 119.1 %all-gather.33.cloned.1.call-start = ((), (), s32[]{:S(2)}) async-start(), calls=%async_computation.30 | async-start | bytes 2621440 | tf_op jit(solution)/shard_map/all_gather | solution.py:115
  313.6 151.4 %all-gather.47.cloned.1.call-start = ((), (), s32[]{:S(2)}) async-start(), calls=%async_computation.44 | async-start | bytes 2621440 | tf_op jit(solution)/shard_map/all_gather | solution.py:123
  315.4 194.6 %all-gather.29.cloned.1.call-start = ((), (), s32[]{:S(2)}) async-start(), calls=%async_computation.26 | async-start | bytes 2359296 | tf_op jit(solution)/shard_map/all_gather | solution.py:284
  316.2 216.1 %all-gather.51.cloned.1.call-start = ((), (), s32[]{:S(2)}) async-start(), calls=%async_computation.48 | async-start | bytes 2621440 | tf_op jit(solution)/shard_map/all_gather | solution.py:123
  316.8 239.6 %all-gather.55.cloned.1.call-start = ((), (), s32[]{:S(2)}) async-start(), calls=%async_computation.52 | async-start | bytes 2621440 | tf_op jit(solution)/shard_map/all_gather | solution.py:123
  317.4 286.1 %reduce-scatter.44.cloned.1.call-start = ((), (), s32[]{:S(2)}) async-start(), calls=%async_computation.45 | async-start | bytes 5242880 | tf_op jit(solution)/shard_map/reduce_scatter | solution.py:127
  317.4 238.9 %copy-start.223 = (f32[1,2,4,128]{3,1,2,0:T(2,128)}, f32[1,2,4,128]{3,1,2,0:T(2,128)S(1)}, u32[]{:S(2)}) copy-start(f32[1,2,4,128]{3,1,2,0:T(2,128)S(1)} %copy.255) | copy-start | bytes 12292
  361.2 204.3 %copy-start.80 = (bf16[128,8,4,256]{3,1,2,0:T(8,128)(2,1)}, bf16[128,8,4,256]{3,1,2,0:T(8,128)(2,1)S(1)}, u32[]{:S(2)}) copy-start(bf16[128,8,4,256]{3,1,2,0:T(8,128)(2,1)S(1)} %copy.254) | copy-start | bytes 6291460
  524.7 125.7 %reduce-scatter.48.cloned.1.call-start = ((), (), s32[]{:S(2)}) async-start(), calls=%async_computation.49 | async-start | bytes 5242880 | tf_op jit(solution)/shard_map/reduce_scatter | solution.py:127
  547.1 150.3 %reduce-scatter.52.cloned.1.call-start = ((), (), s32[]{:S(2)}) async-start(), calls=%async_computation.53 | async-start | bytes 5242880 | tf_op jit(solution)/shard_map/reduce_scatter | solution.py:127
  571.2 173.9 %reduce-scatter.30.cloned.1.call-start = ((), (), s32[]{:S(2)}) async-start(), calls=%async_computation.31 | async-start | bytes 5242880 | tf_op jit(solution)/shard_map/reduce_scatter | solution.py:119
  578.7 74.6 %copy-start.209 = (f32[256]{0:T(256)S(1)}, f32[256]{0:T(256)}, u32[]{:S(2)}) copy-start(f32[256]{0:T(256)} %copy-done.208) | copy-start | bytes 3076
  578.7 166.3 %copy-start.22 = (f32[1,256,1024]{2,1,0:T(8,128)S(1)}, f32[1,256,1024]{2,1,0:T(8,128)}, u32[]{:S(2)}) copy-start(f32[1,256,1024]{2,1,0:T(8,128)} %copy-done.21) | copy-start | bytes 3145732
  578.8 166.3 %copy-start.132 = (f32[1,1024]{1,0:T(1,128)S(1)}, f32[1,1024]{1,0:T(1,128)}, u32[]{:S(2)}) copy-start(f32[1,1024]{1,0:T(1,128)} %get-tuple-element.1002) | copy-start | bytes 12292
  578.8 197.0 %all-gather.53.cloned.1.call-start = ((), (), s32[]{:S(2)}) async-start(), calls=%async_computation.50 | async-start | bytes 2621440 | tf_op jit(solution)/shard_map/all_gather | solution.py:123
  753.1 62.9 %all-gather.57.cloned.1.call-start = ((), (), s32[]{:S(2)}) async-start(), calls=%async_computation.54 | async-start | bytes 2621440 | tf_op jit(solution)/shard_map/all_gather | solution.py:123
  753.8 102.2 %all-gather.49.cloned.1.call-start = ((), (), s32[]{:S(2)}) async-start(), calls=%async_computation.46 | async-start | bytes 2621440 | tf_op jit(solution)/shard_map/all_gather | solution.py:123
  754.6 142.3 %reduce-scatter.50.cloned.1.call-start = ((), (), s32[]{:S(2)}) async-start(), calls=%async_computation.51 | async-start | bytes 5242880 | tf_op jit(solution)/shard_map/reduce_scatter | solution.py:127
  815.7 103.9 %reduce-scatter.54.cloned.1.call-start = ((), (), s32[]{:S(2)}) async-start(), calls=%async_computation.55 | async-start | bytes 5242880 | tf_op jit(solution)/shard_map/reduce_scatter | solution.py:127
  855.7 111.7 %reduce-scatter.46.cloned.1.call-start = ((), (), s32[]{:S(2)}) async-start(), calls=%async_computation.47 | async-start | bytes 5242880 | tf_op jit(solution)/shard_map/reduce_scatter | solution.py:127
  896.3 74.6 %copy-start.146 = (f32[1,1024]{1,0:T(1,128)S(1)}, f32[1,1024]{1,0:T(1,128)}, u32[]{:S(2)}) copy-start(f32[1,1024]{1,0:T(1,128)} %copy-done.145) | copy-start | bytes 12292
  896.3 98.4 %all-gather.21.cloned.1.call-start = ((), (), s32[]{:S(2)}) async-start(), calls=%async_computation.21 | async-start | bytes 2621440 | tf_op jit(solution)/shard_map/all_gather | solution.py:115
  896.9 97.8 %copy-start.147 = (f32[256]{0:T(256)}, f32[256]{0:T(256)S(1)}, u32[]{:S(2)}) copy-start(f32[256]{0:T(256)S(1)} %broadcast_multiply_fusion.7) | copy-start | bytes 3076
  971.9 97.5 %reduce-scatter.24.cloned.1.call-start = ((), (), s32[]{:S(2)}) async-start(), calls=%async_computation.23 | async-start | bytes 5242880 | tf_op jit(solution)/shard_map/reduce_scatter | solution.py:119
  1024.8 70.9 %all-gather.25.cloned.1.call-start = ((), (), s32[]{:S(2)}) async-start(), calls=%async_computation.24 | async-start | bytes 2621440 | tf_op jit(solution)/shard_map/all_gather | solution.py:115
  1073.0 47.0 %all-gather.43.cloned.1.call-start = ((), (), s32[]{:S(2)}) async-start(), calls=%async_computation.40 | async-start | bytes 2621440 | tf_op jit(solution)/shard_map/all_gather | solution.py:123
  1073.7 105.3 %reduce-scatter.40.cloned.1.call-start = ((), (), s32[]{:S(2)}) async-start(), calls=%async_computation.41 | async-start | bytes 5242880 | tf_op jit(solution)/shard_map/reduce_scatter | solution.py:127
  1134.4 91.7 %reduce-scatter.26.cloned.1.call-start = ((), (), s32[]{:S(2)}) async-start(), calls=%async_computation.27 | async-start | bytes 5242880 | tf_op jit(solution)/shard_map/reduce_scatter | solution.py:119
  1140.5 133.4 %reduce-scatter.38.cloned.1.call-start = ((), (), s32[]{:S(2)}) async-start(), calls=%async_computation.39 | async-start | bytes 5242880 | tf_op jit(solution)/shard_map/reduce_scatter | solution.py:119
  1148.6 172.3 %reduce-scatter.34.cloned.1.call-start = ((), (), s32[]{:S(2)}) async-start(), calls=%async_computation.35 | async-start | bytes 5242880 | tf_op jit(solution)/shard_map/reduce_scatter | solution.py:119
  1154.6 166.2 %copy-start.12 = (bf16[4,1,256,1024]{3,2,1,0:T(8,128)(2,1)S(1)}, bf16[4,1,256,1024]{3,2,1,0:T(8,128)(2,1)}, u32[]{:S(2)}) copy-start(bf16[4,1,256,1024]{3,2,1,0:T(8,128)(2,1)} %param.37) | copy-start | bytes 6291460
  1154.6 232.3 %all-gather.45.cloned.1.call-start = ((), (), s32[]{:S(2)}) async-start(), calls=%async_computation.42 | async-start | bytes 2621440 | tf_op jit(solution)/shard_map/all_gather | solution.py:123
  1229.6 97.5 %copy-start.212 = (f32[256]{0:T(256)}, f32[256]{0:T(256)S(1)}, u32[]{:S(2)}) copy-start(f32[256]{0:T(256)S(1)} %negate_multiply_fusion.11) | copy-start | bytes 3076
  1327.1 183.2 %all-reduce.3.cloned.1.call-start = ((), (), s32[]{:S(2)}) async-start(), calls=%async_computation.61 | async-start | bytes 8388608
  1347.6 254.1 %reduce-scatter.60.cloned.1.call-start = ((), (), s32[]{:S(2)}) async-start(), calls=%async_computation.58 | async-start | bytes 4718592 | tf_op jit(solution)/shard_map/reduce_scatter | solution.py:319
  1377.7 288.4 %reduce-scatter.64.cloned.1.call-start = ((), (), s32[]{:S(2)}) async-start(), calls=%async_computation.60 | async-start | bytes 147456
  1420.3 312.3 %reduce-scatter.58.cloned.1.call-start = ((), (), s32[]{:S(2)}) async-start(), calls=%async_computation.57 | async-start | bytes 1179648 | tf_op jit(solution)/shard_map/reduce_scatter | solution.py:317
  1424.9 385.6 %reduce-scatter.56.cloned.1.call-start = ((), (), s32[]{:S(2)}) async-start(), calls=%async_computation.56 | async-start | bytes 3538944 | tf_op jit(solution)/shard_map/reduce_scatter | solution.py:316
  1449.0 408.5 %reduce-scatter.42.cloned.1.call-start = ((), (), s32[]{:S(2)}) async-start(), calls=%async_computation.43 | async-start | bytes 5242880 | tf_op jit(solution)/shard_map/reduce_scatter | solution.py:127
  1453.0 463.5 %reduce-scatter.62.cloned.1.call-start = ((), (), s32[]{:S(2)}) async-start(), calls=%async_computation.59 | async-start | bytes 36864 | tf_op jit(solution)/shard_map/reduce_scatter | solution.py:321
  1457.8 144.0 %copy-start.79 = (f32[4,256,128]{2,1,0:T(8,128)S(1)}, f32[4,256,128]{2,1,0:T(8,128)}, u32[]{:S(2)}) copy-start(f32[4,256,128]{2,1,0:T(8,128)} %param.47) | copy-start | bytes 1572868
  1513.6 219.0 %copy-start.98 = (f32[256,128]{1,0:T(8,128)S(1)}, f32[256,128]{1,0:T(8,128)}, u32[]{:S(2)}) copy-start(f32[256,128]{1,0:T(8,128)} %param.41) | copy-start | bytes 393220
  1513.6 297.0 %copy-start.74 = (f32[3,128,256]{1,2,0:T(8,128)S(1)}, f32[3,128,256]{1,2,0:T(8,128)}, u32[]{:S(2)}) copy-start(f32[3,128,256]{1,2,0:T(8,128)} %copy-done.73) | copy-start | bytes 1179652
  1513.6 297.0 %copy-start.90 = (f32[3,128,256]{1,2,0:T(8,128)S(1)}, f32[3,128,256]{1,2,0:T(8,128)}, u32[]{:S(2)}) copy-start(f32[3,128,256]{1,2,0:T(8,128)} %copy.215) | copy-start | bytes 1179652
  1518.3 339.2 %copy-start.9 = (bf16[4,1,256,1024]{3,2,1,0:T(8,128)(2,1)S(1)}, bf16[4,1,256,1024]{3,2,1,0:T(8,128)(2,1)}, u32[]{:S(2)}) copy-start(bf16[4,1,256,1024]{3,2,1,0:T(8,128)(2,1)} %param.36) | copy-start | bytes 6291460
  1518.3 339.3 %copy-start.113 = (f32[1,1024]{1,0:T(1,128)S(1)}, f32[1,1024]{1,0:T(1,128)}, u32[]{:S(2)}) copy-start(f32[1,1024]{1,0:T(1,128)} %copy-done.111) | copy-start | bytes 12292
  1518.3 339.3 %copy-start.136 = (f32[256]{0:T(256)S(1)}, f32[256]{0:T(256)}, u32[]{:S(2)}) copy-start(f32[256]{0:T(256)} %copy-done.134) | copy-start | bytes 3076
  1518.3 339.2 %copy-start.139 = (f32[256]{0:T(256)S(1)}, f32[256]{0:T(256)}, u32[]{:S(2)}) copy-start(f32[256]{0:T(256)} %copy-done.137) | copy-start | bytes 3076
  1518.3 339.2 %copy-start.148 = (f32[256]{0:T(256)S(1)}, f32[256]{0:T(256)}, u32[]{:S(2)}) copy-start(f32[256]{0:T(256)} %copy-done.147) | copy-start | bytes 3076
  (241 other events, 3884.0 us)
Sparse Core Ops, SparseCore 0:
  10.7 48.1 all-gather.22
  61.0 20.8 all-gather.38
  84.0 22.5 all-gather.30
  108.6 22.5 all-gather.34
  168.2 44.4 reduce-scatter.27
  215.3 44.4 reduce-scatter.31
  262.3 44.4 reduce-scatter.35
  309.8 49.2 all-gather.26
  361.3 21.0 all-gather.40
  384.5 22.5 all-gather.36
  409.3 22.5 all-gather.32
  433.4 22.5 all-gather.46
  458.9 51.0 all-gather.28
  511.5 20.7 all-gather.50
  533.8 22.5 all-gather.54
  558.9 44.4 reduce-scatter.43
  605.8 44.4 reduce-scatter.47
  652.9 44.4 reduce-scatter.51
  700.5 44.4 reduce-scatter.29
  753.2 22.5 all-gather.52
  778.1 22.5 all-gather.56
  802.9 22.5 all-gather.48
  828.2 44.4 reduce-scatter.49
  875.1 44.4 reduce-scatter.53
  922.9 44.4 reduce-scatter.45
  972.1 22.5 all-gather.20
  1024.9 44.4 reduce-scatter.23
  1073.1 22.5 all-gather.24
  1097.4 22.5 all-gather.42
  1134.5 44.5 reduce-scatter.39
  1181.6 44.4 reduce-scatter.25
  1229.4 44.4 reduce-scatter.37
  1276.3 44.4 reduce-scatter.33
  1327.2 22.5 all-gather.44
  1354.0 156.3 all-reduce.2
  1514.3 87.4 reduce-scatter.59
  1605.5 60.5 reduce-scatter.63
  1669.5 63.0 reduce-scatter.57
  1736.5 74.0 reduce-scatter.55
  1813.8 43.6 reduce-scatter.41
  1862.9 53.5 reduce-scatter.61
where the time goes:
time: 1930 us
  waiting for transfers between devices  1220 us (63%)
  matrix products  370 us (19%)
  other arithmetic  123 us (6%)
  local copies, waits for them, and re-layouts  104 us (5%)
  blocking collectives  87.4 us (5%)
    reduce_scatter x8, waiting for transfers between devices, rows_sum_forward(): return lax.psum_scatter(part, 'mp', scatter_dimension=1, tiled=True)  331 us
    reduce_scatter x8, waiting for transfers between devices, rows_sum_backward(): return lax.psum_scatter(part, 'mp', scatter_dimension=1, tiled=True)  249 us
    all_gather x8, waiting for transfers between devices, rows_forward(): return lax.all_gather(part, 'mp', axis=1, tiled=True)  121 us
    unnamed x43, waiting for transfers between devices  116 us
    reduce_scatter x1, waiting for transfers between devices, local(): lax.psum_scatter(grad_down, 'dp', scatter_dimension=2, tiled=True)  83.4 us
    reduce_scatter x1, waiting for transfers between devices, local(): lax.psum_scatter(grad_qkv, 'dp', scatter_dimension=1, tiled=True)  76.1 us
    reduce_scatter x1, waiting for transfers between devices, local(): lax.psum_scatter(grad_out_weight, 'dp', scatter_dimension=1, tiled=True)  64.3 us
    dot_general x4, matrix products, forward(): jnp.einsum('isd,df->isf', normed_two_all, up_full, preferred_element_type...  59.6 us
  transfers between devices with their start and end apart: 41, of which 33 were waited for; matrix products, arithmetic and copies ran while one was open for 24% of the time, Pallas kernels for 0%

commit v1 on v0

--- a/solution.py
+++ b/solution.py
@@ -1,6 +1,10 @@
+import functools
+
 import jax
 import jax.numpy as jnp
 from jax import lax
+from jax.experimental import pallas as pl
+from jax.experimental.pallas import tpu as pltpu
 from jax.sharding import PartitionSpec as P
 
 DH = 64
@@ -253,7 +257,7 @@
     return (grad_input, (grad_qkv, grad_out_weight, grad_up, grad_down, grad_biases, grad_vectors))
 
 
-def local(
+def local_general(
     tokens,
     cotangent,
     qkv_weight,
@@ -353,9 +357,499 @@
     )
 
 
+ZS, YS, MP = (4, 2, 4)
+DP = ZS * YS
+LANES = 128
+BF = jnp.bfloat16
+F32 = jnp.float32
+
+
+def swap_z(part, step):
+    return lax.ppermute(
+        part, "dp", [(z * YS + y, (z ^ step) * YS + y) for z in range(ZS) for y in range(YS)]
+    )
+
+
+def swap_y(part):
+    return lax.ppermute(part, "dp", [(each, each ^ 1) for each in range(DP)])
+
+
+def swap_mp(part, step):
+    return lax.ppermute(part, "mp", [(each, each ^ step) for each in range(MP)])
+
+
+def gather_rows_z(shard):
+    return jnp.concatenate([shard] + [swap_z(shard, step) for step in range(1, ZS)], 0)
+
+
+def gather_weight(shard, y_first):
+    rows = gather_rows_z(shard)
+    if y_first:
+        rows = jnp.concatenate([rows, swap_y(rows)], 0)
+        rows = jnp.concatenate([rows, swap_mp(rows, 2)], 1)
+    else:
+        rows = jnp.concatenate([rows, swap_mp(rows, 2)], 1)
+        rows = jnp.concatenate([rows, swap_y(rows)], 0)
+    return (rows, swap_mp(rows, 1))
+
+
+def add_low(first, second):
+    return (first.astype(F32) + second.astype(F32)).astype(BF)
+
+
+def reduce_x(total):
+    width = total.shape[1] // 2
+    return add_low(total[:, :width], swap_mp(total[:, width:], 2))
+
+
+def reduce_y(total):
+    rows = total.shape[0] // 2
+    return add_low(total[:rows], swap_y(total[rows:]))
+
+
+def reduce_weight(own_part, other_part, x_first):
+    total = add_low(own_part, swap_mp(other_part, 1))
+    if x_first:
+        total = reduce_y(reduce_x(total))
+    else:
+        total = reduce_x(reduce_y(total))
+    rows = total.shape[0] // ZS
+    result = total[:rows].astype(F32)
+    for step in range(1, ZS):
+        result = result + swap_z(total[step * rows : (step + 1) * rows], step).astype(F32)
+    return result
+
+
+def assemble_kernel(place_ref, own_ref, *refs):
+    chunk_rows = own_ref.shape[1]
+    out_ref = refs[-1]
+    out_ref[0:chunk_rows, :] = own_ref[0]
+    for at, part_ref in enumerate(refs[:-1]):
+        out_ref[(at + 1) * chunk_rows : (at + 2) * chunk_rows, :] = part_ref[...]
+
+
+def assemble_image(place, arrays, parts):
+    chunk_rows, width = parts[0].shape
+    return pl.pallas_call(
+        assemble_kernel,
+        grid_spec=pltpu.PrefetchScalarGridSpec(
+            num_scalar_prefetch=1,
+            grid=(width // LANES,),
+            in_specs=[
+                pl.BlockSpec((1, chunk_rows, LANES), lambda j, place_ref: (place_ref[DP], 0, place_ref[j]))
+            ]
+            + [pl.BlockSpec((chunk_rows, LANES), lambda j, place_ref: (0, place_ref[j]))] * len(parts),
+            out_specs=pl.BlockSpec((chunk_rows * MP, LANES), lambda j, place_ref: (0, j)),
+        ),
+        out_shape=jax.ShapeDtypeStruct((chunk_rows * MP, width), arrays.dtype),
+        name="assemble_image",
+    )(place, arrays, *parts)
+
+
+def spread_kernel(place_ref, own_ref, *refs):
+    out_ref = refs[-1]
+    mine = place_ref[DP]
+    out_ref[mine] = own_ref[...].astype(out_ref.dtype)
+    for at, part_ref in enumerate(refs[:-1]):
+        out_ref[mine ^ (at + 1)] = part_ref[...].astype(out_ref.dtype)
+
+
+def spread_image(place, own, parts, dtype):
+    chunk_rows, width = parts[0].shape
+    block = pl.BlockSpec((chunk_rows, LANES), lambda j, place_ref: (0, j))
+    return pl.pallas_call(
+        spread_kernel,
+        grid_spec=pltpu.PrefetchScalarGridSpec(
+            num_scalar_prefetch=1,
+            grid=(width // LANES,),
+            in_specs=[block] * (1 + len(parts)),
+            out_specs=pl.BlockSpec((MP, chunk_rows, LANES), lambda j, place_ref: (0, 0, place_ref[j])),
+        ),
+        out_shape=jax.ShapeDtypeStruct((MP, chunk_rows, width), dtype),
+        name="spread_image",
+    )(place, own, *parts)
+
+
+def lane_dot(left, right):
+    return lax.dot_general(left, right, (((1,), (1,)), ((), ())), preferred_element_type=F32)
+
+
+def head_masks(width):
+    lane = lax.broadcasted_iota(jnp.int32, (1, width), 1)
+    return [lane // DH == head for head in range(width // DH)]
+
+
+def attend_kernel(block_rows, q_ref, k_ref, v_ref, o_ref, lse_ref):
+    masks = head_masks(LANES)
+    key_rows = k_ref[...]
+    values = v_ref[...]
+    zero = jnp.zeros((), BF)
+    for block in range(q_ref.shape[0] // block_rows):
+        rows = slice(block * block_rows, (block + 1) * block_rows)
+        queries = q_ref[rows, :] * jnp.asarray(DH**-0.5, BF)
+        blended = []
+        for head, mask in enumerate(masks):
+            scores = lane_dot(jnp.where(mask, queries, zero), key_rows)
+            peak = jnp.max(scores, 1, keepdims=True)
+            shifted = jnp.exp(scores - peak)
+            total = jnp.sum(shifted, 1, keepdims=True)
+            part = jnp.dot(shifted.astype(BF), values, preferred_element_type=F32)
+            blended.append(part * (1.0 / total))
+            log_total = jnp.broadcast_to(peak + jnp.log(total), (block_rows, LANES))
+            lse_ref[0, head : head + 1, rows] = jnp.transpose(log_total)[0:1, :]
+        o_ref[rows, :] = jnp.where(masks[0], blended[0], blended[1]).astype(BF)
+
+
+def attend_back_kernel(
+    block_rows, q_ref, k_ref, v_ref, g_ref, lse_ref, dq_ref, dk_ref, dv_ref, dk_acc, dv_acc
+):
+    masks = head_masks(LANES)
+    key_rows = k_ref[...]
+    values = v_ref[...]
+    zero = jnp.zeros((), BF)
+    factor = DH**-0.5
+    key_heads = [jnp.where(mask, key_rows, zero) for mask in masks]
+    for block in range(q_ref.shape[0] // block_rows):
+        rows = slice(block * block_rows, (block + 1) * block_rows)
+        queries = q_ref[rows, :] * jnp.asarray(factor, BF)
+        grads = g_ref[rows, :]
+        grad_query = None
+        grad_keys = None
+        grad_values = None
+        for head, mask in enumerate(masks):
+            query_head = jnp.where(mask, queries, zero)
+            grad_head = jnp.where(mask, grads, zero)
+            scores = lane_dot(key_rows, query_head)
+            weights = jnp.exp(scores - lse_ref[0, head : head + 1, rows])
+            value_part = jnp.dot(weights.astype(BF), grad_head, preferred_element_type=F32)
+            grad_rows = lane_dot(values, grad_head)
+            delta = jnp.sum(grad_rows * weights, 0, keepdims=True)
+            grad_scores = (weights * (grad_rows - delta)).astype(BF)
+            key_part = jnp.dot(grad_scores, query_head, preferred_element_type=F32)
+            query_part = lax.dot_general(
+                grad_scores, key_heads[head], (((0,), (0,)), ((), ())), preferred_element_type=F32
+            )
+            grad_query = query_part if head == 0 else grad_query + query_part
+            grad_keys = key_part if head == 0 else grad_keys + key_part
+            grad_values = value_part if head == 0 else grad_values + value_part
+        dq_ref[rows, :] = (grad_query * factor).astype(BF)
+        if block == 0:
+            dk_acc[...] = grad_keys
+            dv_acc[...] = grad_values
+        else:
+            dk_acc[...] += grad_keys
+            dv_acc[...] += grad_values
+    dk_ref[...] = dk_acc[...].astype(BF)
+    dv_ref[...] = dv_acc[...].astype(BF)
+
+
+def pair_spec(rows, first):
+    kinds, kind = first
+    return pl.BlockSpec((rows, LANES), lambda p: (0, (p // 2) * (2 * kinds) + 2 * kind + p % 2))
+
+
+def attend(query_keys, values):
+    rows, width = values.shape
+    pairs = width // LANES
+    scores_size = rows * rows * 2 * pairs
+    return pl.pallas_call(
+        functools.partial(attend_kernel, 256),
+        grid=(pairs,),
+        in_specs=[pair_spec(rows, (2, 0)), pair_spec(rows, (2, 1)), pair_spec(rows, (1, 0))],
+        out_specs=[pair_spec(rows, (1, 0)), pl.BlockSpec((1, 8, rows), lambda p: (p, 0, 0))],
+        out_shape=[
+            jax.ShapeDtypeStruct((rows, width), BF),
+            jax.ShapeDtypeStruct((pairs, 8, rows), F32),
+        ],
+        compiler_params=pltpu.CompilerParams(vmem_limit_bytes=32 * 2**20),
+        cost_estimate=pl.CostEstimate(
+            flops=scores_size * 2 * 512, bytes_accessed=rows * width * 8, transcendentals=scores_size
+        ),
+        name="attend",
+    )(query_keys, query_keys, values)
+
+
+def attend_back(query_keys, values, grad_blended, log_total):
+    rows, width = values.shape
+    pairs = width // LANES
+    scores_size = rows * rows * 2 * pairs
+    single = pair_spec(rows, (1, 0))
+    return pl.pallas_call(
+        functools.partial(attend_back_kernel, 256),
+        grid=(pairs,),
+        in_specs=[
+            pair_spec(rows, (2, 0)),
+            pair_spec(rows, (2, 1)),
+            single,
+            single,
+            pl.BlockSpec((1, 8, rows), lambda p: (p, 0, 0)),
+        ],
+        out_specs=[single] * 3,
+        out_shape=[jax.ShapeDtypeStruct((rows, width), BF)] * 3,
+        scratch_shapes=[pltpu.VMEM((rows, LANES), F32)] * 2,
+        compiler_params=pltpu.CompilerParams(vmem_limit_bytes=32 * 2**20),
+        cost_estimate=pl.CostEstimate(
+            flops=scores_size * 2 * 1280, bytes_accessed=rows * width * 14, transcendentals=scores_size
+        ),
+        name="attend_back",
+    )(query_keys, query_keys, values, grad_blended, log_total)
+
+
+def dot_nn(left, right):
+    return lax.dot_general(left, right, (((1,), (0,)), ((), ())), preferred_element_type=F32)
+
+
+def dot_nt(left, right):
+    return lax.dot_general(left, right, (((1,), (1,)), ((), ())), preferred_element_type=F32)
+
+
+def dot_tn(left, right):
+    return lax.dot_general(left, right, (((0,), (0,)), ((), ())), preferred_element_type=F32)
+
+
+def norm_parts(values):
+    center = values - jnp.mean(values, -1, keepdims=True)
+    spread = lax.rsqrt(jnp.mean(center * center, -1, keepdims=True) + 1e-06)
+    return (center * spread, spread)
+
+
+def norm_back(grad, normal, spread, gain):
+    scaled = grad * gain
+    inner = scaled - jnp.mean(scaled, -1, keepdims=True)
+    inner = inner - normal * jnp.mean(scaled * normal, -1, keepdims=True)
+    return (spread * inner, jnp.sum(grad * normal, 0), jnp.sum(grad, 0))
+
+
+def gelu_pair(values):
+    share = 0.5 * (1.0 + lax.erf(values * 0.7071067811865476))
+    slope = share + values * (0.3989422804014327 * jnp.exp(-0.5 * values * values))
+    return ((values * share).astype(BF), slope.astype(BF))
+
+
+def local_image(
+    tokens,
+    cotangent,
+    qkv_weight,
+    qkv_first,
+    qkv_second,
+    out_weight,
+    out_first,
+    out_second,
+    up_weight,
+    up_first,
+    up_second,
+    down_weight,
+    down_first,
+    down_second,
+    head_biases,
+    bias_first,
+    bias_second,
+    vectors,
+    vector_first,
+    vector_second,
+):
+    dp_at = lax.axis_index("dp")
+    mp_at = lax.axis_index("mp")
+    units = up_weight.shape[1]
+    block_width = qkv_weight.shape[2]
+    depth = qkv_weight.shape[1]
+    bias_width = head_biases.shape[1]
+    chunk_rows, width = tokens.shape[2:]
+    order = [((zk * YS) + yk) for yk in range(YS) for zk in range(ZS)]
+    places = [dp_at ^ each for each in order]
+    place = jnp.stack(places + [mp_at]).astype(jnp.int32)
+
+    def fetch_image(array):
+        chunks = array[:, 0]
+        parts = [
+            swap_mp(lax.dynamic_index_in_dim(chunks, mp_at ^ step, 0, keepdims=False), step)
+            for step in range(1, MP)
+        ]
+        return assemble_image(place, chunks, parts)
+
+    small = jnp.concatenate(
+        [vectors.astype(BF).reshape(-1), head_biases.astype(BF).reshape(-1)]
+    ).reshape(1, -1)
+    vector_size = vectors.size
+    small = gather_rows_z(small)
+    small = jnp.concatenate([small, swap_y(small)], 0)
+    vector_full = (
+        small[:, :vector_size].reshape(DP, vectors.shape[0], LANES).transpose(1, 0, 2)
+    ).reshape(vectors.shape[0], width).astype(F32)
+    bias_small = small[:, vector_size:]
+    bias_small = jnp.stack([bias_small, swap_mp(bias_small, 2)], 0)
+    bias_small = jnp.stack([bias_small, swap_mp(bias_small, 1)], 0)
+    back_places = jnp.stack([((each ^ dp_at) & 1) * ZS + ((each ^ dp_at) >> 1) for each in range(DP)])
+    bias_rows = jnp.take(bias_small, back_places, axis=2).reshape(2, 2, DP, -1, bias_width)
+    bias_full = bias_rows.transpose(0, 3, 1, 2, 4).reshape(2, head_biases.shape[0], 2, block_width)
+    bias_full = bias_full.astype(F32)
+
+    inputs = fetch_image(tokens)
+    qkv_low = qkv_weight.astype(BF)
+    up_low = up_weight.astype(BF)
+    half_units = units // 2
+    down_low = down_weight.transpose(2, 0, 1).astype(BF)
+    w_qk = gather_weight(jnp.concatenate([qkv_low[0], qkv_low[1]], 1), False)
+    w_v = gather_weight(qkv_low[2], True)
+    w_out = gather_weight(out_weight.T.astype(BF), True)
+    w_up = [
+        gather_weight(up_low[:, at : at + half_units].reshape(depth, -1), at == 0)
+        for at in (0, half_units)
+    ]
+    w_down = [
+        gather_weight(down_low[:, at : at + half_units].reshape(depth, -1), at == 0)
+        for at in (0, half_units)
+    ]
+    cores = (0, 1)
+    gain_one, shift_one, out_bias, scale_one, gain_two, shift_two, down_bias, scale_two = vector_full
+
+    base = inputs.astype(F32)
+    normal_one, spread_one = norm_parts(base)
+    normed_one = (normal_one * gain_one + shift_one).astype(BF)
+    query_keys, values, blended, log_total = ([], [], [], [])
+    for core in cores:
+        query_bias = jnp.stack([bias_full[core, 0], jnp.zeros_like(bias_full[core, 0])], 1).reshape(-1)
+        query_keys.append((dot_nn(normed_one, w_qk[core]) + query_bias).astype(BF))
+        values.append((dot_nn(normed_one, w_v[core]) + bias_full[core, 1].reshape(-1)).astype(BF))
+    for core in cores:
+        part, part_total = attend(query_keys[core], values[core])
+        blended.append(part)
+        log_total.append(part_total)
+    branch_one = dot_nt(blended[0], w_out[0]) + dot_nt(blended[1], w_out[1]) + out_bias
+    hidden = base + scale_one * branch_one
+    normal_two, spread_two = norm_parts(hidden)
+    normed_two = (normal_two * gain_two + shift_two).astype(BF)
+    parts = [(half, core) for half in (0, 1) for core in cores]
+    activ, slope = ({}, {})
+    branch_two = down_bias
+    for half, core in parts:
+        rows = bias_full[core, 2 + half * half_units : 2 + (half + 1) * half_units]
+        unit_bias = rows.transpose(1, 0, 2).reshape(-1)
+        pre_act = dot_nn(normed_two, w_up[half][core]) + unit_bias
+        activ[half, core], slope[half, core] = gelu_pair(pre_act)
+        branch_two = branch_two + dot_nt(activ[half, core], w_down[half][core])
+    output = (hidden + scale_two * branch_two).astype(BF)
+
+    def send_back(array, dtype):
+        low = array.astype(BF)
+        back = [
+            swap_mp(low[step * chunk_rows : (step + 1) * chunk_rows], step) for step in range(1, MP)
+        ]
+        return spread_image(place, array[:chunk_rows], back, dtype)[:, None]
+
+    layer_output = send_back(output, BF)
+
+    grad_out = fetch_image(cotangent).astype(F32)
+    grad_scale_two = jnp.sum(grad_out * branch_two, 0)
+    grad_down_bias = jnp.sum(grad_out, 0) * scale_two
+    grad_branch = (grad_out * scale_two).astype(BF)
+    sums = {}
+    for half in (0, 1):
+        own, other = [dot_tn(grad_branch, activ[half, core]).astype(BF) for core in cores]
+        sums["down", half] = reduce_weight(own, other, half == 0)
+    grad_pre = {}
+    grad_normed_two = 0.0
+    for half in (0, 1):
+        for core in cores:
+            grad_activ = dot_nn(grad_branch, w_down[half][core])
+            grad_pre[half, core] = (grad_activ * slope[half, core].astype(F32)).astype(BF)
+        own, other = [dot_tn(normed_two, grad_pre[half, core]).astype(BF) for core in cores]
+        sums["up", half] = reduce_weight(own, other, half == 0)
+        for core in cores:
+            grad_normed_two = grad_normed_two + dot_nt(grad_pre[half, core], w_up[half][core])
+    grad_unit_bias = {key: jnp.sum(grad_pre[key].astype(F32), 0) for key in parts}
+    grad_hidden, grad_gain_two, grad_shift_two = norm_back(
+        grad_normed_two, normal_two, spread_two, gain_two
+    )
+    grad_hidden = grad_out + grad_hidden
+    grad_scale_one = jnp.sum(grad_hidden * branch_one, 0)
+    grad_out_bias = jnp.sum(grad_hidden, 0) * scale_one
+    grad_projected = (grad_hidden * scale_one).astype(BF)
+    own, other = [dot_tn(grad_projected, blended[core]).astype(BF) for core in cores]
+    sums["out"] = reduce_weight(own, other, True)
+    grad_qk, grad_v = ([], [])
+    for core in cores:
+        grad_blended = dot_nn(grad_projected, w_out[core]).astype(BF)
+        grad_query, grad_key, grad_value = attend_back(
+            query_keys[core], values[core], grad_blended, log_total[core]
+        )
+        pair_shape = (grad_query.shape[0], 2, -1)
+        stacked = jnp.stack([grad_query.reshape(pair_shape), grad_key.reshape(pair_shape)], 2)
+        grad_qk.append(stacked.reshape(grad_query.shape[0], -1))
+        grad_v.append(grad_value)
+    own, other = [dot_tn(normed_one, grad_qk[core]).astype(BF) for core in cores]
+    sums["qk"] = reduce_weight(own, other, False)
+    own, other = [dot_tn(normed_one, grad_v[core]).astype(BF) for core in cores]
+    sums["v"] = reduce_weight(own, other, True)
+    grad_normed_one = 0.0
+    for core in cores:
+        grad_normed_one = grad_normed_one + dot_nt(grad_qk[core], w_qk[core])
+        grad_normed_one = grad_normed_one + dot_nt(grad_v[core], w_v[core])
+    grad_input, grad_gain_one, grad_shift_one = norm_back(
+        grad_normed_one, normal_one, spread_one, gain_one
+    )
+    input_grad = send_back(grad_hidden + grad_input, F32)
+
+    grad_vectors = jnp.stack(
+        [
+            grad_gain_one,
+            grad_shift_one,
+            grad_out_bias,
+            grad_scale_one,
+            grad_gain_two,
+            grad_shift_two,
+            grad_down_bias,
+            grad_scale_two,
+        ]
+    )
+    grad_vectors = grad_vectors.reshape(-1, DP, LANES).transpose(1, 0, 2).reshape(DP, -1)
+    bias_parts = []
+    for core in cores:
+        query_part = jnp.sum(grad_qk[core].astype(F32), 0).reshape(2, 2, block_width)[:, 0]
+        value_part = jnp.sum(grad_v[core].astype(F32), 0).reshape(2, block_width)
+        rows = [query_part, value_part]
+        for half in (0, 1):
+            unit_part = grad_unit_bias[half, core].reshape(2, half_units, block_width)
+            rows += [unit_part[:, at] for at in range(half_units)]
+        bias_parts.append(jnp.stack(rows, 1))
+    grad_biases = jnp.stack(bias_parts).reshape(2, 2, -1, DP, bias_width).transpose(0, 1, 3, 2, 4)
+    grad_biases = jnp.take(grad_biases, place[:DP], axis=2).reshape(2, 2, DP, -1)
+    total_vectors = grad_vectors + swap_mp(grad_vectors, 1)
+    total_biases = grad_biases[0] + swap_mp(grad_biases[1], 1)
+    total_vectors = total_vectors + swap_mp(total_vectors, 2)
+    total_biases = total_biases[0] + swap_mp(total_biases[1], 2)
+    small_grads = jnp.concatenate([total_vectors, total_biases], 1)
+    small_grads = small_grads[:ZS] + swap_y(small_grads[ZS:])
+    small_total = small_grads[0]
+    for step in range(1, ZS):
+        small_total = small_total + swap_z(small_grads[step], step)
+    vector_grad = small_total[:vector_size].reshape(vectors.shape)
+    bias_grad = small_total[vector_size:].reshape(head_biases.shape)
+
+    qk_sum = sums["qk"].reshape(depth, 2, block_width).transpose(1, 0, 2)
+    qkv_grad = jnp.concatenate([qk_sum, sums["v"][None]], 0)
+    up_grad = jnp.concatenate(
+        [sums["up", half].reshape(depth, half_units, block_width) for half in (0, 1)], 1
+    )
+    down_grad = jnp.concatenate(
+        [sums["down", half].reshape(depth, half_units, block_width) for half in (0, 1)], 1
+    ).transpose(1, 2, 0)
+    grads = (qkv_grad, sums["out"].T, up_grad, down_grad, bias_grad, vector_grad)
+    params = (qkv_weight, out_weight, up_weight, down_weight, head_biases, vectors)
+    firsts = (qkv_first, out_first, up_first, down_first, bias_first, vector_first)
+    seconds = (qkv_second, out_second, up_second, down_second, bias_second, vector_second)
+    results = [layer_output, input_grad]
+    for slot in range(6):
+        results.extend(
+            adam_update(params[slot], firsts[slot], seconds[slot], grads[slot], RATES[slot])
+        )
+    return tuple(results)
+
+
 def solution(mesh):
+    whole_image = mesh.shape["mp"] == MICRO == MP and mesh.shape["dp"] == DP
     return jax.shard_map(
-        local,
+        local_image if whole_image else local_general,
         mesh=mesh,
         in_specs=(
             P(None, "dp", "mp", None),

time: 1930 us -> 824 us (0.43)
  waiting for transfers between devices: 1220 us -> 271 us
  matrix products: 370 us -> 151 us
  Pallas kernels: 0 us -> 128 us
  starting transfers between devices: 4.51 us -> 120 us
  blocking collectives: 87.4 us -> 0 us
  other arithmetic: 123 us -> 80.8 us
  local copies, waits for them, and re-layouts: 104 us -> 64 us
    reduce_scatter x20 -> x0, waiting for transfers between devices: 850 us -> none  [the longest x8 331 us: rows_sum_forward(): return lax.psum_scatter(part, 'mp', scatter_dimension=1, tiled=True)]
    ppermute x0 -> x110, waiting for transfers between devices: none -> 271 us  [the longest x46 113 us: swap_mp(): return lax.ppermute(part, 'mp', [(each, each ^ step) for each in range(MP)])]
    all_gather x19 -> x0, waiting for transfers between devices: 255 us -> none  [the longest x8 121 us: rows_forward(): return lax.all_gather(part, 'mp', axis=1, tiled=True)]
    dot_general x104 -> x42, matrix products: 370 us -> 151 us  [the longest x14 58.2 us: dot_nt(): lax.dot_general(left, right, (((1,), (1,)), ((), ())), preferred_element_...]
    pallas_call x0 -> x8, Pallas kernels: none -> 128 us  [the longest x2 64.3 us: attend_back(): pl.pallas_call(functools.partial(attend_back_kernel, 256), grid=(pairs,),...]
    ppermute x0 -> x110, starting transfers between devices: none -> 120 us  [the longest x48 70.5 us: swap_z(): lax.ppermute(part, 'dp', [(z * YS + y, (z ^ step) * YS + y) for z in rang...]
    unnamed x43 -> x0, waiting for transfers between devices: 116 us -> none
    all_gather x3 -> x0, blocking collectives: 81.6 us -> none  [the longest x1 27.8 us: gather_params(): lax.all_gather(vectors.astype(jnp.bfloat16), 'dp', axis=1, tiled=True)]
  transfers between devices with their start and end apart: 41 -> 110, of which waited for: 33 -> 44; matrix products, arithmetic and copies ran while one was open for 24% -> 24% of each run, Pallas kernels for 0% -> 8%
where the time goes in v1:
time: 824 us; the launch traced here: 817 us
  waiting for transfers between devices  271 us (33%)
  matrix products  151 us (18%)
  Pallas kernels  128 us (16%)
  starting transfers between devices  120 us (15%)
  other arithmetic  80.8 us (10%)
  local copies, waits for them, and re-layouts  64 us (8%)
    ppermute x46, waiting for transfers between devices, swap_mp(): return lax.ppermute(part, 'mp', [(each, each ^ step) for each in range(MP)])  113 us
    ppermute x16, waiting for transfers between devices, swap_y(): return lax.ppermute(part, 'dp', [(each, each ^ 1) for each in range(DP)])  99.8 us
    ppermute x48, starting transfers between devices, swap_z(): lax.ppermute(part, 'dp', [(z * YS + y, (z ^ step) * YS + y) for z in rang...  70.5 us
    pallas_call x2, Pallas kernels, attend_back(): pl.pallas_call(functools.partial(attend_back_kernel, 256), grid=(pairs,),...  64.3 us
    dot_general x14, matrix products, dot_nt(): lax.dot_general(left, right, (((1,), (1,)), ((), ())), preferred_element_...  58.2 us
    ppermute x48, waiting for transfers between devices, swap_z(): lax.ppermute(part, 'dp', [(z * YS + y, (z ^ step) * YS + y) for z in rang...  57.7 us
    dot_general x14, matrix products, dot_nn(): lax.dot_general(left, right, (((1,), (0,)), ((), ())), preferred_element_...  53.1 us
    dot_general x14, matrix products, dot_tn(): lax.dot_general(left, right, (((0,), (0,)), ((), ())), preferred_element_...  39.9 us
  transfers between devices with their start and end apart: 110, of which 44 were waited for; matrix products, arithmetic and copies ran while one was open for 24% of the time, Pallas kernels for 8%

profile of v1, /device:TPU:0, one launch (start us, length us, event | category | flops | bytes accessed | tf_op | source)
XLA Modules:
  0.0 817.5 jit_solution(6564529950188898606)
XLA Ops:
  10.3 3.8 collective-permute-start.9
  57.1 3.6 collective-permute-start.41
  63.3 8.4 %collective-permute-done.28 = bf16[128,512]{0,1:T(8,128)(2,1)S(1)} collective-permute-done((bf16[128,512]{0,1:T(8,128)(2,1)S(1)}, bf16[128,512]{0,1:T(8,128)(2,1)S(1)}, u32[]{:S(2)}, u32[]{:S(2)}) %collective-permute-start.28) | collective-permute-done | bytes 131104 | tf_op jit(solution)/shard_map/ppermute | solution.py:368
  74.5 4.0 collective-permute-done.40
  81.7 6.1 collective-permute-done.17
  92.9 4.2 collective-permute-done.2.refs_2_
  98.6 6.8 assemble_image.2
  108.4 23.3 %collective-permute-done.10 = bf16[512,512]{1,0:T(8,128)(2,1)} collective-permute-done((bf16[512,512]{1,0:T(8,128)(2,1)}, bf16[512,512]{1,0:T(8,128)(2,1)}, u32[]{:S(2)}, u32[]{:S(2)}) %collective-permute-start.10) | collective-permute-done | bytes 524320 | tf_op jit(solution)/shard_map/ppermute | solution.py:378
  140.1 6.4 assemble_image.3
  155.3 10.0 %collective-permute-done.23 = bf16[1024,256]{0,1:T(8,128)(2,1)} collective-permute-done((bf16[1024,256]{0,1:T(8,128)(2,1)S(1)}, bf16[1024,256]{0,1:T(8,128)(2,1)}, u32[]{:S(2)}, u32[]{:S(2)}) %collective-permute-start.23) | collective-permute-done | bytes 524320 | tf_op jit(solution)/shard_map/ppermute | solution.py:378
  174.4 15.6 %collective-permute-done.43 = bf16[512,1024]{0,1:T(8,128)(2,1)S(1)} collective-permute-done((bf16[512,1024]{0,1:T(8,128)(2,1)S(1)}, bf16[512,1024]{0,1:T(8,128)(2,1)S(1)}, u32[]{:S(2)}, u32[]{:S(2)}) %collective-permute-start.43) | collective-permute-done | bytes 1048608 | tf_op jit(solution)/shard_map/ppermute | solution.py:374
  193.5 18.1 %attend.2 = (bf16[1024,512]{1,0:T(8,128)(2,1)S(1)}, f32[4,8,1024]{2,1,0:T(8,128)S(1)}) custom-call(bf16[1024,1024]{1,0:T(8,128)(2,1)S(1)} %add_convert_fusion.8.q_ref.k_ref, bf16[1024,1024]{1,0:T(8,128)(2,1)S(1)} %add_convert_fusion.8.q_ref.k_ref, bf16[1024,512]{1,0:T(8,128)(2,1)S(1)} %add_convert_fusion.17.v_ref), custom_call_target="tpu_custom_call" | custom-call | flops 8589934592 | bytes 4194304 | tf_op jit(solution)/shard_map/attend/pallas_call | solution.py:555
  215.4 18.4 %attend.3 = (bf16[1024,512]{1,0:T(8,128)(2,1)S(1)}, f32[4,8,1024]{2,1,0:T(8,128)S(1)}) custom-call(bf16[1024,1024]{1,0:T(8,128)(2,1)S(1)} %add_convert_fusion.7.q_ref.k_ref, bf16[1024,1024]{1,0:T(8,128)(2,1)S(1)} %add_convert_fusion.7.q_ref.k_ref, bf16[1024,512]{1,0:T(8,128)(2,1)S(1)} %add_convert_fusion.16.v_ref), custom_call_target="tpu_custom_call" | custom-call | flops 8589934592 | bytes 4194304 | tf_op jit(solution)/shard_map/attend/pallas_call | solution.py:555
  235.1 4.6 fusion.71
  242.6 4.3 multiply_convert_fusion.5
  249.5 4.2 multiply_convert_fusion.7
  256.7 4.4 multiply_convert_fusion.6
  263.5 5.2 multiply_convert_fusion.8
  276.4 18.6 %collective-permute-done.97 = bf16[512,1024]{0,1:T(8,128)(2,1)S(1)} collective-permute-done((bf16[512,1024]{0,1:T(8,128)(2,1)S(1)}, bf16[512,1024]{0,1:T(8,128)(2,1)S(1)}, u32[]{:S(2)}, u32[]{:S(2)}) %collective-permute-start.97) | collective-permute-done | bytes 1048608 | tf_op jit(solution)/shard_map/ppermute | solution.py:374
  297.0 4.0 collective-permute-done.91
  302.0 9.0 %collective-permute-done.98 = bf16[512,512]{0,1:T(8,128)(2,1)S(1)} collective-permute-done((bf16[512,512]{0,1:T(8,128)(2,1)S(1)}, bf16[512,512]{0,1:T(8,128)(2,1)S(1)}, u32[]{:S(2)}, u32[]{:S(2)}) %collective-permute-start.98) | collective-permute-done | bytes 524320 | tf_op jit(solution)/shard_map/ppermute | solution.py:378
  320.4 6.3 collective-permute-done.100
  328.0 6.3 collective-permute-done.94
  340.9 3.9 collective-permute-done.46
  344.7 4.8 collective-permute-done.45
  378.2 24.3 %collective-permute-done.35 = bf16[512,512]{0,1:T(8,128)(2,1)S(1)} collective-permute-done((bf16[512,512]{0,1:T(8,128)(2,1)S(1)}, bf16[512,512]{0,1:T(8,128)(2,1)S(1)}, u32[]{:S(2)}, u32[]{:S(2)}) %collective-permute-start.35) | collective-permute-done | bytes 524320 | tf_op jit(solution)/shard_map/ppermute | solution.py:374
  404.7 6.8 pad_maximum_fusion.4
  411.6 6.2 fusion.87
  417.8 8.3 %collective-permute-done.36 = bf16[1024,512]{0,1:T(8,128)(2,1)S(1)} collective-permute-done((bf16[1024,512]{0,1:T(8,128)(2,1)S(1)}, bf16[1024,512]{0,1:T(8,128)(2,1)S(1)}, u32[]{:S(2)}, u32[]{:S(2)}) %collective-permute-start.36) | collective-permute-done | bytes 1048608 | tf_op jit(solution)/shard_map/ppermute | solution.py:378
  427.6 4.9 convert_reduce_fusion.6
  432.6 4.3 fusion.59
  436.9 6.6 convert_reduce_fusion.5
  443.6 4.3 fusion.60
  448.1 4.7 fusion.89
  452.8 5.6 convert_reduce_fusion.3
  461.4 5.4 convert_reduce_fusion.2
  466.8 3.9 multiply_reduce_fusion
  470.8 6.7 fusion.86
  477.5 6.1 fusion.35
  483.6 3.5 multiply_reduce_fusion.1
  492.1 32.2 %attend_back.2 = (bf16[1024,512]{1,0:T(8,128)(2,1)S(1)}, bf16[1024,512]{1,0:T(8,128)(2,1)S(1)}, bf16[1024,512]{1,0:T(8,128)(2,1)S(1)}) custom-call(bf16[1024,1024]{1,0:T(8,128)(2,1)S(1)} %copy-done.10, bf16[1024,1024]{1,0:T(8,128)(2,1)S(1)} %copy-done.10, bf16[1024,512]{1,0:T(8,128)(2,1)S(1)} %copy-done.6, ...), custom_call_target="tpu_custom_call" | custom-call | flops 21474836480 | bytes 7340032 | tf_op jit(solution)/shard_map/attend_back/pallas_call | solution.py:577
  529.2 4.5 fusion.90
  533.7 3.7 fusion.92
  539.8 3.8 convolution_convert_fusion.3
  543.6 3.8 convolution_convert_fusion.4
  549.3 32.1 %attend_back.3 = (bf16[1024,512]{1,0:T(8,128)(2,1)S(1)}, bf16[1024,512]{1,0:T(8,128)(2,1)S(1)}, bf16[1024,512]{1,0:T(8,128)(2,1)S(1)}) custom-call(bf16[1024,1024]{1,0:T(8,128)(2,1)S(1)} %copy-done.12, bf16[1024,1024]{1,0:T(8,128)(2,1)S(1)} %copy-done.12, bf16[1024,512]{1,0:T(8,128)(2,1)S(1)} %copy-done.8, ...), custom_call_target="tpu_custom_call" | custom-call | flops 21474836480 | bytes 7340032 | tf_op jit(solution)/shard_map/attend_back/pallas_call | solution.py:577
  593.5 3.8 convolution_convert_fusion
  603.0 4.5 fusion.12
  609.7 6.7 fusion.69
  638.3 10.3 %collective-permute-done.52.refs_1_ = bf16[256,1024]{1,0:T(8,128)(2,1)S(1)} collective-permute-done((bf16[256,1024]{1,0:T(8,128)(2,1)S(1)}, bf16[256,1024]{1,0:T(8,128)(2,1)S(1)}, u32[]{:S(2)}, u32[]{:S(2)}) %collective-permute-start.52) | collective-permute-done | bytes 524320 | tf_op jit(solution)/shard_map/ppermute | solution.py:378
  648.8 10.2 %collective-permute-done.53.refs_2_ = bf16[256,1024]{1,0:T(8,128)(2,1)S(1)} collective-permute-done((bf16[256,1024]{1,0:T(8,128)(2,1)S(1)}, bf16[256,1024]{1,0:T(8,128)(2,1)S(1)}, u32[]{:S(2)}, u32[]{:S(2)}) %collective-permute-start.53) | collective-permute-done | bytes 524320 | tf_op jit(solution)/shard_map/ppermute | solution.py:378
  667.1 6.3 spread_image.2
  673.4 8.1 collective-permute-done.59.refs_2_
  682.3 7.1 spread_image.3
  689.4 4.3 collective-permute-done.67
  695.9 8.6 %collective-permute-done.73 = bf16[1024,256]{1,0:T(8,128)(2,1)} collective-permute-done((bf16[1024,256]{1,0:T(8,128)(2,1)}, bf16[1024,256]{1,0:T(8,128)(2,1)}, u32[]{:S(2)}, u32[]{:S(2)}) %collective-permute-start.73) | collective-permute-done | bytes 524320 | tf_op jit(solution)/shard_map/ppermute | solution.py:378
  709.5 4.1 collective-permute-done.74
  716.1 4.2 add_convert_fusion.2
  730.4 4.0 add_convert_fusion.3
  745.9 8.9 %collective-permute-done.61 = bf16[512,1024]{0,1:T(8,128)(2,1)} collective-permute-done((bf16[512,1024]{0,1:T(8,128)(2,1)}, bf16[512,1024]{0,1:T(8,128)(2,1)}, u32[]{:S(2)}, u32[]{:S(2)}) %collective-permute-start.61) | collective-permute-done | bytes 1048608 | tf_op jit(solution)/shard_map/ppermute | solution.py:374
  757.5 16.5 %collective-permute-done.85 = bf16[512,1024]{0,1:T(8,128)(2,1)S(1)} collective-permute-done((bf16[512,1024]{0,1:T(8,128)(2,1)}, bf16[512,1024]{0,1:T(8,128)(2,1)S(1)}, u32[]{:S(2)}, u32[]{:S(2)}) %collective-permute-start.85) | collective-permute-done | bytes 1048608 | tf_op jit(solution)/shard_map/ppermute | solution.py:374
  791.6 7.3 collective-permute-done.64
  803.6 3.8 collective-permute-done.88
  807.7 4.0 collective-permute-done.82
  (773 shorter events, 305.0 us)
Async XLA Ops:
  2.3 21.7 %collective-permute-start.3 = (bf16[1,1216]{1,0:T(2,128)(2,1)S(1)}, bf16[1,1216]{1,0:T(2,128)(2,1)S(1)}, u32[]{:S(2)}, u32[]{:S(2)}) collective-permute-start(bf16[1,1216]{1,0:T(2,128)(2,1)S(1)} %reshape.934), channel_id=1, source_target_pairs={{0,8},{4,12},{8,0},{12,4},{16,24},{20,28},{24,16},{28,20},{1,9},{5... | collective-permute-start | bytes 7304 | tf_op jit(solution)/shard_map/ppermute | solution.py:368
  5.4 19.2 %collective-permute-start.4 = (bf16[1,1216]{1,0:T(2,128)(2,1)S(1)}, bf16[1,1216]{1,0:T(2,128)(2,1)}, u32[]{:S(2)}, u32[]{:S(2)}) collective-permute-start(bf16[1,1216]{1,0:T(2,128)(2,1)S(1)} %reshape.934), channel_id=1, source_target_pairs={{0,16},{4,20},{8,24},{12,28},{16,0},{20,4},{24,8},{28,12},{1,17},{... | collective-permute-start | bytes 7304 | tf_op jit(solution)/shard_map/ppermute | solution.py:368
  8.0 19.0 %collective-permute-start.5 = (bf16[1,1216]{1,0:T(2,128)(2,1)S(1)}, bf16[1,1216]{1,0:T(2,128)(2,1)}, u32[]{:S(2)}, u32[]{:S(2)}) collective-permute-start(bf16[1,1216]{1,0:T(2,128)(2,1)S(1)} %reshape.934), channel_id=1, source_target_pairs={{0,24},{4,28},{8,16},{12,20},{16,8},{20,12},{24,0},{28,4},{1,25},{... | collective-permute-start | bytes 7304 | tf_op jit(solution)/shard_map/ppermute | solution.py:368
  10.3 46.4 %collective-permute-start.9 = (bf16[128,512]{1,0:T(8,128)(2,1)}, bf16[128,512]{1,0:T(8,128)(2,1)S(1)}, u32[]{:S(2)}, u32[]{:S(2)}) collective-permute-start(bf16[128,512]{1,0:T(8,128)(2,1)} %pad_maximum_fusion.21), channel_id=1, source_target_pairs={{0,24},{4,28},{8,16},{12,20},{16,8},{20,12},{24,0},{28,4},{1,25},{... | collective-permute-start | bytes 393224 | tf_op jit(solution)/shard_map/ppermute | solution.py:368
  14.2 42.9 %collective-permute-start.8 = (bf16[128,512]{1,0:T(8,128)(2,1)}, bf16[128,512]{1,0:T(8,128)(2,1)}, u32[]{:S(2)}, u32[]{:S(2)}) collective-permute-start(bf16[128,512]{1,0:T(8,128)(2,1)} %pad_maximum_fusion.21), channel_id=1, source_target_pairs={{0,16},{4,20},{8,24},{12,28},{16,0},{20,4},{24,8},{28,12},{1,17},{... | collective-permute-start | bytes 393224 | tf_op jit(solution)/shard_map/ppermute | solution.py:368
  24.0 20.5 %collective-permute-start.14 = (bf16[128,256]{1,0:T(8,128)(2,1)S(1)}, bf16[128,256]{1,0:T(8,128)(2,1)S(1)}, u32[]{:S(2)}, u32[]{:S(2)}) collective-permute-start(bf16[128,256]{1,0:T(8,128)(2,1)S(1)} %copy-done.109), channel_id=1, source_target_pairs={{0,8},{4,12},{8,0},{12,4},{16,24},{20,28},{24,16},{28,20},{1,9},{5... | collective-permute-start | bytes 196616 | tf_op jit(solution)/shard_map/ppermute | solution.py:368
  24.5 20.5 %collective-permute-start.15 = (bf16[128,256]{1,0:T(8,128)(2,1)S(1)}, bf16[128,256]{1,0:T(8,128)(2,1)S(1)}, u32[]{:S(2)}, u32[]{:S(2)}) collective-permute-start(bf16[128,256]{1,0:T(8,128)(2,1)S(1)} %copy-done.109), channel_id=1, source_target_pairs={{0,16},{4,20},{8,24},{12,28},{16,0},{20,4},{24,8},{28,12},{1,17},{... | collective-permute-start | bytes 196616 | tf_op jit(solution)/shard_map/ppermute | solution.py:368
  54.4 17.2 %collective-permute-start.28 = (bf16[128,512]{0,1:T(8,128)(2,1)S(1)}, bf16[128,512]{0,1:T(8,128)(2,1)S(1)}, u32[]{:S(2)}, u32[]{:S(2)}) collective-permute-start(bf16[128,512]{0,1:T(8,128)(2,1)S(1)} %bitcast.323), channel_id=1, source_target_pairs={{0,16},{4,20},{8,24},{12,28},{16,0},{20,4},{24,8},{28,12},{1,17},{... | collective-permute-start | bytes 393224 | tf_op jit(solution)/shard_map/ppermute | solution.py:368
  57.1 17.0 %collective-permute-start.41 = (bf16[128,512]{0,1:T(8,128)(2,1)S(1)}, bf16[128,512]{0,1:T(8,128)(2,1)S(1)}, u32[]{:S(2)}, u32[]{:S(2)}) collective-permute-start(bf16[128,512]{0,1:T(8,128)(2,1)S(1)} %bitcast.309), channel_id=1, source_target_pairs={{0,24},{4,28},{8,16},{12,20},{16,8},{20,12},{24,0},{28,4},{1,25},{... | collective-permute-start | bytes 393224 | tf_op jit(solution)/shard_map/ppermute | solution.py:368
  60.7 17.8 %collective-permute-start.40 = (bf16[128,512]{0,1:T(8,128)(2,1)S(1)}, bf16[128,512]{0,1:T(8,128)(2,1)S(1)}, u32[]{:S(2)}, u32[]{:S(2)}) collective-permute-start(bf16[128,512]{0,1:T(8,128)(2,1)S(1)} %bitcast.310), channel_id=1, source_target_pairs={{0,16},{4,20},{8,24},{12,28},{16,0},{20,4},{24,8},{28,12},{1,17},{... | collective-permute-start | bytes 393224 | tf_op jit(solution)/shard_map/ppermute | solution.py:368
  62.5 17.6 %collective-permute-start.39 = (bf16[128,512]{0,1:T(8,128)(2,1)S(1)}, bf16[128,512]{0,1:T(8,128)(2,1)S(1)}, u32[]{:S(2)}, u32[]{:S(2)}) collective-permute-start(bf16[128,512]{0,1:T(8,128)(2,1)S(1)} %bitcast.311), channel_id=1, source_target_pairs={{0,8},{4,12},{8,0},{12,4},{16,24},{20,28},{24,16},{28,20},{1,9},{5... | collective-permute-start | bytes 393224 | tf_op jit(solution)/shard_map/ppermute | solution.py:368
  71.7 20.5 %collective-permute-start = (bf16[256,1024]{1,0:T(8,128)(2,1)}, bf16[256,1024]{1,0:T(8,128)(2,1)S(1)}, u32[]{:S(2)}, u32[]{:S(2)}) collective-permute-start(bf16[256,1024]{1,0:T(8,128)(2,1)} %get-tuple-element.196), channel_id=1, source_target_pairs={{0,1},{1,0},{2,3},{3,2},{4,5},{5,4},{6,7},{7,6},{8,9},{9,8},{10,11... | collective-permute-start | bytes 1572872 | tf_op jit(solution)/shard_map/ppermute | solution.py:378
  71.7 20.6 %collective-permute-start.1 = (bf16[256,1024]{1,0:T(8,128)(2,1)}, bf16[256,1024]{1,0:T(8,128)(2,1)S(1)}, u32[]{:S(2)}, u32[]{:S(2)}) collective-permute-start(bf16[256,1024]{1,0:T(8,128)(2,1)} %get-tuple-element.197), channel_id=1, source_target_pairs={{0,2},{1,3},{2,0},{3,1},{4,6},{5,7},{6,4},{7,5},{8,10},{9,11},{10,... | collective-permute-start | bytes 1572872 | tf_op jit(solution)/shard_map/ppermute | solution.py:378
  74.1 23.0 %collective-permute-start.2 = (bf16[256,1024]{1,0:T(8,128)(2,1)S(1)}, bf16[256,1024]{1,0:T(8,128)(2,1)S(1)}, u32[]{:S(2)}, u32[]{:S(2)}) collective-permute-start(bf16[256,1024]{1,0:T(8,128)(2,1)S(1)} %copy-done.98), channel_id=1, source_target_pairs={{0,3},{1,2},{2,1},{3,0},{4,7},{5,6},{6,5},{7,4},{8,11},{9,10},{10,... | collective-permute-start | bytes 1572872 | tf_op jit(solution)/shard_map/ppermute | solution.py:378
  87.8 47.5 %collective-permute-start.54 = (bf16[256,1024]{1,0:T(8,128)(2,1)}, bf16[256,1024]{1,0:T(8,128)(2,1)}, u32[]{:S(2)}, u32[]{:S(2)}) collective-permute-start(bf16[256,1024]{1,0:T(8,128)(2,1)} %get-tuple-element.193), channel_id=1, source_target_pairs={{0,1},{1,0},{2,3},{3,2},{4,5},{5,4},{6,7},{7,6},{8,9},{9,8},{10,11... | collective-permute-start | bytes 1572872 | tf_op jit(solution)/shard_map/ppermute | solution.py:378
  90.6 46.2 %collective-permute-start.55 = (bf16[256,1024]{1,0:T(8,128)(2,1)}, bf16[256,1024]{1,0:T(8,128)(2,1)}, u32[]{:S(2)}, u32[]{:S(2)}) collective-permute-start(bf16[256,1024]{1,0:T(8,128)(2,1)} %get-tuple-element.194), channel_id=1, source_target_pairs={{0,2},{1,3},{2,0},{3,1},{4,6},{5,7},{6,4},{7,5},{8,10},{9,11},{10,... | collective-permute-start | bytes 1572872 | tf_op jit(solution)/shard_map/ppermute | solution.py:378
  92.2 45.2 %collective-permute-start.56 = (bf16[256,1024]{1,0:T(8,128)(2,1)}, bf16[256,1024]{1,0:T(8,128)(2,1)}, u32[]{:S(2)}, u32[]{:S(2)}) collective-permute-start(bf16[256,1024]{1,0:T(8,128)(2,1)} %get-tuple-element.192), channel_id=1, source_target_pairs={{0,3},{1,2},{2,1},{3,0},{4,7},{5,6},{6,5},{7,4},{8,11},{9,10},{10,... | collective-permute-start | bytes 1572872 | tf_op jit(solution)/shard_map/ppermute | solution.py:378
  92.3 39.4 %collective-permute-start.10 = (bf16[512,512]{1,0:T(8,128)(2,1)}, bf16[512,512]{1,0:T(8,128)(2,1)}, u32[]{:S(2)}, u32[]{:S(2)}) collective-permute-start(bf16[512,512]{1,0:T(8,128)(2,1)} %pad_maximum_fusion.12), channel_id=1, source_target_pairs={{0,2},{1,3},{2,0},{3,1},{4,6},{5,7},{6,4},{7,5},{8,10},{9,11},{10,... | collective-permute-start | bytes 1572872 | tf_op jit(solution)/shard_map/ppermute | solution.py:378
  97.1 49.5 %collective-permute-start.42 = (bf16[512,512]{0,1:T(8,128)(2,1)}, bf16[512,512]{0,1:T(8,128)(2,1)}, u32[]{:S(2)}, u32[]{:S(2)}) collective-permute-start(bf16[512,512]{0,1:T(8,128)(2,1)} %pad_maximum_fusion.15), channel_id=1, source_target_pairs={{0,2},{1,3},{2,0},{3,1},{4,6},{5,7},{6,4},{7,5},{8,10},{9,11},{10,... | collective-permute-start | bytes 1572872 | tf_op jit(solution)/shard_map/ppermute | solution.py:378
  131.7 17.8 %collective-permute-start.30 = (bf16[512,512]{0,1:T(8,128)(2,1)}, bf16[512,512]{0,1:T(8,128)(2,1)}, u32[]{:S(2)}, u32[]{:S(2)}) collective-permute-start(bf16[512,512]{0,1:T(8,128)(2,1)} %pad_maximum_fusion.13), channel_id=1, source_target_pairs={{0,4},{4,0},{8,12},{12,8},{16,20},{20,16},{24,28},{28,24},{1,5},{5... | collective-permute-start | bytes 1572872 | tf_op jit(solution)/shard_map/ppermute | solution.py:374
  135.3 18.8 %collective-permute-start.18 = (bf16[1024,256]{1,0:T(8,128)(2,1)S(1)}, bf16[1024,256]{1,0:T(8,128)(2,1)}, u32[]{:S(2)}, u32[]{:S(2)}) collective-permute-start(bf16[1024,256]{1,0:T(8,128)(2,1)S(1)} %constant_dynamic-update-slice_fusion), channel_id=1, source_target_pairs={{0,2},{1,3},{2,0},{3,1},{4,6},{5,7},{6,4},{7,5},{8,10},{9,11},{10,... | collective-permute-start | bytes 1572872 | tf_op jit(solution)/shard_map/ppermute | solution.py:378
  136.8 28.5 %collective-permute-start.23 = (bf16[1024,256]{0,1:T(8,128)(2,1)S(1)}, bf16[1024,256]{0,1:T(8,128)(2,1)}, u32[]{:S(2)}, u32[]{:S(2)}) collective-permute-start(bf16[1024,256]{0,1:T(8,128)(2,1)S(1)} %constant_dynamic-update-slice_fusion.5), channel_id=1, source_target_pairs={{0,2},{1,3},{2,0},{3,1},{4,6},{5,7},{6,4},{7,5},{8,10},{9,11},{10,... | collective-permute-start | bytes 1572872 | tf_op jit(solution)/shard_map/ppermute | solution.py:378
  137.4 31.9 %collective-permute-start.11 = (bf16[512,1024]{1,0:T(8,128)(2,1)}, bf16[512,1024]{1,0:T(8,128)(2,1)}, u32[]{:S(2)}, u32[]{:S(2)}) collective-permute-start(bf16[512,1024]{1,0:T(8,128)(2,1)} %pad_maximum_fusion.7), channel_id=1, source_target_pairs={{0,4},{4,0},{8,12},{12,8},{16,20},{20,16},{24,28},{28,24},{1,5},{5... | collective-permute-start | bytes 3145736 | tf_op jit(solution)/shard_map/ppermute | solution.py:374
  147.9 42.1 %collective-permute-start.43 = (bf16[512,1024]{0,1:T(8,128)(2,1)S(1)}, bf16[512,1024]{0,1:T(8,128)(2,1)S(1)}, u32[]{:S(2)}, u32[]{:S(2)}) collective-permute-start(bf16[512,1024]{0,1:T(8,128)(2,1)S(1)} %pad_maximum_fusion.10), channel_id=1, source_target_pairs={{0,4},{4,0},{8,12},{12,8},{16,20},{20,16},{24,28},{28,24},{1,5},{5... | collective-permute-start | bytes 3145736 | tf_op jit(solution)/shard_map/ppermute | solution.py:374
  150.6 42.1 %collective-permute-start.31 = (bf16[1024,512]{0,1:T(8,128)(2,1)S(1)}, bf16[1024,512]{0,1:T(8,128)(2,1)S(1)}, u32[]{:S(2)}, u32[]{:S(2)}) collective-permute-start(bf16[1024,512]{0,1:T(8,128)(2,1)S(1)} %constant_dynamic-update-slice_fusion.10), channel_id=1, source_target_pairs={{0,2},{1,3},{2,0},{3,1},{4,6},{5,7},{6,4},{7,5},{8,10},{9,11},{10,... | collective-permute-start | bytes 3145736 | tf_op jit(solution)/shard_map/ppermute | solution.py:378
  155.3 56.4 %collective-permute-start.25 = (bf16[1024,512]{1,0:T(8,128)(2,1)S(1)}, bf16[1024,512]{1,0:T(8,128)(2,1)S(1)}, u32[]{:S(2)}, u32[]{:S(2)}) collective-permute-start(bf16[1024,512]{1,0:T(8,128)(2,1)S(1)} %pad_maximum_fusion.8), channel_id=1, source_target_pairs={{0,1},{1,0},{2,3},{3,2},{4,5},{5,4},{6,7},{7,6},{8,9},{9,8},{10,11... | collective-permute-start | bytes 3145736 | tf_op jit(solution)/shard_map/ppermute | solution.py:378
  166.5 67.3 %collective-permute-start.26 = (bf16[1024,512]{0,1:T(8,128)(2,1)S(1)}, bf16[1024,512]{0,1:T(8,128)(2,1)S(1)}, u32[]{:S(2)}, u32[]{:S(2)}) collective-permute-start(bf16[1024,512]{0,1:T(8,128)(2,1)S(1)} %pad_maximum_fusion.9), channel_id=1, source_target_pairs={{0,1},{1,0},{2,3},{3,2},{4,5},{5,4},{6,7},{7,6},{8,9},{9,8},{10,11... | collective-permute-start | bytes 3145736 | tf_op jit(solution)/shard_map/ppermute | solution.py:378
  171.5 41.5 %collective-permute-start.24 = (bf16[1024,1024]{1,0:T(8,128)(2,1)S(1)}, bf16[1024,1024]{1,0:T(8,128)(2,1)S(1)}, u32[]{:S(2)}, u32[]{:S(2)}) collective-permute-start(bf16[1024,1024]{1,0:T(8,128)(2,1)S(1)} %pad_maximum_fusion), channel_id=1, source_target_pairs={{0,1},{1,0},{2,3},{3,2},{4,5},{5,4},{6,7},{7,6},{8,9},{9,8},{10,11... | collective-permute-start | bytes 6291464 | tf_op jit(solution)/shard_map/ppermute | solution.py:378
  192.6 49.9 %collective-permute-start.49 = (bf16[1024,1024]{0,1:T(8,128)(2,1)S(1)}, bf16[1024,1024]{0,1:T(8,128)(2,1)S(1)}, u32[]{:S(2)}, u32[]{:S(2)}) collective-permute-start(bf16[1024,1024]{0,1:T(8,128)(2,1)S(1)} %pad_maximum_fusion.3), channel_id=1, source_target_pairs={{0,1},{1,0},{2,3},{3,2},{4,5},{5,4},{6,7},{7,6},{8,9},{9,8},{10,11... | collective-permute-start | bytes 6291464 | tf_op jit(solution)/shard_map/ppermute | solution.py:378
  192.9 56.6 %collective-permute-start.37 = (bf16[1024,1024]{0,1:T(8,128)(2,1)S(1)}, bf16[1024,1024]{0,1:T(8,128)(2,1)S(1)}, u32[]{:S(2)}, u32[]{:S(2)}) collective-permute-start(bf16[1024,1024]{0,1:T(8,128)(2,1)S(1)} %pad_maximum_fusion.1), channel_id=1, source_target_pairs={{0,1},{1,0},{2,3},{3,2},{4,5},{5,4},{6,7},{7,6},{8,9},{9,8},{10,11... | collective-permute-start | bytes 6291464 | tf_op jit(solution)/shard_map/ppermute | solution.py:378
  249.4 19.3 %collective-permute-start.96 = (bf16[1024,1024]{0,1:T(8,128)(2,1)S(1)}, bf16[1024,1024]{0,1:T(8,128)(2,1)S(1)}, u32[]{:S(2)}, u32[]{:S(2)}) collective-permute-start(bf16[1024,1024]{0,1:T(8,128)(2,1)S(1)} %convolution_convert_fusion.1), channel_id=1, source_target_pairs={{0,1},{1,0},{2,3},{3,2},{4,5},{5,4},{6,7},{7,6},{8,9},{9,8},{10,11... | collective-permute-start | bytes 6291464 | tf_op jit(solution)/shard_map/ppermute | solution.py:378
  256.2 17.6 %collective-permute-start.90 = (bf16[1024,1024]{0,1:T(8,128)(2,1)S(1)}, bf16[1024,1024]{0,1:T(8,128)(2,1)S(1)}, u32[]{:S(2)}, u32[]{:S(2)}) collective-permute-start(bf16[1024,1024]{0,1:T(8,128)(2,1)S(1)} %convolution_convert_fusion.2), channel_id=1, source_target_pairs={{0,1},{1,0},{2,3},{3,2},{4,5},{5,4},{6,7},{7,6},{8,9},{9,8},{10,11... | collective-permute-start | bytes 6291464 | tf_op jit(solution)/shard_map/ppermute | solution.py:378
  269.8 25.2 %collective-permute-start.97 = (bf16[512,1024]{0,1:T(8,128)(2,1)S(1)}, bf16[512,1024]{0,1:T(8,128)(2,1)S(1)}, u32[]{:S(2)}, u32[]{:S(2)}) collective-permute-start(bf16[512,1024]{0,1:T(8,128)(2,1)S(1)} %slice.493), channel_id=1, source_target_pairs={{0,4},{4,0},{8,12},{12,8},{16,20},{20,16},{24,28},{28,24},{1,5},{5... | collective-permute-start | bytes 3145736 | tf_op jit(solution)/shard_map/ppermute | solution.py:374
  274.9 26.1 %collective-permute-start.91 = (bf16[1024,512]{0,1:T(8,128)(2,1)S(1)}, bf16[1024,512]{0,1:T(8,128)(2,1)S(1)}, u32[]{:S(2)}, u32[]{:S(2)}) collective-permute-start(bf16[1024,512]{0,1:T(8,128)(2,1)S(1)} %slice.485), channel_id=1, source_target_pairs={{0,2},{1,3},{2,0},{3,1},{4,6},{5,7},{6,4},{7,5},{8,10},{9,11},{10,... | collective-permute-start | bytes 3145736 | tf_op jit(solution)/shard_map/ppermute | solution.py:378
  295.4 15.6 %collective-permute-start.98 = (bf16[512,512]{0,1:T(8,128)(2,1)S(1)}, bf16[512,512]{0,1:T(8,128)(2,1)S(1)}, u32[]{:S(2)}, u32[]{:S(2)}) collective-permute-start(bf16[512,512]{0,1:T(8,128)(2,1)S(1)} %slice.495), channel_id=1, source_target_pairs={{0,2},{1,3},{2,0},{3,1},{4,6},{5,7},{6,4},{7,5},{8,10},{9,11},{10,... | collective-permute-start | bytes 1572872 | tf_op jit(solution)/shard_map/ppermute | solution.py:378
  318.6 15.7 %collective-permute-start.94 = (bf16[128,512]{0,1:T(8,128)(2,1)S(1)}, bf16[128,512]{0,1:T(8,128)(2,1)S(1)}, u32[]{:S(2)}, u32[]{:S(2)}) collective-permute-start(bf16[128,512]{0,1:T(8,128)(2,1)S(1)} %get-tuple-element.201), channel_id=1, source_target_pairs={{0,16},{4,20},{8,24},{12,28},{16,0},{20,4},{24,8},{28,12},{1,17},{... | collective-permute-start | bytes 393224 | tf_op jit(solution)/shard_map/ppermute | solution.py:368
  366.7 38.0 %collective-permute-start.48 = (bf16[512,1024]{0,1:T(8,128)(2,1)}, bf16[512,1024]{0,1:T(8,128)(2,1)}, u32[]{:S(2)}, u32[]{:S(2)}) collective-permute-start(bf16[512,1024]{0,1:T(8,128)(2,1)} %pad_maximum_fusion.11), channel_id=1, source_target_pairs={{0,4},{4,0},{8,12},{12,8},{16,20},{20,16},{24,28},{28,24},{1,5},{5... | collective-permute-start | bytes 3145736 | tf_op jit(solution)/shard_map/ppermute | solution.py:374
  372.3 30.3 %collective-permute-start.35 = (bf16[512,512]{0,1:T(8,128)(2,1)S(1)}, bf16[512,512]{0,1:T(8,128)(2,1)S(1)}, u32[]{:S(2)}, u32[]{:S(2)}) collective-permute-start(bf16[512,512]{0,1:T(8,128)(2,1)S(1)} %pad_maximum_fusion.14), channel_id=1, source_target_pairs={{0,4},{4,0},{8,12},{12,8},{16,20},{20,16},{24,28},{28,24},{1,5},{5... | collective-permute-start | bytes 1572872 | tf_op jit(solution)/shard_map/ppermute | solution.py:374
  402.6 23.5 %collective-permute-start.36 = (bf16[1024,512]{0,1:T(8,128)(2,1)S(1)}, bf16[1024,512]{0,1:T(8,128)(2,1)S(1)}, u32[]{:S(2)}, u32[]{:S(2)}) collective-permute-start(bf16[1024,512]{0,1:T(8,128)(2,1)S(1)} %constant_dynamic-update-slice_fusion.15), channel_id=1, source_target_pairs={{0,2},{1,3},{2,0},{3,1},{4,6},{5,7},{6,4},{7,5},{8,10},{9,11},{10,... | collective-permute-start | bytes 3145736 | tf_op jit(solution)/shard_map/ppermute | solution.py:378
  411.5 49.3 %collective-permute-start.50 = (bf16[1024,1024]{0,1:T(8,128)(2,1)}, bf16[1024,1024]{0,1:T(8,128)(2,1)}, u32[]{:S(2)}, u32[]{:S(2)}) collective-permute-start(bf16[1024,1024]{0,1:T(8,128)(2,1)} %pad_maximum_fusion.4), channel_id=1, source_target_pairs={{0,1},{1,0},{2,3},{3,2},{4,5},{5,4},{6,7},{7,6},{8,9},{9,8},{10,11... | collective-permute-start | bytes 6291464 | tf_op jit(solution)/shard_map/ppermute | solution.py:378
  427.6 25.2 %collective-permute-start.38 = (bf16[1024,1024]{0,1:T(8,128)(2,1)}, bf16[1024,1024]{0,1:T(8,128)(2,1)}, u32[]{:S(2)}, u32[]{:S(2)}) collective-permute-start(bf16[1024,1024]{0,1:T(8,128)(2,1)} %pad_maximum_fusion.2), channel_id=1, source_target_pairs={{0,1},{1,0},{2,3},{3,2},{4,5},{5,4},{6,7},{7,6},{8,9},{9,8},{10,11... | collective-permute-start | bytes 6291464 | tf_op jit(solution)/shard_map/ppermute | solution.py:378
  624.7 35.0 %collective-permute-start.72 = (bf16[1024,512]{1,0:T(8,128)(2,1)S(1)}, bf16[1024,512]{1,0:T(8,128)(2,1)S(1)}, u32[]{:S(2)}, u32[]{:S(2)}) collective-permute-start(bf16[1024,512]{1,0:T(8,128)(2,1)S(1)} %copy-done.153), channel_id=1, source_target_pairs={{0,1},{1,0},{2,3},{3,2},{4,5},{5,4},{6,7},{7,6},{8,9},{9,8},{10,11... | collective-permute-start | bytes 3145736 | tf_op jit(solution)/shard_map/ppermute | solution.py:378
  635.0 24.0 %collective-permute-start.53 = (bf16[256,1024]{1,0:T(8,128)(2,1)S(1)}, bf16[256,1024]{1,0:T(8,128)(2,1)S(1)}, u32[]{:S(2)}, u32[]{:S(2)}) collective-permute-start(bf16[256,1024]{1,0:T(8,128)(2,1)S(1)} %get-tuple-element.188), channel_id=1, source_target_pairs={{0,3},{1,2},{2,1},{3,0},{4,7},{5,6},{6,5},{7,4},{8,11},{9,10},{10,... | collective-permute-start | bytes 1572872 | tf_op jit(solution)/shard_map/ppermute | solution.py:378
  635.8 28.2 %collective-permute-start.57 = (bf16[256,1024]{1,0:T(8,128)(2,1)S(1)}, bf16[256,1024]{1,0:T(8,128)(2,1)S(1)}, u32[]{:S(2)}, u32[]{:S(2)}) collective-permute-start(bf16[256,1024]{1,0:T(8,128)(2,1)S(1)} %get-tuple-element.187), channel_id=1, source_target_pairs={{0,1},{1,0},{2,3},{3,2},{4,5},{5,4},{6,7},{7,6},{8,9},{9,8},{10,11... | collective-permute-start | bytes 1572872 | tf_op jit(solution)/shard_map/ppermute | solution.py:378
  637.3 36.1 %collective-permute-start.58 = (bf16[256,1024]{1,0:T(8,128)(2,1)}, bf16[256,1024]{1,0:T(8,128)(2,1)}, u32[]{:S(2)}, u32[]{:S(2)}) collective-permute-start(bf16[256,1024]{1,0:T(8,128)(2,1)} %get-tuple-element.186), channel_id=1, source_target_pairs={{0,2},{1,3},{2,0},{3,1},{4,6},{5,7},{6,4},{7,5},{8,10},{9,11},{10,... | collective-permute-start | bytes 1572872 | tf_op jit(solution)/shard_map/ppermute | solution.py:378
  648.7 32.8 %collective-permute-start.59 = (bf16[256,1024]{1,0:T(8,128)(2,1)}, bf16[256,1024]{1,0:T(8,128)(2,1)}, u32[]{:S(2)}, u32[]{:S(2)}) collective-permute-start(bf16[256,1024]{1,0:T(8,128)(2,1)} %get-tuple-element.185), channel_id=1, source_target_pairs={{0,3},{1,2},{2,1},{3,0},{4,7},{5,6},{6,5},{7,4},{8,11},{9,10},{10,... | collective-permute-start | bytes 1572872 | tf_op jit(solution)/shard_map/ppermute | solution.py:378
  659.0 57.1 %collective-permute-start.84 = (bf16[1024,1024]{0,1:T(8,128)(2,1)}, bf16[1024,1024]{0,1:T(8,128)(2,1)}, u32[]{:S(2)}, u32[]{:S(2)}) collective-permute-start(bf16[1024,1024]{0,1:T(8,128)(2,1)} %convolution_convert_fusion.3), channel_id=1, source_target_pairs={{0,1},{1,0},{2,3},{3,2},{4,5},{5,4},{6,7},{7,6},{8,9},{9,8},{10,11... | collective-permute-start | bytes 6291464 | tf_op jit(solution)/shard_map/ppermute | solution.py:378
  659.7 34.0 %collective-permute-start.67 = (bf16[1024,256]{1,0:T(8,128)(2,1)}, bf16[1024,256]{1,0:T(8,128)(2,1)}, u32[]{:S(2)}, u32[]{:S(2)}) collective-permute-start(bf16[1024,256]{1,0:T(8,128)(2,1)} %slice.453), channel_id=1, source_target_pairs={{0,2},{1,3},{2,0},{3,1},{4,6},{5,7},{6,4},{7,5},{8,10},{9,11},{10,... | collective-permute-start | bytes 1572872 | tf_op jit(solution)/shard_map/ppermute | solution.py:378
  664.7 39.8 %collective-permute-start.73 = (bf16[1024,256]{1,0:T(8,128)(2,1)}, bf16[1024,256]{1,0:T(8,128)(2,1)}, u32[]{:S(2)}, u32[]{:S(2)}) collective-permute-start(bf16[1024,256]{1,0:T(8,128)(2,1)} %slice.461), channel_id=1, source_target_pairs={{0,2},{1,3},{2,0},{3,1},{4,6},{5,7},{6,4},{7,5},{8,10},{9,11},{10,... | collective-permute-start | bytes 1572872 | tf_op jit(solution)/shard_map/ppermute | solution.py:378
  673.4 46.8 %collective-permute-start.60 = (bf16[1024,1024]{0,1:T(8,128)(2,1)}, bf16[1024,1024]{0,1:T(8,128)(2,1)S(1)}, u32[]{:S(2)}, u32[]{:S(2)}) collective-permute-start(bf16[1024,1024]{0,1:T(8,128)(2,1)} %convolution_convert_fusion), channel_id=1, source_target_pairs={{0,1},{1,0},{2,3},{3,2},{4,5},{5,4},{6,7},{7,6},{8,9},{9,8},{10,11... | collective-permute-start | bytes 6291464 | tf_op jit(solution)/shard_map/ppermute | solution.py:378
  681.6 47.6 %collective-permute-start.78 = (bf16[1024,1024]{0,1:T(8,128)(2,1)}, bf16[1024,1024]{0,1:T(8,128)(2,1)}, u32[]{:S(2)}, u32[]{:S(2)}) collective-permute-start(bf16[1024,1024]{0,1:T(8,128)(2,1)} %convolution_convert_fusion.4), channel_id=1, source_target_pairs={{0,1},{1,0},{2,3},{3,2},{4,5},{5,4},{6,7},{7,6},{8,9},{9,8},{10,11... | collective-permute-start | bytes 6291464 | tf_op jit(solution)/shard_map/ppermute | solution.py:378
  707.4 21.0 %collective-permute-start.71 = (bf16[128,256]{1,0:T(8,128)(2,1)S(1)}, bf16[128,256]{1,0:T(8,128)(2,1)S(1)}, u32[]{:S(2)}, u32[]{:S(2)}) collective-permute-start(bf16[128,256]{1,0:T(8,128)(2,1)S(1)} %get-tuple-element.218), channel_id=1, source_target_pairs={{0,24},{4,28},{8,16},{12,20},{16,8},{20,12},{24,0},{28,4},{1,25},{... | collective-permute-start | bytes 196616 | tf_op jit(solution)/shard_map/ppermute | solution.py:368
  713.7 22.4 %collective-permute-start.77 = (bf16[128,256]{1,0:T(8,128)(2,1)S(1)}, bf16[128,256]{1,0:T(8,128)(2,1)S(1)}, u32[]{:S(2)}, u32[]{:S(2)}) collective-permute-start(bf16[128,256]{1,0:T(8,128)(2,1)S(1)} %get-tuple-element.215), channel_id=1, source_target_pairs={{0,24},{4,28},{8,16},{12,20},{16,8},{20,12},{24,0},{28,4},{1,25},{... | collective-permute-start | bytes 196616 | tf_op jit(solution)/shard_map/ppermute | solution.py:368
  716.1 20.9 %collective-permute-start.76 = (bf16[128,256]{1,0:T(8,128)(2,1)S(1)}, bf16[128,256]{1,0:T(8,128)(2,1)S(1)}, u32[]{:S(2)}, u32[]{:S(2)}) collective-permute-start(bf16[128,256]{1,0:T(8,128)(2,1)S(1)} %get-tuple-element.216), channel_id=1, source_target_pairs={{0,16},{4,20},{8,24},{12,28},{16,0},{20,4},{24,8},{28,12},{1,17},{... | collective-permute-start | bytes 196616 | tf_op jit(solution)/shard_map/ppermute | solution.py:368
  721.6 17.4 %collective-permute-start.75 = (bf16[128,256]{1,0:T(8,128)(2,1)S(1)}, bf16[128,256]{1,0:T(8,128)(2,1)S(1)}, u32[]{:S(2)}, u32[]{:S(2)}) collective-permute-start(bf16[128,256]{1,0:T(8,128)(2,1)S(1)} %get-tuple-element.214), channel_id=1, source_target_pairs={{0,8},{4,12},{8,0},{12,4},{16,24},{20,28},{24,16},{28,20},{1,9},{5... | collective-permute-start | bytes 196616 | tf_op jit(solution)/shard_map/ppermute | solution.py:368
  728.3 26.4 %collective-permute-start.61 = (bf16[512,1024]{0,1:T(8,128)(2,1)}, bf16[512,1024]{0,1:T(8,128)(2,1)}, u32[]{:S(2)}, u32[]{:S(2)}) collective-permute-start(bf16[512,1024]{0,1:T(8,128)(2,1)} %slice.445), channel_id=1, source_target_pairs={{0,4},{4,0},{8,12},{12,8},{16,20},{20,16},{24,28},{28,24},{1,5},{5... | collective-permute-start | bytes 3145736 | tf_op jit(solution)/shard_map/ppermute | solution.py:374
  729.2 44.8 %collective-permute-start.85 = (bf16[512,1024]{0,1:T(8,128)(2,1)}, bf16[512,1024]{0,1:T(8,128)(2,1)S(1)}, u32[]{:S(2)}, u32[]{:S(2)}) collective-permute-start(bf16[512,1024]{0,1:T(8,128)(2,1)} %slice.477), channel_id=1, source_target_pairs={{0,4},{4,0},{8,12},{12,8},{16,20},{20,16},{24,28},{28,24},{1,5},{5... | collective-permute-start | bytes 3145736 | tf_op jit(solution)/shard_map/ppermute | solution.py:374
  739.0 36.5 %collective-permute-start.79 = (bf16[1024,512]{0,1:T(8,128)(2,1)}, bf16[1024,512]{0,1:T(8,128)(2,1)}, u32[]{:S(2)}, u32[]{:S(2)}) collective-permute-start(bf16[1024,512]{0,1:T(8,128)(2,1)} %slice.469), channel_id=1, source_target_pairs={{0,2},{1,3},{2,0},{3,1},{4,6},{5,7},{6,4},{7,5},{8,10},{9,11},{10,... | collective-permute-start | bytes 3145736 | tf_op jit(solution)/shard_map/ppermute | solution.py:378
  756.4 21.7 %collective-permute-start.62 = (bf16[512,512]{0,1:T(8,128)(2,1)S(1)}, bf16[512,512]{0,1:T(8,128)(2,1)S(1)}, u32[]{:S(2)}, u32[]{:S(2)}) collective-permute-start(bf16[512,512]{0,1:T(8,128)(2,1)S(1)} %slice.447), channel_id=1, source_target_pairs={{0,2},{1,3},{2,0},{3,1},{4,6},{5,7},{6,4},{7,5},{8,10},{9,11},{10,... | collective-permute-start | bytes 1572872 | tf_op jit(solution)/shard_map/ppermute | solution.py:378
  780.6 18.3 %collective-permute-start.64 = (bf16[128,512]{0,1:T(8,128)(2,1)S(1)}, bf16[128,512]{0,1:T(8,128)(2,1)S(1)}, u32[]{:S(2)}, u32[]{:S(2)}) collective-permute-start(bf16[128,512]{0,1:T(8,128)(2,1)S(1)} %get-tuple-element.213), channel_id=1, source_target_pairs={{0,16},{4,20},{8,24},{12,28},{16,0},{20,4},{24,8},{28,12},{1,17},{... | collective-permute-start | bytes 393224 | tf_op jit(solution)/shard_map/ppermute | solution.py:368
  780.6 20.6 %collective-permute-start.63 = (bf16[128,512]{0,1:T(8,128)(2,1)S(1)}, bf16[128,512]{0,1:T(8,128)(2,1)S(1)}, u32[]{:S(2)}, u32[]{:S(2)}) collective-permute-start(bf16[128,512]{0,1:T(8,128)(2,1)S(1)} %get-tuple-element.211), channel_id=1, source_target_pairs={{0,8},{4,12},{8,0},{12,4},{16,24},{20,28},{24,16},{28,20},{1,9},{5... | collective-permute-start | bytes 393224 | tf_op jit(solution)/shard_map/ppermute | solution.py:368
  785.5 15.8 %collective-permute-start.89 = (bf16[128,512]{0,1:T(8,128)(2,1)S(1)}, bf16[128,512]{0,1:T(8,128)(2,1)S(1)}, u32[]{:S(2)}, u32[]{:S(2)}) collective-permute-start(bf16[128,512]{0,1:T(8,128)(2,1)S(1)} %get-tuple-element.209), channel_id=1, source_target_pairs={{0,24},{4,28},{8,16},{12,20},{16,8},{20,12},{24,0},{28,4},{1,25},{... | collective-permute-start | bytes 393224 | tf_op jit(solution)/shard_map/ppermute | solution.py:368
  787.9 19.5 %collective-permute-start.88 = (bf16[128,512]{0,1:T(8,128)(2,1)S(1)}, bf16[128,512]{0,1:T(8,128)(2,1)S(1)}, u32[]{:S(2)}, u32[]{:S(2)}) collective-permute-start(bf16[128,512]{0,1:T(8,128)(2,1)S(1)} %get-tuple-element.210), channel_id=1, source_target_pairs={{0,16},{4,20},{8,24},{12,28},{16,0},{20,4},{24,8},{28,12},{1,17},{... | collective-permute-start | bytes 393224 | tf_op jit(solution)/shard_map/ppermute | solution.py:368
  790.1 17.3 %collective-permute-start.87 = (bf16[128,512]{0,1:T(8,128)(2,1)S(1)}, bf16[128,512]{0,1:T(8,128)(2,1)S(1)}, u32[]{:S(2)}, u32[]{:S(2)}) collective-permute-start(bf16[128,512]{0,1:T(8,128)(2,1)S(1)} %get-tuple-element.208), channel_id=1, source_target_pairs={{0,8},{4,12},{8,0},{12,4},{16,24},{20,28},{24,16},{28,20},{1,9},{5... | collective-permute-start | bytes 393224 | tf_op jit(solution)/shard_map/ppermute | solution.py:368
  (215 other events, 2567.9 us)

commit v2 on v1

--- a/solution.py
+++ b/solution.py
@@ -378,46 +378,98 @@
     return lax.ppermute(part, "mp", [(each, each ^ step) for each in range(MP)])
 
 
-def gather_rows_z(shard):
-    return jnp.concatenate([shard] + [swap_z(shard, step) for step in range(1, ZS)], 0)
-
-
-def gather_weight(shard, y_first):
-    rows = gather_rows_z(shard)
-    if y_first:
-        rows = jnp.concatenate([rows, swap_y(rows)], 0)
-        rows = jnp.concatenate([rows, swap_mp(rows, 2)], 1)
-    else:
-        rows = jnp.concatenate([rows, swap_mp(rows, 2)], 1)
-        rows = jnp.concatenate([rows, swap_y(rows)], 0)
-    return (rows, swap_mp(rows, 1))
+class Chain:
+    def __init__(self, steps, *args):
+        self.own = None
+        self.result = None
+        self.steps = steps(self, *args)
+        self.flight = next(self.steps)
+
+    def land(self, arrived):
+        try:
+            self.flight = self.steps.send(arrived)
+        except StopIteration as end:
+            self.flight = None
+            self.result = end.value
+
+
+def meet(values, *chains):
+    values, flights = lax.optimization_barrier((values, [each.flight for each in chains]))
+    for each, flight in zip(chains, flights):
+        each.land(flight)
+    return values
+
+
+def gather_steps(chain, shard, order):
+    rows = shard
+    for axis in order:
+        if axis == "z":
+            arrived = yield [swap_z(rows, step) for step in range(1, ZS)]
+            rows = jnp.concatenate([rows] + arrived, 0)
+        elif axis == "y":
+            arrived = yield [swap_y(rows)]
+            rows = jnp.concatenate([rows] + arrived, 0)
+        else:
+            arrived = yield [swap_mp(rows, 2)]
+            rows = jnp.concatenate([rows] + arrived, 1)
+    chain.own = rows
+    arrived = yield [swap_mp(rows, 1)]
+    return (rows, arrived[0])
 
 
 def add_low(first, second):
     return (first.astype(F32) + second.astype(F32)).astype(BF)
 
 
-def reduce_x(total):
-    width = total.shape[1] // 2
-    return add_low(total[:, :width], swap_mp(total[:, width:], 2))
-
-
-def reduce_y(total):
-    rows = total.shape[0] // 2
-    return add_low(total[:rows], swap_y(total[rows:]))
-
-
-def reduce_weight(own_part, other_part, x_first):
-    total = add_low(own_part, swap_mp(other_part, 1))
-    if x_first:
-        total = reduce_y(reduce_x(total))
-    else:
-        total = reduce_x(reduce_y(total))
-    rows = total.shape[0] // ZS
-    result = total[:rows].astype(F32)
-    for step in range(1, ZS):
-        result = result + swap_z(total[step * rows : (step + 1) * rows], step).astype(F32)
-    return result
+def reduce_steps(chain, other_part, order):
+    arrived = yield [swap_mp(other_part, 1)]
+    total = add_low(chain.own, arrived[0])
+    for axis in order:
+        rows, width = total.shape[-2:]
+        if axis == "z":
+            rows = rows // ZS
+            arrived = yield [
+                swap_z(total[..., step * rows : (step + 1) * rows, :], step) for step in range(1, ZS)
+            ]
+            total = total[..., :rows, :].astype(F32)
+            for each in arrived:
+                total = total + each.astype(F32)
+        elif axis == "y":
+            arrived = yield [swap_y(total[..., rows // 2 :, :])]
+            total = add_low(total[..., : rows // 2, :], arrived[0])
+        else:
+            arrived = yield [swap_mp(total[..., width // 2 :], 2)]
+            total = add_low(total[..., : width // 2], arrived[0])
+    return total
+
+
+def mp_steps(chain, parts):
+    arrived = yield [swap_mp(part, step + 1) for step, part in enumerate(parts)]
+    return arrived
+
+
+def small_steps(chain, shard, vector_size):
+    arrived = yield [swap_z(shard, step) for step in range(1, ZS)]
+    rows = jnp.concatenate([shard] + arrived, 0)
+    arrived = yield [swap_y(rows)]
+    rows = jnp.concatenate([rows] + arrived, 0)
+    arrived = yield [swap_mp(rows[:, vector_size:], step) for step in range(1, MP)]
+    return (rows[:, :vector_size], jnp.stack([rows[:, vector_size:]] + arrived, 0))
+
+
+def small_reduce_steps(chain, vector_part, bias_part):
+    arrived = yield [swap_mp(vector_part, 1), swap_mp(bias_part[1], 1), swap_mp(bias_part[3], 1)]
+    vector_part = vector_part + arrived[0]
+    even, odd = (bias_part[0] + arrived[1], bias_part[2] + arrived[2])
+    arrived = yield [swap_mp(vector_part, 2), swap_mp(odd, 2)]
+    total = jnp.concatenate([vector_part + arrived[0], even + arrived[1]], 1)
+    arrived = yield [swap_y(total[ZS:])]
+    total = total[:ZS] + arrived[0]
+    arrived = yield [swap_z(total[step], step) for step in range(1, ZS)]
+    total = total[0]
+    for each in arrived:
+        total = total + each
+    return total
 
 
 def assemble_kernel(place_ref, own_ref, *refs):
@@ -501,7 +553,7 @@
 
 
 def attend_back_kernel(
-    block_rows, q_ref, k_ref, v_ref, g_ref, lse_ref, dq_ref, dk_ref, dv_ref, dk_acc, dv_acc
+    block_rows, q_ref, k_ref, v_ref, g_ref, lse_ref, out_ref, dk_acc, dv_acc
 ):
     masks = head_masks(LANES)
     key_rows = k_ref[...]
@@ -532,31 +584,30 @@
             grad_query = query_part if head == 0 else grad_query + query_part
             grad_keys = key_part if head == 0 else grad_keys + key_part
             grad_values = value_part if head == 0 else grad_values + value_part
-        dq_ref[rows, :] = (grad_query * factor).astype(BF)
+        out_ref[0, rows, :] = (grad_query * factor).astype(BF)
         if block == 0:
             dk_acc[...] = grad_keys
             dv_acc[...] = grad_values
         else:
             dk_acc[...] += grad_keys
             dv_acc[...] += grad_values
-    dk_ref[...] = dk_acc[...].astype(BF)
-    dv_ref[...] = dv_acc[...].astype(BF)
-
-
-def pair_spec(rows, first):
-    kinds, kind = first
-    return pl.BlockSpec((rows, LANES), lambda p: (0, (p // 2) * (2 * kinds) + 2 * kind + p % 2))
-
-
-def attend(query_keys, values):
+    out_ref[1] = dk_acc[...].astype(BF)
+    out_ref[2] = dv_acc[...].astype(BF)
+
+
+def pair_spec(rows):
+    return pl.BlockSpec((rows, LANES), lambda p: (0, p))
+
+
+def attend(queries, key_rows, values):
     rows, width = values.shape
     pairs = width // LANES
     scores_size = rows * rows * 2 * pairs
     return pl.pallas_call(
         functools.partial(attend_kernel, 256),
         grid=(pairs,),
-        in_specs=[pair_spec(rows, (2, 0)), pair_spec(rows, (2, 1)), pair_spec(rows, (1, 0))],
-        out_specs=[pair_spec(rows, (1, 0)), pl.BlockSpec((1, 8, rows), lambda p: (p, 0, 0))],
+        in_specs=[pair_spec(rows)] * 3,
+        out_specs=[pair_spec(rows), pl.BlockSpec((1, 8, rows), lambda p: (p, 0, 0))],
         out_shape=[
             jax.ShapeDtypeStruct((rows, width), BF),
             jax.ShapeDtypeStruct((pairs, 8, rows), F32),
@@ -566,33 +617,26 @@
             flops=scores_size * 2 * 512, bytes_accessed=rows * width * 8, transcendentals=scores_size
         ),
         name="attend",
-    )(query_keys, query_keys, values)
-
-
-def attend_back(query_keys, values, grad_blended, log_total):
+    )(queries, key_rows, values)
+
+
+def attend_back(queries, key_rows, values, grad_blended, log_total):
     rows, width = values.shape
     pairs = width // LANES
     scores_size = rows * rows * 2 * pairs
-    single = pair_spec(rows, (1, 0))
     return pl.pallas_call(
         functools.partial(attend_back_kernel, 256),
         grid=(pairs,),
-        in_specs=[
-            pair_spec(rows, (2, 0)),
-            pair_spec(rows, (2, 1)),
-            single,
-            single,
-            pl.BlockSpec((1, 8, rows), lambda p: (p, 0, 0)),
-        ],
-        out_specs=[single] * 3,
-        out_shape=[jax.ShapeDtypeStruct((rows, width), BF)] * 3,
+        in_specs=[pair_spec(rows)] * 4 + [pl.BlockSpec((1, 8, rows), lambda p: (p, 0, 0))],
+        out_specs=pl.BlockSpec((3, rows, LANES), lambda p: (0, 0, p)),
+        out_shape=jax.ShapeDtypeStruct((3, rows, width), BF),
         scratch_shapes=[pltpu.VMEM((rows, LANES), F32)] * 2,
         compiler_params=pltpu.CompilerParams(vmem_limit_bytes=32 * 2**20),
         cost_estimate=pl.CostEstimate(
             flops=scores_size * 2 * 1280, bytes_accessed=rows * width * 14, transcendentals=scores_size
         ),
         name="attend_back",
-    )(query_keys, query_keys, values, grad_blended, log_total)
+    )(queries, key_rows, values, grad_blended, log_total)
 
 
 def dot_nn(left, right):
@@ -651,190 +695,234 @@
     dp_at = lax.axis_index("dp")
     mp_at = lax.axis_index("mp")
     units = up_weight.shape[1]
+    half_units = units // 2
     block_width = qkv_weight.shape[2]
     depth = qkv_weight.shape[1]
     bias_width = head_biases.shape[1]
     chunk_rows, width = tokens.shape[2:]
     order = [((zk * YS) + yk) for yk in range(YS) for zk in range(ZS)]
-    places = [dp_at ^ each for each in order]
-    place = jnp.stack(places + [mp_at]).astype(jnp.int32)
+    place = jnp.stack([dp_at ^ each for each in order] + [mp_at]).astype(jnp.int32)
+    cores = (0, 1)
 
     def fetch_image(array):
         chunks = array[:, 0]
-        parts = [
-            swap_mp(lax.dynamic_index_in_dim(chunks, mp_at ^ step, 0, keepdims=False), step)
-            for step in range(1, MP)
-        ]
-        return assemble_image(place, chunks, parts)
-
-    small = jnp.concatenate(
+        return Chain(
+            mp_steps,
+            [
+                lax.dynamic_index_in_dim(chunks, mp_at ^ step, 0, keepdims=False)
+                for step in range(1, MP)
+            ],
+        )
+
+    def send_back(array):
+        low = array.astype(BF)
+        return Chain(
+            mp_steps, [low[step * chunk_rows : (step + 1) * chunk_rows] for step in range(1, MP)]
+        )
+
+    small_shard = jnp.concatenate(
         [vectors.astype(BF).reshape(-1), head_biases.astype(BF).reshape(-1)]
     ).reshape(1, -1)
     vector_size = vectors.size
-    small = gather_rows_z(small)
-    small = jnp.concatenate([small, swap_y(small)], 0)
-    vector_full = (
-        small[:, :vector_size].reshape(DP, vectors.shape[0], LANES).transpose(1, 0, 2)
-    ).reshape(vectors.shape[0], width).astype(F32)
-    bias_small = small[:, vector_size:]
-    bias_small = jnp.stack([bias_small, swap_mp(bias_small, 2)], 0)
-    bias_small = jnp.stack([bias_small, swap_mp(bias_small, 1)], 0)
-    back_places = jnp.stack([((each ^ dp_at) & 1) * ZS + ((each ^ dp_at) >> 1) for each in range(DP)])
-    bias_rows = jnp.take(bias_small, back_places, axis=2).reshape(2, 2, DP, -1, bias_width)
-    bias_full = bias_rows.transpose(0, 3, 1, 2, 4).reshape(2, head_biases.shape[0], 2, block_width)
-    bias_full = bias_full.astype(F32)
-
-    inputs = fetch_image(tokens)
     qkv_low = qkv_weight.astype(BF)
     up_low = up_weight.astype(BF)
-    half_units = units // 2
     down_low = down_weight.transpose(2, 0, 1).astype(BF)
-    w_qk = gather_weight(jnp.concatenate([qkv_low[0], qkv_low[1]], 1), False)
-    w_v = gather_weight(qkv_low[2], True)
-    w_out = gather_weight(out_weight.T.astype(BF), True)
-    w_up = [
-        gather_weight(up_low[:, at : at + half_units].reshape(depth, -1), at == 0)
-        for at in (0, half_units)
-    ]
-    w_down = [
-        gather_weight(down_low[:, at : at + half_units].reshape(depth, -1), at == 0)
-        for at in (0, half_units)
-    ]
-    cores = (0, 1)
+    out_low = out_weight.T.astype(BF)
+    up_shards = [up_low[:, at : at + half_units].reshape(depth, -1) for at in (0, half_units)]
+    down_shards = [down_low[:, at : at + half_units].reshape(depth, -1) for at in (0, half_units)]
+
+    small = Chain(small_steps, small_shard, vector_size)
+    get_q = Chain(gather_steps, qkv_low[0], "zxy")
+    get_k = Chain(gather_steps, qkv_low[1], "zxy")
+    get_v = Chain(gather_steps, qkv_low[2], "zyx")
+    fetch_tokens = fetch_image(tokens)
+    out_low, up_shards, down_shards = meet((out_low, up_shards, down_shards), small, get_q, get_k, get_v)
+    get_out = Chain(gather_steps, out_low, "zyx")
+    up_shards, down_shards = meet((up_shards, down_shards), small, get_q, get_k, get_v, get_out)
+    get_up = [Chain(gather_steps, up_shards[0], "zxy"), None]
+    tokens, down_shards, up_shards = meet(
+        (tokens, down_shards, up_shards), small, fetch_tokens, get_k, get_q
+    )
+    get_up[1] = Chain(gather_steps, up_shards[1], "zxy")
+
+    vector_full, bias_small = small.result
+    vector_full = vector_full.reshape(DP, vectors.shape[0], LANES).transpose(1, 0, 2)
+    vector_full = vector_full.reshape(vectors.shape[0], width).astype(F32)
+    back_places = jnp.stack([((each ^ dp_at) & 1) * ZS + ((each ^ dp_at) >> 1) for each in range(DP)])
+    bias_rows = jnp.take(bias_small, back_places, axis=1).reshape(2, 2, DP, -1, bias_width)
+    bias_full = bias_rows.transpose(1, 3, 0, 2, 4).reshape(2, head_biases.shape[0], 2, block_width)
+    bias_full = bias_full.astype(F32)
     gain_one, shift_one, out_bias, scale_one, gain_two, shift_two, down_bias, scale_two = vector_full
 
-    base = inputs.astype(F32)
+    base = assemble_image(place, tokens[:, 0], fetch_tokens.result).astype(F32)
     normal_one, spread_one = norm_parts(base)
     normed_one = (normal_one * gain_one + shift_one).astype(BF)
-    query_keys, values, blended, log_total = ([], [], [], [])
-    for core in cores:
-        query_bias = jnp.stack([bias_full[core, 0], jnp.zeros_like(bias_full[core, 0])], 1).reshape(-1)
-        query_keys.append((dot_nn(normed_one, w_qk[core]) + query_bias).astype(BF))
-        values.append((dot_nn(normed_one, w_v[core]) + bias_full[core, 1].reshape(-1)).astype(BF))
-    for core in cores:
-        part, part_total = attend(query_keys[core], values[core])
-        blended.append(part)
-        log_total.append(part_total)
+    normed_one = meet(normed_one, get_v, get_up[0], get_out)
+
+    def project(core, weights):
+        w_q, w_k, w_v = weights
+        return (
+            (dot_nn(normed_one, w_q) + bias_full[core, 0].reshape(-1)).astype(BF),
+            dot_nn(normed_one, w_k).astype(BF),
+            (dot_nn(normed_one, w_v) + bias_full[core, 1].reshape(-1)).astype(BF),
+        )
+
+    heads, blended, log_total = ([None, None], [None, None], [None, None])
+    heads[0] = project(0, (get_q.own, get_k.own, get_v.own))
+    heads[0] = meet(heads[0], get_q, get_k, get_v, get_up[1])
+    blended[0], log_total[0] = attend(*heads[0])
+    blended[0], normed_one, down_shards, cotangent = meet(
+        (blended[0], normed_one, down_shards, cotangent), get_up[0], get_out
+    )
+    get_down = [Chain(gather_steps, down_shards[0], "zxy"), None]
+    heads[1] = project(1, (get_q.result[1], get_k.result[1], get_v.result[1]))
+    blended[1], log_total[1] = attend(*heads[1])
+    blended, down_shards = meet((blended, down_shards), get_up[0], get_up[1], get_out, get_down[0])
+    get_down[1] = Chain(gather_steps, down_shards[1], "zxy")
+    w_out = get_out.result
     branch_one = dot_nt(blended[0], w_out[0]) + dot_nt(blended[1], w_out[1]) + out_bias
     hidden = base + scale_one * branch_one
     normal_two, spread_two = norm_parts(hidden)
     normed_two = (normal_two * gain_two + shift_two).astype(BF)
-    parts = [(half, core) for half in (0, 1) for core in cores]
+    normed_two, cotangent = meet(
+        (normed_two, cotangent), get_up[0], get_up[1], get_down[0], get_down[1]
+    )
+    fetch_cotangent = fetch_image(cotangent)
+    w_up = [get_up[0].result, None]
     activ, slope = ({}, {})
+
+    def expand(half, core):
+        rows = bias_full[core, 2 + half * half_units : 2 + (half + 1) * half_units]
+        pre_act = dot_nn(normed_two, w_up[half][core]) + rows.transpose(1, 0, 2).reshape(-1)
+        activ[half, core], slope[half, core] = gelu_pair(pre_act)
+
+    expand(0, 0)
+    expand(0, 1)
+    activ, normed_two, slope = meet((activ, normed_two, slope), get_up[1], get_down[0])
+    w_up[1] = get_up[1].result
+    expand(1, 0)
+    expand(1, 1)
+    activ, slope, cotangent = meet(
+        (activ, slope, cotangent), get_down[0], get_down[1], fetch_cotangent
+    )
+
+    grad_out = assemble_image(place, cotangent[:, 0], fetch_cotangent.result).astype(F32)
+    grad_branch = (grad_out * scale_two).astype(BF)
+    sum_down, sum_up = ([None, None], [None, None])
+
+    def grads_down(half):
+        sum_down[half] = Chain(reduce_steps, dot_tn(grad_branch, activ[half, 1]).astype(BF), "yxz")
+        sum_down[half].own = dot_tn(grad_branch, activ[half, 0]).astype(BF)
+
+    grads_down(0)
+    grad_branch, activ = meet((grad_branch, activ), sum_down[0], get_down[1])
+    grads_down(1)
+    activ = meet(activ, get_down[1])
+    w_down = [get_down[0].result, get_down[1].result]
     branch_two = down_bias
-    for half, core in parts:
-        rows = bias_full[core, 2 + half * half_units : 2 + (half + 1) * half_units]
-        unit_bias = rows.transpose(1, 0, 2).reshape(-1)
-        pre_act = dot_nn(normed_two, w_up[half][core]) + unit_bias
-        activ[half, core], slope[half, core] = gelu_pair(pre_act)
-        branch_two = branch_two + dot_nt(activ[half, core], w_down[half][core])
+    for half in (0, 1):
+        for core in cores:
+            branch_two = branch_two + dot_nt(activ[half, core], w_down[half][core])
     output = (hidden + scale_two * branch_two).astype(BF)
-
-    def send_back(array, dtype):
-        low = array.astype(BF)
-        back = [
-            swap_mp(low[step * chunk_rows : (step + 1) * chunk_rows], step) for step in range(1, MP)
-        ]
-        return spread_image(place, array[:chunk_rows], back, dtype)[:, None]
-
-    layer_output = send_back(output, BF)
-
-    grad_out = fetch_image(cotangent).astype(F32)
-    grad_scale_two = jnp.sum(grad_out * branch_two, 0)
-    grad_down_bias = jnp.sum(grad_out, 0) * scale_two
-    grad_branch = (grad_out * scale_two).astype(BF)
-    sums = {}
-    for half in (0, 1):
-        own, other = [dot_tn(grad_branch, activ[half, core]).astype(BF) for core in cores]
-        sums["down", half] = reduce_weight(own, other, half == 0)
+    grad_branch, output, normed_two = meet((grad_branch, output, normed_two), sum_down[1])
+    send_output = send_back(output)
     grad_pre = {}
+
+    def grads_up(half):
+        for core in (1, 0):
+            grad_activ = dot_nn(grad_branch, w_down[half][core])
+            grad_pre[half, core] = (grad_activ * slope[half, core].astype(F32)).astype(BF)
+        sum_up[half] = Chain(reduce_steps, dot_tn(normed_two, grad_pre[half, 1]).astype(BF), "yxz")
+        sum_up[half].own = dot_tn(normed_two, grad_pre[half, 0]).astype(BF)
+
+    grads_up(0)
+    grad_branch, normed_two, grad_pre = meet((grad_branch, normed_two, grad_pre), sum_down[0], sum_up[0])
+    grads_up(1)
     grad_normed_two = 0.0
     for half in (0, 1):
         for core in cores:
-            grad_activ = dot_nn(grad_branch, w_down[half][core])
-            grad_pre[half, core] = (grad_activ * slope[half, core].astype(F32)).astype(BF)
-        own, other = [dot_tn(normed_two, grad_pre[half, core]).astype(BF) for core in cores]
-        sums["up", half] = reduce_weight(own, other, half == 0)
-        for core in cores:
             grad_normed_two = grad_normed_two + dot_nt(grad_pre[half, core], w_up[half][core])
-    grad_unit_bias = {key: jnp.sum(grad_pre[key].astype(F32), 0) for key in parts}
     grad_hidden, grad_gain_two, grad_shift_two = norm_back(
         grad_normed_two, normal_two, spread_two, gain_two
     )
     grad_hidden = grad_out + grad_hidden
-    grad_scale_one = jnp.sum(grad_hidden * branch_one, 0)
-    grad_out_bias = jnp.sum(grad_hidden, 0) * scale_one
     grad_projected = (grad_hidden * scale_one).astype(BF)
-    own, other = [dot_tn(grad_projected, blended[core]).astype(BF) for core in cores]
-    sums["out"] = reduce_weight(own, other, True)
-    grad_qk, grad_v = ([], [])
-    for core in cores:
+    grad_projected = meet(
+        grad_projected, sum_down[0], sum_down[1], sum_up[0], sum_up[1], send_output
+    )
+    sum_out = Chain(reduce_steps, dot_tn(grad_projected, blended[1]).astype(BF), "xyz")
+    sum_out.own = dot_tn(grad_projected, blended[0]).astype(BF)
+    sums_qkv = None
+    grad_heads = [None, None]
+
+    def back_heads(core):
         grad_blended = dot_nn(grad_projected, w_out[core]).astype(BF)
-        grad_query, grad_key, grad_value = attend_back(
-            query_keys[core], values[core], grad_blended, log_total[core]
-        )
-        pair_shape = (grad_query.shape[0], 2, -1)
-        stacked = jnp.stack([grad_query.reshape(pair_shape), grad_key.reshape(pair_shape)], 2)
-        grad_qk.append(stacked.reshape(grad_query.shape[0], -1))
-        grad_v.append(grad_value)
-    own, other = [dot_tn(normed_one, grad_qk[core]).astype(BF) for core in cores]
-    sums["qk"] = reduce_weight(own, other, False)
-    own, other = [dot_tn(normed_one, grad_v[core]).astype(BF) for core in cores]
-    sums["v"] = reduce_weight(own, other, True)
+        grad_heads[core] = attend_back(*heads[core], grad_blended, log_total[core])
+        return jnp.einsum(
+            "sd,tse->tde", normed_one, grad_heads[core], preferred_element_type=F32
+        ).astype(BF)
+
+    grad_other = back_heads(1)
+    grad_other, grad_projected = meet(
+        (grad_other, grad_projected), sum_down[0], sum_down[1], sum_up[0], sum_up[1], sum_out
+    )
+    sum_qkv = Chain(reduce_steps, grad_other, "yxz")
+    sum_qkv.own = back_heads(0)
+    grad_heads, normed_one = meet((grad_heads, normed_one), sum_qkv, sum_up[0], sum_up[1], sum_out, sum_down[1])
+    weights = [[each.own for each in (get_q, get_k, get_v)], [each.result[1] for each in (get_q, get_k, get_v)]]
     grad_normed_one = 0.0
     for core in cores:
-        grad_normed_one = grad_normed_one + dot_nt(grad_qk[core], w_qk[core])
-        grad_normed_one = grad_normed_one + dot_nt(grad_v[core], w_v[core])
+        for kind in range(3):
+            grad_normed_one = grad_normed_one + dot_nt(grad_heads[core][kind], weights[core][kind])
     grad_input, grad_gain_one, grad_shift_one = norm_back(
         grad_normed_one, normal_one, spread_one, gain_one
     )
-    input_grad = send_back(grad_hidden + grad_input, F32)
+    grad_input = grad_hidden + grad_input
 
     grad_vectors = jnp.stack(
         [
             grad_gain_one,
             grad_shift_one,
-            grad_out_bias,
-            grad_scale_one,
+            jnp.sum(grad_hidden, 0) * scale_one,
+            jnp.sum(grad_hidden * branch_one, 0),
             grad_gain_two,
             grad_shift_two,
-            grad_down_bias,
-            grad_scale_two,
+            jnp.sum(grad_out, 0) * scale_two,
+            jnp.sum(grad_out * branch_two, 0),
         ]
     )
     grad_vectors = grad_vectors.reshape(-1, DP, LANES).transpose(1, 0, 2).reshape(DP, -1)
     bias_parts = []
     for core in cores:
-        query_part = jnp.sum(grad_qk[core].astype(F32), 0).reshape(2, 2, block_width)[:, 0]
-        value_part = jnp.sum(grad_v[core].astype(F32), 0).reshape(2, block_width)
-        rows = [query_part, value_part]
+        rows = [
+            jnp.sum(grad_heads[core][kind].astype(F32), 0).reshape(2, block_width) for kind in (0, 2)
+        ]
         for half in (0, 1):
-            unit_part = grad_unit_bias[half, core].reshape(2, half_units, block_width)
+            unit_part = jnp.sum(grad_pre[half, core].astype(F32), 0)
+            unit_part = unit_part.reshape(2, half_units, block_width)
             rows += [unit_part[:, at] for at in range(half_units)]
         bias_parts.append(jnp.stack(rows, 1))
-    grad_biases = jnp.stack(bias_parts).reshape(2, 2, -1, DP, bias_width).transpose(0, 1, 3, 2, 4)
-    grad_biases = jnp.take(grad_biases, place[:DP], axis=2).reshape(2, 2, DP, -1)
-    total_vectors = grad_vectors + swap_mp(grad_vectors, 1)
-    total_biases = grad_biases[0] + swap_mp(grad_biases[1], 1)
-    total_vectors = total_vectors + swap_mp(total_vectors, 2)
-    total_biases = total_biases[0] + swap_mp(total_biases[1], 2)
-    small_grads = jnp.concatenate([total_vectors, total_biases], 1)
-    small_grads = small_grads[:ZS] + swap_y(small_grads[ZS:])
-    small_total = small_grads[0]
-    for step in range(1, ZS):
-        small_total = small_total + swap_z(small_grads[step], step)
+    grad_biases = jnp.stack(bias_parts, 1).reshape(MP, -1, DP, bias_width).transpose(0, 2, 1, 3)
+    grad_biases = jnp.take(grad_biases, place[:DP], axis=1).reshape(MP, DP, -1)
+    sum_small = Chain(small_reduce_steps, grad_vectors, grad_biases)
+    send_grad = send_back(grad_input)
+    grad_input = meet(grad_input, sum_qkv, sum_small, sum_up[1], sum_out)
+    grad_input = meet(grad_input, sum_qkv, sum_small, sum_out, send_grad)
+    grad_input = meet(grad_input, sum_qkv, sum_small)
+    meet((), sum_small)
+    layer_output = spread_image(place, output[:chunk_rows], send_output.result, BF)[:, None]
+    input_grad = spread_image(place, grad_input[:chunk_rows], send_grad.result, F32)[:, None]
+
+    small_total = sum_small.result
     vector_grad = small_total[:vector_size].reshape(vectors.shape)
     bias_grad = small_total[vector_size:].reshape(head_biases.shape)
-
-    qk_sum = sums["qk"].reshape(depth, 2, block_width).transpose(1, 0, 2)
-    qkv_grad = jnp.concatenate([qk_sum, sums["v"][None]], 0)
     up_grad = jnp.concatenate(
-        [sums["up", half].reshape(depth, half_units, block_width) for half in (0, 1)], 1
+        [each.result.reshape(depth, half_units, block_width) for each in sum_up], 1
     )
     down_grad = jnp.concatenate(
-        [sums["down", half].reshape(depth, half_units, block_width) for half in (0, 1)], 1
+        [each.result.reshape(depth, half_units, block_width) for each in sum_down], 1
     ).transpose(1, 2, 0)
-    grads = (qkv_grad, sums["out"].T, up_grad, down_grad, bias_grad, vector_grad)
+    grads = (sum_qkv.result, sum_out.result.T, up_grad, down_grad, bias_grad, vector_grad)
     params = (qkv_weight, out_weight, up_weight, down_weight, head_biases, vectors)
     firsts = (qkv_first, out_first, up_first, down_first, bias_first, vector_first)
     seconds = (qkv_second, out_second, up_second, down_second, bias_second, vector_second)

time: 824 us -> 752 us (0.913)
  waiting for transfers between devices: 271 us -> 180 us
  local copies, waits for them, and re-layouts: 64 us -> 82.1 us
    ppermute x46 -> x48, waiting for transfers between devices: 113 us -> 78.3 us  [swap_mp(): return lax.ppermute(part, 'mp', [(each, each ^ step) for each in range(MP)])]
    ppermute x16, waiting for transfers between devices: 99.8 us -> 67 us  [swap_y(): return lax.ppermute(part, 'dp', [(each, each ^ 1) for each in range(DP)])]
    ppermute x48, waiting for transfers between devices: 57.7 us -> 34.7 us  [swap_z(): lax.ppermute(part, 'dp', [(z * YS + y, (z ^ step) * YS + y) for z in rang...]
    convert_element_type x18, other arithmetic: 12.4 us -> 32.8 us  [add_low(): return (first.astype(F32) + second.astype(F32)).astype(BF)]
    concatenate x20, other arithmetic: 28.2 us -> 8.55 us  [the longest x10 6.22 us: gather_steps(): rows = jnp.concatenate([rows] + arrived, 0)]
    unnamed x382 -> x529, local copies, waits for them, and re-layouts: 32.6 us -> 44.3 us
    dot_general x0 -> x2, matrix products: none -> 10 us  [back_heads(): jnp.einsum('sd,tse->tde', normed_one, grad_heads[core], preferred_element...]
    dot_general x14 -> x16, matrix products: 58.2 us -> 49.5 us  [dot_nt(): lax.dot_general(left, right, (((1,), (1,)), ((), ())), preferred_element_...]
  transfers between devices with their start and end apart: 110 -> 112, of which waited for: 44 -> 30; matrix products, arithmetic and copies ran while one was open for 24% -> 33% of each run, Pallas kernels for 8% -> 16%
where the time goes in v2:
time: 752 us; the launch traced here: 746 us
  waiting for transfers between devices  180 us (24%)
  matrix products  147 us (20%)
  Pallas kernels  126 us (17%)
  starting transfers between devices  118 us (16%)
  other arithmetic  88.5 us (12%)
  local copies, waits for them, and re-layouts  82.1 us (11%)
    ppermute x48, waiting for transfers between devices, swap_mp(): return lax.ppermute(part, 'mp', [(each, each ^ step) for each in range(MP)])  78.3 us
    ppermute x48, starting transfers between devices, swap_z(): lax.ppermute(part, 'dp', [(z * YS + y, (z ^ step) * YS + y) for z in rang...  69.5 us
    ppermute x16, waiting for transfers between devices, swap_y(): return lax.ppermute(part, 'dp', [(each, each ^ 1) for each in range(DP)])  67 us
    pallas_call x2, Pallas kernels, attend_back(): pl.pallas_call(functools.partial(attend_back_kernel, 256), grid=(pairs,),...  63.6 us
    dot_general x16, matrix products, dot_nn(): lax.dot_general(left, right, (((1,), (0,)), ((), ())), preferred_element_...  54.2 us
    dot_general x16, matrix products, dot_nt(): lax.dot_general(left, right, (((1,), (1,)), ((), ())), preferred_element_...  49.5 us
    unnamed x529, local copies, waits for them, and re-layouts  44.3 us
    pallas_call x2, Pallas kernels, attend(): pl.pallas_call(functools.partial(attend_kernel, 256), grid=(pairs,), in_s...  35.7 us
  transfers between devices with their start and end apart: 112, of which 30 were waited for; matrix products, arithmetic and copies ran while one was open for 33% of the time, Pallas kernels for 16%

profile of v2, /device:TPU:0, one launch (start us, length us, event | category | flops | bytes accessed | tf_op | source)
XLA Modules:
  0.0 745.7 jit_solution(7341683625685660629)
XLA Ops:
  2.3 3.1 collective-permute-start
  5.4 2.6 collective-permute-start.1
  10.0 3.5 collective-permute-start.4
  22.3 3.8 collective-permute-start.7
  26.8 3.7 collective-permute-start.10
  32.7 2.6 collective-permute-done.10
  45.7 3.0 collective-permute-start.18
  61.8 4.7 collective-permute-done.20
  72.7 3.1 collective-permute-done.24.refs_2_
  76.6 2.8 collective-permute-start.30
  83.5 6.1 collective-permute-done.26
  93.0 6.6 assemble_image.2
  135.2 17.8 %attend.2 = (bf16[1024,512]{1,0:T(8,128)(2,1)S(1)}, f32[4,8,1024]{2,1,0:T(8,128)S(1)}) custom-call(bf16[1024,512]{1,0:T(8,128)(2,1)S(1)} %add_convert_fusion.15.q_ref, bf16[1024,512]{1,0:T(8,128)(2,1)S(1)} %convolution_convert_fusion.9.k_ref, bf16[1024,512]{1,0:T(8,128)(2,1)S(1)} %add_convert_fusion.14.v_ref), custom_call_target="tpu_custom_call" | custom-call | flops 8589934592 | bytes 4194304 | tf_op jit(solution)/shard_map/attend/pallas_call | solution.py:606
  165.8 17.9 %attend.3 = (bf16[1024,512]{1,0:T(8,128)(2,1)S(1)}, f32[4,8,1024]{2,1,0:T(8,128)S(1)}) custom-call(bf16[1024,512]{1,0:T(8,128)(2,1)S(1)} %add_convert_fusion.13.q_ref, bf16[1024,512]{1,0:T(8,128)(2,1)S(1)} %convolution_convert_fusion.8.k_ref, bf16[1024,512]{1,0:T(8,128)(2,1)S(1)} %add_convert_fusion.12.v_ref), custom_call_target="tpu_custom_call" | custom-call | flops 8589934592 | bytes 4194304 | tf_op jit(solution)/shard_map/attend/pallas_call | solution.py:606
  184.0 2.8 collective-permute-start.50
  190.3 3.6 fusion.86
  196.9 4.9 collective-permute-done.51
  202.7 10.1 %collective-permute-done.47 = bf16[512,1024]{0,1:T(8,128)(2,1)S(1)} collective-permute-done((bf16[512,1024]{0,1:T(8,128)(2,1)S(1)}, bf16[512,1024]{0,1:T(8,128)(2,1)S(1)}, u32[]{:S(2)}, u32[]{:S(2)}) %collective-permute-start.47) | collective-permute-done | bytes 1048608 | tf_op jit(solution)/shard_map/ppermute | solution.py:374
  214.7 5.4 fusion.24
  220.1 7.7 %fusion.19 = (bf16[1024,1024]{1,0:T(8,128)(2,1)}, bf16[1024,1024]{1,0:T(8,128)(2,1)}) fusion(f32[1024]{0:T(1024)S(1)} %bitcast.354, bf16[1024,1024]{1,0:T(8,128)(2,1)S(1)} %add_convert_fusion.5, bf16[512,1024]{0,1:T(8,128)(2,1)S(1)} %collective-permute-done.40, bf16[512,512]{0,1:T(8,128)(2,1)S(1)} %collective-permute-done.38, ...), kind=kOutput, calls=%fused_computation.33 | convolution fusion | flops 2166358016 | bytes 8392704 | tf_op jit(solution)/shard_map/dot_general | solution.py:643
  227.8 11.2 %collective-permute-done.53 = bf16[512,1024]{0,1:T(8,128)(2,1)S(1)} collective-permute-done((bf16[512,1024]{0,1:T(8,128)(2,1)S(1)}, bf16[512,1024]{0,1:T(8,128)(2,1)S(1)}, u32[]{:S(2)}, u32[]{:S(2)}) %collective-permute-start.53) | collective-permute-done | bytes 1048608 | tf_op jit(solution)/shard_map/ppermute | solution.py:374
  244.0 7.7 %fusion.29 = (bf16[1024,1024]{1,0:T(8,128)(2,1)}, bf16[1024,1024]{1,0:T(8,128)(2,1)}) fusion(f32[1024]{0:T(1024)S(1)} %bitcast.352, bf16[1024,1024]{1,0:T(8,128)(2,1)S(1)} %add_convert_fusion.5, bf16[512,1024]{0,1:T(8,128)(2,1)S(1)} %collective-permute-done.47, bf16[512,512]{0,1:T(8,128)(2,1)S(1)} %collective-permute-done.41, ...), kind=kOutput, calls=%fused_computation.43 | convolution fusion | flops 2166358016 | bytes 8392704 | tf_op jit(solution)/shard_map/dot_general | solution.py:643
  251.7 5.4 fusion.34
  257.1 9.1 %collective-permute-done.57.refs_1_ = bf16[256,1024]{1,0:T(8,128)(2,1)S(1)} collective-permute-done((bf16[256,1024]{1,0:T(8,128)(2,1)S(1)}, bf16[256,1024]{1,0:T(8,128)(2,1)S(1)}, u32[]{:S(2)}, u32[]{:S(2)}) %collective-permute-start.57) | collective-permute-done | bytes 524320 | tf_op jit(solution)/shard_map/ppermute | solution.py:378
  266.2 10.5 %collective-permute-done.58.refs_2_ = bf16[256,1024]{1,0:T(8,128)(2,1)S(1)} collective-permute-done((bf16[256,1024]{1,0:T(8,128)(2,1)S(1)}, bf16[256,1024]{1,0:T(8,128)(2,1)S(1)}, u32[]{:S(2)}, u32[]{:S(2)}) %collective-permute-start.58) | collective-permute-done | bytes 524320 | tf_op jit(solution)/shard_map/ppermute | solution.py:378
  278.2 6.5 assemble_image.3
  291.1 24.1 %collective-permute-done.60 = bf16[512,1024]{0,1:T(8,128)(2,1)S(1)} collective-permute-done((bf16[512,1024]{0,1:T(8,128)(2,1)S(1)}, bf16[512,1024]{0,1:T(8,128)(2,1)S(1)}, u32[]{:S(2)}, u32[]{:S(2)}) %collective-permute-start.60) | collective-permute-done | bytes 1048608 | tf_op jit(solution)/shard_map/ppermute | solution.py:374
  323.5 6.0 fusion.100
  329.6 3.8 convolution_convert_fusion.2
  333.8 3.8 fusion.102
  340.0 2.6 fusion.99
  345.0 5.3 fusion.36
  370.9 3.8 fusion.103
  374.7 12.2 %collective-permute-done.63 = bf16[512,1024]{1,0:T(8,128)(2,1)S(1)} collective-permute-done((bf16[512,1024]{1,0:T(8,128)(2,1)S(1)}, bf16[512,1024]{1,0:T(8,128)(2,1)S(1)}, u32[]{:S(2)}, u32[]{:S(2)}) %collective-permute-start.63) | collective-permute-done | bytes 1048608 | tf_op jit(solution)/shard_map/ppermute | solution.py:374
  386.9 6.5 convert_reduce_fusion.2
  404.4 6.8 multiply_reduce_fusion
  413.2 2.7 add_convert_fusion.1
  418.6 3.8 convolution_convert_fusion
  422.8 4.2 multiply_reduce_fusion.1
  428.9 2.9 multiply_convert_fusion
  436.5 9.0 %collective-permute-done.71.refs_2_ = bf16[256,1024]{1,0:T(8,128)(2,1)S(1)} collective-permute-done((bf16[256,1024]{1,0:T(8,128)(2,1)S(1)}, bf16[256,1024]{1,0:T(8,128)(2,1)S(1)}, u32[]{:S(2)}, u32[]{:S(2)}) %collective-permute-start.71) | collective-permute-done | bytes 524320 | tf_op jit(solution)/shard_map/ppermute | solution.py:378
  445.5 11.9 %collective-permute-done.65 = bf16[512,512]{1,0:T(8,128)(2,1)S(1)} collective-permute-done((bf16[512,512]{1,0:T(8,128)(2,1)S(1)}, bf16[512,512]{1,0:T(8,128)(2,1)S(1)}, u32[]{:S(2)}, u32[]{:S(2)}) %collective-permute-start.65) | collective-permute-done | bytes 524320 | tf_op jit(solution)/shard_map/ppermute | solution.py:378
  466.8 2.6 add_convert_fusion
  472.1 32.0 %attend_back.2 = bf16[3,1024,512]{2,1,0:T(8,128)(2,1)S(1)} custom-call(bf16[1024,512]{1,0:T(8,128)(2,1)S(1)} %copy-done.11, bf16[1024,512]{1,0:T(8,128)(2,1)S(1)} %copy-done.7, bf16[1024,512]{1,0:T(8,128)(2,1)S(1)} %copy-done.13, bf16[1024,512]{1,0:T(8,128)(2,1)S(1)} %convolution_convert_fusion.7.g_ref, f32[4,8,1024]{2,1,0:T(8,128)S(1)} %get-tuple-element.329.lse_ref), custom_call_target="tpu_custom_call" | custom-call | flops 21474836480 | bytes 7340032 | tf_op jit(solution)/shard_map/attend_back/pallas_call | solution.py:627
  509.2 4.9 convert_bitcast_fusion
  518.8 6.5 spread_image.2
  525.3 3.2 convolution_convert_fusion.5.g_ref
  541.8 31.6 %attend_back.3 = bf16[3,1024,512]{2,1,0:T(8,128)(2,1)S(1)} custom-call(bf16[1024,512]{1,0:T(8,128)(2,1)S(1)} %copy-done.17, bf16[1024,512]{1,0:T(8,128)(2,1)S(1)} %copy-done.15, bf16[1024,512]{1,0:T(8,128)(2,1)S(1)} %copy-done.9, bf16[1024,512]{1,0:T(8,128)(2,1)S(1)} %convolution_convert_fusion.5.g_ref, f32[4,8,1024]{2,1,0:T(8,128)S(1)} %get-tuple-element.335.lse_ref), custom_call_target="tpu_custom_call" | custom-call | flops 21474836480 | bytes 7340032 | tf_op jit(solution)/shard_map/attend_back/pallas_call | solution.py:627
  575.9 5.1 fusion.37
  587.3 6.1 collective-permute-done.86
  598.0 2.6 fusion.48
  602.0 3.3 fusion.50
  606.9 7.0 fusion.13
  614.0 4.4 fusion
  636.8 5.6 fusion.84
  654.9 7.7 %collective-permute-done.93 = bf16[128,512]{1,0:T(8,128)(2,1)} collective-permute-done((bf16[128,512]{1,0:T(8,128)(2,1)}, bf16[128,512]{1,0:T(8,128)(2,1)}, u32[]{:S(2)}, u32[]{:S(2)}) %collective-permute-start.93) | collective-permute-done | bytes 131104 | tf_op jit(solution)/shard_map/ppermute | solution.py:368
  674.8 3.0 collective-permute-done.103.refs_1_
  677.8 9.3 %collective-permute-done.104.refs_2_ = bf16[256,1024]{1,0:T(8,128)(2,1)} collective-permute-done((bf16[256,1024]{1,0:T(8,128)(2,1)}, bf16[256,1024]{1,0:T(8,128)(2,1)}, u32[]{:S(2)}, u32[]{:S(2)}) %collective-permute-start.104) | collective-permute-done | bytes 524320 | tf_op jit(solution)/shard_map/ppermute | solution.py:378
  687.1 15.1 %collective-permute-done.98 = f32[8,192]{1,0:T(8,128)S(1)} collective-permute-done((f32[8,192]{1,0:T(8,128)S(1)}, f32[8,192]{1,0:T(8,128)S(1)}, u32[]{:S(2)}, u32[]{:S(2)}) %collective-permute-start.98) | collective-permute-done | bytes 6176 | tf_op jit(solution)/shard_map/ppermute | solution.py:378
  702.8 3.2 multiply_subtract_fusion.1
  712.4 2.6 collective-permute-start.107
  719.6 4.4 collective-permute-done.106
  724.8 2.7 collective-permute-start.109
  736.2 7.1 spread_image.3
  (913 shorter events, 296.1 us)
Async XLA Ops:
  2.3 17.6 %collective-permute-start = (bf16[1,1216]{1,0:T(2,128)(2,1)S(1)}, bf16[1,1216]{1,0:T(2,128)(2,1)S(1)}, u32[]{:S(2)}, u32[]{:S(2)}) collective-permute-start(bf16[1,1216]{1,0:T(2,128)(2,1)S(1)} %reshape.919), channel_id=1, source_target_pairs={{0,8},{4,12},{8,0},{12,4},{16,24},{20,28},{24,16},{28,20},{1,9},{5... | collective-permute-start | bytes 7304 | tf_op jit(solution)/shard_map/ppermute | solution.py:368
  9.1 17.0 %collective-permute-start.3 = (bf16[128,256]{1,0:T(8,128)(2,1)S(1)}, bf16[128,256]{1,0:T(8,128)(2,1)S(1)}, u32[]{:S(2)}, u32[]{:S(2)}) collective-permute-start(bf16[128,256]{1,0:T(8,128)(2,1)S(1)} %get-tuple-element.595), channel_id=1, source_target_pairs={{0,8},{4,12},{8,0},{12,4},{16,24},{20,28},{24,16},{28,20},{1,9},{5... | collective-permute-start | bytes 196616 | tf_op jit(solution)/shard_map/ppermute | solution.py:368
  50.8 19.4 %collective-permute-start.22 = (bf16[256,1024]{1,0:T(8,128)(2,1)}, bf16[256,1024]{1,0:T(8,128)(2,1)S(1)}, u32[]{:S(2)}, u32[]{:S(2)}) collective-permute-start(bf16[256,1024]{1,0:T(8,128)(2,1)} %get-tuple-element.570), channel_id=1, source_target_pairs={{0,1},{1,0},{2,3},{3,2},{4,5},{5,4},{6,7},{7,6},{8,9},{9,8},{10,11... | collective-permute-start | bytes 1572872 | tf_op jit(solution)/shard_map/ppermute | solution.py:378
  52.0 19.7 %collective-permute-start.23 = (bf16[256,1024]{1,0:T(8,128)(2,1)}, bf16[256,1024]{1,0:T(8,128)(2,1)}, u32[]{:S(2)}, u32[]{:S(2)}) collective-permute-start(bf16[256,1024]{1,0:T(8,128)(2,1)} %get-tuple-element.569), channel_id=1, source_target_pairs={{0,2},{1,3},{2,0},{3,1},{4,6},{5,7},{6,4},{7,5},{8,10},{9,11},{10,... | collective-permute-start | bytes 1572872 | tf_op jit(solution)/shard_map/ppermute | solution.py:378
  68.1 21.6 %collective-permute-start.26 = (bf16[512,512]{1,0:T(8,128)(2,1)S(1)}, bf16[512,512]{1,0:T(8,128)(2,1)S(1)}, u32[]{:S(2)}, u32[]{:S(2)}) collective-permute-start(bf16[512,512]{1,0:T(8,128)(2,1)S(1)} %pad_maximum_fusion.13), channel_id=1, source_target_pairs={{0,4},{4,0},{8,12},{12,8},{16,20},{20,16},{24,28},{28,24},{1,5},{5... | collective-permute-start | bytes 1572872 | tf_op jit(solution)/shard_map/ppermute | solution.py:374
  70.2 39.8 %collective-permute-start.28 = (bf16[128,512]{0,1:T(8,128)(2,1)}, bf16[128,512]{0,1:T(8,128)(2,1)}, u32[]{:S(2)}, u32[]{:S(2)}) collective-permute-start(bf16[128,512]{0,1:T(8,128)(2,1)} %bitcast.10), channel_id=1, source_target_pairs={{0,8},{4,12},{8,0},{12,4},{16,24},{20,28},{24,16},{28,20},{1,9},{5... | collective-permute-start | bytes 393224 | tf_op jit(solution)/shard_map/ppermute | solution.py:368
  71.8 39.9 %collective-permute-start.29 = (bf16[128,512]{0,1:T(8,128)(2,1)}, bf16[128,512]{0,1:T(8,128)(2,1)}, u32[]{:S(2)}, u32[]{:S(2)}) collective-permute-start(bf16[128,512]{0,1:T(8,128)(2,1)} %bitcast.10), channel_id=1, source_target_pairs={{0,16},{4,20},{8,24},{12,28},{16,0},{20,4},{24,8},{28,12},{1,17},{... | collective-permute-start | bytes 393224 | tf_op jit(solution)/shard_map/ppermute | solution.py:368
  76.6 35.8 %collective-permute-start.30 = (bf16[128,512]{0,1:T(8,128)(2,1)}, bf16[128,512]{0,1:T(8,128)(2,1)}, u32[]{:S(2)}, u32[]{:S(2)}) collective-permute-start(bf16[128,512]{0,1:T(8,128)(2,1)} %bitcast.10), channel_id=1, source_target_pairs={{0,24},{4,28},{8,16},{12,20},{16,8},{20,12},{24,0},{28,4},{1,25},{... | collective-permute-start | bytes 393224 | tf_op jit(solution)/shard_map/ppermute | solution.py:368
  81.4 31.0 %collective-permute-start.27 = (bf16[1024,256]{1,0:T(8,128)(2,1)}, bf16[1024,256]{1,0:T(8,128)(2,1)}, u32[]{:S(2)}, u32[]{:S(2)}) collective-permute-start(bf16[1024,256]{1,0:T(8,128)(2,1)} %constant_dynamic-update-slice_fusion), channel_id=1, source_target_pairs={{0,2},{1,3},{2,0},{3,1},{4,6},{5,7},{6,4},{7,5},{8,10},{9,11},{10,... | collective-permute-start | bytes 1572872 | tf_op jit(solution)/shard_map/ppermute | solution.py:378
  89.7 22.7 %collective-permute-start.31 = (bf16[512,256]{0,1:T(8,128)(2,1)}, bf16[512,256]{0,1:T(8,128)(2,1)}, u32[]{:S(2)}, u32[]{:S(2)}) collective-permute-start(bf16[512,256]{0,1:T(8,128)(2,1)} %pad_maximum_fusion.18), channel_id=1, source_target_pairs={{0,4},{4,0},{8,12},{12,8},{16,20},{20,16},{24,28},{28,24},{1,5},{5... | collective-permute-start | bytes 786440 | tf_op jit(solution)/shard_map/ppermute | solution.py:374
  111.7 17.2 %collective-permute-start.36 = (bf16[128,512]{0,1:T(8,128)(2,1)}, bf16[128,512]{0,1:T(8,128)(2,1)S(1)}, u32[]{:S(2)}, u32[]{:S(2)}) collective-permute-start(bf16[128,512]{0,1:T(8,128)(2,1)} %bitcast.331), channel_id=1, source_target_pairs={{0,16},{4,20},{8,24},{12,28},{16,0},{20,4},{24,8},{28,12},{1,17},{... | collective-permute-start | bytes 393224 | tf_op jit(solution)/shard_map/ppermute | solution.py:368
  116.9 18.3 %collective-permute-start.32 = (bf16[1024,512]{1,0:T(8,128)(2,1)S(1)}, bf16[1024,512]{1,0:T(8,128)(2,1)S(1)}, u32[]{:S(2)}, u32[]{:S(2)}) collective-permute-start(bf16[1024,512]{1,0:T(8,128)(2,1)S(1)} %pad_maximum_fusion.4), channel_id=1, source_target_pairs={{0,1},{1,0},{2,3},{3,2},{4,5},{5,4},{6,7},{7,6},{8,9},{9,8},{10,11... | collective-permute-start | bytes 3145736 | tf_op jit(solution)/shard_map/ppermute | solution.py:378
  116.9 18.2 %collective-permute-start.33 = (bf16[1024,512]{1,0:T(8,128)(2,1)S(1)}, bf16[1024,512]{1,0:T(8,128)(2,1)S(1)}, u32[]{:S(2)}, u32[]{:S(2)}) collective-permute-start(bf16[1024,512]{1,0:T(8,128)(2,1)S(1)} %pad_maximum_fusion.5), channel_id=1, source_target_pairs={{0,1},{1,0},{2,3},{3,2},{4,5},{5,4},{6,7},{7,6},{8,9},{9,8},{10,11... | collective-permute-start | bytes 3145736 | tf_op jit(solution)/shard_map/ppermute | solution.py:378
  128.9 24.1 %collective-permute-start.38 = (bf16[512,512]{0,1:T(8,128)(2,1)S(1)}, bf16[512,512]{0,1:T(8,128)(2,1)S(1)}, u32[]{:S(2)}, u32[]{:S(2)}) collective-permute-start(bf16[512,512]{0,1:T(8,128)(2,1)S(1)} %constant_dynamic-update-slice_fusion.5), channel_id=1, source_target_pairs={{0,2},{1,3},{2,0},{3,1},{4,6},{5,7},{6,4},{7,5},{8,10},{9,11},{10,... | collective-permute-start | bytes 1572872 | tf_op jit(solution)/shard_map/ppermute | solution.py:378
  132.6 22.0 %collective-permute-start.39 = (bf16[1024,256]{0,1:T(8,128)(2,1)S(1)}, bf16[1024,256]{0,1:T(8,128)(2,1)S(1)}, u32[]{:S(2)}, u32[]{:S(2)}) collective-permute-start(bf16[1024,256]{0,1:T(8,128)(2,1)S(1)} %constant_dynamic-update-slice_fusion.9), channel_id=1, source_target_pairs={{0,2},{1,3},{2,0},{3,1},{4,6},{5,7},{6,4},{7,5},{8,10},{9,11},{10,... | collective-permute-start | bytes 1572872 | tf_op jit(solution)/shard_map/ppermute | solution.py:378
  154.9 28.9 %collective-permute-start.44 = (bf16[128,512]{0,1:T(8,128)(2,1)S(1)}, bf16[128,512]{0,1:T(8,128)(2,1)S(1)}, u32[]{:S(2)}, u32[]{:S(2)}) collective-permute-start(bf16[128,512]{0,1:T(8,128)(2,1)S(1)} %bitcast.327), channel_id=1, source_target_pairs={{0,16},{4,20},{8,24},{12,28},{16,0},{20,4},{24,8},{28,12},{1,17},{... | collective-permute-start | bytes 393224 | tf_op jit(solution)/shard_map/ppermute | solution.py:368
  157.3 26.5 %collective-permute-start.45 = (bf16[128,512]{0,1:T(8,128)(2,1)S(1)}, bf16[128,512]{0,1:T(8,128)(2,1)S(1)}, u32[]{:S(2)}, u32[]{:S(2)}) collective-permute-start(bf16[128,512]{0,1:T(8,128)(2,1)S(1)} %bitcast.328), channel_id=1, source_target_pairs={{0,24},{4,28},{8,16},{12,20},{16,8},{20,12},{24,0},{28,4},{1,25},{... | collective-permute-start | bytes 393224 | tf_op jit(solution)/shard_map/ppermute | solution.py:368
  159.0 24.8 %collective-permute-start.40 = (bf16[512,1024]{0,1:T(8,128)(2,1)S(1)}, bf16[512,1024]{0,1:T(8,128)(2,1)S(1)}, u32[]{:S(2)}, u32[]{:S(2)}) collective-permute-start(bf16[512,1024]{0,1:T(8,128)(2,1)S(1)} %pad_maximum_fusion.7), channel_id=1, source_target_pairs={{0,4},{4,0},{8,12},{12,8},{16,20},{20,16},{24,28},{28,24},{1,5},{5... | collective-permute-start | bytes 3145736 | tf_op jit(solution)/shard_map/ppermute | solution.py:374
  159.9 23.9 %collective-permute-start.42 = (bf16[1024,512]{0,1:T(8,128)(2,1)S(1)}, bf16[1024,512]{0,1:T(8,128)(2,1)S(1)}, u32[]{:S(2)}, u32[]{:S(2)}) collective-permute-start(bf16[1024,512]{0,1:T(8,128)(2,1)S(1)} %pad_maximum_fusion.8), channel_id=1, source_target_pairs={{0,1},{1,0},{2,3},{3,2},{4,5},{5,4},{6,7},{7,6},{8,9},{9,8},{10,11... | collective-permute-start | bytes 3145736 | tf_op jit(solution)/shard_map/ppermute | solution.py:378
  164.0 19.8 %collective-permute-start.41 = (bf16[512,512]{0,1:T(8,128)(2,1)S(1)}, bf16[512,512]{0,1:T(8,128)(2,1)S(1)}, u32[]{:S(2)}, u32[]{:S(2)}) collective-permute-start(bf16[512,512]{0,1:T(8,128)(2,1)S(1)} %constant_dynamic-update-slice_fusion.14), channel_id=1, source_target_pairs={{0,2},{1,3},{2,0},{3,1},{4,6},{5,7},{6,4},{7,5},{8,10},{9,11},{10,... | collective-permute-start | bytes 1572872 | tf_op jit(solution)/shard_map/ppermute | solution.py:378
  187.0 25.8 %collective-permute-start.46 = (bf16[1024,1024]{0,1:T(8,128)(2,1)S(1)}, bf16[1024,1024]{0,1:T(8,128)(2,1)S(1)}, u32[]{:S(2)}, u32[]{:S(2)}) collective-permute-start(bf16[1024,1024]{0,1:T(8,128)(2,1)S(1)} %pad_maximum_fusion), channel_id=1, source_target_pairs={{0,1},{1,0},{2,3},{3,2},{4,5},{5,4},{6,7},{7,6},{8,9},{9,8},{10,11... | collective-permute-start | bytes 6291464 | tf_op jit(solution)/shard_map/ppermute | solution.py:378
  187.2 25.6 %collective-permute-start.47 = (bf16[512,1024]{0,1:T(8,128)(2,1)S(1)}, bf16[512,1024]{0,1:T(8,128)(2,1)S(1)}, u32[]{:S(2)}, u32[]{:S(2)}) collective-permute-start(bf16[512,1024]{0,1:T(8,128)(2,1)S(1)} %pad_maximum_fusion.9), channel_id=1, source_target_pairs={{0,4},{4,0},{8,12},{12,8},{16,20},{20,16},{24,28},{28,24},{1,5},{5... | collective-permute-start | bytes 3145736 | tf_op jit(solution)/shard_map/ppermute | solution.py:374
  213.1 25.9 %collective-permute-start.52 = (bf16[1024,1024]{0,1:T(8,128)(2,1)S(1)}, bf16[1024,1024]{0,1:T(8,128)(2,1)S(1)}, u32[]{:S(2)}, u32[]{:S(2)}) collective-permute-start(bf16[1024,1024]{0,1:T(8,128)(2,1)S(1)} %pad_maximum_fusion.1), channel_id=1, source_target_pairs={{0,1},{1,0},{2,3},{3,2},{4,5},{5,4},{6,7},{7,6},{8,9},{9,8},{10,11... | collective-permute-start | bytes 6291464 | tf_op jit(solution)/shard_map/ppermute | solution.py:378
  213.4 25.6 %collective-permute-start.53 = (bf16[512,1024]{0,1:T(8,128)(2,1)S(1)}, bf16[512,1024]{0,1:T(8,128)(2,1)S(1)}, u32[]{:S(2)}, u32[]{:S(2)}) collective-permute-start(bf16[512,1024]{0,1:T(8,128)(2,1)S(1)} %pad_maximum_fusion.10), channel_id=1, source_target_pairs={{0,4},{4,0},{8,12},{12,8},{16,20},{20,16},{24,28},{28,24},{1,5},{5... | collective-permute-start | bytes 3145736 | tf_op jit(solution)/shard_map/ppermute | solution.py:374
  240.0 36.7 %collective-permute-start.54 = (bf16[1024,1024]{0,1:T(8,128)(2,1)S(1)}, bf16[1024,1024]{0,1:T(8,128)(2,1)S(1)}, u32[]{:S(2)}, u32[]{:S(2)}) collective-permute-start(bf16[1024,1024]{0,1:T(8,128)(2,1)S(1)} %pad_maximum_fusion.2), channel_id=1, source_target_pairs={{0,1},{1,0},{2,3},{3,2},{4,5},{5,4},{6,7},{7,6},{8,9},{9,8},{10,11... | collective-permute-start | bytes 6291464 | tf_op jit(solution)/shard_map/ppermute | solution.py:378
  240.2 16.9 %collective-permute-start.55 = (bf16[512,512]{0,1:T(8,128)(2,1)S(1)}, bf16[512,512]{0,1:T(8,128)(2,1)S(1)}, u32[]{:S(2)}, u32[]{:S(2)}) collective-permute-start(bf16[512,512]{0,1:T(8,128)(2,1)S(1)} %constant_dynamic-update-slice_fusion.22), channel_id=1, source_target_pairs={{0,2},{1,3},{2,0},{3,1},{4,6},{5,7},{6,4},{7,5},{8,10},{9,11},{10,... | collective-permute-start | bytes 1572872 | tf_op jit(solution)/shard_map/ppermute | solution.py:378
  242.1 24.1 %collective-permute-start.57 = (bf16[256,1024]{1,0:T(8,128)(2,1)S(1)}, bf16[256,1024]{1,0:T(8,128)(2,1)S(1)}, u32[]{:S(2)}, u32[]{:S(2)}) collective-permute-start(bf16[256,1024]{1,0:T(8,128)(2,1)S(1)} %get-tuple-element.566), channel_id=1, source_target_pairs={{0,2},{1,3},{2,0},{3,1},{4,6},{5,7},{6,4},{7,5},{8,10},{9,11},{10,... | collective-permute-start | bytes 1572872 | tf_op jit(solution)/shard_map/ppermute | solution.py:378
  242.7 33.9 %collective-permute-start.58 = (bf16[256,1024]{1,0:T(8,128)(2,1)S(1)}, bf16[256,1024]{1,0:T(8,128)(2,1)S(1)}, u32[]{:S(2)}, u32[]{:S(2)}) collective-permute-start(bf16[256,1024]{1,0:T(8,128)(2,1)S(1)} %get-tuple-element.565), channel_id=1, source_target_pairs={{0,3},{1,2},{2,1},{3,0},{4,7},{5,6},{6,5},{7,4},{8,11},{9,10},{10,... | collective-permute-start | bytes 1572872 | tf_op jit(solution)/shard_map/ppermute | solution.py:378
  289.4 25.8 %collective-permute-start.59 = (bf16[1024,1024]{1,0:T(8,128)(2,1)S(1)}, bf16[1024,1024]{1,0:T(8,128)(2,1)}, u32[]{:S(2)}, u32[]{:S(2)}) collective-permute-start(bf16[1024,1024]{1,0:T(8,128)(2,1)S(1)} %convolution_convert_fusion.3), channel_id=1, source_target_pairs={{0,1},{1,0},{2,3},{3,2},{4,5},{5,4},{6,7},{7,6},{8,9},{9,8},{10,11... | collective-permute-start | bytes 6291464 | tf_op jit(solution)/shard_map/ppermute | solution.py:378
  289.8 25.4 %collective-permute-start.60 = (bf16[512,1024]{0,1:T(8,128)(2,1)S(1)}, bf16[512,1024]{0,1:T(8,128)(2,1)S(1)}, u32[]{:S(2)}, u32[]{:S(2)}) collective-permute-start(bf16[512,1024]{0,1:T(8,128)(2,1)S(1)} %pad_maximum_fusion.11), channel_id=1, source_target_pairs={{0,4},{4,0},{8,12},{12,8},{16,20},{20,16},{24,28},{28,24},{1,5},{5... | collective-permute-start | bytes 3145736 | tf_op jit(solution)/shard_map/ppermute | solution.py:374
  316.9 20.8 %collective-permute-start.61 = (bf16[1024,1024]{0,1:T(8,128)(2,1)}, bf16[1024,1024]{0,1:T(8,128)(2,1)}, u32[]{:S(2)}, u32[]{:S(2)}) collective-permute-start(bf16[1024,1024]{0,1:T(8,128)(2,1)} %pad_maximum_fusion.3), channel_id=1, source_target_pairs={{0,1},{1,0},{2,3},{3,2},{4,5},{5,4},{6,7},{7,6},{8,9},{9,8},{10,11... | collective-permute-start | bytes 6291464 | tf_op jit(solution)/shard_map/ppermute | solution.py:378
  333.3 18.2 %collective-permute-start.62 = (bf16[1024,1024]{1,0:T(8,128)(2,1)}, bf16[1024,1024]{1,0:T(8,128)(2,1)S(1)}, u32[]{:S(2)}, u32[]{:S(2)}) collective-permute-start(bf16[1024,1024]{1,0:T(8,128)(2,1)} %convolution_convert_fusion.2), channel_id=1, source_target_pairs={{0,1},{1,0},{2,3},{3,2},{4,5},{5,4},{6,7},{7,6},{8,9},{9,8},{10,11... | collective-permute-start | bytes 6291464 | tf_op jit(solution)/shard_map/ppermute | solution.py:378
  358.1 28.8 %collective-permute-start.64 = (bf16[1024,1024]{1,0:T(8,128)(2,1)S(1)}, bf16[1024,1024]{1,0:T(8,128)(2,1)S(1)}, u32[]{:S(2)}, u32[]{:S(2)}) collective-permute-start(bf16[1024,1024]{1,0:T(8,128)(2,1)S(1)} %convolution_convert_fusion.1), channel_id=1, source_target_pairs={{0,1},{1,0},{2,3},{3,2},{4,5},{5,4},{6,7},{7,6},{8,9},{9,8},{10,11... | collective-permute-start | bytes 6291464 | tf_op jit(solution)/shard_map/ppermute | solution.py:378
  360.8 26.0 %collective-permute-start.63 = (bf16[512,1024]{1,0:T(8,128)(2,1)S(1)}, bf16[512,1024]{1,0:T(8,128)(2,1)S(1)}, u32[]{:S(2)}, u32[]{:S(2)}) collective-permute-start(bf16[512,1024]{1,0:T(8,128)(2,1)S(1)} %slice.429), channel_id=1, source_target_pairs={{0,4},{4,0},{8,12},{12,8},{16,20},{20,16},{24,28},{28,24},{1,5},{5... | collective-permute-start | bytes 3145736 | tf_op jit(solution)/shard_map/ppermute | solution.py:374
  364.8 80.7 %collective-permute-start.66 = (bf16[512,1024]{1,0:T(8,128)(2,1)}, bf16[512,1024]{1,0:T(8,128)(2,1)}, u32[]{:S(2)}, u32[]{:S(2)}) collective-permute-start(bf16[512,1024]{1,0:T(8,128)(2,1)} %slice.432), channel_id=1, source_target_pairs={{0,4},{4,0},{8,12},{12,8},{16,20},{20,16},{24,28},{28,24},{1,5},{5... | collective-permute-start | bytes 3145736 | tf_op jit(solution)/shard_map/ppermute | solution.py:374
  367.4 64.5 %collective-permute-start.69 = (bf16[256,1024]{1,0:T(8,128)(2,1)}, bf16[256,1024]{1,0:T(8,128)(2,1)}, u32[]{:S(2)}, u32[]{:S(2)}) collective-permute-start(bf16[256,1024]{1,0:T(8,128)(2,1)} %get-tuple-element.563), channel_id=1, source_target_pairs={{0,1},{1,0},{2,3},{3,2},{4,5},{5,4},{6,7},{7,6},{8,9},{9,8},{10,11... | collective-permute-start | bytes 1572872 | tf_op jit(solution)/shard_map/ppermute | solution.py:378
  367.6 65.0 %collective-permute-start.70 = (bf16[256,1024]{1,0:T(8,128)(2,1)}, bf16[256,1024]{1,0:T(8,128)(2,1)}, u32[]{:S(2)}, u32[]{:S(2)}) collective-permute-start(bf16[256,1024]{1,0:T(8,128)(2,1)} %get-tuple-element.562), channel_id=1, source_target_pairs={{0,2},{1,3},{2,0},{3,1},{4,6},{5,7},{6,4},{7,5},{8,10},{9,11},{10,... | collective-permute-start | bytes 1572872 | tf_op jit(solution)/shard_map/ppermute | solution.py:378
  417.0 40.4 %collective-permute-start.67 = (bf16[512,1024]{1,0:T(8,128)(2,1)}, bf16[512,1024]{1,0:T(8,128)(2,1)}, u32[]{:S(2)}, u32[]{:S(2)}) collective-permute-start(bf16[512,1024]{1,0:T(8,128)(2,1)} %slice.433), channel_id=1, source_target_pairs={{0,4},{4,0},{8,12},{12,8},{16,20},{20,16},{24,28},{28,24},{1,5},{5... | collective-permute-start | bytes 3145736 | tf_op jit(solution)/shard_map/ppermute | solution.py:374
  422.4 35.0 %collective-permute-start.68 = (bf16[1024,1024]{1,0:T(8,128)(2,1)}, bf16[1024,1024]{1,0:T(8,128)(2,1)}, u32[]{:S(2)}, u32[]{:S(2)}) collective-permute-start(bf16[1024,1024]{1,0:T(8,128)(2,1)} %convolution_convert_fusion), channel_id=1, source_target_pairs={{0,1},{1,0},{2,3},{3,2},{4,5},{5,4},{6,7},{7,6},{8,9},{9,8},{10,11... | collective-permute-start | bytes 6291464 | tf_op jit(solution)/shard_map/ppermute | solution.py:378
  432.6 24.8 %collective-permute-start.65 = (bf16[512,512]{1,0:T(8,128)(2,1)S(1)}, bf16[512,512]{1,0:T(8,128)(2,1)S(1)}, u32[]{:S(2)}, u32[]{:S(2)}) collective-permute-start(bf16[512,512]{1,0:T(8,128)(2,1)S(1)} %copy-done.144), channel_id=1, source_target_pairs={{0,2},{1,3},{2,0},{3,1},{4,6},{5,7},{6,4},{7,5},{8,10},{9,11},{10,... | collective-permute-start | bytes 1572872 | tf_op jit(solution)/shard_map/ppermute | solution.py:378
  461.2 48.0 %collective-permute-start.72 = (bf16[128,512]{1,0:T(8,128)(2,1)S(1)}, bf16[128,512]{1,0:T(8,128)(2,1)S(1)}, u32[]{:S(2)}, u32[]{:S(2)}) collective-permute-start(bf16[128,512]{1,0:T(8,128)(2,1)S(1)} %get-tuple-element.585), channel_id=1, source_target_pairs={{0,8},{4,12},{8,0},{12,4},{16,24},{20,28},{24,16},{28,20},{1,9},{5... | collective-permute-start | bytes 393224 | tf_op jit(solution)/shard_map/ppermute | solution.py:368
  461.4 52.8 %collective-permute-start.73 = (bf16[128,512]{1,0:T(8,128)(2,1)S(1)}, bf16[128,512]{1,0:T(8,128)(2,1)S(1)}, u32[]{:S(2)}, u32[]{:S(2)}) collective-permute-start(bf16[128,512]{1,0:T(8,128)(2,1)S(1)} %get-tuple-element.584), channel_id=1, source_target_pairs={{0,16},{4,20},{8,24},{12,28},{16,0},{20,4},{24,8},{28,12},{1,17},{... | collective-permute-start | bytes 393224 | tf_op jit(solution)/shard_map/ppermute | solution.py:368
  466.3 59.0 %collective-permute-start.75 = (bf16[512,512]{1,0:T(8,128)(2,1)}, bf16[512,512]{1,0:T(8,128)(2,1)}, u32[]{:S(2)}, u32[]{:S(2)}) collective-permute-start(bf16[512,512]{1,0:T(8,128)(2,1)} %slice.439), channel_id=1, source_target_pairs={{0,2},{1,3},{2,0},{3,1},{4,6},{5,7},{6,4},{7,5},{8,10},{9,11},{10,... | collective-permute-start | bytes 1572872 | tf_op jit(solution)/shard_map/ppermute | solution.py:378
  470.5 54.8 %collective-permute-start.77 = (bf16[512,1024]{1,0:T(8,128)(2,1)}, bf16[512,1024]{1,0:T(8,128)(2,1)}, u32[]{:S(2)}, u32[]{:S(2)}) collective-permute-start(bf16[512,1024]{1,0:T(8,128)(2,1)} %slice.442), channel_id=1, source_target_pairs={{0,4},{4,0},{8,12},{12,8},{16,20},{20,16},{24,28},{28,24},{1,5},{5... | collective-permute-start | bytes 3145736 | tf_op jit(solution)/shard_map/ppermute | solution.py:374
  507.7 17.6 %collective-permute-start.76 = (bf16[512,512]{1,0:T(8,128)(2,1)}, bf16[512,512]{1,0:T(8,128)(2,1)}, u32[]{:S(2)}, u32[]{:S(2)}) collective-permute-start(bf16[512,512]{1,0:T(8,128)(2,1)} %slice.441), channel_id=1, source_target_pairs={{0,2},{1,3},{2,0},{3,1},{4,6},{5,7},{6,4},{7,5},{8,10},{9,11},{10,... | collective-permute-start | bytes 1572872 | tf_op jit(solution)/shard_map/ppermute | solution.py:378
  528.6 64.9 %collective-permute-start.79 = (bf16[3,1024,512]{1,2,0:T(8,128)(2,1)}, bf16[3,1024,512]{1,2,0:T(8,128)(2,1)}, u32[]{:S(2)}, u32[]{:S(2)}) collective-permute-start(bf16[3,1024,512]{1,2,0:T(8,128)(2,1)} %convert_bitcast_fusion), channel_id=1, source_target_pairs={{0,1},{1,0},{2,3},{3,2},{4,5},{5,4},{6,7},{7,6},{8,9},{9,8},{10,11... | collective-permute-start | bytes 9437192 | tf_op jit(solution)/shard_map/ppermute | solution.py:378
  530.2 44.0 %collective-permute-start.80 = (bf16[128,512]{1,0:T(8,128)(2,1)S(1)}, bf16[128,512]{1,0:T(8,128)(2,1)S(1)}, u32[]{:S(2)}, u32[]{:S(2)}) collective-permute-start(bf16[128,512]{1,0:T(8,128)(2,1)S(1)} %get-tuple-element.582), channel_id=1, source_target_pairs={{0,8},{4,12},{8,0},{12,4},{16,24},{20,28},{24,16},{28,20},{1,9},{5... | collective-permute-start | bytes 393224 | tf_op jit(solution)/shard_map/ppermute | solution.py:368
  530.3 45.5 %collective-permute-start.81 = (bf16[128,512]{1,0:T(8,128)(2,1)S(1)}, bf16[128,512]{1,0:T(8,128)(2,1)S(1)}, u32[]{:S(2)}, u32[]{:S(2)}) collective-permute-start(bf16[128,512]{1,0:T(8,128)(2,1)S(1)} %get-tuple-element.581), channel_id=1, source_target_pairs={{0,16},{4,20},{8,24},{12,28},{16,0},{20,4},{24,8},{28,12},{1,17},{... | collective-permute-start | bytes 393224 | tf_op jit(solution)/shard_map/ppermute | solution.py:368
  532.5 48.5 %collective-permute-start.82 = (bf16[128,512]{1,0:T(8,128)(2,1)S(1)}, bf16[128,512]{1,0:T(8,128)(2,1)S(1)}, u32[]{:S(2)}, u32[]{:S(2)}) collective-permute-start(bf16[128,512]{1,0:T(8,128)(2,1)S(1)} %get-tuple-element.580), channel_id=1, source_target_pairs={{0,24},{4,28},{8,16},{12,20},{16,8},{20,12},{24,0},{28,4},{1,25},{... | collective-permute-start | bytes 393224 | tf_op jit(solution)/shard_map/ppermute | solution.py:368
  537.2 56.2 %collective-permute-start.83 = (bf16[512,512]{1,0:T(8,128)(2,1)}, bf16[512,512]{1,0:T(8,128)(2,1)}, u32[]{:S(2)}, u32[]{:S(2)}) collective-permute-start(bf16[512,512]{1,0:T(8,128)(2,1)} %slice.448), channel_id=1, source_target_pairs={{0,2},{1,3},{2,0},{3,1},{4,6},{5,7},{6,4},{7,5},{8,10},{9,11},{10,... | collective-permute-start | bytes 1572872 | tf_op jit(solution)/shard_map/ppermute | solution.py:378
  574.3 19.2 %collective-permute-start.84 = (bf16[1024,256]{1,0:T(8,128)(2,1)}, bf16[1024,256]{1,0:T(8,128)(2,1)}, u32[]{:S(2)}, u32[]{:S(2)}) collective-permute-start(bf16[1024,256]{1,0:T(8,128)(2,1)} %slice.449), channel_id=1, source_target_pairs={{0,2},{1,3},{2,0},{3,1},{4,6},{5,7},{6,4},{7,5},{8,10},{9,11},{10,... | collective-permute-start | bytes 1572872 | tf_op jit(solution)/shard_map/ppermute | solution.py:378
  621.4 41.8 %collective-permute-start.88 = (bf16[3,512,512]{1,2,0:T(8,128)(2,1)}, bf16[3,512,512]{1,2,0:T(8,128)(2,1)}, u32[]{:S(2)}, u32[]{:S(2)}) collective-permute-start(bf16[3,512,512]{1,2,0:T(8,128)(2,1)} %slice.454), channel_id=1, source_target_pairs={{0,4},{4,0},{8,12},{12,8},{16,20},{20,16},{24,28},{28,24},{1,5},{5... | collective-permute-start | bytes 4718600 | tf_op jit(solution)/shard_map/ppermute | solution.py:374
  627.3 22.3 %collective-permute-start.89 = (f32[8,1024]{1,0:T(8,128)}, f32[8,1024]{1,0:T(8,128)}, u32[]{:S(2)}, u32[]{:S(2)}) collective-permute-start(f32[8,1024]{1,0:T(8,128)} %bitcast.93), channel_id=1, source_target_pairs={{0,1},{1,0},{2,3},{3,2},{4,5},{5,4},{6,7},{7,6},{8,9},{9,8},{10,11... | collective-permute-start | bytes 98312 | tf_op jit(solution)/shard_map/ppermute | solution.py:378
  628.8 17.9 %collective-permute-start.90 = (f32[8,192]{1,0:T(8,128)S(1)}, f32[8,192]{1,0:T(8,128)S(1)}, u32[]{:S(2)}, u32[]{:S(2)}) collective-permute-start(f32[8,192]{1,0:T(8,128)S(1)} %squeeze.115), channel_id=1, source_target_pairs={{0,1},{1,0},{2,3},{3,2},{4,5},{5,4},{6,7},{7,6},{8,9},{9,8},{10,11... | collective-permute-start | bytes 18440 | tf_op jit(solution)/shard_map/ppermute | solution.py:378
  630.0 19.5 %collective-permute-start.91 = (f32[8,192]{1,0:T(8,128)}, f32[8,192]{1,0:T(8,128)}, u32[]{:S(2)}, u32[]{:S(2)}) collective-permute-start(f32[8,192]{1,0:T(8,128)} %squeeze.116), channel_id=1, source_target_pairs={{0,1},{1,0},{2,3},{3,2},{4,5},{5,4},{6,7},{7,6},{8,9},{9,8},{10,11... | collective-permute-start | bytes 18440 | tf_op jit(solution)/shard_map/ppermute | solution.py:378
  634.9 28.3 %collective-permute-start.95 = (bf16[512,256]{1,0:T(8,128)(2,1)}, bf16[512,256]{1,0:T(8,128)(2,1)}, u32[]{:S(2)}, u32[]{:S(2)}) collective-permute-start(bf16[512,256]{1,0:T(8,128)(2,1)} %slice.462), channel_id=1, source_target_pairs={{0,4},{4,0},{8,12},{12,8},{16,20},{20,16},{24,28},{28,24},{1,5},{5... | collective-permute-start | bytes 786440 | tf_op jit(solution)/shard_map/ppermute | solution.py:374
  654.9 18.3 %collective-permute-start.102 = (bf16[256,1024]{1,0:T(8,128)(2,1)}, bf16[256,1024]{1,0:T(8,128)(2,1)}, u32[]{:S(2)}, u32[]{:S(2)}) collective-permute-start(bf16[256,1024]{1,0:T(8,128)(2,1)} %get-tuple-element.560), channel_id=1, source_target_pairs={{0,1},{1,0},{2,3},{3,2},{4,5},{5,4},{6,7},{7,6},{8,9},{9,8},{10,11... | collective-permute-start | bytes 1572872 | tf_op jit(solution)/shard_map/ppermute | solution.py:378
  663.2 23.9 %collective-permute-start.104 = (bf16[256,1024]{1,0:T(8,128)(2,1)}, bf16[256,1024]{1,0:T(8,128)(2,1)}, u32[]{:S(2)}, u32[]{:S(2)}) collective-permute-start(bf16[256,1024]{1,0:T(8,128)(2,1)} %get-tuple-element.558), channel_id=1, source_target_pairs={{0,3},{1,2},{2,1},{3,0},{4,7},{5,6},{6,5},{7,4},{8,11},{9,10},{10,... | collective-permute-start | bytes 1572872 | tf_op jit(solution)/shard_map/ppermute | solution.py:378
  667.4 40.9 %collective-permute-start.96 = (bf16[3,512,256]{1,2,0:T(8,128)(2,1)}, bf16[3,512,256]{1,2,0:T(8,128)(2,1)}, u32[]{:S(2)}, u32[]{:S(2)}) collective-permute-start(bf16[3,512,256]{1,2,0:T(8,128)(2,1)} %slice.464), channel_id=1, source_target_pairs={{0,2},{1,3},{2,0},{3,1},{4,6},{5,7},{6,4},{7,5},{8,10},{9,11},{10,... | collective-permute-start | bytes 2359304 | tf_op jit(solution)/shard_map/ppermute | solution.py:378
  669.6 32.7 %collective-permute-start.98 = (f32[8,192]{1,0:T(8,128)S(1)}, f32[8,192]{1,0:T(8,128)S(1)}, u32[]{:S(2)}, u32[]{:S(2)}) collective-permute-start(f32[8,192]{1,0:T(8,128)S(1)} %add.594), channel_id=1, source_target_pairs={{0,2},{1,3},{2,0},{3,1},{4,6},{5,7},{6,4},{7,5},{8,10},{9,11},{10,... | collective-permute-start | bytes 18440 | tf_op jit(solution)/shard_map/ppermute | solution.py:378
  673.2 32.9 %collective-permute-start.97 = (f32[8,1024]{1,0:T(8,128)S(1)}, f32[8,1024]{1,0:T(8,128)S(1)}, u32[]{:S(2)}, u32[]{:S(2)}) collective-permute-start(f32[8,1024]{1,0:T(8,128)S(1)} %bitcast_add_fusion.1), channel_id=1, source_target_pairs={{0,2},{1,3},{2,0},{3,1},{4,6},{5,7},{6,4},{7,5},{8,10},{9,11},{10,... | collective-permute-start | bytes 98312 | tf_op jit(solution)/shard_map/ppermute | solution.py:378
  677.8 28.3 %collective-permute-start.99 = (bf16[128,256]{1,0:T(8,128)(2,1)S(1)}, bf16[128,256]{1,0:T(8,128)(2,1)S(1)}, u32[]{:S(2)}, u32[]{:S(2)}) collective-permute-start(bf16[128,256]{1,0:T(8,128)(2,1)S(1)} %get-tuple-element.588), channel_id=1, source_target_pairs={{0,8},{4,12},{8,0},{12,4},{16,24},{20,28},{24,16},{28,20},{1,9},{5... | collective-permute-start | bytes 196616 | tf_op jit(solution)/shard_map/ppermute | solution.py:368
  687.1 19.0 %collective-permute-start.100 = (bf16[128,256]{1,0:T(8,128)(2,1)S(1)}, bf16[128,256]{1,0:T(8,128)(2,1)S(1)}, u32[]{:S(2)}, u32[]{:S(2)}) collective-permute-start(bf16[128,256]{1,0:T(8,128)(2,1)S(1)} %get-tuple-element.587), channel_id=1, source_target_pairs={{0,16},{4,20},{8,24},{12,28},{16,0},{20,4},{24,8},{28,12},{1,17},{... | collective-permute-start | bytes 196616 | tf_op jit(solution)/shard_map/ppermute | solution.py:368
  724.8 18.6 %collective-permute-start.109 = (f32[1216]{0:T(1024)}, f32[1216]{0:T(1024)S(1)}, u32[]{:S(2)}, u32[]{:S(2)}) collective-permute-start(f32[1216]{0:T(1024)} %get-tuple-element.525), channel_id=1, source_target_pairs={{0,8},{4,12},{8,0},{12,4},{16,24},{20,28},{24,16},{28,20},{1,9},{5... | collective-permute-start | bytes 14600 | tf_op jit(solution)/shard_map/ppermute | solution.py:368
  (288 other events, 3675.8 us)

commit v3 on v2

--- a/solution.py
+++ b/solution.py
@@ -400,46 +400,55 @@
     return values
 
 
-def gather_steps(chain, shard, order):
-    rows = shard
-    for axis in order:
-        if axis == "z":
-            arrived = yield [swap_z(rows, step) for step in range(1, ZS)]
-            rows = jnp.concatenate([rows] + arrived, 0)
-        elif axis == "y":
-            arrived = yield [swap_y(rows)]
-            rows = jnp.concatenate([rows] + arrived, 0)
-        else:
-            arrived = yield [swap_mp(rows, 2)]
-            rows = jnp.concatenate([rows] + arrived, 1)
-    chain.own = rows
-    arrived = yield [swap_mp(rows, 1)]
-    return (rows, arrived[0])
+def join(rows, arrived, axis):
+    return jnp.concatenate([rows, arrived], -2 if axis == "y" else -1)
+
+
+def swap_plane(part, axis):
+    return swap_y(part) if axis == "y" else swap_mp(part, 2)
+
+
+def rows_z_steps(chain, shard):
+    arrived = yield [swap_z(shard, step) for step in range(1, ZS)]
+    return jnp.concatenate([shard] + arrived, 0)
+
+
+def gather_steps(chain, parts, orders):
+    for axes in zip(*orders):
+        arrived = yield [swap_plane(part, axis) for part, axis in zip(parts, axes)]
+        parts = [join(part, each, axis) for part, each, axis in zip(parts, arrived, axes)]
+    chain.own = parts
+    arrived = yield [swap_mp(part, 1) for part in parts]
+    return arrived
 
 
 def add_low(first, second):
     return (first.astype(F32) + second.astype(F32)).astype(BF)
 
 
-def reduce_steps(chain, other_part, order):
-    arrived = yield [swap_mp(other_part, 1)]
-    total = add_low(chain.own, arrived[0])
-    for axis in order:
-        rows, width = total.shape[-2:]
-        if axis == "z":
-            rows = rows // ZS
-            arrived = yield [
-                swap_z(total[..., step * rows : (step + 1) * rows, :], step) for step in range(1, ZS)
-            ]
-            total = total[..., :rows, :].astype(F32)
-            for each in arrived:
-                total = total + each.astype(F32)
-        elif axis == "y":
-            arrived = yield [swap_y(total[..., rows // 2 :, :])]
-            total = add_low(total[..., : rows // 2, :], arrived[0])
-        else:
-            arrived = yield [swap_mp(total[..., width // 2 :], 2)]
-            total = add_low(total[..., : width // 2], arrived[0])
+def halve(total, axis):
+    rows, width = total.shape[-2:]
+    if axis == "y":
+        return (total[..., : rows // 2, :], total[..., rows // 2 :, :])
+    return (total[..., : width // 2], total[..., width // 2 :])
+
+
+def reduce_steps(chain, other_parts, orders):
+    arrived = yield [swap_mp(part, 1) for part in other_parts]
+    totals = [add_low(own, each) for own, each in zip(chain.own, arrived)]
+    for axes in zip(*orders):
+        halves = [halve(total, axis) for total, axis in zip(totals, axes)]
+        arrived = yield [swap_plane(half[1], axis) for half, axis in zip(halves, axes)]
+        totals = [add_low(half[0], each) for half, each in zip(halves, arrived)]
+    return totals
+
+
+def sum_z_steps(chain, total):
+    rows = total.shape[0] // ZS
+    arrived = yield [swap_z(total[step * rows : (step + 1) * rows], step) for step in range(1, ZS)]
+    total = total[:rows].astype(F32)
+    for each in arrived:
+        total = total + each.astype(F32)
     return total
 
 
@@ -458,11 +467,9 @@
 
 
 def small_reduce_steps(chain, vector_part, bias_part):
-    arrived = yield [swap_mp(vector_part, 1), swap_mp(bias_part[1], 1), swap_mp(bias_part[3], 1)]
-    vector_part = vector_part + arrived[0]
-    even, odd = (bias_part[0] + arrived[1], bias_part[2] + arrived[2])
-    arrived = yield [swap_mp(vector_part, 2), swap_mp(odd, 2)]
-    total = jnp.concatenate([vector_part + arrived[0], even + arrived[1]], 1)
+    packed = [jnp.concatenate([vector_part, each], 1) for each in bias_part]
+    arrived = yield [swap_mp(packed[step], step) for step in range(1, MP)]
+    total = (packed[0] + arrived[0]) + (arrived[1] + arrived[2])
     arrived = yield [swap_y(total[ZS:])]
     total = total[:ZS] + arrived[0]
     arrived = yield [swap_z(total[step], step) for step in range(1, ZS)]
@@ -584,32 +591,35 @@
             grad_query = query_part if head == 0 else grad_query + query_part
             grad_keys = key_part if head == 0 else grad_keys + key_part
             grad_values = value_part if head == 0 else grad_values + value_part
-        out_ref[0, rows, :] = (grad_query * factor).astype(BF)
+        out_ref[rows, 0:LANES] = (grad_query * factor).astype(BF)
         if block == 0:
             dk_acc[...] = grad_keys
             dv_acc[...] = grad_values
         else:
             dk_acc[...] += grad_keys
             dv_acc[...] += grad_values
-    out_ref[1] = dk_acc[...].astype(BF)
-    out_ref[2] = dv_acc[...].astype(BF)
-
-
-def pair_spec(rows):
-    return pl.BlockSpec((rows, LANES), lambda p: (0, p))
-
-
-def attend(queries, key_rows, values):
-    rows, width = values.shape
-    pairs = width // LANES
+    out_ref[:, LANES : 2 * LANES] = dk_acc[...].astype(BF)
+    out_ref[:, 2 * LANES : 3 * LANES] = dv_acc[...].astype(BF)
+
+
+def kind_spec(rows, kind):
+    return pl.BlockSpec((rows, LANES), lambda p: (0, p * 3 + kind))
+
+
+def attend(heads):
+    rows, width = heads.shape
+    pairs = width // LANES // 3
     scores_size = rows * rows * 2 * pairs
     return pl.pallas_call(
         functools.partial(attend_kernel, 256),
         grid=(pairs,),
-        in_specs=[pair_spec(rows)] * 3,
-        out_specs=[pair_spec(rows), pl.BlockSpec((1, 8, rows), lambda p: (p, 0, 0))],
+        in_specs=[kind_spec(rows, kind) for kind in range(3)],
+        out_specs=[
+            pl.BlockSpec((rows, LANES), lambda p: (0, p)),
+            pl.BlockSpec((1, 8, rows), lambda p: (p, 0, 0)),
+        ],
         out_shape=[
-            jax.ShapeDtypeStruct((rows, width), BF),
+            jax.ShapeDtypeStruct((rows, pairs * LANES), BF),
             jax.ShapeDtypeStruct((pairs, 8, rows), F32),
         ],
         compiler_params=pltpu.CompilerParams(vmem_limit_bytes=32 * 2**20),
@@ -617,26 +627,30 @@
             flops=scores_size * 2 * 512, bytes_accessed=rows * width * 8, transcendentals=scores_size
         ),
         name="attend",
-    )(queries, key_rows, values)
-
-
-def attend_back(queries, key_rows, values, grad_blended, log_total):
-    rows, width = values.shape
-    pairs = width // LANES
+    )(heads, heads, heads)
+
+
+def attend_back(heads, grad_blended, log_total):
+    rows, width = heads.shape
+    pairs = width // LANES // 3
     scores_size = rows * rows * 2 * pairs
     return pl.pallas_call(
         functools.partial(attend_back_kernel, 256),
         grid=(pairs,),
-        in_specs=[pair_spec(rows)] * 4 + [pl.BlockSpec((1, 8, rows), lambda p: (p, 0, 0))],
-        out_specs=pl.BlockSpec((3, rows, LANES), lambda p: (0, 0, p)),
-        out_shape=jax.ShapeDtypeStruct((3, rows, width), BF),
+        in_specs=[kind_spec(rows, kind) for kind in range(3)]
+        + [
+            pl.BlockSpec((rows, LANES), lambda p: (0, p)),
+            pl.BlockSpec((1, 8, rows), lambda p: (p, 0, 0)),
+        ],
+        out_specs=pl.BlockSpec((rows, 3 * LANES), lambda p: (0, p)),
+        out_shape=jax.ShapeDtypeStruct((rows, width), BF),
         scratch_shapes=[pltpu.VMEM((rows, LANES), F32)] * 2,
         compiler_params=pltpu.CompilerParams(vmem_limit_bytes=32 * 2**20),
         cost_estimate=pl.CostEstimate(
             flops=scores_size * 2 * 1280, bytes_accessed=rows * width * 14, transcendentals=scores_size
         ),
         name="attend_back",
-    )(queries, key_rows, values, grad_blended, log_total)
+    )(heads, heads, heads, grad_blended, log_total)
 
 
 def dot_nn(left, right):
@@ -724,26 +738,31 @@
         [vectors.astype(BF).reshape(-1), head_biases.astype(BF).reshape(-1)]
     ).reshape(1, -1)
     vector_size = vectors.size
-    qkv_low = qkv_weight.astype(BF)
-    up_low = up_weight.astype(BF)
-    down_low = down_weight.transpose(2, 0, 1).astype(BF)
-    out_low = out_weight.T.astype(BF)
-    up_shards = [up_low[:, at : at + half_units].reshape(depth, -1) for at in (0, half_units)]
-    down_shards = [down_low[:, at : at + half_units].reshape(depth, -1) for at in (0, half_units)]
-
+    kinds = qkv_weight.shape[0]
+    qkv_shard = qkv_weight.astype(BF).reshape(kinds, depth, 2, LANES).transpose(1, 2, 0, 3)
+    qkv_shard = qkv_shard.reshape(depth, -1)
+    rest_shard = jnp.concatenate(
+        [
+            out_weight.T.astype(BF),
+            up_weight.astype(BF).reshape(depth, -1),
+            down_weight.transpose(2, 0, 1).astype(BF).reshape(depth, -1),
+        ],
+        1,
+    )
+    both = ("xy", "yx")
     small = Chain(small_steps, small_shard, vector_size)
-    get_q = Chain(gather_steps, qkv_low[0], "zxy")
-    get_k = Chain(gather_steps, qkv_low[1], "zxy")
-    get_v = Chain(gather_steps, qkv_low[2], "zyx")
+    rows_qkv = Chain(rows_z_steps, qkv_shard)
     fetch_tokens = fetch_image(tokens)
-    out_low, up_shards, down_shards = meet((out_low, up_shards, down_shards), small, get_q, get_k, get_v)
-    get_out = Chain(gather_steps, out_low, "zyx")
-    up_shards, down_shards = meet((up_shards, down_shards), small, get_q, get_k, get_v, get_out)
-    get_up = [Chain(gather_steps, up_shards[0], "zxy"), None]
-    tokens, down_shards, up_shards = meet(
-        (tokens, down_shards, up_shards), small, fetch_tokens, get_k, get_q
-    )
-    get_up[1] = Chain(gather_steps, up_shards[1], "zxy")
+    rest_shard = meet(rest_shard, small, rows_qkv)
+    rows_rest = Chain(rows_z_steps, rest_shard)
+    get_qkv = Chain(gather_steps, jnp.split(rows_qkv.result, 2, 1), both)
+    meet((), small, get_qkv)
+    tokens = meet(tokens, small, fetch_tokens, rows_rest)
+    out_rows, up_rows, down_rows = jnp.split(
+        rows_rest.result, [block_width, block_width * (1 + units)], 1
+    )
+    get_out = Chain(gather_steps, [jnp.stack(jnp.split(out_rows, 2, 1))], ("yx",))
+    get_up = Chain(gather_steps, jnp.split(up_rows, 2, 1), both)
 
     vector_full, bias_small = small.result
     vector_full = vector_full.reshape(DP, vectors.shape[0], LANES).transpose(1, 0, 2)
@@ -757,123 +776,106 @@
     base = assemble_image(place, tokens[:, 0], fetch_tokens.result).astype(F32)
     normal_one, spread_one = norm_parts(base)
     normed_one = (normal_one * gain_one + shift_one).astype(BF)
-    normed_one = meet(normed_one, get_v, get_up[0], get_out)
+    normed_one = meet(normed_one, get_qkv, get_up, get_out)
 
     def project(core, weights):
-        w_q, w_k, w_v = weights
-        return (
-            (dot_nn(normed_one, w_q) + bias_full[core, 0].reshape(-1)).astype(BF),
-            dot_nn(normed_one, w_k).astype(BF),
-            (dot_nn(normed_one, w_v) + bias_full[core, 1].reshape(-1)).astype(BF),
-        )
+        results = []
+        for half in (0, 1):
+            lanes = slice(half * LANES, (half + 1) * LANES)
+            zero = jnp.zeros((2, LANES), F32)
+            bias = jnp.stack([bias_full[core, 0, :, lanes], zero, bias_full[core, 1, :, lanes]], 1)
+            results.append((dot_nn(normed_one, weights[half]) + bias.reshape(-1)).astype(BF))
+        return results
 
     heads, blended, log_total = ([None, None], [None, None], [None, None])
-    heads[0] = project(0, (get_q.own, get_k.own, get_v.own))
-    heads[0] = meet(heads[0], get_q, get_k, get_v, get_up[1])
-    blended[0], log_total[0] = attend(*heads[0])
-    blended[0], normed_one, down_shards, cotangent = meet(
-        (blended[0], normed_one, down_shards, cotangent), get_up[0], get_out
-    )
-    get_down = [Chain(gather_steps, down_shards[0], "zxy"), None]
-    heads[1] = project(1, (get_q.result[1], get_k.result[1], get_v.result[1]))
-    blended[1], log_total[1] = attend(*heads[1])
-    blended, down_shards = meet((blended, down_shards), get_up[0], get_up[1], get_out, get_down[0])
-    get_down[1] = Chain(gather_steps, down_shards[1], "zxy")
-    w_out = get_out.result
-    branch_one = dot_nt(blended[0], w_out[0]) + dot_nt(blended[1], w_out[1]) + out_bias
+    heads[0] = project(0, get_qkv.own)
+    heads[0] = meet(heads[0], get_qkv, get_out)
+    w_qkv = [get_qkv.own, get_qkv.result]
+    blended[0], log_total[0] = zip(*[attend(each) for each in heads[0]])
+    blended[0], normed_one, down_rows, cotangent = meet(
+        (blended[0], normed_one, down_rows, cotangent), get_up, get_out
+    )
+    get_down = Chain(gather_steps, jnp.split(down_rows, 2, 1), both)
+    fetch_cotangent = fetch_image(cotangent)
+    heads[1] = project(1, w_qkv[1])
+    blended[1], log_total[1] = zip(*[attend(each) for each in heads[1]])
+    blended = meet(blended, get_up, get_down)
+    w_up = [get_up.own, get_up.result]
+    blended = [jnp.concatenate(each, 1) for each in blended]
+    w_out = [jnp.concatenate([each[0][0], each[0][1]], 1) for each in (get_out.own, get_out.result)]
+    branch_one = dot_nt(jnp.concatenate(blended, 1), jnp.concatenate(w_out, 1)) + out_bias
     hidden = base + scale_one * branch_one
     normal_two, spread_two = norm_parts(hidden)
     normed_two = (normal_two * gain_two + shift_two).astype(BF)
-    normed_two, cotangent = meet(
-        (normed_two, cotangent), get_up[0], get_up[1], get_down[0], get_down[1]
-    )
-    fetch_cotangent = fetch_image(cotangent)
-    w_up = [get_up[0].result, None]
-    activ, slope = ({}, {})
-
-    def expand(half, core):
-        rows = bias_full[core, 2 + half * half_units : 2 + (half + 1) * half_units]
-        pre_act = dot_nn(normed_two, w_up[half][core]) + rows.transpose(1, 0, 2).reshape(-1)
-        activ[half, core], slope[half, core] = gelu_pair(pre_act)
-
-    expand(0, 0)
-    expand(0, 1)
-    activ, normed_two, slope = meet((activ, normed_two, slope), get_up[1], get_down[0])
-    w_up[1] = get_up[1].result
-    expand(1, 0)
-    expand(1, 1)
-    activ, slope, cotangent = meet(
-        (activ, slope, cotangent), get_down[0], get_down[1], fetch_cotangent
-    )
-
+    normed_two = meet(normed_two, fetch_cotangent)
     grad_out = assemble_image(place, cotangent[:, 0], fetch_cotangent.result).astype(F32)
     grad_branch = (grad_out * scale_two).astype(BF)
-    sum_down, sum_up = ([None, None], [None, None])
-
-    def grads_down(half):
-        sum_down[half] = Chain(reduce_steps, dot_tn(grad_branch, activ[half, 1]).astype(BF), "yxz")
-        sum_down[half].own = dot_tn(grad_branch, activ[half, 0]).astype(BF)
-
-    grads_down(0)
-    grad_branch, activ = meet((grad_branch, activ), sum_down[0], get_down[1])
-    grads_down(1)
-    activ = meet(activ, get_down[1])
-    w_down = [get_down[0].result, get_down[1].result]
+    parts = [(half, core) for core in (1, 0) for half in (0, 1)]
+    activ, slope = ({}, {})
+    for half, core in parts:
+        rows = bias_full[core, 2 + half * half_units : 2 + (half + 1) * half_units]
+        pre_act = dot_nn(normed_two, w_up[core][half]) + rows.transpose(1, 0, 2).reshape(-1)
+        activ[half, core], slope[half, core] = gelu_pair(pre_act)
+    activ, slope, grad_branch = meet((activ, slope, grad_branch), get_down)
+
+    def reduce_pairs(left, rights):
+        chain = Chain(reduce_steps, [dot_tn(left, rights[half, 1]).astype(BF) for half in (0, 1)], both[::-1])
+        chain.own = [dot_tn(left, rights[half, 0]).astype(BF) for half in (0, 1)]
+        return chain
+
+    sum_down = reduce_pairs(grad_branch, activ)
+    grad_branch, activ = meet((grad_branch, activ), sum_down, get_down)
+    w_down = [get_down.own, get_down.result]
     branch_two = down_bias
-    for half in (0, 1):
-        for core in cores:
-            branch_two = branch_two + dot_nt(activ[half, core], w_down[half][core])
+    for half, core in parts:
+        branch_two = branch_two + dot_nt(activ[half, core], w_down[core][half])
     output = (hidden + scale_two * branch_two).astype(BF)
-    grad_branch, output, normed_two = meet((grad_branch, output, normed_two), sum_down[1])
+    output, grad_branch, slope = meet((output, grad_branch, slope))
     send_output = send_back(output)
     grad_pre = {}
-
-    def grads_up(half):
-        for core in (1, 0):
-            grad_activ = dot_nn(grad_branch, w_down[half][core])
-            grad_pre[half, core] = (grad_activ * slope[half, core].astype(F32)).astype(BF)
-        sum_up[half] = Chain(reduce_steps, dot_tn(normed_two, grad_pre[half, 1]).astype(BF), "yxz")
-        sum_up[half].own = dot_tn(normed_two, grad_pre[half, 0]).astype(BF)
-
-    grads_up(0)
-    grad_branch, normed_two, grad_pre = meet((grad_branch, normed_two, grad_pre), sum_down[0], sum_up[0])
-    grads_up(1)
+    for half, core in parts:
+        grad_activ = dot_nn(grad_branch, w_down[core][half])
+        grad_pre[half, core] = (grad_activ * slope[half, core].astype(F32)).astype(BF)
+    grad_pre, normed_two = meet((grad_pre, normed_two), sum_down)
+    sum_up = reduce_pairs(normed_two, grad_pre)
     grad_normed_two = 0.0
-    for half in (0, 1):
-        for core in cores:
-            grad_normed_two = grad_normed_two + dot_nt(grad_pre[half, core], w_up[half][core])
+    for half, core in parts:
+        grad_normed_two = grad_normed_two + dot_nt(grad_pre[half, core], w_up[core][half])
     grad_hidden, grad_gain_two, grad_shift_two = norm_back(
         grad_normed_two, normal_two, spread_two, gain_two
     )
     grad_hidden = grad_out + grad_hidden
     grad_projected = (grad_hidden * scale_one).astype(BF)
-    grad_projected = meet(
-        grad_projected, sum_down[0], sum_down[1], sum_up[0], sum_up[1], send_output
-    )
-    sum_out = Chain(reduce_steps, dot_tn(grad_projected, blended[1]).astype(BF), "xyz")
-    sum_out.own = dot_tn(grad_projected, blended[0]).astype(BF)
-    sums_qkv = None
-    grad_heads = [None, None]
-
-    def back_heads(core):
-        grad_blended = dot_nn(grad_projected, w_out[core]).astype(BF)
-        grad_heads[core] = attend_back(*heads[core], grad_blended, log_total[core])
-        return jnp.einsum(
-            "sd,tse->tde", normed_one, grad_heads[core], preferred_element_type=F32
-        ).astype(BF)
-
-    grad_other = back_heads(1)
-    grad_other, grad_projected = meet(
-        (grad_other, grad_projected), sum_down[0], sum_down[1], sum_up[0], sum_up[1], sum_out
-    )
-    sum_qkv = Chain(reduce_steps, grad_other, "yxz")
-    sum_qkv.own = back_heads(0)
-    grad_heads, normed_one = meet((grad_heads, normed_one), sum_qkv, sum_up[0], sum_up[1], sum_out, sum_down[1])
-    weights = [[each.own for each in (get_q, get_k, get_v)], [each.result[1] for each in (get_q, get_k, get_v)]]
+    grad_projected = meet(grad_projected, sum_up, sum_down, send_output)
+    rows_down = Chain(sum_z_steps, jnp.concatenate(sum_down.result, 1))
+    grad_w_out = [jnp.stack(jnp.split(dot_tn(grad_projected, each).astype(BF), 2, 1)) for each in blended]
+    sum_out = Chain(reduce_steps, [grad_w_out[1]], ("xy",))
+    sum_out.own = [grad_w_out[0]]
+    grad_blended = [jnp.split(dot_nn(grad_projected, each).astype(BF), 2, 1) for each in w_out]
+    grad_heads = [[None, None], [None, None]]
+
+    def back_heads(core, half):
+        grad_heads[core][half] = attend_back(
+            heads[core][half], grad_blended[core][half], log_total[core][half]
+        )
+        return dot_tn(normed_one, grad_heads[core][half]).astype(BF)
+
+    other = back_heads(1, 0)
+    other, grad_blended = meet((other, grad_blended), sum_up, sum_out, rows_down)
+    sum_qkv = [Chain(reduce_steps, [other], ("yx",)), None]
+    sum_qkv[0].own = [back_heads(0, 0)]
+    grad_heads[0][0], grad_blended = meet((grad_heads[0][0], grad_blended), sum_qkv[0], sum_out, sum_up)
+    other = back_heads(1, 1)
+    other, grad_blended = meet((other, grad_blended), sum_out)
+    sum_qkv[1] = Chain(reduce_steps, [other], ("xy",))
+    out_rows = jnp.concatenate([sum_out.result[0][0], sum_out.result[0][1]], 1)
+    rows_rest = Chain(sum_z_steps, jnp.concatenate(sum_up.result + [out_rows], 1))
+    sum_qkv[1].own = [back_heads(0, 1)]
+    grad_heads = meet(grad_heads, sum_qkv[0], sum_qkv[1])
     grad_normed_one = 0.0
     for core in cores:
-        for kind in range(3):
-            grad_normed_one = grad_normed_one + dot_nt(grad_heads[core][kind], weights[core][kind])
+        for half in (0, 1):
+            grad_normed_one = grad_normed_one + dot_nt(grad_heads[core][half], w_qkv[core][half])
     grad_input, grad_gain_one, grad_shift_one = norm_back(
         grad_normed_one, normal_one, spread_one, gain_one
     )
@@ -894,9 +896,10 @@
     grad_vectors = grad_vectors.reshape(-1, DP, LANES).transpose(1, 0, 2).reshape(DP, -1)
     bias_parts = []
     for core in cores:
-        rows = [
-            jnp.sum(grad_heads[core][kind].astype(F32), 0).reshape(2, block_width) for kind in (0, 2)
+        head_part = [
+            jnp.sum(each.astype(F32), 0).reshape(2, kinds, LANES) for each in grad_heads[core]
         ]
+        rows = [jnp.concatenate([each[:, kind] for each in head_part], 1) for kind in (0, 2)]
         for half in (0, 1):
             unit_part = jnp.sum(grad_pre[half, core].astype(F32), 0)
             unit_part = unit_part.reshape(2, half_units, block_width)
@@ -906,23 +909,28 @@
     grad_biases = jnp.take(grad_biases, place[:DP], axis=1).reshape(MP, DP, -1)
     sum_small = Chain(small_reduce_steps, grad_vectors, grad_biases)
     send_grad = send_back(grad_input)
-    grad_input = meet(grad_input, sum_qkv, sum_small, sum_up[1], sum_out)
-    grad_input = meet(grad_input, sum_qkv, sum_small, sum_out, send_grad)
-    grad_input = meet(grad_input, sum_qkv, sum_small)
-    meet((), sum_small)
+    meet((), sum_qkv[0], sum_qkv[1], sum_small, rows_rest)
+    meet((), sum_qkv[1], sum_small)
+    rows_qkv = Chain(sum_z_steps, jnp.concatenate(sum_qkv[0].result + sum_qkv[1].result, 1))
+    meet((), rows_qkv, sum_small, send_grad)
     layer_output = spread_image(place, output[:chunk_rows], send_output.result, BF)[:, None]
     input_grad = spread_image(place, grad_input[:chunk_rows], send_grad.result, F32)[:, None]
 
     small_total = sum_small.result
     vector_grad = small_total[:vector_size].reshape(vectors.shape)
     bias_grad = small_total[vector_size:].reshape(head_biases.shape)
-    up_grad = jnp.concatenate(
-        [each.result.reshape(depth, half_units, block_width) for each in sum_up], 1
-    )
-    down_grad = jnp.concatenate(
-        [each.result.reshape(depth, half_units, block_width) for each in sum_down], 1
-    ).transpose(1, 2, 0)
-    grads = (sum_qkv.result, sum_out.result.T, up_grad, down_grad, bias_grad, vector_grad)
+    qkv_grad = rows_qkv.result.reshape(depth, 2, kinds, LANES).transpose(2, 0, 1, 3)
+    up_size = block_width * units
+    up_grad = rows_rest.result[:, :up_size].reshape(depth, units, block_width)
+    down_grad = rows_down.result.reshape(depth, units, block_width).transpose(1, 2, 0)
+    grads = (
+        qkv_grad.reshape(qkv_weight.shape),
+        rows_rest.result[:, up_size:].T,
+        up_grad,
+        down_grad,
+        bias_grad,
+        vector_grad,
+    )
     params = (qkv_weight, out_weight, up_weight, down_weight, head_biases, vectors)
     firsts = (qkv_first, out_first, up_first, down_first, bias_first, vector_first)
     seconds = (qkv_second, out_second, up_second, down_second, bias_second, vector_second)

time: 752 us -> 674 us (0.90)
  waiting for transfers between devices: 180 us -> 110 us
  starting transfers between devices: 118 us -> 94.2 us
  matrix products: 147 us -> 168 us
  local copies, waits for them, and re-layouts: 82.1 us -> 66 us
  other arithmetic: 88.5 us -> 98.3 us
    ppermute x16, waiting for transfers between devices: 67 us -> 22 us  [swap_y(): return lax.ppermute(part, 'dp', [(each, each ^ 1) for each in range(DP)])]
    ppermute x48 -> x46, waiting for transfers between devices: 78.3 us -> 38.3 us  [swap_mp(): return lax.ppermute(part, 'mp', [(each, each ^ step) for each in range(MP)])]
    ppermute x48 -> x21, starting transfers between devices: 69.5 us -> 47.6 us  [swap_z(): lax.ppermute(part, 'dp', [(z * YS + y, (z ^ step) * YS + y) for z in rang...]
    concatenate x19 -> x22, other arithmetic: 8.51 us -> 25.6 us  [the longest x14 21.6 us: join(): return jnp.concatenate([rows, arrived], -2 if axis == 'y' else -1)]
    dot_general x16 -> x13, matrix products: 49.5 us -> 64.5 us  [dot_nt(): lax.dot_general(left, right, (((1,), (1,)), ((), ())), preferred_element_...]
    ppermute x48 -> x21, waiting for transfers between devices: 34.7 us -> 49.2 us  [swap_z(): lax.ppermute(part, 'dp', [(z * YS + y, (z ^ step) * YS + y) for z in rang...]
    unnamed x529 -> x396, local copies, waits for them, and re-layouts: 44.3 us -> 30.1 us
    dot_general x2 -> x0, matrix products: 10 us -> none  [back_heads(): jnp.einsum('sd,tse->tde', normed_one, grad_heads[core], preferred_element...]
  transfers between devices with their start and end apart: 112 -> 83, of which waited for: 30 -> 18; matrix products, arithmetic and copies ran while one was open for 33% -> 44% of each run, Pallas kernels for 16% -> 18%
where the time goes in v3:
time: 674 us; the launch traced here: 667 us
  matrix products  168 us (25%)
  Pallas kernels  127 us (19%)
  waiting for transfers between devices  110 us (16%)
  other arithmetic  98.3 us (15%)
  starting transfers between devices  94.2 us (14%)
  local copies, waits for them, and re-layouts  66 us (10%)
    dot_general x13, matrix products, dot_nt(): lax.dot_general(left, right, (((1,), (1,)), ((), ())), preferred_element_...  64.5 us
    pallas_call x4, Pallas kernels, attend_back(): pl.pallas_call(functools.partial(attend_back_kernel, 256), grid=(pairs,),...  63.9 us
    dot_general x14, matrix products, dot_nn(): lax.dot_general(left, right, (((1,), (0,)), ((), ())), preferred_element_...  61.4 us
    ppermute x21, waiting for transfers between devices, swap_z(): lax.ppermute(part, 'dp', [(z * YS + y, (z ^ step) * YS + y) for z in rang...  49.2 us
    ppermute x21, starting transfers between devices, swap_z(): lax.ppermute(part, 'dp', [(z * YS + y, (z ^ step) * YS + y) for z in rang...  47.6 us
    dot_general x14, matrix products, dot_tn(): lax.dot_general(left, right, (((0,), (0,)), ((), ())), preferred_element_...  42.2 us
    ppermute x46, waiting for transfers between devices, swap_mp(): return lax.ppermute(part, 'mp', [(each, each ^ step) for each in range(MP)])  38.3 us
    pallas_call x4, Pallas kernels, attend(): pl.pallas_call(functools.partial(attend_kernel, 256), grid=(pairs,), in_s...  36.1 us
  transfers between devices with their start and end apart: 83, of which 18 were waited for; matrix products, arithmetic and copies ran while one was open for 44% of the time, Pallas kernels for 18%

profile of v3, /device:TPU:0, one launch (start us, length us, event | category | flops | bytes accessed | tf_op | source)
XLA Modules:
  0.0 667.0 jit_solution(739827173112092370)
XLA Ops:
  3.4 3.0 collective-permute-start.3
  11.5 3.5 collective-permute-start.1
  23.8 3.3 collective-permute-done.1
  34.7 7.1 %collective-permute-done.6 = bf16[4,1216]{1,0:T(4,128)(2,1)S(1)} collective-permute-done((bf16[4,1216]{1,0:T(4,128)(2,1)S(1)}, bf16[4,1216]{1,0:T(4,128)(2,1)S(1)}, u32[]{:S(2)}, u32[]{:S(2)}) %collective-permute-start.6) | collective-permute-done | bytes 9760 | tf_op jit(solution)/shard_map/ppermute | solution.py:374
  42.0 8.5 %collective-permute-done.7 = bf16[512,384]{0,1:T(8,128)(2,1)S(1)} collective-permute-done((bf16[512,384]{0,1:T(8,128)(2,1)S(1)}, bf16[512,384]{0,1:T(8,128)(2,1)S(1)}, u32[]{:S(2)}, u32[]{:S(2)}) %collective-permute-start.7) | collective-permute-done | bytes 393248 | tf_op jit(solution)/shard_map/ppermute | solution.py:378
  68.4 7.9 %collective-permute-done.15 = bf16[128,2304]{0,1:T(8,128)(2,1)} collective-permute-done((bf16[128,2304]{0,1:T(8,128)(2,1)}, bf16[128,2304]{0,1:T(8,128)(2,1)}, u32[]{:S(2)}, u32[]{:S(2)}) %collective-permute-start.15) | collective-permute-done | bytes 589856 | tf_op jit(solution)/shard_map/ppermute | solution.py:368
  76.3 18.3 %collective-permute-done.16 = bf16[128,2304]{0,1:T(8,128)(2,1)} collective-permute-done((bf16[128,2304]{0,1:T(8,128)(2,1)}, bf16[128,2304]{0,1:T(8,128)(2,1)}, u32[]{:S(2)}, u32[]{:S(2)}) %collective-permute-start.16) | collective-permute-done | bytes 589856 | tf_op jit(solution)/shard_map/ppermute | solution.py:368
  102.6 6.7 %assemble_image.2 = bf16[1024,1024]{1,0:T(8,128)(2,1)} custom-call(s32[9]{0:T(128)} %stack.214.place_ref, bf16[4,256,1024]{2,1,0:T(8,128)(2,1)} %bitcast.324, bf16[256,1024]{1,0:T(8,128)(2,1)} %collective-permute-done.12.refs_0_, bf16[256,1024]{1,0:T(8,128)(2,1)} %collective-permute-done.13.refs_1_, bf16[256,1024]{1,0:T(8,128)(2,1)} %collective-permute-done.14.refs_2_), custom_call_target="tpu_custom_call" | custom-call | tf_op jit(solution)/shard_map/assemble_image/pallas_call | solution.py:492
  115.8 2.8 pad_maximum_fusion.5
  131.1 3.0 add_convert_fusion.10.q_ref.k_ref.v_ref
  134.1 3.5 add_convert_fusion.11.q_ref.k_ref.v_ref
  137.6 3.1 collective-permute-done.25
  142.0 8.8 %attend.4 = (bf16[1024,256]{1,0:T(8,128)(2,1)S(1)}, f32[2,8,1024]{2,1,0:T(8,128)S(1)}) custom-call(bf16[1024,768]{1,0:T(8,128)(2,1)S(1)} %add_convert_fusion.11.q_ref.k_ref.v_ref, bf16[1024,768]{1,0:T(8,128)(2,1)S(1)} %add_convert_fusion.11.q_ref.k_ref.v_ref, bf16[1024,768]{1,0:T(8,128)(2,1)S(1)} %add_convert_fusion.11.q_ref.k_ref.v_ref), custom_call_target="tpu_custom_call" | custom-call | flops 4294967296 | bytes 6291456 | tf_op jit(solution)/shard_map/attend/pallas_call | solution.py:613
  150.9 9.4 %attend.5 = (bf16[1024,256]{1,0:T(8,128)(2,1)S(1)}, f32[2,8,1024]{2,1,0:T(8,128)S(1)}) custom-call(bf16[1024,768]{1,0:T(8,128)(2,1)S(1)} %add_convert_fusion.10.q_ref.k_ref.v_ref, bf16[1024,768]{1,0:T(8,128)(2,1)S(1)} %add_convert_fusion.10.q_ref.k_ref.v_ref, bf16[1024,768]{1,0:T(8,128)(2,1)S(1)} %add_convert_fusion.10.q_ref.k_ref.v_ref), custom_call_target="tpu_custom_call" | custom-call | flops 4294967296 | bytes 6291456 | tf_op jit(solution)/shard_map/attend/pallas_call | solution.py:613
  167.5 3.6 add_convert_fusion.8.q_ref.k_ref.v_ref
  171.1 8.8 %attend.7 = (bf16[1024,256]{1,0:T(8,128)(2,1)S(1)}, f32[2,8,1024]{2,1,0:T(8,128)S(1)}) custom-call(bf16[1024,768]{1,0:T(8,128)(2,1)S(1)} %add_convert_fusion.8.q_ref.k_ref.v_ref, bf16[1024,768]{1,0:T(8,128)(2,1)S(1)} %add_convert_fusion.8.q_ref.k_ref.v_ref, bf16[1024,768]{1,0:T(8,128)(2,1)S(1)} %add_convert_fusion.8.q_ref.k_ref.v_ref), custom_call_target="tpu_custom_call" | custom-call | flops 4294967296 | bytes 6291456 | tf_op jit(solution)/shard_map/attend/pallas_call | solution.py:613
  180.0 3.4 add_convert_fusion.9.q_ref.k_ref.v_ref
  183.4 9.0 %attend.6 = (bf16[1024,256]{1,0:T(8,128)(2,1)S(1)}, f32[2,8,1024]{2,1,0:T(8,128)S(1)}) custom-call(bf16[1024,768]{1,0:T(8,128)(2,1)S(1)} %add_convert_fusion.9.q_ref.k_ref.v_ref, bf16[1024,768]{1,0:T(8,128)(2,1)S(1)} %add_convert_fusion.9.q_ref.k_ref.v_ref, bf16[1024,768]{1,0:T(8,128)(2,1)S(1)} %add_convert_fusion.9.q_ref.k_ref.v_ref), custom_call_target="tpu_custom_call" | custom-call | flops 4294967296 | bytes 6291456 | tf_op jit(solution)/shard_map/attend/pallas_call | solution.py:613
  198.9 4.5 fusion.102
  207.3 10.4 %collective-permute-done.35.refs_2_ = bf16[256,1024]{1,0:T(8,128)(2,1)S(1)} collective-permute-done((bf16[256,1024]{1,0:T(8,128)(2,1)S(1)}, bf16[256,1024]{1,0:T(8,128)(2,1)S(1)}, u32[]{:S(2)}, u32[]{:S(2)}) %collective-permute-start.35) | collective-permute-done | bytes 524320 | tf_op jit(solution)/shard_map/ppermute | solution.py:378
  217.7 8.1 %fusion.28 = (bf16[1024,1024]{1,0:T(8,128)(2,1)}, bf16[1024,1024]{1,0:T(8,128)(2,1)}) fusion(f32[1024]{0:T(1024)S(1)} %bitcast.353, bf16[1024,1024]{1,0:T(8,128)(2,1)S(1)} %add_convert_fusion.5, bf16[1024,512]{0,1:T(8,128)(2,1)S(1)} %collective-permute-done.27, bf16[512,512]{0,1:T(8,128)(2,1)S(1)} %copy-done.40, bf16[512,512]{0,1:T(8,128)(2,1)S(1)} %get-tuple-element.485), kind=kOutput, calls=%fused_computation.41 | convolution fusion | flops 2166358016 | bytes 8392704 | tf_op jit(solution)/shard_map/dot_general | solution.py:657
  225.9 5.4 fusion.33
  231.3 5.4 fusion.23
  236.7 6.3 assemble_image.3
  245.5 7.6 %fusion.18 = (bf16[1024,1024]{1,0:T(8,128)(2,1)}, bf16[1024,1024]{1,0:T(8,128)(2,1)}) fusion(f32[1024]{0:T(1024)S(1)} %bitcast.351, bf16[1024,1024]{1,0:T(8,128)(2,1)S(1)} %copy-done.73, bf16[512,1024]{0,1:T(8,128)(2,1)S(1)} %copy-done.108, bf16[512,512]{0,1:T(8,128)(2,1)} %collective-permute-done.20, bf16[512,512]{0,1:T(8,128)(2,1)} %get-tuple-element.486), kind=kOutput, calls=%fused_computation.31 | convolution fusion | flops 2166358016 | bytes 8392704 | tf_op jit(solution)/shard_map/dot_general | solution.py:657
  257.0 2.9 pad_maximum_fusion.2
  260.1 3.7 convolution_convert_fusion.2
  264.2 3.8 convolution_convert_fusion.3
  276.6 4.8 fusion.119
  283.9 3.3 add_convert_fusion.2
  294.3 3.7 fusion.88
  298.0 4.1 fusion.116
  302.1 6.1 fusion.117
  308.3 7.2 %fusion.35 = (f32[1024]{0:T(1024)}, f32[1024]{0:T(1024)S(1)}, bf16[1024,1024]{1,0:T(8,128)(2,1)S(1)}) fusion(bf16[1024,1024]{1,0:T(8,128)(2,1)S(1)} %copy-done.23, f32[1024,1024]{1,0:T(8,128)S(1)} %copy-done.19, f32[1024]{0:T(1024)S(1)} %get-tuple-element.532, bf16[1024,1024]{1,0:T(8,128)(2,1)} %get-tuple-element.232, ...), kind=kOutput, calls=%fused_computation.48 | convolution fusion | flops 2165307392 | bytes 25182208 | tf_op jit(solution)/shard_map/dot_general | solution.py:661
  315.5 5.4 multiply_convert_fusion.1
  320.9 3.6 multiply_convert_fusion.2
  328.3 4.0 multiply_convert_fusion.4
  332.3 4.8 multiply_convert_fusion.3
  339.5 3.7 convolution_convert_fusion
  343.2 3.7 convolution_convert_fusion.1
  349.3 3.9 fusion.91
  360.9 5.8 multiply_reduce_fusion
  366.8 6.0 multiply_reduce_fusion.1
  383.3 9.9 %collective-permute-done.47 = bf16[512,512]{1,0:T(8,128)(2,1)S(1)} collective-permute-done((bf16[512,512]{1,0:T(8,128)(2,1)S(1)}, bf16[512,512]{1,0:T(8,128)(2,1)S(1)}, u32[]{:S(2)}, u32[]{:S(2)}) %collective-permute-start.47) | collective-permute-done | bytes 524320 | tf_op jit(solution)/shard_map/ppermute | solution.py:374
  400.4 12.5 %collective-permute-start.55 = (bf16[128,1024]{1,0:T(8,128)(2,1)}, bf16[128,1024]{1,0:T(8,128)(2,1)}, u32[]{:S(2)}, u32[]{:S(2)}) collective-permute-start(bf16[128,1024]{1,0:T(8,128)(2,1)} %get-tuple-element.507), channel_id=1, source_target_pairs={{0,16},{4,20},{8,24},{12,28},{16,0},{20,4},{24,8},{28,12},{1,17},{... | collective-permute-start | bytes 786440 | tf_op jit(solution)/shard_map/ppermute | solution.py:368
  424.6 16.0 %attend_back.4 = bf16[1024,768]{1,0:T(8,128)(2,1)S(1)} custom-call(bf16[1024,768]{1,0:T(8,128)(2,1)S(1)} %copy-done.17, bf16[1024,768]{1,0:T(8,128)(2,1)S(1)} %copy-done.17, bf16[1024,768]{1,0:T(8,128)(2,1)S(1)} %copy-done.17, bf16[1024,256]{1,0:T(8,128)(2,1)S(1)} %get-tuple-element.511.g_ref, f32[2,8,1024]{2,1,0:T(8,128)S(1)} %get-tuple-element.257.lse_ref), custom_call_target="tpu_custom_call" | custom-call | flops 10737418240 | bytes 11010048 | tf_op jit(solution)/shard_map/attend_back/pallas_call | solution.py:637
  442.9 6.7 %spread_image.2 = bf16[4,256,1024]{2,1,0:T(8,128)(2,1)} custom-call(s32[9]{0:T(128)} %stack.214.place_ref, bf16[256,1024]{1,0:T(8,128)(2,1)} %get-tuple-element.493.own_ref, bf16[256,1024]{1,0:T(8,128)(2,1)} %copy-done.114, bf16[256,1024]{1,0:T(8,128)(2,1)} %collective-permute-done.49.refs_1_, bf16[256,1024]{1,0:T(8,128)(2,1)} %collective-permute-done.50.refs_2_), custom_call_target="tpu_custom_call" | custom-call | tf_op jit(solution)/shard_map/spread_image/pallas_call | solution.py:519
  449.6 4.8 convolution_convert_fusion.7
  456.9 8.5 %collective-permute-done.56 = bf16[128,1024]{1,0:T(8,128)(2,1)S(1)} collective-permute-done((bf16[128,1024]{1,0:T(8,128)(2,1)S(1)}, bf16[128,1024]{1,0:T(8,128)(2,1)S(1)}, u32[]{:S(2)}, u32[]{:S(2)}) %collective-permute-start.56) | collective-permute-done | bytes 262176 | tf_op jit(solution)/shard_map/ppermute | solution.py:368
  481.1 15.9 %attend_back.5 = bf16[1024,768]{1,0:T(8,128)(2,1)S(1)} custom-call(bf16[1024,768]{1,0:T(8,128)(2,1)S(1)} %copy-done.13, bf16[1024,768]{1,0:T(8,128)(2,1)S(1)} %copy-done.13, bf16[1024,768]{1,0:T(8,128)(2,1)S(1)} %copy-done.13, bf16[1024,256]{1,0:T(8,128)(2,1)S(1)} %get-tuple-element.262.g_ref, f32[2,8,1024]{2,1,0:T(8,128)S(1)} %get-tuple-element.263.lse_ref), custom_call_target="tpu_custom_call" | custom-call | flops 10737418240 | bytes 11010048 | tf_op jit(solution)/shard_map/attend_back/pallas_call | solution.py:637
  504.6 15.9 %attend_back.6 = bf16[1024,768]{1,0:T(8,128)(2,1)S(1)} custom-call(bf16[1024,768]{1,0:T(8,128)(2,1)S(1)} %copy-done.15, bf16[1024,768]{1,0:T(8,128)(2,1)S(1)} %copy-done.15, bf16[1024,768]{1,0:T(8,128)(2,1)S(1)} %copy-done.15, bf16[1024,256]{1,0:T(8,128)(2,1)S(1)} %copy-done.1, f32[2,8,1024]{2,1,0:T(8,128)S(1)} %get-tuple-element.272.lse_ref), custom_call_target="tpu_custom_call" | custom-call | flops 10737418240 | bytes 11010048 | tf_op jit(solution)/shard_map/attend_back/pallas_call | solution.py:637
  528.1 5.5 collective-permute-start.69
  536.0 16.1 %attend_back.7 = bf16[1024,768]{1,0:T(8,128)(2,1)S(1)} custom-call(bf16[1024,768]{1,0:T(8,128)(2,1)S(1)} %copy-done.11, bf16[1024,768]{1,0:T(8,128)(2,1)S(1)} %copy-done.11, bf16[1024,768]{1,0:T(8,128)(2,1)S(1)} %copy-done.11, bf16[1024,256]{1,0:T(8,128)(2,1)S(1)} %copy-done, f32[2,8,1024]{2,1,0:T(8,128)S(1)} %get-tuple-element.276.lse_ref), custom_call_target="tpu_custom_call" | custom-call | flops 10737418240 | bytes 11010048 | tf_op jit(solution)/shard_map/attend_back/pallas_call | solution.py:637
  552.1 3.0 convolution_convert_fusion.4
  555.5 5.4 fusion.85
  561.2 5.0 fusion.86
  566.5 5.2 fusion.124
  572.4 9.0 %fusion.12 = (f32[1024]{0:T(1024)S(1)}, f32[1024]{0:T(1024)S(1)}, f32[1024]{0:T(1024)S(1)}, f32[1024]{0:T(1024)S(1)}, f32[1024,1024]{1,0:T(8,128)}) fusion(bf16[1024,1024]{1,0:T(8,128)(2,1)} %assemble_image.2, f32[1024]{0:T(1024)S(1)} %copy-done.141, f32[1024]{0:T(1024)S(1)} %copy-done.137, f32[1024]{0:T(1024)S(1)} %copy-done.139, ...), kind=kOutput, calls=%fused_computation.25 | convolution fusion | flops 1624240128 | bytes 22048768 | tf_op jit(solution)/shard_map/dot_general | solution.py:661
  586.2 6.1 fusion.100
  600.2 12.0 %collective-permute-done.67 = f32[8,1216]{1,0:T(8,128)S(1)} collective-permute-done((f32[8,1216]{1,0:T(8,128)S(1)}, f32[8,1216]{1,0:T(8,128)S(1)}, u32[]{:S(2)}, u32[]{:S(2)}) %collective-permute-start.67) | collective-permute-done | bytes 38944 | tf_op jit(solution)/shard_map/ppermute | solution.py:378
  620.2 3.2 multiply_subtract_fusion.1
  624.5 4.9 collective-permute-done.72
  646.2 7.9 %collective-permute-done.75 = bf16[128,768]{1,0:T(8,128)(2,1)S(1)} collective-permute-done((bf16[128,768]{1,0:T(8,128)(2,1)}, bf16[128,768]{1,0:T(8,128)(2,1)S(1)}, u32[]{:S(2)}, u32[]{:S(2)}) %collective-permute-start.75) | collective-permute-done | bytes 196640 | tf_op jit(solution)/shard_map/ppermute | solution.py:368
  659.8 7.0 %spread_image.3 = f32[4,256,1024]{2,1,0:T(8,128)} custom-call(s32[9]{0:T(128)} %stack.214.place_ref, f32[256,1024]{1,0:T(8,128)} %slice.432.own_ref, bf16[256,1024]{1,0:T(8,128)(2,1)} %collective-permute-done.80.refs_0_, bf16[256,1024]{1,0:T(8,128)(2,1)} %collective-permute-done.81.refs_1_, bf16[256,1024]{1,0:T(8,128)(2,1)} %collective-permute-done.82.refs_2_), custom_call_target="tpu_custom_call" | custom-call | tf_op jit(solution)/shard_map/spread_image/pallas_call | solution.py:519
  (761 shorter events, 240.2 us)
Async XLA Ops:
  3.4 25.3 %collective-permute-start.3 = (bf16[128,768]{0,1:T(8,128)(2,1)}, bf16[128,768]{0,1:T(8,128)(2,1)}, u32[]{:S(2)}, u32[]{:S(2)}) collective-permute-start(bf16[128,768]{0,1:T(8,128)(2,1)} %bitcast.16), channel_id=1, source_target_pairs={{0,8},{4,12},{8,0},{12,4},{16,24},{20,28},{24,16},{28,20},{1,9},{5... | collective-permute-start | bytes 589832 | tf_op jit(solution)/shard_map/ppermute | solution.py:368
  6.4 22.2 %collective-permute-start.4 = (bf16[128,768]{0,1:T(8,128)(2,1)}, bf16[128,768]{0,1:T(8,128)(2,1)}, u32[]{:S(2)}, u32[]{:S(2)}) collective-permute-start(bf16[128,768]{0,1:T(8,128)(2,1)} %bitcast.16), channel_id=1, source_target_pairs={{0,16},{4,20},{8,24},{12,28},{16,0},{20,4},{24,8},{28,12},{1,17},{... | collective-permute-start | bytes 589832 | tf_op jit(solution)/shard_map/ppermute | solution.py:368
  9.0 19.7 %collective-permute-start.5 = (bf16[128,768]{0,1:T(8,128)(2,1)}, bf16[128,768]{0,1:T(8,128)(2,1)}, u32[]{:S(2)}, u32[]{:S(2)}) collective-permute-start(bf16[128,768]{0,1:T(8,128)(2,1)} %bitcast.16), channel_id=1, source_target_pairs={{0,24},{4,28},{8,16},{12,20},{16,8},{20,12},{24,0},{28,4},{1,25},{... | collective-permute-start | bytes 589832 | tf_op jit(solution)/shard_map/ppermute | solution.py:368
  11.5 15.6 %collective-permute-start.1 = (bf16[1,1216]{1,0:T(2,128)(2,1)S(1)}, bf16[1,1216]{1,0:T(2,128)(2,1)}, u32[]{:S(2)}, u32[]{:S(2)}) collective-permute-start(bf16[1,1216]{1,0:T(2,128)(2,1)S(1)} %reshape.927), channel_id=1, source_target_pairs={{0,16},{4,20},{8,24},{12,28},{16,0},{20,4},{24,8},{28,12},{1,17},{... | collective-permute-start | bytes 7304 | tf_op jit(solution)/shard_map/ppermute | solution.py:368
  27.1 29.3 %collective-permute-start.12 = (bf16[256,1024]{1,0:T(8,128)(2,1)}, bf16[256,1024]{1,0:T(8,128)(2,1)}, u32[]{:S(2)}, u32[]{:S(2)}) collective-permute-start(bf16[256,1024]{1,0:T(8,128)(2,1)} %get-tuple-element.499), channel_id=1, source_target_pairs={{0,1},{1,0},{2,3},{3,2},{4,5},{5,4},{6,7},{7,6},{8,9},{9,8},{10,11... | collective-permute-start | bytes 1572872 | tf_op jit(solution)/shard_map/ppermute | solution.py:378
  27.1 32.0 %collective-permute-start.13 = (bf16[256,1024]{1,0:T(8,128)(2,1)}, bf16[256,1024]{1,0:T(8,128)(2,1)}, u32[]{:S(2)}, u32[]{:S(2)}) collective-permute-start(bf16[256,1024]{1,0:T(8,128)(2,1)} %get-tuple-element.498), channel_id=1, source_target_pairs={{0,2},{1,3},{2,0},{3,1},{4,6},{5,7},{6,4},{7,5},{8,10},{9,11},{10,... | collective-permute-start | bytes 1572872 | tf_op jit(solution)/shard_map/ppermute | solution.py:378
  30.1 20.5 %collective-permute-start.7 = (bf16[512,384]{0,1:T(8,128)(2,1)S(1)}, bf16[512,384]{0,1:T(8,128)(2,1)S(1)}, u32[]{:S(2)}, u32[]{:S(2)}) collective-permute-start(bf16[512,384]{0,1:T(8,128)(2,1)S(1)} %get-tuple-element.524), channel_id=1, source_target_pairs={{0,2},{1,3},{2,0},{3,1},{4,6},{5,7},{6,4},{7,5},{8,10},{9,11},{10,... | collective-permute-start | bytes 1179656 | tf_op jit(solution)/shard_map/ppermute | solution.py:378
  30.7 20.4 %collective-permute-start.8 = (bf16[512,384]{0,1:T(8,128)(2,1)S(1)}, bf16[512,384]{0,1:T(8,128)(2,1)S(1)}, u32[]{:S(2)}, u32[]{:S(2)}) collective-permute-start(bf16[512,384]{0,1:T(8,128)(2,1)S(1)} %get-tuple-element.523), channel_id=1, source_target_pairs={{0,4},{4,0},{8,12},{12,8},{16,20},{20,16},{24,28},{28,24},{1,5},{5... | collective-permute-start | bytes 1179656 | tf_op jit(solution)/shard_map/ppermute | solution.py:374
  41.8 19.8 %collective-permute-start.14 = (bf16[256,1024]{1,0:T(8,128)(2,1)}, bf16[256,1024]{1,0:T(8,128)(2,1)}, u32[]{:S(2)}, u32[]{:S(2)}) collective-permute-start(bf16[256,1024]{1,0:T(8,128)(2,1)} %get-tuple-element.497), channel_id=1, source_target_pairs={{0,3},{1,2},{2,1},{3,0},{4,7},{5,6},{6,5},{7,4},{8,11},{9,10},{10,... | collective-permute-start | bytes 1572872 | tf_op jit(solution)/shard_map/ppermute | solution.py:378
  50.6 25.8 %collective-permute-start.15 = (bf16[128,2304]{0,1:T(8,128)(2,1)}, bf16[128,2304]{0,1:T(8,128)(2,1)}, u32[]{:S(2)}, u32[]{:S(2)}) collective-permute-start(bf16[128,2304]{0,1:T(8,128)(2,1)} %pad_maximum_fusion.16), channel_id=1, source_target_pairs={{0,8},{4,12},{8,0},{12,4},{16,24},{20,28},{24,16},{28,20},{1,9},{5... | collective-permute-start | bytes 1769480 | tf_op jit(solution)/shard_map/ppermute | solution.py:368
  51.9 42.8 %collective-permute-start.16 = (bf16[128,2304]{0,1:T(8,128)(2,1)}, bf16[128,2304]{0,1:T(8,128)(2,1)}, u32[]{:S(2)}, u32[]{:S(2)}) collective-permute-start(bf16[128,2304]{0,1:T(8,128)(2,1)} %pad_maximum_fusion.16), channel_id=1, source_target_pairs={{0,16},{4,20},{8,24},{12,28},{16,0},{20,4},{24,8},{28,12},{1,17},{... | collective-permute-start | bytes 1769480 | tf_op jit(solution)/shard_map/ppermute | solution.py:368
  56.4 38.2 %collective-permute-start.17 = (bf16[128,2304]{0,1:T(8,128)(2,1)}, bf16[128,2304]{0,1:T(8,128)(2,1)S(1)}, u32[]{:S(2)}, u32[]{:S(2)}) collective-permute-start(bf16[128,2304]{0,1:T(8,128)(2,1)} %pad_maximum_fusion.16), channel_id=1, source_target_pairs={{0,24},{4,28},{8,16},{12,20},{16,8},{20,12},{24,0},{28,4},{1,25},{... | collective-permute-start | bytes 1769480 | tf_op jit(solution)/shard_map/ppermute | solution.py:368
  65.4 50.4 %collective-permute-start.18 = (bf16[512,768]{0,1:T(8,128)(2,1)}, bf16[512,768]{0,1:T(8,128)(2,1)}, u32[]{:S(2)}, u32[]{:S(2)}) collective-permute-start(bf16[512,768]{0,1:T(8,128)(2,1)} %pad_maximum_fusion.14), channel_id=1, source_target_pairs={{0,4},{4,0},{8,12},{12,8},{16,20},{20,16},{24,28},{28,24},{1,5},{5... | collective-permute-start | bytes 2359304 | tf_op jit(solution)/shard_map/ppermute | solution.py:374
  66.9 48.9 %collective-permute-start.19 = (bf16[1024,384]{0,1:T(8,128)(2,1)}, bf16[1024,384]{0,1:T(8,128)(2,1)}, u32[]{:S(2)}, u32[]{:S(2)}) collective-permute-start(bf16[1024,384]{0,1:T(8,128)(2,1)} %pad_maximum_fusion.15), channel_id=1, source_target_pairs={{0,2},{1,3},{2,0},{3,1},{4,6},{5,7},{6,4},{7,5},{8,10},{9,11},{10,... | collective-permute-start | bytes 2359304 | tf_op jit(solution)/shard_map/ppermute | solution.py:378
  99.1 16.6 %collective-permute-start.22 = (bf16[2,512,128]{1,2,0:T(8,128)(2,1)}, bf16[2,512,128]{1,2,0:T(8,128)(2,1)}, u32[]{:S(2)}, u32[]{:S(2)}) collective-permute-start(bf16[2,512,128]{1,2,0:T(8,128)(2,1)} %pad_maximum_fusion.19), channel_id=1, source_target_pairs={{0,4},{4,0},{8,12},{12,8},{16,20},{20,16},{24,28},{28,24},{1,5},{5... | collective-permute-start | bytes 786440 | tf_op jit(solution)/shard_map/ppermute | solution.py:374
  100.6 15.1 %collective-permute-start.20 = (bf16[512,512]{0,1:T(8,128)(2,1)}, bf16[512,512]{0,1:T(8,128)(2,1)}, u32[]{:S(2)}, u32[]{:S(2)}) collective-permute-start(bf16[512,512]{0,1:T(8,128)(2,1)} %get-tuple-element.486), channel_id=1, source_target_pairs={{0,2},{1,3},{2,0},{3,1},{4,6},{5,7},{6,4},{7,5},{8,10},{9,11},{10,... | collective-permute-start | bytes 1572872 | tf_op jit(solution)/shard_map/ppermute | solution.py:378
  118.6 22.1 %collective-permute-start.24 = (bf16[1024,768]{0,1:T(8,128)(2,1)}, bf16[1024,768]{0,1:T(8,128)(2,1)}, u32[]{:S(2)}, u32[]{:S(2)}) collective-permute-start(bf16[1024,768]{0,1:T(8,128)(2,1)} %pad_maximum_fusion.5), channel_id=1, source_target_pairs={{0,1},{1,0},{2,3},{3,2},{4,5},{5,4},{6,7},{7,6},{8,9},{9,8},{10,11... | collective-permute-start | bytes 4718600 | tf_op jit(solution)/shard_map/ppermute | solution.py:378
  121.2 19.5 %collective-permute-start.23 = (bf16[1024,768]{0,1:T(8,128)(2,1)}, bf16[1024,768]{0,1:T(8,128)(2,1)}, u32[]{:S(2)}, u32[]{:S(2)}) collective-permute-start(bf16[1024,768]{0,1:T(8,128)(2,1)} %pad_maximum_fusion.4), channel_id=1, source_target_pairs={{0,1},{1,0},{2,3},{3,2},{4,5},{5,4},{6,7},{7,6},{8,9},{9,8},{10,11... | collective-permute-start | bytes 4718600 | tf_op jit(solution)/shard_map/ppermute | solution.py:378
  125.9 14.8 %collective-permute-start.25 = (bf16[2,1024,128]{1,2,0:T(8,128)(2,1)S(1)}, bf16[2,1024,128]{1,2,0:T(8,128)(2,1)S(1)}, u32[]{:S(2)}, u32[]{:S(2)}) collective-permute-start(bf16[2,1024,128]{1,2,0:T(8,128)(2,1)S(1)} %pad_maximum_fusion.17), channel_id=1, source_target_pairs={{0,2},{1,3},{2,0},{3,1},{4,6},{5,7},{6,4},{7,5},{8,10},{9,11},{10,... | collective-permute-start | bytes 1572872 | tf_op jit(solution)/shard_map/ppermute | solution.py:378
  126.6 35.7 %collective-permute-start.27 = (bf16[1024,512]{0,1:T(8,128)(2,1)S(1)}, bf16[1024,512]{0,1:T(8,128)(2,1)S(1)}, u32[]{:S(2)}, u32[]{:S(2)}) collective-permute-start(bf16[1024,512]{0,1:T(8,128)(2,1)S(1)} %pad_maximum_fusion.8), channel_id=1, source_target_pairs={{0,2},{1,3},{2,0},{3,1},{4,6},{5,7},{6,4},{7,5},{8,10},{9,11},{10,... | collective-permute-start | bytes 3145736 | tf_op jit(solution)/shard_map/ppermute | solution.py:378
  129.5 32.8 %collective-permute-start.26 = (bf16[512,1024]{0,1:T(8,128)(2,1)S(1)}, bf16[512,1024]{0,1:T(8,128)(2,1)S(1)}, u32[]{:S(2)}, u32[]{:S(2)}) collective-permute-start(bf16[512,1024]{0,1:T(8,128)(2,1)S(1)} %pad_maximum_fusion.7), channel_id=1, source_target_pairs={{0,4},{4,0},{8,12},{12,8},{16,20},{20,16},{24,28},{28,24},{1,5},{5... | collective-permute-start | bytes 3145736 | tf_op jit(solution)/shard_map/ppermute | solution.py:374
  141.8 20.5 %collective-permute-start.28 = (bf16[2,1024,256]{1,2,0:T(8,128)(2,1)S(1)}, bf16[2,1024,256]{1,2,0:T(8,128)(2,1)S(1)}, u32[]{:S(2)}, u32[]{:S(2)}) collective-permute-start(bf16[2,1024,256]{1,2,0:T(8,128)(2,1)S(1)} %pad_maximum_fusion.9), channel_id=1, source_target_pairs={{0,1},{1,0},{2,3},{3,2},{4,5},{5,4},{6,7},{7,6},{8,9},{9,8},{10,11... | collective-permute-start | bytes 3145736 | tf_op jit(solution)/shard_map/ppermute | solution.py:378
  162.6 31.9 %collective-permute-start.30 = (bf16[1024,1024]{0,1:T(8,128)(2,1)S(1)}, bf16[1024,1024]{0,1:T(8,128)(2,1)S(1)}, u32[]{:S(2)}, u32[]{:S(2)}) collective-permute-start(bf16[1024,1024]{0,1:T(8,128)(2,1)S(1)} %pad_maximum_fusion.1), channel_id=1, source_target_pairs={{0,1},{1,0},{2,3},{3,2},{4,5},{5,4},{6,7},{7,6},{8,9},{9,8},{10,11... | collective-permute-start | bytes 6291464 | tf_op jit(solution)/shard_map/ppermute | solution.py:378
  164.9 29.5 %collective-permute-start.29 = (bf16[1024,1024]{0,1:T(8,128)(2,1)S(1)}, bf16[1024,1024]{0,1:T(8,128)(2,1)S(1)}, u32[]{:S(2)}, u32[]{:S(2)}) collective-permute-start(bf16[1024,1024]{0,1:T(8,128)(2,1)S(1)} %pad_maximum_fusion), channel_id=1, source_target_pairs={{0,1},{1,0},{2,3},{3,2},{4,5},{5,4},{6,7},{7,6},{8,9},{9,8},{10,11... | collective-permute-start | bytes 6291464 | tf_op jit(solution)/shard_map/ppermute | solution.py:378
  165.1 27.4 %collective-permute-start.31 = (bf16[512,512]{0,1:T(8,128)(2,1)S(1)}, bf16[512,512]{0,1:T(8,128)(2,1)S(1)}, u32[]{:S(2)}, u32[]{:S(2)}) collective-permute-start(bf16[512,512]{0,1:T(8,128)(2,1)S(1)} %get-tuple-element.519), channel_id=1, source_target_pairs={{0,2},{1,3},{2,0},{3,1},{4,6},{5,7},{6,4},{7,5},{8,10},{9,11},{10,... | collective-permute-start | bytes 1572872 | tf_op jit(solution)/shard_map/ppermute | solution.py:378
  165.6 28.4 %collective-permute-start.32 = (bf16[512,512]{0,1:T(8,128)(2,1)S(1)}, bf16[512,512]{0,1:T(8,128)(2,1)S(1)}, u32[]{:S(2)}, u32[]{:S(2)}) collective-permute-start(bf16[512,512]{0,1:T(8,128)(2,1)S(1)} %get-tuple-element.518), channel_id=1, source_target_pairs={{0,4},{4,0},{8,12},{12,8},{16,20},{20,16},{24,28},{28,24},{1,5},{5... | collective-permute-start | bytes 1572872 | tf_op jit(solution)/shard_map/ppermute | solution.py:374
  167.3 38.8 %collective-permute-start.33 = (bf16[256,1024]{1,0:T(8,128)(2,1)S(1)}, bf16[256,1024]{1,0:T(8,128)(2,1)S(1)}, u32[]{:S(2)}, u32[]{:S(2)}) collective-permute-start(bf16[256,1024]{1,0:T(8,128)(2,1)S(1)} %get-tuple-element.496), channel_id=1, source_target_pairs={{0,1},{1,0},{2,3},{3,2},{4,5},{5,4},{6,7},{7,6},{8,9},{9,8},{10,11... | collective-permute-start | bytes 1572872 | tf_op jit(solution)/shard_map/ppermute | solution.py:378
  194.1 23.6 %collective-permute-start.35 = (bf16[256,1024]{1,0:T(8,128)(2,1)S(1)}, bf16[256,1024]{1,0:T(8,128)(2,1)S(1)}, u32[]{:S(2)}, u32[]{:S(2)}) collective-permute-start(bf16[256,1024]{1,0:T(8,128)(2,1)S(1)} %get-tuple-element.494), channel_id=1, source_target_pairs={{0,3},{1,2},{2,1},{3,0},{4,7},{5,6},{6,5},{7,4},{8,11},{9,10},{10,... | collective-permute-start | bytes 1572872 | tf_op jit(solution)/shard_map/ppermute | solution.py:378
  195.8 57.4 %collective-permute-start.37 = (bf16[1024,512]{0,1:T(8,128)(2,1)}, bf16[1024,512]{0,1:T(8,128)(2,1)}, u32[]{:S(2)}, u32[]{:S(2)}) collective-permute-start(bf16[1024,512]{0,1:T(8,128)(2,1)} %pad_maximum_fusion.11), channel_id=1, source_target_pairs={{0,2},{1,3},{2,0},{3,1},{4,6},{5,7},{6,4},{7,5},{8,10},{9,11},{10,... | collective-permute-start | bytes 3145736 | tf_op jit(solution)/shard_map/ppermute | solution.py:378
  198.3 54.8 %collective-permute-start.36 = (bf16[512,1024]{0,1:T(8,128)(2,1)}, bf16[512,1024]{0,1:T(8,128)(2,1)}, u32[]{:S(2)}, u32[]{:S(2)}) collective-permute-start(bf16[512,1024]{0,1:T(8,128)(2,1)} %pad_maximum_fusion.10), channel_id=1, source_target_pairs={{0,4},{4,0},{8,12},{12,8},{16,20},{20,16},{24,28},{28,24},{1,5},{5... | collective-permute-start | bytes 3145736 | tf_op jit(solution)/shard_map/ppermute | solution.py:374
  256.0 27.8 %collective-permute-start.41 = (bf16[1024,1024]{0,1:T(8,128)(2,1)}, bf16[1024,1024]{0,1:T(8,128)(2,1)}, u32[]{:S(2)}, u32[]{:S(2)}) collective-permute-start(bf16[1024,1024]{0,1:T(8,128)(2,1)} %pad_maximum_fusion.3), channel_id=1, source_target_pairs={{0,1},{1,0},{2,3},{3,2},{4,5},{5,4},{6,7},{7,6},{8,9},{9,8},{10,11... | collective-permute-start | bytes 6291464 | tf_op jit(solution)/shard_map/ppermute | solution.py:378
  259.9 23.9 %collective-permute-start.40 = (bf16[1024,1024]{0,1:T(8,128)(2,1)}, bf16[1024,1024]{0,1:T(8,128)(2,1)}, u32[]{:S(2)}, u32[]{:S(2)}) collective-permute-start(bf16[1024,1024]{0,1:T(8,128)(2,1)} %pad_maximum_fusion.2), channel_id=1, source_target_pairs={{0,1},{1,0},{2,3},{3,2},{4,5},{5,4},{6,7},{7,6},{8,9},{9,8},{10,11... | collective-permute-start | bytes 6291464 | tf_op jit(solution)/shard_map/ppermute | solution.py:378
  263.8 20.0 %collective-permute-start.39 = (bf16[1024,1024]{1,0:T(8,128)(2,1)}, bf16[1024,1024]{1,0:T(8,128)(2,1)}, u32[]{:S(2)}, u32[]{:S(2)}) collective-permute-start(bf16[1024,1024]{1,0:T(8,128)(2,1)} %convolution_convert_fusion.2), channel_id=1, source_target_pairs={{0,1},{1,0},{2,3},{3,2},{4,5},{5,4},{6,7},{7,6},{8,9},{9,8},{10,11... | collective-permute-start | bytes 6291464 | tf_op jit(solution)/shard_map/ppermute | solution.py:378
  267.9 15.9 %collective-permute-start.38 = (bf16[1024,1024]{1,0:T(8,128)(2,1)}, bf16[1024,1024]{1,0:T(8,128)(2,1)S(1)}, u32[]{:S(2)}, u32[]{:S(2)}) collective-permute-start(bf16[1024,1024]{1,0:T(8,128)(2,1)} %convolution_convert_fusion.3), channel_id=1, source_target_pairs={{0,1},{1,0},{2,3},{3,2},{4,5},{5,4},{6,7},{7,6},{8,9},{9,8},{10,11... | collective-permute-start | bytes 6291464 | tf_op jit(solution)/shard_map/ppermute | solution.py:378
  288.3 48.8 %collective-permute-start.43 = (bf16[1024,512]{1,0:T(8,128)(2,1)}, bf16[1024,512]{1,0:T(8,128)(2,1)}, u32[]{:S(2)}, u32[]{:S(2)}) collective-permute-start(bf16[1024,512]{1,0:T(8,128)(2,1)} %slice.409), channel_id=1, source_target_pairs={{0,2},{1,3},{2,0},{3,1},{4,6},{5,7},{6,4},{7,5},{8,10},{9,11},{10,... | collective-permute-start | bytes 3145736 | tf_op jit(solution)/shard_map/ppermute | solution.py:378
  293.5 43.5 %collective-permute-start.42 = (bf16[512,1024]{1,0:T(8,128)(2,1)}, bf16[512,1024]{1,0:T(8,128)(2,1)}, u32[]{:S(2)}, u32[]{:S(2)}) collective-permute-start(bf16[512,1024]{1,0:T(8,128)(2,1)} %slice.408), channel_id=1, source_target_pairs={{0,4},{4,0},{8,12},{12,8},{16,20},{20,16},{24,28},{28,24},{1,5},{5... | collective-permute-start | bytes 3145736 | tf_op jit(solution)/shard_map/ppermute | solution.py:374
  325.8 53.1 %collective-permute-start.48 = (bf16[256,1024]{1,0:T(8,128)(2,1)}, bf16[256,1024]{1,0:T(8,128)(2,1)S(1)}, u32[]{:S(2)}, u32[]{:S(2)}) collective-permute-start(bf16[256,1024]{1,0:T(8,128)(2,1)} %get-tuple-element.492), channel_id=1, source_target_pairs={{0,1},{1,0},{2,3},{3,2},{4,5},{5,4},{6,7},{7,6},{8,9},{9,8},{10,11... | collective-permute-start | bytes 1572872 | tf_op jit(solution)/shard_map/ppermute | solution.py:378
  325.9 54.4 %collective-permute-start.49 = (bf16[256,1024]{1,0:T(8,128)(2,1)}, bf16[256,1024]{1,0:T(8,128)(2,1)}, u32[]{:S(2)}, u32[]{:S(2)}) collective-permute-start(bf16[256,1024]{1,0:T(8,128)(2,1)} %get-tuple-element.491), channel_id=1, source_target_pairs={{0,2},{1,3},{2,0},{3,1},{4,6},{5,7},{6,4},{7,5},{8,10},{9,11},{10,... | collective-permute-start | bytes 1572872 | tf_op jit(solution)/shard_map/ppermute | solution.py:378
  326.6 56.7 %collective-permute-start.50 = (bf16[256,1024]{1,0:T(8,128)(2,1)}, bf16[256,1024]{1,0:T(8,128)(2,1)}, u32[]{:S(2)}, u32[]{:S(2)}) collective-permute-start(bf16[256,1024]{1,0:T(8,128)(2,1)} %get-tuple-element.490), channel_id=1, source_target_pairs={{0,3},{1,2},{2,1},{3,0},{4,7},{5,6},{6,5},{7,4},{8,11},{9,10},{10,... | collective-permute-start | bytes 1572872 | tf_op jit(solution)/shard_map/ppermute | solution.py:378
  359.8 34.3 %collective-permute-start.45 = (bf16[1024,1024]{1,0:T(8,128)(2,1)}, bf16[1024,1024]{1,0:T(8,128)(2,1)}, u32[]{:S(2)}, u32[]{:S(2)}) collective-permute-start(bf16[1024,1024]{1,0:T(8,128)(2,1)} %convolution_convert_fusion), channel_id=1, source_target_pairs={{0,1},{1,0},{2,3},{3,2},{4,5},{5,4},{6,7},{7,6},{8,9},{9,8},{10,11... | collective-permute-start | bytes 6291464 | tf_op jit(solution)/shard_map/ppermute | solution.py:378
  360.1 34.0 %collective-permute-start.44 = (bf16[1024,1024]{1,0:T(8,128)(2,1)}, bf16[1024,1024]{1,0:T(8,128)(2,1)}, u32[]{:S(2)}, u32[]{:S(2)}) collective-permute-start(bf16[1024,1024]{1,0:T(8,128)(2,1)} %convolution_convert_fusion.1), channel_id=1, source_target_pairs={{0,1},{1,0},{2,3},{3,2},{4,5},{5,4},{6,7},{7,6},{8,9},{9,8},{10,11... | collective-permute-start | bytes 6291464 | tf_op jit(solution)/shard_map/ppermute | solution.py:378
  400.4 56.5 %collective-permute-start.55 = (bf16[128,1024]{1,0:T(8,128)(2,1)}, bf16[128,1024]{1,0:T(8,128)(2,1)}, u32[]{:S(2)}, u32[]{:S(2)}) collective-permute-start(bf16[128,1024]{1,0:T(8,128)(2,1)} %get-tuple-element.507), channel_id=1, source_target_pairs={{0,16},{4,20},{8,24},{12,28},{16,0},{20,4},{24,8},{28,12},{1,17},{... | collective-permute-start | bytes 786440 | tf_op jit(solution)/shard_map/ppermute | solution.py:368
  414.0 51.4 %collective-permute-start.53 = (bf16[2,1024,256]{2,1,0:T(8,128)(2,1)}, bf16[2,1024,256]{2,1,0:T(8,128)(2,1)}, u32[]{:S(2)}, u32[]{:S(2)}) collective-permute-start(bf16[2,1024,256]{2,1,0:T(8,128)(2,1)} %pad_maximum_fusion.12), channel_id=1, source_target_pairs={{0,1},{1,0},{2,3},{3,2},{4,5},{5,4},{6,7},{7,6},{8,9},{9,8},{10,11... | collective-permute-start | bytes 3145736 | tf_op jit(solution)/shard_map/ppermute | solution.py:378
  417.8 47.6 %collective-permute-start.52 = (bf16[1024,512]{1,0:T(8,128)(2,1)}, bf16[1024,512]{1,0:T(8,128)(2,1)}, u32[]{:S(2)}, u32[]{:S(2)}) collective-permute-start(bf16[1024,512]{1,0:T(8,128)(2,1)} %slice.415), channel_id=1, source_target_pairs={{0,2},{1,3},{2,0},{3,1},{4,6},{5,7},{6,4},{7,5},{8,10},{9,11},{10,... | collective-permute-start | bytes 3145736 | tf_op jit(solution)/shard_map/ppermute | solution.py:378
  422.9 42.5 %collective-permute-start.51 = (bf16[512,1024]{1,0:T(8,128)(2,1)}, bf16[512,1024]{1,0:T(8,128)(2,1)}, u32[]{:S(2)}, u32[]{:S(2)}) collective-permute-start(bf16[512,1024]{1,0:T(8,128)(2,1)} %slice.414), channel_id=1, source_target_pairs={{0,4},{4,0},{8,12},{12,8},{16,20},{20,16},{24,28},{28,24},{1,5},{5... | collective-permute-start | bytes 3145736 | tf_op jit(solution)/shard_map/ppermute | solution.py:374
  468.1 33.0 %collective-permute-start.60 = (bf16[512,512]{1,0:T(8,128)(2,1)}, bf16[512,512]{1,0:T(8,128)(2,1)}, u32[]{:S(2)}, u32[]{:S(2)}) collective-permute-start(bf16[512,512]{1,0:T(8,128)(2,1)} %slice.428), channel_id=1, source_target_pairs={{0,4},{4,0},{8,12},{12,8},{16,20},{20,16},{24,28},{28,24},{1,5},{5... | collective-permute-start | bytes 1572872 | tf_op jit(solution)/shard_map/ppermute | solution.py:374
  471.8 29.3 %collective-permute-start.59 = (bf16[512,512]{1,0:T(8,128)(2,1)}, bf16[512,512]{1,0:T(8,128)(2,1)}, u32[]{:S(2)}, u32[]{:S(2)}) collective-permute-start(bf16[512,512]{1,0:T(8,128)(2,1)} %slice.426), channel_id=1, source_target_pairs={{0,2},{1,3},{2,0},{3,1},{4,6},{5,7},{6,4},{7,5},{8,10},{9,11},{10,... | collective-permute-start | bytes 1572872 | tf_op jit(solution)/shard_map/ppermute | solution.py:378
  475.0 26.1 %collective-permute-start.58 = (bf16[2,1024,128]{2,1,0:T(8,128)(2,1)}, bf16[2,1024,128]{2,1,0:T(8,128)(2,1)}, u32[]{:S(2)}, u32[]{:S(2)}) collective-permute-start(bf16[2,1024,128]{2,1,0:T(8,128)(2,1)} %slice.424), channel_id=1, source_target_pairs={{0,2},{1,3},{2,0},{3,1},{4,6},{5,7},{6,4},{7,5},{8,10},{9,11},{10,... | collective-permute-start | bytes 1572872 | tf_op jit(solution)/shard_map/ppermute | solution.py:378
  476.5 24.6 %collective-permute-start.57 = (bf16[1024,768]{1,0:T(8,128)(2,1)}, bf16[1024,768]{1,0:T(8,128)(2,1)}, u32[]{:S(2)}, u32[]{:S(2)}) collective-permute-start(bf16[1024,768]{1,0:T(8,128)(2,1)} %convolution_convert_fusion.7), channel_id=1, source_target_pairs={{0,1},{1,0},{2,3},{3,2},{4,5},{5,4},{6,7},{7,6},{8,9},{9,8},{10,11... | collective-permute-start | bytes 4718600 | tf_op jit(solution)/shard_map/ppermute | solution.py:378
  503.7 23.1 %collective-permute-start.61 = (bf16[2,512,128]{2,1,0:T(8,128)(2,1)S(1)}, bf16[2,512,128]{2,1,0:T(8,128)(2,1)S(1)}, u32[]{:S(2)}, u32[]{:S(2)}) collective-permute-start(bf16[2,512,128]{2,1,0:T(8,128)(2,1)S(1)} %slice.430), channel_id=1, source_target_pairs={{0,4},{4,0},{8,12},{12,8},{16,20},{20,16},{24,28},{28,24},{1,5},{5... | collective-permute-start | bytes 786440 | tf_op jit(solution)/shard_map/ppermute | solution.py:374
  524.4 30.8 %collective-permute-start.62 = (bf16[512,768]{1,0:T(8,128)(2,1)S(1)}, bf16[512,768]{1,0:T(8,128)(2,1)S(1)}, u32[]{:S(2)}, u32[]{:S(2)}) collective-permute-start(bf16[512,768]{1,0:T(8,128)(2,1)S(1)} %slice.431), channel_id=1, source_target_pairs={{0,4},{4,0},{8,12},{12,8},{16,20},{20,16},{24,28},{28,24},{1,5},{5... | collective-permute-start | bytes 2359304 | tf_op jit(solution)/shard_map/ppermute | solution.py:374
  526.9 28.2 %collective-permute-start.63 = (bf16[1024,768]{1,0:T(8,128)(2,1)S(1)}, bf16[1024,768]{1,0:T(8,128)(2,1)S(1)}, u32[]{:S(2)}, u32[]{:S(2)}) collective-permute-start(bf16[1024,768]{1,0:T(8,128)(2,1)S(1)} %convolution_convert_fusion.6), channel_id=1, source_target_pairs={{0,1},{1,0},{2,3},{3,2},{4,5},{5,4},{6,7},{7,6},{8,9},{9,8},{10,11... | collective-permute-start | bytes 4718600 | tf_op jit(solution)/shard_map/ppermute | solution.py:378
  528.1 64.7 %collective-permute-start.69 = (bf16[128,1280]{1,0:T(8,128)(2,1)}, bf16[128,1280]{1,0:T(8,128)(2,1)}, u32[]{:S(2)}, u32[]{:S(2)}) collective-permute-start(bf16[128,1280]{1,0:T(8,128)(2,1)} %get-tuple-element.502), channel_id=1, source_target_pairs={{0,8},{4,12},{8,0},{12,4},{16,24},{20,28},{24,16},{28,20},{1,9},{5... | collective-permute-start | bytes 983048 | tf_op jit(solution)/shard_map/ppermute | solution.py:368
  533.6 59.3 %collective-permute-start.70 = (bf16[128,1280]{1,0:T(8,128)(2,1)}, bf16[128,1280]{1,0:T(8,128)(2,1)}, u32[]{:S(2)}, u32[]{:S(2)}) collective-permute-start(bf16[128,1280]{1,0:T(8,128)(2,1)} %get-tuple-element.501), channel_id=1, source_target_pairs={{0,16},{4,20},{8,24},{12,28},{16,0},{20,4},{24,8},{28,12},{1,17},{... | collective-permute-start | bytes 983048 | tf_op jit(solution)/shard_map/ppermute | solution.py:368
  533.6 60.1 %collective-permute-start.71 = (bf16[128,1280]{1,0:T(8,128)(2,1)}, bf16[128,1280]{1,0:T(8,128)(2,1)}, u32[]{:S(2)}, u32[]{:S(2)}) collective-permute-start(bf16[128,1280]{1,0:T(8,128)(2,1)} %get-tuple-element.500), channel_id=1, source_target_pairs={{0,24},{4,28},{8,16},{12,20},{16,8},{20,12},{24,0},{28,4},{1,25},{... | collective-permute-start | bytes 983048 | tf_op jit(solution)/shard_map/ppermute | solution.py:368
  582.9 29.9 %collective-permute-start.65 = (bf16[1024,384]{1,0:T(8,128)(2,1)}, bf16[1024,384]{1,0:T(8,128)(2,1)}, u32[]{:S(2)}, u32[]{:S(2)}) collective-permute-start(bf16[1024,384]{1,0:T(8,128)(2,1)} %slice.436), channel_id=1, source_target_pairs={{0,2},{1,3},{2,0},{3,1},{4,6},{5,7},{6,4},{7,5},{8,10},{9,11},{10,... | collective-permute-start | bytes 2359304 | tf_op jit(solution)/shard_map/ppermute | solution.py:378
  583.8 28.9 %collective-permute-start.64 = (bf16[512,384]{1,0:T(8,128)(2,1)S(1)}, bf16[512,384]{1,0:T(8,128)(2,1)}, u32[]{:S(2)}, u32[]{:S(2)}) collective-permute-start(bf16[512,384]{1,0:T(8,128)(2,1)S(1)} %slice.435), channel_id=1, source_target_pairs={{0,2},{1,3},{2,0},{3,1},{4,6},{5,7},{6,4},{7,5},{8,10},{9,11},{10,... | collective-permute-start | bytes 1179656 | tf_op jit(solution)/shard_map/ppermute | solution.py:378
  592.9 19.2 %collective-permute-start.67 = (f32[8,1216]{1,0:T(8,128)S(1)}, f32[8,1216]{1,0:T(8,128)S(1)}, u32[]{:S(2)}, u32[]{:S(2)}) collective-permute-start(f32[8,1216]{1,0:T(8,128)S(1)} %get-tuple-element.528), channel_id=1, source_target_pairs={{0,2},{1,3},{2,0},{3,1},{4,6},{5,7},{6,4},{7,5},{8,10},{9,11},{10,... | collective-permute-start | bytes 116744 | tf_op jit(solution)/shard_map/ppermute | solution.py:378
  593.7 19.0 %collective-permute-start.68 = (f32[8,1216]{1,0:T(8,128)S(1)}, f32[8,1216]{1,0:T(8,128)S(1)}, u32[]{:S(2)}, u32[]{:S(2)}) collective-permute-start(f32[8,1216]{1,0:T(8,128)S(1)} %get-tuple-element.527), channel_id=1, source_target_pairs={{0,3},{1,2},{2,1},{3,0},{4,7},{5,6},{6,5},{7,4},{8,11},{9,10},{10,... | collective-permute-start | bytes 116744 | tf_op jit(solution)/shard_map/ppermute | solution.py:378
  599.8 34.5 %collective-permute-start.80 = (bf16[256,1024]{1,0:T(8,128)(2,1)}, bf16[256,1024]{1,0:T(8,128)(2,1)}, u32[]{:S(2)}, u32[]{:S(2)}) collective-permute-start(bf16[256,1024]{1,0:T(8,128)(2,1)} %get-tuple-element.489), channel_id=1, source_target_pairs={{0,1},{1,0},{2,3},{3,2},{4,5},{5,4},{6,7},{7,6},{8,9},{9,8},{10,11... | collective-permute-start | bytes 1572872 | tf_op jit(solution)/shard_map/ppermute | solution.py:378
  612.2 24.5 %collective-permute-start.81 = (bf16[256,1024]{1,0:T(8,128)(2,1)}, bf16[256,1024]{1,0:T(8,128)(2,1)}, u32[]{:S(2)}, u32[]{:S(2)}) collective-permute-start(bf16[256,1024]{1,0:T(8,128)(2,1)} %get-tuple-element.488), channel_id=1, source_target_pairs={{0,2},{1,3},{2,0},{3,1},{4,6},{5,7},{6,4},{7,5},{8,10},{9,11},{10,... | collective-permute-start | bytes 1572872 | tf_op jit(solution)/shard_map/ppermute | solution.py:378
  612.7 23.9 %collective-permute-start.82 = (bf16[256,1024]{1,0:T(8,128)(2,1)}, bf16[256,1024]{1,0:T(8,128)(2,1)}, u32[]{:S(2)}, u32[]{:S(2)}) collective-permute-start(bf16[256,1024]{1,0:T(8,128)(2,1)} %get-tuple-element.487), channel_id=1, source_target_pairs={{0,3},{1,2},{2,1},{3,0},{4,7},{5,6},{6,5},{7,4},{8,11},{9,10},{10,... | collective-permute-start | bytes 1572872 | tf_op jit(solution)/shard_map/ppermute | solution.py:378
  636.7 17.4 %collective-permute-start.75 = (bf16[128,768]{1,0:T(8,128)(2,1)}, bf16[128,768]{1,0:T(8,128)(2,1)S(1)}, u32[]{:S(2)}, u32[]{:S(2)}) collective-permute-start(bf16[128,768]{1,0:T(8,128)(2,1)} %get-tuple-element.522), channel_id=1, source_target_pairs={{0,16},{4,20},{8,24},{12,28},{16,0},{20,4},{24,8},{28,12},{1,17},{... | collective-permute-start | bytes 589832 | tf_op jit(solution)/shard_map/ppermute | solution.py:368
  638.7 15.4 %collective-permute-start.76 = (bf16[128,768]{1,0:T(8,128)(2,1)}, bf16[128,768]{1,0:T(8,128)(2,1)}, u32[]{:S(2)}, u32[]{:S(2)}) collective-permute-start(bf16[128,768]{1,0:T(8,128)(2,1)} %get-tuple-element.520), channel_id=1, source_target_pairs={{0,24},{4,28},{8,16},{12,20},{16,8},{20,12},{24,0},{28,4},{1,25},{... | collective-permute-start | bytes 589832 | tf_op jit(solution)/shard_map/ppermute | solution.py:368
  (204 other events, 1986.9 us)

commit v4 on v3

--- a/solution.py
+++ b/solution.py
@@ -479,54 +479,203 @@
     return total
 
 
-def assemble_kernel(place_ref, own_ref, *refs):
-    chunk_rows = own_ref.shape[1]
-    out_ref = refs[-1]
-    out_ref[0:chunk_rows, :] = own_ref[0]
-    for at, part_ref in enumerate(refs[:-1]):
-        out_ref[(at + 1) * chunk_rows : (at + 2) * chunk_rows, :] = part_ref[...]
-
-
-def assemble_image(place, arrays, parts):
+def norm_parts(values):
+    center = values - jnp.mean(values, -1, keepdims=True)
+    spread = lax.rsqrt(jnp.mean(center * center, -1, keepdims=True) + 1e-06)
+    return (center * spread, spread)
+
+
+def norm_back(grad, normal, spread, gain):
+    scaled = grad * gain
+    inner = scaled - jnp.mean(scaled, -1, keepdims=True)
+    return spread * (inner - normal * jnp.mean(scaled * normal, -1, keepdims=True))
+
+
+GAIN_ONE, SHIFT_ONE, OUT_BIAS, SCALE_ONE, GAIN_TWO, SHIFT_TWO, DOWN_BIAS, SCALE_TWO = range(8)
+
+
+def vector_row(vector_ref, at):
+    return vector_ref[at : at + 1, :]
+
+
+def assemble_kernel(with_norm, place_ref, vector_ref, own_ref, *refs):
+    out_ref, second_ref = refs[-2:]
+    part_refs = [own_ref.at[0]] + list(refs[:-2])
+    for at, part_ref in enumerate(part_refs):
+        for block in range(DP):
+            lanes = pl.ds(pl.multiple_of(place_ref[block] * LANES, LANES), LANES)
+            out_ref[at, :, block * LANES : (block + 1) * LANES] = part_ref[:, lanes]
+        values = out_ref[at].astype(F32)
+        if with_norm:
+            normal, _ = norm_parts(values)
+            values = normal * vector_row(vector_ref, GAIN_ONE) + vector_row(vector_ref, SHIFT_ONE)
+        else:
+            values = values * vector_row(vector_ref, SCALE_TWO)
+        second_ref[at] = values.astype(BF)
+
+
+def assemble_image(place, vector_full, arrays, parts, with_norm):
     chunk_rows, width = parts[0].shape
-    return pl.pallas_call(
-        assemble_kernel,
+    rows = chunk_rows // 4
+    block = pl.BlockSpec((rows, width), lambda i, place_ref: (i, 0))
+    result = pl.BlockSpec((MP, rows, width), lambda i, place_ref: (0, i, 0))
+    shape = jax.ShapeDtypeStruct((MP, chunk_rows, width), BF)
+    image, second = pl.pallas_call(
+        functools.partial(assemble_kernel, with_norm),
         grid_spec=pltpu.PrefetchScalarGridSpec(
             num_scalar_prefetch=1,
-            grid=(width // LANES,),
+            grid=(4,),
             in_specs=[
-                pl.BlockSpec((1, chunk_rows, LANES), lambda j, place_ref: (place_ref[DP], 0, place_ref[j]))
+                pl.BlockSpec(vector_full.shape, lambda i, place_ref: (0, 0)),
+                pl.BlockSpec((1, rows, width), lambda i, place_ref: (place_ref[DP], i, 0)),
             ]
-            + [pl.BlockSpec((chunk_rows, LANES), lambda j, place_ref: (0, place_ref[j]))] * len(parts),
-            out_specs=pl.BlockSpec((chunk_rows * MP, LANES), lambda j, place_ref: (0, j)),
+            + [block] * len(parts),
+            out_specs=[result] * 2,
         ),
-        out_shape=jax.ShapeDtypeStruct((chunk_rows * MP, width), arrays.dtype),
+        out_shape=[shape] * 2,
+        compiler_params=pltpu.CompilerParams(vmem_limit_bytes=32 * 2**20),
+        cost_estimate=pl.CostEstimate(
+            flops=chunk_rows * width * 40, bytes_accessed=chunk_rows * width * 24, transcendentals=0
+        ),
         name="assemble_image",
-    )(place, arrays, *parts)
+    )(place, vector_full, arrays, *parts)
+    return (image.reshape(-1, width), second.reshape(-1, width))
 
 
 def spread_kernel(place_ref, own_ref, *refs):
     out_ref = refs[-1]
     mine = place_ref[DP]
-    out_ref[mine] = own_ref[...].astype(out_ref.dtype)
-    for at, part_ref in enumerate(refs[:-1]):
-        out_ref[mine ^ (at + 1)] = part_ref[...].astype(out_ref.dtype)
+    for at, part_ref in enumerate([own_ref] + list(refs[:-1])):
+        for block in range(DP):
+            lanes = pl.ds(pl.multiple_of(place_ref[block] * LANES, LANES), LANES)
+            part = part_ref[:, block * LANES : (block + 1) * LANES]
+            out_ref[mine ^ at, :, lanes] = part.astype(out_ref.dtype)
 
 
 def spread_image(place, own, parts, dtype):
     chunk_rows, width = parts[0].shape
-    block = pl.BlockSpec((chunk_rows, LANES), lambda j, place_ref: (0, j))
+    rows = chunk_rows // 4
+    block = pl.BlockSpec((rows, width), lambda i, place_ref: (i, 0))
     return pl.pallas_call(
         spread_kernel,
         grid_spec=pltpu.PrefetchScalarGridSpec(
             num_scalar_prefetch=1,
-            grid=(width // LANES,),
+            grid=(4,),
             in_specs=[block] * (1 + len(parts)),
-            out_specs=pl.BlockSpec((MP, chunk_rows, LANES), lambda j, place_ref: (0, 0, place_ref[j])),
+            out_specs=pl.BlockSpec((MP, rows, width), lambda i, place_ref: (0, i, 0)),
         ),
         out_shape=jax.ShapeDtypeStruct((MP, chunk_rows, width), dtype),
+        compiler_params=pltpu.CompilerParams(vmem_limit_bytes=32 * 2**20),
+        cost_estimate=pl.CostEstimate(
+            flops=chunk_rows * width * 4, bytes_accessed=chunk_rows * width * 20, transcendentals=0
+        ),
         name="spread_image",
     )(place, own, *parts)
+
+
+ROWS = 256
+
+
+def product_nt(left_refs, right_refs):
+    total = None
+    for left_ref, right_ref in zip(left_refs, right_refs):
+        part = lax.dot_general(
+            left_ref[...], right_ref[...], (((1,), (1,)), ((), ())), preferred_element_type=F32
+        )
+        total = part if total is None else total + part
+    return total
+
+
+def add_rows(sums_ref, rows):
+    @pl.when(pl.program_id(0) == 0)
+    def _():
+        sums_ref[...] = jnp.zeros_like(sums_ref)
+
+    for at, each in enumerate(rows):
+        sums_ref[at : at + 1, :] += jnp.sum(each, 0, keepdims=True)
+
+
+def out_kernel(count, *refs):
+    lefts, rights = (refs[:count], refs[count : 2 * count])
+    vector_ref, base_ref, branch_ref, hidden_ref, normed_ref = refs[2 * count :]
+    branch = product_nt(lefts, rights) + vector_row(vector_ref, OUT_BIAS)
+    hidden = base_ref[...].astype(F32) + vector_row(vector_ref, SCALE_ONE) * branch
+    normal, _ = norm_parts(hidden)
+    branch_ref[...] = branch
+    hidden_ref[...] = hidden
+    normed = normal * vector_row(vector_ref, GAIN_TWO) + vector_row(vector_ref, SHIFT_TWO)
+    normed_ref[...] = normed.astype(BF)
+
+
+def down_kernel(count, *refs):
+    lefts, rights = (refs[:count], refs[count : 2 * count])
+    vector_ref, hidden_ref, grad_ref, output_ref, sums_ref = refs[2 * count :]
+    branch = product_nt(lefts, rights) + vector_row(vector_ref, DOWN_BIAS)
+    output = hidden_ref[...] + vector_row(vector_ref, SCALE_TWO) * branch
+    output_ref[...] = output.astype(BF)
+    grad = grad_ref[...].astype(F32)
+    add_rows(sums_ref, [grad * branch, grad])
+
+
+def up_back_kernel(count, *refs):
+    lefts, rights = (refs[:count], refs[count : 2 * count])
+    vector_ref, hidden_ref, branch_ref, grad_ref, out_ref, low_ref, sums_ref = refs[2 * count :]
+    grad_normed = product_nt(lefts, rights)
+    normal, spread = norm_parts(hidden_ref[...])
+    grad = norm_back(grad_normed, normal, spread, vector_row(vector_ref, GAIN_TWO))
+    grad = grad + grad_ref[...].astype(F32)
+    out_ref[...] = grad
+    low_ref[...] = (grad * vector_row(vector_ref, SCALE_ONE)).astype(BF)
+    add_rows(sums_ref, [grad_normed * normal, grad_normed, grad * branch_ref[...], grad])
+
+
+def in_back_kernel(count, *refs):
+    lefts, rights = (refs[:count], refs[count : 2 * count])
+    vector_ref, base_ref, grad_ref, own_ref, low_ref, sums_ref = refs[2 * count :]
+    grad_normed = product_nt(lefts, rights)
+    normal, spread = norm_parts(base_ref[...].astype(F32))
+    grad = norm_back(grad_normed, normal, spread, vector_row(vector_ref, GAIN_ONE))
+    grad = grad + grad_ref[...]
+    low_ref[...] = grad.astype(BF)
+
+    @pl.when(pl.program_id(0) == 0)
+    def _():
+        own_ref[...] = grad
+
+    add_rows(sums_ref, [grad_normed * normal, grad_normed])
+
+
+def row_call(kernel, name, lefts, rights, vector_full, row_inputs, outs):
+    rows, width = row_inputs[0].shape
+    once = pl.Buffered(1)
+    block = pl.BlockSpec((ROWS, width), lambda i: (i, 0))
+    specs = {
+        "sums": (pl.BlockSpec((8, width), lambda i: (0, 0)), jax.ShapeDtypeStruct((8, width), F32)),
+        "own": (
+            pl.BlockSpec((ROWS, width), lambda i: (0, 0)),
+            jax.ShapeDtypeStruct((ROWS, width), F32),
+        ),
+    }
+    pairs = [
+        specs[each] if isinstance(each, str) else (block, jax.ShapeDtypeStruct((rows, width), each))
+        for each in outs
+    ]
+    depth = sum(each.shape[1] for each in lefts)
+    return pl.pallas_call(
+        functools.partial(kernel, len(lefts)),
+        grid=(rows // ROWS,),
+        in_specs=[pl.BlockSpec((ROWS, each.shape[1]), lambda i: (i, 0)) for each in lefts]
+        + [pl.BlockSpec(each.shape, lambda i: (0, 0), pipeline_mode=once) for each in rights]
+        + [pl.BlockSpec(vector_full.shape, lambda i: (0, 0))]
+        + [block] * len(row_inputs),
+        out_specs=[each[0] for each in pairs],
+        out_shape=[each[1] for each in pairs],
+        compiler_params=pltpu.CompilerParams(vmem_limit_bytes=48 * 2**20),
+        cost_estimate=pl.CostEstimate(
+            flops=2 * rows * width * depth, bytes_accessed=rows * width * 24, transcendentals=0
+        ),
+        name=name,
+    )(*lefts, *rights, vector_full, *row_inputs)
 
 
 def lane_dot(left, right):
@@ -665,19 +814,6 @@
     return lax.dot_general(left, right, (((0,), (0,)), ((), ())), preferred_element_type=F32)
 
 
-def norm_parts(values):
-    center = values - jnp.mean(values, -1, keepdims=True)
-    spread = lax.rsqrt(jnp.mean(center * center, -1, keepdims=True) + 1e-06)
-    return (center * spread, spread)
-
-
-def norm_back(grad, normal, spread, gain):
-    scaled = grad * gain
-    inner = scaled - jnp.mean(scaled, -1, keepdims=True)
-    inner = inner - normal * jnp.mean(scaled * normal, -1, keepdims=True)
-    return (spread * inner, jnp.sum(grad * normal, 0), jnp.sum(grad, 0))
-
-
 def gelu_pair(values):
     share = 0.5 * (1.0 + lax.erf(values * 0.7071067811865476))
     slope = share + values * (0.3989422804014327 * jnp.exp(-0.5 * values * values))
@@ -750,19 +886,15 @@
         1,
     )
     both = ("xy", "yx")
+    rows_qkv = [Chain(rows_z_steps, each) for each in jnp.split(qkv_shard, 2, 1)]
     small = Chain(small_steps, small_shard, vector_size)
-    rows_qkv = Chain(rows_z_steps, qkv_shard)
     fetch_tokens = fetch_image(tokens)
-    rest_shard = meet(rest_shard, small, rows_qkv)
+    rest_shard = meet(rest_shard, rows_qkv[0], small)
+    get_qkv = [Chain(gather_steps, [rows_qkv[0].result], ("xy",)), None]
+    rest_shard = meet(rest_shard, small, rows_qkv[1])
+    get_qkv[1] = Chain(gather_steps, [rows_qkv[1].result], ("yx",))
     rows_rest = Chain(rows_z_steps, rest_shard)
-    get_qkv = Chain(gather_steps, jnp.split(rows_qkv.result, 2, 1), both)
-    meet((), small, get_qkv)
-    tokens = meet(tokens, small, fetch_tokens, rows_rest)
-    out_rows, up_rows, down_rows = jnp.split(
-        rows_rest.result, [block_width, block_width * (1 + units)], 1
-    )
-    get_out = Chain(gather_steps, [jnp.stack(jnp.split(out_rows, 2, 1))], ("yx",))
-    get_up = Chain(gather_steps, jnp.split(up_rows, 2, 1), both)
+    tokens = meet(tokens, small, get_qkv[0], fetch_tokens)
 
     vector_full, bias_small = small.result
     vector_full = vector_full.reshape(DP, vectors.shape[0], LANES).transpose(1, 0, 2)
@@ -771,52 +903,65 @@
     bias_rows = jnp.take(bias_small, back_places, axis=1).reshape(2, 2, DP, -1, bias_width)
     bias_full = bias_rows.transpose(1, 3, 0, 2, 4).reshape(2, head_biases.shape[0], 2, block_width)
     bias_full = bias_full.astype(F32)
-    gain_one, shift_one, out_bias, scale_one, gain_two, shift_two, down_bias, scale_two = vector_full
-
-    base = assemble_image(place, tokens[:, 0], fetch_tokens.result).astype(F32)
-    normal_one, spread_one = norm_parts(base)
-    normed_one = (normal_one * gain_one + shift_one).astype(BF)
-    normed_one = meet(normed_one, get_qkv, get_up, get_out)
-
-    def project(core, weights):
-        results = []
-        for half in (0, 1):
-            lanes = slice(half * LANES, (half + 1) * LANES)
-            zero = jnp.zeros((2, LANES), F32)
-            bias = jnp.stack([bias_full[core, 0, :, lanes], zero, bias_full[core, 1, :, lanes]], 1)
-            results.append((dot_nn(normed_one, weights[half]) + bias.reshape(-1)).astype(BF))
-        return results
-
-    heads, blended, log_total = ([None, None], [None, None], [None, None])
-    heads[0] = project(0, get_qkv.own)
-    heads[0] = meet(heads[0], get_qkv, get_out)
-    w_qkv = [get_qkv.own, get_qkv.result]
-    blended[0], log_total[0] = zip(*[attend(each) for each in heads[0]])
-    blended[0], normed_one, down_rows, cotangent = meet(
-        (blended[0], normed_one, down_rows, cotangent), get_up, get_out
-    )
+
+    base, normed_one = assemble_image(place, vector_full, tokens[:, 0], fetch_tokens.result, True)
+    normed_one = meet(normed_one, *get_qkv, rows_rest)
+    out_rows, up_rows, down_rows = jnp.split(
+        rows_rest.result, [block_width, block_width * (1 + units)], 1
+    )
+    get_out = Chain(gather_steps, [jnp.stack(jnp.split(out_rows, 2, 1))], ("yx",))
+    get_up = Chain(gather_steps, jnp.split(up_rows, 2, 1), both)
+
+    def project(core, half, weight):
+        lanes = slice(half * LANES, (half + 1) * LANES)
+        zero = jnp.zeros((2, LANES), F32)
+        bias = jnp.stack([bias_full[core, 0, :, lanes], zero, bias_full[core, 1, :, lanes]], 1)
+        return (dot_nn(normed_one, weight) + bias.reshape(-1)).astype(BF)
+
+    heads, blended, log_total = ([[None, None], [None, None]] for _ in range(3))
+
+    def forward_heads(core, half):
+        blended[core][half], log_total[core][half] = attend(heads[core][half])
+
+    heads[0][0] = project(0, 0, get_qkv[0].own[0])
+    forward_heads(0, 0)
+    blended[0][0], normed_one = meet((blended[0][0], normed_one), *get_qkv, get_out, get_up)
+    heads[0][1] = project(0, 1, get_qkv[1].own[0])
+    forward_heads(0, 1)
+    blended[0][1], normed_one, down_rows = meet((blended[0][1], normed_one, down_rows), get_qkv[1], get_out)
+    w_qkv = [[each.own[0] for each in get_qkv], [each.result[0] for each in get_qkv]]
     get_down = Chain(gather_steps, jnp.split(down_rows, 2, 1), both)
+    heads[1][0] = project(1, 0, w_qkv[1][0])
+    forward_heads(1, 0)
+    blended[1][0], normed_one, cotangent = meet(
+        (blended[1][0], normed_one, cotangent), get_up, get_out
+    )
     fetch_cotangent = fetch_image(cotangent)
-    heads[1] = project(1, w_qkv[1])
-    blended[1], log_total[1] = zip(*[attend(each) for each in heads[1]])
+    heads[1][1] = project(1, 1, w_qkv[1][1])
+    forward_heads(1, 1)
     blended = meet(blended, get_up, get_down)
     w_up = [get_up.own, get_up.result]
-    blended = [jnp.concatenate(each, 1) for each in blended]
-    w_out = [jnp.concatenate([each[0][0], each[0][1]], 1) for each in (get_out.own, get_out.result)]
-    branch_one = dot_nt(jnp.concatenate(blended, 1), jnp.concatenate(w_out, 1)) + out_bias
-    hidden = base + scale_one * branch_one
-    normal_two, spread_two = norm_parts(hidden)
-    normed_two = (normal_two * gain_two + shift_two).astype(BF)
-    normed_two = meet(normed_two, fetch_cotangent)
-    grad_out = assemble_image(place, cotangent[:, 0], fetch_cotangent.result).astype(F32)
-    grad_branch = (grad_out * scale_two).astype(BF)
+    w_out = [[each[0][half] for half in (0, 1)] for each in (get_out.own, get_out.result)]
+    pairs = [(core, half) for core in cores for half in (0, 1)]
+    branch_one, hidden, normed_two = row_call(
+        out_kernel,
+        "out_norm",
+        [blended[core][half] for core, half in pairs],
+        [w_out[core][half] for core, half in pairs],
+        vector_full,
+        [base],
+        [F32, F32, BF],
+    )
     parts = [(half, core) for core in (1, 0) for half in (0, 1)]
     activ, slope = ({}, {})
     for half, core in parts:
         rows = bias_full[core, 2 + half * half_units : 2 + (half + 1) * half_units]
         pre_act = dot_nn(normed_two, w_up[core][half]) + rows.transpose(1, 0, 2).reshape(-1)
         activ[half, core], slope[half, core] = gelu_pair(pre_act)
-    activ, slope, grad_branch = meet((activ, slope, grad_branch), get_down)
+    activ, slope, cotangent = meet((activ, slope, cotangent), get_down, fetch_cotangent)
+    grad_out, grad_branch = assemble_image(
+        place, vector_full, cotangent[:, 0], fetch_cotangent.result, False
+    )
 
     def reduce_pairs(left, rights):
         chain = Chain(reduce_steps, [dot_tn(left, rights[half, 1]).astype(BF) for half in (0, 1)], both[::-1])
@@ -826,10 +971,15 @@
     sum_down = reduce_pairs(grad_branch, activ)
     grad_branch, activ = meet((grad_branch, activ), sum_down, get_down)
     w_down = [get_down.own, get_down.result]
-    branch_two = down_bias
-    for half, core in parts:
-        branch_two = branch_two + dot_nt(activ[half, core], w_down[core][half])
-    output = (hidden + scale_two * branch_two).astype(BF)
+    output, sums_two = row_call(
+        down_kernel,
+        "down_output",
+        [activ[each] for each in parts],
+        [w_down[core][half] for half, core in parts],
+        vector_full,
+        [hidden, grad_out],
+        [BF, "sums"],
+    )
     output, grad_branch, slope = meet((output, grad_branch, slope))
     send_output = send_back(output)
     grad_pre = {}
@@ -838,20 +988,23 @@
         grad_pre[half, core] = (grad_activ * slope[half, core].astype(F32)).astype(BF)
     grad_pre, normed_two = meet((grad_pre, normed_two), sum_down)
     sum_up = reduce_pairs(normed_two, grad_pre)
-    grad_normed_two = 0.0
-    for half, core in parts:
-        grad_normed_two = grad_normed_two + dot_nt(grad_pre[half, core], w_up[core][half])
-    grad_hidden, grad_gain_two, grad_shift_two = norm_back(
-        grad_normed_two, normal_two, spread_two, gain_two
-    )
-    grad_hidden = grad_out + grad_hidden
-    grad_projected = (grad_hidden * scale_one).astype(BF)
+    grad_hidden, grad_projected, sums_one = row_call(
+        up_back_kernel,
+        "up_norm_back",
+        [grad_pre[each] for each in parts],
+        [w_up[core][half] for half, core in parts],
+        vector_full,
+        [hidden, branch_one, grad_out],
+        [F32, BF, "sums"],
+    )
     grad_projected = meet(grad_projected, sum_up, sum_down, send_output)
     rows_down = Chain(sum_z_steps, jnp.concatenate(sum_down.result, 1))
-    grad_w_out = [jnp.stack(jnp.split(dot_tn(grad_projected, each).astype(BF), 2, 1)) for each in blended]
+    grad_w_out = [
+        jnp.stack([dot_tn(grad_projected, each).astype(BF) for each in blended[core]]) for core in cores
+    ]
     sum_out = Chain(reduce_steps, [grad_w_out[1]], ("xy",))
     sum_out.own = [grad_w_out[0]]
-    grad_blended = [jnp.split(dot_nn(grad_projected, each).astype(BF), 2, 1) for each in w_out]
+    grad_blended = [[dot_nn(grad_projected, each).astype(BF) for each in w_out[core]] for core in cores]
     grad_heads = [[None, None], [None, None]]
 
     def back_heads(core, half):
@@ -872,25 +1025,26 @@
     rows_rest = Chain(sum_z_steps, jnp.concatenate(sum_up.result + [out_rows], 1))
     sum_qkv[1].own = [back_heads(0, 1)]
     grad_heads = meet(grad_heads, sum_qkv[0], sum_qkv[1])
-    grad_normed_one = 0.0
-    for core in cores:
-        for half in (0, 1):
-            grad_normed_one = grad_normed_one + dot_nt(grad_heads[core][half], w_qkv[core][half])
-    grad_input, grad_gain_one, grad_shift_one = norm_back(
-        grad_normed_one, normal_one, spread_one, gain_one
-    )
-    grad_input = grad_hidden + grad_input
+    own_grad, grad_input, sums_input = row_call(
+        in_back_kernel,
+        "in_norm_back",
+        [grad_heads[core][half] for core, half in pairs],
+        [w_qkv[core][half] for core, half in pairs],
+        vector_full,
+        [base, grad_hidden],
+        ["own", BF, "sums"],
+    )
 
     grad_vectors = jnp.stack(
         [
-            grad_gain_one,
-            grad_shift_one,
-            jnp.sum(grad_hidden, 0) * scale_one,
-            jnp.sum(grad_hidden * branch_one, 0),
-            grad_gain_two,
-            grad_shift_two,
-            jnp.sum(grad_out, 0) * scale_two,
-            jnp.sum(grad_out * branch_two, 0),
+            sums_input[0],
+            sums_input[1],
+            sums_one[3] * vector_full[SCALE_ONE],
+            sums_one[2],
+            sums_one[0],
+            sums_one[1],
+            sums_two[1] * vector_full[SCALE_TWO],
+            sums_two[0],
         ]
     )
     grad_vectors = grad_vectors.reshape(-1, DP, LANES).transpose(1, 0, 2).reshape(DP, -1)
@@ -914,7 +1068,7 @@
     rows_qkv = Chain(sum_z_steps, jnp.concatenate(sum_qkv[0].result + sum_qkv[1].result, 1))
     meet((), rows_qkv, sum_small, send_grad)
     layer_output = spread_image(place, output[:chunk_rows], send_output.result, BF)[:, None]
-    input_grad = spread_image(place, grad_input[:chunk_rows], send_grad.result, F32)[:, None]
+    input_grad = spread_image(place, own_grad, send_grad.result, F32)[:, None]
 
     small_total = sum_small.result
     vector_grad = small_total[:vector_size].reshape(vectors.shape)

time: 674 us -> 661 us (0.981)
  matrix products: 168 us -> 107 us
  Pallas kernels: 127 us -> 170 us
  waiting for transfers between devices: 110 us -> 150 us
  other arithmetic: 98.3 us -> 68.7 us
    dot_general x13 -> x0, matrix products: 64.5 us -> none  [dot_nt(): lax.dot_general(left, right, (((1,), (1,)), ((), ())), preferred_element_...]
    pallas_call x2 -> x6, Pallas kernels: 13 us -> 62.2 us  [the longest x4 55.8 us: row_call(): pl.pallas_call(functools.partial(kernel, len(lefts)), grid=(rows // ROWS,...]
    ppermute x46, waiting for transfers between devices: 38.3 us -> 74.9 us  [swap_mp(): return lax.ppermute(part, 'mp', [(each, each ^ step) for each in range(MP)])]
    convert_element_type x5 -> x0, other arithmetic: 12 us -> none  [the longest x1 6.12 us: send_back(): low = array.astype(BF)]
    reduce_sum x4 -> x0, other arithmetic: 9.3 us -> none  [the longest x1 5.97 us: local_image(): jnp.sum(grad_hidden * branch_one, 0)]
    dot_general x14 -> x16, matrix products: 61.4 us -> 68.8 us  [dot_nn(): lax.dot_general(left, right, (((1,), (0,)), ((), ())), preferred_element_...]
    convert_element_type x21, other arithmetic: 29.4 us -> 22.6 us  [add_low(): return (first.astype(F32) + second.astype(F32)).astype(BF)]
    dot_general x14 -> x16, matrix products: 42.2 us -> 38.5 us  [dot_tn(): lax.dot_general(left, right, (((0,), (0,)), ((), ())), preferred_element_...]
  transfers between devices with their start and end apart: 83 -> 86, of which waited for: 18 -> 20; matrix products, arithmetic and copies ran while one was open for 44% -> 28% of each run, Pallas kernels for 18% -> 20%
where the time goes in v4:
time: 661 us; the launch traced here: 656 us
  Pallas kernels  170 us (26%)
  waiting for transfers between devices  150 us (23%)
  matrix products  107 us (16%)
  starting transfers between devices  91 us (14%)
  other arithmetic  68.7 us (10%)
  local copies, waits for them, and re-layouts  64.9 us (10%)
    ppermute x46, waiting for transfers between devices, swap_mp(): return lax.ppermute(part, 'mp', [(each, each ^ step) for each in range(MP)])  74.9 us
    dot_general x16, matrix products, dot_nn(): lax.dot_general(left, right, (((1,), (0,)), ((), ())), preferred_element_...  68.8 us
    pallas_call x4, Pallas kernels, attend_back(): pl.pallas_call(functools.partial(attend_back_kernel, 256), grid=(pairs,),...  64.1 us
    pallas_call x4, Pallas kernels, row_call(): pl.pallas_call(functools.partial(kernel, len(lefts)), grid=(rows // ROWS,...  55.8 us
    ppermute x24, waiting for transfers between devices, swap_z(): lax.ppermute(part, 'dp', [(z * YS + y, (z ^ step) * YS + y) for z in rang...  48.7 us
    ppermute x24, starting transfers between devices, swap_z(): lax.ppermute(part, 'dp', [(z * YS + y, (z ^ step) * YS + y) for z in rang...  46.4 us
    dot_general x16, matrix products, dot_tn(): lax.dot_general(left, right, (((0,), (0,)), ((), ())), preferred_element_...  38.5 us
    pallas_call x4, Pallas kernels, attend(): pl.pallas_call(functools.partial(attend_kernel, 256), grid=(pairs,), in_s...  35.9 us
  transfers between devices with their start and end apart: 86, of which 20 were waited for; matrix products, arithmetic and copies ran while one was open for 28% of the time, Pallas kernels for 20%

profile of v4, /device:TPU:0, one launch (start us, length us, event | category | flops | bytes accessed | tf_op | source)
XLA Modules:
  0.0 655.6 jit_solution(11115373842778957497)
XLA Ops:
  2.9 3.1 collective-permute-start
  5.9 2.6 collective-permute-start.1
  9.6 3.5 collective-permute-start.4
  20.2 4.6 collective-permute-done.5
  41.9 21.7 %collective-permute-done.11 = bf16[8,192]{1,0:T(8,128)(2,1)S(1)} collective-permute-done((bf16[8,192]{1,0:T(8,128)(2,1)S(1)}, bf16[8,192]{1,0:T(8,128)(2,1)S(1)}, u32[]{:S(2)}, u32[]{:S(2)}) %collective-permute-start.11) | collective-permute-done | bytes 3104 | tf_op jit(solution)/shard_map/ppermute | solution.py:378
  66.7 2.8 collective-permute-start.19
  77.1 4.7 assemble_image.2
  81.8 2.4 collective-permute-done.18
  84.2 10.2 %collective-permute-done.19 = bf16[128,2304]{1,0:T(8,128)(2,1)} collective-permute-done((bf16[128,2304]{1,0:T(8,128)(2,1)}, bf16[128,2304]{1,0:T(8,128)(2,1)}, u32[]{:S(2)}, u32[]{:S(2)}) %collective-permute-start.19) | collective-permute-done | bytes 589856 | tf_op jit(solution)/shard_map/ppermute | solution.py:368
  94.4 17.8 %collective-permute-done.20 = bf16[128,2304]{1,0:T(8,128)(2,1)} collective-permute-done((bf16[128,2304]{1,0:T(8,128)(2,1)}, bf16[128,2304]{1,0:T(8,128)(2,1)}, u32[]{:S(2)}, u32[]{:S(2)}) %collective-permute-start.20) | collective-permute-done | bytes 589856 | tf_op jit(solution)/shard_map/ppermute | solution.py:368
  122.9 3.1 add_convert_fusion.9.q_ref.k_ref.v_ref
  126.0 8.8 %attend.4 = (bf16[1024,256]{1,0:T(8,128)(2,1)S(1)}, f32[2,8,1024]{2,1,0:T(8,128)S(1)}) custom-call(bf16[1024,768]{1,0:T(8,128)(2,1)S(1)} %add_convert_fusion.9.q_ref.k_ref.v_ref, bf16[1024,768]{1,0:T(8,128)(2,1)S(1)} %add_convert_fusion.9.q_ref.k_ref.v_ref, bf16[1024,768]{1,0:T(8,128)(2,1)S(1)} %add_convert_fusion.9.q_ref.k_ref.v_ref), custom_call_target="tpu_custom_call" | custom-call | flops 4294967296 | bytes 6291456 | tf_op jit(solution)/shard_map/attend/pallas_call | solution.py:762
  134.9 11.1 %collective-permute-done.25 = bf16[512,512]{1,0:T(8,128)(2,1)S(1)} collective-permute-done((bf16[512,512]{1,0:T(8,128)(2,1)S(1)}, bf16[512,512]{1,0:T(8,128)(2,1)S(1)}, u32[]{:S(2)}, u32[]{:S(2)}) %collective-permute-start.25) | collective-permute-done | bytes 524320 | tf_op jit(solution)/shard_map/ppermute | solution.py:378
  159.6 9.0 %attend.5 = (bf16[1024,256]{1,0:T(8,128)(2,1)S(1)}, f32[2,8,1024]{2,1,0:T(8,128)S(1)}) custom-call(bf16[1024,768]{1,0:T(8,128)(2,1)S(1)} %add_convert_fusion.8.q_ref.k_ref.v_ref, bf16[1024,768]{1,0:T(8,128)(2,1)S(1)} %add_convert_fusion.8.q_ref.k_ref.v_ref, bf16[1024,768]{1,0:T(8,128)(2,1)S(1)} %add_convert_fusion.8.q_ref.k_ref.v_ref), custom_call_target="tpu_custom_call" | custom-call | flops 4294967296 | bytes 6291456 | tf_op jit(solution)/shard_map/attend/pallas_call | solution.py:762
  169.8 3.2 add_convert_fusion.7.q_ref.k_ref.v_ref
  173.0 9.2 %attend.6 = (bf16[1024,256]{1,0:T(8,128)(2,1)S(1)}, f32[2,8,1024]{2,1,0:T(8,128)S(1)}) custom-call(bf16[1024,768]{1,0:T(8,128)(2,1)S(1)} %add_convert_fusion.7.q_ref.k_ref.v_ref, bf16[1024,768]{1,0:T(8,128)(2,1)S(1)} %add_convert_fusion.7.q_ref.k_ref.v_ref, bf16[1024,768]{1,0:T(8,128)(2,1)S(1)} %add_convert_fusion.7.q_ref.k_ref.v_ref), custom_call_target="tpu_custom_call" | custom-call | flops 4294967296 | bytes 6291456 | tf_op jit(solution)/shard_map/attend/pallas_call | solution.py:762
  182.3 4.6 collective-permute-done.30
  186.9 2.9 pad_maximum_fusion.refs_6_
  189.9 2.8 pad_maximum_fusion.1.refs_7_
  200.6 3.2 add_convert_fusion.6.q_ref.k_ref.v_ref
  203.8 8.8 %attend.7 = (bf16[1024,256]{1,0:T(8,128)(2,1)S(1)}, f32[2,8,1024]{2,1,0:T(8,128)S(1)}) custom-call(bf16[1024,768]{1,0:T(8,128)(2,1)S(1)} %add_convert_fusion.6.q_ref.k_ref.v_ref, bf16[1024,768]{1,0:T(8,128)(2,1)S(1)} %add_convert_fusion.6.q_ref.k_ref.v_ref, bf16[1024,768]{1,0:T(8,128)(2,1)S(1)} %add_convert_fusion.6.q_ref.k_ref.v_ref), custom_call_target="tpu_custom_call" | custom-call | flops 4294967296 | bytes 6291456 | tf_op jit(solution)/shard_map/attend/pallas_call | solution.py:762
  214.6 7.1 %out_norm.1 = (f32[1024,1024]{1,0:T(8,128)}, f32[1024,1024]{1,0:T(8,128)}, bf16[1024,1024]{1,0:T(8,128)(2,1)}) custom-call(bf16[1024,256]{1,0:T(8,128)(2,1)S(1)} %get-tuple-element.231.refs_0_, bf16[1024,256]{1,0:T(8,128)(2,1)S(1)} %get-tuple-element.232.refs_1_, bf16[1024,256]{1,0:T(8,128)(2,1)S(1)} %copy-done.18, ...), custom_call_target="tpu_custom_call" | custom-call | flops 2147483648 | bytes 25165824 | tf_op jit(solution)/shard_map/out_norm/pallas_call | solution.py:664
  221.7 10.3 %fusion.4 = (bf16[1024,1024]{1,0:T(8,128)(2,1)}, bf16[1024,1024]{1,0:T(8,128)(2,1)}) fusion(f32[1024]{0:T(1024)S(1)} %bitcast.368, bf16[1024,1024]{1,0:T(8,128)(2,1)} %get-tuple-element.282, bf16[512,1024]{1,0:T(8,128)(2,1)} %collective-permute-done.29, bf16[512,512]{1,0:T(8,128)(2,1)S(1)} %copy-done.79, bf16[512,512]{1,0:T(8,128)(2,1)S(1)} %copy-done.41), kind=kOutput, calls=%fused_computation.10 | convolution fusion | flops 2166358016 | bytes 8392704 | tf_op jit(solution)/shard_map/dot_general | solution.py:806
  232.0 8.6 %fusion.14 = (bf16[1024,1024]{1,0:T(8,128)(2,1)}, bf16[1024,1024]{1,0:T(8,128)(2,1)}) fusion(f32[1024]{0:T(1024)S(1)} %bitcast.369, bf16[1024,1024]{1,0:T(8,128)(2,1)S(1)} %copy-done.123, bf16[1024,512]{1,0:T(8,128)(2,1)} %collective-permute-done.30, bf16[512,512]{1,0:T(8,128)(2,1)S(1)} %copy-done.76, bf16[512,512]{1,0:T(8,128)(2,1)S(1)} %copy-done.38), kind=kOutput, calls=%fused_computation.20 | convolution fusion | flops 2166358016 | bytes 8392704 | tf_op jit(solution)/shard_map/dot_general | solution.py:806
  243.0 6.6 %fusion.9 = (bf16[1024,1024]{1,0:T(8,128)(2,1)}, bf16[1024,1024]{1,0:T(8,128)(2,1)S(1)}) fusion(f32[1024]{0:T(1024)S(1)} %bitcast.366, bf16[1024,1024]{1,0:T(8,128)(2,1)S(1)} %copy-done.123, bf16[1024,1024]{1,0:T(8,128)(2,1)} %collective-permute-done.32.refs_4_), kind=kOutput, calls=%fused_computation.15 | convolution fusion | flops 2160066560 | bytes 8392704 | tf_op jit(solution)/shard_map/dot_general | solution.py:806
  249.7 7.4 %fusion.19 = (bf16[1024,1024]{1,0:T(8,128)(2,1)}, bf16[1024,1024]{1,0:T(8,128)(2,1)S(1)}) fusion(f32[1024]{0:T(1024)S(1)} %bitcast.367, bf16[1024,1024]{1,0:T(8,128)(2,1)S(1)} %copy-done.123, bf16[1024,1024]{1,0:T(8,128)(2,1)} %collective-permute-done.33.refs_5_), kind=kOutput, calls=%fused_computation.25 | convolution fusion | flops 2160066560 | bytes 8392704 | tf_op jit(solution)/shard_map/dot_general | solution.py:806
  257.1 9.1 %collective-permute-done.36 = bf16[512,1024]{1,0:T(8,128)(2,1)S(1)} collective-permute-done((bf16[512,1024]{1,0:T(8,128)(2,1)S(1)}, bf16[512,1024]{1,0:T(8,128)(2,1)S(1)}, u32[]{:S(2)}, u32[]{:S(2)}) %collective-permute-start.36) | collective-permute-done | bytes 1048608 | tf_op jit(solution)/shard_map/ppermute | solution.py:374
  269.4 3.8 convolution_convert_fusion.3
  273.2 3.7 convolution_convert_fusion.2
  285.1 4.2 fusion.64
  291.8 15.7 %down_output.1 = (bf16[1024,1024]{1,0:T(8,128)(2,1)S(1)}, f32[8,1024]{1,0:T(8,128)S(1)}) custom-call(bf16[1024,1024]{1,0:T(8,128)(2,1)S(1)} %copy-done.29, bf16[1024,1024]{1,0:T(8,128)(2,1)} %copy-done.131, bf16[1024,1024]{1,0:T(8,128)(2,1)} %get-tuple-element.256.refs_2_, bf16[1024,1024]{1,0:T(8,128)(2,1)} %get-tuple-element.257.refs_3_, ...), custom_call_target="tpu_custom_call" | custom-call | flops 8589934592 | bytes 25165824 | tf_op jit(solution)/shard_map/down_output/pallas_call | solution.py:664
  310.4 3.7 multiply_convert_fusion.3.refs_2_
  314.1 4.6 multiply_convert_fusion.2.refs_0_
  318.6 2.6 add_convert_fusion.3
  321.8 2.7 add_convert_fusion.2
  327.1 3.8 multiply_convert_fusion.1.refs_3_
  330.9 3.9 multiply_convert_fusion.refs_1_
  334.9 11.5 %collective-permute-done.45 = bf16[512,1024]{1,0:T(8,128)(2,1)S(1)} collective-permute-done((bf16[512,1024]{1,0:T(8,128)(2,1)S(1)}, bf16[512,1024]{1,0:T(8,128)(2,1)S(1)}, u32[]{:S(2)}, u32[]{:S(2)}) %collective-permute-start.45) | collective-permute-done | bytes 1048608 | tf_op jit(solution)/shard_map/ppermute | solution.py:374
  346.4 4.4 collective-permute-done.46
  351.2 3.7 convolution_convert_fusion
  355.0 4.0 convolution_convert_fusion.1
  367.4 19.0 %up_norm_back.1 = (f32[1024,1024]{1,0:T(8,128)}, bf16[1024,1024]{1,0:T(8,128)(2,1)S(1)}, f32[8,1024]{1,0:T(8,128)S(1)}) custom-call(bf16[1024,1024]{1,0:T(8,128)(2,1)S(1)} %multiply_convert_fusion.2.refs_0_, bf16[1024,1024]{1,0:T(8,128)(2,1)} %copy-done.69, bf16[1024,1024]{1,0:T(8,128)(2,1)} %multiply_convert_fusion.3.refs_2_, ...), custom_call_target="tpu_custom_call" | custom-call | flops 8589934592 | bytes 25165824 | tf_op jit(solution)/shard_map/up_norm_back/pallas_call | solution.py:664
  386.5 2.4 fusion.66
  393.5 9.4 %collective-permute-done.49 = bf16[512,512]{1,0:T(8,128)(2,1)S(1)} collective-permute-done((bf16[512,512]{1,0:T(8,128)(2,1)S(1)}, bf16[512,512]{1,0:T(8,128)(2,1)S(1)}, u32[]{:S(2)}, u32[]{:S(2)}) %collective-permute-start.49) | collective-permute-done | bytes 524320 | tf_op jit(solution)/shard_map/ppermute | solution.py:378
  404.9 2.5 convolution_convert_fusion.14.g_ref
  409.2 2.6 convolution_convert_fusion.12.g_ref
  413.6 2.6 add_convert_fusion.1
  417.9 2.6 add_convert_fusion
  422.8 11.6 %collective-permute-start.57 = (bf16[128,1024]{1,0:T(8,128)(2,1)S(1)}, bf16[128,1024]{1,0:T(8,128)(2,1)S(1)}, u32[]{:S(2)}, u32[]{:S(2)}) collective-permute-start(bf16[128,1024]{1,0:T(8,128)(2,1)S(1)} %get-tuple-element.523), channel_id=1, source_target_pairs={{0,8},{4,12},{8,0},{12,4},{16,24},{20,28},{24,16},{28,20},{1,9},{5... | collective-permute-start | bytes 786440 | tf_op jit(solution)/shard_map/ppermute | solution.py:368
  434.4 16.1 %attend_back.4.refs_2_ = bf16[1024,768]{1,0:T(8,128)(2,1)S(1)} custom-call(bf16[1024,768]{1,0:T(8,128)(2,1)S(1)} %copy-done.27, bf16[1024,768]{1,0:T(8,128)(2,1)S(1)} %copy-done.27, bf16[1024,768]{1,0:T(8,128)(2,1)S(1)} %copy-done.27, bf16[1024,256]{1,0:T(8,128)(2,1)S(1)} %convolution_convert_fusion.15.g_ref, f32[2,8,1024]{2,1,0:T(8,128)S(1)} %get-tuple-element.289.lse_ref), custom_call_target="tpu_custom_call" | custom-call | flops 10737418240 | bytes 11010048 | tf_op jit(solution)/shard_map/attend_back/pallas_call | solution.py:786
  450.6 4.4 spread_image.2
  455.0 3.0 convolution_convert_fusion.7
  458.8 2.5 collective-permute-start.59
  462.1 7.0 %collective-permute-done.59 = bf16[128,1024]{1,0:T(8,128)(2,1)S(1)} collective-permute-done((bf16[128,1024]{1,0:T(8,128)(2,1)S(1)}, bf16[128,1024]{1,0:T(8,128)(2,1)S(1)}, u32[]{:S(2)}, u32[]{:S(2)}) %collective-permute-start.59) | collective-permute-done | bytes 262176 | tf_op jit(solution)/shard_map/ppermute | solution.py:368
  478.6 15.9 %attend_back.5.refs_0_ = bf16[1024,768]{1,0:T(8,128)(2,1)S(1)} custom-call(bf16[1024,768]{1,0:T(8,128)(2,1)S(1)} %copy-done.31, bf16[1024,768]{1,0:T(8,128)(2,1)S(1)} %copy-done.31, bf16[1024,768]{1,0:T(8,128)(2,1)S(1)} %copy-done.31, bf16[1024,256]{1,0:T(8,128)(2,1)S(1)} %copy-done.12, f32[2,8,1024]{2,1,0:T(8,128)S(1)} %get-tuple-element.295.lse_ref), custom_call_target="tpu_custom_call" | custom-call | flops 10737418240 | bytes 11010048 | tf_op jit(solution)/shard_map/attend_back/pallas_call | solution.py:786
  498.7 16.0 %attend_back.6.refs_3_ = bf16[1024,768]{1,0:T(8,128)(2,1)S(1)} custom-call(bf16[1024,768]{1,0:T(8,128)(2,1)S(1)} %copy-done.25, bf16[1024,768]{1,0:T(8,128)(2,1)S(1)} %copy-done.25, bf16[1024,768]{1,0:T(8,128)(2,1)S(1)} %copy-done.25, bf16[1024,256]{1,0:T(8,128)(2,1)S(1)} %copy-done.11, f32[2,8,1024]{2,1,0:T(8,128)S(1)} %get-tuple-element.304.lse_ref), custom_call_target="tpu_custom_call" | custom-call | flops 10737418240 | bytes 11010048 | tf_op jit(solution)/shard_map/attend_back/pallas_call | solution.py:786
  524.3 2.8 collective-permute-done.64
  528.3 5.2 collective-permute-start.72
  536.1 16.1 %attend_back.7.refs_1_ = bf16[1024,768]{1,0:T(8,128)(2,1)S(1)} custom-call(bf16[1024,768]{1,0:T(8,128)(2,1)S(1)} %copy-done.23, bf16[1024,768]{1,0:T(8,128)(2,1)S(1)} %copy-done.23, bf16[1024,768]{1,0:T(8,128)(2,1)S(1)} %copy-done.23, bf16[1024,256]{1,0:T(8,128)(2,1)S(1)} %convolution_convert_fusion.13.g_ref, f32[2,8,1024]{2,1,0:T(8,128)S(1)} %get-tuple-element.308.lse_ref), custom_call_target="tpu_custom_call" | custom-call | flops 10737418240 | bytes 11010048 | tf_op jit(solution)/shard_map/attend_back/pallas_call | solution.py:786
  555.4 14.0 %in_norm_back.1 = (f32[256,1024]{1,0:T(8,128)S(1)}, bf16[1024,1024]{1,0:T(8,128)(2,1)}, f32[8,1024]{1,0:T(8,128)S(1)}) custom-call(bf16[1024,768]{1,0:T(8,128)(2,1)S(1)} %attend_back.5.refs_0_, bf16[1024,768]{1,0:T(8,128)(2,1)S(1)} %attend_back.7.refs_1_, bf16[1024,768]{1,0:T(8,128)(2,1)S(1)} %attend_back.4.refs_2_, bf16[1024,768]{1,0:T(8,128)(2,1)} %copy-done.2, ...), custom_call_target="tpu_custom_call" | custom-call | flops 6442450944 | bytes 25165824 | tf_op jit(solution)/shard_map/in_norm_back/pallas_call | solution.py:664
  579.4 20.3 %collective-permute-done.70 = f32[8,1216]{1,0:T(8,128)S(1)} collective-permute-done((f32[8,1216]{1,0:T(8,128)S(1)}, f32[8,1216]{1,0:T(8,128)S(1)}, u32[]{:S(2)}, u32[]{:S(2)}) %collective-permute-start.70) | collective-permute-done | bytes 38944 | tf_op jit(solution)/shard_map/ppermute | solution.py:378
  611.5 3.4 multiply_subtract_fusion.1
  633.5 8.2 %collective-permute-done.81 = f32[1216]{0:T(1024)S(1)} collective-permute-done((f32[1216]{0:T(1024)S(1)}, f32[1216]{0:T(1024)S(1)}, u32[]{:S(2)}, u32[]{:S(2)}) %collective-permute-start.81) | collective-permute-done | bytes 4896 | tf_op jit(solution)/shard_map/ppermute | solution.py:368
  652.3 3.1 spread_image.3
  (641 shorter events, 199.6 us)
Async XLA Ops:
  2.9 22.0 %collective-permute-start = (bf16[128,384]{1,0:T(8,128)(2,1)S(1)}, bf16[128,384]{1,0:T(8,128)(2,1)}, u32[]{:S(2)}, u32[]{:S(2)}) collective-permute-start(bf16[128,384]{1,0:T(8,128)(2,1)S(1)} %copy.347), channel_id=1, source_target_pairs={{0,8},{4,12},{8,0},{12,4},{16,24},{20,28},{24,16},{28,20},{1,9},{5... | collective-permute-start | bytes 294920 | tf_op jit(solution)/shard_map/ppermute | solution.py:368
  5.9 19.6 %collective-permute-start.1 = (bf16[128,384]{1,0:T(8,128)(2,1)S(1)}, bf16[128,384]{1,0:T(8,128)(2,1)}, u32[]{:S(2)}, u32[]{:S(2)}) collective-permute-start(bf16[128,384]{1,0:T(8,128)(2,1)S(1)} %copy.347), channel_id=1, source_target_pairs={{0,16},{4,20},{8,24},{12,28},{16,0},{20,4},{24,8},{28,12},{1,17},{... | collective-permute-start | bytes 294920 | tf_op jit(solution)/shard_map/ppermute | solution.py:368
  8.5 17.0 %collective-permute-start.2 = (bf16[128,384]{1,0:T(8,128)(2,1)S(1)}, bf16[128,384]{1,0:T(8,128)(2,1)}, u32[]{:S(2)}, u32[]{:S(2)}) collective-permute-start(bf16[128,384]{1,0:T(8,128)(2,1)S(1)} %copy.347), channel_id=1, source_target_pairs={{0,24},{4,28},{8,16},{12,20},{16,8},{20,12},{24,0},{28,4},{1,25},{... | collective-permute-start | bytes 294920 | tf_op jit(solution)/shard_map/ppermute | solution.py:368
  25.5 44.9 %collective-permute-start.14 = (bf16[256,1024]{1,0:T(8,128)(2,1)}, bf16[256,1024]{1,0:T(8,128)(2,1)S(1)}, u32[]{:S(2)}, u32[]{:S(2)}) collective-permute-start(bf16[256,1024]{1,0:T(8,128)(2,1)} %get-tuple-element.518), channel_id=1, source_target_pairs={{0,1},{1,0},{2,3},{3,2},{4,5},{5,4},{6,7},{7,6},{8,9},{9,8},{10,11... | collective-permute-start | bytes 1572872 | tf_op jit(solution)/shard_map/ppermute | solution.py:378
  29.5 42.3 %collective-permute-start.15 = (bf16[256,1024]{1,0:T(8,128)(2,1)}, bf16[256,1024]{1,0:T(8,128)(2,1)S(1)}, u32[]{:S(2)}, u32[]{:S(2)}) collective-permute-start(bf16[256,1024]{1,0:T(8,128)(2,1)} %get-tuple-element.517), channel_id=1, source_target_pairs={{0,2},{1,3},{2,0},{3,1},{4,6},{5,7},{6,4},{7,5},{8,10},{9,11},{10,... | collective-permute-start | bytes 1572872 | tf_op jit(solution)/shard_map/ppermute | solution.py:378
  31.9 40.4 %collective-permute-start.16 = (bf16[256,1024]{1,0:T(8,128)(2,1)}, bf16[256,1024]{1,0:T(8,128)(2,1)}, u32[]{:S(2)}, u32[]{:S(2)}) collective-permute-start(bf16[256,1024]{1,0:T(8,128)(2,1)} %get-tuple-element.516), channel_id=1, source_target_pairs={{0,3},{1,2},{2,1},{3,0},{4,7},{5,6},{6,5},{7,4},{8,11},{9,10},{10,... | collective-permute-start | bytes 1572872 | tf_op jit(solution)/shard_map/ppermute | solution.py:378
  32.6 36.9 %collective-permute-start.13 = (bf16[512,384]{1,0:T(8,128)(2,1)}, bf16[512,384]{1,0:T(8,128)(2,1)}, u32[]{:S(2)}, u32[]{:S(2)}) collective-permute-start(bf16[512,384]{1,0:T(8,128)(2,1)} %pad_maximum_fusion.16), channel_id=1, source_target_pairs={{0,2},{1,3},{2,0},{3,1},{4,6},{5,7},{6,4},{7,5},{8,10},{9,11},{10,... | collective-permute-start | bytes 1179656 | tf_op jit(solution)/shard_map/ppermute | solution.py:378
  40.1 23.6 %collective-permute-start.11 = (bf16[8,192]{1,0:T(8,128)(2,1)S(1)}, bf16[8,192]{1,0:T(8,128)(2,1)S(1)}, u32[]{:S(2)}, u32[]{:S(2)}) collective-permute-start(bf16[8,192]{1,0:T(8,128)(2,1)S(1)} %get-tuple-element.560), channel_id=1, source_target_pairs={{0,2},{1,3},{2,0},{3,1},{4,6},{5,7},{6,4},{7,5},{8,10},{9,11},{10,... | collective-permute-start | bytes 9224 | tf_op jit(solution)/shard_map/ppermute | solution.py:378
  66.7 27.8 %collective-permute-start.19 = (bf16[128,2304]{1,0:T(8,128)(2,1)}, bf16[128,2304]{1,0:T(8,128)(2,1)}, u32[]{:S(2)}, u32[]{:S(2)}) collective-permute-start(bf16[128,2304]{1,0:T(8,128)(2,1)} %pad_maximum_fusion.14), channel_id=1, source_target_pairs={{0,8},{4,12},{8,0},{12,4},{16,24},{20,28},{24,16},{28,20},{1,9},{5... | collective-permute-start | bytes 1769480 | tf_op jit(solution)/shard_map/ppermute | solution.py:368
  69.5 42.7 %collective-permute-start.20 = (bf16[128,2304]{1,0:T(8,128)(2,1)}, bf16[128,2304]{1,0:T(8,128)(2,1)}, u32[]{:S(2)}, u32[]{:S(2)}) collective-permute-start(bf16[128,2304]{1,0:T(8,128)(2,1)} %pad_maximum_fusion.14), channel_id=1, source_target_pairs={{0,16},{4,20},{8,24},{12,28},{16,0},{20,4},{24,8},{28,12},{1,17},{... | collective-permute-start | bytes 1769480 | tf_op jit(solution)/shard_map/ppermute | solution.py:368
  70.4 41.8 %collective-permute-start.21 = (bf16[128,2304]{1,0:T(8,128)(2,1)}, bf16[128,2304]{1,0:T(8,128)(2,1)}, u32[]{:S(2)}, u32[]{:S(2)}) collective-permute-start(bf16[128,2304]{1,0:T(8,128)(2,1)} %pad_maximum_fusion.14), channel_id=1, source_target_pairs={{0,24},{4,28},{8,16},{12,20},{16,8},{20,12},{24,0},{28,4},{1,25},{... | collective-permute-start | bytes 1769480 | tf_op jit(solution)/shard_map/ppermute | solution.py:368
  74.5 37.7 %collective-permute-start.17 = (bf16[512,768]{1,0:T(8,128)(2,1)}, bf16[512,768]{1,0:T(8,128)(2,1)}, u32[]{:S(2)}, u32[]{:S(2)}) collective-permute-start(bf16[512,768]{1,0:T(8,128)(2,1)} %pad_maximum_fusion.13), channel_id=1, source_target_pairs={{0,4},{4,0},{8,12},{12,8},{16,20},{20,16},{24,28},{28,24},{1,5},{5... | collective-permute-start | bytes 2359304 | tf_op jit(solution)/shard_map/ppermute | solution.py:374
  113.7 32.4 %collective-permute-start.22 = (bf16[1024,768]{1,0:T(8,128)(2,1)S(1)}, bf16[1024,768]{1,0:T(8,128)(2,1)S(1)}, u32[]{:S(2)}, u32[]{:S(2)}) collective-permute-start(bf16[1024,768]{1,0:T(8,128)(2,1)S(1)} %pad_maximum_fusion.4.refs_4_), channel_id=1, source_target_pairs={{0,1},{1,0},{2,3},{3,2},{4,5},{5,4},{6,7},{7,6},{8,9},{9,8},{10,11... | collective-permute-start | bytes 4718600 | tf_op jit(solution)/shard_map/ppermute | solution.py:378
  115.1 31.0 %collective-permute-start.23 = (bf16[1024,384]{1,0:T(8,128)(2,1)S(1)}, bf16[1024,384]{1,0:T(8,128)(2,1)S(1)}, u32[]{:S(2)}, u32[]{:S(2)}) collective-permute-start(bf16[1024,384]{1,0:T(8,128)(2,1)S(1)} %constant_dynamic-update-slice_fusion), channel_id=1, source_target_pairs={{0,2},{1,3},{2,0},{3,1},{4,6},{5,7},{6,4},{7,5},{8,10},{9,11},{10,... | collective-permute-start | bytes 2359304 | tf_op jit(solution)/shard_map/ppermute | solution.py:378
  120.8 25.2 %collective-permute-start.25 = (bf16[512,512]{1,0:T(8,128)(2,1)S(1)}, bf16[512,512]{1,0:T(8,128)(2,1)S(1)}, u32[]{:S(2)}, u32[]{:S(2)}) collective-permute-start(bf16[512,512]{1,0:T(8,128)(2,1)S(1)} %get-tuple-element.503), channel_id=1, source_target_pairs={{0,2},{1,3},{2,0},{3,1},{4,6},{5,7},{6,4},{7,5},{8,10},{9,11},{10,... | collective-permute-start | bytes 1572872 | tf_op jit(solution)/shard_map/ppermute | solution.py:378
  121.4 24.7 %collective-permute-start.26 = (bf16[512,512]{1,0:T(8,128)(2,1)S(1)}, bf16[512,512]{1,0:T(8,128)(2,1)S(1)}, u32[]{:S(2)}, u32[]{:S(2)}) collective-permute-start(bf16[512,512]{1,0:T(8,128)(2,1)S(1)} %get-tuple-element.502), channel_id=1, source_target_pairs={{0,4},{4,0},{8,12},{12,8},{16,20},{20,16},{24,28},{28,24},{1,5},{5... | collective-permute-start | bytes 1572872 | tf_op jit(solution)/shard_map/ppermute | solution.py:374
  147.5 21.1 %collective-permute-start.27 = (bf16[1024,768]{1,0:T(8,128)(2,1)}, bf16[1024,768]{1,0:T(8,128)(2,1)}, u32[]{:S(2)}, u32[]{:S(2)}) collective-permute-start(bf16[1024,768]{1,0:T(8,128)(2,1)} %pad_maximum_fusion.5.refs_5_), channel_id=1, source_target_pairs={{0,1},{1,0},{2,3},{3,2},{4,5},{5,4},{6,7},{7,6},{8,9},{9,8},{10,11... | collective-permute-start | bytes 4718600 | tf_op jit(solution)/shard_map/ppermute | solution.py:378
  150.5 18.1 %collective-permute-start.28 = (bf16[2,1024,128]{2,1,0:T(8,128)(2,1)S(1)}, bf16[2,1024,128]{2,1,0:T(8,128)(2,1)S(1)}, u32[]{:S(2)}, u32[]{:S(2)}) collective-permute-start(bf16[2,1024,128]{2,1,0:T(8,128)(2,1)S(1)} %pad_maximum_fusion.15), channel_id=1, source_target_pairs={{0,2},{1,3},{2,0},{3,1},{4,6},{5,7},{6,4},{7,5},{8,10},{9,11},{10,... | collective-permute-start | bytes 1572872 | tf_op jit(solution)/shard_map/ppermute | solution.py:378
  154.3 27.9 %collective-permute-start.29 = (bf16[512,1024]{1,0:T(8,128)(2,1)}, bf16[512,1024]{1,0:T(8,128)(2,1)}, u32[]{:S(2)}, u32[]{:S(2)}) collective-permute-start(bf16[512,1024]{1,0:T(8,128)(2,1)} %pad_maximum_fusion.7), channel_id=1, source_target_pairs={{0,4},{4,0},{8,12},{12,8},{16,20},{20,16},{24,28},{28,24},{1,5},{5... | collective-permute-start | bytes 3145736 | tf_op jit(solution)/shard_map/ppermute | solution.py:374
  156.9 30.0 %collective-permute-start.30 = (bf16[1024,512]{1,0:T(8,128)(2,1)}, bf16[1024,512]{1,0:T(8,128)(2,1)}, u32[]{:S(2)}, u32[]{:S(2)}) collective-permute-start(bf16[1024,512]{1,0:T(8,128)(2,1)} %pad_maximum_fusion.8), channel_id=1, source_target_pairs={{0,2},{1,3},{2,0},{3,1},{4,6},{5,7},{6,4},{7,5},{8,10},{9,11},{10,... | collective-permute-start | bytes 3145736 | tf_op jit(solution)/shard_map/ppermute | solution.py:378
  169.8 17.1 %collective-permute-start.31 = (bf16[2,1024,256]{2,1,0:T(8,128)(2,1)}, bf16[2,1024,256]{2,1,0:T(8,128)(2,1)}, u32[]{:S(2)}, u32[]{:S(2)}) collective-permute-start(bf16[2,1024,256]{2,1,0:T(8,128)(2,1)} %pad_maximum_fusion.9), channel_id=1, source_target_pairs={{0,1},{1,0},{2,3},{3,2},{4,5},{5,4},{6,7},{7,6},{8,9},{9,8},{10,11... | collective-permute-start | bytes 3145736 | tf_op jit(solution)/shard_map/ppermute | solution.py:378
  189.9 24.7 %collective-permute-start.32 = (bf16[1024,1024]{1,0:T(8,128)(2,1)}, bf16[1024,1024]{1,0:T(8,128)(2,1)}, u32[]{:S(2)}, u32[]{:S(2)}) collective-permute-start(bf16[1024,1024]{1,0:T(8,128)(2,1)} %pad_maximum_fusion.refs_6_), channel_id=1, source_target_pairs={{0,1},{1,0},{2,3},{3,2},{4,5},{5,4},{6,7},{7,6},{8,9},{9,8},{10,11... | collective-permute-start | bytes 6291464 | tf_op jit(solution)/shard_map/ppermute | solution.py:378
  192.7 21.9 %collective-permute-start.33 = (bf16[1024,1024]{1,0:T(8,128)(2,1)}, bf16[1024,1024]{1,0:T(8,128)(2,1)}, u32[]{:S(2)}, u32[]{:S(2)}) collective-permute-start(bf16[1024,1024]{1,0:T(8,128)(2,1)} %pad_maximum_fusion.1.refs_7_), channel_id=1, source_target_pairs={{0,1},{1,0},{2,3},{3,2},{4,5},{5,4},{6,7},{7,6},{8,9},{9,8},{10,11... | collective-permute-start | bytes 6291464 | tf_op jit(solution)/shard_map/ppermute | solution.py:378
  194.8 17.9 %collective-permute-start.34 = (bf16[512,512]{1,0:T(8,128)(2,1)S(1)}, bf16[512,512]{1,0:T(8,128)(2,1)S(1)}, u32[]{:S(2)}, u32[]{:S(2)}) collective-permute-start(bf16[512,512]{1,0:T(8,128)(2,1)S(1)} %get-tuple-element.530), channel_id=1, source_target_pairs={{0,2},{1,3},{2,0},{3,1},{4,6},{5,7},{6,4},{7,5},{8,10},{9,11},{10,... | collective-permute-start | bytes 1572872 | tf_op jit(solution)/shard_map/ppermute | solution.py:378
  196.4 16.8 %collective-permute-start.35 = (bf16[512,512]{1,0:T(8,128)(2,1)S(1)}, bf16[512,512]{1,0:T(8,128)(2,1)S(1)}, u32[]{:S(2)}, u32[]{:S(2)}) collective-permute-start(bf16[512,512]{1,0:T(8,128)(2,1)S(1)} %get-tuple-element.529), channel_id=1, source_target_pairs={{0,4},{4,0},{8,12},{12,8},{16,20},{20,16},{24,28},{28,24},{1,5},{5... | collective-permute-start | bytes 1572872 | tf_op jit(solution)/shard_map/ppermute | solution.py:374
  199.3 57.8 %collective-permute-start.38 = (bf16[256,1024]{1,0:T(8,128)(2,1)}, bf16[256,1024]{1,0:T(8,128)(2,1)S(1)}, u32[]{:S(2)}, u32[]{:S(2)}) collective-permute-start(bf16[256,1024]{1,0:T(8,128)(2,1)} %get-tuple-element.515), channel_id=1, source_target_pairs={{0,1},{1,0},{2,3},{3,2},{4,5},{5,4},{6,7},{7,6},{8,9},{9,8},{10,11... | collective-permute-start | bytes 1572872 | tf_op jit(solution)/shard_map/ppermute | solution.py:378
  212.7 44.4 %collective-permute-start.39 = (bf16[256,1024]{1,0:T(8,128)(2,1)}, bf16[256,1024]{1,0:T(8,128)(2,1)S(1)}, u32[]{:S(2)}, u32[]{:S(2)}) collective-permute-start(bf16[256,1024]{1,0:T(8,128)(2,1)} %get-tuple-element.514), channel_id=1, source_target_pairs={{0,2},{1,3},{2,0},{3,1},{4,6},{5,7},{6,4},{7,5},{8,10},{9,11},{10,... | collective-permute-start | bytes 1572872 | tf_op jit(solution)/shard_map/ppermute | solution.py:378
  213.2 43.8 %collective-permute-start.40 = (bf16[256,1024]{1,0:T(8,128)(2,1)S(1)}, bf16[256,1024]{1,0:T(8,128)(2,1)S(1)}, u32[]{:S(2)}, u32[]{:S(2)}) collective-permute-start(bf16[256,1024]{1,0:T(8,128)(2,1)S(1)} %get-tuple-element.513), channel_id=1, source_target_pairs={{0,3},{1,2},{2,1},{3,0},{4,7},{5,6},{6,5},{7,4},{8,11},{9,10},{10,... | collective-permute-start | bytes 1572872 | tf_op jit(solution)/shard_map/ppermute | solution.py:378
  240.8 25.4 %collective-permute-start.36 = (bf16[512,1024]{1,0:T(8,128)(2,1)S(1)}, bf16[512,1024]{1,0:T(8,128)(2,1)S(1)}, u32[]{:S(2)}, u32[]{:S(2)}) collective-permute-start(bf16[512,1024]{1,0:T(8,128)(2,1)S(1)} %pad_maximum_fusion.10), channel_id=1, source_target_pairs={{0,4},{4,0},{8,12},{12,8},{16,20},{20,16},{24,28},{28,24},{1,5},{5... | collective-permute-start | bytes 3145736 | tf_op jit(solution)/shard_map/ppermute | solution.py:374
  242.5 25.1 %collective-permute-start.37 = (bf16[1024,512]{1,0:T(8,128)(2,1)S(1)}, bf16[1024,512]{1,0:T(8,128)(2,1)S(1)}, u32[]{:S(2)}, u32[]{:S(2)}) collective-permute-start(bf16[1024,512]{1,0:T(8,128)(2,1)S(1)} %pad_maximum_fusion.11), channel_id=1, source_target_pairs={{0,2},{1,3},{2,0},{3,1},{4,6},{5,7},{6,4},{7,5},{8,10},{9,11},{10,... | collective-permute-start | bytes 3145736 | tf_op jit(solution)/shard_map/ppermute | solution.py:378
  273.1 18.6 %collective-permute-start.41 = (bf16[1024,1024]{1,0:T(8,128)(2,1)}, bf16[1024,1024]{1,0:T(8,128)(2,1)}, u32[]{:S(2)}, u32[]{:S(2)}) collective-permute-start(bf16[1024,1024]{1,0:T(8,128)(2,1)} %convolution_convert_fusion.3), channel_id=1, source_target_pairs={{0,1},{1,0},{2,3},{3,2},{4,5},{5,4},{6,7},{7,6},{8,9},{9,8},{10,11... | collective-permute-start | bytes 6291464 | tf_op jit(solution)/shard_map/ppermute | solution.py:378
  321.3 25.2 %collective-permute-start.45 = (bf16[512,1024]{1,0:T(8,128)(2,1)S(1)}, bf16[512,1024]{1,0:T(8,128)(2,1)S(1)}, u32[]{:S(2)}, u32[]{:S(2)}) collective-permute-start(bf16[512,1024]{1,0:T(8,128)(2,1)S(1)} %slice.440), channel_id=1, source_target_pairs={{0,4},{4,0},{8,12},{12,8},{16,20},{20,16},{24,28},{28,24},{1,5},{5... | collective-permute-start | bytes 3145736 | tf_op jit(solution)/shard_map/ppermute | solution.py:374
  324.7 26.1 %collective-permute-start.46 = (bf16[1024,512]{1,0:T(8,128)(2,1)S(1)}, bf16[1024,512]{1,0:T(8,128)(2,1)S(1)}, u32[]{:S(2)}, u32[]{:S(2)}) collective-permute-start(bf16[1024,512]{1,0:T(8,128)(2,1)S(1)} %slice.441), channel_id=1, source_target_pairs={{0,2},{1,3},{2,0},{3,1},{4,6},{5,7},{6,4},{7,5},{8,10},{9,11},{10,... | collective-permute-start | bytes 3145736 | tf_op jit(solution)/shard_map/ppermute | solution.py:378
  325.3 63.7 %collective-permute-start.51 = (bf16[256,1024]{1,0:T(8,128)(2,1)}, bf16[256,1024]{1,0:T(8,128)(2,1)S(1)}, u32[]{:S(2)}, u32[]{:S(2)}) collective-permute-start(bf16[256,1024]{1,0:T(8,128)(2,1)} %get-tuple-element.511), channel_id=1, source_target_pairs={{0,1},{1,0},{2,3},{3,2},{4,5},{5,4},{6,7},{7,6},{8,9},{9,8},{10,11... | collective-permute-start | bytes 1572872 | tf_op jit(solution)/shard_map/ppermute | solution.py:378
  325.3 64.2 %collective-permute-start.52 = (bf16[256,1024]{1,0:T(8,128)(2,1)}, bf16[256,1024]{1,0:T(8,128)(2,1)}, u32[]{:S(2)}, u32[]{:S(2)}) collective-permute-start(bf16[256,1024]{1,0:T(8,128)(2,1)} %get-tuple-element.510), channel_id=1, source_target_pairs={{0,2},{1,3},{2,0},{3,1},{4,6},{5,7},{6,4},{7,5},{8,10},{9,11},{10,... | collective-permute-start | bytes 1572872 | tf_op jit(solution)/shard_map/ppermute | solution.py:378
  326.8 66.7 %collective-permute-start.53 = (bf16[256,1024]{1,0:T(8,128)(2,1)}, bf16[256,1024]{1,0:T(8,128)(2,1)}, u32[]{:S(2)}, u32[]{:S(2)}) collective-permute-start(bf16[256,1024]{1,0:T(8,128)(2,1)} %get-tuple-element.509), channel_id=1, source_target_pairs={{0,3},{1,2},{2,1},{3,0},{4,7},{5,6},{6,5},{7,4},{8,11},{9,10},{10,... | collective-permute-start | bytes 1572872 | tf_op jit(solution)/shard_map/ppermute | solution.py:378
  359.3 43.8 %collective-permute-start.47 = (bf16[1024,1024]{1,0:T(8,128)(2,1)}, bf16[1024,1024]{1,0:T(8,128)(2,1)}, u32[]{:S(2)}, u32[]{:S(2)}) collective-permute-start(bf16[1024,1024]{1,0:T(8,128)(2,1)} %convolution_convert_fusion.1), channel_id=1, source_target_pairs={{0,1},{1,0},{2,3},{3,2},{4,5},{5,4},{6,7},{7,6},{8,9},{9,8},{10,11... | collective-permute-start | bytes 6291464 | tf_op jit(solution)/shard_map/ppermute | solution.py:378
  359.3 43.8 %collective-permute-start.48 = (bf16[1024,1024]{1,0:T(8,128)(2,1)}, bf16[1024,1024]{1,0:T(8,128)(2,1)}, u32[]{:S(2)}, u32[]{:S(2)}) collective-permute-start(bf16[1024,1024]{1,0:T(8,128)(2,1)} %convolution_convert_fusion), channel_id=1, source_target_pairs={{0,1},{1,0},{2,3},{3,2},{4,5},{5,4},{6,7},{7,6},{8,9},{9,8},{10,11... | collective-permute-start | bytes 6291464 | tf_op jit(solution)/shard_map/ppermute | solution.py:378
  416.3 52.8 %collective-permute-start.54 = (bf16[512,1024]{1,0:T(8,128)(2,1)S(1)}, bf16[512,1024]{1,0:T(8,128)(2,1)S(1)}, u32[]{:S(2)}, u32[]{:S(2)}) collective-permute-start(bf16[512,1024]{1,0:T(8,128)(2,1)S(1)} %slice.446), channel_id=1, source_target_pairs={{0,4},{4,0},{8,12},{12,8},{16,20},{20,16},{24,28},{28,24},{1,5},{5... | collective-permute-start | bytes 3145736 | tf_op jit(solution)/shard_map/ppermute | solution.py:374
  420.6 48.5 %collective-permute-start.55 = (bf16[1024,512]{1,0:T(8,128)(2,1)S(1)}, bf16[1024,512]{1,0:T(8,128)(2,1)S(1)}, u32[]{:S(2)}, u32[]{:S(2)}) collective-permute-start(bf16[1024,512]{1,0:T(8,128)(2,1)S(1)} %slice.447), channel_id=1, source_target_pairs={{0,2},{1,3},{2,0},{3,1},{4,6},{5,7},{6,4},{7,5},{8,10},{9,11},{10,... | collective-permute-start | bytes 3145736 | tf_op jit(solution)/shard_map/ppermute | solution.py:378
  422.3 46.8 %collective-permute-start.56 = (bf16[2,1024,256]{2,1,0:T(8,128)(2,1)S(1)}, bf16[2,1024,256]{2,1,0:T(8,128)(2,1)S(1)}, u32[]{:S(2)}, u32[]{:S(2)}) collective-permute-start(bf16[2,1024,256]{2,1,0:T(8,128)(2,1)S(1)} %pad_maximum_fusion.12), channel_id=1, source_target_pairs={{0,1},{1,0},{2,3},{3,2},{4,5},{5,4},{6,7},{7,6},{8,9},{9,8},{10,11... | collective-permute-start | bytes 3145736 | tf_op jit(solution)/shard_map/ppermute | solution.py:378
  422.8 36.0 %collective-permute-start.57 = (bf16[128,1024]{1,0:T(8,128)(2,1)S(1)}, bf16[128,1024]{1,0:T(8,128)(2,1)S(1)}, u32[]{:S(2)}, u32[]{:S(2)}) collective-permute-start(bf16[128,1024]{1,0:T(8,128)(2,1)S(1)} %get-tuple-element.523), channel_id=1, source_target_pairs={{0,8},{4,12},{8,0},{12,4},{16,24},{20,28},{24,16},{28,20},{1,9},{5... | collective-permute-start | bytes 786440 | tf_op jit(solution)/shard_map/ppermute | solution.py:368
  434.4 27.6 %collective-permute-start.58 = (bf16[128,1024]{1,0:T(8,128)(2,1)S(1)}, bf16[128,1024]{1,0:T(8,128)(2,1)S(1)}, u32[]{:S(2)}, u32[]{:S(2)}) collective-permute-start(bf16[128,1024]{1,0:T(8,128)(2,1)S(1)} %get-tuple-element.524), channel_id=1, source_target_pairs={{0,16},{4,20},{8,24},{12,28},{16,0},{20,4},{24,8},{28,12},{1,17},{... | collective-permute-start | bytes 786440 | tf_op jit(solution)/shard_map/ppermute | solution.py:368
  469.0 29.6 %collective-permute-start.60 = (bf16[1024,768]{1,0:T(8,128)(2,1)}, bf16[1024,768]{1,0:T(8,128)(2,1)}, u32[]{:S(2)}, u32[]{:S(2)}) collective-permute-start(bf16[1024,768]{1,0:T(8,128)(2,1)} %convolution_convert_fusion.7), channel_id=1, source_target_pairs={{0,1},{1,0},{2,3},{3,2},{4,5},{5,4},{6,7},{7,6},{8,9},{9,8},{10,11... | collective-permute-start | bytes 4718600 | tf_op jit(solution)/shard_map/ppermute | solution.py:378
  470.6 28.0 %collective-permute-start.61 = (bf16[2,1024,128]{2,1,0:T(8,128)(2,1)}, bf16[2,1024,128]{2,1,0:T(8,128)(2,1)}, u32[]{:S(2)}, u32[]{:S(2)}) collective-permute-start(bf16[2,1024,128]{2,1,0:T(8,128)(2,1)} %slice.456), channel_id=1, source_target_pairs={{0,2},{1,3},{2,0},{3,1},{4,6},{5,7},{6,4},{7,5},{8,10},{9,11},{10,... | collective-permute-start | bytes 1572872 | tf_op jit(solution)/shard_map/ppermute | solution.py:378
  473.1 25.5 %collective-permute-start.62 = (bf16[512,512]{1,0:T(8,128)(2,1)}, bf16[512,512]{1,0:T(8,128)(2,1)}, u32[]{:S(2)}, u32[]{:S(2)}) collective-permute-start(bf16[512,512]{1,0:T(8,128)(2,1)} %slice.458), channel_id=1, source_target_pairs={{0,2},{1,3},{2,0},{3,1},{4,6},{5,7},{6,4},{7,5},{8,10},{9,11},{10,... | collective-permute-start | bytes 1572872 | tf_op jit(solution)/shard_map/ppermute | solution.py:378
  475.5 23.1 %collective-permute-start.63 = (bf16[512,512]{1,0:T(8,128)(2,1)}, bf16[512,512]{1,0:T(8,128)(2,1)}, u32[]{:S(2)}, u32[]{:S(2)}) collective-permute-start(bf16[512,512]{1,0:T(8,128)(2,1)} %slice.460), channel_id=1, source_target_pairs={{0,4},{4,0},{8,12},{12,8},{16,20},{20,16},{24,28},{28,24},{1,5},{5... | collective-permute-start | bytes 1572872 | tf_op jit(solution)/shard_map/ppermute | solution.py:374
  521.3 32.9 %collective-permute-start.65 = (bf16[512,768]{1,0:T(8,128)(2,1)S(1)}, bf16[512,768]{1,0:T(8,128)(2,1)S(1)}, u32[]{:S(2)}, u32[]{:S(2)}) collective-permute-start(bf16[512,768]{1,0:T(8,128)(2,1)S(1)} %slice.463), channel_id=1, source_target_pairs={{0,4},{4,0},{8,12},{12,8},{16,20},{20,16},{24,28},{28,24},{1,5},{5... | collective-permute-start | bytes 2359304 | tf_op jit(solution)/shard_map/ppermute | solution.py:374
  527.1 27.1 %collective-permute-start.66 = (bf16[1024,768]{1,0:T(8,128)(2,1)S(1)}, bf16[1024,768]{1,0:T(8,128)(2,1)S(1)}, u32[]{:S(2)}, u32[]{:S(2)}) collective-permute-start(bf16[1024,768]{1,0:T(8,128)(2,1)S(1)} %convolution_convert_fusion.6), channel_id=1, source_target_pairs={{0,1},{1,0},{2,3},{3,2},{4,5},{5,4},{6,7},{7,6},{8,9},{9,8},{10,11... | collective-permute-start | bytes 4718600 | tf_op jit(solution)/shard_map/ppermute | solution.py:378
  528.3 47.5 %collective-permute-start.72 = (bf16[128,1280]{1,0:T(8,128)(2,1)}, bf16[128,1280]{1,0:T(8,128)(2,1)}, u32[]{:S(2)}, u32[]{:S(2)}) collective-permute-start(bf16[128,1280]{1,0:T(8,128)(2,1)} %get-tuple-element.521), channel_id=1, source_target_pairs={{0,8},{4,12},{8,0},{12,4},{16,24},{20,28},{24,16},{28,20},{1,9},{5... | collective-permute-start | bytes 983048 | tf_op jit(solution)/shard_map/ppermute | solution.py:368
  533.5 42.4 %collective-permute-start.73 = (bf16[128,1280]{1,0:T(8,128)(2,1)}, bf16[128,1280]{1,0:T(8,128)(2,1)}, u32[]{:S(2)}, u32[]{:S(2)}) collective-permute-start(bf16[128,1280]{1,0:T(8,128)(2,1)} %get-tuple-element.520), channel_id=1, source_target_pairs={{0,16},{4,20},{8,24},{12,28},{16,0},{20,4},{24,8},{28,12},{1,17},{... | collective-permute-start | bytes 983048 | tf_op jit(solution)/shard_map/ppermute | solution.py:368
  534.7 42.5 %collective-permute-start.74 = (bf16[128,1280]{1,0:T(8,128)(2,1)}, bf16[128,1280]{1,0:T(8,128)(2,1)}, u32[]{:S(2)}, u32[]{:S(2)}) collective-permute-start(bf16[128,1280]{1,0:T(8,128)(2,1)} %get-tuple-element.519), channel_id=1, source_target_pairs={{0,24},{4,28},{8,16},{12,20},{16,8},{20,12},{24,0},{28,4},{1,25},{... | collective-permute-start | bytes 983048 | tf_op jit(solution)/shard_map/ppermute | solution.py:368
  570.4 30.6 %collective-permute-start.67 = (bf16[512,384]{1,0:T(8,128)(2,1)}, bf16[512,384]{1,0:T(8,128)(2,1)}, u32[]{:S(2)}, u32[]{:S(2)}) collective-permute-start(bf16[512,384]{1,0:T(8,128)(2,1)} %slice.466), channel_id=1, source_target_pairs={{0,2},{1,3},{2,0},{3,1},{4,6},{5,7},{6,4},{7,5},{8,10},{9,11},{10,... | collective-permute-start | bytes 1179656 | tf_op jit(solution)/shard_map/ppermute | solution.py:378
  573.1 27.8 %collective-permute-start.68 = (bf16[1024,384]{1,0:T(8,128)(2,1)}, bf16[1024,384]{1,0:T(8,128)(2,1)}, u32[]{:S(2)}, u32[]{:S(2)}) collective-permute-start(bf16[1024,384]{1,0:T(8,128)(2,1)} %slice.467), channel_id=1, source_target_pairs={{0,2},{1,3},{2,0},{3,1},{4,6},{5,7},{6,4},{7,5},{8,10},{9,11},{10,... | collective-permute-start | bytes 2359304 | tf_op jit(solution)/shard_map/ppermute | solution.py:378
  575.9 23.8 %collective-permute-start.70 = (f32[8,1216]{1,0:T(8,128)S(1)}, f32[8,1216]{1,0:T(8,128)S(1)}, u32[]{:S(2)}, u32[]{:S(2)}) collective-permute-start(f32[8,1216]{1,0:T(8,128)S(1)} %get-tuple-element.539), channel_id=1, source_target_pairs={{0,2},{1,3},{2,0},{3,1},{4,6},{5,7},{6,4},{7,5},{8,10},{9,11},{10,... | collective-permute-start | bytes 116744 | tf_op jit(solution)/shard_map/ppermute | solution.py:378
  577.2 23.8 %collective-permute-start.71 = (f32[8,1216]{1,0:T(8,128)S(1)}, f32[8,1216]{1,0:T(8,128)S(1)}, u32[]{:S(2)}, u32[]{:S(2)}) collective-permute-start(f32[8,1216]{1,0:T(8,128)S(1)} %get-tuple-element.538), channel_id=1, source_target_pairs={{0,3},{1,2},{2,1},{3,0},{4,7},{5,6},{6,5},{7,4},{8,11},{9,10},{10,... | collective-permute-start | bytes 116744 | tf_op jit(solution)/shard_map/ppermute | solution.py:378
  579.1 41.8 %collective-permute-start.83 = (bf16[256,1024]{1,0:T(8,128)(2,1)}, bf16[256,1024]{1,0:T(8,128)(2,1)S(1)}, u32[]{:S(2)}, u32[]{:S(2)}) collective-permute-start(bf16[256,1024]{1,0:T(8,128)(2,1)} %get-tuple-element.508), channel_id=1, source_target_pairs={{0,1},{1,0},{2,3},{3,2},{4,5},{5,4},{6,7},{7,6},{8,9},{9,8},{10,11... | collective-permute-start | bytes 1572872 | tf_op jit(solution)/shard_map/ppermute | solution.py:378
  599.8 22.9 %collective-permute-start.84 = (bf16[256,1024]{1,0:T(8,128)(2,1)}, bf16[256,1024]{1,0:T(8,128)(2,1)S(1)}, u32[]{:S(2)}, u32[]{:S(2)}) collective-permute-start(bf16[256,1024]{1,0:T(8,128)(2,1)} %get-tuple-element.507), channel_id=1, source_target_pairs={{0,2},{1,3},{2,0},{3,1},{4,6},{5,7},{6,4},{7,5},{8,10},{9,11},{10,... | collective-permute-start | bytes 1572872 | tf_op jit(solution)/shard_map/ppermute | solution.py:378
  601.0 22.9 %collective-permute-start.85 = (bf16[256,1024]{1,0:T(8,128)(2,1)}, bf16[256,1024]{1,0:T(8,128)(2,1)S(1)}, u32[]{:S(2)}, u32[]{:S(2)}) collective-permute-start(bf16[256,1024]{1,0:T(8,128)(2,1)} %get-tuple-element.506), channel_id=1, source_target_pairs={{0,3},{1,2},{2,1},{3,0},{4,7},{5,6},{6,5},{7,4},{8,11},{9,10},{10,... | collective-permute-start | bytes 1572872 | tf_op jit(solution)/shard_map/ppermute | solution.py:378
  619.5 22.2 %collective-permute-start.77 = (bf16[128,768]{1,0:T(8,128)(2,1)}, bf16[128,768]{1,0:T(8,128)(2,1)}, u32[]{:S(2)}, u32[]{:S(2)}) collective-permute-start(bf16[128,768]{1,0:T(8,128)(2,1)} %get-tuple-element.532), channel_id=1, source_target_pairs={{0,8},{4,12},{8,0},{12,4},{16,24},{20,28},{24,16},{28,20},{1,9},{5... | collective-permute-start | bytes 589832 | tf_op jit(solution)/shard_map/ppermute | solution.py:368
  620.9 20.7 %collective-permute-start.78 = (bf16[128,768]{1,0:T(8,128)(2,1)}, bf16[128,768]{1,0:T(8,128)(2,1)}, u32[]{:S(2)}, u32[]{:S(2)}) collective-permute-start(bf16[128,768]{1,0:T(8,128)(2,1)} %get-tuple-element.533), channel_id=1, source_target_pairs={{0,16},{4,20},{8,24},{12,28},{16,0},{20,4},{24,8},{28,12},{1,17},{... | collective-permute-start | bytes 589832 | tf_op jit(solution)/shard_map/ppermute | solution.py:368
  622.6 19.0 %collective-permute-start.79 = (bf16[128,768]{1,0:T(8,128)(2,1)}, bf16[128,768]{1,0:T(8,128)(2,1)}, u32[]{:S(2)}, u32[]{:S(2)}) collective-permute-start(bf16[128,768]{1,0:T(8,128)(2,1)} %get-tuple-element.531), channel_id=1, source_target_pairs={{0,24},{4,28},{8,16},{12,20},{16,8},{20,12},{24,0},{28,4},{1,25},{... | collective-permute-start | bytes 589832 | tf_op jit(solution)/shard_map/ppermute | solution.py:368
  623.9 17.8 %collective-permute-start.81 = (f32[1216]{0:T(1024)S(1)}, f32[1216]{0:T(1024)S(1)}, u32[]{:S(2)}, u32[]{:S(2)}) collective-permute-start(f32[1216]{0:T(1024)S(1)} %get-tuple-element.474), channel_id=1, source_target_pairs={{0,16},{4,20},{8,24},{12,28},{16,0},{20,4},{24,8},{28,12},{1,17},{... | collective-permute-start | bytes 14600 | tf_op jit(solution)/shard_map/ppermute | solution.py:368
  625.3 16.3 %collective-permute-start.82 = (f32[1216]{0:T(1024)S(1)}, f32[1216]{0:T(1024)S(1)}, u32[]{:S(2)}, u32[]{:S(2)}) collective-permute-start(f32[1216]{0:T(1024)S(1)} %get-tuple-element.473), channel_id=1, source_target_pairs={{0,24},{4,28},{8,16},{12,20},{16,8},{20,12},{24,0},{28,4},{1,25},{... | collective-permute-start | bytes 14600 | tf_op jit(solution)/shard_map/ppermute | solution.py:368
  (154 other events, 1730.1 us)

commit v5 on v4

--- a/solution.py
+++ b/solution.py
@@ -452,18 +452,21 @@
     return total
 
 
-def mp_steps(chain, parts):
-    arrived = yield [swap_mp(part, step + 1) for step, part in enumerate(parts)]
+def mp_steps(chain, parts, first=1):
+    arrived = yield [swap_mp(part, step + first) for step, part in enumerate(parts)]
     return arrived
 
 
 def small_steps(chain, shard, vector_size):
-    arrived = yield [swap_z(shard, step) for step in range(1, ZS)]
-    rows = jnp.concatenate([shard] + arrived, 0)
+    biases = shard[:, vector_size:]
+    arrived = yield [swap_mp(biases, step) for step in range(1, MP)]
+    rows = jnp.concatenate([shard] + arrived, 1)
+    arrived = yield [swap_z(rows, step) for step in range(1, ZS)]
+    rows = jnp.concatenate([rows] + arrived, 0)
     arrived = yield [swap_y(rows)]
     rows = jnp.concatenate([rows] + arrived, 0)
-    arrived = yield [swap_mp(rows[:, vector_size:], step) for step in range(1, MP)]
-    return (rows[:, :vector_size], jnp.stack([rows[:, vector_size:]] + arrived, 0))
+    biases = rows[:, vector_size:].reshape(DP, MP, -1).transpose(1, 0, 2)
+    return (rows[:, :vector_size], biases)
 
 
 def small_reduce_steps(chain, vector_part, bias_part):
@@ -573,7 +576,7 @@
     )(place, own, *parts)
 
 
-ROWS = 256
+ROWS = 512
 
 
 def product_nt(left_refs, right_refs):
@@ -631,29 +634,60 @@
 
 def in_back_kernel(count, *refs):
     lefts, rights = (refs[:count], refs[count : 2 * count])
-    vector_ref, base_ref, grad_ref, own_ref, low_ref, sums_ref = refs[2 * count :]
+    vector_ref, base_ref, grad_ref, low_ref, sums_ref = refs[2 * count : 2 * count + 5]
     grad_normed = product_nt(lefts, rights)
     normal, spread = norm_parts(base_ref[...].astype(F32))
     grad = norm_back(grad_normed, normal, spread, vector_row(vector_ref, GAIN_ONE))
     grad = grad + grad_ref[...]
     low_ref[...] = grad.astype(BF)
 
-    @pl.when(pl.program_id(0) == 0)
-    def _():
-        own_ref[...] = grad
-
+    for own_ref in refs[2 * count + 5 :]:
+        own_ref[...] = grad[: own_ref.shape[0]]
     add_rows(sums_ref, [grad_normed * normal, grad_normed])
 
 
-def row_call(kernel, name, lefts, rights, vector_full, row_inputs, outs):
+def expand_kernel(left_ref, right_ref, bias_ref, activ_ref, slope_ref):
+    values = jnp.dot(left_ref[...], right_ref[...], preferred_element_type=F32) + bias_ref[0:1, :]
+    share = 0.5 * (1.0 + lax.erf(values * 0.7071067811865476))
+    activ_ref[...] = (values * share).astype(BF)
+    slope = share + values * (0.3989422804014327 * jnp.exp(-0.5 * values * values))
+    slope_ref[...] = slope.astype(BF)
+
+
+def expand(left, right, bias):
+    rows, depth = left.shape
+    width = right.shape[1]
+    block = pl.BlockSpec((256, width), lambda i: (i, 0))
+    return pl.pallas_call(
+        expand_kernel,
+        grid=(rows // 256,),
+        in_specs=[
+            pl.BlockSpec((256, depth), lambda i: (i, 0)),
+            pl.BlockSpec((depth, width), lambda i: (0, 0), pipeline_mode=pl.Buffered(1)),
+            pl.BlockSpec((1, width), lambda i: (0, 0)),
+        ],
+        out_specs=[block] * 2,
+        out_shape=[jax.ShapeDtypeStruct((rows, width), BF)] * 2,
+        compiler_params=pltpu.CompilerParams(vmem_limit_bytes=32 * 2**20),
+        cost_estimate=pl.CostEstimate(
+            flops=2 * rows * width * depth, bytes_accessed=rows * width * 8, transcendentals=rows * width
+        ),
+        name="expand",
+    )(left, right, bias.reshape(1, width))
+
+
+def row_call(kernel, name, lefts, rights, vector_full, row_inputs, outs, span=None, own_rows=0):
     rows, width = row_inputs[0].shape
+    first, count = span or (0, rows // ROWS)
+    rows = count * ROWS
     once = pl.Buffered(1)
     block = pl.BlockSpec((ROWS, width), lambda i: (i, 0))
+    source = pl.BlockSpec((ROWS, width), lambda i: (i + first, 0))
     specs = {
         "sums": (pl.BlockSpec((8, width), lambda i: (0, 0)), jax.ShapeDtypeStruct((8, width), F32)),
         "own": (
-            pl.BlockSpec((ROWS, width), lambda i: (0, 0)),
-            jax.ShapeDtypeStruct((ROWS, width), F32),
+            pl.BlockSpec((own_rows, width), lambda i: (0, 0)),
+            jax.ShapeDtypeStruct((own_rows, width), F32),
         ),
     }
     pairs = [
@@ -663,15 +697,17 @@
     depth = sum(each.shape[1] for each in lefts)
     return pl.pallas_call(
         functools.partial(kernel, len(lefts)),
-        grid=(rows // ROWS,),
-        in_specs=[pl.BlockSpec((ROWS, each.shape[1]), lambda i: (i, 0)) for each in lefts]
+        grid=(count,),
+        in_specs=[pl.BlockSpec((ROWS, each.shape[1]), lambda i: (i + first, 0)) for each in lefts]
         + [pl.BlockSpec(each.shape, lambda i: (0, 0), pipeline_mode=once) for each in rights]
         + [pl.BlockSpec(vector_full.shape, lambda i: (0, 0))]
-        + [block] * len(row_inputs),
+        + [source] * len(row_inputs),
         out_specs=[each[0] for each in pairs],
         out_shape=[each[1] for each in pairs],
         compiler_params=pltpu.CompilerParams(vmem_limit_bytes=48 * 2**20),
-        cost_estimate=pl.CostEstimate(
+        cost_estimate=None
+        if span
+        else pl.CostEstimate(
             flops=2 * rows * width * depth, bytes_accessed=rows * width * 24, transcendentals=0
         ),
         name=name,
@@ -814,12 +850,6 @@
     return lax.dot_general(left, right, (((0,), (0,)), ((), ())), preferred_element_type=F32)
 
 
-def gelu_pair(values):
-    share = 0.5 * (1.0 + lax.erf(values * 0.7071067811865476))
-    slope = share + values * (0.3989422804014327 * jnp.exp(-0.5 * values * values))
-    return ((values * share).astype(BF), slope.astype(BF))
-
-
 def local_image(
     tokens,
     cotangent,
@@ -890,9 +920,9 @@
     small = Chain(small_steps, small_shard, vector_size)
     fetch_tokens = fetch_image(tokens)
     rest_shard = meet(rest_shard, rows_qkv[0], small)
-    get_qkv = [Chain(gather_steps, [rows_qkv[0].result], ("xy",)), None]
+    get_qkv = [Chain(gather_steps, [rows_qkv[0].result], ("yx",)), None]
     rest_shard = meet(rest_shard, small, rows_qkv[1])
-    get_qkv[1] = Chain(gather_steps, [rows_qkv[1].result], ("yx",))
+    get_qkv[1] = Chain(gather_steps, [rows_qkv[1].result], ("xy",))
     rows_rest = Chain(rows_z_steps, rest_shard)
     tokens = meet(tokens, small, get_qkv[0], fetch_tokens)
 
@@ -905,12 +935,7 @@
     bias_full = bias_full.astype(F32)
 
     base, normed_one = assemble_image(place, vector_full, tokens[:, 0], fetch_tokens.result, True)
-    normed_one = meet(normed_one, *get_qkv, rows_rest)
-    out_rows, up_rows, down_rows = jnp.split(
-        rows_rest.result, [block_width, block_width * (1 + units)], 1
-    )
-    get_out = Chain(gather_steps, [jnp.stack(jnp.split(out_rows, 2, 1))], ("yx",))
-    get_up = Chain(gather_steps, jnp.split(up_rows, 2, 1), both)
+    normed_one = meet(normed_one, *get_qkv)
 
     def project(core, half, weight):
         lanes = slice(half * LANES, (half + 1) * LANES)
@@ -925,10 +950,17 @@
 
     heads[0][0] = project(0, 0, get_qkv[0].own[0])
     forward_heads(0, 0)
-    blended[0][0], normed_one = meet((blended[0][0], normed_one), *get_qkv, get_out, get_up)
+    blended[0][0], normed_one = meet((blended[0][0], normed_one), *get_qkv, rows_rest)
+    out_rows, up_rows, down_rows = jnp.split(
+        rows_rest.result, [block_width, block_width * (1 + units)], 1
+    )
+    get_out = Chain(gather_steps, [jnp.stack(jnp.split(out_rows, 2, 1))], ("yx",))
+    get_up = Chain(gather_steps, jnp.split(up_rows, 2, 1), both)
     heads[0][1] = project(0, 1, get_qkv[1].own[0])
     forward_heads(0, 1)
-    blended[0][1], normed_one, down_rows = meet((blended[0][1], normed_one, down_rows), get_qkv[1], get_out)
+    blended[0][1], normed_one, down_rows = meet(
+        (blended[0][1], normed_one, down_rows), get_qkv[1], get_out, get_up
+    )
     w_qkv = [[each.own[0] for each in get_qkv], [each.result[0] for each in get_qkv]]
     get_down = Chain(gather_steps, jnp.split(down_rows, 2, 1), both)
     heads[1][0] = project(1, 0, w_qkv[1][0])
@@ -939,7 +971,7 @@
     fetch_cotangent = fetch_image(cotangent)
     heads[1][1] = project(1, 1, w_qkv[1][1])
     forward_heads(1, 1)
-    blended = meet(blended, get_up, get_down)
+    blended = meet(blended, get_up, get_out, get_down)
     w_up = [get_up.own, get_up.result]
     w_out = [[each[0][half] for half in (0, 1)] for each in (get_out.own, get_out.result)]
     pairs = [(core, half) for core in cores for half in (0, 1)]
@@ -956,9 +988,11 @@
     activ, slope = ({}, {})
     for half, core in parts:
         rows = bias_full[core, 2 + half * half_units : 2 + (half + 1) * half_units]
-        pre_act = dot_nn(normed_two, w_up[core][half]) + rows.transpose(1, 0, 2).reshape(-1)
-        activ[half, core], slope[half, core] = gelu_pair(pre_act)
-    activ, slope, cotangent = meet((activ, slope, cotangent), get_down, fetch_cotangent)
+        unit_bias = rows.transpose(1, 0, 2).reshape(-1)
+        activ[half, core], slope[half, core] = expand(normed_two, w_up[core][half], unit_bias)
+        if (half, core) == (0, 0):
+            activ, normed_two = meet((activ, normed_two), get_down)
+    activ, slope, cotangent = meet((activ, slope, cotangent), fetch_cotangent)
     grad_out, grad_branch = assemble_image(
         place, vector_full, cotangent[:, 0], fetch_cotangent.result, False
     )
@@ -986,7 +1020,7 @@
     for half, core in parts:
         grad_activ = dot_nn(grad_branch, w_down[core][half])
         grad_pre[half, core] = (grad_activ * slope[half, core].astype(F32)).astype(BF)
-    grad_pre, normed_two = meet((grad_pre, normed_two), sum_down)
+    grad_pre, normed_two = meet((grad_pre, normed_two))
     sum_up = reduce_pairs(normed_two, grad_pre)
     grad_hidden, grad_projected, sums_one = row_call(
         up_back_kernel,
@@ -998,7 +1032,6 @@
         [F32, BF, "sums"],
     )
     grad_projected = meet(grad_projected, sum_up, sum_down, send_output)
-    rows_down = Chain(sum_z_steps, jnp.concatenate(sum_down.result, 1))
     grad_w_out = [
         jnp.stack([dot_tn(grad_projected, each).astype(BF) for each in blended[core]]) for core in cores
     ]
@@ -1014,26 +1047,37 @@
         return dot_tn(normed_one, grad_heads[core][half]).astype(BF)
 
     other = back_heads(1, 0)
-    other, grad_blended = meet((other, grad_blended), sum_up, sum_out, rows_down)
-    sum_qkv = [Chain(reduce_steps, [other], ("yx",)), None]
+    other, grad_blended = meet((other, grad_blended), sum_up, sum_out, sum_down)
+    sum_qkv = [Chain(reduce_steps, [other], ("xy",)), None]
     sum_qkv[0].own = [back_heads(0, 0)]
     grad_heads[0][0], grad_blended = meet((grad_heads[0][0], grad_blended), sum_qkv[0], sum_out, sum_up)
     other = back_heads(1, 1)
-    other, grad_blended = meet((other, grad_blended), sum_out)
-    sum_qkv[1] = Chain(reduce_steps, [other], ("xy",))
+    other, grad_blended = meet((other, grad_blended), sum_out, sum_qkv[0])
+    sum_qkv[1] = Chain(reduce_steps, [other], ("yx",))
     out_rows = jnp.concatenate([sum_out.result[0][0], sum_out.result[0][1]], 1)
-    rows_rest = Chain(sum_z_steps, jnp.concatenate(sum_up.result + [out_rows], 1))
+    rows_rest = Chain(sum_z_steps, jnp.concatenate(sum_up.result + sum_down.result + [out_rows], 1))
     sum_qkv[1].own = [back_heads(0, 1)]
     grad_heads = meet(grad_heads, sum_qkv[0], sum_qkv[1])
-    own_grad, grad_input, sums_input = row_call(
-        in_back_kernel,
-        "in_norm_back",
-        [grad_heads[core][half] for core, half in pairs],
-        [w_qkv[core][half] for core, half in pairs],
-        vector_full,
-        [base, grad_hidden],
-        ["own", BF, "sums"],
-    )
+
+    def input_back(span, outs):
+        return row_call(
+            in_back_kernel,
+            "in_norm_back",
+            [grad_heads[core][half] for core, half in pairs],
+            [w_qkv[core][half] for core, half in pairs],
+            vector_full,
+            [base, grad_hidden],
+            outs,
+            span,
+            chunk_rows,
+        )
+
+    grad_far, sums_far = input_back((1, 1), [BF, "sums"])
+    send_far = Chain(mp_steps, [grad_far[:chunk_rows], grad_far[chunk_rows:]], 2)
+    grad_heads = meet(grad_heads, sum_qkv[1])
+    grad_near, sums_near, own_grad = input_back((0, 1), [BF, "sums", "own"])
+    send_near = Chain(mp_steps, [grad_near[chunk_rows:]], 1)
+    sums_input = sums_far + sums_near
 
     grad_vectors = jnp.stack(
         [
@@ -1062,13 +1106,16 @@
     grad_biases = jnp.stack(bias_parts, 1).reshape(MP, -1, DP, bias_width).transpose(0, 2, 1, 3)
     grad_biases = jnp.take(grad_biases, place[:DP], axis=1).reshape(MP, DP, -1)
     sum_small = Chain(small_reduce_steps, grad_vectors, grad_biases)
-    send_grad = send_back(grad_input)
-    meet((), sum_qkv[0], sum_qkv[1], sum_small, rows_rest)
-    meet((), sum_qkv[1], sum_small)
+    meet((), sum_qkv[1])
     rows_qkv = Chain(sum_z_steps, jnp.concatenate(sum_qkv[0].result + sum_qkv[1].result, 1))
-    meet((), rows_qkv, sum_small, send_grad)
+    meet((), send_far)
+    meet((), rows_rest)
+    meet((), rows_qkv)
+    meet((), send_near)
+    for _ in range(3):
+        meet((), sum_small)
     layer_output = spread_image(place, output[:chunk_rows], send_output.result, BF)[:, None]
-    input_grad = spread_image(place, own_grad, send_grad.result, F32)[:, None]
+    input_grad = spread_image(place, own_grad, send_near.result + send_far.result, F32)[:, None]
 
     small_total = sum_small.result
     vector_grad = small_total[:vector_size].reshape(vectors.shape)
@@ -1076,10 +1123,10 @@
     qkv_grad = rows_qkv.result.reshape(depth, 2, kinds, LANES).transpose(2, 0, 1, 3)
     up_size = block_width * units
     up_grad = rows_rest.result[:, :up_size].reshape(depth, units, block_width)
-    down_grad = rows_down.result.reshape(depth, units, block_width).transpose(1, 2, 0)
+    down_grad = rows_rest.result[:, up_size : 2 * up_size].reshape(depth, units, block_width).transpose(1, 2, 0)
     grads = (
         qkv_grad.reshape(qkv_weight.shape),
-        rows_rest.result[:, up_size:].T,
+        rows_rest.result[:, 2 * up_size :].T,
         up_grad,
         down_grad,
         bias_grad,

time: 661 us -> 676 us (1.023)
  matrix products: 107 us -> 72 us
  waiting for transfers between devices: 150 us -> 176 us
  Pallas kernels: 170 us -> 195 us
  other arithmetic: 68.7 us -> 58.1 us
  local copies, waits for them, and re-layouts: 64.9 us -> 72.3 us
    ppermute x46, waiting for transfers between devices: 74.9 us -> 126 us  [swap_mp(): return lax.ppermute(part, 'mp', [(each, each ^ step) for each in range(MP)])]
    dot_general x16 -> x12, matrix products: 68.8 us -> 31.1 us  [dot_nn(): lax.dot_general(left, right, (((1,), (0,)), ((), ())), preferred_element_...]
    pallas_call x4 -> x9, Pallas kernels: 55.8 us -> 84.2 us  [the longest x5 60.7 us: row_call(): pl.pallas_call(functools.partial(kernel, len(lefts)), grid=(count,), in_s...]
    unnamed x297 -> x310, local copies, waits for them, and re-layouts: 33 us -> 47.9 us
    ppermute x16, waiting for transfers between devices: 26.9 us -> 13.6 us  [swap_y(): return lax.ppermute(part, 'dp', [(each, each ^ 1) for each in range(DP)])]
    ppermute x24 -> x21, waiting for transfers between devices: 48.7 us -> 36.5 us  [swap_z(): lax.ppermute(part, 'dp', [(z * YS + y, (z ^ step) * YS + y) for z in rang...]
    convert_element_type x21 -> x17, other arithmetic: 22.6 us -> 18.5 us  [add_low(): return (first.astype(F32) + second.astype(F32)).astype(BF)]
    ppermute x24 -> x21, starting transfers between devices: 46.4 us -> 45.5 us  [swap_z(): lax.ppermute(part, 'dp', [(z * YS + y, (z ^ step) * YS + y) for z in rang...]
  transfers between devices with their start and end apart: 86 -> 83, of which waited for: 20 -> 24; matrix products, arithmetic and copies ran while one was open for 28% -> 18% of each run, Pallas kernels for 20% -> 25%
where the time goes in v5:
time: 676 us; the launch traced here: 671 us
  Pallas kernels  195 us (29%)
  waiting for transfers between devices  176 us (26%)
  starting transfers between devices  93.7 us (14%)
  local copies, waits for them, and re-layouts  72.3 us (11%)
  matrix products  72 us (11%)
  other arithmetic  58.1 us (9%)
    ppermute x46, waiting for transfers between devices, swap_mp(): return lax.ppermute(part, 'mp', [(each, each ^ step) for each in range(MP)])  126 us
    pallas_call x4, Pallas kernels, attend_back(): pl.pallas_call(functools.partial(attend_back_kernel, 256), grid=(pairs,),...  63.7 us
    pallas_call x5, Pallas kernels, row_call(): pl.pallas_call(functools.partial(kernel, len(lefts)), grid=(count,), in_s...  60.7 us
    unnamed x310, local copies, waits for them, and re-layouts  47.9 us
    ppermute x21, starting transfers between devices, swap_z(): lax.ppermute(part, 'dp', [(z * YS + y, (z ^ step) * YS + y) for z in rang...  45.5 us
    dot_general x16, matrix products, dot_tn(): lax.dot_general(left, right, (((0,), (0,)), ((), ())), preferred_element_...  40.9 us
    ppermute x21, waiting for transfers between devices, swap_z(): lax.ppermute(part, 'dp', [(z * YS + y, (z ^ step) * YS + y) for z in rang...  36.5 us
    pallas_call x4, Pallas kernels, attend(): pl.pallas_call(functools.partial(attend_kernel, 256), grid=(pairs,), in_s...  35.9 us
  transfers between devices with their start and end apart: 83, of which 24 were waited for; matrix products, arithmetic and copies ran while one was open for 18% of the time, Pallas kernels for 25%

profile of v5, /device:TPU:0, one launch (start us, length us, event | category | flops | bytes accessed | tf_op | source)
XLA Modules:
  0.0 670.7 jit_solution(5248496342901452567)
XLA Ops:
  3.5 3.0 collective-permute-start
  6.5 2.6 collective-permute-start.1
  27.7 4.0 collective-permute-done.10
  31.7 3.1 collective-permute-start.7
  45.0 2.7 collective-permute-done.12
  52.6 2.8 collective-permute-start.22
  64.0 3.4 assemble_image.2
  70.2 9.7 %collective-permute-done.18 = bf16[512,384]{1,0:T(8,128)(2,1)} collective-permute-done((bf16[512,384]{1,0:T(8,128)(2,1)}, bf16[512,384]{1,0:T(8,128)(2,1)}, u32[]{:S(2)}, u32[]{:S(2)}) %collective-permute-start.18) | collective-permute-done | bytes 393248 | tf_op jit(solution)/shard_map/ppermute | solution.py:378
  79.9 2.6 pad_maximum_fusion.4.refs_4_
  85.6 2.9 add_convert_fusion.9.q_ref.k_ref.v_ref
  88.5 8.8 %attend.4 = (bf16[1024,256]{1,0:T(8,128)(2,1)S(1)}, f32[2,8,1024]{2,1,0:T(8,128)S(1)}) custom-call(bf16[1024,768]{1,0:T(8,128)(2,1)S(1)} %add_convert_fusion.9.q_ref.k_ref.v_ref, bf16[1024,768]{1,0:T(8,128)(2,1)S(1)} %add_convert_fusion.9.q_ref.k_ref.v_ref, bf16[1024,768]{1,0:T(8,128)(2,1)S(1)} %add_convert_fusion.9.q_ref.k_ref.v_ref), custom_call_target="tpu_custom_call" | custom-call | flops 4294967296 | bytes 6291456 | tf_op jit(solution)/shard_map/attend/pallas_call | solution.py:798
  97.4 6.6 collective-permute-done.20
  113.1 2.8 add_convert_fusion.8.q_ref.k_ref.v_ref
  115.9 9.0 %attend.5 = (bf16[1024,256]{1,0:T(8,128)(2,1)S(1)}, f32[2,8,1024]{2,1,0:T(8,128)S(1)}) custom-call(bf16[1024,768]{1,0:T(8,128)(2,1)S(1)} %add_convert_fusion.8.q_ref.k_ref.v_ref, bf16[1024,768]{1,0:T(8,128)(2,1)S(1)} %add_convert_fusion.8.q_ref.k_ref.v_ref, bf16[1024,768]{1,0:T(8,128)(2,1)S(1)} %add_convert_fusion.8.q_ref.k_ref.v_ref), custom_call_target="tpu_custom_call" | custom-call | flops 4294967296 | bytes 6291456 | tf_op jit(solution)/shard_map/attend/pallas_call | solution.py:798
  126.1 4.2 collective-permute-done.27
  137.4 3.2 add_convert_fusion.7.q_ref.k_ref.v_ref
  140.6 9.2 %attend.6 = (bf16[1024,256]{1,0:T(8,128)(2,1)S(1)}, f32[2,8,1024]{2,1,0:T(8,128)S(1)}) custom-call(bf16[1024,768]{1,0:T(8,128)(2,1)S(1)} %add_convert_fusion.7.q_ref.k_ref.v_ref, bf16[1024,768]{1,0:T(8,128)(2,1)S(1)} %add_convert_fusion.7.q_ref.k_ref.v_ref, bf16[1024,768]{1,0:T(8,128)(2,1)S(1)} %add_convert_fusion.7.q_ref.k_ref.v_ref), custom_call_target="tpu_custom_call" | custom-call | flops 4294967296 | bytes 6291456 | tf_op jit(solution)/shard_map/attend/pallas_call | solution.py:798
  149.9 20.3 %collective-permute-done.30 = bf16[2,1024,128]{2,1,0:T(8,128)(2,1)S(1)} collective-permute-done((bf16[2,1024,128]{2,1,0:T(8,128)(2,1)S(1)}, bf16[2,1024,128]{2,1,0:T(8,128)(2,1)S(1)}, u32[]{:S(2)}, u32[]{:S(2)}) %collective-permute-start.30) | collective-permute-done | bytes 524320 | tf_op jit(solution)/shard_map/ppermute | solution.py:378
  172.0 3.4 pad_maximum_fusion.1.right_ref.refs_7_
  182.8 8.8 %attend.7 = (bf16[1024,256]{1,0:T(8,128)(2,1)S(1)}, f32[2,8,1024]{2,1,0:T(8,128)S(1)}) custom-call(bf16[1024,768]{1,0:T(8,128)(2,1)S(1)} %add_convert_fusion.6.q_ref.k_ref.v_ref, bf16[1024,768]{1,0:T(8,128)(2,1)S(1)} %add_convert_fusion.6.q_ref.k_ref.v_ref, bf16[1024,768]{1,0:T(8,128)(2,1)S(1)} %add_convert_fusion.6.q_ref.k_ref.v_ref), custom_call_target="tpu_custom_call" | custom-call | flops 4294967296 | bytes 6291456 | tf_op jit(solution)/shard_map/attend/pallas_call | solution.py:798
  198.7 6.9 %out_norm.1 = (f32[1024,1024]{1,0:T(8,128)}, f32[1024,1024]{1,0:T(8,128)}, bf16[1024,1024]{1,0:T(8,128)(2,1)}) custom-call(bf16[1024,256]{1,0:T(8,128)(2,1)S(1)} %get-tuple-element.243.refs_0_, bf16[1024,256]{1,0:T(8,128)(2,1)S(1)} %copy-done.29, bf16[1024,256]{1,0:T(8,128)(2,1)S(1)} %copy-done.32, bf16[1024,256]{1,0:T(8,128)(2,1)S(1)} %get-tuple-element.246.refs_3_, ...), custom_call_target="tpu_custom_call" | custom-call | flops 2147483648 | bytes 25165824 | tf_op jit(solution)/shard_map/out_norm/pallas_call | solution.py:698
  207.2 4.5 expand.4
  214.3 6.0 expand.5
  221.7 6.8 %expand.6 = (bf16[1024,1024]{1,0:T(8,128)(2,1)S(1)}, bf16[1024,1024]{1,0:T(8,128)(2,1)S(1)}) custom-call(bf16[1024,1024]{1,0:T(8,128)(2,1)S(1)} %copy-done.25, bf16[1024,1024]{1,0:T(8,128)(2,1)} %collective-permute-done.32.right_ref.refs_5_, f32[1,1024]{1,0:T(1,128)S(1)} %reshape_reshape.14.bias_ref), custom_call_target="tpu_custom_call" | custom-call | flops 2147483648 | bytes 8388608 | tf_op jit(solution)/shard_map/expand/pallas_call | solution.py:661
  229.9 10.2 %collective-permute-done.37 = bf16[1024,512]{1,0:T(8,128)(2,1)} collective-permute-done((bf16[1024,512]{1,0:T(8,128)(2,1)}, bf16[1024,512]{1,0:T(8,128)(2,1)}, u32[]{:S(2)}, u32[]{:S(2)}) %collective-permute-start.37) | collective-permute-done | bytes 1048608 | tf_op jit(solution)/shard_map/ppermute | solution.py:378
  240.1 6.2 expand.7
  249.5 3.7 convolution_convert_fusion.3
  253.3 3.7 convolution_convert_fusion.2
  257.5 2.8 pad_maximum_fusion.2.refs_6_
  260.4 2.8 pad_maximum_fusion.3.refs_7_
  270.3 5.5 fusion.46
  278.3 16.6 %down_output.1 = (bf16[1024,1024]{1,0:T(8,128)(2,1)S(1)}, f32[8,1024]{1,0:T(8,128)S(1)}) custom-call(bf16[1024,1024]{1,0:T(8,128)(2,1)S(1)} %copy-done.44, bf16[1024,1024]{1,0:T(8,128)(2,1)} %copy-done.47, bf16[1024,1024]{1,0:T(8,128)(2,1)} %copy-done.42, bf16[1024,1024]{1,0:T(8,128)(2,1)} %copy-done.48, bf16[1024,1024]{1,0:T(8,128)(2,1)} %collective-permute-done.43.refs_4_, ...), custom_call_target="tpu_custom_call" | custom-call | flops 8589934592 | bytes 25165824 | tf_op jit(solution)/shard_map/down_output/pallas_call | solution.py:698
  295.0 5.1 multiply_convert_fusion.3.refs_2_
  300.1 4.1 multiply_convert_fusion.2.refs_0_
  304.2 3.7 multiply_convert_fusion.1.refs_3_
  308.0 4.7 multiply_convert_fusion.refs_1_
  315.0 3.7 convolution_convert_fusion
  318.8 3.8 convolution_convert_fusion.1
  330.4 20.0 %up_norm_back.1 = (f32[1024,1024]{1,0:T(8,128)}, bf16[1024,1024]{1,0:T(8,128)(2,1)S(1)}, f32[8,1024]{1,0:T(8,128)S(1)}) custom-call(bf16[1024,1024]{1,0:T(8,128)(2,1)S(1)} %multiply_convert_fusion.2.refs_0_, bf16[1024,1024]{1,0:T(8,128)(2,1)} %copy-done.88, bf16[1024,1024]{1,0:T(8,128)(2,1)} %multiply_convert_fusion.3.refs_2_, ...), custom_call_target="tpu_custom_call" | custom-call | flops 8589934592 | bytes 25165824 | tf_op jit(solution)/shard_map/up_norm_back/pallas_call | solution.py:698
  350.8 2.9 add_convert_fusion.2
  357.6 4.9 fusion.48
  362.5 29.9 %collective-permute-done.50.refs_1_ = bf16[256,1024]{1,0:T(8,128)(2,1)S(1)} collective-permute-done((bf16[256,1024]{1,0:T(8,128)(2,1)}, bf16[256,1024]{1,0:T(8,128)(2,1)S(1)}, u32[]{:S(2)}, u32[]{:S(2)}) %collective-permute-start.50) | collective-permute-done | bytes 524320 | tf_op jit(solution)/shard_map/ppermute | solution.py:378
  395.7 10.9 %collective-permute-done.51.refs_2_ = bf16[256,1024]{1,0:T(8,128)(2,1)S(1)} collective-permute-done((bf16[256,1024]{1,0:T(8,128)(2,1)S(1)}, bf16[256,1024]{1,0:T(8,128)(2,1)S(1)}, u32[]{:S(2)}, u32[]{:S(2)}) %collective-permute-start.51) | collective-permute-done | bytes 524320 | tf_op jit(solution)/shard_map/ppermute | solution.py:378
  412.1 2.6 add_convert_fusion.1
  415.6 2.6 add_convert_fusion
  425.0 15.7 %attend_back.4.refs_2_ = bf16[1024,768]{1,0:T(8,128)(2,1)S(1)} custom-call(bf16[1024,768]{1,0:T(8,128)(2,1)S(1)} %copy-done.55, bf16[1024,768]{1,0:T(8,128)(2,1)S(1)} %copy-done.55, bf16[1024,768]{1,0:T(8,128)(2,1)S(1)} %copy-done.55, bf16[1024,256]{1,0:T(8,128)(2,1)S(1)} %convolution_convert_fusion.15.g_ref, f32[2,8,1024]{2,1,0:T(8,128)S(1)} %get-tuple-element.311.lse_ref), custom_call_target="tpu_custom_call" | custom-call | flops 10737418240 | bytes 11010048 | tf_op jit(solution)/shard_map/attend_back/pallas_call | solution.py:822
  442.3 2.7 spread_image.2
  447.0 7.5 %collective-permute-done.55 = bf16[512,512]{1,0:T(8,128)(2,1)S(1)} collective-permute-done((bf16[512,512]{1,0:T(8,128)(2,1)S(1)}, bf16[512,512]{1,0:T(8,128)(2,1)S(1)}, u32[]{:S(2)}, u32[]{:S(2)}) %collective-permute-start.55) | collective-permute-done | bytes 524320 | tf_op jit(solution)/shard_map/ppermute | solution.py:378
  459.3 15.9 %attend_back.5.refs_0_ = bf16[1024,768]{1,0:T(8,128)(2,1)S(1)} custom-call(bf16[1024,768]{1,0:T(8,128)(2,1)S(1)} %copy-done.51, bf16[1024,768]{1,0:T(8,128)(2,1)S(1)} %copy-done.51, bf16[1024,768]{1,0:T(8,128)(2,1)S(1)} %copy-done.51, bf16[1024,256]{1,0:T(8,128)(2,1)S(1)} %convolution_convert_fusion.14.g_ref, f32[2,8,1024]{2,1,0:T(8,128)S(1)} %get-tuple-element.317.lse_ref), custom_call_target="tpu_custom_call" | custom-call | flops 10737418240 | bytes 11010048 | tf_op jit(solution)/shard_map/attend_back/pallas_call | solution.py:822
  477.2 3.4 collective-permute-done.59
  484.2 16.2 %attend_back.6.refs_3_ = bf16[1024,768]{1,0:T(8,128)(2,1)S(1)} custom-call(bf16[1024,768]{1,0:T(8,128)(2,1)S(1)} %copy-done.53, bf16[1024,768]{1,0:T(8,128)(2,1)S(1)} %copy-done.53, bf16[1024,768]{1,0:T(8,128)(2,1)S(1)} %copy-done.53, bf16[1024,256]{1,0:T(8,128)(2,1)S(1)} %convolution_convert_fusion.12.g_ref, f32[2,8,1024]{2,1,0:T(8,128)S(1)} %get-tuple-element.326.lse_ref), custom_call_target="tpu_custom_call" | custom-call | flops 10737418240 | bytes 11010048 | tf_op jit(solution)/shard_map/attend_back/pallas_call | solution.py:822
  504.2 3.9 collective-permute-start.73
  511.0 15.9 %attend_back.7.refs_1_ = bf16[1024,768]{1,0:T(8,128)(2,1)S(1)} custom-call(bf16[1024,768]{1,0:T(8,128)(2,1)S(1)} %copy-done.57, bf16[1024,768]{1,0:T(8,128)(2,1)S(1)} %copy-done.57, bf16[1024,768]{1,0:T(8,128)(2,1)S(1)} %copy-done.57, bf16[1024,256]{1,0:T(8,128)(2,1)S(1)} %convolution_convert_fusion.13.g_ref, f32[2,8,1024]{2,1,0:T(8,128)S(1)} %get-tuple-element.331.lse_ref), custom_call_target="tpu_custom_call" | custom-call | flops 10737418240 | bytes 11010048 | tf_op jit(solution)/shard_map/attend_back/pallas_call | solution.py:822
  528.8 5.7 collective-permute-done.73
  534.5 16.0 %collective-permute-done.74 = bf16[128,2304]{1,0:T(8,128)(2,1)S(1)} collective-permute-done((bf16[128,2304]{1,0:T(8,128)(2,1)S(1)}, bf16[128,2304]{1,0:T(8,128)(2,1)S(1)}, u32[]{:S(2)}, u32[]{:S(2)}) %collective-permute-start.74) | collective-permute-done | bytes 589856 | tf_op jit(solution)/shard_map/ppermute | solution.py:368
  564.1 3.0 multiply_subtract_fusion
  569.1 8.4 %in_norm_back.3 = (bf16[512,1024]{1,0:T(8,128)(2,1)S(1)}, f32[8,1024]{1,0:T(8,128)S(1)}) custom-call(bf16[1024,768]{1,0:T(8,128)(2,1)S(1)} %attend_back.5.refs_0_, bf16[1024,768]{1,0:T(8,128)(2,1)S(1)} %copy-done.4, bf16[1024,768]{1,0:T(8,128)(2,1)S(1)} %attend_back.4.refs_2_, bf16[1024,768]{1,0:T(8,128)(2,1)} %copy-done.1, ...), custom_call_target="tpu_custom_call" | custom-call | tf_op jit(solution)/shard_map/in_norm_back/pallas_call | solution.py:698
  578.5 8.8 %in_norm_back.2 = (bf16[512,1024]{1,0:T(8,128)(2,1)S(1)}, f32[8,1024]{1,0:T(8,128)S(1)}, f32[256,1024]{1,0:T(8,128)S(1)}) custom-call(bf16[1024,768]{1,0:T(8,128)(2,1)S(1)} %attend_back.5.refs_0_, bf16[1024,768]{1,0:T(8,128)(2,1)S(1)} %copy-done.4, bf16[1024,768]{1,0:T(8,128)(2,1)} %copy-done, bf16[1024,768]{1,0:T(8,128)(2,1)} %copy-done.1, ...), custom_call_target="tpu_custom_call" | custom-call | tf_op jit(solution)/shard_map/in_norm_back/pallas_call | solution.py:698
  597.8 11.0 %collective-permute-done.67.refs_1_ = bf16[256,1024]{1,0:T(8,128)(2,1)S(1)} collective-permute-done((bf16[256,1024]{1,0:T(8,128)(2,1)}, bf16[256,1024]{1,0:T(8,128)(2,1)S(1)}, u32[]{:S(2)}, u32[]{:S(2)}) %collective-permute-start.67) | collective-permute-done | bytes 524320 | tf_op jit(solution)/shard_map/ppermute | solution.py:378
  608.9 10.1 %collective-permute-done.68.refs_2_ = bf16[256,1024]{1,0:T(8,128)(2,1)S(1)} collective-permute-done((bf16[256,1024]{1,0:T(8,128)(2,1)S(1)}, bf16[256,1024]{1,0:T(8,128)(2,1)S(1)}, u32[]{:S(2)}, u32[]{:S(2)}) %collective-permute-start.68) | collective-permute-done | bytes 524320 | tf_op jit(solution)/shard_map/ppermute | solution.py:378
  620.3 12.6 %collective-permute-start.80 = (f32[1216]{0:T(1024)S(1)}, f32[1216]{0:T(1024)S(1)}, u32[]{:S(2)}, u32[]{:S(2)}) collective-permute-start(f32[1216]{0:T(1024)S(1)} %get-tuple-element.439), channel_id=1, source_target_pairs={{0,8},{4,12},{8,0},{12,4},{16,24},{20,28},{24,16},{28,20},{1,9},{5... | collective-permute-start | bytes 14600 | tf_op jit(solution)/shard_map/ppermute | solution.py:368
  640.5 8.2 %collective-permute-done.69 = bf16[512,384]{1,0:T(8,128)(2,1)} collective-permute-done((bf16[512,384]{1,0:T(8,128)(2,1)S(1)}, bf16[512,384]{1,0:T(8,128)(2,1)}, u32[]{:S(2)}, u32[]{:S(2)}) %collective-permute-start.69) | collective-permute-done | bytes 393248 | tf_op jit(solution)/shard_map/ppermute | solution.py:378
  655.1 3.1 spread_image.3
  659.2 7.9 %collective-permute-done.71 = bf16[128,768]{1,0:T(8,128)(2,1)S(1)} collective-permute-done((bf16[128,768]{1,0:T(8,128)(2,1)S(1)}, bf16[128,768]{1,0:T(8,128)(2,1)S(1)}, u32[]{:S(2)}, u32[]{:S(2)}) %collective-permute-start.71) | collective-permute-done | bytes 196640 | tf_op jit(solution)/shard_map/ppermute | solution.py:368
  (649 shorter events, 203.5 us)
Async XLA Ops:
  3.5 19.2 %collective-permute-start = (bf16[128,384]{1,0:T(8,128)(2,1)}, bf16[128,384]{1,0:T(8,128)(2,1)}, u32[]{:S(2)}, u32[]{:S(2)}) collective-permute-start(bf16[128,384]{1,0:T(8,128)(2,1)} %copy.173), channel_id=1, source_target_pairs={{0,8},{4,12},{8,0},{12,4},{16,24},{20,28},{24,16},{28,20},{1,9},{5... | collective-permute-start | bytes 294920 | tf_op jit(solution)/shard_map/ppermute | solution.py:368
  6.5 18.0 %collective-permute-start.1 = (bf16[128,384]{1,0:T(8,128)(2,1)}, bf16[128,384]{1,0:T(8,128)(2,1)}, u32[]{:S(2)}, u32[]{:S(2)}) collective-permute-start(bf16[128,384]{1,0:T(8,128)(2,1)} %copy.173), channel_id=1, source_target_pairs={{0,16},{4,20},{8,24},{12,28},{16,0},{20,4},{24,8},{28,12},{1,17},{... | collective-permute-start | bytes 294920 | tf_op jit(solution)/shard_map/ppermute | solution.py:368
  9.1 15.5 %collective-permute-start.2 = (bf16[128,384]{1,0:T(8,128)(2,1)}, bf16[128,384]{1,0:T(8,128)(2,1)}, u32[]{:S(2)}, u32[]{:S(2)}) collective-permute-start(bf16[128,384]{1,0:T(8,128)(2,1)} %copy.173), channel_id=1, source_target_pairs={{0,24},{4,28},{8,16},{12,20},{16,8},{20,12},{24,0},{28,4},{1,25},{... | collective-permute-start | bytes 294920 | tf_op jit(solution)/shard_map/ppermute | solution.py:368
  24.5 23.2 %collective-permute-start.14 = (bf16[256,1024]{1,0:T(8,128)(2,1)}, bf16[256,1024]{1,0:T(8,128)(2,1)S(1)}, u32[]{:S(2)}, u32[]{:S(2)}) collective-permute-start(bf16[256,1024]{1,0:T(8,128)(2,1)} %get-tuple-element.474), channel_id=1, source_target_pairs={{0,1},{1,0},{2,3},{3,2},{4,5},{5,4},{6,7},{7,6},{8,9},{9,8},{10,11... | collective-permute-start | bytes 1572872 | tf_op jit(solution)/shard_map/ppermute | solution.py:378
  24.5 23.2 %collective-permute-start.15 = (bf16[256,1024]{1,0:T(8,128)(2,1)}, bf16[256,1024]{1,0:T(8,128)(2,1)S(1)}, u32[]{:S(2)}, u32[]{:S(2)}) collective-permute-start(bf16[256,1024]{1,0:T(8,128)(2,1)} %get-tuple-element.473), channel_id=1, source_target_pairs={{0,2},{1,3},{2,0},{3,1},{4,6},{5,7},{6,4},{7,5},{8,10},{9,11},{10,... | collective-permute-start | bytes 1572872 | tf_op jit(solution)/shard_map/ppermute | solution.py:378
  26.3 23.5 %collective-permute-start.16 = (bf16[256,1024]{1,0:T(8,128)(2,1)}, bf16[256,1024]{1,0:T(8,128)(2,1)S(1)}, u32[]{:S(2)}, u32[]{:S(2)}) collective-permute-start(bf16[256,1024]{1,0:T(8,128)(2,1)} %get-tuple-element.472), channel_id=1, source_target_pairs={{0,3},{1,2},{2,1},{3,0},{4,7},{5,6},{6,5},{7,4},{8,11},{9,10},{10,... | collective-permute-start | bytes 1572872 | tf_op jit(solution)/shard_map/ppermute | solution.py:378
  51.4 28.5 %collective-permute-start.17 = (bf16[1024,384]{1,0:T(8,128)(2,1)}, bf16[1024,384]{1,0:T(8,128)(2,1)}, u32[]{:S(2)}, u32[]{:S(2)}) collective-permute-start(bf16[1024,384]{1,0:T(8,128)(2,1)} %constant_dynamic-update-slice_fusion), channel_id=1, source_target_pairs={{0,2},{1,3},{2,0},{3,1},{4,6},{5,7},{6,4},{7,5},{8,10},{9,11},{10,... | collective-permute-start | bytes 2359304 | tf_op jit(solution)/shard_map/ppermute | solution.py:378
  52.0 45.4 %collective-permute-start.21 = (bf16[128,2304]{1,0:T(8,128)(2,1)}, bf16[128,2304]{1,0:T(8,128)(2,1)}, u32[]{:S(2)}, u32[]{:S(2)}) collective-permute-start(bf16[128,2304]{1,0:T(8,128)(2,1)} %pad_maximum_fusion.13), channel_id=1, source_target_pairs={{0,8},{4,12},{8,0},{12,4},{16,24},{20,28},{24,16},{28,20},{1,9},{5... | collective-permute-start | bytes 1769480 | tf_op jit(solution)/shard_map/ppermute | solution.py:368
  52.6 44.7 %collective-permute-start.22 = (bf16[128,2304]{1,0:T(8,128)(2,1)}, bf16[128,2304]{1,0:T(8,128)(2,1)}, u32[]{:S(2)}, u32[]{:S(2)}) collective-permute-start(bf16[128,2304]{1,0:T(8,128)(2,1)} %pad_maximum_fusion.13), channel_id=1, source_target_pairs={{0,16},{4,20},{8,24},{12,28},{16,0},{20,4},{24,8},{28,12},{1,17},{... | collective-permute-start | bytes 1769480 | tf_op jit(solution)/shard_map/ppermute | solution.py:368
  55.4 42.0 %collective-permute-start.23 = (bf16[128,2304]{1,0:T(8,128)(2,1)}, bf16[128,2304]{1,0:T(8,128)(2,1)}, u32[]{:S(2)}, u32[]{:S(2)}) collective-permute-start(bf16[128,2304]{1,0:T(8,128)(2,1)} %pad_maximum_fusion.13), channel_id=1, source_target_pairs={{0,24},{4,28},{8,16},{12,20},{16,8},{20,12},{24,0},{28,4},{1,25},{... | collective-permute-start | bytes 1769480 | tf_op jit(solution)/shard_map/ppermute | solution.py:368
  58.0 21.9 %collective-permute-start.18 = (bf16[512,384]{1,0:T(8,128)(2,1)}, bf16[512,384]{1,0:T(8,128)(2,1)}, u32[]{:S(2)}, u32[]{:S(2)}) collective-permute-start(bf16[512,384]{1,0:T(8,128)(2,1)} %pad_maximum_fusion.16), channel_id=1, source_target_pairs={{0,2},{1,3},{2,0},{3,1},{4,6},{5,7},{6,4},{7,5},{8,10},{9,11},{10,... | collective-permute-start | bytes 1179656 | tf_op jit(solution)/shard_map/ppermute | solution.py:378
  82.5 21.5 %collective-permute-start.19 = (bf16[1024,768]{1,0:T(8,128)(2,1)}, bf16[1024,768]{1,0:T(8,128)(2,1)}, u32[]{:S(2)}, u32[]{:S(2)}) collective-permute-start(bf16[1024,768]{1,0:T(8,128)(2,1)} %pad_maximum_fusion.4.refs_4_), channel_id=1, source_target_pairs={{0,1},{1,0},{2,3},{3,2},{4,5},{5,4},{6,7},{7,6},{8,9},{9,8},{10,11... | collective-permute-start | bytes 4718600 | tf_op jit(solution)/shard_map/ppermute | solution.py:378
  84.0 20.0 %collective-permute-start.20 = (bf16[512,768]{1,0:T(8,128)(2,1)S(1)}, bf16[512,768]{1,0:T(8,128)(2,1)S(1)}, u32[]{:S(2)}, u32[]{:S(2)}) collective-permute-start(bf16[512,768]{1,0:T(8,128)(2,1)S(1)} %pad_maximum_fusion.12), channel_id=1, source_target_pairs={{0,4},{4,0},{8,12},{12,8},{16,20},{20,16},{24,28},{28,24},{1,5},{5... | collective-permute-start | bytes 2359304 | tf_op jit(solution)/shard_map/ppermute | solution.py:374
  109.6 20.7 %collective-permute-start.24 = (bf16[1024,768]{1,0:T(8,128)(2,1)S(1)}, bf16[1024,768]{1,0:T(8,128)(2,1)S(1)}, u32[]{:S(2)}, u32[]{:S(2)}) collective-permute-start(bf16[1024,768]{1,0:T(8,128)(2,1)S(1)} %pad_maximum_fusion.5.refs_5_), channel_id=1, source_target_pairs={{0,1},{1,0},{2,3},{3,2},{4,5},{5,4},{6,7},{7,6},{8,9},{9,8},{10,11... | collective-permute-start | bytes 4718600 | tf_op jit(solution)/shard_map/ppermute | solution.py:378
  110.4 14.6 %collective-permute-start.25 = (bf16[2,512,128]{2,1,0:T(8,128)(2,1)S(1)}, bf16[2,512,128]{2,1,0:T(8,128)(2,1)S(1)}, u32[]{:S(2)}, u32[]{:S(2)}) collective-permute-start(bf16[2,512,128]{2,1,0:T(8,128)(2,1)S(1)} %pad_maximum_fusion.17), channel_id=1, source_target_pairs={{0,4},{4,0},{8,12},{12,8},{16,20},{20,16},{24,28},{28,24},{1,5},{5... | collective-permute-start | bytes 786440 | tf_op jit(solution)/shard_map/ppermute | solution.py:374
  112.0 14.1 %collective-permute-start.26 = (bf16[512,512]{1,0:T(8,128)(2,1)S(1)}, bf16[512,512]{1,0:T(8,128)(2,1)S(1)}, u32[]{:S(2)}, u32[]{:S(2)}) collective-permute-start(bf16[512,512]{1,0:T(8,128)(2,1)S(1)} %get-tuple-element.462), channel_id=1, source_target_pairs={{0,2},{1,3},{2,0},{3,1},{4,6},{5,7},{6,4},{7,5},{8,10},{9,11},{10,... | collective-permute-start | bytes 1572872 | tf_op jit(solution)/shard_map/ppermute | solution.py:378
  112.6 17.7 %collective-permute-start.27 = (bf16[512,512]{1,0:T(8,128)(2,1)S(1)}, bf16[512,512]{1,0:T(8,128)(2,1)S(1)}, u32[]{:S(2)}, u32[]{:S(2)}) collective-permute-start(bf16[512,512]{1,0:T(8,128)(2,1)S(1)} %get-tuple-element.461), channel_id=1, source_target_pairs={{0,4},{4,0},{8,12},{12,8},{16,20},{20,16},{24,28},{28,24},{1,5},{5... | collective-permute-start | bytes 1572872 | tf_op jit(solution)/shard_map/ppermute | solution.py:374
  131.6 38.6 %collective-permute-start.28 = (bf16[512,1024]{1,0:T(8,128)(2,1)}, bf16[512,1024]{1,0:T(8,128)(2,1)}, u32[]{:S(2)}, u32[]{:S(2)}) collective-permute-start(bf16[512,1024]{1,0:T(8,128)(2,1)} %pad_maximum_fusion.6), channel_id=1, source_target_pairs={{0,4},{4,0},{8,12},{12,8},{16,20},{20,16},{24,28},{28,24},{1,5},{5... | collective-permute-start | bytes 3145736 | tf_op jit(solution)/shard_map/ppermute | solution.py:374
  134.2 36.0 %collective-permute-start.29 = (bf16[1024,512]{1,0:T(8,128)(2,1)}, bf16[1024,512]{1,0:T(8,128)(2,1)}, u32[]{:S(2)}, u32[]{:S(2)}) collective-permute-start(bf16[1024,512]{1,0:T(8,128)(2,1)} %pad_maximum_fusion.7), channel_id=1, source_target_pairs={{0,2},{1,3},{2,0},{3,1},{4,6},{5,7},{6,4},{7,5},{8,10},{9,11},{10,... | collective-permute-start | bytes 3145736 | tf_op jit(solution)/shard_map/ppermute | solution.py:378
  135.9 34.3 %collective-permute-start.30 = (bf16[2,1024,128]{2,1,0:T(8,128)(2,1)S(1)}, bf16[2,1024,128]{2,1,0:T(8,128)(2,1)S(1)}, u32[]{:S(2)}, u32[]{:S(2)}) collective-permute-start(bf16[2,1024,128]{2,1,0:T(8,128)(2,1)S(1)} %pad_maximum_fusion.14), channel_id=1, source_target_pairs={{0,2},{1,3},{2,0},{3,1},{4,6},{5,7},{6,4},{7,5},{8,10},{9,11},{10,... | collective-permute-start | bytes 1572872 | tf_op jit(solution)/shard_map/ppermute | solution.py:378
  171.9 21.8 %collective-permute-start.31 = (bf16[1024,1024]{1,0:T(8,128)(2,1)S(1)}, bf16[1024,1024]{1,0:T(8,128)(2,1)}, u32[]{:S(2)}, u32[]{:S(2)}) collective-permute-start(bf16[1024,1024]{1,0:T(8,128)(2,1)S(1)} %pad_maximum_fusion.right_ref.refs_6_), channel_id=1, source_target_pairs={{0,1},{1,0},{2,3},{3,2},{4,5},{5,4},{6,7},{7,6},{8,9},{9,8},{10,11... | collective-permute-start | bytes 6291464 | tf_op jit(solution)/shard_map/ppermute | solution.py:378
  175.5 18.2 %collective-permute-start.32 = (bf16[1024,1024]{1,0:T(8,128)(2,1)}, bf16[1024,1024]{1,0:T(8,128)(2,1)}, u32[]{:S(2)}, u32[]{:S(2)}) collective-permute-start(bf16[1024,1024]{1,0:T(8,128)(2,1)} %pad_maximum_fusion.1.right_ref.refs_7_), channel_id=1, source_target_pairs={{0,1},{1,0},{2,3},{3,2},{4,5},{5,4},{6,7},{7,6},{8,9},{9,8},{10,11... | collective-permute-start | bytes 6291464 | tf_op jit(solution)/shard_map/ppermute | solution.py:378
  177.0 14.6 %collective-permute-start.34 = (bf16[512,512]{1,0:T(8,128)(2,1)S(1)}, bf16[512,512]{1,0:T(8,128)(2,1)S(1)}, u32[]{:S(2)}, u32[]{:S(2)}) collective-permute-start(bf16[512,512]{1,0:T(8,128)(2,1)S(1)} %get-tuple-element.484), channel_id=1, source_target_pairs={{0,2},{1,3},{2,0},{3,1},{4,6},{5,7},{6,4},{7,5},{8,10},{9,11},{10,... | collective-permute-start | bytes 1572872 | tf_op jit(solution)/shard_map/ppermute | solution.py:378
  177.6 14.6 %collective-permute-start.35 = (bf16[512,512]{1,0:T(8,128)(2,1)S(1)}, bf16[512,512]{1,0:T(8,128)(2,1)S(1)}, u32[]{:S(2)}, u32[]{:S(2)}) collective-permute-start(bf16[512,512]{1,0:T(8,128)(2,1)S(1)} %get-tuple-element.483), channel_id=1, source_target_pairs={{0,4},{4,0},{8,12},{12,8},{16,20},{20,16},{24,28},{28,24},{1,5},{5... | collective-permute-start | bytes 1572872 | tf_op jit(solution)/shard_map/ppermute | solution.py:374
  179.5 14.2 %collective-permute-start.33 = (bf16[2,1024,256]{2,1,0:T(8,128)(2,1)S(1)}, bf16[2,1024,256]{2,1,0:T(8,128)(2,1)S(1)}, u32[]{:S(2)}, u32[]{:S(2)}) collective-permute-start(bf16[2,1024,256]{2,1,0:T(8,128)(2,1)S(1)} %pad_maximum_fusion.8), channel_id=1, source_target_pairs={{0,1},{1,0},{2,3},{3,2},{4,5},{5,4},{6,7},{7,6},{8,9},{9,8},{10,11... | collective-permute-start | bytes 3145736 | tf_op jit(solution)/shard_map/ppermute | solution.py:378
  191.6 56.1 %collective-permute-start.38 = (bf16[256,1024]{1,0:T(8,128)(2,1)}, bf16[256,1024]{1,0:T(8,128)(2,1)S(1)}, u32[]{:S(2)}, u32[]{:S(2)}) collective-permute-start(bf16[256,1024]{1,0:T(8,128)(2,1)} %get-tuple-element.471), channel_id=1, source_target_pairs={{0,1},{1,0},{2,3},{3,2},{4,5},{5,4},{6,7},{7,6},{8,9},{9,8},{10,11... | collective-permute-start | bytes 1572872 | tf_op jit(solution)/shard_map/ppermute | solution.py:378
  192.2 55.5 %collective-permute-start.39 = (bf16[256,1024]{1,0:T(8,128)(2,1)}, bf16[256,1024]{1,0:T(8,128)(2,1)S(1)}, u32[]{:S(2)}, u32[]{:S(2)}) collective-permute-start(bf16[256,1024]{1,0:T(8,128)(2,1)} %get-tuple-element.470), channel_id=1, source_target_pairs={{0,2},{1,3},{2,0},{3,1},{4,6},{5,7},{6,4},{7,5},{8,10},{9,11},{10,... | collective-permute-start | bytes 1572872 | tf_op jit(solution)/shard_map/ppermute | solution.py:378
  193.7 54.0 %collective-permute-start.40 = (bf16[256,1024]{1,0:T(8,128)(2,1)}, bf16[256,1024]{1,0:T(8,128)(2,1)S(1)}, u32[]{:S(2)}, u32[]{:S(2)}) collective-permute-start(bf16[256,1024]{1,0:T(8,128)(2,1)} %get-tuple-element.469), channel_id=1, source_target_pairs={{0,3},{1,2},{2,1},{3,0},{4,7},{5,6},{6,5},{7,4},{8,11},{9,10},{10,... | collective-permute-start | bytes 1572872 | tf_op jit(solution)/shard_map/ppermute | solution.py:378
  195.1 34.9 %collective-permute-start.36 = (bf16[512,1024]{1,0:T(8,128)(2,1)}, bf16[512,1024]{1,0:T(8,128)(2,1)}, u32[]{:S(2)}, u32[]{:S(2)}) collective-permute-start(bf16[512,1024]{1,0:T(8,128)(2,1)} %pad_maximum_fusion.9), channel_id=1, source_target_pairs={{0,4},{4,0},{8,12},{12,8},{16,20},{20,16},{24,28},{28,24},{1,5},{5... | collective-permute-start | bytes 3145736 | tf_op jit(solution)/shard_map/ppermute | solution.py:374
  197.4 42.7 %collective-permute-start.37 = (bf16[1024,512]{1,0:T(8,128)(2,1)}, bf16[1024,512]{1,0:T(8,128)(2,1)}, u32[]{:S(2)}, u32[]{:S(2)}) collective-permute-start(bf16[1024,512]{1,0:T(8,128)(2,1)} %pad_maximum_fusion.10), channel_id=1, source_target_pairs={{0,2},{1,3},{2,0},{3,1},{4,6},{5,7},{6,4},{7,5},{8,10},{9,11},{10,... | collective-permute-start | bytes 3145736 | tf_op jit(solution)/shard_map/ppermute | solution.py:378
  253.3 25.0 %collective-permute-start.41 = (bf16[1024,1024]{1,0:T(8,128)(2,1)}, bf16[1024,1024]{1,0:T(8,128)(2,1)}, u32[]{:S(2)}, u32[]{:S(2)}) collective-permute-start(bf16[1024,1024]{1,0:T(8,128)(2,1)} %convolution_convert_fusion.3), channel_id=1, source_target_pairs={{0,1},{1,0},{2,3},{3,2},{4,5},{5,4},{6,7},{7,6},{8,9},{9,8},{10,11... | collective-permute-start | bytes 6291464 | tf_op jit(solution)/shard_map/ppermute | solution.py:378
  257.0 21.3 %collective-permute-start.42 = (bf16[1024,1024]{1,0:T(8,128)(2,1)}, bf16[1024,1024]{1,0:T(8,128)(2,1)}, u32[]{:S(2)}, u32[]{:S(2)}) collective-permute-start(bf16[1024,1024]{1,0:T(8,128)(2,1)} %convolution_convert_fusion.2), channel_id=1, source_target_pairs={{0,1},{1,0},{2,3},{3,2},{4,5},{5,4},{6,7},{7,6},{8,9},{9,8},{10,11... | collective-permute-start | bytes 6291464 | tf_op jit(solution)/shard_map/ppermute | solution.py:378
  260.3 18.0 %collective-permute-start.43 = (bf16[1024,1024]{1,0:T(8,128)(2,1)}, bf16[1024,1024]{1,0:T(8,128)(2,1)}, u32[]{:S(2)}, u32[]{:S(2)}) collective-permute-start(bf16[1024,1024]{1,0:T(8,128)(2,1)} %pad_maximum_fusion.2.refs_6_), channel_id=1, source_target_pairs={{0,1},{1,0},{2,3},{3,2},{4,5},{5,4},{6,7},{7,6},{8,9},{9,8},{10,11... | collective-permute-start | bytes 6291464 | tf_op jit(solution)/shard_map/ppermute | solution.py:378
  263.2 15.1 %collective-permute-start.44 = (bf16[1024,1024]{1,0:T(8,128)(2,1)}, bf16[1024,1024]{1,0:T(8,128)(2,1)}, u32[]{:S(2)}, u32[]{:S(2)}) collective-permute-start(bf16[1024,1024]{1,0:T(8,128)(2,1)} %pad_maximum_fusion.3.refs_7_), channel_id=1, source_target_pairs={{0,1},{1,0},{2,3},{3,2},{4,5},{5,4},{6,7},{7,6},{8,9},{9,8},{10,11... | collective-permute-start | bytes 6291464 | tf_op jit(solution)/shard_map/ppermute | solution.py:378
  324.2 82.4 %collective-permute-start.45 = (bf16[1024,1024]{1,0:T(8,128)(2,1)}, bf16[1024,1024]{1,0:T(8,128)(2,1)}, u32[]{:S(2)}, u32[]{:S(2)}) collective-permute-start(bf16[1024,1024]{1,0:T(8,128)(2,1)} %convolution_convert_fusion.1), channel_id=1, source_target_pairs={{0,1},{1,0},{2,3},{3,2},{4,5},{5,4},{6,7},{7,6},{8,9},{9,8},{10,11... | collective-permute-start | bytes 6291464 | tf_op jit(solution)/shard_map/ppermute | solution.py:378
  324.3 82.3 %collective-permute-start.46 = (bf16[1024,1024]{1,0:T(8,128)(2,1)}, bf16[1024,1024]{1,0:T(8,128)(2,1)}, u32[]{:S(2)}, u32[]{:S(2)}) collective-permute-start(bf16[1024,1024]{1,0:T(8,128)(2,1)} %convolution_convert_fusion), channel_id=1, source_target_pairs={{0,1},{1,0},{2,3},{3,2},{4,5},{5,4},{6,7},{7,6},{8,9},{9,8},{10,11... | collective-permute-start | bytes 6291464 | tf_op jit(solution)/shard_map/ppermute | solution.py:378
  328.7 77.8 %collective-permute-start.47 = (bf16[512,1024]{1,0:T(8,128)(2,1)}, bf16[512,1024]{1,0:T(8,128)(2,1)S(1)}, u32[]{:S(2)}, u32[]{:S(2)}) collective-permute-start(bf16[512,1024]{1,0:T(8,128)(2,1)} %slice.430), channel_id=1, source_target_pairs={{0,4},{4,0},{8,12},{12,8},{16,20},{20,16},{24,28},{28,24},{1,5},{5... | collective-permute-start | bytes 3145736 | tf_op jit(solution)/shard_map/ppermute | solution.py:374
  330.0 27.0 %collective-permute-start.49 = (bf16[256,1024]{1,0:T(8,128)(2,1)}, bf16[256,1024]{1,0:T(8,128)(2,1)S(1)}, u32[]{:S(2)}, u32[]{:S(2)}) collective-permute-start(bf16[256,1024]{1,0:T(8,128)(2,1)} %get-tuple-element.467), channel_id=1, source_target_pairs={{0,1},{1,0},{2,3},{3,2},{4,5},{5,4},{6,7},{7,6},{8,9},{9,8},{10,11... | collective-permute-start | bytes 1572872 | tf_op jit(solution)/shard_map/ppermute | solution.py:378
  355.4 51.2 %collective-permute-start.48 = (bf16[1024,512]{1,0:T(8,128)(2,1)}, bf16[1024,512]{1,0:T(8,128)(2,1)}, u32[]{:S(2)}, u32[]{:S(2)}) collective-permute-start(bf16[1024,512]{1,0:T(8,128)(2,1)} %slice.431), channel_id=1, source_target_pairs={{0,2},{1,3},{2,0},{3,1},{4,6},{5,7},{6,4},{7,5},{8,10},{9,11},{10,... | collective-permute-start | bytes 3145736 | tf_op jit(solution)/shard_map/ppermute | solution.py:378
  357.0 35.4 %collective-permute-start.50 = (bf16[256,1024]{1,0:T(8,128)(2,1)}, bf16[256,1024]{1,0:T(8,128)(2,1)S(1)}, u32[]{:S(2)}, u32[]{:S(2)}) collective-permute-start(bf16[256,1024]{1,0:T(8,128)(2,1)} %get-tuple-element.466), channel_id=1, source_target_pairs={{0,2},{1,3},{2,0},{3,1},{4,6},{5,7},{6,4},{7,5},{8,10},{9,11},{10,... | collective-permute-start | bytes 1572872 | tf_op jit(solution)/shard_map/ppermute | solution.py:378
  392.4 14.2 %collective-permute-start.51 = (bf16[256,1024]{1,0:T(8,128)(2,1)S(1)}, bf16[256,1024]{1,0:T(8,128)(2,1)S(1)}, u32[]{:S(2)}, u32[]{:S(2)}) collective-permute-start(bf16[256,1024]{1,0:T(8,128)(2,1)S(1)} %copy-done.122), channel_id=1, source_target_pairs={{0,3},{1,2},{2,1},{3,0},{4,7},{5,6},{6,5},{7,4},{8,11},{9,10},{10,... | collective-permute-start | bytes 1572872 | tf_op jit(solution)/shard_map/ppermute | solution.py:378
  414.8 39.8 %collective-permute-start.52 = (bf16[512,1024]{1,0:T(8,128)(2,1)S(1)}, bf16[512,1024]{1,0:T(8,128)(2,1)S(1)}, u32[]{:S(2)}, u32[]{:S(2)}) collective-permute-start(bf16[512,1024]{1,0:T(8,128)(2,1)S(1)} %slice.432), channel_id=1, source_target_pairs={{0,4},{4,0},{8,12},{12,8},{16,20},{20,16},{24,28},{28,24},{1,5},{5... | collective-permute-start | bytes 3145736 | tf_op jit(solution)/shard_map/ppermute | solution.py:374
  418.3 36.2 %collective-permute-start.53 = (bf16[1024,512]{1,0:T(8,128)(2,1)S(1)}, bf16[1024,512]{1,0:T(8,128)(2,1)S(1)}, u32[]{:S(2)}, u32[]{:S(2)}) collective-permute-start(bf16[1024,512]{1,0:T(8,128)(2,1)S(1)} %slice.433), channel_id=1, source_target_pairs={{0,2},{1,3},{2,0},{3,1},{4,6},{5,7},{6,4},{7,5},{8,10},{9,11},{10,... | collective-permute-start | bytes 3145736 | tf_op jit(solution)/shard_map/ppermute | solution.py:378
  419.9 34.6 %collective-permute-start.54 = (bf16[2,1024,256]{2,1,0:T(8,128)(2,1)S(1)}, bf16[2,1024,256]{2,1,0:T(8,128)(2,1)S(1)}, u32[]{:S(2)}, u32[]{:S(2)}) collective-permute-start(bf16[2,1024,256]{2,1,0:T(8,128)(2,1)S(1)} %pad_maximum_fusion.11), channel_id=1, source_target_pairs={{0,1},{1,0},{2,3},{3,2},{4,5},{5,4},{6,7},{7,6},{8,9},{9,8},{10,11... | collective-permute-start | bytes 3145736 | tf_op jit(solution)/shard_map/ppermute | solution.py:378
  420.5 34.0 %collective-permute-start.55 = (bf16[512,512]{1,0:T(8,128)(2,1)S(1)}, bf16[512,512]{1,0:T(8,128)(2,1)S(1)}, u32[]{:S(2)}, u32[]{:S(2)}) collective-permute-start(bf16[512,512]{1,0:T(8,128)(2,1)S(1)} %slice.435), channel_id=1, source_target_pairs={{0,2},{1,3},{2,0},{3,1},{4,6},{5,7},{6,4},{7,5},{8,10},{9,11},{10,... | collective-permute-start | bytes 1572872 | tf_op jit(solution)/shard_map/ppermute | solution.py:378
  423.3 31.2 %collective-permute-start.56 = (bf16[512,512]{1,0:T(8,128)(2,1)S(1)}, bf16[512,512]{1,0:T(8,128)(2,1)S(1)}, u32[]{:S(2)}, u32[]{:S(2)}) collective-permute-start(bf16[512,512]{1,0:T(8,128)(2,1)S(1)} %slice.437), channel_id=1, source_target_pairs={{0,4},{4,0},{8,12},{12,8},{16,20},{20,16},{24,28},{28,24},{1,5},{5... | collective-permute-start | bytes 1572872 | tf_op jit(solution)/shard_map/ppermute | solution.py:374
  454.5 26.0 %collective-permute-start.57 = (bf16[1024,768]{1,0:T(8,128)(2,1)S(1)}, bf16[1024,768]{1,0:T(8,128)(2,1)S(1)}, u32[]{:S(2)}, u32[]{:S(2)}) collective-permute-start(bf16[1024,768]{1,0:T(8,128)(2,1)S(1)} %convolution_convert_fusion.7), channel_id=1, source_target_pairs={{0,1},{1,0},{2,3},{3,2},{4,5},{5,4},{6,7},{7,6},{8,9},{9,8},{10,11... | collective-permute-start | bytes 4718600 | tf_op jit(solution)/shard_map/ppermute | solution.py:378
  454.9 22.3 %collective-permute-start.58 = (bf16[2,1024,128]{2,1,0:T(8,128)(2,1)S(1)}, bf16[2,1024,128]{2,1,0:T(8,128)(2,1)S(1)}, u32[]{:S(2)}, u32[]{:S(2)}) collective-permute-start(bf16[2,1024,128]{2,1,0:T(8,128)(2,1)S(1)} %slice.438), channel_id=1, source_target_pairs={{0,2},{1,3},{2,0},{3,1},{4,6},{5,7},{6,4},{7,5},{8,10},{9,11},{10,... | collective-permute-start | bytes 1572872 | tf_op jit(solution)/shard_map/ppermute | solution.py:378
  456.8 23.7 %collective-permute-start.59 = (bf16[512,512]{1,0:T(8,128)(2,1)S(1)}, bf16[512,512]{1,0:T(8,128)(2,1)S(1)}, u32[]{:S(2)}, u32[]{:S(2)}) collective-permute-start(bf16[512,512]{1,0:T(8,128)(2,1)S(1)} %slice.440), channel_id=1, source_target_pairs={{0,2},{1,3},{2,0},{3,1},{4,6},{5,7},{6,4},{7,5},{8,10},{9,11},{10,... | collective-permute-start | bytes 1572872 | tf_op jit(solution)/shard_map/ppermute | solution.py:378
  458.0 22.5 %collective-permute-start.60 = (bf16[512,512]{1,0:T(8,128)(2,1)S(1)}, bf16[512,512]{1,0:T(8,128)(2,1)S(1)}, u32[]{:S(2)}, u32[]{:S(2)}) collective-permute-start(bf16[512,512]{1,0:T(8,128)(2,1)S(1)} %slice.442), channel_id=1, source_target_pairs={{0,4},{4,0},{8,12},{12,8},{16,20},{20,16},{24,28},{28,24},{1,5},{5... | collective-permute-start | bytes 1572872 | tf_op jit(solution)/shard_map/ppermute | solution.py:374
  480.7 22.0 %collective-permute-start.61 = (bf16[2,512,128]{2,1,0:T(8,128)(2,1)S(1)}, bf16[2,512,128]{2,1,0:T(8,128)(2,1)S(1)}, u32[]{:S(2)}, u32[]{:S(2)}) collective-permute-start(bf16[2,512,128]{2,1,0:T(8,128)(2,1)S(1)} %slice.444), channel_id=1, source_target_pairs={{0,4},{4,0},{8,12},{12,8},{16,20},{20,16},{24,28},{28,24},{1,5},{5... | collective-permute-start | bytes 786440 | tf_op jit(solution)/shard_map/ppermute | solution.py:374
  482.6 20.2 %collective-permute-start.62 = (bf16[1024,384]{1,0:T(8,128)(2,1)S(1)}, bf16[1024,384]{1,0:T(8,128)(2,1)S(1)}, u32[]{:S(2)}, u32[]{:S(2)}) collective-permute-start(bf16[1024,384]{1,0:T(8,128)(2,1)S(1)} %slice.445), channel_id=1, source_target_pairs={{0,2},{1,3},{2,0},{3,1},{4,6},{5,7},{6,4},{7,5},{8,10},{9,11},{10,... | collective-permute-start | bytes 2359304 | tf_op jit(solution)/shard_map/ppermute | solution.py:378
  503.1 48.8 %collective-permute-start.63 = (bf16[512,384]{1,0:T(8,128)(2,1)S(1)}, bf16[512,384]{1,0:T(8,128)(2,1)S(1)}, u32[]{:S(2)}, u32[]{:S(2)}) collective-permute-start(bf16[512,384]{1,0:T(8,128)(2,1)S(1)} %slice.447), channel_id=1, source_target_pairs={{0,4},{4,0},{8,12},{12,8},{16,20},{20,16},{24,28},{28,24},{1,5},{5... | collective-permute-start | bytes 1179656 | tf_op jit(solution)/shard_map/ppermute | solution.py:374
  503.9 48.0 %collective-permute-start.64 = (bf16[1024,768]{1,0:T(8,128)(2,1)S(1)}, bf16[1024,768]{1,0:T(8,128)(2,1)S(1)}, u32[]{:S(2)}, u32[]{:S(2)}) collective-permute-start(bf16[1024,768]{1,0:T(8,128)(2,1)S(1)} %convolution_convert_fusion.6), channel_id=1, source_target_pairs={{0,1},{1,0},{2,3},{3,2},{4,5},{5,4},{6,7},{7,6},{8,9},{9,8},{10,11... | collective-permute-start | bytes 4718600 | tf_op jit(solution)/shard_map/ppermute | solution.py:378
  504.2 30.3 %collective-permute-start.73 = (bf16[128,2304]{1,0:T(8,128)(2,1)S(1)}, bf16[128,2304]{1,0:T(8,128)(2,1)S(1)}, u32[]{:S(2)}, u32[]{:S(2)}) collective-permute-start(bf16[128,2304]{1,0:T(8,128)(2,1)S(1)} %get-tuple-element.460), channel_id=1, source_target_pairs={{0,8},{4,12},{8,0},{12,4},{16,24},{20,28},{24,16},{28,20},{1,9},{5... | collective-permute-start | bytes 1769480 | tf_op jit(solution)/shard_map/ppermute | solution.py:368
  508.1 42.4 %collective-permute-start.74 = (bf16[128,2304]{1,0:T(8,128)(2,1)S(1)}, bf16[128,2304]{1,0:T(8,128)(2,1)S(1)}, u32[]{:S(2)}, u32[]{:S(2)}) collective-permute-start(bf16[128,2304]{1,0:T(8,128)(2,1)S(1)} %get-tuple-element.459), channel_id=1, source_target_pairs={{0,16},{4,20},{8,24},{12,28},{16,0},{20,4},{24,8},{28,12},{1,17},{... | collective-permute-start | bytes 1769480 | tf_op jit(solution)/shard_map/ppermute | solution.py:368
  509.6 40.9 %collective-permute-start.75 = (bf16[128,2304]{1,0:T(8,128)(2,1)S(1)}, bf16[128,2304]{1,0:T(8,128)(2,1)S(1)}, u32[]{:S(2)}, u32[]{:S(2)}) collective-permute-start(bf16[128,2304]{1,0:T(8,128)(2,1)S(1)} %get-tuple-element.458), channel_id=1, source_target_pairs={{0,24},{4,28},{8,16},{12,20},{16,8},{20,12},{24,0},{28,4},{1,25},{... | collective-permute-start | bytes 1769480 | tf_op jit(solution)/shard_map/ppermute | solution.py:368
  554.8 22.7 %collective-permute-start.65 = (bf16[512,768]{1,0:T(8,128)(2,1)}, bf16[512,768]{1,0:T(8,128)(2,1)}, u32[]{:S(2)}, u32[]{:S(2)}) collective-permute-start(bf16[512,768]{1,0:T(8,128)(2,1)} %slice.448), channel_id=1, source_target_pairs={{0,4},{4,0},{8,12},{12,8},{16,20},{20,16},{24,28},{28,24},{1,5},{5... | collective-permute-start | bytes 2359304 | tf_op jit(solution)/shard_map/ppermute | solution.py:374
  593.9 14.9 %collective-permute-start.67 = (bf16[256,1024]{1,0:T(8,128)(2,1)}, bf16[256,1024]{1,0:T(8,128)(2,1)S(1)}, u32[]{:S(2)}, u32[]{:S(2)}) collective-permute-start(bf16[256,1024]{1,0:T(8,128)(2,1)} %get-tuple-element.478), channel_id=1, source_target_pairs={{0,2},{1,3},{2,0},{3,1},{4,6},{5,7},{6,4},{7,5},{8,10},{9,11},{10,... | collective-permute-start | bytes 1572872 | tf_op jit(solution)/shard_map/ppermute | solution.py:378
  594.9 24.0 %collective-permute-start.68 = (bf16[256,1024]{1,0:T(8,128)(2,1)S(1)}, bf16[256,1024]{1,0:T(8,128)(2,1)S(1)}, u32[]{:S(2)}, u32[]{:S(2)}) collective-permute-start(bf16[256,1024]{1,0:T(8,128)(2,1)S(1)} %get-tuple-element.477), channel_id=1, source_target_pairs={{0,3},{1,2},{2,1},{3,0},{4,7},{5,6},{6,5},{7,4},{8,11},{9,10},{10,... | collective-permute-start | bytes 1572872 | tf_op jit(solution)/shard_map/ppermute | solution.py:378
  595.8 24.4 %collective-permute-start.79 = (f32[4,1216]{1,0:T(4,128)S(1)}, f32[4,1216]{1,0:T(4,128)S(1)}, u32[]{:S(2)}, u32[]{:S(2)}) collective-permute-start(f32[4,1216]{1,0:T(4,128)S(1)} %slice.486), channel_id=1, source_target_pairs={{0,4},{4,0},{8,12},{12,8},{16,20},{20,16},{24,28},{28,24},{1,5},{5... | collective-permute-start | bytes 58376 | tf_op jit(solution)/shard_map/ppermute | solution.py:374
  619.8 35.3 %collective-permute-start.66 = (bf16[256,1024]{1,0:T(8,128)(2,1)}, bf16[256,1024]{1,0:T(8,128)(2,1)S(1)}, u32[]{:S(2)}, u32[]{:S(2)}) collective-permute-start(bf16[256,1024]{1,0:T(8,128)(2,1)} %slice.357), channel_id=1, source_target_pairs={{0,1},{1,0},{2,3},{3,2},{4,5},{5,4},{6,7},{7,6},{8,9},{9,8},{10,11... | collective-permute-start | bytes 1572872 | tf_op jit(solution)/shard_map/ppermute | solution.py:378
  620.3 18.8 %collective-permute-start.80 = (f32[1216]{0:T(1024)S(1)}, f32[1216]{0:T(1024)S(1)}, u32[]{:S(2)}, u32[]{:S(2)}) collective-permute-start(f32[1216]{0:T(1024)S(1)} %get-tuple-element.439), channel_id=1, source_target_pairs={{0,8},{4,12},{8,0},{12,4},{16,24},{20,28},{24,16},{28,20},{1,9},{5... | collective-permute-start | bytes 14600 | tf_op jit(solution)/shard_map/ppermute | solution.py:368
  650.6 16.5 %collective-permute-start.71 = (bf16[128,768]{1,0:T(8,128)(2,1)S(1)}, bf16[128,768]{1,0:T(8,128)(2,1)S(1)}, u32[]{:S(2)}, u32[]{:S(2)}) collective-permute-start(bf16[128,768]{1,0:T(8,128)(2,1)S(1)} %get-tuple-element.487), channel_id=1, source_target_pairs={{0,16},{4,20},{8,24},{12,28},{16,0},{20,4},{24,8},{28,12},{1,17},{... | collective-permute-start | bytes 589832 | tf_op jit(solution)/shard_map/ppermute | solution.py:368
  (159 other events, 1694.0 us)

commit v6 on v5

--- a/solution.py
+++ b/solution.py
@@ -452,9 +452,19 @@
     return total
 
 
-def mp_steps(chain, parts, first=1):
-    arrived = yield [swap_mp(part, step + first) for step, part in enumerate(parts)]
-    return arrived
+def sum_z_halves_steps(chain, total):
+    half = total.shape[0] // 2
+    (arrived,) = yield [swap_z(total[half:], 2)]
+    total = add_low(total[:half], arrived)
+    (arrived,) = yield [swap_z(total[half // 2 :], 1)]
+    return total[: half // 2].astype(F32) + arrived.astype(F32)
+
+
+def image_steps(chain, far, near):
+    (arrived,) = yield [swap_mp(far, 2)]
+    second, passing = arrived
+    (arrived,) = yield [swap_mp(jnp.stack([near(), passing]), 1)]
+    return [arrived[0], second, arrived[1]]
 
 
 def small_steps(chain, shard, vector_size):
@@ -537,9 +547,6 @@
         ),
         out_shape=[shape] * 2,
         compiler_params=pltpu.CompilerParams(vmem_limit_bytes=32 * 2**20),
-        cost_estimate=pl.CostEstimate(
-            flops=chunk_rows * width * 40, bytes_accessed=chunk_rows * width * 24, transcendentals=0
-        ),
         name="assemble_image",
     )(place, vector_full, arrays, *parts)
     return (image.reshape(-1, width), second.reshape(-1, width))
@@ -569,9 +576,6 @@
         ),
         out_shape=jax.ShapeDtypeStruct((MP, chunk_rows, width), dtype),
         compiler_params=pltpu.CompilerParams(vmem_limit_bytes=32 * 2**20),
-        cost_estimate=pl.CostEstimate(
-            flops=chunk_rows * width * 4, bytes_accessed=chunk_rows * width * 20, transcendentals=0
-        ),
         name="spread_image",
     )(place, own, *parts)
 
@@ -669,11 +673,34 @@
         out_specs=[block] * 2,
         out_shape=[jax.ShapeDtypeStruct((rows, width), BF)] * 2,
         compiler_params=pltpu.CompilerParams(vmem_limit_bytes=32 * 2**20),
-        cost_estimate=pl.CostEstimate(
-            flops=2 * rows * width * depth, bytes_accessed=rows * width * 8, transcendentals=rows * width
-        ),
         name="expand",
     )(left, right, bias.reshape(1, width))
+
+
+def slope_kernel(left_ref, right_ref, slope_ref, grad_ref, sums_ref):
+    grad = jnp.dot(left_ref[...], right_ref[...], preferred_element_type=F32)
+    low = (grad * slope_ref[...].astype(F32)).astype(BF)
+    grad_ref[...] = low
+    add_rows(sums_ref, [low.astype(F32)])
+
+
+def slope_product(left, right, slope):
+    rows, depth = left.shape
+    width = right.shape[1]
+    block = pl.BlockSpec((256, width), lambda i: (i, 0))
+    return pl.pallas_call(
+        slope_kernel,
+        grid=(rows // 256,),
+        in_specs=[
+            pl.BlockSpec((256, depth), lambda i: (i, 0)),
+            pl.BlockSpec((depth, width), lambda i: (0, 0), pipeline_mode=pl.Buffered(1)),
+            block,
+        ],
+        out_specs=[block, pl.BlockSpec((8, width), lambda i: (0, 0))],
+        out_shape=[jax.ShapeDtypeStruct((rows, width), BF), jax.ShapeDtypeStruct((8, width), F32)],
+        compiler_params=pltpu.CompilerParams(vmem_limit_bytes=32 * 2**20),
+        name="slope_product",
+    )(left, right, slope)
 
 
 def row_call(kernel, name, lefts, rights, vector_full, row_inputs, outs, span=None, own_rows=0):
@@ -694,7 +721,6 @@
         specs[each] if isinstance(each, str) else (block, jax.ShapeDtypeStruct((rows, width), each))
         for each in outs
     ]
-    depth = sum(each.shape[1] for each in lefts)
     return pl.pallas_call(
         functools.partial(kernel, len(lefts)),
         grid=(count,),
@@ -705,11 +731,6 @@
         out_specs=[each[0] for each in pairs],
         out_shape=[each[1] for each in pairs],
         compiler_params=pltpu.CompilerParams(vmem_limit_bytes=48 * 2**20),
-        cost_estimate=None
-        if span
-        else pl.CostEstimate(
-            flops=2 * rows * width * depth, bytes_accessed=rows * width * 24, transcendentals=0
-        ),
         name=name,
     )(*lefts, *rights, vector_full, *row_inputs)
 
@@ -794,7 +815,6 @@
 def attend(heads):
     rows, width = heads.shape
     pairs = width // LANES // 3
-    scores_size = rows * rows * 2 * pairs
     return pl.pallas_call(
         functools.partial(attend_kernel, 256),
         grid=(pairs,),
@@ -808,9 +828,6 @@
             jax.ShapeDtypeStruct((pairs, 8, rows), F32),
         ],
         compiler_params=pltpu.CompilerParams(vmem_limit_bytes=32 * 2**20),
-        cost_estimate=pl.CostEstimate(
-            flops=scores_size * 2 * 512, bytes_accessed=rows * width * 8, transcendentals=scores_size
-        ),
         name="attend",
     )(heads, heads, heads)
 
@@ -818,7 +835,6 @@
 def attend_back(heads, grad_blended, log_total):
     rows, width = heads.shape
     pairs = width // LANES // 3
-    scores_size = rows * rows * 2 * pairs
     return pl.pallas_call(
         functools.partial(attend_back_kernel, 256),
         grid=(pairs,),
@@ -831,9 +847,6 @@
         out_shape=jax.ShapeDtypeStruct((rows, width), BF),
         scratch_shapes=[pltpu.VMEM((rows, LANES), F32)] * 2,
         compiler_params=pltpu.CompilerParams(vmem_limit_bytes=32 * 2**20),
-        cost_estimate=pl.CostEstimate(
-            flops=scores_size * 2 * 1280, bytes_accessed=rows * width * 14, transcendentals=scores_size
-        ),
         name="attend_back",
     )(heads, heads, heads, grad_blended, log_total)
 
@@ -886,19 +899,15 @@
 
     def fetch_image(array):
         chunks = array[:, 0]
-        return Chain(
-            mp_steps,
-            [
-                lax.dynamic_index_in_dim(chunks, mp_at ^ step, 0, keepdims=False)
-                for step in range(1, MP)
-            ],
-        )
-
-    def send_back(array):
-        low = array.astype(BF)
-        return Chain(
-            mp_steps, [low[step * chunk_rows : (step + 1) * chunk_rows] for step in range(1, MP)]
-        )
+
+        def chunk(step):
+            return lax.dynamic_index_in_dim(chunks, mp_at ^ step, 0, keepdims=False)
+
+        return Chain(image_steps, jnp.stack([chunk(2), chunk(3)]), lambda: chunk(1))
+
+    def send_back(low):
+        chunks = low.reshape(MP, chunk_rows, width)
+        return Chain(image_steps, chunks[2:], lambda: chunks[1])
 
     small_shard = jnp.concatenate(
         [vectors.astype(BF).reshape(-1), head_biases.astype(BF).reshape(-1)]
@@ -924,7 +933,8 @@
     rest_shard = meet(rest_shard, small, rows_qkv[1])
     get_qkv[1] = Chain(gather_steps, [rows_qkv[1].result], ("xy",))
     rows_rest = Chain(rows_z_steps, rest_shard)
-    tokens = meet(tokens, small, get_qkv[0], fetch_tokens)
+    meet((), small, get_qkv[0], fetch_tokens)
+    tokens = meet(tokens, fetch_tokens)
 
     vector_full, bias_small = small.result
     vector_full = vector_full.reshape(DP, vectors.shape[0], LANES).transpose(1, 0, 2)
@@ -971,7 +981,7 @@
     fetch_cotangent = fetch_image(cotangent)
     heads[1][1] = project(1, 1, w_qkv[1][1])
     forward_heads(1, 1)
-    blended = meet(blended, get_up, get_out, get_down)
+    blended = meet(blended, get_up, get_out, get_down, fetch_cotangent)
     w_up = [get_up.own, get_up.result]
     w_out = [[each[0][half] for half in (0, 1)] for each in (get_out.own, get_out.result)]
     pairs = [(core, half) for core in cores for half in (0, 1)]
@@ -991,8 +1001,8 @@
         unit_bias = rows.transpose(1, 0, 2).reshape(-1)
         activ[half, core], slope[half, core] = expand(normed_two, w_up[core][half], unit_bias)
         if (half, core) == (0, 0):
-            activ, normed_two = meet((activ, normed_two), get_down)
-    activ, slope, cotangent = meet((activ, slope, cotangent), fetch_cotangent)
+            activ, normed_two, cotangent = meet((activ, normed_two, cotangent), get_down, fetch_cotangent)
+    activ, slope = meet((activ, slope))
     grad_out, grad_branch = assemble_image(
         place, vector_full, cotangent[:, 0], fetch_cotangent.result, False
     )
@@ -1016,11 +1026,12 @@
     )
     output, grad_branch, slope = meet((output, grad_branch, slope))
     send_output = send_back(output)
-    grad_pre = {}
+    grad_pre, unit_sums = ({}, {})
     for half, core in parts:
-        grad_activ = dot_nn(grad_branch, w_down[core][half])
-        grad_pre[half, core] = (grad_activ * slope[half, core].astype(F32)).astype(BF)
-    grad_pre, normed_two = meet((grad_pre, normed_two))
+        grad_pre[half, core], unit_sums[half, core] = slope_product(
+            grad_branch, w_down[core][half], slope[half, core]
+        )
+    grad_pre, normed_two = meet((grad_pre, normed_two), sum_down)
     sum_up = reduce_pairs(normed_two, grad_pre)
     grad_hidden, grad_projected, sums_one = row_call(
         up_back_kernel,
@@ -1032,6 +1043,7 @@
         [F32, BF, "sums"],
     )
     grad_projected = meet(grad_projected, sum_up, sum_down, send_output)
+    rows_down = Chain(sum_z_halves_steps, jnp.concatenate(sum_down.result, 1))
     grad_w_out = [
         jnp.stack([dot_tn(grad_projected, each).astype(BF) for each in blended[core]]) for core in cores
     ]
@@ -1047,17 +1059,19 @@
         return dot_tn(normed_one, grad_heads[core][half]).astype(BF)
 
     other = back_heads(1, 0)
-    other, grad_blended = meet((other, grad_blended), sum_up, sum_out, sum_down)
+    other, grad_blended = meet((other, grad_blended), sum_up, sum_out, rows_down, send_output)
     sum_qkv = [Chain(reduce_steps, [other], ("xy",)), None]
     sum_qkv[0].own = [back_heads(0, 0)]
-    grad_heads[0][0], grad_blended = meet((grad_heads[0][0], grad_blended), sum_qkv[0], sum_out, sum_up)
+    grad_heads[0][0], grad_blended = meet(
+        (grad_heads[0][0], grad_blended), sum_qkv[0], sum_out, sum_up, rows_down
+    )
+    rows_up = Chain(sum_z_halves_steps, jnp.concatenate(sum_up.result, 1))
     other = back_heads(1, 1)
     other, grad_blended = meet((other, grad_blended), sum_out, sum_qkv[0])
     sum_qkv[1] = Chain(reduce_steps, [other], ("yx",))
     out_rows = jnp.concatenate([sum_out.result[0][0], sum_out.result[0][1]], 1)
-    rows_rest = Chain(sum_z_steps, jnp.concatenate(sum_up.result + sum_down.result + [out_rows], 1))
     sum_qkv[1].own = [back_heads(0, 1)]
-    grad_heads = meet(grad_heads, sum_qkv[0], sum_qkv[1])
+    grad_heads = meet(grad_heads, sum_qkv[0], sum_qkv[1], rows_up)
 
     def input_back(span, outs):
         return row_call(
@@ -1073,10 +1087,13 @@
         )
 
     grad_far, sums_far = input_back((1, 1), [BF, "sums"])
-    send_far = Chain(mp_steps, [grad_far[:chunk_rows], grad_far[chunk_rows:]], 2)
+    grad_near = []
+    send_grad = Chain(
+        image_steps, grad_far.reshape(2, chunk_rows, width), lambda: grad_near[0][chunk_rows:]
+    )
     grad_heads = meet(grad_heads, sum_qkv[1])
-    grad_near, sums_near, own_grad = input_back((0, 1), [BF, "sums", "own"])
-    send_near = Chain(mp_steps, [grad_near[chunk_rows:]], 1)
+    near, sums_near, own_grad = input_back((0, 1), [BF, "sums", "own"])
+    grad_near.append(near)
     sums_input = sums_far + sums_near
 
     grad_vectors = jnp.stack(
@@ -1099,36 +1116,33 @@
         ]
         rows = [jnp.concatenate([each[:, kind] for each in head_part], 1) for kind in (0, 2)]
         for half in (0, 1):
-            unit_part = jnp.sum(grad_pre[half, core].astype(F32), 0)
-            unit_part = unit_part.reshape(2, half_units, block_width)
+            unit_part = unit_sums[half, core][0].reshape(2, half_units, block_width)
             rows += [unit_part[:, at] for at in range(half_units)]
         bias_parts.append(jnp.stack(rows, 1))
     grad_biases = jnp.stack(bias_parts, 1).reshape(MP, -1, DP, bias_width).transpose(0, 2, 1, 3)
     grad_biases = jnp.take(grad_biases, place[:DP], axis=1).reshape(MP, DP, -1)
     sum_small = Chain(small_reduce_steps, grad_vectors, grad_biases)
     meet((), sum_qkv[1])
-    rows_qkv = Chain(sum_z_steps, jnp.concatenate(sum_qkv[0].result + sum_qkv[1].result, 1))
-    meet((), send_far)
-    meet((), rows_rest)
+    rows_qkv = Chain(sum_z_steps, jnp.concatenate(sum_qkv[0].result + sum_qkv[1].result + [out_rows], 1))
+    meet((), rows_up)
+    meet((), send_grad)
+    meet((), send_grad)
     meet((), rows_qkv)
-    meet((), send_near)
     for _ in range(3):
         meet((), sum_small)
     layer_output = spread_image(place, output[:chunk_rows], send_output.result, BF)[:, None]
-    input_grad = spread_image(place, own_grad, send_near.result + send_far.result, F32)[:, None]
+    input_grad = spread_image(place, own_grad, send_grad.result, F32)[:, None]
 
     small_total = sum_small.result
     vector_grad = small_total[:vector_size].reshape(vectors.shape)
     bias_grad = small_total[vector_size:].reshape(head_biases.shape)
-    qkv_grad = rows_qkv.result.reshape(depth, 2, kinds, LANES).transpose(2, 0, 1, 3)
-    up_size = block_width * units
-    up_grad = rows_rest.result[:, :up_size].reshape(depth, units, block_width)
-    down_grad = rows_rest.result[:, up_size : 2 * up_size].reshape(depth, units, block_width).transpose(1, 2, 0)
+    qkv_size = kinds * block_width
+    qkv_grad = rows_qkv.result[:, :qkv_size].reshape(depth, 2, kinds, LANES).transpose(2, 0, 1, 3)
     grads = (
         qkv_grad.reshape(qkv_weight.shape),
-        rows_rest.result[:, 2 * up_size :].T,
-        up_grad,
-        down_grad,
+        rows_qkv.result[:, qkv_size:].T,
+        rows_up.result.reshape(depth, units, block_width),
+        rows_down.result.reshape(depth, units, block_width).transpose(1, 2, 0),
         bias_grad,
         vector_grad,
     )

time: 676 us -> 637 us (0.942)
  waiting for transfers between devices: 176 us -> 118 us
  Pallas kernels: 195 us -> 213 us
  local copies, waits for them, and re-layouts: 72.3 us -> 89.4 us
  starting transfers between devices: 93.7 us -> 77.8 us
  matrix products: 72 us -> 57.9 us
  other arithmetic: 58.1 us -> 71.7 us
    ppermute x46 -> x42, waiting for transfers between devices: 126 us -> 77.1 us  [swap_mp(): return lax.ppermute(part, 'mp', [(each, each ^ step) for each in range(MP)])]
    pallas_call x0 -> x4, Pallas kernels: none -> 14.7 us  [slope_product(): pl.pallas_call(slope_kernel, grid=(rows // 256,), in_specs=[pl.BlockSpec(...]
    ppermute x21 -> x22, waiting for transfers between devices: 36.5 us -> 24.4 us  [swap_z(): lax.ppermute(part, 'dp', [(z * YS + y, (z ^ step) * YS + y) for z in rang...]
    dot_general x12 -> x8, matrix products: 31.1 us -> 22.4 us  [dot_nn(): lax.dot_general(left, right, (((1,), (0,)), ((), ())), preferred_element_...]
    ppermute x21 -> x22, starting transfers between devices: 45.5 us -> 36.9 us  [swap_z(): lax.ppermute(part, 'dp', [(z * YS + y, (z ^ step) * YS + y) for z in rang...]
    ppermute x46 -> x42, starting transfers between devices: 28.7 us -> 23.9 us  [swap_mp(): return lax.ppermute(part, 'mp', [(each, each ^ step) for each in range(MP)])]
    unnamed x310 -> x335, local copies, waits for them, and re-layouts: 47.9 us -> 49.2 us
    convert_element_type x17 -> x23, other arithmetic: 18.5 us -> 19.6 us  [add_low(): return (first.astype(F32) + second.astype(F32)).astype(BF)]
  transfers between devices with their start and end apart: 83 -> 80, of which waited for: 24 -> 22; matrix products, arithmetic and copies ran while one was open for 18% -> 26% of each run, Pallas kernels for 25% -> 32%
where the time goes in v6:
time: 637 us; the launch traced here: 631 us
  Pallas kernels  213 us (33%)
  waiting for transfers between devices  118 us (19%)
  local copies, waits for them, and re-layouts  89.4 us (14%)
  starting transfers between devices  77.8 us (12%)
  other arithmetic  71.7 us (11%)
  matrix products  57.9 us (9%)
    ppermute x42, waiting for transfers between devices, swap_mp(): return lax.ppermute(part, 'mp', [(each, each ^ step) for each in range(MP)])  77.1 us
    pallas_call x4, Pallas kernels, attend_back(): pl.pallas_call(functools.partial(attend_back_kernel, 256), grid=(pairs,),...  63.5 us
    pallas_call x5, Pallas kernels, row_call(): pl.pallas_call(functools.partial(kernel, len(lefts)), grid=(count,), in_s...  61.3 us
    unnamed x335, local copies, waits for them, and re-layouts  49.2 us
    ppermute x22, starting transfers between devices, swap_z(): lax.ppermute(part, 'dp', [(z * YS + y, (z ^ step) * YS + y) for z in rang...  36.9 us
    pallas_call x4, Pallas kernels, attend(): pl.pallas_call(functools.partial(attend_kernel, 256), grid=(pairs,), in_s...  36 us
    dot_general x16, matrix products, dot_tn(): lax.dot_general(left, right, (((0,), (0,)), ((), ())), preferred_element_...  35.5 us
    pallas_call x4, Pallas kernels, expand(): pl.pallas_call(expand_kernel, grid=(rows // 256,), in_specs=[pl.BlockSpec...  25.7 us
  transfers between devices with their start and end apart: 80, of which 22 were waited for; matrix products, arithmetic and copies ran while one was open for 26% of the time, Pallas kernels for 32%

profile of v6, /device:TPU:0, one launch (start us, length us, event | category | flops | bytes accessed | tf_op | source)
XLA Modules:
  0.0 631.0 jit_solution(11779469695769313255)
XLA Ops:
  2.9 3.1 collective-permute-start
  6.0 2.6 collective-permute-start.1
  18.1 18.6 %collective-permute-done.4 = bf16[1,192]{1,0:T(2,128)(2,1)S(1)} collective-permute-done((bf16[1,192]{1,0:T(2,128)(2,1)S(1)}, bf16[1,192]{1,0:T(2,128)(2,1)S(1)}, u32[]{:S(2)}, u32[]{:S(2)}) %collective-permute-start.4) | collective-permute-done | bytes 416 | tf_op jit(solution)/shard_map/ppermute | solution.py:378
  40.6 3.5 collective-permute-start.10
  45.9 3.8 collective-permute-start.7
  49.7 2.4 collective-permute-done.10
  52.0 2.3 collective-permute-start.8
  59.8 4.0 collective-permute-done.12
  79.7 2.9 collective-permute-start.22
  83.8 3.2 assemble_image.2
  87.1 15.2 %collective-permute-done.17 = bf16[512,384]{1,0:T(8,128)(2,1)S(1)} collective-permute-done((bf16[512,384]{1,0:T(8,128)(2,1)}, bf16[512,384]{1,0:T(8,128)(2,1)S(1)}, u32[]{:S(2)}, u32[]{:S(2)}) %collective-permute-start.17) | collective-permute-done | bytes 393248 | tf_op jit(solution)/shard_map/ppermute | solution.py:378
  103.9 2.4 constant_dynamic-update-slice_fusion.8
  109.9 3.8 add_convert_fusion.9.q_ref.k_ref.v_ref
  113.7 8.8 %attend.4 = (bf16[1024,256]{1,0:T(8,128)(2,1)S(1)}, f32[2,8,1024]{2,1,0:T(8,128)S(1)}) custom-call(bf16[1024,768]{1,0:T(8,128)(2,1)S(1)} %add_convert_fusion.9.q_ref.k_ref.v_ref, bf16[1024,768]{1,0:T(8,128)(2,1)S(1)} %add_convert_fusion.9.q_ref.k_ref.v_ref, bf16[1024,768]{1,0:T(8,128)(2,1)S(1)} %add_convert_fusion.9.q_ref.k_ref.v_ref), custom_call_target="tpu_custom_call" | custom-call | tf_op jit(solution)/shard_map/attend/pallas_call | solution.py:818
  122.6 5.4 collective-permute-done.19
  136.0 2.9 add_convert_fusion.8.q_ref.k_ref.v_ref
  140.1 9.3 %attend.5 = (bf16[1024,256]{1,0:T(8,128)(2,1)S(1)}, f32[2,8,1024]{2,1,0:T(8,128)S(1)}) custom-call(bf16[1024,768]{1,0:T(8,128)(2,1)S(1)} %add_convert_fusion.8.q_ref.k_ref.v_ref, bf16[1024,768]{1,0:T(8,128)(2,1)S(1)} %add_convert_fusion.8.q_ref.k_ref.v_ref, bf16[1024,768]{1,0:T(8,128)(2,1)S(1)} %add_convert_fusion.8.q_ref.k_ref.v_ref), custom_call_target="tpu_custom_call" | custom-call | tf_op jit(solution)/shard_map/attend/pallas_call | solution.py:818
  149.5 3.6 collective-permute-done.26
  159.8 3.8 add_convert_fusion.7.q_ref.k_ref.v_ref
  163.7 9.0 %attend.6 = (bf16[1024,256]{1,0:T(8,128)(2,1)S(1)}, f32[2,8,1024]{2,1,0:T(8,128)S(1)}) custom-call(bf16[1024,768]{1,0:T(8,128)(2,1)S(1)} %add_convert_fusion.7.q_ref.k_ref.v_ref, bf16[1024,768]{1,0:T(8,128)(2,1)S(1)} %add_convert_fusion.7.q_ref.k_ref.v_ref, bf16[1024,768]{1,0:T(8,128)(2,1)S(1)} %add_convert_fusion.7.q_ref.k_ref.v_ref), custom_call_target="tpu_custom_call" | custom-call | tf_op jit(solution)/shard_map/attend/pallas_call | solution.py:818
  172.7 19.8 %collective-permute-done.29 = bf16[2,1024,128]{2,1,0:T(8,128)(2,1)} collective-permute-done((bf16[2,1024,128]{2,1,0:T(8,128)(2,1)}, bf16[2,1024,128]{2,1,0:T(8,128)(2,1)}, u32[]{:S(2)}, u32[]{:S(2)}) %collective-permute-start.29) | collective-permute-done | bytes 524320 | tf_op jit(solution)/shard_map/ppermute | solution.py:378
  192.6 2.9 pad_maximum_fusion.right_ref.refs_6_
  195.5 2.9 pad_maximum_fusion.1.right_ref.refs_7_
  205.9 8.6 %collective-permute-done.33 = bf16[512,512]{1,0:T(8,128)(2,1)S(1)} collective-permute-done((bf16[512,512]{1,0:T(8,128)(2,1)S(1)}, bf16[512,512]{1,0:T(8,128)(2,1)S(1)}, u32[]{:S(2)}, u32[]{:S(2)}) %collective-permute-start.33) | collective-permute-done | bytes 524320 | tf_op jit(solution)/shard_map/ppermute | solution.py:378
  215.8 3.8 add_convert_fusion.6.q_ref.k_ref.v_ref
  219.7 8.8 %attend.7 = (bf16[1024,256]{1,0:T(8,128)(2,1)S(1)}, f32[2,8,1024]{2,1,0:T(8,128)S(1)}) custom-call(bf16[1024,768]{1,0:T(8,128)(2,1)S(1)} %add_convert_fusion.6.q_ref.k_ref.v_ref, bf16[1024,768]{1,0:T(8,128)(2,1)S(1)} %add_convert_fusion.6.q_ref.k_ref.v_ref, bf16[1024,768]{1,0:T(8,128)(2,1)S(1)} %add_convert_fusion.6.q_ref.k_ref.v_ref), custom_call_target="tpu_custom_call" | custom-call | tf_op jit(solution)/shard_map/attend/pallas_call | solution.py:818
  228.5 7.6 %collective-permute-done.35 = bf16[2,256,1024]{2,1,0:T(8,128)(2,1)} collective-permute-done((bf16[2,256,1024]{2,1,0:T(8,128)(2,1)}, bf16[2,256,1024]{2,1,0:T(8,128)(2,1)}, u32[]{:S(2)}, u32[]{:S(2)}) %collective-permute-start.35) | collective-permute-done | bytes 1048608 | tf_op jit(solution)/shard_map/ppermute | solution.py:378
  246.5 6.9 %out_norm.1 = (f32[1024,1024]{1,0:T(8,128)}, f32[1024,1024]{1,0:T(8,128)}, bf16[1024,1024]{1,0:T(8,128)(2,1)}) custom-call(bf16[1024,256]{1,0:T(8,128)(2,1)S(1)} %copy-done.51, bf16[1024,256]{1,0:T(8,128)(2,1)S(1)} %copy-done.54, bf16[1024,256]{1,0:T(8,128)(2,1)S(1)} %copy-done.57, bf16[1024,256]{1,0:T(8,128)(2,1)S(1)} %copy-done.60, ...), custom_call_target="tpu_custom_call" | custom-call | tf_op jit(solution)/shard_map/out_norm/pallas_call | solution.py:724
  255.0 6.0 expand.4
  262.3 6.8 %expand.5 = (bf16[1024,1024]{1,0:T(8,128)(2,1)S(1)}, bf16[1024,1024]{1,0:T(8,128)(2,1)S(1)}) custom-call(bf16[1024,1024]{1,0:T(8,128)(2,1)S(1)} %copy-done.6, bf16[1024,1024]{1,0:T(8,128)(2,1)} %collective-permute-done.30.right_ref.refs_4_, f32[1,1024]{1,0:T(1,128)S(1)} %reshape_reshape.13.bias_ref), custom_call_target="tpu_custom_call" | custom-call | tf_op jit(solution)/shard_map/expand/pallas_call | solution.py:665
  270.3 6.8 %expand.6 = (bf16[1024,1024]{1,0:T(8,128)(2,1)S(1)}, bf16[1024,1024]{1,0:T(8,128)(2,1)S(1)}) custom-call(bf16[1024,1024]{1,0:T(8,128)(2,1)S(1)} %copy-done.6, bf16[1024,1024]{1,0:T(8,128)(2,1)} %collective-permute-done.31.right_ref.refs_5_, f32[1,1024]{1,0:T(1,128)S(1)} %reshape_reshape.14.bias_ref), custom_call_target="tpu_custom_call" | custom-call | tf_op jit(solution)/shard_map/expand/pallas_call | solution.py:665
  280.6 6.2 expand.7
  290.4 2.4 convolution_convert_fusion.3
  293.4 2.4 convolution_convert_fusion.2
  300.4 2.4 fusion.36
  302.9 2.4 fusion.37
  323.3 16.2 %down_output.1 = (bf16[1024,1024]{1,0:T(8,128)(2,1)S(1)}, f32[8,1024]{1,0:T(8,128)S(1)}) custom-call(bf16[1024,1024]{1,0:T(8,128)(2,1)S(1)} %copy-done.41, bf16[1024,1024]{1,0:T(8,128)(2,1)} %copy-done.44, bf16[1024,1024]{1,0:T(8,128)(2,1)} %copy-done.39, bf16[1024,1024]{1,0:T(8,128)(2,1)} %copy-done.49, bf16[1024,1024]{1,0:T(8,128)(2,1)} %copy-done.20, ...), custom_call_target="tpu_custom_call" | custom-call | tf_op jit(solution)/shard_map/down_output/pallas_call | solution.py:724
  342.4 3.2 slope_product.4
  346.9 3.2 slope_product.5
  351.5 3.2 slope_product.6
  356.7 5.0 slope_product.7
  367.3 5.4 convolution_convert_fusion.1
  372.8 3.8 convolution_convert_fusion
  384.4 20.4 %up_norm_back.1 = (f32[1024,1024]{1,0:T(8,128)}, bf16[1024,1024]{1,0:T(8,128)(2,1)S(1)}, f32[8,1024]{1,0:T(8,128)S(1)}) custom-call(bf16[1024,1024]{1,0:T(8,128)(2,1)S(1)} %copy-done.46, bf16[1024,1024]{1,0:T(8,128)(2,1)} %copy-done.47, bf16[1024,1024]{1,0:T(8,128)(2,1)} %copy-done.37, bf16[1024,1024]{1,0:T(8,128)(2,1)} %copy-done.42, ...), custom_call_target="tpu_custom_call" | custom-call | tf_op jit(solution)/shard_map/up_norm_back/pallas_call | solution.py:724
  404.8 2.4 fusion.38
  407.2 2.4 fusion.39
  413.4 2.5 convolution_convert_fusion.13.g_ref
  419.6 2.5 add_convert_fusion.1
  423.8 2.6 add_convert_fusion
  429.0 3.9 collective-permute-start.53
  436.8 15.9 %attend_back.4.refs_2_ = bf16[1024,768]{1,0:T(8,128)(2,1)S(1)} custom-call(bf16[1024,768]{1,0:T(8,128)(2,1)S(1)} %copy-done.3, bf16[1024,768]{1,0:T(8,128)(2,1)S(1)} %copy-done.3, bf16[1024,768]{1,0:T(8,128)(2,1)S(1)} %copy-done.3, bf16[1024,256]{1,0:T(8,128)(2,1)S(1)} %convolution_convert_fusion.15.g_ref, f32[2,8,1024]{2,1,0:T(8,128)S(1)} %get-tuple-element.315.lse_ref), custom_call_target="tpu_custom_call" | custom-call | tf_op jit(solution)/shard_map/attend_back/pallas_call | solution.py:838
  461.1 15.7 %attend_back.5.refs_0_ = bf16[1024,768]{1,0:T(8,128)(2,1)S(1)} custom-call(bf16[1024,768]{1,0:T(8,128)(2,1)S(1)} %add_convert_fusion.9.q_ref.k_ref.v_ref, bf16[1024,768]{1,0:T(8,128)(2,1)S(1)} %add_convert_fusion.9.q_ref.k_ref.v_ref, bf16[1024,768]{1,0:T(8,128)(2,1)S(1)} %add_convert_fusion.9.q_ref.k_ref.v_ref, ...), custom_call_target="tpu_custom_call" | custom-call | tf_op jit(solution)/shard_map/attend_back/pallas_call | solution.py:838
  476.9 3.0 spread_image.2
  485.3 15.9 %attend_back.6.refs_3_ = bf16[1024,768]{1,0:T(8,128)(2,1)S(1)} custom-call(bf16[1024,768]{1,0:T(8,128)(2,1)S(1)} %copy-done.1, bf16[1024,768]{1,0:T(8,128)(2,1)S(1)} %copy-done.1, bf16[1024,768]{1,0:T(8,128)(2,1)S(1)} %copy-done.1, bf16[1024,256]{1,0:T(8,128)(2,1)S(1)} %convolution_convert_fusion.12.g_ref, f32[2,8,1024]{2,1,0:T(8,128)S(1)} %get-tuple-element.333.lse_ref), custom_call_target="tpu_custom_call" | custom-call | tf_op jit(solution)/shard_map/attend_back/pallas_call | solution.py:838
  501.2 3.0 convolution_convert_fusion.6
  510.5 3.0 multiply_subtract_fusion
  514.8 15.9 %attend_back.7.refs_1_ = bf16[1024,768]{1,0:T(8,128)(2,1)S(1)} custom-call(bf16[1024,768]{1,0:T(8,128)(2,1)S(1)} %add_convert_fusion.8.q_ref.k_ref.v_ref, bf16[1024,768]{1,0:T(8,128)(2,1)S(1)} %add_convert_fusion.8.q_ref.k_ref.v_ref, bf16[1024,768]{1,0:T(8,128)(2,1)S(1)} %add_convert_fusion.8.q_ref.k_ref.v_ref, bf16[1024,256]{1,0:T(8,128)(2,1)S(1)} %copy-done.62, ...), custom_call_target="tpu_custom_call" | custom-call | tf_op jit(solution)/shard_map/attend_back/pallas_call | solution.py:838
  539.1 9.3 %in_norm_back.3 = (bf16[512,1024]{1,0:T(8,128)(2,1)}, f32[8,1024]{1,0:T(8,128)S(1)}) custom-call(bf16[1024,768]{1,0:T(8,128)(2,1)S(1)} %copy-done.11, bf16[1024,768]{1,0:T(8,128)(2,1)S(1)} %attend_back.7.refs_1_, bf16[1024,768]{1,0:T(8,128)(2,1)S(1)} %copy-done.9, bf16[1024,768]{1,0:T(8,128)(2,1)} %copy-done.12, bf16[1024,768]{1,0:T(8,128)(2,1)} %copy-done.71, ...), custom_call_target="tpu_custom_call" | custom-call | tf_op jit(solution)/shard_map/in_norm_back/pallas_call | solution.py:724
  557.5 8.6 %in_norm_back.2 = (bf16[512,1024]{1,0:T(8,128)(2,1)S(1)}, f32[8,1024]{1,0:T(8,128)S(1)}, f32[256,1024]{1,0:T(8,128)S(1)}) custom-call(bf16[1024,768]{1,0:T(8,128)(2,1)S(1)} %copy-done.11, bf16[1024,768]{1,0:T(8,128)(2,1)S(1)} %copy-done.14, bf16[1024,768]{1,0:T(8,128)(2,1)} %copy-done.8, bf16[1024,768]{1,0:T(8,128)(2,1)} %copy-done.12, ...), custom_call_target="tpu_custom_call" | custom-call | tf_op jit(solution)/shard_map/in_norm_back/pallas_call | solution.py:724
  570.7 3.5 multiply_subtract_fusion.1
  589.2 3.1 collective-permute-done.68
  599.3 5.4 collective-permute-done.69
  604.7 10.1 %collective-permute-done.70 = bf16[128,1024]{1,0:T(8,128)(2,1)} collective-permute-done((bf16[128,1024]{1,0:T(8,128)(2,1)}, bf16[128,1024]{1,0:T(8,128)(2,1)}, u32[]{:S(2)}, u32[]{:S(2)}) %collective-permute-start.70) | collective-permute-done | bytes 262176 | tf_op jit(solution)/shard_map/ppermute | solution.py:368
  627.6 3.1 spread_image.3
  (690 shorter events, 227.5 us)
Async XLA Ops:
  2.9 37.7 %collective-permute-start = (bf16[128,384]{1,0:T(8,128)(2,1)S(1)}, bf16[128,384]{1,0:T(8,128)(2,1)}, u32[]{:S(2)}, u32[]{:S(2)}) collective-permute-start(bf16[128,384]{1,0:T(8,128)(2,1)S(1)} %copy.174), channel_id=1, source_target_pairs={{0,8},{4,12},{8,0},{12,4},{16,24},{20,28},{24,16},{28,20},{1,9},{5... | collective-permute-start | bytes 294920 | tf_op jit(solution)/shard_map/ppermute | solution.py:368
  6.0 38.1 %collective-permute-start.1 = (bf16[128,384]{1,0:T(8,128)(2,1)S(1)}, bf16[128,384]{1,0:T(8,128)(2,1)}, u32[]{:S(2)}, u32[]{:S(2)}) collective-permute-start(bf16[128,384]{1,0:T(8,128)(2,1)S(1)} %copy.174), channel_id=1, source_target_pairs={{0,16},{4,20},{8,24},{12,28},{16,0},{20,4},{24,8},{28,12},{1,17},{... | collective-permute-start | bytes 294920 | tf_op jit(solution)/shard_map/ppermute | solution.py:368
  8.6 35.5 %collective-permute-start.2 = (bf16[128,384]{1,0:T(8,128)(2,1)S(1)}, bf16[128,384]{1,0:T(8,128)(2,1)}, u32[]{:S(2)}, u32[]{:S(2)}) collective-permute-start(bf16[128,384]{1,0:T(8,128)(2,1)S(1)} %copy.174), channel_id=1, source_target_pairs={{0,24},{4,28},{8,16},{12,20},{16,8},{20,12},{24,0},{28,4},{1,25},{... | collective-permute-start | bytes 294920 | tf_op jit(solution)/shard_map/ppermute | solution.py:368
  10.8 53.7 %collective-permute-start.14 = (bf16[2,256,1024]{2,1,0:T(8,128)(2,1)}, bf16[2,256,1024]{2,1,0:T(8,128)(2,1)}, u32[]{:S(2)}, u32[]{:S(2)}) collective-permute-start(bf16[2,256,1024]{2,1,0:T(8,128)(2,1)} %pad_maximum_fusion.6), channel_id=1, source_target_pairs={{0,2},{1,3},{2,0},{3,1},{4,6},{5,7},{6,4},{7,5},{8,10},{9,11},{10,... | collective-permute-start | bytes 3145736 | tf_op jit(solution)/shard_map/ppermute | solution.py:378
  17.6 19.1 %collective-permute-start.4 = (bf16[1,192]{1,0:T(2,128)(2,1)S(1)}, bf16[1,192]{1,0:T(2,128)(2,1)S(1)}, u32[]{:S(2)}, u32[]{:S(2)}) collective-permute-start(bf16[1,192]{1,0:T(2,128)(2,1)S(1)} %slice.469), channel_id=1, source_target_pairs={{0,2},{1,3},{2,0},{3,1},{4,6},{5,7},{6,4},{7,5},{8,10},{9,11},{10,... | collective-permute-start | bytes 1160 | tf_op jit(solution)/shard_map/ppermute | solution.py:378
  40.6 11.5 %collective-permute-start.10 = (bf16[128,384]{1,0:T(8,128)(2,1)S(1)}, bf16[128,384]{1,0:T(8,128)(2,1)S(1)}, u32[]{:S(2)}, u32[]{:S(2)}) collective-permute-start(bf16[128,384]{1,0:T(8,128)(2,1)S(1)} %copy.175), channel_id=1, source_target_pairs={{0,16},{4,20},{8,24},{12,28},{16,0},{20,4},{24,8},{28,12},{1,17},{... | collective-permute-start | bytes 294920 | tf_op jit(solution)/shard_map/ppermute | solution.py:368
  44.1 10.3 %collective-permute-start.11 = (bf16[128,384]{1,0:T(8,128)(2,1)S(1)}, bf16[128,384]{1,0:T(8,128)(2,1)S(1)}, u32[]{:S(2)}, u32[]{:S(2)}) collective-permute-start(bf16[128,384]{1,0:T(8,128)(2,1)S(1)} %copy.175), channel_id=1, source_target_pairs={{0,24},{4,28},{8,16},{12,20},{16,8},{20,12},{24,0},{28,4},{1,25},{... | collective-permute-start | bytes 294920 | tf_op jit(solution)/shard_map/ppermute | solution.py:368
  44.2 11.7 %collective-permute-start.6 = (bf16[1,1792]{1,0:T(2,128)(2,1)S(1)}, bf16[1,1792]{1,0:T(2,128)(2,1)S(1)}, u32[]{:S(2)}, u32[]{:S(2)}) collective-permute-start(bf16[1,1792]{1,0:T(2,128)(2,1)S(1)} %concatenate.147), channel_id=1, source_target_pairs={{0,8},{4,12},{8,0},{12,4},{16,24},{20,28},{24,16},{28,20},{1,9},{5... | collective-permute-start | bytes 10760 | tf_op jit(solution)/shard_map/ppermute | solution.py:368
  45.9 10.1 %collective-permute-start.7 = (bf16[1,1792]{1,0:T(2,128)(2,1)S(1)}, bf16[1,1792]{1,0:T(2,128)(2,1)S(1)}, u32[]{:S(2)}, u32[]{:S(2)}) collective-permute-start(bf16[1,1792]{1,0:T(2,128)(2,1)S(1)} %concatenate.147), channel_id=1, source_target_pairs={{0,16},{4,20},{8,24},{12,28},{16,0},{20,4},{24,8},{28,12},{1,17},{... | collective-permute-start | bytes 10760 | tf_op jit(solution)/shard_map/ppermute | solution.py:368
  66.9 12.7 %collective-permute-start.15 = (bf16[2,256,1024]{2,1,0:T(8,128)(2,1)}, bf16[2,256,1024]{2,1,0:T(8,128)(2,1)}, u32[]{:S(2)}, u32[]{:S(2)}) collective-permute-start(bf16[2,256,1024]{2,1,0:T(8,128)(2,1)} %pad_maximum_fusion.7), channel_id=1, source_target_pairs={{0,1},{1,0},{2,3},{3,2},{4,5},{5,4},{6,7},{7,6},{8,9},{9,8},{10,11... | collective-permute-start | bytes 3145736 | tf_op jit(solution)/shard_map/ppermute | solution.py:378
  73.7 28.6 %collective-permute-start.16 = (bf16[1024,384]{1,0:T(8,128)(2,1)}, bf16[1024,384]{1,0:T(8,128)(2,1)}, u32[]{:S(2)}, u32[]{:S(2)}) collective-permute-start(bf16[1024,384]{1,0:T(8,128)(2,1)} %constant_dynamic-update-slice_fusion), channel_id=1, source_target_pairs={{0,2},{1,3},{2,0},{3,1},{4,6},{5,7},{6,4},{7,5},{8,10},{9,11},{10,... | collective-permute-start | bytes 2359304 | tf_op jit(solution)/shard_map/ppermute | solution.py:378
  74.3 48.3 %collective-permute-start.20 = (bf16[128,2304]{1,0:T(8,128)(2,1)}, bf16[128,2304]{1,0:T(8,128)(2,1)}, u32[]{:S(2)}, u32[]{:S(2)}) collective-permute-start(bf16[128,2304]{1,0:T(8,128)(2,1)} %pad_maximum_fusion.20), channel_id=1, source_target_pairs={{0,8},{4,12},{8,0},{12,4},{16,24},{20,28},{24,16},{28,20},{1,9},{5... | collective-permute-start | bytes 1769480 | tf_op jit(solution)/shard_map/ppermute | solution.py:368
  75.5 47.1 %collective-permute-start.21 = (bf16[128,2304]{1,0:T(8,128)(2,1)}, bf16[128,2304]{1,0:T(8,128)(2,1)}, u32[]{:S(2)}, u32[]{:S(2)}) collective-permute-start(bf16[128,2304]{1,0:T(8,128)(2,1)} %pad_maximum_fusion.20), channel_id=1, source_target_pairs={{0,16},{4,20},{8,24},{12,28},{16,0},{20,4},{24,8},{28,12},{1,17},{... | collective-permute-start | bytes 1769480 | tf_op jit(solution)/shard_map/ppermute | solution.py:368
  77.9 24.4 %collective-permute-start.17 = (bf16[512,384]{1,0:T(8,128)(2,1)}, bf16[512,384]{1,0:T(8,128)(2,1)S(1)}, u32[]{:S(2)}, u32[]{:S(2)}) collective-permute-start(bf16[512,384]{1,0:T(8,128)(2,1)} %pad_maximum_fusion.25), channel_id=1, source_target_pairs={{0,2},{1,3},{2,0},{3,1},{4,6},{5,7},{6,4},{7,5},{8,10},{9,11},{10,... | collective-permute-start | bytes 1179656 | tf_op jit(solution)/shard_map/ppermute | solution.py:378
  79.7 42.9 %collective-permute-start.22 = (bf16[128,2304]{1,0:T(8,128)(2,1)}, bf16[128,2304]{1,0:T(8,128)(2,1)}, u32[]{:S(2)}, u32[]{:S(2)}) collective-permute-start(bf16[128,2304]{1,0:T(8,128)(2,1)} %pad_maximum_fusion.20), channel_id=1, source_target_pairs={{0,24},{4,28},{8,16},{12,20},{16,8},{20,12},{24,0},{28,4},{1,25},{... | collective-permute-start | bytes 1769480 | tf_op jit(solution)/shard_map/ppermute | solution.py:368
  103.8 24.3 %collective-permute-start.18 = (bf16[1024,768]{1,0:T(8,128)(2,1)S(1)}, bf16[1024,768]{1,0:T(8,128)(2,1)}, u32[]{:S(2)}, u32[]{:S(2)}) collective-permute-start(bf16[1024,768]{1,0:T(8,128)(2,1)S(1)} %pad_maximum_fusion.4.refs_4_), channel_id=1, source_target_pairs={{0,1},{1,0},{2,3},{3,2},{4,5},{5,4},{6,7},{7,6},{8,9},{9,8},{10,11... | collective-permute-start | bytes 4718600 | tf_op jit(solution)/shard_map/ppermute | solution.py:378
  108.3 19.8 %collective-permute-start.19 = (bf16[512,768]{1,0:T(8,128)(2,1)}, bf16[512,768]{1,0:T(8,128)(2,1)}, u32[]{:S(2)}, u32[]{:S(2)}) collective-permute-start(bf16[512,768]{1,0:T(8,128)(2,1)} %pad_maximum_fusion.19), channel_id=1, source_target_pairs={{0,4},{4,0},{8,12},{12,8},{16,20},{20,16},{24,28},{28,24},{1,5},{5... | collective-permute-start | bytes 2359304 | tf_op jit(solution)/shard_map/ppermute | solution.py:374
  129.4 23.7 %collective-permute-start.23 = (bf16[1024,768]{1,0:T(8,128)(2,1)S(1)}, bf16[1024,768]{1,0:T(8,128)(2,1)S(1)}, u32[]{:S(2)}, u32[]{:S(2)}) collective-permute-start(bf16[1024,768]{1,0:T(8,128)(2,1)S(1)} %pad_maximum_fusion.5.refs_5_), channel_id=1, source_target_pairs={{0,1},{1,0},{2,3},{3,2},{4,5},{5,4},{6,7},{7,6},{8,9},{9,8},{10,11... | collective-permute-start | bytes 4718600 | tf_op jit(solution)/shard_map/ppermute | solution.py:378
  133.5 16.0 %collective-permute-start.24 = (bf16[2,512,128]{2,1,0:T(8,128)(2,1)S(1)}, bf16[2,512,128]{2,1,0:T(8,128)(2,1)S(1)}, u32[]{:S(2)}, u32[]{:S(2)}) collective-permute-start(bf16[2,512,128]{2,1,0:T(8,128)(2,1)S(1)} %pad_maximum_fusion.26), channel_id=1, source_target_pairs={{0,4},{4,0},{8,12},{12,8},{16,20},{20,16},{24,28},{28,24},{1,5},{5... | collective-permute-start | bytes 786440 | tf_op jit(solution)/shard_map/ppermute | solution.py:374
  135.2 14.3 %collective-permute-start.25 = (bf16[512,512]{1,0:T(8,128)(2,1)S(1)}, bf16[512,512]{1,0:T(8,128)(2,1)S(1)}, u32[]{:S(2)}, u32[]{:S(2)}) collective-permute-start(bf16[512,512]{1,0:T(8,128)(2,1)S(1)} %get-tuple-element.465), channel_id=1, source_target_pairs={{0,2},{1,3},{2,0},{3,1},{4,6},{5,7},{6,4},{7,5},{8,10},{9,11},{10,... | collective-permute-start | bytes 1572872 | tf_op jit(solution)/shard_map/ppermute | solution.py:378
  135.5 17.5 %collective-permute-start.26 = (bf16[512,512]{1,0:T(8,128)(2,1)S(1)}, bf16[512,512]{1,0:T(8,128)(2,1)S(1)}, u32[]{:S(2)}, u32[]{:S(2)}) collective-permute-start(bf16[512,512]{1,0:T(8,128)(2,1)S(1)} %get-tuple-element.464), channel_id=1, source_target_pairs={{0,4},{4,0},{8,12},{12,8},{16,20},{20,16},{24,28},{28,24},{1,5},{5... | collective-permute-start | bytes 1572872 | tf_op jit(solution)/shard_map/ppermute | solution.py:374
  154.3 38.2 %collective-permute-start.27 = (bf16[512,1024]{1,0:T(8,128)(2,1)}, bf16[512,1024]{1,0:T(8,128)(2,1)}, u32[]{:S(2)}, u32[]{:S(2)}) collective-permute-start(bf16[512,1024]{1,0:T(8,128)(2,1)} %pad_maximum_fusion.8), channel_id=1, source_target_pairs={{0,4},{4,0},{8,12},{12,8},{16,20},{20,16},{24,28},{28,24},{1,5},{5... | collective-permute-start | bytes 3145736 | tf_op jit(solution)/shard_map/ppermute | solution.py:374
  156.9 35.6 %collective-permute-start.28 = (bf16[1024,512]{1,0:T(8,128)(2,1)}, bf16[1024,512]{1,0:T(8,128)(2,1)}, u32[]{:S(2)}, u32[]{:S(2)}) collective-permute-start(bf16[1024,512]{1,0:T(8,128)(2,1)} %pad_maximum_fusion.9), channel_id=1, source_target_pairs={{0,2},{1,3},{2,0},{3,1},{4,6},{5,7},{6,4},{7,5},{8,10},{9,11},{10,... | collective-permute-start | bytes 3145736 | tf_op jit(solution)/shard_map/ppermute | solution.py:378
  158.1 34.4 %collective-permute-start.29 = (bf16[2,1024,128]{2,1,0:T(8,128)(2,1)}, bf16[2,1024,128]{2,1,0:T(8,128)(2,1)}, u32[]{:S(2)}, u32[]{:S(2)}) collective-permute-start(bf16[2,1024,128]{2,1,0:T(8,128)(2,1)} %pad_maximum_fusion.23), channel_id=1, source_target_pairs={{0,2},{1,3},{2,0},{3,1},{4,6},{5,7},{6,4},{7,5},{8,10},{9,11},{10,... | collective-permute-start | bytes 1572872 | tf_op jit(solution)/shard_map/ppermute | solution.py:378
  195.4 40.8 %collective-permute-start.30 = (bf16[1024,1024]{1,0:T(8,128)(2,1)}, bf16[1024,1024]{1,0:T(8,128)(2,1)}, u32[]{:S(2)}, u32[]{:S(2)}) collective-permute-start(bf16[1024,1024]{1,0:T(8,128)(2,1)} %pad_maximum_fusion.right_ref.refs_6_), channel_id=1, source_target_pairs={{0,1},{1,0},{2,3},{3,2},{4,5},{5,4},{6,7},{7,6},{8,9},{9,8},{10,11... | collective-permute-start | bytes 6291464 | tf_op jit(solution)/shard_map/ppermute | solution.py:378
  198.4 37.8 %collective-permute-start.31 = (bf16[1024,1024]{1,0:T(8,128)(2,1)}, bf16[1024,1024]{1,0:T(8,128)(2,1)}, u32[]{:S(2)}, u32[]{:S(2)}) collective-permute-start(bf16[1024,1024]{1,0:T(8,128)(2,1)} %pad_maximum_fusion.1.right_ref.refs_7_), channel_id=1, source_target_pairs={{0,1},{1,0},{2,3},{3,2},{4,5},{5,4},{6,7},{7,6},{8,9},{9,8},{10,11... | collective-permute-start | bytes 6291464 | tf_op jit(solution)/shard_map/ppermute | solution.py:378
  199.7 14.8 %collective-permute-start.33 = (bf16[512,512]{1,0:T(8,128)(2,1)S(1)}, bf16[512,512]{1,0:T(8,128)(2,1)S(1)}, u32[]{:S(2)}, u32[]{:S(2)}) collective-permute-start(bf16[512,512]{1,0:T(8,128)(2,1)S(1)} %get-tuple-element.496), channel_id=1, source_target_pairs={{0,2},{1,3},{2,0},{3,1},{4,6},{5,7},{6,4},{7,5},{8,10},{9,11},{10,... | collective-permute-start | bytes 1572872 | tf_op jit(solution)/shard_map/ppermute | solution.py:378
  202.2 26.4 %collective-permute-start.32 = (bf16[2,1024,256]{2,1,0:T(8,128)(2,1)}, bf16[2,1024,256]{2,1,0:T(8,128)(2,1)}, u32[]{:S(2)}, u32[]{:S(2)}) collective-permute-start(bf16[2,1024,256]{2,1,0:T(8,128)(2,1)} %pad_maximum_fusion.10), channel_id=1, source_target_pairs={{0,1},{1,0},{2,3},{3,2},{4,5},{5,4},{6,7},{7,6},{8,9},{9,8},{10,11... | collective-permute-start | bytes 3145736 | tf_op jit(solution)/shard_map/ppermute | solution.py:378
  204.1 32.0 %collective-permute-start.35 = (bf16[2,256,1024]{2,1,0:T(8,128)(2,1)}, bf16[2,256,1024]{2,1,0:T(8,128)(2,1)}, u32[]{:S(2)}, u32[]{:S(2)}) collective-permute-start(bf16[2,256,1024]{2,1,0:T(8,128)(2,1)} %pad_maximum_fusion.11), channel_id=1, source_target_pairs={{0,2},{1,3},{2,0},{3,1},{4,6},{5,7},{6,4},{7,5},{8,10},{9,11},{10,... | collective-permute-start | bytes 3145736 | tf_op jit(solution)/shard_map/ppermute | solution.py:378
  215.3 13.2 %collective-permute-start.34 = (bf16[512,512]{1,0:T(8,128)(2,1)}, bf16[512,512]{1,0:T(8,128)(2,1)}, u32[]{:S(2)}, u32[]{:S(2)}) collective-permute-start(bf16[512,512]{1,0:T(8,128)(2,1)} %get-tuple-element.495), channel_id=1, source_target_pairs={{0,4},{4,0},{8,12},{12,8},{16,20},{20,16},{24,28},{28,24},{1,5},{5... | collective-permute-start | bytes 1572872 | tf_op jit(solution)/shard_map/ppermute | solution.py:374
  237.4 41.1 %collective-permute-start.36 = (bf16[512,1024]{1,0:T(8,128)(2,1)}, bf16[512,1024]{1,0:T(8,128)(2,1)}, u32[]{:S(2)}, u32[]{:S(2)}) collective-permute-start(bf16[512,1024]{1,0:T(8,128)(2,1)} %pad_maximum_fusion.12), channel_id=1, source_target_pairs={{0,4},{4,0},{8,12},{12,8},{16,20},{20,16},{24,28},{28,24},{1,5},{5... | collective-permute-start | bytes 3145736 | tf_op jit(solution)/shard_map/ppermute | solution.py:374
  240.1 38.4 %collective-permute-start.37 = (bf16[1024,512]{1,0:T(8,128)(2,1)}, bf16[1024,512]{1,0:T(8,128)(2,1)}, u32[]{:S(2)}, u32[]{:S(2)}) collective-permute-start(bf16[1024,512]{1,0:T(8,128)(2,1)} %pad_maximum_fusion.13), channel_id=1, source_target_pairs={{0,2},{1,3},{2,0},{3,1},{4,6},{5,7},{6,4},{7,5},{8,10},{9,11},{10,... | collective-permute-start | bytes 3145736 | tf_op jit(solution)/shard_map/ppermute | solution.py:378
  243.6 34.9 %collective-permute-start.38 = (bf16[2,256,1024]{2,1,0:T(8,128)(2,1)}, bf16[2,256,1024]{2,1,0:T(8,128)(2,1)}, u32[]{:S(2)}, u32[]{:S(2)}) collective-permute-start(bf16[2,256,1024]{2,1,0:T(8,128)(2,1)} %pad_maximum_fusion.14), channel_id=1, source_target_pairs={{0,1},{1,0},{2,3},{3,2},{4,5},{5,4},{6,7},{7,6},{8,9},{9,8},{10,11... | collective-permute-start | bytes 3145736 | tf_op jit(solution)/shard_map/ppermute | solution.py:378
  292.8 12.5 %collective-permute-start.39 = (bf16[1024,1024]{1,0:T(8,128)(2,1)S(1)}, bf16[1024,1024]{1,0:T(8,128)(2,1)S(1)}, u32[]{:S(2)}, u32[]{:S(2)}) collective-permute-start(bf16[1024,1024]{1,0:T(8,128)(2,1)S(1)} %convolution_convert_fusion.3), channel_id=1, source_target_pairs={{0,1},{1,0},{2,3},{3,2},{4,5},{5,4},{6,7},{7,6},{8,9},{9,8},{10,11... | collective-permute-start | bytes 6291464 | tf_op jit(solution)/shard_map/ppermute | solution.py:378
  295.8 9.5 %collective-permute-start.40 = (bf16[1024,1024]{1,0:T(8,128)(2,1)S(1)}, bf16[1024,1024]{1,0:T(8,128)(2,1)S(1)}, u32[]{:S(2)}, u32[]{:S(2)}) collective-permute-start(bf16[1024,1024]{1,0:T(8,128)(2,1)S(1)} %convolution_convert_fusion.2), channel_id=1, source_target_pairs={{0,1},{1,0},{2,3},{3,2},{4,5},{5,4},{6,7},{7,6},{8,9},{9,8},{10,11... | collective-permute-start | bytes 6291464 | tf_op jit(solution)/shard_map/ppermute | solution.py:378
  308.4 58.4 %collective-permute-start.43 = (bf16[512,1024]{1,0:T(8,128)(2,1)}, bf16[512,1024]{1,0:T(8,128)(2,1)}, u32[]{:S(2)}, u32[]{:S(2)}) collective-permute-start(bf16[512,1024]{1,0:T(8,128)(2,1)} %slice.486), channel_id=1, source_target_pairs={{0,4},{4,0},{8,12},{12,8},{16,20},{20,16},{24,28},{28,24},{1,5},{5... | collective-permute-start | bytes 3145736 | tf_op jit(solution)/shard_map/ppermute | solution.py:374
  312.6 54.3 %collective-permute-start.44 = (bf16[1024,512]{1,0:T(8,128)(2,1)}, bf16[1024,512]{1,0:T(8,128)(2,1)}, u32[]{:S(2)}, u32[]{:S(2)}) collective-permute-start(bf16[1024,512]{1,0:T(8,128)(2,1)} %slice.487), channel_id=1, source_target_pairs={{0,2},{1,3},{2,0},{3,1},{4,6},{5,7},{6,4},{7,5},{8,10},{9,11},{10,... | collective-permute-start | bytes 3145736 | tf_op jit(solution)/shard_map/ppermute | solution.py:378
  363.4 46.2 %collective-permute-start.49 = (bf16[2,256,1024]{2,1,0:T(8,128)(2,1)}, bf16[2,256,1024]{2,1,0:T(8,128)(2,1)}, u32[]{:S(2)}, u32[]{:S(2)}) collective-permute-start(bf16[2,256,1024]{2,1,0:T(8,128)(2,1)} %bitcast.79), channel_id=1, source_target_pairs={{0,2},{1,3},{2,0},{3,1},{4,6},{5,7},{6,4},{7,5},{8,10},{9,11},{10,... | collective-permute-start | bytes 3145736 | tf_op jit(solution)/shard_map/ppermute | solution.py:378
  372.8 36.9 %collective-permute-start.45 = (bf16[1024,1024]{1,0:T(8,128)(2,1)}, bf16[1024,1024]{1,0:T(8,128)(2,1)}, u32[]{:S(2)}, u32[]{:S(2)}) collective-permute-start(bf16[1024,1024]{1,0:T(8,128)(2,1)} %convolution_convert_fusion.1), channel_id=1, source_target_pairs={{0,1},{1,0},{2,3},{3,2},{4,5},{5,4},{6,7},{7,6},{8,9},{9,8},{10,11... | collective-permute-start | bytes 6291464 | tf_op jit(solution)/shard_map/ppermute | solution.py:378
  376.5 33.2 %collective-permute-start.46 = (bf16[1024,1024]{1,0:T(8,128)(2,1)}, bf16[1024,1024]{1,0:T(8,128)(2,1)}, u32[]{:S(2)}, u32[]{:S(2)}) collective-permute-start(bf16[1024,1024]{1,0:T(8,128)(2,1)} %convolution_convert_fusion), channel_id=1, source_target_pairs={{0,1},{1,0},{2,3},{3,2},{4,5},{5,4},{6,7},{7,6},{8,9},{9,8},{10,11... | collective-permute-start | bytes 6291464 | tf_op jit(solution)/shard_map/ppermute | solution.py:378
  379.6 30.0 %collective-permute-start.47 = (bf16[512,512]{1,0:T(8,128)(2,1)}, bf16[512,512]{1,0:T(8,128)(2,1)S(1)}, u32[]{:S(2)}, u32[]{:S(2)}) collective-permute-start(bf16[512,512]{1,0:T(8,128)(2,1)} %slice.489), channel_id=1, source_target_pairs={{0,2},{1,3},{2,0},{3,1},{4,6},{5,7},{6,4},{7,5},{8,10},{9,11},{10,... | collective-permute-start | bytes 1572872 | tf_op jit(solution)/shard_map/ppermute | solution.py:378
  383.9 25.8 %collective-permute-start.48 = (bf16[512,512]{1,0:T(8,128)(2,1)}, bf16[512,512]{1,0:T(8,128)(2,1)}, u32[]{:S(2)}, u32[]{:S(2)}) collective-permute-start(bf16[512,512]{1,0:T(8,128)(2,1)} %slice.491), channel_id=1, source_target_pairs={{0,4},{4,0},{8,12},{12,8},{16,20},{20,16},{24,28},{28,24},{1,5},{5... | collective-permute-start | bytes 1572872 | tf_op jit(solution)/shard_map/ppermute | solution.py:374
  422.2 34.5 %collective-permute-start.50 = (bf16[512,1024]{1,0:T(8,128)(2,1)S(1)}, bf16[512,1024]{1,0:T(8,128)(2,1)S(1)}, u32[]{:S(2)}, u32[]{:S(2)}) collective-permute-start(bf16[512,1024]{1,0:T(8,128)(2,1)S(1)} %slice.492), channel_id=1, source_target_pairs={{0,4},{4,0},{8,12},{12,8},{16,20},{20,16},{24,28},{28,24},{1,5},{5... | collective-permute-start | bytes 3145736 | tf_op jit(solution)/shard_map/ppermute | solution.py:374
  426.5 30.3 %collective-permute-start.51 = (bf16[1024,512]{1,0:T(8,128)(2,1)S(1)}, bf16[1024,512]{1,0:T(8,128)(2,1)S(1)}, u32[]{:S(2)}, u32[]{:S(2)}) collective-permute-start(bf16[1024,512]{1,0:T(8,128)(2,1)S(1)} %slice.493), channel_id=1, source_target_pairs={{0,2},{1,3},{2,0},{3,1},{4,6},{5,7},{6,4},{7,5},{8,10},{9,11},{10,... | collective-permute-start | bytes 3145736 | tf_op jit(solution)/shard_map/ppermute | solution.py:378
  427.1 29.7 %collective-permute-start.52 = (bf16[2,1024,256]{2,1,0:T(8,128)(2,1)S(1)}, bf16[2,1024,256]{2,1,0:T(8,128)(2,1)S(1)}, u32[]{:S(2)}, u32[]{:S(2)}) collective-permute-start(bf16[2,1024,256]{2,1,0:T(8,128)(2,1)S(1)} %pad_maximum_fusion.15), channel_id=1, source_target_pairs={{0,1},{1,0},{2,3},{3,2},{4,5},{5,4},{6,7},{7,6},{8,9},{9,8},{10,11... | collective-permute-start | bytes 3145736 | tf_op jit(solution)/shard_map/ppermute | solution.py:378
  429.0 27.7 %collective-permute-start.53 = (bf16[256,1024]{1,0:T(8,128)(2,1)S(1)}, bf16[256,1024]{1,0:T(8,128)(2,1)S(1)}, u32[]{:S(2)}, u32[]{:S(2)}) collective-permute-start(bf16[256,1024]{1,0:T(8,128)(2,1)S(1)} %fusion.7), channel_id=1, source_target_pairs={{0,16},{4,20},{8,24},{12,28},{16,0},{20,4},{24,8},{28,12},{1,17},{... | collective-permute-start | bytes 1572872 | tf_op jit(solution)/shard_map/ppermute | solution.py:368
  434.3 22.4 %collective-permute-start.54 = (bf16[2,256,1024]{2,1,0:T(8,128)(2,1)S(1)}, bf16[2,256,1024]{2,1,0:T(8,128)(2,1)S(1)}, u32[]{:S(2)}, u32[]{:S(2)}) collective-permute-start(bf16[2,256,1024]{2,1,0:T(8,128)(2,1)S(1)} %pad_maximum_fusion.16), channel_id=1, source_target_pairs={{0,1},{1,0},{2,3},{3,2},{4,5},{5,4},{6,7},{7,6},{8,9},{9,8},{10,11... | collective-permute-start | bytes 3145736 | tf_op jit(solution)/shard_map/ppermute | solution.py:378
  456.8 26.0 %collective-permute-start.55 = (bf16[1024,768]{1,0:T(8,128)(2,1)S(1)}, bf16[1024,768]{1,0:T(8,128)(2,1)S(1)}, u32[]{:S(2)}, u32[]{:S(2)}) collective-permute-start(bf16[1024,768]{1,0:T(8,128)(2,1)S(1)} %convolution_convert_fusion.7), channel_id=1, source_target_pairs={{0,1},{1,0},{2,3},{3,2},{4,5},{5,4},{6,7},{7,6},{8,9},{9,8},{10,11... | collective-permute-start | bytes 4718600 | tf_op jit(solution)/shard_map/ppermute | solution.py:378
  457.2 24.6 %collective-permute-start.56 = (bf16[2,1024,128]{2,1,0:T(8,128)(2,1)S(1)}, bf16[2,1024,128]{2,1,0:T(8,128)(2,1)S(1)}, u32[]{:S(2)}, u32[]{:S(2)}) collective-permute-start(bf16[2,1024,128]{2,1,0:T(8,128)(2,1)S(1)} %slice.498), channel_id=1, source_target_pairs={{0,2},{1,3},{2,0},{3,1},{4,6},{5,7},{6,4},{7,5},{8,10},{9,11},{10,... | collective-permute-start | bytes 1572872 | tf_op jit(solution)/shard_map/ppermute | solution.py:378
  458.2 24.5 %collective-permute-start.57 = (bf16[512,512]{1,0:T(8,128)(2,1)S(1)}, bf16[512,512]{1,0:T(8,128)(2,1)S(1)}, u32[]{:S(2)}, u32[]{:S(2)}) collective-permute-start(bf16[512,512]{1,0:T(8,128)(2,1)S(1)} %slice.500), channel_id=1, source_target_pairs={{0,2},{1,3},{2,0},{3,1},{4,6},{5,7},{6,4},{7,5},{8,10},{9,11},{10,... | collective-permute-start | bytes 1572872 | tf_op jit(solution)/shard_map/ppermute | solution.py:378
  460.2 22.6 %collective-permute-start.58 = (bf16[512,512]{1,0:T(8,128)(2,1)S(1)}, bf16[512,512]{1,0:T(8,128)(2,1)S(1)}, u32[]{:S(2)}, u32[]{:S(2)}) collective-permute-start(bf16[512,512]{1,0:T(8,128)(2,1)S(1)} %slice.502), channel_id=1, source_target_pairs={{0,4},{4,0},{8,12},{12,8},{16,20},{20,16},{24,28},{28,24},{1,5},{5... | collective-permute-start | bytes 1572872 | tf_op jit(solution)/shard_map/ppermute | solution.py:374
  461.0 20.7 %collective-permute-start.59 = (bf16[128,1024]{1,0:T(8,128)(2,1)S(1)}, bf16[128,1024]{1,0:T(8,128)(2,1)S(1)}, u32[]{:S(2)}, u32[]{:S(2)}) collective-permute-start(bf16[128,1024]{1,0:T(8,128)(2,1)S(1)} %slice.503), channel_id=1, source_target_pairs={{0,8},{4,12},{8,0},{12,4},{16,24},{20,28},{24,16},{28,20},{1,9},{5... | collective-permute-start | bytes 786440 | tf_op jit(solution)/shard_map/ppermute | solution.py:368
  483.0 21.5 %collective-permute-start.60 = (bf16[2,512,128]{2,1,0:T(8,128)(2,1)S(1)}, bf16[2,512,128]{2,1,0:T(8,128)(2,1)S(1)}, u32[]{:S(2)}, u32[]{:S(2)}) collective-permute-start(bf16[2,512,128]{2,1,0:T(8,128)(2,1)S(1)} %slice.505), channel_id=1, source_target_pairs={{0,4},{4,0},{8,12},{12,8},{16,20},{20,16},{24,28},{28,24},{1,5},{5... | collective-permute-start | bytes 786440 | tf_op jit(solution)/shard_map/ppermute | solution.py:374
  484.0 20.4 %collective-permute-start.61 = (bf16[1024,384]{1,0:T(8,128)(2,1)S(1)}, bf16[1024,384]{1,0:T(8,128)(2,1)S(1)}, u32[]{:S(2)}, u32[]{:S(2)}) collective-permute-start(bf16[1024,384]{1,0:T(8,128)(2,1)S(1)} %slice.506), channel_id=1, source_target_pairs={{0,2},{1,3},{2,0},{3,1},{4,6},{5,7},{6,4},{7,5},{8,10},{9,11},{10,... | collective-permute-start | bytes 2359304 | tf_op jit(solution)/shard_map/ppermute | solution.py:378
  504.5 28.2 %collective-permute-start.63 = (bf16[1024,768]{1,0:T(8,128)(2,1)}, bf16[1024,768]{1,0:T(8,128)(2,1)}, u32[]{:S(2)}, u32[]{:S(2)}) collective-permute-start(bf16[1024,768]{1,0:T(8,128)(2,1)} %convolution_convert_fusion.6), channel_id=1, source_target_pairs={{0,1},{1,0},{2,3},{3,2},{4,5},{5,4},{6,7},{7,6},{8,9},{9,8},{10,11... | collective-permute-start | bytes 4718600 | tf_op jit(solution)/shard_map/ppermute | solution.py:378
  505.6 27.0 %collective-permute-start.64 = (bf16[256,1024]{1,0:T(8,128)(2,1)}, bf16[256,1024]{1,0:T(8,128)(2,1)}, u32[]{:S(2)}, u32[]{:S(2)}) collective-permute-start(bf16[256,1024]{1,0:T(8,128)(2,1)} %fusion.6), channel_id=1, source_target_pairs={{0,16},{4,20},{8,24},{12,28},{16,0},{20,4},{24,8},{28,12},{1,17},{... | collective-permute-start | bytes 1572872 | tf_op jit(solution)/shard_map/ppermute | solution.py:368
  513.8 18.9 %collective-permute-start.62 = (bf16[512,384]{1,0:T(8,128)(2,1)S(1)}, bf16[512,384]{1,0:T(8,128)(2,1)S(1)}, u32[]{:S(2)}, u32[]{:S(2)}) collective-permute-start(bf16[512,384]{1,0:T(8,128)(2,1)S(1)} %slice.508), channel_id=1, source_target_pairs={{0,4},{4,0},{8,12},{12,8},{16,20},{20,16},{24,28},{28,24},{1,5},{5... | collective-permute-start | bytes 1179656 | tf_op jit(solution)/shard_map/ppermute | solution.py:374
  535.5 19.8 %collective-permute-start.65 = (bf16[512,768]{1,0:T(8,128)(2,1)}, bf16[512,768]{1,0:T(8,128)(2,1)}, u32[]{:S(2)}, u32[]{:S(2)}) collective-permute-start(bf16[512,768]{1,0:T(8,128)(2,1)} %slice.513), channel_id=1, source_target_pairs={{0,4},{4,0},{8,12},{12,8},{16,20},{20,16},{24,28},{28,24},{1,5},{5... | collective-permute-start | bytes 2359304 | tf_op jit(solution)/shard_map/ppermute | solution.py:374
  538.0 12.3 %collective-permute-start.72 = (bf16[128,1024]{1,0:T(8,128)(2,1)S(1)}, bf16[128,1024]{1,0:T(8,128)(2,1)S(1)}, u32[]{:S(2)}, u32[]{:S(2)}) collective-permute-start(bf16[128,1024]{1,0:T(8,128)(2,1)S(1)} %slice.530), channel_id=1, source_target_pairs={{0,8},{4,12},{8,0},{12,4},{16,24},{20,28},{24,16},{28,20},{1,9},{5... | collective-permute-start | bytes 786440 | tf_op jit(solution)/shard_map/ppermute | solution.py:368
  548.4 38.4 %collective-permute-start.66 = (bf16[2,256,1024]{2,1,0:T(8,128)(2,1)}, bf16[2,256,1024]{2,1,0:T(8,128)(2,1)}, u32[]{:S(2)}, u32[]{:S(2)}) collective-permute-start(bf16[2,256,1024]{2,1,0:T(8,128)(2,1)} %bitcast.91), channel_id=1, source_target_pairs={{0,2},{1,3},{2,0},{3,1},{4,6},{5,7},{6,4},{7,5},{8,10},{9,11},{10,... | collective-permute-start | bytes 3145736 | tf_op jit(solution)/shard_map/ppermute | solution.py:378
  589.2 37.1 %collective-permute-start.67 = (bf16[2,256,1024]{2,1,0:T(8,128)(2,1)}, bf16[2,256,1024]{2,1,0:T(8,128)(2,1)}, u32[]{:S(2)}, u32[]{:S(2)}) collective-permute-start(bf16[2,256,1024]{2,1,0:T(8,128)(2,1)} %pad_maximum_fusion.17), channel_id=1, source_target_pairs={{0,1},{1,0},{2,3},{3,2},{4,5},{5,4},{6,7},{7,6},{8,9},{9,8},{10,11... | collective-permute-start | bytes 3145736 | tf_op jit(solution)/shard_map/ppermute | solution.py:378
  593.5 11.1 %collective-permute-start.69 = (bf16[128,1024]{1,0:T(8,128)(2,1)}, bf16[128,1024]{1,0:T(8,128)(2,1)S(1)}, u32[]{:S(2)}, u32[]{:S(2)}) collective-permute-start(bf16[128,1024]{1,0:T(8,128)(2,1)} %get-tuple-element.478), channel_id=1, source_target_pairs={{0,8},{4,12},{8,0},{12,4},{16,24},{20,28},{24,16},{28,20},{1,9},{5... | collective-permute-start | bytes 786440 | tf_op jit(solution)/shard_map/ppermute | solution.py:368
  594.2 20.6 %collective-permute-start.70 = (bf16[128,1024]{1,0:T(8,128)(2,1)}, bf16[128,1024]{1,0:T(8,128)(2,1)}, u32[]{:S(2)}, u32[]{:S(2)}) collective-permute-start(bf16[128,1024]{1,0:T(8,128)(2,1)} %get-tuple-element.477), channel_id=1, source_target_pairs={{0,16},{4,20},{8,24},{12,28},{16,0},{20,4},{24,8},{28,12},{1,17},{... | collective-permute-start | bytes 786440 | tf_op jit(solution)/shard_map/ppermute | solution.py:368
  596.4 18.3 %collective-permute-start.71 = (bf16[128,1024]{1,0:T(8,128)(2,1)}, bf16[128,1024]{1,0:T(8,128)(2,1)}, u32[]{:S(2)}, u32[]{:S(2)}) collective-permute-start(bf16[128,1024]{1,0:T(8,128)(2,1)} %get-tuple-element.476), channel_id=1, source_target_pairs={{0,24},{4,28},{8,16},{12,20},{16,8},{20,12},{24,0},{28,4},{1,25},{... | collective-permute-start | bytes 786440 | tf_op jit(solution)/shard_map/ppermute | solution.py:368
  (169 other events, 1365.1 us)

commit v7 on v6

--- a/solution.py
+++ b/solution.py
@@ -409,14 +409,23 @@
 
 
 def rows_z_steps(chain, shard):
-    arrived = yield [swap_z(shard, step) for step in range(1, ZS)]
-    return jnp.concatenate([shard] + arrived, 0)
-
-
-def gather_steps(chain, parts, orders):
-    for axes in zip(*orders):
-        arrived = yield [swap_plane(part, axis) for part, axis in zip(parts, axes)]
-        parts = [join(part, each, axis) for part, each, axis in zip(parts, arrived, axes)]
+    rows = shard
+    for step in (1, 2):
+        (arrived,) = yield [swap_z(rows, step)]
+        rows = jnp.concatenate([rows, arrived], 0)
+    return rows
+
+
+def cut(part, axis, pieces):
+    return jnp.split(part, pieces, -2 if axis == "y" else -1) if pieces > 1 else [part]
+
+
+def gather_steps(chain, parts, orders, pieces=(1, 1)):
+    for axes, count in zip(zip(*orders), pieces):
+        sent = [cut(part, axis, count) for part, axis in zip(parts, axes)]
+        for at in range(count):
+            arrived = yield [swap_plane(each[at], axis) for each, axis in zip(sent, axes)]
+            parts = [join(part, each, axis) for part, each, axis in zip(parts, arrived, axes)]
     chain.own = parts
     arrived = yield [swap_mp(part, 1) for part in parts]
     return arrived
@@ -433,13 +442,19 @@
     return (total[..., : width // 2], total[..., width // 2 :])
 
 
-def reduce_steps(chain, other_parts, orders):
+def reduce_steps(chain, other_parts, orders, pieces=(1, 1)):
     arrived = yield [swap_mp(part, 1) for part in other_parts]
     totals = [add_low(own, each) for own, each in zip(chain.own, arrived)]
-    for axes in zip(*orders):
+    for axes, count in zip(zip(*orders), pieces):
         halves = [halve(total, axis) for total, axis in zip(totals, axes)]
-        arrived = yield [swap_plane(half[1], axis) for half, axis in zip(halves, axes)]
-        totals = [add_low(half[0], each) for half, each in zip(halves, arrived)]
+        sent = [cut(half[1], axis, count) for half, axis in zip(halves, axes)]
+        received = []
+        for at in range(count):
+            received.append((yield [swap_plane(each[at], axis) for each, axis in zip(sent, axes)]))
+        totals = []
+        for half, axis, each in zip(halves, axes, zip(*received)):
+            whole = each[0] if count == 1 else jnp.concatenate(each, -2 if axis == "y" else -1)
+            totals.append(add_low(half[0], whole))
     return totals
 
 
@@ -471,8 +486,9 @@
     biases = shard[:, vector_size:]
     arrived = yield [swap_mp(biases, step) for step in range(1, MP)]
     rows = jnp.concatenate([shard] + arrived, 1)
-    arrived = yield [swap_z(rows, step) for step in range(1, ZS)]
-    rows = jnp.concatenate([rows] + arrived, 0)
+    for step in (1, 2):
+        arrived = yield [swap_z(rows, step)]
+        rows = jnp.concatenate([rows] + arrived, 0)
     arrived = yield [swap_y(rows)]
     rows = jnp.concatenate([rows] + arrived, 0)
     biases = rows[:, vector_size:].reshape(DP, MP, -1).transpose(1, 0, 2)
@@ -616,12 +632,11 @@
 
 def down_kernel(count, *refs):
     lefts, rights = (refs[:count], refs[count : 2 * count])
-    vector_ref, hidden_ref, grad_ref, output_ref, sums_ref = refs[2 * count :]
+    vector_ref, hidden_ref, output_ref, branch_ref = refs[2 * count :]
     branch = product_nt(lefts, rights) + vector_row(vector_ref, DOWN_BIAS)
     output = hidden_ref[...] + vector_row(vector_ref, SCALE_TWO) * branch
     output_ref[...] = output.astype(BF)
-    grad = grad_ref[...].astype(F32)
-    add_rows(sums_ref, [grad * branch, grad])
+    branch_ref[...] = branch
 
 
 def up_back_kernel(count, *refs):
@@ -916,23 +931,20 @@
     kinds = qkv_weight.shape[0]
     qkv_shard = qkv_weight.astype(BF).reshape(kinds, depth, 2, LANES).transpose(1, 2, 0, 3)
     qkv_shard = qkv_shard.reshape(depth, -1)
-    rest_shard = jnp.concatenate(
-        [
-            out_weight.T.astype(BF),
-            up_weight.astype(BF).reshape(depth, -1),
-            down_weight.transpose(2, 0, 1).astype(BF).reshape(depth, -1),
-        ],
-        1,
-    )
+    up_shard = jnp.concatenate(
+        [out_weight.T.astype(BF), up_weight.astype(BF).reshape(depth, -1)], 1
+    )
+    down_shard = down_weight.transpose(2, 0, 1).astype(BF).reshape(depth, -1)
     both = ("xy", "yx")
-    rows_qkv = [Chain(rows_z_steps, each) for each in jnp.split(qkv_shard, 2, 1)]
     small = Chain(small_steps, small_shard, vector_size)
+    rows_qkv = Chain(rows_z_steps, qkv_shard)
+    rows_up = Chain(rows_z_steps, up_shard)
+    tokens = meet(tokens, small, rows_qkv)
     fetch_tokens = fetch_image(tokens)
-    rest_shard = meet(rest_shard, rows_qkv[0], small)
-    get_qkv = [Chain(gather_steps, [rows_qkv[0].result], ("yx",)), None]
-    rest_shard = meet(rest_shard, small, rows_qkv[1])
-    get_qkv[1] = Chain(gather_steps, [rows_qkv[1].result], ("xy",))
-    rows_rest = Chain(rows_z_steps, rest_shard)
+    meet((), small)
+    meet((), small, rows_qkv, rows_up)
+    part_a, part_b = jnp.split(rows_qkv.result, 2, 1)
+    get_qkv = [Chain(gather_steps, [part_a], ("yx",)), Chain(gather_steps, [part_b], ("xy",))]
     meet((), small, get_qkv[0], fetch_tokens)
     tokens = meet(tokens, fetch_tokens)
 
@@ -960,29 +972,28 @@
 
     heads[0][0] = project(0, 0, get_qkv[0].own[0])
     forward_heads(0, 0)
-    blended[0][0], normed_one = meet((blended[0][0], normed_one), *get_qkv, rows_rest)
-    out_rows, up_rows, down_rows = jnp.split(
-        rows_rest.result, [block_width, block_width * (1 + units)], 1
-    )
+    blended[0][0], normed_one, down_shard = meet(
+        (blended[0][0], normed_one, down_shard), *get_qkv, rows_up
+    )
+    out_rows, up_rows = jnp.split(rows_up.result, [block_width], 1)
     get_out = Chain(gather_steps, [jnp.stack(jnp.split(out_rows, 2, 1))], ("yx",))
-    get_up = Chain(gather_steps, jnp.split(up_rows, 2, 1), both)
+    get_up = Chain(gather_steps, jnp.split(up_rows, 2, 1), both, (1, 2))
+    rows_down = Chain(rows_z_steps, down_shard)
     heads[0][1] = project(0, 1, get_qkv[1].own[0])
     forward_heads(0, 1)
-    blended[0][1], normed_one, down_rows = meet(
-        (blended[0][1], normed_one, down_rows), get_qkv[1], get_out, get_up
+    blended[0][1], normed_one = meet(
+        (blended[0][1], normed_one), get_qkv[1], get_out, get_up, rows_down
     )
     w_qkv = [[each.own[0] for each in get_qkv], [each.result[0] for each in get_qkv]]
-    get_down = Chain(gather_steps, jnp.split(down_rows, 2, 1), both)
     heads[1][0] = project(1, 0, w_qkv[1][0])
     forward_heads(1, 0)
-    blended[1][0], normed_one, cotangent = meet(
-        (blended[1][0], normed_one, cotangent), get_up, get_out
-    )
-    fetch_cotangent = fetch_image(cotangent)
+    blended[1][0], normed_one = meet(
+        (blended[1][0], normed_one), get_out, rows_down, get_up
+    )
+    get_down = Chain(gather_steps, jnp.split(rows_down.result, 2, 1), both)
     heads[1][1] = project(1, 1, w_qkv[1][1])
     forward_heads(1, 1)
-    blended = meet(blended, get_up, get_out, get_down, fetch_cotangent)
-    w_up = [get_up.own, get_up.result]
+    blended = meet(blended, get_up, get_out)
     w_out = [[each[0][half] for half in (0, 1)] for each in (get_out.own, get_out.result)]
     pairs = [(core, half) for core in cores for half in (0, 1)]
     branch_one, hidden, normed_two = row_call(
@@ -994,45 +1005,56 @@
         [base],
         [F32, F32, BF],
     )
+    activ, slope = ({}, {})
+
+    def expand_units(core, weights):
+        for half in (0, 1):
+            rows = bias_full[core, 2 + half * half_units : 2 + (half + 1) * half_units]
+            unit_bias = rows.transpose(1, 0, 2).reshape(-1)
+            activ[half, core], slope[half, core] = expand(normed_two, weights[half], unit_bias)
+
+    expand_units(0, get_up.own)
+    activ, normed_two = meet((activ, normed_two), get_up, get_down)
+    w_up = [get_up.own, get_up.result]
+    expand_units(1, w_up[1])
+    activ, slope, cotangent = meet((activ, slope, cotangent), get_down)
+    fetch_cotangent = fetch_image(cotangent)
+    activ = meet(activ, get_down)
+    w_down = [get_down.own, get_down.result]
     parts = [(half, core) for core in (1, 0) for half in (0, 1)]
-    activ, slope = ({}, {})
-    for half, core in parts:
-        rows = bias_full[core, 2 + half * half_units : 2 + (half + 1) * half_units]
-        unit_bias = rows.transpose(1, 0, 2).reshape(-1)
-        activ[half, core], slope[half, core] = expand(normed_two, w_up[core][half], unit_bias)
-        if (half, core) == (0, 0):
-            activ, normed_two, cotangent = meet((activ, normed_two, cotangent), get_down, fetch_cotangent)
-    activ, slope = meet((activ, slope))
-    grad_out, grad_branch = assemble_image(
-        place, vector_full, cotangent[:, 0], fetch_cotangent.result, False
-    )
-
-    def reduce_pairs(left, rights):
-        chain = Chain(reduce_steps, [dot_tn(left, rights[half, 1]).astype(BF) for half in (0, 1)], both[::-1])
-        chain.own = [dot_tn(left, rights[half, 0]).astype(BF) for half in (0, 1)]
-        return chain
-
-    sum_down = reduce_pairs(grad_branch, activ)
-    grad_branch, activ = meet((grad_branch, activ), sum_down, get_down)
-    w_down = [get_down.own, get_down.result]
-    output, sums_two = row_call(
+    output, branch_two = row_call(
         down_kernel,
         "down_output",
         [activ[each] for each in parts],
         [w_down[core][half] for half, core in parts],
         vector_full,
-        [hidden, grad_out],
-        [BF, "sums"],
-    )
-    output, grad_branch, slope = meet((output, grad_branch, slope))
+        [hidden],
+        [BF, F32],
+    )
+    output = meet(output, fetch_cotangent)
+    output, cotangent = meet((output, cotangent), fetch_cotangent)
+    grad_out, grad_branch = assemble_image(
+        place, vector_full, cotangent[:, 0], fetch_cotangent.result, False
+    )
+
+    def reduce_pairs(left, rights, pieces):
+        chain = Chain(reduce_steps, [dot_tn(left, rights[half, 1]).astype(BF) for half in (0, 1)], both[::-1], pieces)
+        chain.own = [dot_tn(left, rights[half, 0]).astype(BF) for half in (0, 1)]
+        return chain
+
+    sum_down = reduce_pairs(grad_branch, activ, (2, 1))
+    grad_branch, output, slope = meet((grad_branch, output, slope), sum_down)
     send_output = send_back(output)
     grad_pre, unit_sums = ({}, {})
     for half, core in parts:
         grad_pre[half, core], unit_sums[half, core] = slope_product(
             grad_branch, w_down[core][half], slope[half, core]
         )
-    grad_pre, normed_two = meet((grad_pre, normed_two), sum_down)
-    sum_up = reduce_pairs(normed_two, grad_pre)
+        if (half, core) == (0, 0):
+            grad_pre, grad_branch = meet((grad_pre, grad_branch), sum_down)
+    grad_pre, normed_two = meet((grad_pre, normed_two))
+    sum_up = reduce_pairs(normed_two, grad_pre, (1, 1))
+    grad_pre = meet(grad_pre, sum_down)
     grad_hidden, grad_projected, sums_one = row_call(
         up_back_kernel,
         "up_norm_back",
@@ -1104,8 +1126,8 @@
             sums_one[2],
             sums_one[0],
             sums_one[1],
-            sums_two[1] * vector_full[SCALE_TWO],
-            sums_two[0],
+            jnp.sum(grad_out.astype(F32), 0) * vector_full[SCALE_TWO],
+            jnp.sum(grad_out.astype(F32) * branch_two, 0),
         ]
     )
     grad_vectors = grad_vectors.reshape(-1, DP, LANES).transpose(1, 0, 2).reshape(DP, -1)

time: 637 us -> 625 us (0.981)
  other arithmetic: 71.7 us -> 86 us
  local copies, waits for them, and re-layouts: 89.4 us -> 75.2 us
  waiting for transfers between devices: 118 us -> 111 us
    ppermute x42 -> x44, waiting for transfers between devices: 77.1 us -> 41.5 us  [swap_mp(): return lax.ppermute(part, 'mp', [(each, each ^ step) for each in range(MP)])]
    ppermute x22 -> x18, waiting for transfers between devices: 24.4 us -> 54.1 us  [swap_z(): lax.ppermute(part, 'dp', [(z * YS + y, (z ^ step) * YS + y) for z in rang...]
    ppermute x22 -> x18, starting transfers between devices: 36.9 us -> 26.4 us  [swap_z(): lax.ppermute(part, 'dp', [(z * YS + y, (z ^ step) * YS + y) for z in rang...]
    unnamed x335 -> x334, local copies, waits for them, and re-layouts: 49.2 us -> 43.6 us
    ppermute x42 -> x44, starting transfers between devices: 23.9 us -> 29.4 us  [swap_mp(): return lax.ppermute(part, 'mp', [(each, each ^ step) for each in range(MP)])]
    ppermute x16 -> x18, starting transfers between devices: 17 us -> 19.5 us  [swap_y(): return lax.ppermute(part, 'dp', [(each, each ^ 1) for each in range(DP)])]
    concatenate x13 -> x14, other arithmetic: 21.5 us -> 24 us  [join(): return jnp.concatenate([rows, arrived], -2 if axis == 'y' else -1)]
    ppermute x16 -> x18, waiting for transfers between devices: 16.3 us -> 15.1 us  [swap_y(): return lax.ppermute(part, 'dp', [(each, each ^ 1) for each in range(DP)])]
  transfers between devices with their start and end apart: 80 -> 80, of which waited for: 22 -> 26; matrix products, arithmetic and copies ran while one was open for 26% -> 24% of each run, Pallas kernels for 32% -> 33%
where the time goes in v7:
time: 625 us; the launch traced here: 618 us
  Pallas kernels  209 us (33%)
  waiting for transfers between devices  111 us (18%)
  other arithmetic  86 us (14%)
  local copies, waits for them, and re-layouts  75.2 us (12%)
  starting transfers between devices  75.2 us (12%)
  matrix products  58.6 us (9%)
    pallas_call x4, Pallas kernels, attend_back(): pl.pallas_call(functools.partial(attend_back_kernel, 256), grid=(pairs,),...  63.7 us
    pallas_call x5, Pallas kernels, row_call(): pl.pallas_call(functools.partial(kernel, len(lefts)), grid=(count,), in_s...  60.6 us
    ppermute x18, waiting for transfers between devices, swap_z(): lax.ppermute(part, 'dp', [(z * YS + y, (z ^ step) * YS + y) for z in rang...  54.1 us
    unnamed x334, local copies, waits for them, and re-layouts  43.6 us
    ppermute x44, waiting for transfers between devices, swap_mp(): return lax.ppermute(part, 'mp', [(each, each ^ step) for each in range(MP)])  41.5 us
    dot_general x16, matrix products, dot_tn(): lax.dot_general(left, right, (((0,), (0,)), ((), ())), preferred_element_...  36.5 us
    pallas_call x4, Pallas kernels, attend(): pl.pallas_call(functools.partial(attend_kernel, 256), grid=(pairs,), in_s...  36.1 us
    ppermute x44, starting transfers between devices, swap_mp(): return lax.ppermute(part, 'mp', [(each, each ^ step) for each in range(MP)])  29.4 us
  transfers between devices with their start and end apart: 80, of which 26 were waited for; matrix products, arithmetic and copies ran while one was open for 24% of the time, Pallas kernels for 33%

profile of v7, /device:TPU:0, one launch (start us, length us, event | category | flops | bytes accessed | tf_op | source)
XLA Modules:
  0.0 618.0 jit_solution(11482968282355542888)
XLA Ops:
  2.8 2.6 collective-permute-start.1
  10.7 4.6 collective-permute-done.3
  16.1 2.8 collective-permute-start.6
  24.0 5.7 collective-permute-done.4
  29.8 3.5 collective-permute-start.5
  33.3 2.8 collective-permute-done.5
  44.3 3.4 collective-permute-done.8
  53.0 3.2 assemble_image.2
  56.3 22.9 %collective-permute-done.13 = bf16[512,384]{1,0:T(8,128)(2,1)S(1)} collective-permute-done((bf16[512,384]{1,0:T(8,128)(2,1)S(1)}, bf16[512,384]{1,0:T(8,128)(2,1)S(1)}, u32[]{:S(2)}, u32[]{:S(2)}) %collective-permute-start.13) | collective-permute-done | bytes 393248 | tf_op jit(solution)/shard_map/ppermute | solution.py:378
  88.4 3.8 add_convert_fusion.9.q_ref.k_ref.v_ref
  92.2 8.8 %attend.4 = (bf16[1024,256]{1,0:T(8,128)(2,1)S(1)}, f32[2,8,1024]{2,1,0:T(8,128)S(1)}) custom-call(bf16[1024,768]{1,0:T(8,128)(2,1)S(1)} %add_convert_fusion.9.q_ref.k_ref.v_ref, bf16[1024,768]{1,0:T(8,128)(2,1)S(1)} %add_convert_fusion.9.q_ref.k_ref.v_ref, bf16[1024,768]{1,0:T(8,128)(2,1)S(1)} %add_convert_fusion.9.q_ref.k_ref.v_ref), custom_call_target="tpu_custom_call" | custom-call | tf_op jit(solution)/shard_map/attend/pallas_call | solution.py:833
  101.9 12.1 %collective-permute-done.16 = bf16[256,1280]{1,0:T(8,128)(2,1)} collective-permute-done((bf16[256,1280]{1,0:T(8,128)(2,1)}, bf16[256,1280]{1,0:T(8,128)(2,1)}, u32[]{:S(2)}, u32[]{:S(2)}) %collective-permute-start.16) | collective-permute-done | bytes 655392 | tf_op jit(solution)/shard_map/ppermute | solution.py:368
  114.1 2.5 pad_maximum_fusion.5.refs_5_
  122.8 2.9 add_convert_fusion.8.q_ref.k_ref.v_ref
  125.8 9.4 %attend.5 = (bf16[1024,256]{1,0:T(8,128)(2,1)S(1)}, f32[2,8,1024]{2,1,0:T(8,128)S(1)}) custom-call(bf16[1024,768]{1,0:T(8,128)(2,1)S(1)} %add_convert_fusion.8.q_ref.k_ref.v_ref, bf16[1024,768]{1,0:T(8,128)(2,1)S(1)} %add_convert_fusion.8.q_ref.k_ref.v_ref, bf16[1024,768]{1,0:T(8,128)(2,1)S(1)} %add_convert_fusion.8.q_ref.k_ref.v_ref), custom_call_target="tpu_custom_call" | custom-call | tf_op jit(solution)/shard_map/attend/pallas_call | solution.py:833
  135.2 3.9 collective-permute-done.18
  146.9 3.8 add_convert_fusion.7.q_ref.k_ref.v_ref
  150.7 9.0 %attend.6 = (bf16[1024,256]{1,0:T(8,128)(2,1)S(1)}, f32[2,8,1024]{2,1,0:T(8,128)S(1)}) custom-call(bf16[1024,768]{1,0:T(8,128)(2,1)S(1)} %add_convert_fusion.7.q_ref.k_ref.v_ref, bf16[1024,768]{1,0:T(8,128)(2,1)S(1)} %add_convert_fusion.7.q_ref.k_ref.v_ref, bf16[1024,768]{1,0:T(8,128)(2,1)S(1)} %add_convert_fusion.7.q_ref.k_ref.v_ref), custom_call_target="tpu_custom_call" | custom-call | tf_op jit(solution)/shard_map/attend/pallas_call | solution.py:833
  160.6 9.0 %collective-permute-done.23 = bf16[256,1024]{1,0:T(8,128)(2,1)} collective-permute-done((bf16[256,1024]{1,0:T(8,128)(2,1)}, bf16[256,1024]{1,0:T(8,128)(2,1)}, u32[]{:S(2)}, u32[]{:S(2)}) %collective-permute-start.23) | collective-permute-done | bytes 524320 | tf_op jit(solution)/shard_map/ppermute | solution.py:368
  173.8 3.8 add_convert_fusion.6.q_ref.k_ref.v_ref
  177.7 8.8 %attend.7 = (bf16[1024,256]{1,0:T(8,128)(2,1)S(1)}, f32[2,8,1024]{2,1,0:T(8,128)S(1)}) custom-call(bf16[1024,768]{1,0:T(8,128)(2,1)S(1)} %add_convert_fusion.6.q_ref.k_ref.v_ref, bf16[1024,768]{1,0:T(8,128)(2,1)S(1)} %add_convert_fusion.6.q_ref.k_ref.v_ref, bf16[1024,768]{1,0:T(8,128)(2,1)S(1)} %add_convert_fusion.6.q_ref.k_ref.v_ref), custom_call_target="tpu_custom_call" | custom-call | tf_op jit(solution)/shard_map/attend/pallas_call | solution.py:833
  187.7 2.9 pad_maximum_fusion.1.right_ref.refs_7_
  190.6 2.7 pad_maximum_fusion.right_ref.refs_6_
  200.9 6.9 %out_norm.1 = (f32[1024,1024]{1,0:T(8,128)}, f32[1024,1024]{1,0:T(8,128)}, bf16[1024,1024]{1,0:T(8,128)(2,1)}) custom-call(bf16[1024,256]{1,0:T(8,128)(2,1)S(1)} %copy-done.59, bf16[1024,256]{1,0:T(8,128)(2,1)S(1)} %copy-done.62, bf16[1024,256]{1,0:T(8,128)(2,1)S(1)} %copy-done.65, bf16[1024,256]{1,0:T(8,128)(2,1)S(1)} %copy-done.68, ...), custom_call_target="tpu_custom_call" | custom-call | tf_op jit(solution)/shard_map/out_norm/pallas_call | solution.py:739
  209.4 6.0 expand.5
  218.1 6.0 expand.4
  231.0 6.0 expand.7
  239.8 6.1 expand.6
  245.9 4.5 collective-permute-done.34
  262.8 15.7 %down_output.1 = (bf16[1024,1024]{1,0:T(8,128)(2,1)S(1)}, f32[1024,1024]{1,0:T(8,128)}) custom-call(bf16[1024,1024]{1,0:T(8,128)(2,1)S(1)} %get-tuple-element.275.refs_0_, bf16[1024,1024]{1,0:T(8,128)(2,1)} %copy-done.44, bf16[1024,1024]{1,0:T(8,128)(2,1)} %copy-done.38, bf16[1024,1024]{1,0:T(8,128)(2,1)} %copy-done.36, bf16[1024,1024]{1,0:T(8,128)(2,1)} %copy-done.28, ...), custom_call_target="tpu_custom_call" | custom-call | tf_op jit(solution)/shard_map/down_output/pallas_call | solution.py:739
  278.5 5.3 collective-permute-done.37
  285.2 2.6 collective-permute-done.38
  290.1 3.7 convolution_convert_fusion.2
  293.8 3.7 convolution_convert_fusion.3
  307.3 2.9 multiply_reduce_fusion
  313.2 2.4 fusion.38
  315.6 2.6 add_convert_fusion.2
  320.2 2.9 add_convert_fusion.3
  326.2 3.2 slope_product.6
  330.8 3.2 slope_product.5
  335.4 3.2 slope_product.4
  348.5 3.2 slope_product.7
  353.1 3.7 convolution_convert_fusion
  356.7 3.7 convolution_convert_fusion.1
  370.1 20.2 %up_norm_back.1 = (f32[1024,1024]{1,0:T(8,128)}, bf16[1024,1024]{1,0:T(8,128)(2,1)S(1)}, f32[8,1024]{1,0:T(8,128)S(1)}) custom-call(bf16[1024,1024]{1,0:T(8,128)(2,1)S(1)} %copy-done.55, bf16[1024,1024]{1,0:T(8,128)(2,1)} %copy-done.51, bf16[1024,1024]{1,0:T(8,128)(2,1)} %copy-done.49, bf16[1024,1024]{1,0:T(8,128)(2,1)} %copy-done.56, ...), custom_call_target="tpu_custom_call" | custom-call | tf_op jit(solution)/shard_map/up_norm_back/pallas_call | solution.py:739
  390.4 2.4 fusion.41
  398.8 2.5 convolution_convert_fusion.13.g_ref
  409.7 2.6 add_convert_fusion
  413.3 2.6 add_convert_fusion.1
  419.2 15.9 %attend_back.4.refs_2_ = bf16[1024,768]{1,0:T(8,128)(2,1)S(1)} custom-call(bf16[1024,768]{1,0:T(8,128)(2,1)S(1)} %copy-done.3, bf16[1024,768]{1,0:T(8,128)(2,1)S(1)} %copy-done.3, bf16[1024,768]{1,0:T(8,128)(2,1)S(1)} %copy-done.3, bf16[1024,256]{1,0:T(8,128)(2,1)S(1)} %convolution_convert_fusion.15.g_ref, f32[2,8,1024]{2,1,0:T(8,128)S(1)} %get-tuple-element.327.lse_ref), custom_call_target="tpu_custom_call" | custom-call | tf_op jit(solution)/shard_map/attend_back/pallas_call | solution.py:853
  437.6 3.3 collective-permute-done.50
  447.5 15.7 %attend_back.5.refs_0_ = bf16[1024,768]{1,0:T(8,128)(2,1)S(1)} custom-call(bf16[1024,768]{1,0:T(8,128)(2,1)S(1)} %add_convert_fusion.9.q_ref.k_ref.v_ref, bf16[1024,768]{1,0:T(8,128)(2,1)S(1)} %add_convert_fusion.9.q_ref.k_ref.v_ref, bf16[1024,768]{1,0:T(8,128)(2,1)S(1)} %add_convert_fusion.9.q_ref.k_ref.v_ref, ...), custom_call_target="tpu_custom_call" | custom-call | tf_op jit(solution)/shard_map/attend_back/pallas_call | solution.py:853
  463.3 2.8 spread_image.2
  474.2 16.1 %attend_back.6.refs_3_ = bf16[1024,768]{1,0:T(8,128)(2,1)S(1)} custom-call(bf16[1024,768]{1,0:T(8,128)(2,1)S(1)} %copy-done.1, bf16[1024,768]{1,0:T(8,128)(2,1)S(1)} %copy-done.1, bf16[1024,768]{1,0:T(8,128)(2,1)S(1)} %copy-done.1, bf16[1024,256]{1,0:T(8,128)(2,1)S(1)} %convolution_convert_fusion.12.g_ref, f32[2,8,1024]{2,1,0:T(8,128)S(1)} %get-tuple-element.345.lse_ref), custom_call_target="tpu_custom_call" | custom-call | tf_op jit(solution)/shard_map/attend_back/pallas_call | solution.py:853
  490.4 3.1 convolution_convert_fusion.6
  499.0 3.0 multiply_subtract_fusion
  503.4 15.9 %attend_back.7.refs_1_ = bf16[1024,768]{1,0:T(8,128)(2,1)S(1)} custom-call(bf16[1024,768]{1,0:T(8,128)(2,1)S(1)} %add_convert_fusion.8.q_ref.k_ref.v_ref, bf16[1024,768]{1,0:T(8,128)(2,1)S(1)} %add_convert_fusion.8.q_ref.k_ref.v_ref, bf16[1024,768]{1,0:T(8,128)(2,1)S(1)} %add_convert_fusion.8.q_ref.k_ref.v_ref, bf16[1024,256]{1,0:T(8,128)(2,1)S(1)} %copy-done.70, ...), custom_call_target="tpu_custom_call" | custom-call | tf_op jit(solution)/shard_map/attend_back/pallas_call | solution.py:853
  529.1 9.3 %in_norm_back.3 = (bf16[512,1024]{1,0:T(8,128)(2,1)}, f32[8,1024]{1,0:T(8,128)S(1)}) custom-call(bf16[1024,768]{1,0:T(8,128)(2,1)S(1)} %copy-done.14, bf16[1024,768]{1,0:T(8,128)(2,1)S(1)} %attend_back.7.refs_1_, bf16[1024,768]{1,0:T(8,128)(2,1)S(1)} %copy-done.12, bf16[1024,768]{1,0:T(8,128)(2,1)} %copy-done.15, bf16[1024,768]{1,0:T(8,128)(2,1)} %copy-done.77, ...), custom_call_target="tpu_custom_call" | custom-call | tf_op jit(solution)/shard_map/in_norm_back/pallas_call | solution.py:739
  546.7 8.6 %in_norm_back.2 = (bf16[512,1024]{1,0:T(8,128)(2,1)S(1)}, f32[8,1024]{1,0:T(8,128)S(1)}, f32[256,1024]{1,0:T(8,128)S(1)}) custom-call(bf16[1024,768]{1,0:T(8,128)(2,1)S(1)} %copy-done.14, bf16[1024,768]{1,0:T(8,128)(2,1)S(1)} %copy-done.18, bf16[1024,768]{1,0:T(8,128)(2,1)} %copy-done.11, bf16[1024,768]{1,0:T(8,128)(2,1)} %copy-done.15, ...), custom_call_target="tpu_custom_call" | custom-call | tf_op jit(solution)/shard_map/in_norm_back/pallas_call | solution.py:739
  559.9 3.5 multiply_subtract_fusion.1
  570.2 2.6 collective-permute-start.79
  585.0 8.1 %collective-permute-done.69 = bf16[128,1024]{1,0:T(8,128)(2,1)S(1)} collective-permute-done((bf16[128,1024]{1,0:T(8,128)(2,1)}, bf16[128,1024]{1,0:T(8,128)(2,1)S(1)}, u32[]{:S(2)}, u32[]{:S(2)}) %collective-permute-start.69) | collective-permute-done | bytes 262176 | tf_op jit(solution)/shard_map/ppermute | solution.py:368
  593.1 8.7 %collective-permute-done.70 = bf16[128,1024]{1,0:T(8,128)(2,1)} collective-permute-done((bf16[128,1024]{1,0:T(8,128)(2,1)}, bf16[128,1024]{1,0:T(8,128)(2,1)}, u32[]{:S(2)}, u32[]{:S(2)}) %collective-permute-start.70) | collective-permute-done | bytes 262176 | tf_op jit(solution)/shard_map/ppermute | solution.py:368
  614.7 3.1 spread_image.3
  (694 shorter events, 231.9 us)
Async XLA Ops:
  2.2 8.5 %collective-permute-start = (bf16[1,192]{1,0:T(2,128)(2,1)S(1)}, bf16[1,192]{1,0:T(2,128)(2,1)S(1)}, u32[]{:S(2)}, u32[]{:S(2)}) collective-permute-start(bf16[1,192]{1,0:T(2,128)(2,1)S(1)} %slice.459), channel_id=1, source_target_pairs={{0,1},{1,0},{2,3},{3,2},{4,5},{5,4},{6,7},{7,6},{8,9},{9,8},{10,11... | collective-permute-start | bytes 1160 | tf_op jit(solution)/shard_map/ppermute | solution.py:378
  10.5 25.6 %collective-permute-start.7 = (bf16[128,1280]{1,0:T(8,128)(2,1)}, bf16[128,1280]{1,0:T(8,128)(2,1)S(1)}, u32[]{:S(2)}, u32[]{:S(2)}) collective-permute-start(bf16[128,1280]{1,0:T(8,128)(2,1)} %pad_maximum_fusion.32), channel_id=1, source_target_pairs={{0,8},{4,12},{8,0},{12,4},{16,24},{20,28},{24,16},{28,20},{1,9},{5... | collective-permute-start | bytes 983048 | tf_op jit(solution)/shard_map/ppermute | solution.py:368
  16.1 20.0 %collective-permute-start.6 = (bf16[256,768]{1,0:T(8,128)(2,1)}, bf16[256,768]{1,0:T(8,128)(2,1)}, u32[]{:S(2)}, u32[]{:S(2)}) collective-permute-start(bf16[256,768]{1,0:T(8,128)(2,1)} %pad_maximum_fusion.31), channel_id=1, source_target_pairs={{0,16},{4,20},{8,24},{12,28},{16,0},{20,4},{24,8},{28,12},{1,17},{... | collective-permute-start | bytes 1179656 | tf_op jit(solution)/shard_map/ppermute | solution.py:368
  20.9 26.8 %collective-permute-start.10 = (bf16[2,256,1024]{2,1,0:T(8,128)(2,1)}, bf16[2,256,1024]{2,1,0:T(8,128)(2,1)}, u32[]{:S(2)}, u32[]{:S(2)}) collective-permute-start(bf16[2,256,1024]{2,1,0:T(8,128)(2,1)} %pad_maximum_fusion.6), channel_id=1, source_target_pairs={{0,2},{1,3},{2,0},{3,1},{4,6},{5,7},{6,4},{7,5},{8,10},{9,11},{10,... | collective-permute-start | bytes 3145736 | tf_op jit(solution)/shard_map/ppermute | solution.py:378
  38.0 9.7 %collective-permute-start.9 = (bf16[512,384]{1,0:T(8,128)(2,1)S(1)}, bf16[512,384]{1,0:T(8,128)(2,1)}, u32[]{:S(2)}, u32[]{:S(2)}) collective-permute-start(bf16[512,384]{1,0:T(8,128)(2,1)S(1)} %get-tuple-element.522), channel_id=1, source_target_pairs={{0,4},{4,0},{8,12},{12,8},{16,20},{20,16},{24,28},{28,24},{1,5},{5... | collective-permute-start | bytes 1179656 | tf_op jit(solution)/shard_map/ppermute | solution.py:374
  39.7 8.0 %collective-permute-start.8 = (bf16[4,1792]{1,0:T(4,128)(2,1)S(1)}, bf16[4,1792]{1,0:T(4,128)(2,1)S(1)}, u32[]{:S(2)}, u32[]{:S(2)}) collective-permute-start(bf16[4,1792]{1,0:T(4,128)(2,1)S(1)} %pad_maximum_fusion.40), channel_id=1, source_target_pairs={{0,4},{4,0},{8,12},{12,8},{16,20},{20,16},{24,28},{28,24},{1,5},{5... | collective-permute-start | bytes 43016 | tf_op jit(solution)/shard_map/ppermute | solution.py:374
  50.8 28.4 %collective-permute-start.12 = (bf16[1024,384]{1,0:T(8,128)(2,1)S(1)}, bf16[1024,384]{1,0:T(8,128)(2,1)S(1)}, u32[]{:S(2)}, u32[]{:S(2)}) collective-permute-start(bf16[1024,384]{1,0:T(8,128)(2,1)S(1)} %pad_maximum_fusion.18), channel_id=1, source_target_pairs={{0,2},{1,3},{2,0},{3,1},{4,6},{5,7},{6,4},{7,5},{8,10},{9,11},{10,... | collective-permute-start | bytes 2359304 | tf_op jit(solution)/shard_map/ppermute | solution.py:378
  52.2 27.0 %collective-permute-start.13 = (bf16[512,384]{1,0:T(8,128)(2,1)S(1)}, bf16[512,384]{1,0:T(8,128)(2,1)S(1)}, u32[]{:S(2)}, u32[]{:S(2)}) collective-permute-start(bf16[512,384]{1,0:T(8,128)(2,1)S(1)} %get-tuple-element.521), channel_id=1, source_target_pairs={{0,2},{1,3},{2,0},{3,1},{4,6},{5,7},{6,4},{7,5},{8,10},{9,11},{10,... | collective-permute-start | bytes 1179656 | tf_op jit(solution)/shard_map/ppermute | solution.py:378
  80.6 33.4 %collective-permute-start.14 = (bf16[1024,768]{1,0:T(8,128)(2,1)S(1)}, bf16[1024,768]{1,0:T(8,128)(2,1)}, u32[]{:S(2)}, u32[]{:S(2)}) collective-permute-start(bf16[1024,768]{1,0:T(8,128)(2,1)S(1)} %pad_maximum_fusion.4.refs_4_), channel_id=1, source_target_pairs={{0,1},{1,0},{2,3},{3,2},{4,5},{5,4},{6,7},{7,6},{8,9},{9,8},{10,11... | collective-permute-start | bytes 4718600 | tf_op jit(solution)/shard_map/ppermute | solution.py:378
  81.8 32.3 %collective-permute-start.16 = (bf16[256,1280]{1,0:T(8,128)(2,1)}, bf16[256,1280]{1,0:T(8,128)(2,1)}, u32[]{:S(2)}, u32[]{:S(2)}) collective-permute-start(bf16[256,1280]{1,0:T(8,128)(2,1)} %pad_maximum_fusion.20), channel_id=1, source_target_pairs={{0,16},{4,20},{8,24},{12,28},{16,0},{20,4},{24,8},{28,12},{1,17},{... | collective-permute-start | bytes 1966088 | tf_op jit(solution)/shard_map/ppermute | solution.py:368
  86.8 27.2 %collective-permute-start.15 = (bf16[512,768]{1,0:T(8,128)(2,1)}, bf16[512,768]{1,0:T(8,128)(2,1)}, u32[]{:S(2)}, u32[]{:S(2)}) collective-permute-start(bf16[512,768]{1,0:T(8,128)(2,1)} %pad_maximum_fusion.19), channel_id=1, source_target_pairs={{0,4},{4,0},{8,12},{12,8},{16,20},{20,16},{24,28},{28,24},{1,5},{5... | collective-permute-start | bytes 2359304 | tf_op jit(solution)/shard_map/ppermute | solution.py:374
  116.5 22.6 %collective-permute-start.17 = (bf16[1024,768]{1,0:T(8,128)(2,1)}, bf16[1024,768]{1,0:T(8,128)(2,1)}, u32[]{:S(2)}, u32[]{:S(2)}) collective-permute-start(bf16[1024,768]{1,0:T(8,128)(2,1)} %pad_maximum_fusion.5.refs_5_), channel_id=1, source_target_pairs={{0,1},{1,0},{2,3},{3,2},{4,5},{5,4},{6,7},{7,6},{8,9},{9,8},{10,11... | collective-permute-start | bytes 4718600 | tf_op jit(solution)/shard_map/ppermute | solution.py:378
  118.0 21.1 %collective-permute-start.19 = (bf16[512,512]{1,0:T(8,128)(2,1)S(1)}, bf16[512,512]{1,0:T(8,128)(2,1)S(1)}, u32[]{:S(2)}, u32[]{:S(2)}) collective-permute-start(bf16[512,512]{1,0:T(8,128)(2,1)S(1)} %get-tuple-element.489), channel_id=1, source_target_pairs={{0,2},{1,3},{2,0},{3,1},{4,6},{5,7},{6,4},{7,5},{8,10},{9,11},{10,... | collective-permute-start | bytes 1572872 | tf_op jit(solution)/shard_map/ppermute | solution.py:378
  119.5 19.7 %collective-permute-start.20 = (bf16[512,512]{1,0:T(8,128)(2,1)S(1)}, bf16[512,512]{1,0:T(8,128)(2,1)S(1)}, u32[]{:S(2)}, u32[]{:S(2)}) collective-permute-start(bf16[512,512]{1,0:T(8,128)(2,1)S(1)} %get-tuple-element.488), channel_id=1, source_target_pairs={{0,4},{4,0},{8,12},{12,8},{16,20},{20,16},{24,28},{28,24},{1,5},{5... | collective-permute-start | bytes 1572872 | tf_op jit(solution)/shard_map/ppermute | solution.py:374
  121.9 17.2 %collective-permute-start.18 = (bf16[2,512,128]{2,1,0:T(8,128)(2,1)S(1)}, bf16[2,512,128]{2,1,0:T(8,128)(2,1)S(1)}, u32[]{:S(2)}, u32[]{:S(2)}) collective-permute-start(bf16[2,512,128]{2,1,0:T(8,128)(2,1)S(1)} %pad_maximum_fusion.33), channel_id=1, source_target_pairs={{0,4},{4,0},{8,12},{12,8},{16,20},{20,16},{24,28},{28,24},{1,5},{5... | collective-permute-start | bytes 786440 | tf_op jit(solution)/shard_map/ppermute | solution.py:374
  122.5 16.6 %collective-permute-start.21 = (bf16[128,1024]{1,0:T(8,128)(2,1)S(1)}, bf16[128,1024]{1,0:T(8,128)(2,1)S(1)}, u32[]{:S(2)}, u32[]{:S(2)}) collective-permute-start(bf16[128,1024]{1,0:T(8,128)(2,1)S(1)} %copy-done.110), channel_id=1, source_target_pairs={{0,8},{4,12},{8,0},{12,4},{16,24},{20,28},{24,16},{28,20},{1,9},{5... | collective-permute-start | bytes 786440 | tf_op jit(solution)/shard_map/ppermute | solution.py:368
  140.4 20.2 %collective-permute-start.25 = (bf16[1024,256]{1,0:T(8,128)(2,1)}, bf16[1024,256]{1,0:T(8,128)(2,1)}, u32[]{:S(2)}, u32[]{:S(2)}) collective-permute-start(bf16[1024,256]{1,0:T(8,128)(2,1)} %get-tuple-element.514), channel_id=1, source_target_pairs={{0,2},{1,3},{2,0},{3,1},{4,6},{5,7},{6,4},{7,5},{8,10},{9,11},{10,... | collective-permute-start | bytes 1572872 | tf_op jit(solution)/shard_map/ppermute | solution.py:378
  142.2 18.4 %collective-permute-start.24 = (bf16[256,1024]{1,0:T(8,128)(2,1)}, bf16[256,1024]{1,0:T(8,128)(2,1)}, u32[]{:S(2)}, u32[]{:S(2)}) collective-permute-start(bf16[256,1024]{1,0:T(8,128)(2,1)} %get-tuple-element.516), channel_id=1, source_target_pairs={{0,4},{4,0},{8,12},{12,8},{16,20},{20,16},{24,28},{28,24},{1,5},{5... | collective-permute-start | bytes 1572872 | tf_op jit(solution)/shard_map/ppermute | solution.py:374
  144.5 25.1 %collective-permute-start.23 = (bf16[256,1024]{1,0:T(8,128)(2,1)}, bf16[256,1024]{1,0:T(8,128)(2,1)}, u32[]{:S(2)}, u32[]{:S(2)}) collective-permute-start(bf16[256,1024]{1,0:T(8,128)(2,1)} %pad_maximum_fusion.30), channel_id=1, source_target_pairs={{0,16},{4,20},{8,24},{12,28},{16,0},{20,4},{24,8},{28,12},{1,17},{... | collective-permute-start | bytes 1572872 | tf_op jit(solution)/shard_map/ppermute | solution.py:368
  145.4 24.3 %collective-permute-start.22 = (bf16[2,1024,128]{2,1,0:T(8,128)(2,1)}, bf16[2,1024,128]{2,1,0:T(8,128)(2,1)}, u32[]{:S(2)}, u32[]{:S(2)}) collective-permute-start(bf16[2,1024,128]{2,1,0:T(8,128)(2,1)} %pad_maximum_fusion.29), channel_id=1, source_target_pairs={{0,2},{1,3},{2,0},{3,1},{4,6},{5,7},{6,4},{7,5},{8,10},{9,11},{10,... | collective-permute-start | bytes 1572872 | tf_op jit(solution)/shard_map/ppermute | solution.py:378
  171.8 15.9 %collective-permute-start.28 = (bf16[2,1024,256]{2,1,0:T(8,128)(2,1)}, bf16[2,1024,256]{2,1,0:T(8,128)(2,1)}, u32[]{:S(2)}, u32[]{:S(2)}) collective-permute-start(bf16[2,1024,256]{2,1,0:T(8,128)(2,1)} %pad_maximum_fusion.8), channel_id=1, source_target_pairs={{0,1},{1,0},{2,3},{3,2},{4,5},{5,4},{6,7},{7,6},{8,9},{9,8},{10,11... | collective-permute-start | bytes 3145736 | tf_op jit(solution)/shard_map/ppermute | solution.py:378
  171.8 14.7 %collective-permute-start.27 = (bf16[1024,256]{1,0:T(8,128)(2,1)}, bf16[1024,256]{1,0:T(8,128)(2,1)}, u32[]{:S(2)}, u32[]{:S(2)}) collective-permute-start(bf16[1024,256]{1,0:T(8,128)(2,1)} %get-tuple-element.513), channel_id=1, source_target_pairs={{0,2},{1,3},{2,0},{3,1},{4,6},{5,7},{6,4},{7,5},{8,10},{9,11},{10,... | collective-permute-start | bytes 1572872 | tf_op jit(solution)/shard_map/ppermute | solution.py:378
  173.3 14.4 %collective-permute-start.26 = (bf16[256,1024]{1,0:T(8,128)(2,1)}, bf16[256,1024]{1,0:T(8,128)(2,1)}, u32[]{:S(2)}, u32[]{:S(2)}) collective-permute-start(bf16[256,1024]{1,0:T(8,128)(2,1)} %get-tuple-element.515), channel_id=1, source_target_pairs={{0,4},{4,0},{8,12},{12,8},{16,20},{20,16},{24,28},{28,24},{1,5},{5... | collective-permute-start | bytes 1572872 | tf_op jit(solution)/shard_map/ppermute | solution.py:374
  190.6 33.6 %collective-permute-start.30 = (bf16[1024,1024]{1,0:T(8,128)(2,1)}, bf16[1024,1024]{1,0:T(8,128)(2,1)}, u32[]{:S(2)}, u32[]{:S(2)}) collective-permute-start(bf16[1024,1024]{1,0:T(8,128)(2,1)} %pad_maximum_fusion.1.right_ref.refs_7_), channel_id=1, source_target_pairs={{0,1},{1,0},{2,3},{3,2},{4,5},{5,4},{6,7},{7,6},{8,9},{9,8},{10,11... | collective-permute-start | bytes 6291464 | tf_op jit(solution)/shard_map/ppermute | solution.py:378
  193.3 30.8 %collective-permute-start.29 = (bf16[1024,1024]{1,0:T(8,128)(2,1)}, bf16[1024,1024]{1,0:T(8,128)(2,1)}, u32[]{:S(2)}, u32[]{:S(2)}) collective-permute-start(bf16[1024,1024]{1,0:T(8,128)(2,1)} %pad_maximum_fusion.right_ref.refs_6_), channel_id=1, source_target_pairs={{0,1},{1,0},{2,3},{3,2},{4,5},{5,4},{6,7},{7,6},{8,9},{9,8},{10,11... | collective-permute-start | bytes 6291464 | tf_op jit(solution)/shard_map/ppermute | solution.py:378
  197.0 27.1 %collective-permute-start.31 = (bf16[512,512]{1,0:T(8,128)(2,1)S(1)}, bf16[512,512]{1,0:T(8,128)(2,1)S(1)}, u32[]{:S(2)}, u32[]{:S(2)}) collective-permute-start(bf16[512,512]{1,0:T(8,128)(2,1)S(1)} %get-tuple-element.508), channel_id=1, source_target_pairs={{0,2},{1,3},{2,0},{3,1},{4,6},{5,7},{6,4},{7,5},{8,10},{9,11},{10,... | collective-permute-start | bytes 1572872 | tf_op jit(solution)/shard_map/ppermute | solution.py:378
  197.6 26.5 %collective-permute-start.32 = (bf16[512,512]{1,0:T(8,128)(2,1)S(1)}, bf16[512,512]{1,0:T(8,128)(2,1)S(1)}, u32[]{:S(2)}, u32[]{:S(2)}) collective-permute-start(bf16[512,512]{1,0:T(8,128)(2,1)S(1)} %get-tuple-element.507), channel_id=1, source_target_pairs={{0,4},{4,0},{8,12},{12,8},{16,20},{20,16},{24,28},{28,24},{1,5},{5... | collective-permute-start | bytes 1572872 | tf_op jit(solution)/shard_map/ppermute | solution.py:374
  225.4 25.0 %collective-permute-start.34 = (bf16[1024,512]{1,0:T(8,128)(2,1)}, bf16[1024,512]{1,0:T(8,128)(2,1)}, u32[]{:S(2)}, u32[]{:S(2)}) collective-permute-start(bf16[1024,512]{1,0:T(8,128)(2,1)} %pad_maximum_fusion.10), channel_id=1, source_target_pairs={{0,2},{1,3},{2,0},{3,1},{4,6},{5,7},{6,4},{7,5},{8,10},{9,11},{10,... | collective-permute-start | bytes 3145736 | tf_op jit(solution)/shard_map/ppermute | solution.py:378
  227.9 24.7 %collective-permute-start.33 = (bf16[512,1024]{1,0:T(8,128)(2,1)}, bf16[512,1024]{1,0:T(8,128)(2,1)}, u32[]{:S(2)}, u32[]{:S(2)}) collective-permute-start(bf16[512,1024]{1,0:T(8,128)(2,1)} %pad_maximum_fusion.9), channel_id=1, source_target_pairs={{0,4},{4,0},{8,12},{12,8},{16,20},{20,16},{24,28},{28,24},{1,5},{5... | collective-permute-start | bytes 3145736 | tf_op jit(solution)/shard_map/ppermute | solution.py:374
  258.3 25.4 %collective-permute-start.37 = (bf16[2,256,1024]{2,1,0:T(8,128)(2,1)}, bf16[2,256,1024]{2,1,0:T(8,128)(2,1)}, u32[]{:S(2)}, u32[]{:S(2)}) collective-permute-start(bf16[2,256,1024]{2,1,0:T(8,128)(2,1)} %pad_maximum_fusion.11), channel_id=1, source_target_pairs={{0,2},{1,3},{2,0},{3,1},{4,6},{5,7},{6,4},{7,5},{8,10},{9,11},{10,... | collective-permute-start | bytes 3145736 | tf_op jit(solution)/shard_map/ppermute | solution.py:378
  297.5 18.1 %collective-permute-start.40 = (bf16[1024,1024]{1,0:T(8,128)(2,1)}, bf16[1024,1024]{1,0:T(8,128)(2,1)}, u32[]{:S(2)}, u32[]{:S(2)}) collective-permute-start(bf16[1024,1024]{1,0:T(8,128)(2,1)} %convolution_convert_fusion.2), channel_id=1, source_target_pairs={{0,1},{1,0},{2,3},{3,2},{4,5},{5,4},{6,7},{7,6},{8,9},{9,8},{10,11... | collective-permute-start | bytes 6291464 | tf_op jit(solution)/shard_map/ppermute | solution.py:378
  297.6 18.0 %collective-permute-start.39 = (bf16[1024,1024]{1,0:T(8,128)(2,1)}, bf16[1024,1024]{1,0:T(8,128)(2,1)}, u32[]{:S(2)}, u32[]{:S(2)}) collective-permute-start(bf16[1024,1024]{1,0:T(8,128)(2,1)} %convolution_convert_fusion.3), channel_id=1, source_target_pairs={{0,1},{1,0},{2,3},{3,2},{4,5},{5,4},{6,7},{7,6},{8,9},{9,8},{10,11... | collective-permute-start | bytes 6291464 | tf_op jit(solution)/shard_map/ppermute | solution.py:378
  319.3 25.9 %collective-permute-start.42 = (bf16[1024,256]{1,0:T(8,128)(2,1)}, bf16[1024,256]{1,0:T(8,128)(2,1)}, u32[]{:S(2)}, u32[]{:S(2)}) collective-permute-start(bf16[1024,256]{1,0:T(8,128)(2,1)} %get-tuple-element.479), channel_id=1, source_target_pairs={{0,2},{1,3},{2,0},{3,1},{4,6},{5,7},{6,4},{7,5},{8,10},{9,11},{10,... | collective-permute-start | bytes 1572872 | tf_op jit(solution)/shard_map/ppermute | solution.py:378
  324.8 20.4 %collective-permute-start.41 = (bf16[256,1024]{1,0:T(8,128)(2,1)}, bf16[256,1024]{1,0:T(8,128)(2,1)}, u32[]{:S(2)}, u32[]{:S(2)}) collective-permute-start(bf16[256,1024]{1,0:T(8,128)(2,1)} %get-tuple-element.481), channel_id=1, source_target_pairs={{0,4},{4,0},{8,12},{12,8},{16,20},{20,16},{24,28},{28,24},{1,5},{5... | collective-permute-start | bytes 1572872 | tf_op jit(solution)/shard_map/ppermute | solution.py:374
  338.6 21.8 %collective-permute-start.44 = (bf16[1024,256]{1,0:T(8,128)(2,1)}, bf16[1024,256]{1,0:T(8,128)(2,1)}, u32[]{:S(2)}, u32[]{:S(2)}) collective-permute-start(bf16[1024,256]{1,0:T(8,128)(2,1)} %get-tuple-element.478), channel_id=1, source_target_pairs={{0,2},{1,3},{2,0},{3,1},{4,6},{5,7},{6,4},{7,5},{8,10},{9,11},{10,... | collective-permute-start | bytes 1572872 | tf_op jit(solution)/shard_map/ppermute | solution.py:378
  339.8 20.6 %collective-permute-start.43 = (bf16[256,1024]{1,0:T(8,128)(2,1)}, bf16[256,1024]{1,0:T(8,128)(2,1)}, u32[]{:S(2)}, u32[]{:S(2)}) collective-permute-start(bf16[256,1024]{1,0:T(8,128)(2,1)} %get-tuple-element.480), channel_id=1, source_target_pairs={{0,4},{4,0},{8,12},{12,8},{16,20},{20,16},{24,28},{28,24},{1,5},{5... | collective-permute-start | bytes 1572872 | tf_op jit(solution)/shard_map/ppermute | solution.py:374
  341.9 53.4 %collective-permute-start.49 = (bf16[2,256,1024]{2,1,0:T(8,128)(2,1)}, bf16[2,256,1024]{2,1,0:T(8,128)(2,1)}, u32[]{:S(2)}, u32[]{:S(2)}) collective-permute-start(bf16[2,256,1024]{2,1,0:T(8,128)(2,1)} %bitcast.79), channel_id=1, source_target_pairs={{0,2},{1,3},{2,0},{3,1},{4,6},{5,7},{6,4},{7,5},{8,10},{9,11},{10,... | collective-permute-start | bytes 3145736 | tf_op jit(solution)/shard_map/ppermute | solution.py:378
  360.4 34.8 %collective-permute-start.46 = (bf16[1024,1024]{1,0:T(8,128)(2,1)}, bf16[1024,1024]{1,0:T(8,128)(2,1)}, u32[]{:S(2)}, u32[]{:S(2)}) collective-permute-start(bf16[1024,1024]{1,0:T(8,128)(2,1)} %convolution_convert_fusion), channel_id=1, source_target_pairs={{0,1},{1,0},{2,3},{3,2},{4,5},{5,4},{6,7},{7,6},{8,9},{9,8},{10,11... | collective-permute-start | bytes 6291464 | tf_op jit(solution)/shard_map/ppermute | solution.py:378
  360.5 34.7 %collective-permute-start.45 = (bf16[1024,1024]{1,0:T(8,128)(2,1)}, bf16[1024,1024]{1,0:T(8,128)(2,1)}, u32[]{:S(2)}, u32[]{:S(2)}) collective-permute-start(bf16[1024,1024]{1,0:T(8,128)(2,1)} %convolution_convert_fusion.1), channel_id=1, source_target_pairs={{0,1},{1,0},{2,3},{3,2},{4,5},{5,4},{6,7},{7,6},{8,9},{9,8},{10,11... | collective-permute-start | bytes 6291464 | tf_op jit(solution)/shard_map/ppermute | solution.py:378
  363.5 31.7 %collective-permute-start.48 = (bf16[512,512]{1,0:T(8,128)(2,1)}, bf16[512,512]{1,0:T(8,128)(2,1)}, u32[]{:S(2)}, u32[]{:S(2)}) collective-permute-start(bf16[512,512]{1,0:T(8,128)(2,1)} %slice.478), channel_id=1, source_target_pairs={{0,4},{4,0},{8,12},{12,8},{16,20},{20,16},{24,28},{28,24},{1,5},{5... | collective-permute-start | bytes 1572872 | tf_op jit(solution)/shard_map/ppermute | solution.py:374
  367.4 27.9 %collective-permute-start.47 = (bf16[512,512]{1,0:T(8,128)(2,1)}, bf16[512,512]{1,0:T(8,128)(2,1)}, u32[]{:S(2)}, u32[]{:S(2)}) collective-permute-start(bf16[512,512]{1,0:T(8,128)(2,1)} %slice.476), channel_id=1, source_target_pairs={{0,2},{1,3},{2,0},{3,1},{4,6},{5,7},{6,4},{7,5},{8,10},{9,11},{10,... | collective-permute-start | bytes 1572872 | tf_op jit(solution)/shard_map/ppermute | solution.py:378
  406.4 30.6 %collective-permute-start.54 = (bf16[2,256,1024]{2,1,0:T(8,128)(2,1)S(1)}, bf16[2,256,1024]{2,1,0:T(8,128)(2,1)S(1)}, u32[]{:S(2)}, u32[]{:S(2)}) collective-permute-start(bf16[2,256,1024]{2,1,0:T(8,128)(2,1)S(1)} %pad_maximum_fusion.14), channel_id=1, source_target_pairs={{0,1},{1,0},{2,3},{3,2},{4,5},{5,4},{6,7},{7,6},{8,9},{9,8},{10,11... | collective-permute-start | bytes 3145736 | tf_op jit(solution)/shard_map/ppermute | solution.py:378
  409.1 28.0 %collective-permute-start.53 = (bf16[256,1024]{1,0:T(8,128)(2,1)S(1)}, bf16[256,1024]{1,0:T(8,128)(2,1)S(1)}, u32[]{:S(2)}, u32[]{:S(2)}) collective-permute-start(bf16[256,1024]{1,0:T(8,128)(2,1)S(1)} %fusion.7), channel_id=1, source_target_pairs={{0,16},{4,20},{8,24},{12,28},{16,0},{20,4},{24,8},{28,12},{1,17},{... | collective-permute-start | bytes 1572872 | tf_op jit(solution)/shard_map/ppermute | solution.py:368
  409.3 27.8 %collective-permute-start.52 = (bf16[2,1024,256]{2,1,0:T(8,128)(2,1)S(1)}, bf16[2,1024,256]{2,1,0:T(8,128)(2,1)S(1)}, u32[]{:S(2)}, u32[]{:S(2)}) collective-permute-start(bf16[2,1024,256]{2,1,0:T(8,128)(2,1)S(1)} %pad_maximum_fusion.13), channel_id=1, source_target_pairs={{0,1},{1,0},{2,3},{3,2},{4,5},{5,4},{6,7},{7,6},{8,9},{9,8},{10,11... | collective-permute-start | bytes 3145736 | tf_op jit(solution)/shard_map/ppermute | solution.py:378
  412.4 25.3 %collective-permute-start.51 = (bf16[1024,512]{1,0:T(8,128)(2,1)S(1)}, bf16[1024,512]{1,0:T(8,128)(2,1)S(1)}, u32[]{:S(2)}, u32[]{:S(2)}) collective-permute-start(bf16[1024,512]{1,0:T(8,128)(2,1)S(1)} %slice.480), channel_id=1, source_target_pairs={{0,2},{1,3},{2,0},{3,1},{4,6},{5,7},{6,4},{7,5},{8,10},{9,11},{10,... | collective-permute-start | bytes 3145736 | tf_op jit(solution)/shard_map/ppermute | solution.py:378
  416.0 25.0 %collective-permute-start.50 = (bf16[512,1024]{1,0:T(8,128)(2,1)S(1)}, bf16[512,1024]{1,0:T(8,128)(2,1)S(1)}, u32[]{:S(2)}, u32[]{:S(2)}) collective-permute-start(bf16[512,1024]{1,0:T(8,128)(2,1)S(1)} %slice.479), channel_id=1, source_target_pairs={{0,4},{4,0},{8,12},{12,8},{16,20},{20,16},{24,28},{28,24},{1,5},{5... | collective-permute-start | bytes 3145736 | tf_op jit(solution)/shard_map/ppermute | solution.py:374
  441.1 26.9 %collective-permute-start.59 = (bf16[128,1024]{1,0:T(8,128)(2,1)S(1)}, bf16[128,1024]{1,0:T(8,128)(2,1)S(1)}, u32[]{:S(2)}, u32[]{:S(2)}) collective-permute-start(bf16[128,1024]{1,0:T(8,128)(2,1)S(1)} %slice.490), channel_id=1, source_target_pairs={{0,8},{4,12},{8,0},{12,4},{16,24},{20,28},{24,16},{28,20},{1,9},{5... | collective-permute-start | bytes 786440 | tf_op jit(solution)/shard_map/ppermute | solution.py:368
  443.0 27.3 %collective-permute-start.55 = (bf16[1024,768]{1,0:T(8,128)(2,1)S(1)}, bf16[1024,768]{1,0:T(8,128)(2,1)S(1)}, u32[]{:S(2)}, u32[]{:S(2)}) collective-permute-start(bf16[1024,768]{1,0:T(8,128)(2,1)S(1)} %convolution_convert_fusion.7), channel_id=1, source_target_pairs={{0,1},{1,0},{2,3},{3,2},{4,5},{5,4},{6,7},{7,6},{8,9},{9,8},{10,11... | collective-permute-start | bytes 4718600 | tf_op jit(solution)/shard_map/ppermute | solution.py:378
  443.4 24.6 %collective-permute-start.58 = (bf16[512,512]{1,0:T(8,128)(2,1)S(1)}, bf16[512,512]{1,0:T(8,128)(2,1)S(1)}, u32[]{:S(2)}, u32[]{:S(2)}) collective-permute-start(bf16[512,512]{1,0:T(8,128)(2,1)S(1)} %slice.489), channel_id=1, source_target_pairs={{0,4},{4,0},{8,12},{12,8},{16,20},{20,16},{24,28},{28,24},{1,5},{5... | collective-permute-start | bytes 1572872 | tf_op jit(solution)/shard_map/ppermute | solution.py:374
  444.9 23.1 %collective-permute-start.57 = (bf16[512,512]{1,0:T(8,128)(2,1)S(1)}, bf16[512,512]{1,0:T(8,128)(2,1)S(1)}, u32[]{:S(2)}, u32[]{:S(2)}) collective-permute-start(bf16[512,512]{1,0:T(8,128)(2,1)S(1)} %slice.487), channel_id=1, source_target_pairs={{0,2},{1,3},{2,0},{3,1},{4,6},{5,7},{6,4},{7,5},{8,10},{9,11},{10,... | collective-permute-start | bytes 1572872 | tf_op jit(solution)/shard_map/ppermute | solution.py:378
  446.5 23.8 %collective-permute-start.56 = (bf16[2,1024,128]{2,1,0:T(8,128)(2,1)S(1)}, bf16[2,1024,128]{2,1,0:T(8,128)(2,1)S(1)}, u32[]{:S(2)}, u32[]{:S(2)}) collective-permute-start(bf16[2,1024,128]{2,1,0:T(8,128)(2,1)S(1)} %slice.485), channel_id=1, source_target_pairs={{0,2},{1,3},{2,0},{3,1},{4,6},{5,7},{6,4},{7,5},{8,10},{9,11},{10,... | collective-permute-start | bytes 1572872 | tf_op jit(solution)/shard_map/ppermute | solution.py:378
  470.8 22.8 %collective-permute-start.61 = (bf16[1024,384]{1,0:T(8,128)(2,1)S(1)}, bf16[1024,384]{1,0:T(8,128)(2,1)S(1)}, u32[]{:S(2)}, u32[]{:S(2)}) collective-permute-start(bf16[1024,384]{1,0:T(8,128)(2,1)S(1)} %slice.493), channel_id=1, source_target_pairs={{0,2},{1,3},{2,0},{3,1},{4,6},{5,7},{6,4},{7,5},{8,10},{9,11},{10,... | collective-permute-start | bytes 2359304 | tf_op jit(solution)/shard_map/ppermute | solution.py:378
  473.0 20.6 %collective-permute-start.60 = (bf16[2,512,128]{2,1,0:T(8,128)(2,1)S(1)}, bf16[2,512,128]{2,1,0:T(8,128)(2,1)S(1)}, u32[]{:S(2)}, u32[]{:S(2)}) collective-permute-start(bf16[2,512,128]{2,1,0:T(8,128)(2,1)S(1)} %slice.492), channel_id=1, source_target_pairs={{0,4},{4,0},{8,12},{12,8},{16,20},{20,16},{24,28},{28,24},{1,5},{5... | collective-permute-start | bytes 786440 | tf_op jit(solution)/shard_map/ppermute | solution.py:374
  493.7 27.7 %collective-permute-start.63 = (bf16[1024,768]{1,0:T(8,128)(2,1)}, bf16[1024,768]{1,0:T(8,128)(2,1)}, u32[]{:S(2)}, u32[]{:S(2)}) collective-permute-start(bf16[1024,768]{1,0:T(8,128)(2,1)} %convolution_convert_fusion.6), channel_id=1, source_target_pairs={{0,1},{1,0},{2,3},{3,2},{4,5},{5,4},{6,7},{7,6},{8,9},{9,8},{10,11... | collective-permute-start | bytes 4718600 | tf_op jit(solution)/shard_map/ppermute | solution.py:378
  494.8 26.5 %collective-permute-start.64 = (bf16[256,1024]{1,0:T(8,128)(2,1)}, bf16[256,1024]{1,0:T(8,128)(2,1)}, u32[]{:S(2)}, u32[]{:S(2)}) collective-permute-start(bf16[256,1024]{1,0:T(8,128)(2,1)} %fusion.6), channel_id=1, source_target_pairs={{0,16},{4,20},{8,24},{12,28},{16,0},{20,4},{24,8},{28,12},{1,17},{... | collective-permute-start | bytes 1572872 | tf_op jit(solution)/shard_map/ppermute | solution.py:368
  502.2 19.1 %collective-permute-start.62 = (bf16[512,384]{1,0:T(8,128)(2,1)S(1)}, bf16[512,384]{1,0:T(8,128)(2,1)S(1)}, u32[]{:S(2)}, u32[]{:S(2)}) collective-permute-start(bf16[512,384]{1,0:T(8,128)(2,1)S(1)} %slice.495), channel_id=1, source_target_pairs={{0,4},{4,0},{8,12},{12,8},{16,20},{20,16},{24,28},{28,24},{1,5},{5... | collective-permute-start | bytes 1179656 | tf_op jit(solution)/shard_map/ppermute | solution.py:374
  524.3 19.7 %collective-permute-start.65 = (bf16[512,768]{1,0:T(8,128)(2,1)}, bf16[512,768]{1,0:T(8,128)(2,1)}, u32[]{:S(2)}, u32[]{:S(2)}) collective-permute-start(bf16[512,768]{1,0:T(8,128)(2,1)} %slice.500), channel_id=1, source_target_pairs={{0,4},{4,0},{8,12},{12,8},{16,20},{20,16},{24,28},{28,24},{1,5},{5... | collective-permute-start | bytes 2359304 | tf_op jit(solution)/shard_map/ppermute | solution.py:374
  526.5 13.7 %collective-permute-start.72 = (bf16[128,1024]{1,0:T(8,128)(2,1)S(1)}, bf16[128,1024]{1,0:T(8,128)(2,1)S(1)}, u32[]{:S(2)}, u32[]{:S(2)}) collective-permute-start(bf16[128,1024]{1,0:T(8,128)(2,1)S(1)} %slice.517), channel_id=1, source_target_pairs={{0,8},{4,12},{8,0},{12,4},{16,24},{20,28},{24,16},{28,20},{1,9},{5... | collective-permute-start | bytes 786440 | tf_op jit(solution)/shard_map/ppermute | solution.py:368
  538.4 37.2 %collective-permute-start.66 = (bf16[2,256,1024]{2,1,0:T(8,128)(2,1)}, bf16[2,256,1024]{2,1,0:T(8,128)(2,1)}, u32[]{:S(2)}, u32[]{:S(2)}) collective-permute-start(bf16[2,256,1024]{2,1,0:T(8,128)(2,1)} %bitcast.91), channel_id=1, source_target_pairs={{0,2},{1,3},{2,0},{3,1},{4,6},{5,7},{6,4},{7,5},{8,10},{9,11},{10,... | collective-permute-start | bytes 3145736 | tf_op jit(solution)/shard_map/ppermute | solution.py:378
  567.0 11.1 %collective-permute-start.68 = (bf16[512,384]{1,0:T(8,128)(2,1)S(1)}, bf16[512,384]{1,0:T(8,128)(2,1)S(1)}, u32[]{:S(2)}, u32[]{:S(2)}) collective-permute-start(bf16[512,384]{1,0:T(8,128)(2,1)S(1)} %slice.506), channel_id=1, source_target_pairs={{0,2},{1,3},{2,0},{3,1},{4,6},{5,7},{6,4},{7,5},{8,10},{9,11},{10,... | collective-permute-start | bytes 1179656 | tf_op jit(solution)/shard_map/ppermute | solution.py:378
  578.0 35.4 %collective-permute-start.67 = (bf16[2,256,1024]{2,1,0:T(8,128)(2,1)}, bf16[2,256,1024]{2,1,0:T(8,128)(2,1)}, u32[]{:S(2)}, u32[]{:S(2)}) collective-permute-start(bf16[2,256,1024]{2,1,0:T(8,128)(2,1)} %pad_maximum_fusion.15), channel_id=1, source_target_pairs={{0,1},{1,0},{2,3},{3,2},{4,5},{5,4},{6,7},{7,6},{8,9},{9,8},{10,11... | collective-permute-start | bytes 3145736 | tf_op jit(solution)/shard_map/ppermute | solution.py:378
  579.3 13.8 %collective-permute-start.69 = (bf16[128,1024]{1,0:T(8,128)(2,1)}, bf16[128,1024]{1,0:T(8,128)(2,1)S(1)}, u32[]{:S(2)}, u32[]{:S(2)}) collective-permute-start(bf16[128,1024]{1,0:T(8,128)(2,1)} %get-tuple-element.494), channel_id=1, source_target_pairs={{0,8},{4,12},{8,0},{12,4},{16,24},{20,28},{24,16},{28,20},{1,9},{5... | collective-permute-start | bytes 786440 | tf_op jit(solution)/shard_map/ppermute | solution.py:368
  580.2 21.6 %collective-permute-start.70 = (bf16[128,1024]{1,0:T(8,128)(2,1)}, bf16[128,1024]{1,0:T(8,128)(2,1)}, u32[]{:S(2)}, u32[]{:S(2)}) collective-permute-start(bf16[128,1024]{1,0:T(8,128)(2,1)} %get-tuple-element.493), channel_id=1, source_target_pairs={{0,16},{4,20},{8,24},{12,28},{16,0},{20,4},{24,8},{28,12},{1,17},{... | collective-permute-start | bytes 786440 | tf_op jit(solution)/shard_map/ppermute | solution.py:368
  582.4 19.4 %collective-permute-start.71 = (bf16[128,1024]{1,0:T(8,128)(2,1)}, bf16[128,1024]{1,0:T(8,128)(2,1)}, u32[]{:S(2)}, u32[]{:S(2)}) collective-permute-start(bf16[128,1024]{1,0:T(8,128)(2,1)} %get-tuple-element.492), channel_id=1, source_target_pairs={{0,24},{4,28},{8,16},{12,20},{16,8},{20,12},{24,0},{28,4},{1,25},{... | collective-permute-start | bytes 786440 | tf_op jit(solution)/shard_map/ppermute | solution.py:368
  (172 other events, 1248.6 us)

commit v8 on v7

--- a/solution.py
+++ b/solution.py
@@ -957,7 +957,10 @@
     bias_full = bias_full.astype(F32)
 
     base, normed_one = assemble_image(place, vector_full, tokens[:, 0], fetch_tokens.result, True)
-    normed_one = meet(normed_one, *get_qkv)
+    normed_one, down_shard = meet((normed_one, down_shard), *get_qkv, rows_up)
+    out_rows, up_rows = jnp.split(rows_up.result, [block_width], 1)
+    get_out = Chain(gather_steps, [jnp.stack(jnp.split(out_rows, 2, 1))], ("yx",))
+    get_up = Chain(gather_steps, jnp.split(up_rows, 2, 1), both, (1, 2))
 
     def project(core, half, weight):
         lanes = slice(half * LANES, (half + 1) * LANES)
@@ -973,11 +976,8 @@
     heads[0][0] = project(0, 0, get_qkv[0].own[0])
     forward_heads(0, 0)
     blended[0][0], normed_one, down_shard = meet(
-        (blended[0][0], normed_one, down_shard), *get_qkv, rows_up
-    )
-    out_rows, up_rows = jnp.split(rows_up.result, [block_width], 1)
-    get_out = Chain(gather_steps, [jnp.stack(jnp.split(out_rows, 2, 1))], ("yx",))
-    get_up = Chain(gather_steps, jnp.split(up_rows, 2, 1), both, (1, 2))
+        (blended[0][0], normed_one, down_shard), *get_qkv, get_out, get_up
+    )
     rows_down = Chain(rows_z_steps, down_shard)
     heads[0][1] = project(0, 1, get_qkv[1].own[0])
     forward_heads(0, 1)
@@ -993,7 +993,7 @@
     get_down = Chain(gather_steps, jnp.split(rows_down.result, 2, 1), both)
     heads[1][1] = project(1, 1, w_qkv[1][1])
     forward_heads(1, 1)
-    blended = meet(blended, get_up, get_out)
+    blended = meet(blended, get_up, get_down)
     w_out = [[each[0][half] for half in (0, 1)] for each in (get_out.own, get_out.result)]
     pairs = [(core, half) for core in cores for half in (0, 1)]
     branch_one, hidden, normed_two = row_call(
@@ -1013,12 +1013,11 @@
             unit_bias = rows.transpose(1, 0, 2).reshape(-1)
             activ[half, core], slope[half, core] = expand(normed_two, weights[half], unit_bias)
 
-    expand_units(0, get_up.own)
-    activ, normed_two = meet((activ, normed_two), get_up, get_down)
     w_up = [get_up.own, get_up.result]
+    expand_units(0, w_up[0])
+    activ, normed_two, cotangent = meet((activ, normed_two, cotangent), get_down)
+    fetch_cotangent = fetch_image(cotangent)
     expand_units(1, w_up[1])
-    activ, slope, cotangent = meet((activ, slope, cotangent), get_down)
-    fetch_cotangent = fetch_image(cotangent)
     activ = meet(activ, get_down)
     w_down = [get_down.own, get_down.result]
     parts = [(half, core) for core in (1, 0) for half in (0, 1)]
@@ -1115,6 +1114,7 @@
     )
     grad_heads = meet(grad_heads, sum_qkv[1])
     near, sums_near, own_grad = input_back((0, 1), [BF, "sums", "own"])
+    near, sums_near, own_grad = meet((near, sums_near, own_grad), sum_qkv[1])
     grad_near.append(near)
     sums_input = sums_far + sums_near
 
@@ -1144,7 +1144,6 @@
     grad_biases = jnp.stack(bias_parts, 1).reshape(MP, -1, DP, bias_width).transpose(0, 2, 1, 3)
     grad_biases = jnp.take(grad_biases, place[:DP], axis=1).reshape(MP, DP, -1)
     sum_small = Chain(small_reduce_steps, grad_vectors, grad_biases)
-    meet((), sum_qkv[1])
     rows_qkv = Chain(sum_z_steps, jnp.concatenate(sum_qkv[0].result + sum_qkv[1].result + [out_rows], 1))
     meet((), rows_up)
     meet((), send_grad)

time: 625 us -> 633 us (1.013)
  other arithmetic: 86 us -> 95.1 us
  waiting for transfers between devices: 111 us -> 103 us
  Pallas kernels: 209 us -> 216 us
  starting transfers between devices: 75.2 us -> 68.5 us
    ppermute x44, waiting for transfers between devices: 41.5 us -> 14.7 us  [swap_mp(): return lax.ppermute(part, 'mp', [(each, each ^ step) for each in range(MP)])]
    ppermute x18, waiting for transfers between devices: 15.1 us -> 29.1 us  [swap_y(): return lax.ppermute(part, 'dp', [(each, each ^ 1) for each in range(DP)])]
    concatenate x14, other arithmetic: 24 us -> 31.3 us  [join(): return jnp.concatenate([rows, arrived], -2 if axis == 'y' else -1)]
    pallas_call x4, Pallas kernels: 12.9 us -> 19.8 us  [slope_product(): pl.pallas_call(slope_kernel, grid=(rows // 256,), in_specs=[pl.BlockSpec(...]
    unnamed x334 -> x300, local copies, waits for them, and re-layouts: 43.6 us -> 44 us
  transfers between devices with their start and end apart: 80 -> 80, of which waited for: 26 -> 17; matrix products, arithmetic and copies ran while one was open for 24% -> 25% of each run, Pallas kernels for 33% -> 34%
where the time goes in v8:
time: 633 us; the launch traced here: 626 us
  Pallas kernels  216 us (34%)
  waiting for transfers between devices  103 us (16%)
  other arithmetic  95.1 us (15%)
  local copies, waits for them, and re-layouts  81.3 us (13%)
  starting transfers between devices  68.5 us (11%)
  matrix products  58.9 us (9%)
    pallas_call x4, Pallas kernels, attend_back(): pl.pallas_call(functools.partial(attend_back_kernel, 256), grid=(pairs,),...  63.6 us
    pallas_call x5, Pallas kernels, row_call(): pl.pallas_call(functools.partial(kernel, len(lefts)), grid=(count,), in_s...  60.8 us
    ppermute x18, waiting for transfers between devices, swap_z(): lax.ppermute(part, 'dp', [(z * YS + y, (z ^ step) * YS + y) for z in rang...  59.2 us
    unnamed x300, local copies, waits for them, and re-layouts  44 us
    dot_general x16, matrix products, dot_tn(): lax.dot_general(left, right, (((0,), (0,)), ((), ())), preferred_element_...  36.6 us
    pallas_call x4, Pallas kernels, attend(): pl.pallas_call(functools.partial(attend_kernel, 256), grid=(pairs,), in_s...  36.1 us
    concatenate x14, other arithmetic, join(): return jnp.concatenate([rows, arrived], -2 if axis == 'y' else -1)  31.3 us
    ppermute x18, waiting for transfers between devices, swap_y(): return lax.ppermute(part, 'dp', [(each, each ^ 1) for each in range(DP)])  29.1 us
  transfers between devices with their start and end apart: 80, of which 17 were waited for; matrix products, arithmetic and copies ran while one was open for 25% of the time, Pallas kernels for 34%

profile of v8, /device:TPU:0, one launch (start us, length us, event | category | flops | bytes accessed | tf_op | source)
XLA Modules:
  0.0 625.8 jit_solution(10470806002436588479)
XLA Ops:
  2.8 2.6 collective-permute-start.1
  10.7 4.7 collective-permute-done.3
  19.0 2.6 collective-permute-start.6
  25.8 12.9 %collective-permute-done.5 = bf16[2,1792]{1,0:T(2,128)(2,1)S(1)} collective-permute-done((bf16[2,1792]{1,0:T(2,128)(2,1)S(1)}, bf16[2,1792]{1,0:T(2,128)(2,1)S(1)}, u32[]{:S(2)}, u32[]{:S(2)}) %collective-permute-start.5) | collective-permute-done | bytes 7200 | tf_op jit(solution)/shard_map/ppermute | solution.py:368
  60.1 3.2 assemble_image.2
  66.0 20.8 %collective-permute-done.14 = bf16[256,1280]{1,0:T(8,128)(2,1)} collective-permute-done((bf16[256,1280]{1,0:T(8,128)(2,1)}, bf16[256,1280]{1,0:T(8,128)(2,1)}, u32[]{:S(2)}, u32[]{:S(2)}) %collective-permute-start.14) | collective-permute-done | bytes 655392 | tf_op jit(solution)/shard_map/ppermute | solution.py:368
  86.8 2.6 pad_maximum_fusion.4.refs_4_
  97.2 3.0 add_convert_fusion.9.q_ref.k_ref.v_ref
  100.2 8.8 %attend.4 = (bf16[1024,256]{1,0:T(8,128)(2,1)S(1)}, f32[2,8,1024]{2,1,0:T(8,128)S(1)}) custom-call(bf16[1024,768]{1,0:T(8,128)(2,1)S(1)} %add_convert_fusion.9.q_ref.k_ref.v_ref, bf16[1024,768]{1,0:T(8,128)(2,1)S(1)} %add_convert_fusion.9.q_ref.k_ref.v_ref, bf16[1024,768]{1,0:T(8,128)(2,1)S(1)} %add_convert_fusion.9.q_ref.k_ref.v_ref), custom_call_target="tpu_custom_call" | custom-call | tf_op jit(solution)/shard_map/attend/pallas_call | solution.py:833
  109.1 18.6 %collective-permute-done.17 = bf16[2,512,128]{2,1,0:T(8,128)(2,1)S(1)} collective-permute-done((bf16[2,512,128]{2,1,0:T(8,128)(2,1)S(1)}, bf16[2,512,128]{2,1,0:T(8,128)(2,1)S(1)}, u32[]{:S(2)}, u32[]{:S(2)}) %collective-permute-start.17) | collective-permute-done | bytes 262176 | tf_op jit(solution)/shard_map/ppermute | solution.py:374
  127.8 2.6 pad_maximum_fusion.5.refs_5_
  137.0 3.8 add_convert_fusion.8.q_ref.k_ref.v_ref
  140.8 9.4 %attend.5 = (bf16[1024,256]{1,0:T(8,128)(2,1)S(1)}, f32[2,8,1024]{2,1,0:T(8,128)S(1)}) custom-call(bf16[1024,768]{1,0:T(8,128)(2,1)S(1)} %add_convert_fusion.8.q_ref.k_ref.v_ref, bf16[1024,768]{1,0:T(8,128)(2,1)S(1)} %add_convert_fusion.8.q_ref.k_ref.v_ref, bf16[1024,768]{1,0:T(8,128)(2,1)S(1)} %add_convert_fusion.8.q_ref.k_ref.v_ref), custom_call_target="tpu_custom_call" | custom-call | tf_op jit(solution)/shard_map/attend/pallas_call | solution.py:833
  151.0 6.3 %collective-permute-done.21 = bf16[2,1024,128]{2,1,0:T(8,128)(2,1)} collective-permute-done((bf16[2,1024,128]{2,1,0:T(8,128)(2,1)}, bf16[2,1024,128]{2,1,0:T(8,128)(2,1)}, u32[]{:S(2)}, u32[]{:S(2)}) %collective-permute-start.21) | collective-permute-done | bytes 524320 | tf_op jit(solution)/shard_map/ppermute | solution.py:378
  163.3 3.8 add_convert_fusion.7.q_ref.k_ref.v_ref
  167.2 9.0 %attend.6 = (bf16[1024,256]{1,0:T(8,128)(2,1)S(1)}, f32[2,8,1024]{2,1,0:T(8,128)S(1)}) custom-call(bf16[1024,768]{1,0:T(8,128)(2,1)S(1)} %add_convert_fusion.7.q_ref.k_ref.v_ref, bf16[1024,768]{1,0:T(8,128)(2,1)S(1)} %add_convert_fusion.7.q_ref.k_ref.v_ref, bf16[1024,768]{1,0:T(8,128)(2,1)S(1)} %add_convert_fusion.7.q_ref.k_ref.v_ref), custom_call_target="tpu_custom_call" | custom-call | tf_op jit(solution)/shard_map/attend/pallas_call | solution.py:833
  176.2 11.8 %collective-permute-done.26 = bf16[256,1024]{1,0:T(8,128)(2,1)} collective-permute-done((bf16[256,1024]{1,0:T(8,128)(2,1)}, bf16[256,1024]{1,0:T(8,128)(2,1)}, u32[]{:S(2)}, u32[]{:S(2)}) %collective-permute-start.26) | collective-permute-done | bytes 524320 | tf_op jit(solution)/shard_map/ppermute | solution.py:368
  188.1 2.9 pad_maximum_fusion.1.right_ref.refs_7_
  191.1 2.8 pad_maximum_fusion.right_ref.refs_6_
  199.4 3.8 add_convert_fusion.6.q_ref.k_ref.v_ref
  203.3 8.8 %attend.7 = (bf16[1024,256]{1,0:T(8,128)(2,1)S(1)}, f32[2,8,1024]{2,1,0:T(8,128)S(1)}) custom-call(bf16[1024,768]{1,0:T(8,128)(2,1)S(1)} %add_convert_fusion.6.q_ref.k_ref.v_ref, bf16[1024,768]{1,0:T(8,128)(2,1)S(1)} %add_convert_fusion.6.q_ref.k_ref.v_ref, bf16[1024,768]{1,0:T(8,128)(2,1)S(1)} %add_convert_fusion.6.q_ref.k_ref.v_ref), custom_call_target="tpu_custom_call" | custom-call | tf_op jit(solution)/shard_map/attend/pallas_call | solution.py:833
  221.8 6.9 %out_norm.1 = (f32[1024,1024]{1,0:T(8,128)}, f32[1024,1024]{1,0:T(8,128)}, bf16[1024,1024]{1,0:T(8,128)(2,1)}) custom-call(bf16[1024,256]{1,0:T(8,128)(2,1)S(1)} %copy-done.53, bf16[1024,256]{1,0:T(8,128)(2,1)S(1)} %copy-done.56, bf16[1024,256]{1,0:T(8,128)(2,1)S(1)} %copy-done.59, bf16[1024,256]{1,0:T(8,128)(2,1)S(1)} %copy-done.62, ...), custom_call_target="tpu_custom_call" | custom-call | tf_op jit(solution)/shard_map/out_norm/pallas_call | solution.py:739
  230.2 6.0 expand.5
  238.8 6.0 expand.4
  244.9 4.7 pad_maximum_fusion.3.refs_7_.right_ref
  249.6 3.1 pad_maximum_fusion.2.refs_6_.right_ref
  258.3 6.0 expand.7
  266.9 6.0 expand.6
  274.3 15.7 %down_output.1 = (bf16[1024,1024]{1,0:T(8,128)(2,1)S(1)}, f32[1024,1024]{1,0:T(8,128)}) custom-call(bf16[1024,1024]{1,0:T(8,128)(2,1)S(1)} %get-tuple-element.265.refs_0_, bf16[1024,1024]{1,0:T(8,128)(2,1)} %copy-done.36, bf16[1024,1024]{1,0:T(8,128)(2,1)} %copy-done.30, bf16[1024,1024]{1,0:T(8,128)(2,1)} %copy-done.28, ...), custom_call_target="tpu_custom_call" | custom-call | tf_op jit(solution)/shard_map/down_output/pallas_call | solution.py:739
  292.3 2.6 collective-permute-done.38
  297.3 3.7 convolution_convert_fusion.2
  301.0 3.7 convolution_convert_fusion.3
  314.5 2.9 multiply_reduce_fusion
  320.4 2.4 fusion.38
  322.8 2.6 add_convert_fusion.2
  327.1 2.7 add_convert_fusion.3
  332.6 4.8 slope_product.6
  338.7 5.0 slope_product.5
  345.1 5.0 slope_product.4
  358.3 5.0 slope_product.7
  364.6 3.7 convolution_convert_fusion
  368.3 3.8 convolution_convert_fusion.1
  382.2 20.2 %up_norm_back.1 = (f32[1024,1024]{1,0:T(8,128)}, bf16[1024,1024]{1,0:T(8,128)(2,1)S(1)}, f32[8,1024]{1,0:T(8,128)S(1)}) custom-call(bf16[1024,1024]{1,0:T(8,128)(2,1)S(1)} %copy-done.47, bf16[1024,1024]{1,0:T(8,128)(2,1)} %copy-done.43, bf16[1024,1024]{1,0:T(8,128)(2,1)} %copy-done.41, bf16[1024,1024]{1,0:T(8,128)(2,1)} %copy-done.48, ...), custom_call_target="tpu_custom_call" | custom-call | tf_op jit(solution)/shard_map/up_norm_back/pallas_call | solution.py:739
  410.9 2.5 convolution_convert_fusion.13.g_ref
  421.7 2.6 add_convert_fusion
  425.0 2.6 add_convert_fusion.1
  430.9 15.9 %attend_back.4.refs_2_ = bf16[1024,768]{1,0:T(8,128)(2,1)S(1)} custom-call(bf16[1024,768]{1,0:T(8,128)(2,1)S(1)} %copy-done.3, bf16[1024,768]{1,0:T(8,128)(2,1)S(1)} %copy-done.3, bf16[1024,768]{1,0:T(8,128)(2,1)S(1)} %copy-done.3, bf16[1024,256]{1,0:T(8,128)(2,1)S(1)} %convolution_convert_fusion.15.g_ref, f32[2,8,1024]{2,1,0:T(8,128)S(1)} %get-tuple-element.317.lse_ref), custom_call_target="tpu_custom_call" | custom-call | tf_op jit(solution)/shard_map/attend_back/pallas_call | solution.py:853
  449.7 3.0 collective-permute-done.50
  452.8 3.3 collective-permute-start.59
  460.7 15.7 %attend_back.5.refs_0_ = bf16[1024,768]{1,0:T(8,128)(2,1)S(1)} custom-call(bf16[1024,768]{1,0:T(8,128)(2,1)S(1)} %add_convert_fusion.9.q_ref.k_ref.v_ref, bf16[1024,768]{1,0:T(8,128)(2,1)S(1)} %add_convert_fusion.9.q_ref.k_ref.v_ref, bf16[1024,768]{1,0:T(8,128)(2,1)S(1)} %add_convert_fusion.9.q_ref.k_ref.v_ref, ...), custom_call_target="tpu_custom_call" | custom-call | tf_op jit(solution)/shard_map/attend_back/pallas_call | solution.py:853
  476.4 2.8 spread_image.2
  488.9 16.1 %attend_back.6.refs_3_ = bf16[1024,768]{1,0:T(8,128)(2,1)S(1)} custom-call(bf16[1024,768]{1,0:T(8,128)(2,1)S(1)} %copy-done.1, bf16[1024,768]{1,0:T(8,128)(2,1)S(1)} %copy-done.1, bf16[1024,768]{1,0:T(8,128)(2,1)S(1)} %copy-done.1, bf16[1024,256]{1,0:T(8,128)(2,1)S(1)} %convolution_convert_fusion.12.g_ref, f32[2,8,1024]{2,1,0:T(8,128)S(1)} %get-tuple-element.335.lse_ref), custom_call_target="tpu_custom_call" | custom-call | tf_op jit(solution)/shard_map/attend_back/pallas_call | solution.py:853
  505.0 3.1 convolution_convert_fusion.6
  512.0 3.0 multiply_subtract_fusion
  517.1 15.9 %attend_back.7.refs_1_ = bf16[1024,768]{1,0:T(8,128)(2,1)S(1)} custom-call(bf16[1024,768]{1,0:T(8,128)(2,1)S(1)} %add_convert_fusion.8.q_ref.k_ref.v_ref, bf16[1024,768]{1,0:T(8,128)(2,1)S(1)} %add_convert_fusion.8.q_ref.k_ref.v_ref, bf16[1024,768]{1,0:T(8,128)(2,1)S(1)} %add_convert_fusion.8.q_ref.k_ref.v_ref, bf16[1024,256]{1,0:T(8,128)(2,1)S(1)} %copy-done.64, ...), custom_call_target="tpu_custom_call" | custom-call | tf_op jit(solution)/shard_map/attend_back/pallas_call | solution.py:853
  541.8 9.3 %in_norm_back.3 = (bf16[512,1024]{1,0:T(8,128)(2,1)}, f32[8,1024]{1,0:T(8,128)S(1)}) custom-call(bf16[1024,768]{1,0:T(8,128)(2,1)S(1)} %copy-done.14, bf16[1024,768]{1,0:T(8,128)(2,1)S(1)} %attend_back.7.refs_1_, bf16[1024,768]{1,0:T(8,128)(2,1)S(1)} %copy-done.12, bf16[1024,768]{1,0:T(8,128)(2,1)} %copy-done.15, ...), custom_call_target="tpu_custom_call" | custom-call | tf_op jit(solution)/shard_map/in_norm_back/pallas_call | solution.py:739
  555.4 3.4 multiply_subtract_fusion.1
  569.5 8.8 %in_norm_back.2 = (bf16[512,1024]{1,0:T(8,128)(2,1)S(1)}, f32[8,1024]{1,0:T(8,128)S(1)}, f32[256,1024]{1,0:T(8,128)S(1)}) custom-call(bf16[1024,768]{1,0:T(8,128)(2,1)S(1)} %copy-done.14, bf16[1024,768]{1,0:T(8,128)(2,1)S(1)} %copy-done.17, bf16[1024,768]{1,0:T(8,128)(2,1)} %copy-done.11, bf16[1024,768]{1,0:T(8,128)(2,1)} %copy-done.15, ...), custom_call_target="tpu_custom_call" | custom-call | tf_op jit(solution)/shard_map/in_norm_back/pallas_call | solution.py:739
  582.1 2.5 collective-permute-done.66
  589.2 2.7 collective-permute-start.70
  593.1 2.7 collective-permute-done.76
  597.7 2.6 collective-permute-start.79
  606.2 7.0 %collective-permute-done.71 = bf16[128,1024]{1,0:T(8,128)(2,1)} collective-permute-done((bf16[128,1024]{1,0:T(8,128)(2,1)S(1)}, bf16[128,1024]{1,0:T(8,128)(2,1)}, u32[]{:S(2)}, u32[]{:S(2)}) %collective-permute-start.71) | collective-permute-done | bytes 262176 | tf_op jit(solution)/shard_map/ppermute | solution.py:368
  622.5 3.1 spread_image.3
  (660 shorter events, 226.5 us)
Async XLA Ops:
  10.2 28.4 %collective-permute-start.7 = (bf16[128,1280]{1,0:T(8,128)(2,1)S(1)}, bf16[128,1280]{1,0:T(8,128)(2,1)S(1)}, u32[]{:S(2)}, u32[]{:S(2)}) collective-permute-start(bf16[128,1280]{1,0:T(8,128)(2,1)S(1)} %pad_maximum_fusion.32), channel_id=1, source_target_pairs={{0,8},{4,12},{8,0},{12,4},{16,24},{20,28},{24,16},{28,20},{1,9},{5... | collective-permute-start | bytes 983048 | tf_op jit(solution)/shard_map/ppermute | solution.py:368
  19.0 19.6 %collective-permute-start.6 = (bf16[256,768]{1,0:T(8,128)(2,1)}, bf16[256,768]{1,0:T(8,128)(2,1)}, u32[]{:S(2)}, u32[]{:S(2)}) collective-permute-start(bf16[256,768]{1,0:T(8,128)(2,1)} %pad_maximum_fusion.31), channel_id=1, source_target_pairs={{0,16},{4,20},{8,24},{12,28},{16,0},{20,4},{24,8},{28,12},{1,17},{... | collective-permute-start | bytes 1179656 | tf_op jit(solution)/shard_map/ppermute | solution.py:368
  23.6 26.4 %collective-permute-start.10 = (bf16[2,256,1024]{2,1,0:T(8,128)(2,1)}, bf16[2,256,1024]{2,1,0:T(8,128)(2,1)}, u32[]{:S(2)}, u32[]{:S(2)}) collective-permute-start(bf16[2,256,1024]{2,1,0:T(8,128)(2,1)} %pad_maximum_fusion.6), channel_id=1, source_target_pairs={{0,2},{1,3},{2,0},{3,1},{4,6},{5,7},{6,4},{7,5},{8,10},{9,11},{10,... | collective-permute-start | bytes 3145736 | tf_op jit(solution)/shard_map/ppermute | solution.py:378
  25.1 13.6 %collective-permute-start.5 = (bf16[2,1792]{1,0:T(2,128)(2,1)S(1)}, bf16[2,1792]{1,0:T(2,128)(2,1)S(1)}, u32[]{:S(2)}, u32[]{:S(2)}) collective-permute-start(bf16[2,1792]{1,0:T(2,128)(2,1)S(1)} %pad_maximum_fusion.44), channel_id=1, source_target_pairs={{0,16},{4,20},{8,24},{12,28},{16,0},{20,4},{24,8},{28,12},{1,17},{... | collective-permute-start | bytes 21512 | tf_op jit(solution)/shard_map/ppermute | solution.py:368
  52.3 13.7 %collective-permute-start.13 = (bf16[512,384]{1,0:T(8,128)(2,1)S(1)}, bf16[512,384]{1,0:T(8,128)(2,1)}, u32[]{:S(2)}, u32[]{:S(2)}) collective-permute-start(bf16[512,384]{1,0:T(8,128)(2,1)S(1)} %get-tuple-element.515), channel_id=1, source_target_pairs={{0,2},{1,3},{2,0},{3,1},{4,6},{5,7},{6,4},{7,5},{8,10},{9,11},{10,... | collective-permute-start | bytes 1179656 | tf_op jit(solution)/shard_map/ppermute | solution.py:378
  54.8 32.1 %collective-permute-start.14 = (bf16[256,1280]{1,0:T(8,128)(2,1)}, bf16[256,1280]{1,0:T(8,128)(2,1)}, u32[]{:S(2)}, u32[]{:S(2)}) collective-permute-start(bf16[256,1280]{1,0:T(8,128)(2,1)} %pad_maximum_fusion.20), channel_id=1, source_target_pairs={{0,16},{4,20},{8,24},{12,28},{16,0},{20,4},{24,8},{28,12},{1,17},{... | collective-permute-start | bytes 1966088 | tf_op jit(solution)/shard_map/ppermute | solution.py:368
  56.7 30.1 %collective-permute-start.12 = (bf16[1024,384]{1,0:T(8,128)(2,1)}, bf16[1024,384]{1,0:T(8,128)(2,1)}, u32[]{:S(2)}, u32[]{:S(2)}) collective-permute-start(bf16[1024,384]{1,0:T(8,128)(2,1)} %pad_maximum_fusion.18), channel_id=1, source_target_pairs={{0,2},{1,3},{2,0},{3,1},{4,6},{5,7},{6,4},{7,5},{8,10},{9,11},{10,... | collective-permute-start | bytes 2359304 | tf_op jit(solution)/shard_map/ppermute | solution.py:378
  89.4 38.4 %collective-permute-start.15 = (bf16[1024,768]{1,0:T(8,128)(2,1)}, bf16[1024,768]{1,0:T(8,128)(2,1)}, u32[]{:S(2)}, u32[]{:S(2)}) collective-permute-start(bf16[1024,768]{1,0:T(8,128)(2,1)} %pad_maximum_fusion.4.refs_4_), channel_id=1, source_target_pairs={{0,1},{1,0},{2,3},{3,2},{4,5},{5,4},{6,7},{7,6},{8,9},{9,8},{10,11... | collective-permute-start | bytes 4718600 | tf_op jit(solution)/shard_map/ppermute | solution.py:378
  90.8 36.9 %collective-permute-start.16 = (bf16[512,768]{1,0:T(8,128)(2,1)S(1)}, bf16[512,768]{1,0:T(8,128)(2,1)S(1)}, u32[]{:S(2)}, u32[]{:S(2)}) collective-permute-start(bf16[512,768]{1,0:T(8,128)(2,1)S(1)} %pad_maximum_fusion.19), channel_id=1, source_target_pairs={{0,4},{4,0},{8,12},{12,8},{16,20},{20,16},{24,28},{28,24},{1,5},{5... | collective-permute-start | bytes 2359304 | tf_op jit(solution)/shard_map/ppermute | solution.py:374
  93.5 34.2 %collective-permute-start.18 = (bf16[512,512]{1,0:T(8,128)(2,1)S(1)}, bf16[512,512]{1,0:T(8,128)(2,1)S(1)}, u32[]{:S(2)}, u32[]{:S(2)}) collective-permute-start(bf16[512,512]{1,0:T(8,128)(2,1)S(1)} %get-tuple-element.483), channel_id=1, source_target_pairs={{0,2},{1,3},{2,0},{3,1},{4,6},{5,7},{6,4},{7,5},{8,10},{9,11},{10,... | collective-permute-start | bytes 1572872 | tf_op jit(solution)/shard_map/ppermute | solution.py:378
  94.1 33.6 %collective-permute-start.19 = (bf16[512,512]{1,0:T(8,128)(2,1)S(1)}, bf16[512,512]{1,0:T(8,128)(2,1)S(1)}, u32[]{:S(2)}, u32[]{:S(2)}) collective-permute-start(bf16[512,512]{1,0:T(8,128)(2,1)S(1)} %get-tuple-element.482), channel_id=1, source_target_pairs={{0,4},{4,0},{8,12},{12,8},{16,20},{20,16},{24,28},{28,24},{1,5},{5... | collective-permute-start | bytes 1572872 | tf_op jit(solution)/shard_map/ppermute | solution.py:374
  95.7 32.0 %collective-permute-start.17 = (bf16[2,512,128]{2,1,0:T(8,128)(2,1)S(1)}, bf16[2,512,128]{2,1,0:T(8,128)(2,1)S(1)}, u32[]{:S(2)}, u32[]{:S(2)}) collective-permute-start(bf16[2,512,128]{2,1,0:T(8,128)(2,1)S(1)} %pad_maximum_fusion.33), channel_id=1, source_target_pairs={{0,4},{4,0},{8,12},{12,8},{16,20},{20,16},{24,28},{28,24},{1,5},{5... | collective-permute-start | bytes 786440 | tf_op jit(solution)/shard_map/ppermute | solution.py:374
  130.4 27.0 %collective-permute-start.20 = (bf16[1024,768]{1,0:T(8,128)(2,1)}, bf16[1024,768]{1,0:T(8,128)(2,1)}, u32[]{:S(2)}, u32[]{:S(2)}) collective-permute-start(bf16[1024,768]{1,0:T(8,128)(2,1)} %pad_maximum_fusion.5.refs_5_), channel_id=1, source_target_pairs={{0,1},{1,0},{2,3},{3,2},{4,5},{5,4},{6,7},{7,6},{8,9},{9,8},{10,11... | collective-permute-start | bytes 4718600 | tf_op jit(solution)/shard_map/ppermute | solution.py:378
  131.4 19.6 %collective-permute-start.23 = (bf16[1024,256]{1,0:T(8,128)(2,1)}, bf16[1024,256]{1,0:T(8,128)(2,1)}, u32[]{:S(2)}, u32[]{:S(2)}) collective-permute-start(bf16[1024,256]{1,0:T(8,128)(2,1)} %get-tuple-element.508), channel_id=1, source_target_pairs={{0,2},{1,3},{2,0},{3,1},{4,6},{5,7},{6,4},{7,5},{8,10},{9,11},{10,... | collective-permute-start | bytes 1572872 | tf_op jit(solution)/shard_map/ppermute | solution.py:378
  133.1 17.9 %collective-permute-start.22 = (bf16[256,1024]{1,0:T(8,128)(2,1)}, bf16[256,1024]{1,0:T(8,128)(2,1)}, u32[]{:S(2)}, u32[]{:S(2)}) collective-permute-start(bf16[256,1024]{1,0:T(8,128)(2,1)} %get-tuple-element.510), channel_id=1, source_target_pairs={{0,4},{4,0},{8,12},{12,8},{16,20},{20,16},{24,28},{28,24},{1,5},{5... | collective-permute-start | bytes 1572872 | tf_op jit(solution)/shard_map/ppermute | solution.py:374
  135.5 21.9 %collective-permute-start.21 = (bf16[2,1024,128]{2,1,0:T(8,128)(2,1)}, bf16[2,1024,128]{2,1,0:T(8,128)(2,1)}, u32[]{:S(2)}, u32[]{:S(2)}) collective-permute-start(bf16[2,1024,128]{2,1,0:T(8,128)(2,1)} %pad_maximum_fusion.29), channel_id=1, source_target_pairs={{0,2},{1,3},{2,0},{3,1},{4,6},{5,7},{6,4},{7,5},{8,10},{9,11},{10,... | collective-permute-start | bytes 1572872 | tf_op jit(solution)/shard_map/ppermute | solution.py:378
  137.0 14.0 %collective-permute-start.24 = (bf16[128,1024]{1,0:T(8,128)(2,1)}, bf16[128,1024]{1,0:T(8,128)(2,1)S(1)}, u32[]{:S(2)}, u32[]{:S(2)}) collective-permute-start(bf16[128,1024]{1,0:T(8,128)(2,1)} %copy.174), channel_id=1, source_target_pairs={{0,8},{4,12},{8,0},{12,4},{16,24},{20,28},{24,16},{28,20},{1,9},{5... | collective-permute-start | bytes 786440 | tf_op jit(solution)/shard_map/ppermute | solution.py:368
  159.5 28.6 %collective-permute-start.25 = (bf16[2,1024,256]{2,1,0:T(8,128)(2,1)}, bf16[2,1024,256]{2,1,0:T(8,128)(2,1)}, u32[]{:S(2)}, u32[]{:S(2)}) collective-permute-start(bf16[2,1024,256]{2,1,0:T(8,128)(2,1)} %pad_maximum_fusion.8), channel_id=1, source_target_pairs={{0,1},{1,0},{2,3},{3,2},{4,5},{5,4},{6,7},{7,6},{8,9},{9,8},{10,11... | collective-permute-start | bytes 3145736 | tf_op jit(solution)/shard_map/ppermute | solution.py:378
  159.5 16.8 %collective-permute-start.28 = (bf16[1024,256]{1,0:T(8,128)(2,1)}, bf16[1024,256]{1,0:T(8,128)(2,1)}, u32[]{:S(2)}, u32[]{:S(2)}) collective-permute-start(bf16[1024,256]{1,0:T(8,128)(2,1)} %get-tuple-element.507), channel_id=1, source_target_pairs={{0,2},{1,3},{2,0},{3,1},{4,6},{5,7},{6,4},{7,5},{8,10},{9,11},{10,... | collective-permute-start | bytes 1572872 | tf_op jit(solution)/shard_map/ppermute | solution.py:378
  160.0 16.2 %collective-permute-start.27 = (bf16[256,1024]{1,0:T(8,128)(2,1)}, bf16[256,1024]{1,0:T(8,128)(2,1)}, u32[]{:S(2)}, u32[]{:S(2)}) collective-permute-start(bf16[256,1024]{1,0:T(8,128)(2,1)} %get-tuple-element.509), channel_id=1, source_target_pairs={{0,4},{4,0},{8,12},{12,8},{16,20},{20,16},{24,28},{28,24},{1,5},{5... | collective-permute-start | bytes 1572872 | tf_op jit(solution)/shard_map/ppermute | solution.py:374
  163.3 24.8 %collective-permute-start.26 = (bf16[256,1024]{1,0:T(8,128)(2,1)}, bf16[256,1024]{1,0:T(8,128)(2,1)}, u32[]{:S(2)}, u32[]{:S(2)}) collective-permute-start(bf16[256,1024]{1,0:T(8,128)(2,1)} %pad_maximum_fusion.30), channel_id=1, source_target_pairs={{0,16},{4,20},{8,24},{12,28},{16,0},{20,4},{24,8},{28,12},{1,17},{... | collective-permute-start | bytes 1572872 | tf_op jit(solution)/shard_map/ppermute | solution.py:368
  191.0 21.8 %collective-permute-start.30 = (bf16[1024,1024]{1,0:T(8,128)(2,1)}, bf16[1024,1024]{1,0:T(8,128)(2,1)}, u32[]{:S(2)}, u32[]{:S(2)}) collective-permute-start(bf16[1024,1024]{1,0:T(8,128)(2,1)} %pad_maximum_fusion.1.right_ref.refs_7_), channel_id=1, source_target_pairs={{0,1},{1,0},{2,3},{3,2},{4,5},{5,4},{6,7},{7,6},{8,9},{9,8},{10,11... | collective-permute-start | bytes 6291464 | tf_op jit(solution)/shard_map/ppermute | solution.py:378
  193.8 19.0 %collective-permute-start.29 = (bf16[1024,1024]{1,0:T(8,128)(2,1)}, bf16[1024,1024]{1,0:T(8,128)(2,1)}, u32[]{:S(2)}, u32[]{:S(2)}) collective-permute-start(bf16[1024,1024]{1,0:T(8,128)(2,1)} %pad_maximum_fusion.right_ref.refs_6_), channel_id=1, source_target_pairs={{0,1},{1,0},{2,3},{3,2},{4,5},{5,4},{6,7},{7,6},{8,9},{9,8},{10,11... | collective-permute-start | bytes 6291464 | tf_op jit(solution)/shard_map/ppermute | solution.py:378
  197.4 14.7 %collective-permute-start.31 = (bf16[512,512]{1,0:T(8,128)(2,1)}, bf16[512,512]{1,0:T(8,128)(2,1)}, u32[]{:S(2)}, u32[]{:S(2)}) collective-permute-start(bf16[512,512]{1,0:T(8,128)(2,1)} %get-tuple-element.506), channel_id=1, source_target_pairs={{0,2},{1,3},{2,0},{3,1},{4,6},{5,7},{6,4},{7,5},{8,10},{9,11},{10,... | collective-permute-start | bytes 1572872 | tf_op jit(solution)/shard_map/ppermute | solution.py:378
  198.9 13.9 %collective-permute-start.32 = (bf16[512,512]{1,0:T(8,128)(2,1)}, bf16[512,512]{1,0:T(8,128)(2,1)}, u32[]{:S(2)}, u32[]{:S(2)}) collective-permute-start(bf16[512,512]{1,0:T(8,128)(2,1)} %get-tuple-element.505), channel_id=1, source_target_pairs={{0,4},{4,0},{8,12},{12,8},{16,20},{20,16},{24,28},{28,24},{1,5},{5... | collective-permute-start | bytes 1572872 | tf_op jit(solution)/shard_map/ppermute | solution.py:374
  215.1 29.8 %collective-permute-start.34 = (bf16[1024,512]{1,0:T(8,128)(2,1)}, bf16[1024,512]{1,0:T(8,128)(2,1)}, u32[]{:S(2)}, u32[]{:S(2)}) collective-permute-start(bf16[1024,512]{1,0:T(8,128)(2,1)} %pad_maximum_fusion.10), channel_id=1, source_target_pairs={{0,2},{1,3},{2,0},{3,1},{4,6},{5,7},{6,4},{7,5},{8,10},{9,11},{10,... | collective-permute-start | bytes 3145736 | tf_op jit(solution)/shard_map/ppermute | solution.py:378
  218.0 26.9 %collective-permute-start.33 = (bf16[512,1024]{1,0:T(8,128)(2,1)}, bf16[512,1024]{1,0:T(8,128)(2,1)}, u32[]{:S(2)}, u32[]{:S(2)}) collective-permute-start(bf16[512,1024]{1,0:T(8,128)(2,1)} %pad_maximum_fusion.9), channel_id=1, source_target_pairs={{0,4},{4,0},{8,12},{12,8},{16,20},{20,16},{24,28},{28,24},{1,5},{5... | collective-permute-start | bytes 3145736 | tf_op jit(solution)/shard_map/ppermute | solution.py:374
  249.6 24.7 %collective-permute-start.36 = (bf16[1024,1024]{1,0:T(8,128)(2,1)}, bf16[1024,1024]{1,0:T(8,128)(2,1)}, u32[]{:S(2)}, u32[]{:S(2)}) collective-permute-start(bf16[1024,1024]{1,0:T(8,128)(2,1)} %pad_maximum_fusion.3.refs_7_.right_ref), channel_id=1, source_target_pairs={{0,1},{1,0},{2,3},{3,2},{4,5},{5,4},{6,7},{7,6},{8,9},{9,8},{10,11... | collective-permute-start | bytes 6291464 | tf_op jit(solution)/shard_map/ppermute | solution.py:378
  252.8 21.5 %collective-permute-start.35 = (bf16[1024,1024]{1,0:T(8,128)(2,1)}, bf16[1024,1024]{1,0:T(8,128)(2,1)}, u32[]{:S(2)}, u32[]{:S(2)}) collective-permute-start(bf16[1024,1024]{1,0:T(8,128)(2,1)} %pad_maximum_fusion.2.refs_6_.right_ref), channel_id=1, source_target_pairs={{0,1},{1,0},{2,3},{3,2},{4,5},{5,4},{6,7},{7,6},{8,9},{9,8},{10,11... | collective-permute-start | bytes 6291464 | tf_op jit(solution)/shard_map/ppermute | solution.py:378
  255.2 34.8 %collective-permute-start.37 = (bf16[2,256,1024]{2,1,0:T(8,128)(2,1)}, bf16[2,256,1024]{2,1,0:T(8,128)(2,1)}, u32[]{:S(2)}, u32[]{:S(2)}) collective-permute-start(bf16[2,256,1024]{2,1,0:T(8,128)(2,1)} %pad_maximum_fusion.11), channel_id=1, source_target_pairs={{0,2},{1,3},{2,0},{3,1},{4,6},{5,7},{6,4},{7,5},{8,10},{9,11},{10,... | collective-permute-start | bytes 3145736 | tf_op jit(solution)/shard_map/ppermute | solution.py:378
  304.7 18.2 %collective-permute-start.40 = (bf16[1024,1024]{1,0:T(8,128)(2,1)}, bf16[1024,1024]{1,0:T(8,128)(2,1)}, u32[]{:S(2)}, u32[]{:S(2)}) collective-permute-start(bf16[1024,1024]{1,0:T(8,128)(2,1)} %convolution_convert_fusion.2), channel_id=1, source_target_pairs={{0,1},{1,0},{2,3},{3,2},{4,5},{5,4},{6,7},{7,6},{8,9},{9,8},{10,11... | collective-permute-start | bytes 6291464 | tf_op jit(solution)/shard_map/ppermute | solution.py:378
  304.8 18.0 %collective-permute-start.39 = (bf16[1024,1024]{1,0:T(8,128)(2,1)}, bf16[1024,1024]{1,0:T(8,128)(2,1)}, u32[]{:S(2)}, u32[]{:S(2)}) collective-permute-start(bf16[1024,1024]{1,0:T(8,128)(2,1)} %convolution_convert_fusion.3), channel_id=1, source_target_pairs={{0,1},{1,0},{2,3},{3,2},{4,5},{5,4},{6,7},{7,6},{8,9},{9,8},{10,11... | collective-permute-start | bytes 6291464 | tf_op jit(solution)/shard_map/ppermute | solution.py:378
  326.5 30.2 %collective-permute-start.42 = (bf16[1024,256]{1,0:T(8,128)(2,1)}, bf16[1024,256]{1,0:T(8,128)(2,1)}, u32[]{:S(2)}, u32[]{:S(2)}) collective-permute-start(bf16[1024,256]{1,0:T(8,128)(2,1)} %get-tuple-element.473), channel_id=1, source_target_pairs={{0,2},{1,3},{2,0},{3,1},{4,6},{5,7},{6,4},{7,5},{8,10},{9,11},{10,... | collective-permute-start | bytes 1572872 | tf_op jit(solution)/shard_map/ppermute | solution.py:378
  331.6 25.1 %collective-permute-start.41 = (bf16[256,1024]{1,0:T(8,128)(2,1)}, bf16[256,1024]{1,0:T(8,128)(2,1)}, u32[]{:S(2)}, u32[]{:S(2)}) collective-permute-start(bf16[256,1024]{1,0:T(8,128)(2,1)} %get-tuple-element.475), channel_id=1, source_target_pairs={{0,4},{4,0},{8,12},{12,8},{16,20},{20,16},{24,28},{28,24},{1,5},{5... | collective-permute-start | bytes 1572872 | tf_op jit(solution)/shard_map/ppermute | solution.py:374
  350.1 22.1 %collective-permute-start.44 = (bf16[1024,256]{1,0:T(8,128)(2,1)}, bf16[1024,256]{1,0:T(8,128)(2,1)}, u32[]{:S(2)}, u32[]{:S(2)}) collective-permute-start(bf16[1024,256]{1,0:T(8,128)(2,1)} %get-tuple-element.472), channel_id=1, source_target_pairs={{0,2},{1,3},{2,0},{3,1},{4,6},{5,7},{6,4},{7,5},{8,10},{9,11},{10,... | collective-permute-start | bytes 1572872 | tf_op jit(solution)/shard_map/ppermute | solution.py:378
  351.6 20.5 %collective-permute-start.43 = (bf16[256,1024]{1,0:T(8,128)(2,1)}, bf16[256,1024]{1,0:T(8,128)(2,1)}, u32[]{:S(2)}, u32[]{:S(2)}) collective-permute-start(bf16[256,1024]{1,0:T(8,128)(2,1)} %get-tuple-element.474), channel_id=1, source_target_pairs={{0,4},{4,0},{8,12},{12,8},{16,20},{20,16},{24,28},{28,24},{1,5},{5... | collective-permute-start | bytes 1572872 | tf_op jit(solution)/shard_map/ppermute | solution.py:374
  353.6 53.6 %collective-permute-start.49 = (bf16[2,256,1024]{2,1,0:T(8,128)(2,1)}, bf16[2,256,1024]{2,1,0:T(8,128)(2,1)}, u32[]{:S(2)}, u32[]{:S(2)}) collective-permute-start(bf16[2,256,1024]{2,1,0:T(8,128)(2,1)} %bitcast.79), channel_id=1, source_target_pairs={{0,2},{1,3},{2,0},{3,1},{4,6},{5,7},{6,4},{7,5},{8,10},{9,11},{10,... | collective-permute-start | bytes 3145736 | tf_op jit(solution)/shard_map/ppermute | solution.py:378
  372.1 35.1 %collective-permute-start.46 = (bf16[1024,1024]{1,0:T(8,128)(2,1)}, bf16[1024,1024]{1,0:T(8,128)(2,1)}, u32[]{:S(2)}, u32[]{:S(2)}) collective-permute-start(bf16[1024,1024]{1,0:T(8,128)(2,1)} %convolution_convert_fusion), channel_id=1, source_target_pairs={{0,1},{1,0},{2,3},{3,2},{4,5},{5,4},{6,7},{7,6},{8,9},{9,8},{10,11... | collective-permute-start | bytes 6291464 | tf_op jit(solution)/shard_map/ppermute | solution.py:378
  372.2 35.1 %collective-permute-start.45 = (bf16[1024,1024]{1,0:T(8,128)(2,1)}, bf16[1024,1024]{1,0:T(8,128)(2,1)}, u32[]{:S(2)}, u32[]{:S(2)}) collective-permute-start(bf16[1024,1024]{1,0:T(8,128)(2,1)} %convolution_convert_fusion.1), channel_id=1, source_target_pairs={{0,1},{1,0},{2,3},{3,2},{4,5},{5,4},{6,7},{7,6},{8,9},{9,8},{10,11... | collective-permute-start | bytes 6291464 | tf_op jit(solution)/shard_map/ppermute | solution.py:378
  375.2 32.0 %collective-permute-start.48 = (bf16[512,512]{1,0:T(8,128)(2,1)}, bf16[512,512]{1,0:T(8,128)(2,1)}, u32[]{:S(2)}, u32[]{:S(2)}) collective-permute-start(bf16[512,512]{1,0:T(8,128)(2,1)} %slice.478), channel_id=1, source_target_pairs={{0,4},{4,0},{8,12},{12,8},{16,20},{20,16},{24,28},{28,24},{1,5},{5... | collective-permute-start | bytes 1572872 | tf_op jit(solution)/shard_map/ppermute | solution.py:374
  379.0 28.2 %collective-permute-start.47 = (bf16[512,512]{1,0:T(8,128)(2,1)}, bf16[512,512]{1,0:T(8,128)(2,1)}, u32[]{:S(2)}, u32[]{:S(2)}) collective-permute-start(bf16[512,512]{1,0:T(8,128)(2,1)} %slice.476), channel_id=1, source_target_pairs={{0,2},{1,3},{2,0},{3,1},{4,6},{5,7},{6,4},{7,5},{8,10},{9,11},{10,... | collective-permute-start | bytes 1572872 | tf_op jit(solution)/shard_map/ppermute | solution.py:378
  418.5 30.3 %collective-permute-start.54 = (bf16[2,256,1024]{2,1,0:T(8,128)(2,1)S(1)}, bf16[2,256,1024]{2,1,0:T(8,128)(2,1)S(1)}, u32[]{:S(2)}, u32[]{:S(2)}) collective-permute-start(bf16[2,256,1024]{2,1,0:T(8,128)(2,1)S(1)} %pad_maximum_fusion.14), channel_id=1, source_target_pairs={{0,1},{1,0},{2,3},{3,2},{4,5},{5,4},{6,7},{7,6},{8,9},{9,8},{10,11... | collective-permute-start | bytes 3145736 | tf_op jit(solution)/shard_map/ppermute | solution.py:378
  421.1 27.7 %collective-permute-start.53 = (bf16[256,1024]{1,0:T(8,128)(2,1)S(1)}, bf16[256,1024]{1,0:T(8,128)(2,1)S(1)}, u32[]{:S(2)}, u32[]{:S(2)}) collective-permute-start(bf16[256,1024]{1,0:T(8,128)(2,1)S(1)} %fusion.7), channel_id=1, source_target_pairs={{0,16},{4,20},{8,24},{12,28},{16,0},{20,4},{24,8},{28,12},{1,17},{... | collective-permute-start | bytes 1572872 | tf_op jit(solution)/shard_map/ppermute | solution.py:368
  421.3 27.5 %collective-permute-start.52 = (bf16[2,1024,256]{2,1,0:T(8,128)(2,1)S(1)}, bf16[2,1024,256]{2,1,0:T(8,128)(2,1)S(1)}, u32[]{:S(2)}, u32[]{:S(2)}) collective-permute-start(bf16[2,1024,256]{2,1,0:T(8,128)(2,1)S(1)} %pad_maximum_fusion.13), channel_id=1, source_target_pairs={{0,1},{1,0},{2,3},{3,2},{4,5},{5,4},{6,7},{7,6},{8,9},{9,8},{10,11... | collective-permute-start | bytes 3145736 | tf_op jit(solution)/shard_map/ppermute | solution.py:378
  424.4 25.3 %collective-permute-start.51 = (bf16[1024,512]{1,0:T(8,128)(2,1)S(1)}, bf16[1024,512]{1,0:T(8,128)(2,1)S(1)}, u32[]{:S(2)}, u32[]{:S(2)}) collective-permute-start(bf16[1024,512]{1,0:T(8,128)(2,1)S(1)} %slice.480), channel_id=1, source_target_pairs={{0,2},{1,3},{2,0},{3,1},{4,6},{5,7},{6,4},{7,5},{8,10},{9,11},{10,... | collective-permute-start | bytes 3145736 | tf_op jit(solution)/shard_map/ppermute | solution.py:378
  427.7 25.0 %collective-permute-start.50 = (bf16[512,1024]{1,0:T(8,128)(2,1)S(1)}, bf16[512,1024]{1,0:T(8,128)(2,1)S(1)}, u32[]{:S(2)}, u32[]{:S(2)}) collective-permute-start(bf16[512,1024]{1,0:T(8,128)(2,1)S(1)} %slice.479), channel_id=1, source_target_pairs={{0,4},{4,0},{8,12},{12,8},{16,20},{20,16},{24,28},{28,24},{1,5},{5... | collective-permute-start | bytes 3145736 | tf_op jit(solution)/shard_map/ppermute | solution.py:374
  452.8 28.3 %collective-permute-start.59 = (bf16[128,1024]{1,0:T(8,128)(2,1)S(1)}, bf16[128,1024]{1,0:T(8,128)(2,1)S(1)}, u32[]{:S(2)}, u32[]{:S(2)}) collective-permute-start(bf16[128,1024]{1,0:T(8,128)(2,1)S(1)} %slice.490), channel_id=1, source_target_pairs={{0,8},{4,12},{8,0},{12,4},{16,24},{20,28},{24,16},{28,20},{1,9},{5... | collective-permute-start | bytes 786440 | tf_op jit(solution)/shard_map/ppermute | solution.py:368
  456.1 27.3 %collective-permute-start.55 = (bf16[1024,768]{1,0:T(8,128)(2,1)S(1)}, bf16[1024,768]{1,0:T(8,128)(2,1)S(1)}, u32[]{:S(2)}, u32[]{:S(2)}) collective-permute-start(bf16[1024,768]{1,0:T(8,128)(2,1)S(1)} %convolution_convert_fusion.7), channel_id=1, source_target_pairs={{0,1},{1,0},{2,3},{3,2},{4,5},{5,4},{6,7},{7,6},{8,9},{9,8},{10,11... | collective-permute-start | bytes 4718600 | tf_op jit(solution)/shard_map/ppermute | solution.py:378
  456.6 24.6 %collective-permute-start.58 = (bf16[512,512]{1,0:T(8,128)(2,1)S(1)}, bf16[512,512]{1,0:T(8,128)(2,1)S(1)}, u32[]{:S(2)}, u32[]{:S(2)}) collective-permute-start(bf16[512,512]{1,0:T(8,128)(2,1)S(1)} %slice.489), channel_id=1, source_target_pairs={{0,4},{4,0},{8,12},{12,8},{16,20},{20,16},{24,28},{28,24},{1,5},{5... | collective-permute-start | bytes 1572872 | tf_op jit(solution)/shard_map/ppermute | solution.py:374
  458.1 23.1 %collective-permute-start.57 = (bf16[512,512]{1,0:T(8,128)(2,1)S(1)}, bf16[512,512]{1,0:T(8,128)(2,1)S(1)}, u32[]{:S(2)}, u32[]{:S(2)}) collective-permute-start(bf16[512,512]{1,0:T(8,128)(2,1)S(1)} %slice.487), channel_id=1, source_target_pairs={{0,2},{1,3},{2,0},{3,1},{4,6},{5,7},{6,4},{7,5},{8,10},{9,11},{10,... | collective-permute-start | bytes 1572872 | tf_op jit(solution)/shard_map/ppermute | solution.py:378
  460.0 23.4 %collective-permute-start.56 = (bf16[2,1024,128]{2,1,0:T(8,128)(2,1)S(1)}, bf16[2,1024,128]{2,1,0:T(8,128)(2,1)S(1)}, u32[]{:S(2)}, u32[]{:S(2)}) collective-permute-start(bf16[2,1024,128]{2,1,0:T(8,128)(2,1)S(1)} %slice.485), channel_id=1, source_target_pairs={{0,2},{1,3},{2,0},{3,1},{4,6},{5,7},{6,4},{7,5},{8,10},{9,11},{10,... | collective-permute-start | bytes 1572872 | tf_op jit(solution)/shard_map/ppermute | solution.py:378
  484.0 24.1 %collective-permute-start.61 = (bf16[1024,384]{1,0:T(8,128)(2,1)S(1)}, bf16[1024,384]{1,0:T(8,128)(2,1)S(1)}, u32[]{:S(2)}, u32[]{:S(2)}) collective-permute-start(bf16[1024,384]{1,0:T(8,128)(2,1)S(1)} %slice.493), channel_id=1, source_target_pairs={{0,2},{1,3},{2,0},{3,1},{4,6},{5,7},{6,4},{7,5},{8,10},{9,11},{10,... | collective-permute-start | bytes 2359304 | tf_op jit(solution)/shard_map/ppermute | solution.py:378
  486.5 21.6 %collective-permute-start.60 = (bf16[2,512,128]{2,1,0:T(8,128)(2,1)S(1)}, bf16[2,512,128]{2,1,0:T(8,128)(2,1)S(1)}, u32[]{:S(2)}, u32[]{:S(2)}) collective-permute-start(bf16[2,512,128]{2,1,0:T(8,128)(2,1)S(1)} %slice.492), channel_id=1, source_target_pairs={{0,4},{4,0},{8,12},{12,8},{16,20},{20,16},{24,28},{28,24},{1,5},{5... | collective-permute-start | bytes 786440 | tf_op jit(solution)/shard_map/ppermute | solution.py:374
  488.8 46.1 %collective-permute-start.64 = (bf16[256,1024]{1,0:T(8,128)(2,1)}, bf16[256,1024]{1,0:T(8,128)(2,1)}, u32[]{:S(2)}, u32[]{:S(2)}) collective-permute-start(bf16[256,1024]{1,0:T(8,128)(2,1)} %fusion.6), channel_id=1, source_target_pairs={{0,16},{4,20},{8,24},{12,28},{16,0},{20,4},{24,8},{28,12},{1,17},{... | collective-permute-start | bytes 1572872 | tf_op jit(solution)/shard_map/ppermute | solution.py:368
  509.0 25.9 %collective-permute-start.63 = (bf16[1024,768]{1,0:T(8,128)(2,1)}, bf16[1024,768]{1,0:T(8,128)(2,1)}, u32[]{:S(2)}, u32[]{:S(2)}) collective-permute-start(bf16[1024,768]{1,0:T(8,128)(2,1)} %convolution_convert_fusion.6), channel_id=1, source_target_pairs={{0,1},{1,0},{2,3},{3,2},{4,5},{5,4},{6,7},{7,6},{8,9},{9,8},{10,11... | collective-permute-start | bytes 4718600 | tf_op jit(solution)/shard_map/ppermute | solution.py:378
  515.2 19.7 %collective-permute-start.62 = (bf16[512,384]{1,0:T(8,128)(2,1)S(1)}, bf16[512,384]{1,0:T(8,128)(2,1)S(1)}, u32[]{:S(2)}, u32[]{:S(2)}) collective-permute-start(bf16[512,384]{1,0:T(8,128)(2,1)S(1)} %slice.495), channel_id=1, source_target_pairs={{0,4},{4,0},{8,12},{12,8},{16,20},{20,16},{24,28},{28,24},{1,5},{5... | collective-permute-start | bytes 1179656 | tf_op jit(solution)/shard_map/ppermute | solution.py:374
  536.2 16.3 %collective-permute-start.72 = (bf16[128,1024]{1,0:T(8,128)(2,1)S(1)}, bf16[128,1024]{1,0:T(8,128)(2,1)S(1)}, u32[]{:S(2)}, u32[]{:S(2)}) collective-permute-start(bf16[128,1024]{1,0:T(8,128)(2,1)S(1)} %slice.517), channel_id=1, source_target_pairs={{0,8},{4,12},{8,0},{12,4},{16,24},{20,28},{24,16},{28,20},{1,9},{5... | collective-permute-start | bytes 786440 | tf_op jit(solution)/shard_map/ppermute | solution.py:368
  540.8 19.7 %collective-permute-start.65 = (bf16[512,768]{1,0:T(8,128)(2,1)}, bf16[512,768]{1,0:T(8,128)(2,1)}, u32[]{:S(2)}, u32[]{:S(2)}) collective-permute-start(bf16[512,768]{1,0:T(8,128)(2,1)} %slice.500), channel_id=1, source_target_pairs={{0,4},{4,0},{8,12},{12,8},{16,20},{20,16},{24,28},{28,24},{1,5},{5... | collective-permute-start | bytes 2359304 | tf_op jit(solution)/shard_map/ppermute | solution.py:374
  551.1 29.7 %collective-permute-start.67 = (bf16[2,256,1024]{2,1,0:T(8,128)(2,1)}, bf16[2,256,1024]{2,1,0:T(8,128)(2,1)}, u32[]{:S(2)}, u32[]{:S(2)}) collective-permute-start(bf16[2,256,1024]{2,1,0:T(8,128)(2,1)} %bitcast.91), channel_id=1, source_target_pairs={{0,2},{1,3},{2,0},{3,1},{4,6},{5,7},{6,4},{7,5},{8,10},{9,11},{10,... | collective-permute-start | bytes 3145736 | tf_op jit(solution)/shard_map/ppermute | solution.py:378
  568.2 16.3 %collective-permute-start.66 = (bf16[512,384]{1,0:T(8,128)(2,1)}, bf16[512,384]{1,0:T(8,128)(2,1)}, u32[]{:S(2)}, u32[]{:S(2)}) collective-permute-start(bf16[512,384]{1,0:T(8,128)(2,1)} %slice.502), channel_id=1, source_target_pairs={{0,2},{1,3},{2,0},{3,1},{4,6},{5,7},{6,4},{7,5},{8,10},{9,11},{10,... | collective-permute-start | bytes 1179656 | tf_op jit(solution)/shard_map/ppermute | solution.py:378
  588.7 17.5 %collective-permute-start.69 = (bf16[128,1024]{1,0:T(8,128)(2,1)}, bf16[128,1024]{1,0:T(8,128)(2,1)S(1)}, u32[]{:S(2)}, u32[]{:S(2)}) collective-permute-start(bf16[128,1024]{1,0:T(8,128)(2,1)} %get-tuple-element.488), channel_id=1, source_target_pairs={{0,8},{4,12},{8,0},{12,4},{16,24},{20,28},{24,16},{28,20},{1,9},{5... | collective-permute-start | bytes 786440 | tf_op jit(solution)/shard_map/ppermute | solution.py:368
  589.2 17.0 %collective-permute-start.70 = (bf16[128,1024]{1,0:T(8,128)(2,1)S(1)}, bf16[128,1024]{1,0:T(8,128)(2,1)S(1)}, u32[]{:S(2)}, u32[]{:S(2)}) collective-permute-start(bf16[128,1024]{1,0:T(8,128)(2,1)S(1)} %get-tuple-element.487), channel_id=1, source_target_pairs={{0,16},{4,20},{8,24},{12,28},{16,0},{20,4},{24,8},{28,12},{1,17},{... | collective-permute-start | bytes 786440 | tf_op jit(solution)/shard_map/ppermute | solution.py:368
  603.4 9.8 %collective-permute-start.71 = (bf16[128,1024]{1,0:T(8,128)(2,1)S(1)}, bf16[128,1024]{1,0:T(8,128)(2,1)}, u32[]{:S(2)}, u32[]{:S(2)}) collective-permute-start(bf16[128,1024]{1,0:T(8,128)(2,1)S(1)} %get-tuple-element.486), channel_id=1, source_target_pairs={{0,24},{4,28},{8,16},{12,20},{16,8},{20,12},{24,0},{28,4},{1,25},{... | collective-permute-start | bytes 786440 | tf_op jit(solution)/shard_map/ppermute | solution.py:368
  604.8 16.4 %collective-permute-start.68 = (bf16[2,256,1024]{2,1,0:T(8,128)(2,1)}, bf16[2,256,1024]{2,1,0:T(8,128)(2,1)}, u32[]{:S(2)}, u32[]{:S(2)}) collective-permute-start(bf16[2,256,1024]{2,1,0:T(8,128)(2,1)} %pad_maximum_fusion.15), channel_id=1, source_target_pairs={{0,1},{1,0},{2,3},{3,2},{4,5},{5,4},{6,7},{7,6},{8,9},{9,8},{10,11... | collective-permute-start | bytes 3145736 | tf_op jit(solution)/shard_map/ppermute | solution.py:378
  (155 other events, 1106.9 us)

commit v9 on v8

--- a/solution.py
+++ b/solution.py
@@ -496,9 +496,14 @@
 
 
 def small_reduce_steps(chain, vector_part, bias_part):
-    packed = [jnp.concatenate([vector_part, each], 1) for each in bias_part]
-    arrived = yield [swap_mp(packed[step], step) for step in range(1, MP)]
-    total = (packed[0] + arrived[0]) + (arrived[1] + arrived[2])
+    near = jnp.concatenate([vector_part, bias_part[0], bias_part[2]], 1)
+    far = jnp.concatenate([vector_part, bias_part[1], bias_part[3]], 1)
+    (arrived,) = yield [swap_mp(far, 1)]
+    total = near + arrived
+    kept = vector_part.shape[1] + bias_part.shape[2]
+    far = jnp.concatenate([total[:, : vector_part.shape[1]], total[:, kept:]], 1)
+    (arrived,) = yield [swap_mp(far, 2)]
+    total = total[:, :kept] + arrived
     arrived = yield [swap_y(total[ZS:])]
     total = total[:ZS] + arrived[0]
     arrived = yield [swap_z(total[step], step) for step in range(1, ZS)]
@@ -831,7 +836,7 @@
     rows, width = heads.shape
     pairs = width // LANES // 3
     return pl.pallas_call(
-        functools.partial(attend_kernel, 256),
+        functools.partial(attend_kernel, 512),
         grid=(pairs,),
         in_specs=[kind_spec(rows, kind) for kind in range(3)],
         out_specs=[
@@ -851,7 +856,7 @@
     rows, width = heads.shape
     pairs = width // LANES // 3
     return pl.pallas_call(
-        functools.partial(attend_back_kernel, 256),
+        functools.partial(attend_back_kernel, 512),
         grid=(pairs,),
         in_specs=[kind_spec(rows, kind) for kind in range(3)]
         + [
@@ -944,9 +949,9 @@
     meet((), small)
     meet((), small, rows_qkv, rows_up)
     part_a, part_b = jnp.split(rows_qkv.result, 2, 1)
-    get_qkv = [Chain(gather_steps, [part_a], ("yx",)), Chain(gather_steps, [part_b], ("xy",))]
-    meet((), small, get_qkv[0], fetch_tokens)
-    tokens = meet(tokens, fetch_tokens)
+    get_qkv = [Chain(gather_steps, [part_a], ("xy",)), Chain(gather_steps, [part_b], ("yx",))]
+    meet((), small, get_qkv[1], fetch_tokens)
+    tokens = meet(tokens, fetch_tokens, get_qkv[0])
 
     vector_full, bias_small = small.result
     vector_full = vector_full.reshape(DP, vectors.shape[0], LANES).transpose(1, 0, 2)
@@ -957,7 +962,7 @@
     bias_full = bias_full.astype(F32)
 
     base, normed_one = assemble_image(place, vector_full, tokens[:, 0], fetch_tokens.result, True)
-    normed_one, down_shard = meet((normed_one, down_shard), *get_qkv, rows_up)
+    normed_one = meet(normed_one, *get_qkv, rows_up)
     out_rows, up_rows = jnp.split(rows_up.result, [block_width], 1)
     get_out = Chain(gather_steps, [jnp.stack(jnp.split(out_rows, 2, 1))], ("yx",))
     get_up = Chain(gather_steps, jnp.split(up_rows, 2, 1), both, (1, 2))
@@ -974,17 +979,14 @@
         blended[core][half], log_total[core][half] = attend(heads[core][half])
 
     heads[0][0] = project(0, 0, get_qkv[0].own[0])
+    heads[0][0], down_shard = meet((heads[0][0], down_shard), *get_qkv)
+    w_qkv = [[each.own[0] for each in get_qkv], [each.result[0] for each in get_qkv]]
+    rows_down = Chain(rows_z_steps, down_shard)
     forward_heads(0, 0)
-    blended[0][0], normed_one, down_shard = meet(
-        (blended[0][0], normed_one, down_shard), *get_qkv, get_out, get_up
-    )
-    rows_down = Chain(rows_z_steps, down_shard)
-    heads[0][1] = project(0, 1, get_qkv[1].own[0])
+    blended[0][0], normed_one = meet((blended[0][0], normed_one), get_out, get_up, rows_down)
+    heads[0][1] = project(0, 1, w_qkv[0][1])
     forward_heads(0, 1)
-    blended[0][1], normed_one = meet(
-        (blended[0][1], normed_one), get_qkv[1], get_out, get_up, rows_down
-    )
-    w_qkv = [[each.own[0] for each in get_qkv], [each.result[0] for each in get_qkv]]
+    blended[0][1], normed_one = meet((blended[0][1], normed_one), get_out, get_up)
     heads[1][0] = project(1, 0, w_qkv[1][0])
     forward_heads(1, 0)
     blended[1][0], normed_one = meet(
@@ -1114,8 +1116,8 @@
     )
     grad_heads = meet(grad_heads, sum_qkv[1])
     near, sums_near, own_grad = input_back((0, 1), [BF, "sums", "own"])
-    near, sums_near, own_grad = meet((near, sums_near, own_grad), sum_qkv[1])
     grad_near.append(near)
+    sums_near, own_grad = meet((sums_near, own_grad), sum_qkv[1], send_grad)
     sums_input = sums_far + sums_near
 
     grad_vectors = jnp.stack(
@@ -1147,9 +1149,8 @@
     rows_qkv = Chain(sum_z_steps, jnp.concatenate(sum_qkv[0].result + sum_qkv[1].result + [out_rows], 1))
     meet((), rows_up)
     meet((), send_grad)
-    meet((), send_grad)
     meet((), rows_qkv)
-    for _ in range(3):
+    for _ in range(4):
         meet((), sum_small)
     layer_output = spread_image(place, output[:chunk_rows], send_output.result, BF)[:, None]
     input_grad = spread_image(place, own_grad, send_grad.result, F32)[:, None]

time: 633 us -> 622 us (0.983)
    ppermute x44 -> x43, waiting for transfers between devices: 14.7 us -> 25.8 us  [swap_mp(): return lax.ppermute(part, 'mp', [(each, each ^ step) for each in range(MP)])]
    ppermute x18, waiting for transfers between devices: 29.1 us -> 18.8 us  [swap_y(): return lax.ppermute(part, 'dp', [(each, each ^ 1) for each in range(DP)])]
    unnamed x300 -> x310, local copies, waits for them, and re-layouts: 44 us -> 41.1 us
    ppermute x44 -> x43, starting transfers between devices: 27.5 us -> 28.2 us  [swap_mp(): return lax.ppermute(part, 'mp', [(each, each ^ step) for each in range(MP)])]
  transfers between devices with their start and end apart: 80 -> 79, of which waited for: 17 -> 21; matrix products, arithmetic and copies ran while one was open for 25% -> 25% of each run, Pallas kernels for 34% -> 33%
where the time goes in v9:
time: 622 us; the launch traced here: 619 us
  Pallas kernels  211 us (34%)
  waiting for transfers between devices  104 us (17%)
  other arithmetic  89.9 us (14%)
  local copies, waits for them, and re-layouts  79.9 us (13%)
  starting transfers between devices  71.3 us (11%)
  matrix products  58.4 us (9%)
    pallas_call x5, Pallas kernels, row_call(): pl.pallas_call(functools.partial(kernel, len(lefts)), grid=(count,), in_s...  61.1 us
    ppermute x18, waiting for transfers between devices, swap_z(): lax.ppermute(part, 'dp', [(z * YS + y, (z ^ step) * YS + y) for z in rang...  59.6 us
    pallas_call x4, Pallas kernels, attend_back(): pl.pallas_call(functools.partial(attend_back_kernel, 512), grid=(pairs,),...  56.6 us
    unnamed x310, local copies, waits for them, and re-layouts  41.1 us
    pallas_call x4, Pallas kernels, attend(): pl.pallas_call(functools.partial(attend_kernel, 512), grid=(pairs,), in_s...  38.9 us
    dot_general x16, matrix products, dot_tn(): lax.dot_general(left, right, (((0,), (0,)), ((), ())), preferred_element_...  36.4 us
    concatenate x14, other arithmetic, join(): return jnp.concatenate([rows, arrived], -2 if axis == 'y' else -1)  28.6 us
    ppermute x43, starting transfers between devices, swap_mp(): return lax.ppermute(part, 'mp', [(each, each ^ step) for each in range(MP)])  28.2 us
  transfers between devices with their start and end apart: 79, of which 21 were waited for; matrix products, arithmetic and copies ran while one was open for 25% of the time, Pallas kernels for 33%

profile of v9, /device:TPU:0, one launch (start us, length us, event | category | flops | bytes accessed | tf_op | source)
XLA Modules:
  0.0 618.7 jit_solution(6205970287741764220)
XLA Ops:
  2.8 2.6 collective-permute-start.1
  10.5 4.9 collective-permute-done.3
  17.1 2.8 collective-permute-start.6
  25.1 4.7 collective-permute-done.4
  29.8 3.5 collective-permute-start.5
  33.3 3.9 collective-permute-done.5
  41.4 7.5 %collective-permute-done.8 = bf16[4,1792]{1,0:T(4,128)(2,1)S(1)} collective-permute-done((bf16[4,1792]{1,0:T(4,128)(2,1)S(1)}, bf16[4,1792]{1,0:T(4,128)(2,1)S(1)}, u32[]{:S(2)}, u32[]{:S(2)}) %collective-permute-start.8) | collective-permute-done | bytes 14368 | tf_op jit(solution)/shard_map/ppermute | solution.py:374
  60.4 4.1 collective-permute-done.12
  69.7 3.1 assemble_image.2
  72.9 25.0 %collective-permute-done.15 = bf16[256,1280]{1,0:T(8,128)(2,1)S(1)} collective-permute-done((bf16[256,1280]{1,0:T(8,128)(2,1)S(1)}, bf16[256,1280]{1,0:T(8,128)(2,1)S(1)}, u32[]{:S(2)}, u32[]{:S(2)}) %collective-permute-start.15) | collective-permute-done | bytes 655392 | tf_op jit(solution)/shard_map/ppermute | solution.py:368
  98.2 2.8 pad_maximum_fusion.4.refs_4_
  107.2 2.8 add_convert_fusion.9.q_ref.k_ref.v_ref
  110.1 7.1 %attend.4 = (bf16[1024,256]{1,0:T(8,128)(2,1)S(1)}, f32[2,8,1024]{2,1,0:T(8,128)S(1)}) custom-call(bf16[1024,768]{1,0:T(8,128)(2,1)S(1)} %add_convert_fusion.9.q_ref.k_ref.v_ref, bf16[1024,768]{1,0:T(8,128)(2,1)S(1)} %add_convert_fusion.9.q_ref.k_ref.v_ref, bf16[1024,768]{1,0:T(8,128)(2,1)S(1)} %add_convert_fusion.9.q_ref.k_ref.v_ref), custom_call_target="tpu_custom_call" | custom-call | tf_op jit(solution)/shard_map/attend/pallas_call | solution.py:838
  118.3 5.1 collective-permute-done.20
  129.3 3.8 add_convert_fusion.8.q_ref.k_ref.v_ref
  133.1 7.4 %attend.5 = (bf16[1024,256]{1,0:T(8,128)(2,1)S(1)}, f32[2,8,1024]{2,1,0:T(8,128)S(1)}) custom-call(bf16[1024,768]{1,0:T(8,128)(2,1)S(1)} %add_convert_fusion.8.q_ref.k_ref.v_ref, bf16[1024,768]{1,0:T(8,128)(2,1)S(1)} %add_convert_fusion.8.q_ref.k_ref.v_ref, bf16[1024,768]{1,0:T(8,128)(2,1)S(1)} %add_convert_fusion.8.q_ref.k_ref.v_ref), custom_call_target="tpu_custom_call" | custom-call | tf_op jit(solution)/shard_map/attend/pallas_call | solution.py:838
  141.3 8.3 %collective-permute-done.22 = bf16[2,1024,128]{2,1,0:T(8,128)(2,1)} collective-permute-done((bf16[2,1024,128]{2,1,0:T(8,128)(2,1)}, bf16[2,1024,128]{2,1,0:T(8,128)(2,1)}, u32[]{:S(2)}, u32[]{:S(2)}) %collective-permute-start.22) | collective-permute-done | bytes 524320 | tf_op jit(solution)/shard_map/ppermute | solution.py:378
  154.6 3.8 add_convert_fusion.7.q_ref.k_ref.v_ref
  158.5 7.1 %attend.6 = (bf16[1024,256]{1,0:T(8,128)(2,1)S(1)}, f32[2,8,1024]{2,1,0:T(8,128)S(1)}) custom-call(bf16[1024,768]{1,0:T(8,128)(2,1)S(1)} %add_convert_fusion.7.q_ref.k_ref.v_ref, bf16[1024,768]{1,0:T(8,128)(2,1)S(1)} %add_convert_fusion.7.q_ref.k_ref.v_ref, bf16[1024,768]{1,0:T(8,128)(2,1)S(1)} %add_convert_fusion.7.q_ref.k_ref.v_ref), custom_call_target="tpu_custom_call" | custom-call | tf_op jit(solution)/shard_map/attend/pallas_call | solution.py:838
  165.6 12.9 %collective-permute-done.26 = bf16[256,1024]{1,0:T(8,128)(2,1)} collective-permute-done((bf16[256,1024]{1,0:T(8,128)(2,1)}, bf16[256,1024]{1,0:T(8,128)(2,1)}, u32[]{:S(2)}, u32[]{:S(2)}) %collective-permute-start.26) | collective-permute-done | bytes 524320 | tf_op jit(solution)/shard_map/ppermute | solution.py:368
  178.6 2.9 pad_maximum_fusion.1.right_ref.refs_7_
  181.6 2.8 pad_maximum_fusion.right_ref.refs_6_
  189.0 3.8 add_convert_fusion.6.q_ref.k_ref.v_ref
  192.8 17.3 %attend.7 = (bf16[1024,256]{1,0:T(8,128)(2,1)S(1)}, f32[2,8,1024]{2,1,0:T(8,128)S(1)}) custom-call(bf16[1024,768]{1,0:T(8,128)(2,1)S(1)} %add_convert_fusion.6.q_ref.k_ref.v_ref, bf16[1024,768]{1,0:T(8,128)(2,1)S(1)} %add_convert_fusion.6.q_ref.k_ref.v_ref, bf16[1024,768]{1,0:T(8,128)(2,1)S(1)} %add_convert_fusion.6.q_ref.k_ref.v_ref), custom_call_target="tpu_custom_call" | custom-call | tf_op jit(solution)/shard_map/attend/pallas_call | solution.py:838
  219.8 6.9 %out_norm.1 = (f32[1024,1024]{1,0:T(8,128)}, f32[1024,1024]{1,0:T(8,128)}, bf16[1024,1024]{1,0:T(8,128)(2,1)}) custom-call(bf16[1024,256]{1,0:T(8,128)(2,1)S(1)} %copy-done.53, bf16[1024,256]{1,0:T(8,128)(2,1)S(1)} %copy-done.56, bf16[1024,256]{1,0:T(8,128)(2,1)S(1)} %copy-done.59, bf16[1024,256]{1,0:T(8,128)(2,1)S(1)} %copy-done.62, ...), custom_call_target="tpu_custom_call" | custom-call | tf_op jit(solution)/shard_map/out_norm/pallas_call | solution.py:744
  228.3 6.0 expand.5
  236.9 6.0 expand.4
  242.9 4.7 pad_maximum_fusion.3.refs_7_.right_ref
  247.7 3.1 pad_maximum_fusion.2.refs_6_.right_ref
  256.4 6.0 expand.7
  265.0 6.0 expand.6
  272.4 15.7 %down_output.1 = (bf16[1024,1024]{1,0:T(8,128)(2,1)S(1)}, f32[1024,1024]{1,0:T(8,128)}) custom-call(bf16[1024,1024]{1,0:T(8,128)(2,1)S(1)} %get-tuple-element.262.refs_0_, bf16[1024,1024]{1,0:T(8,128)(2,1)} %copy-done.36, bf16[1024,1024]{1,0:T(8,128)(2,1)} %copy-done.30, bf16[1024,1024]{1,0:T(8,128)(2,1)} %copy-done.28, ...), custom_call_target="tpu_custom_call" | custom-call | tf_op jit(solution)/shard_map/down_output/pallas_call | solution.py:744
  290.4 2.6 collective-permute-done.38
  295.4 3.7 convolution_convert_fusion.2
  299.1 3.7 convolution_convert_fusion.3
  312.6 2.9 multiply_reduce_fusion
  320.9 2.6 add_convert_fusion.2
  325.1 2.7 add_convert_fusion.3
  330.6 4.8 slope_product.6
  336.7 5.0 slope_product.5
  343.1 5.0 slope_product.4
  356.4 5.0 slope_product.7
  362.7 3.7 convolution_convert_fusion
  366.4 3.8 convolution_convert_fusion.1
  380.2 20.4 %up_norm_back.1 = (f32[1024,1024]{1,0:T(8,128)}, bf16[1024,1024]{1,0:T(8,128)(2,1)S(1)}, f32[8,1024]{1,0:T(8,128)S(1)}) custom-call(bf16[1024,1024]{1,0:T(8,128)(2,1)S(1)} %copy-done.47, bf16[1024,1024]{1,0:T(8,128)(2,1)} %copy-done.43, bf16[1024,1024]{1,0:T(8,128)(2,1)} %copy-done.41, bf16[1024,1024]{1,0:T(8,128)(2,1)} %copy-done.48, ...), custom_call_target="tpu_custom_call" | custom-call | tf_op jit(solution)/shard_map/up_norm_back/pallas_call | solution.py:744
  419.9 2.6 add_convert_fusion
  423.2 2.6 add_convert_fusion.1
  429.2 13.9 %attend_back.4.refs_2_ = bf16[1024,768]{1,0:T(8,128)(2,1)S(1)} custom-call(bf16[1024,768]{1,0:T(8,128)(2,1)S(1)} %copy-done.3, bf16[1024,768]{1,0:T(8,128)(2,1)S(1)} %copy-done.3, bf16[1024,768]{1,0:T(8,128)(2,1)S(1)} %copy-done.3, bf16[1024,256]{1,0:T(8,128)(2,1)S(1)} %convolution_convert_fusion.15.g_ref, f32[2,8,1024]{2,1,0:T(8,128)S(1)} %get-tuple-element.314.lse_ref), custom_call_target="tpu_custom_call" | custom-call | tf_op jit(solution)/shard_map/attend_back/pallas_call | solution.py:858
  445.1 2.8 collective-permute-done.51
  447.9 3.0 collective-permute-done.50
  451.1 2.7 collective-permute-start.59
  458.3 14.1 %attend_back.5.refs_0_ = bf16[1024,768]{1,0:T(8,128)(2,1)S(1)} custom-call(bf16[1024,768]{1,0:T(8,128)(2,1)S(1)} %add_convert_fusion.9.q_ref.k_ref.v_ref, bf16[1024,768]{1,0:T(8,128)(2,1)S(1)} %add_convert_fusion.9.q_ref.k_ref.v_ref, bf16[1024,768]{1,0:T(8,128)(2,1)S(1)} %add_convert_fusion.9.q_ref.k_ref.v_ref, ...), custom_call_target="tpu_custom_call" | custom-call | tf_op jit(solution)/shard_map/attend_back/pallas_call | solution.py:858
  472.5 2.6 spread_image.2
  477.0 4.1 collective-permute-done.56
  486.9 14.3 %attend_back.6.refs_3_ = bf16[1024,768]{1,0:T(8,128)(2,1)S(1)} custom-call(bf16[1024,768]{1,0:T(8,128)(2,1)S(1)} %copy-done.1, bf16[1024,768]{1,0:T(8,128)(2,1)S(1)} %copy-done.1, bf16[1024,768]{1,0:T(8,128)(2,1)S(1)} %copy-done.1, bf16[1024,256]{1,0:T(8,128)(2,1)S(1)} %convolution_convert_fusion.12.g_ref, f32[2,8,1024]{2,1,0:T(8,128)S(1)} %get-tuple-element.332.lse_ref), custom_call_target="tpu_custom_call" | custom-call | tf_op jit(solution)/shard_map/attend_back/pallas_call | solution.py:858
  501.2 3.1 convolution_convert_fusion.6
  508.1 3.0 multiply_subtract_fusion
  513.3 14.3 %attend_back.7.refs_1_ = bf16[1024,768]{1,0:T(8,128)(2,1)S(1)} custom-call(bf16[1024,768]{1,0:T(8,128)(2,1)S(1)} %add_convert_fusion.8.q_ref.k_ref.v_ref, bf16[1024,768]{1,0:T(8,128)(2,1)S(1)} %add_convert_fusion.8.q_ref.k_ref.v_ref, bf16[1024,768]{1,0:T(8,128)(2,1)S(1)} %add_convert_fusion.8.q_ref.k_ref.v_ref, bf16[1024,256]{1,0:T(8,128)(2,1)S(1)} %copy-done.64, ...), custom_call_target="tpu_custom_call" | custom-call | tf_op jit(solution)/shard_map/attend_back/pallas_call | solution.py:858
  536.6 9.3 %in_norm_back.3 = (bf16[512,1024]{1,0:T(8,128)(2,1)}, f32[8,1024]{1,0:T(8,128)S(1)}) custom-call(bf16[1024,768]{1,0:T(8,128)(2,1)S(1)} %copy-done.14, bf16[1024,768]{1,0:T(8,128)(2,1)S(1)} %attend_back.7.refs_1_, bf16[1024,768]{1,0:T(8,128)(2,1)S(1)} %copy-done.12, bf16[1024,768]{1,0:T(8,128)(2,1)} %copy-done.15, ...), custom_call_target="tpu_custom_call" | custom-call | tf_op jit(solution)/shard_map/in_norm_back/pallas_call | solution.py:744
  550.2 3.4 multiply_subtract_fusion.1
  564.3 8.8 %in_norm_back.2 = (bf16[512,1024]{1,0:T(8,128)(2,1)S(1)}, f32[8,1024]{1,0:T(8,128)S(1)}, f32[256,1024]{1,0:T(8,128)S(1)}) custom-call(bf16[1024,768]{1,0:T(8,128)(2,1)S(1)} %copy-done.14, bf16[1024,768]{1,0:T(8,128)(2,1)S(1)} %copy-done.17, bf16[1024,768]{1,0:T(8,128)(2,1)} %copy-done.11, bf16[1024,768]{1,0:T(8,128)(2,1)} %copy-done.15, ...), custom_call_target="tpu_custom_call" | custom-call | tf_op jit(solution)/shard_map/in_norm_back/pallas_call | solution.py:744
  576.8 2.7 collective-permute-done.66
  600.0 6.1 collective-permute-done.71
  615.4 3.1 spread_image.3
  (673 shorter events, 228.6 us)
Async XLA Ops:
  10.2 27.0 %collective-permute-start.7 = (bf16[128,1280]{1,0:T(8,128)(2,1)S(1)}, bf16[128,1280]{1,0:T(8,128)(2,1)S(1)}, u32[]{:S(2)}, u32[]{:S(2)}) collective-permute-start(bf16[128,1280]{1,0:T(8,128)(2,1)S(1)} %pad_maximum_fusion.32), channel_id=1, source_target_pairs={{0,8},{4,12},{8,0},{12,4},{16,24},{20,28},{24,16},{28,20},{1,9},{5... | collective-permute-start | bytes 983048 | tf_op jit(solution)/shard_map/ppermute | solution.py:368
  17.1 20.1 %collective-permute-start.6 = (bf16[256,768]{1,0:T(8,128)(2,1)}, bf16[256,768]{1,0:T(8,128)(2,1)}, u32[]{:S(2)}, u32[]{:S(2)}) collective-permute-start(bf16[256,768]{1,0:T(8,128)(2,1)} %pad_maximum_fusion.31), channel_id=1, source_target_pairs={{0,16},{4,20},{8,24},{12,28},{16,0},{20,4},{24,8},{28,12},{1,17},{... | collective-permute-start | bytes 1179656 | tf_op jit(solution)/shard_map/ppermute | solution.py:368
  21.9 27.7 %collective-permute-start.10 = (bf16[2,256,1024]{2,1,0:T(8,128)(2,1)}, bf16[2,256,1024]{2,1,0:T(8,128)(2,1)}, u32[]{:S(2)}, u32[]{:S(2)}) collective-permute-start(bf16[2,256,1024]{2,1,0:T(8,128)(2,1)} %pad_maximum_fusion.6), channel_id=1, source_target_pairs={{0,2},{1,3},{2,0},{3,1},{4,6},{5,7},{6,4},{7,5},{8,10},{9,11},{10,... | collective-permute-start | bytes 3145736 | tf_op jit(solution)/shard_map/ppermute | solution.py:378
  39.3 9.6 %collective-permute-start.9 = (bf16[512,384]{1,0:T(8,128)(2,1)S(1)}, bf16[512,384]{1,0:T(8,128)(2,1)S(1)}, u32[]{:S(2)}, u32[]{:S(2)}) collective-permute-start(bf16[512,384]{1,0:T(8,128)(2,1)S(1)} %get-tuple-element.510), channel_id=1, source_target_pairs={{0,4},{4,0},{8,12},{12,8},{16,20},{20,16},{24,28},{28,24},{1,5},{5... | collective-permute-start | bytes 1179656 | tf_op jit(solution)/shard_map/ppermute | solution.py:374
  52.0 12.5 %collective-permute-start.11 = (bf16[2,256,1024]{2,1,0:T(8,128)(2,1)}, bf16[2,256,1024]{2,1,0:T(8,128)(2,1)}, u32[]{:S(2)}, u32[]{:S(2)}) collective-permute-start(bf16[2,256,1024]{2,1,0:T(8,128)(2,1)} %pad_maximum_fusion.7), channel_id=1, source_target_pairs={{0,1},{1,0},{2,3},{3,2},{4,5},{5,4},{6,7},{7,6},{8,9},{9,8},{10,11... | collective-permute-start | bytes 3145736 | tf_op jit(solution)/shard_map/ppermute | solution.py:378
  52.2 12.3 %collective-permute-start.12 = (bf16[512,384]{1,0:T(8,128)(2,1)}, bf16[512,384]{1,0:T(8,128)(2,1)}, u32[]{:S(2)}, u32[]{:S(2)}) collective-permute-start(bf16[512,384]{1,0:T(8,128)(2,1)} %get-tuple-element.509), channel_id=1, source_target_pairs={{0,2},{1,3},{2,0},{3,1},{4,6},{5,7},{6,4},{7,5},{8,10},{9,11},{10,... | collective-permute-start | bytes 1179656 | tf_op jit(solution)/shard_map/ppermute | solution.py:378
  59.6 38.3 %collective-permute-start.14 = (bf16[1024,384]{1,0:T(8,128)(2,1)S(1)}, bf16[1024,384]{1,0:T(8,128)(2,1)S(1)}, u32[]{:S(2)}, u32[]{:S(2)}) collective-permute-start(bf16[1024,384]{1,0:T(8,128)(2,1)S(1)} %pad_maximum_fusion.19), channel_id=1, source_target_pairs={{0,2},{1,3},{2,0},{3,1},{4,6},{5,7},{6,4},{7,5},{8,10},{9,11},{10,... | collective-permute-start | bytes 2359304 | tf_op jit(solution)/shard_map/ppermute | solution.py:378
  65.7 32.2 %collective-permute-start.13 = (bf16[512,768]{1,0:T(8,128)(2,1)S(1)}, bf16[512,768]{1,0:T(8,128)(2,1)S(1)}, u32[]{:S(2)}, u32[]{:S(2)}) collective-permute-start(bf16[512,768]{1,0:T(8,128)(2,1)S(1)} %pad_maximum_fusion.18), channel_id=1, source_target_pairs={{0,4},{4,0},{8,12},{12,8},{16,20},{20,16},{24,28},{28,24},{1,5},{5... | collective-permute-start | bytes 2359304 | tf_op jit(solution)/shard_map/ppermute | solution.py:374
  67.2 30.7 %collective-permute-start.15 = (bf16[256,1280]{1,0:T(8,128)(2,1)S(1)}, bf16[256,1280]{1,0:T(8,128)(2,1)S(1)}, u32[]{:S(2)}, u32[]{:S(2)}) collective-permute-start(bf16[256,1280]{1,0:T(8,128)(2,1)S(1)} %pad_maximum_fusion.20), channel_id=1, source_target_pairs={{0,16},{4,20},{8,24},{12,28},{16,0},{20,4},{24,8},{28,12},{1,17},{... | collective-permute-start | bytes 1966088 | tf_op jit(solution)/shard_map/ppermute | solution.py:368
  98.1 11.9 %collective-permute-start.17 = (bf16[1024,768]{1,0:T(8,128)(2,1)S(1)}, bf16[1024,768]{1,0:T(8,128)(2,1)}, u32[]{:S(2)}, u32[]{:S(2)}) collective-permute-start(bf16[1024,768]{1,0:T(8,128)(2,1)S(1)} %pad_maximum_fusion.5.refs_5_), channel_id=1, source_target_pairs={{0,1},{1,0},{2,3},{3,2},{4,5},{5,4},{6,7},{7,6},{8,9},{9,8},{10,11... | collective-permute-start | bytes 4718600 | tf_op jit(solution)/shard_map/ppermute | solution.py:378
  103.4 13.8 %collective-permute-start.18 = (bf16[2,512,128]{2,1,0:T(8,128)(2,1)S(1)}, bf16[2,512,128]{2,1,0:T(8,128)(2,1)S(1)}, u32[]{:S(2)}, u32[]{:S(2)}) collective-permute-start(bf16[2,512,128]{2,1,0:T(8,128)(2,1)S(1)} %pad_maximum_fusion.33), channel_id=1, source_target_pairs={{0,4},{4,0},{8,12},{12,8},{16,20},{20,16},{24,28},{28,24},{1,5},{5... | collective-permute-start | bytes 786440 | tf_op jit(solution)/shard_map/ppermute | solution.py:374
  104.2 14.1 %collective-permute-start.19 = (bf16[512,512]{1,0:T(8,128)(2,1)S(1)}, bf16[512,512]{1,0:T(8,128)(2,1)S(1)}, u32[]{:S(2)}, u32[]{:S(2)}) collective-permute-start(bf16[512,512]{1,0:T(8,128)(2,1)S(1)} %get-tuple-element.477), channel_id=1, source_target_pairs={{0,2},{1,3},{2,0},{3,1},{4,6},{5,7},{6,4},{7,5},{8,10},{9,11},{10,... | collective-permute-start | bytes 1572872 | tf_op jit(solution)/shard_map/ppermute | solution.py:378
  105.7 17.8 %collective-permute-start.20 = (bf16[512,512]{1,0:T(8,128)(2,1)S(1)}, bf16[512,512]{1,0:T(8,128)(2,1)S(1)}, u32[]{:S(2)}, u32[]{:S(2)}) collective-permute-start(bf16[512,512]{1,0:T(8,128)(2,1)S(1)} %get-tuple-element.476), channel_id=1, source_target_pairs={{0,4},{4,0},{8,12},{12,8},{16,20},{20,16},{24,28},{28,24},{1,5},{5... | collective-permute-start | bytes 1572872 | tf_op jit(solution)/shard_map/ppermute | solution.py:374
  110.0 13.4 %collective-permute-start.21 = (bf16[128,1024]{1,0:T(8,128)(2,1)S(1)}, bf16[128,1024]{1,0:T(8,128)(2,1)S(1)}, u32[]{:S(2)}, u32[]{:S(2)}) collective-permute-start(bf16[128,1024]{1,0:T(8,128)(2,1)S(1)} %copy-done.99), channel_id=1, source_target_pairs={{0,8},{4,12},{8,0},{12,4},{16,24},{20,28},{24,16},{28,20},{1,9},{5... | collective-permute-start | bytes 786440 | tf_op jit(solution)/shard_map/ppermute | solution.py:368
  124.5 16.7 %collective-permute-start.24 = (bf16[1024,256]{1,0:T(8,128)(2,1)}, bf16[1024,256]{1,0:T(8,128)(2,1)}, u32[]{:S(2)}, u32[]{:S(2)}) collective-permute-start(bf16[1024,256]{1,0:T(8,128)(2,1)} %get-tuple-element.502), channel_id=1, source_target_pairs={{0,2},{1,3},{2,0},{3,1},{4,6},{5,7},{6,4},{7,5},{8,10},{9,11},{10,... | collective-permute-start | bytes 1572872 | tf_op jit(solution)/shard_map/ppermute | solution.py:378
  127.2 14.1 %collective-permute-start.23 = (bf16[256,1024]{1,0:T(8,128)(2,1)}, bf16[256,1024]{1,0:T(8,128)(2,1)}, u32[]{:S(2)}, u32[]{:S(2)}) collective-permute-start(bf16[256,1024]{1,0:T(8,128)(2,1)} %get-tuple-element.504), channel_id=1, source_target_pairs={{0,4},{4,0},{8,12},{12,8},{16,20},{20,16},{24,28},{28,24},{1,5},{5... | collective-permute-start | bytes 1572872 | tf_op jit(solution)/shard_map/ppermute | solution.py:374
  128.6 21.0 %collective-permute-start.22 = (bf16[2,1024,128]{2,1,0:T(8,128)(2,1)}, bf16[2,1024,128]{2,1,0:T(8,128)(2,1)}, u32[]{:S(2)}, u32[]{:S(2)}) collective-permute-start(bf16[2,1024,128]{2,1,0:T(8,128)(2,1)} %pad_maximum_fusion.29), channel_id=1, source_target_pairs={{0,2},{1,3},{2,0},{3,1},{4,6},{5,7},{6,4},{7,5},{8,10},{9,11},{10,... | collective-permute-start | bytes 1572872 | tf_op jit(solution)/shard_map/ppermute | solution.py:378
  151.7 26.8 %collective-permute-start.25 = (bf16[2,1024,256]{2,1,0:T(8,128)(2,1)}, bf16[2,1024,256]{2,1,0:T(8,128)(2,1)}, u32[]{:S(2)}, u32[]{:S(2)}) collective-permute-start(bf16[2,1024,256]{2,1,0:T(8,128)(2,1)} %pad_maximum_fusion.8), channel_id=1, source_target_pairs={{0,1},{1,0},{2,3},{3,2},{4,5},{5,4},{6,7},{7,6},{8,9},{9,8},{10,11... | collective-permute-start | bytes 3145736 | tf_op jit(solution)/shard_map/ppermute | solution.py:378
  152.6 25.9 %collective-permute-start.26 = (bf16[256,1024]{1,0:T(8,128)(2,1)}, bf16[256,1024]{1,0:T(8,128)(2,1)}, u32[]{:S(2)}, u32[]{:S(2)}) collective-permute-start(bf16[256,1024]{1,0:T(8,128)(2,1)} %pad_maximum_fusion.30), channel_id=1, source_target_pairs={{0,16},{4,20},{8,24},{12,28},{16,0},{20,4},{24,8},{28,12},{1,17},{... | collective-permute-start | bytes 1572872 | tf_op jit(solution)/shard_map/ppermute | solution.py:368
  152.6 25.9 %collective-permute-start.28 = (bf16[1024,256]{1,0:T(8,128)(2,1)}, bf16[1024,256]{1,0:T(8,128)(2,1)}, u32[]{:S(2)}, u32[]{:S(2)}) collective-permute-start(bf16[1024,256]{1,0:T(8,128)(2,1)} %get-tuple-element.501), channel_id=1, source_target_pairs={{0,2},{1,3},{2,0},{3,1},{4,6},{5,7},{6,4},{7,5},{8,10},{9,11},{10,... | collective-permute-start | bytes 1572872 | tf_op jit(solution)/shard_map/ppermute | solution.py:378
  154.1 24.4 %collective-permute-start.27 = (bf16[256,1024]{1,0:T(8,128)(2,1)}, bf16[256,1024]{1,0:T(8,128)(2,1)}, u32[]{:S(2)}, u32[]{:S(2)}) collective-permute-start(bf16[256,1024]{1,0:T(8,128)(2,1)} %get-tuple-element.503), channel_id=1, source_target_pairs={{0,4},{4,0},{8,12},{12,8},{16,20},{20,16},{24,28},{28,24},{1,5},{5... | collective-permute-start | bytes 1572872 | tf_op jit(solution)/shard_map/ppermute | solution.py:374
  181.5 28.8 %collective-permute-start.30 = (bf16[1024,1024]{1,0:T(8,128)(2,1)}, bf16[1024,1024]{1,0:T(8,128)(2,1)}, u32[]{:S(2)}, u32[]{:S(2)}) collective-permute-start(bf16[1024,1024]{1,0:T(8,128)(2,1)} %pad_maximum_fusion.1.right_ref.refs_7_), channel_id=1, source_target_pairs={{0,1},{1,0},{2,3},{3,2},{4,5},{5,4},{6,7},{7,6},{8,9},{9,8},{10,11... | collective-permute-start | bytes 6291464 | tf_op jit(solution)/shard_map/ppermute | solution.py:378
  184.4 25.9 %collective-permute-start.29 = (bf16[1024,1024]{1,0:T(8,128)(2,1)}, bf16[1024,1024]{1,0:T(8,128)(2,1)}, u32[]{:S(2)}, u32[]{:S(2)}) collective-permute-start(bf16[1024,1024]{1,0:T(8,128)(2,1)} %pad_maximum_fusion.right_ref.refs_6_), channel_id=1, source_target_pairs={{0,1},{1,0},{2,3},{3,2},{4,5},{5,4},{6,7},{7,6},{8,9},{9,8},{10,11... | collective-permute-start | bytes 6291464 | tf_op jit(solution)/shard_map/ppermute | solution.py:378
  187.0 23.2 %collective-permute-start.31 = (bf16[512,512]{1,0:T(8,128)(2,1)}, bf16[512,512]{1,0:T(8,128)(2,1)}, u32[]{:S(2)}, u32[]{:S(2)}) collective-permute-start(bf16[512,512]{1,0:T(8,128)(2,1)} %get-tuple-element.500), channel_id=1, source_target_pairs={{0,2},{1,3},{2,0},{3,1},{4,6},{5,7},{6,4},{7,5},{8,10},{9,11},{10,... | collective-permute-start | bytes 1572872 | tf_op jit(solution)/shard_map/ppermute | solution.py:378
  188.5 21.7 %collective-permute-start.32 = (bf16[512,512]{1,0:T(8,128)(2,1)}, bf16[512,512]{1,0:T(8,128)(2,1)}, u32[]{:S(2)}, u32[]{:S(2)}) collective-permute-start(bf16[512,512]{1,0:T(8,128)(2,1)} %get-tuple-element.499), channel_id=1, source_target_pairs={{0,4},{4,0},{8,12},{12,8},{16,20},{20,16},{24,28},{28,24},{1,5},{5... | collective-permute-start | bytes 1572872 | tf_op jit(solution)/shard_map/ppermute | solution.py:374
  212.7 30.2 %collective-permute-start.34 = (bf16[1024,512]{1,0:T(8,128)(2,1)}, bf16[1024,512]{1,0:T(8,128)(2,1)}, u32[]{:S(2)}, u32[]{:S(2)}) collective-permute-start(bf16[1024,512]{1,0:T(8,128)(2,1)} %pad_maximum_fusion.10), channel_id=1, source_target_pairs={{0,2},{1,3},{2,0},{3,1},{4,6},{5,7},{6,4},{7,5},{8,10},{9,11},{10,... | collective-permute-start | bytes 3145736 | tf_op jit(solution)/shard_map/ppermute | solution.py:378
  215.5 27.4 %collective-permute-start.33 = (bf16[512,1024]{1,0:T(8,128)(2,1)}, bf16[512,1024]{1,0:T(8,128)(2,1)}, u32[]{:S(2)}, u32[]{:S(2)}) collective-permute-start(bf16[512,1024]{1,0:T(8,128)(2,1)} %pad_maximum_fusion.9), channel_id=1, source_target_pairs={{0,4},{4,0},{8,12},{12,8},{16,20},{20,16},{24,28},{28,24},{1,5},{5... | collective-permute-start | bytes 3145736 | tf_op jit(solution)/shard_map/ppermute | solution.py:374
  247.6 24.8 %collective-permute-start.36 = (bf16[1024,1024]{1,0:T(8,128)(2,1)}, bf16[1024,1024]{1,0:T(8,128)(2,1)}, u32[]{:S(2)}, u32[]{:S(2)}) collective-permute-start(bf16[1024,1024]{1,0:T(8,128)(2,1)} %pad_maximum_fusion.3.refs_7_.right_ref), channel_id=1, source_target_pairs={{0,1},{1,0},{2,3},{3,2},{4,5},{5,4},{6,7},{7,6},{8,9},{9,8},{10,11... | collective-permute-start | bytes 6291464 | tf_op jit(solution)/shard_map/ppermute | solution.py:378
  250.8 21.6 %collective-permute-start.35 = (bf16[1024,1024]{1,0:T(8,128)(2,1)}, bf16[1024,1024]{1,0:T(8,128)(2,1)}, u32[]{:S(2)}, u32[]{:S(2)}) collective-permute-start(bf16[1024,1024]{1,0:T(8,128)(2,1)} %pad_maximum_fusion.2.refs_6_.right_ref), channel_id=1, source_target_pairs={{0,1},{1,0},{2,3},{3,2},{4,5},{5,4},{6,7},{7,6},{8,9},{9,8},{10,11... | collective-permute-start | bytes 6291464 | tf_op jit(solution)/shard_map/ppermute | solution.py:378
  253.3 34.9 %collective-permute-start.37 = (bf16[2,256,1024]{2,1,0:T(8,128)(2,1)}, bf16[2,256,1024]{2,1,0:T(8,128)(2,1)}, u32[]{:S(2)}, u32[]{:S(2)}) collective-permute-start(bf16[2,256,1024]{2,1,0:T(8,128)(2,1)} %pad_maximum_fusion.11), channel_id=1, source_target_pairs={{0,2},{1,3},{2,0},{3,1},{4,6},{5,7},{6,4},{7,5},{8,10},{9,11},{10,... | collective-permute-start | bytes 3145736 | tf_op jit(solution)/shard_map/ppermute | solution.py:378
  302.7 18.1 %collective-permute-start.40 = (bf16[1024,1024]{1,0:T(8,128)(2,1)}, bf16[1024,1024]{1,0:T(8,128)(2,1)}, u32[]{:S(2)}, u32[]{:S(2)}) collective-permute-start(bf16[1024,1024]{1,0:T(8,128)(2,1)} %convolution_convert_fusion.2), channel_id=1, source_target_pairs={{0,1},{1,0},{2,3},{3,2},{4,5},{5,4},{6,7},{7,6},{8,9},{9,8},{10,11... | collective-permute-start | bytes 6291464 | tf_op jit(solution)/shard_map/ppermute | solution.py:378
  302.9 18.0 %collective-permute-start.39 = (bf16[1024,1024]{1,0:T(8,128)(2,1)}, bf16[1024,1024]{1,0:T(8,128)(2,1)}, u32[]{:S(2)}, u32[]{:S(2)}) collective-permute-start(bf16[1024,1024]{1,0:T(8,128)(2,1)} %convolution_convert_fusion.3), channel_id=1, source_target_pairs={{0,1},{1,0},{2,3},{3,2},{4,5},{5,4},{6,7},{7,6},{8,9},{9,8},{10,11... | collective-permute-start | bytes 6291464 | tf_op jit(solution)/shard_map/ppermute | solution.py:378
  324.6 30.2 %collective-permute-start.42 = (bf16[1024,256]{1,0:T(8,128)(2,1)}, bf16[1024,256]{1,0:T(8,128)(2,1)}, u32[]{:S(2)}, u32[]{:S(2)}) collective-permute-start(bf16[1024,256]{1,0:T(8,128)(2,1)} %get-tuple-element.467), channel_id=1, source_target_pairs={{0,2},{1,3},{2,0},{3,1},{4,6},{5,7},{6,4},{7,5},{8,10},{9,11},{10,... | collective-permute-start | bytes 1572872 | tf_op jit(solution)/shard_map/ppermute | solution.py:378
  329.6 25.2 %collective-permute-start.41 = (bf16[256,1024]{1,0:T(8,128)(2,1)}, bf16[256,1024]{1,0:T(8,128)(2,1)}, u32[]{:S(2)}, u32[]{:S(2)}) collective-permute-start(bf16[256,1024]{1,0:T(8,128)(2,1)} %get-tuple-element.469), channel_id=1, source_target_pairs={{0,4},{4,0},{8,12},{12,8},{16,20},{20,16},{24,28},{28,24},{1,5},{5... | collective-permute-start | bytes 1572872 | tf_op jit(solution)/shard_map/ppermute | solution.py:374
  348.1 22.1 %collective-permute-start.44 = (bf16[1024,256]{1,0:T(8,128)(2,1)}, bf16[1024,256]{1,0:T(8,128)(2,1)}, u32[]{:S(2)}, u32[]{:S(2)}) collective-permute-start(bf16[1024,256]{1,0:T(8,128)(2,1)} %get-tuple-element.466), channel_id=1, source_target_pairs={{0,2},{1,3},{2,0},{3,1},{4,6},{5,7},{6,4},{7,5},{8,10},{9,11},{10,... | collective-permute-start | bytes 1572872 | tf_op jit(solution)/shard_map/ppermute | solution.py:378
  349.6 20.5 %collective-permute-start.43 = (bf16[256,1024]{1,0:T(8,128)(2,1)}, bf16[256,1024]{1,0:T(8,128)(2,1)}, u32[]{:S(2)}, u32[]{:S(2)}) collective-permute-start(bf16[256,1024]{1,0:T(8,128)(2,1)} %get-tuple-element.468), channel_id=1, source_target_pairs={{0,4},{4,0},{8,12},{12,8},{16,20},{20,16},{24,28},{28,24},{1,5},{5... | collective-permute-start | bytes 1572872 | tf_op jit(solution)/shard_map/ppermute | solution.py:374
  351.7 53.8 %collective-permute-start.49 = (bf16[2,256,1024]{2,1,0:T(8,128)(2,1)}, bf16[2,256,1024]{2,1,0:T(8,128)(2,1)}, u32[]{:S(2)}, u32[]{:S(2)}) collective-permute-start(bf16[2,256,1024]{2,1,0:T(8,128)(2,1)} %bitcast.79), channel_id=1, source_target_pairs={{0,2},{1,3},{2,0},{3,1},{4,6},{5,7},{6,4},{7,5},{8,10},{9,11},{10,... | collective-permute-start | bytes 3145736 | tf_op jit(solution)/shard_map/ppermute | solution.py:378
  370.2 35.3 %collective-permute-start.46 = (bf16[1024,1024]{1,0:T(8,128)(2,1)}, bf16[1024,1024]{1,0:T(8,128)(2,1)}, u32[]{:S(2)}, u32[]{:S(2)}) collective-permute-start(bf16[1024,1024]{1,0:T(8,128)(2,1)} %convolution_convert_fusion), channel_id=1, source_target_pairs={{0,1},{1,0},{2,3},{3,2},{4,5},{5,4},{6,7},{7,6},{8,9},{9,8},{10,11... | collective-permute-start | bytes 6291464 | tf_op jit(solution)/shard_map/ppermute | solution.py:378
  370.2 35.2 %collective-permute-start.45 = (bf16[1024,1024]{1,0:T(8,128)(2,1)}, bf16[1024,1024]{1,0:T(8,128)(2,1)}, u32[]{:S(2)}, u32[]{:S(2)}) collective-permute-start(bf16[1024,1024]{1,0:T(8,128)(2,1)} %convolution_convert_fusion.1), channel_id=1, source_target_pairs={{0,1},{1,0},{2,3},{3,2},{4,5},{5,4},{6,7},{7,6},{8,9},{9,8},{10,11... | collective-permute-start | bytes 6291464 | tf_op jit(solution)/shard_map/ppermute | solution.py:378
  373.2 32.2 %collective-permute-start.48 = (bf16[512,512]{1,0:T(8,128)(2,1)}, bf16[512,512]{1,0:T(8,128)(2,1)}, u32[]{:S(2)}, u32[]{:S(2)}) collective-permute-start(bf16[512,512]{1,0:T(8,128)(2,1)} %slice.506), channel_id=1, source_target_pairs={{0,4},{4,0},{8,12},{12,8},{16,20},{20,16},{24,28},{28,24},{1,5},{5... | collective-permute-start | bytes 1572872 | tf_op jit(solution)/shard_map/ppermute | solution.py:374
  377.0 28.4 %collective-permute-start.47 = (bf16[512,512]{1,0:T(8,128)(2,1)}, bf16[512,512]{1,0:T(8,128)(2,1)}, u32[]{:S(2)}, u32[]{:S(2)}) collective-permute-start(bf16[512,512]{1,0:T(8,128)(2,1)} %slice.504), channel_id=1, source_target_pairs={{0,2},{1,3},{2,0},{3,1},{4,6},{5,7},{6,4},{7,5},{8,10},{9,11},{10,... | collective-permute-start | bytes 1572872 | tf_op jit(solution)/shard_map/ppermute | solution.py:378
  416.7 28.5 %collective-permute-start.54 = (bf16[2,256,1024]{2,1,0:T(8,128)(2,1)S(1)}, bf16[2,256,1024]{2,1,0:T(8,128)(2,1)S(1)}, u32[]{:S(2)}, u32[]{:S(2)}) collective-permute-start(bf16[2,256,1024]{2,1,0:T(8,128)(2,1)S(1)} %pad_maximum_fusion.14), channel_id=1, source_target_pairs={{0,1},{1,0},{2,3},{3,2},{4,5},{5,4},{6,7},{7,6},{8,9},{9,8},{10,11... | collective-permute-start | bytes 3145736 | tf_op jit(solution)/shard_map/ppermute | solution.py:378
  419.3 25.8 %collective-permute-start.53 = (bf16[256,1024]{1,0:T(8,128)(2,1)S(1)}, bf16[256,1024]{1,0:T(8,128)(2,1)S(1)}, u32[]{:S(2)}, u32[]{:S(2)}) collective-permute-start(bf16[256,1024]{1,0:T(8,128)(2,1)S(1)} %fusion.7), channel_id=1, source_target_pairs={{0,16},{4,20},{8,24},{12,28},{16,0},{20,4},{24,8},{28,12},{1,17},{... | collective-permute-start | bytes 1572872 | tf_op jit(solution)/shard_map/ppermute | solution.py:368
  419.5 25.6 %collective-permute-start.52 = (bf16[2,1024,256]{2,1,0:T(8,128)(2,1)S(1)}, bf16[2,1024,256]{2,1,0:T(8,128)(2,1)S(1)}, u32[]{:S(2)}, u32[]{:S(2)}) collective-permute-start(bf16[2,1024,256]{2,1,0:T(8,128)(2,1)S(1)} %pad_maximum_fusion.13), channel_id=1, source_target_pairs={{0,1},{1,0},{2,3},{3,2},{4,5},{5,4},{6,7},{7,6},{8,9},{9,8},{10,11... | collective-permute-start | bytes 3145736 | tf_op jit(solution)/shard_map/ppermute | solution.py:378
  422.6 25.3 %collective-permute-start.51 = (bf16[1024,512]{1,0:T(8,128)(2,1)S(1)}, bf16[1024,512]{1,0:T(8,128)(2,1)S(1)}, u32[]{:S(2)}, u32[]{:S(2)}) collective-permute-start(bf16[1024,512]{1,0:T(8,128)(2,1)S(1)} %slice.508), channel_id=1, source_target_pairs={{0,2},{1,3},{2,0},{3,1},{4,6},{5,7},{6,4},{7,5},{8,10},{9,11},{10,... | collective-permute-start | bytes 3145736 | tf_op jit(solution)/shard_map/ppermute | solution.py:378
  425.9 25.0 %collective-permute-start.50 = (bf16[512,1024]{1,0:T(8,128)(2,1)S(1)}, bf16[512,1024]{1,0:T(8,128)(2,1)S(1)}, u32[]{:S(2)}, u32[]{:S(2)}) collective-permute-start(bf16[512,1024]{1,0:T(8,128)(2,1)S(1)} %slice.507), channel_id=1, source_target_pairs={{0,4},{4,0},{8,12},{12,8},{16,20},{20,16},{24,28},{28,24},{1,5},{5... | collective-permute-start | bytes 3145736 | tf_op jit(solution)/shard_map/ppermute | solution.py:374
  451.1 25.9 %collective-permute-start.59 = (bf16[128,1024]{1,0:T(8,128)(2,1)S(1)}, bf16[128,1024]{1,0:T(8,128)(2,1)S(1)}, u32[]{:S(2)}, u32[]{:S(2)}) collective-permute-start(bf16[128,1024]{1,0:T(8,128)(2,1)S(1)} %slice.518), channel_id=1, source_target_pairs={{0,8},{4,12},{8,0},{12,4},{16,24},{20,28},{24,16},{28,20},{1,9},{5... | collective-permute-start | bytes 786440 | tf_op jit(solution)/shard_map/ppermute | solution.py:368
  453.7 27.4 %collective-permute-start.55 = (bf16[1024,768]{1,0:T(8,128)(2,1)S(1)}, bf16[1024,768]{1,0:T(8,128)(2,1)S(1)}, u32[]{:S(2)}, u32[]{:S(2)}) collective-permute-start(bf16[1024,768]{1,0:T(8,128)(2,1)S(1)} %convolution_convert_fusion.7), channel_id=1, source_target_pairs={{0,1},{1,0},{2,3},{3,2},{4,5},{5,4},{6,7},{7,6},{8,9},{9,8},{10,11... | collective-permute-start | bytes 4718600 | tf_op jit(solution)/shard_map/ppermute | solution.py:378
  454.2 22.8 %collective-permute-start.58 = (bf16[512,512]{1,0:T(8,128)(2,1)S(1)}, bf16[512,512]{1,0:T(8,128)(2,1)S(1)}, u32[]{:S(2)}, u32[]{:S(2)}) collective-permute-start(bf16[512,512]{1,0:T(8,128)(2,1)S(1)} %slice.517), channel_id=1, source_target_pairs={{0,4},{4,0},{8,12},{12,8},{16,20},{20,16},{24,28},{28,24},{1,5},{5... | collective-permute-start | bytes 1572872 | tf_op jit(solution)/shard_map/ppermute | solution.py:374
  455.7 21.3 %collective-permute-start.57 = (bf16[512,512]{1,0:T(8,128)(2,1)S(1)}, bf16[512,512]{1,0:T(8,128)(2,1)S(1)}, u32[]{:S(2)}, u32[]{:S(2)}) collective-permute-start(bf16[512,512]{1,0:T(8,128)(2,1)S(1)} %slice.515), channel_id=1, source_target_pairs={{0,2},{1,3},{2,0},{3,1},{4,6},{5,7},{6,4},{7,5},{8,10},{9,11},{10,... | collective-permute-start | bytes 1572872 | tf_op jit(solution)/shard_map/ppermute | solution.py:378
  457.6 23.4 %collective-permute-start.56 = (bf16[2,1024,128]{2,1,0:T(8,128)(2,1)S(1)}, bf16[2,1024,128]{2,1,0:T(8,128)(2,1)S(1)}, u32[]{:S(2)}, u32[]{:S(2)}) collective-permute-start(bf16[2,1024,128]{2,1,0:T(8,128)(2,1)S(1)} %slice.513), channel_id=1, source_target_pairs={{0,2},{1,3},{2,0},{3,1},{4,6},{5,7},{6,4},{7,5},{8,10},{9,11},{10,... | collective-permute-start | bytes 1572872 | tf_op jit(solution)/shard_map/ppermute | solution.py:378
  481.6 22.7 %collective-permute-start.61 = (bf16[1024,384]{1,0:T(8,128)(2,1)S(1)}, bf16[1024,384]{1,0:T(8,128)(2,1)S(1)}, u32[]{:S(2)}, u32[]{:S(2)}) collective-permute-start(bf16[1024,384]{1,0:T(8,128)(2,1)S(1)} %slice.521), channel_id=1, source_target_pairs={{0,2},{1,3},{2,0},{3,1},{4,6},{5,7},{6,4},{7,5},{8,10},{9,11},{10,... | collective-permute-start | bytes 2359304 | tf_op jit(solution)/shard_map/ppermute | solution.py:378
  484.1 20.1 %collective-permute-start.60 = (bf16[2,512,128]{2,1,0:T(8,128)(2,1)S(1)}, bf16[2,512,128]{2,1,0:T(8,128)(2,1)S(1)}, u32[]{:S(2)}, u32[]{:S(2)}) collective-permute-start(bf16[2,512,128]{2,1,0:T(8,128)(2,1)S(1)} %slice.520), channel_id=1, source_target_pairs={{0,4},{4,0},{8,12},{12,8},{16,20},{20,16},{24,28},{28,24},{1,5},{5... | collective-permute-start | bytes 786440 | tf_op jit(solution)/shard_map/ppermute | solution.py:374
  486.5 43.0 %collective-permute-start.64 = (bf16[256,1024]{1,0:T(8,128)(2,1)}, bf16[256,1024]{1,0:T(8,128)(2,1)}, u32[]{:S(2)}, u32[]{:S(2)}) collective-permute-start(bf16[256,1024]{1,0:T(8,128)(2,1)} %fusion.6), channel_id=1, source_target_pairs={{0,16},{4,20},{8,24},{12,28},{16,0},{20,4},{24,8},{28,12},{1,17},{... | collective-permute-start | bytes 1572872 | tf_op jit(solution)/shard_map/ppermute | solution.py:368
  505.2 24.3 %collective-permute-start.63 = (bf16[1024,768]{1,0:T(8,128)(2,1)}, bf16[1024,768]{1,0:T(8,128)(2,1)}, u32[]{:S(2)}, u32[]{:S(2)}) collective-permute-start(bf16[1024,768]{1,0:T(8,128)(2,1)} %convolution_convert_fusion.6), channel_id=1, source_target_pairs={{0,1},{1,0},{2,3},{3,2},{4,5},{5,4},{6,7},{7,6},{8,9},{9,8},{10,11... | collective-permute-start | bytes 4718600 | tf_op jit(solution)/shard_map/ppermute | solution.py:378
  511.4 18.1 %collective-permute-start.62 = (bf16[512,384]{1,0:T(8,128)(2,1)S(1)}, bf16[512,384]{1,0:T(8,128)(2,1)S(1)}, u32[]{:S(2)}, u32[]{:S(2)}) collective-permute-start(bf16[512,384]{1,0:T(8,128)(2,1)S(1)} %slice.523), channel_id=1, source_target_pairs={{0,4},{4,0},{8,12},{12,8},{16,20},{20,16},{24,28},{28,24},{1,5},{5... | collective-permute-start | bytes 1179656 | tf_op jit(solution)/shard_map/ppermute | solution.py:374
  530.8 16.5 %collective-permute-start.72 = (bf16[128,1024]{1,0:T(8,128)(2,1)S(1)}, bf16[128,1024]{1,0:T(8,128)(2,1)S(1)}, u32[]{:S(2)}, u32[]{:S(2)}) collective-permute-start(bf16[128,1024]{1,0:T(8,128)(2,1)S(1)} %slice.545), channel_id=1, source_target_pairs={{0,8},{4,12},{8,0},{12,4},{16,24},{20,28},{24,16},{28,20},{1,9},{5... | collective-permute-start | bytes 786440 | tf_op jit(solution)/shard_map/ppermute | solution.py:368
  535.6 19.7 %collective-permute-start.65 = (bf16[512,768]{1,0:T(8,128)(2,1)}, bf16[512,768]{1,0:T(8,128)(2,1)}, u32[]{:S(2)}, u32[]{:S(2)}) collective-permute-start(bf16[512,768]{1,0:T(8,128)(2,1)} %slice.528), channel_id=1, source_target_pairs={{0,4},{4,0},{8,12},{12,8},{16,20},{20,16},{24,28},{28,24},{1,5},{5... | collective-permute-start | bytes 2359304 | tf_op jit(solution)/shard_map/ppermute | solution.py:374
  545.9 30.8 %collective-permute-start.67 = (bf16[2,256,1024]{2,1,0:T(8,128)(2,1)}, bf16[2,256,1024]{2,1,0:T(8,128)(2,1)}, u32[]{:S(2)}, u32[]{:S(2)}) collective-permute-start(bf16[2,256,1024]{2,1,0:T(8,128)(2,1)} %bitcast.90), channel_id=1, source_target_pairs={{0,2},{1,3},{2,0},{3,1},{4,6},{5,7},{6,4},{7,5},{8,10},{9,11},{10,... | collective-permute-start | bytes 3145736 | tf_op jit(solution)/shard_map/ppermute | solution.py:378
  563.1 16.4 %collective-permute-start.66 = (bf16[512,384]{1,0:T(8,128)(2,1)}, bf16[512,384]{1,0:T(8,128)(2,1)}, u32[]{:S(2)}, u32[]{:S(2)}) collective-permute-start(bf16[512,384]{1,0:T(8,128)(2,1)} %slice.530), channel_id=1, source_target_pairs={{0,2},{1,3},{2,0},{3,1},{4,6},{5,7},{6,4},{7,5},{8,10},{9,11},{10,... | collective-permute-start | bytes 1179656 | tf_op jit(solution)/shard_map/ppermute | solution.py:378
  582.6 17.4 %collective-permute-start.69 = (bf16[128,1024]{1,0:T(8,128)(2,1)}, bf16[128,1024]{1,0:T(8,128)(2,1)S(1)}, u32[]{:S(2)}, u32[]{:S(2)}) collective-permute-start(bf16[128,1024]{1,0:T(8,128)(2,1)} %get-tuple-element.482), channel_id=1, source_target_pairs={{0,8},{4,12},{8,0},{12,4},{16,24},{20,28},{24,16},{28,20},{1,9},{5... | collective-permute-start | bytes 786440 | tf_op jit(solution)/shard_map/ppermute | solution.py:368
  583.0 16.9 %collective-permute-start.70 = (bf16[128,1024]{1,0:T(8,128)(2,1)}, bf16[128,1024]{1,0:T(8,128)(2,1)S(1)}, u32[]{:S(2)}, u32[]{:S(2)}) collective-permute-start(bf16[128,1024]{1,0:T(8,128)(2,1)} %get-tuple-element.481), channel_id=1, source_target_pairs={{0,16},{4,20},{8,24},{12,28},{16,0},{20,4},{24,8},{28,12},{1,17},{... | collective-permute-start | bytes 786440 | tf_op jit(solution)/shard_map/ppermute | solution.py:368
  596.4 9.6 %collective-permute-start.71 = (bf16[128,1024]{1,0:T(8,128)(2,1)S(1)}, bf16[128,1024]{1,0:T(8,128)(2,1)}, u32[]{:S(2)}, u32[]{:S(2)}) collective-permute-start(bf16[128,1024]{1,0:T(8,128)(2,1)S(1)} %get-tuple-element.480), channel_id=1, source_target_pairs={{0,24},{4,28},{8,16},{12,20},{16,8},{20,12},{24,0},{28,4},{1,25},{... | collective-permute-start | bytes 786440 | tf_op jit(solution)/shard_map/ppermute | solution.py:368
  598.6 15.5 %collective-permute-start.68 = (bf16[2,256,1024]{2,1,0:T(8,128)(2,1)}, bf16[2,256,1024]{2,1,0:T(8,128)(2,1)}, u32[]{:S(2)}, u32[]{:S(2)}) collective-permute-start(bf16[2,256,1024]{2,1,0:T(8,128)(2,1)} %pad_maximum_fusion.15), channel_id=1, source_target_pairs={{0,1},{1,0},{2,3},{3,2},{4,5},{5,4},{6,7},{7,6},{8,9},{9,8},{10,11... | collective-permute-start | bytes 3145736 | tf_op jit(solution)/shard_map/ppermute | solution.py:378
  (159 other events, 1065.1 us)

commit v10 on v9

--- a/solution.py
+++ b/solution.py
@@ -836,7 +836,7 @@
     rows, width = heads.shape
     pairs = width // LANES // 3
     return pl.pallas_call(
-        functools.partial(attend_kernel, 512),
+        functools.partial(attend_kernel, 1024),
         grid=(pairs,),
         in_specs=[kind_spec(rows, kind) for kind in range(3)],
         out_specs=[
@@ -847,7 +847,7 @@
             jax.ShapeDtypeStruct((rows, pairs * LANES), BF),
             jax.ShapeDtypeStruct((pairs, 8, rows), F32),
         ],
-        compiler_params=pltpu.CompilerParams(vmem_limit_bytes=32 * 2**20),
+        compiler_params=pltpu.CompilerParams(vmem_limit_bytes=40 * 2**20),
         name="attend",
     )(heads, heads, heads)
 
@@ -856,7 +856,7 @@
     rows, width = heads.shape
     pairs = width // LANES // 3
     return pl.pallas_call(
-        functools.partial(attend_back_kernel, 512),
+        functools.partial(attend_back_kernel, 1024),
         grid=(pairs,),
         in_specs=[kind_spec(rows, kind) for kind in range(3)]
         + [
@@ -866,7 +866,7 @@
         out_specs=pl.BlockSpec((rows, 3 * LANES), lambda p: (0, p)),
         out_shape=jax.ShapeDtypeStruct((rows, width), BF),
         scratch_shapes=[pltpu.VMEM((rows, LANES), F32)] * 2,
-        compiler_params=pltpu.CompilerParams(vmem_limit_bytes=32 * 2**20),
+        compiler_params=pltpu.CompilerParams(vmem_limit_bytes=48 * 2**20),
         name="attend_back",
     )(heads, heads, heads, grad_blended, log_total)
 
@@ -936,22 +936,27 @@
     kinds = qkv_weight.shape[0]
     qkv_shard = qkv_weight.astype(BF).reshape(kinds, depth, 2, LANES).transpose(1, 2, 0, 3)
     qkv_shard = qkv_shard.reshape(depth, -1)
-    up_shard = jnp.concatenate(
-        [out_weight.T.astype(BF), up_weight.astype(BF).reshape(depth, -1)], 1
-    )
-    down_shard = down_weight.transpose(2, 0, 1).astype(BF).reshape(depth, -1)
+    up_low = up_weight.astype(BF)
+    up_shards = [
+        jnp.concatenate([out_weight.T.astype(BF), up_low[:, :half_units].reshape(depth, -1)], 1),
+        up_low[:, half_units:].reshape(depth, -1),
+    ]
+    down_low = down_weight.transpose(2, 0, 1).astype(BF)
+    down_shards = [
+        down_low[:, at : at + half_units].reshape(depth, -1) for at in (0, half_units)
+    ]
     both = ("xy", "yx")
     small = Chain(small_steps, small_shard, vector_size)
     rows_qkv = Chain(rows_z_steps, qkv_shard)
-    rows_up = Chain(rows_z_steps, up_shard)
+    rows_up = [Chain(rows_z_steps, each) for each in up_shards]
     tokens = meet(tokens, small, rows_qkv)
     fetch_tokens = fetch_image(tokens)
     meet((), small)
-    meet((), small, rows_qkv, rows_up)
+    meet((), small, rows_qkv, *rows_up)
     part_a, part_b = jnp.split(rows_qkv.result, 2, 1)
     get_qkv = [Chain(gather_steps, [part_a], ("xy",)), Chain(gather_steps, [part_b], ("yx",))]
     meet((), small, get_qkv[1], fetch_tokens)
-    tokens = meet(tokens, fetch_tokens, get_qkv[0])
+    tokens = meet(tokens, fetch_tokens, get_qkv[0], rows_up[0])
 
     vector_full, bias_small = small.result
     vector_full = vector_full.reshape(DP, vectors.shape[0], LANES).transpose(1, 0, 2)
@@ -962,10 +967,10 @@
     bias_full = bias_full.astype(F32)
 
     base, normed_one = assemble_image(place, vector_full, tokens[:, 0], fetch_tokens.result, True)
-    normed_one = meet(normed_one, *get_qkv, rows_up)
-    out_rows, up_rows = jnp.split(rows_up.result, [block_width], 1)
+    normed_one = meet(normed_one, *get_qkv, rows_up[1])
+    out_rows, up_rows = jnp.split(rows_up[0].result, [block_width], 1)
     get_out = Chain(gather_steps, [jnp.stack(jnp.split(out_rows, 2, 1))], ("yx",))
-    get_up = Chain(gather_steps, jnp.split(up_rows, 2, 1), both, (1, 2))
+    get_up = Chain(gather_steps, [up_rows, rows_up[1].result], both, (1, 2))
 
     def project(core, half, weight):
         lanes = slice(half * LANES, (half + 1) * LANES)
@@ -979,23 +984,27 @@
         blended[core][half], log_total[core][half] = attend(heads[core][half])
 
     heads[0][0] = project(0, 0, get_qkv[0].own[0])
-    heads[0][0], down_shard = meet((heads[0][0], down_shard), *get_qkv)
+    heads[0][0], down_shards = meet((heads[0][0], down_shards), *get_qkv)
     w_qkv = [[each.own[0] for each in get_qkv], [each.result[0] for each in get_qkv]]
-    rows_down = Chain(rows_z_steps, down_shard)
+    rows_down = [Chain(rows_z_steps, each) for each in down_shards]
     forward_heads(0, 0)
-    blended[0][0], normed_one = meet((blended[0][0], normed_one), get_out, get_up, rows_down)
+    blended[0][0], normed_one = meet(
+        (blended[0][0], normed_one), get_out, get_up, *rows_down
+    )
     heads[0][1] = project(0, 1, w_qkv[0][1])
     forward_heads(0, 1)
-    blended[0][1], normed_one = meet((blended[0][1], normed_one), get_out, get_up)
+    blended[0][1], normed_one = meet(
+        (blended[0][1], normed_one), get_up, rows_down[0]
+    )
     heads[1][0] = project(1, 0, w_qkv[1][0])
     forward_heads(1, 0)
     blended[1][0], normed_one = meet(
-        (blended[1][0], normed_one), get_out, rows_down, get_up
-    )
-    get_down = Chain(gather_steps, jnp.split(rows_down.result, 2, 1), both)
+        (blended[1][0], normed_one), get_out, rows_down[1], get_up
+    )
+    get_down = Chain(gather_steps, [each.result for each in rows_down], both)
     heads[1][1] = project(1, 1, w_qkv[1][1])
     forward_heads(1, 1)
-    blended = meet(blended, get_up, get_down)
+    blended = meet(blended, get_up, get_down, get_out)
     w_out = [[each[0][half] for half in (0, 1)] for each in (get_out.own, get_out.result)]
     pairs = [(core, half) for core in cores for half in (0, 1)]
     branch_one, hidden, normed_two = row_call(

time: 622 us -> 627 us (level)
  waiting for transfers between devices: 104 us -> 73.1 us
  other arithmetic: 89.9 us -> 109 us
  local copies, waits for them, and re-layouts: 79.9 us -> 97.6 us
  Pallas kernels: 211 us -> 202 us
    ppermute x43, waiting for transfers between devices: 25.8 us -> 5.98 us  [swap_mp(): return lax.ppermute(part, 'mp', [(each, each ^ step) for each in range(MP)])]
    ppermute x18 -> x22, waiting for transfers between devices: 59.6 us -> 42.9 us  [swap_z(): lax.ppermute(part, 'dp', [(z * YS + y, (z ^ step) * YS + y) for z in rang...]
    pallas_call x8, Pallas kernels: 95.5 us -> 86 us  [the longest x4 55.5 us: attend_back(): pl.pallas_call(functools.partial(attend_back_kernel, 1024), grid=(pairs,)...]
    unnamed x310 -> x331, local copies, waits for them, and re-layouts: 41.1 us -> 49.4 us
    convert_element_type x23, other arithmetic: 25.2 us -> 32.2 us  [add_low(): return (first.astype(F32) + second.astype(F32)).astype(BF)]
    ppermute x18 -> x22, starting transfers between devices: 25.4 us -> 27.2 us  [swap_z(): lax.ppermute(part, 'dp', [(z * YS + y, (z ^ step) * YS + y) for z in rang...]
    concatenate x14 -> x13, other arithmetic: 28.6 us -> 29.5 us  [join(): return jnp.concatenate([rows, arrived], -2 if axis == 'y' else -1)]
  transfers between devices with their start and end apart: 79 -> 83, of which waited for: 21 -> 20; matrix products, arithmetic and copies ran while one was open for 25% -> 30% of each run, Pallas kernels for 33% -> 32%
where the time goes in v10:
time: 627 us; the launch traced here: 618 us
  Pallas kernels  202 us (32%)
  other arithmetic  109 us (17%)
  local copies, waits for them, and re-layouts  97.6 us (16%)
  starting transfers between devices  77.1 us (12%)
  waiting for transfers between devices  73.1 us (12%)
  matrix products  55.7 us (9%)
    pallas_call x5, Pallas kernels, row_call(): pl.pallas_call(functools.partial(kernel, len(lefts)), grid=(count,), in_s...  61.1 us
    pallas_call x4, Pallas kernels, attend_back(): pl.pallas_call(functools.partial(attend_back_kernel, 1024), grid=(pairs,)...  55.5 us
    unnamed x331, local copies, waits for them, and re-layouts  49.4 us
    ppermute x22, waiting for transfers between devices, swap_z(): lax.ppermute(part, 'dp', [(z * YS + y, (z ^ step) * YS + y) for z in rang...  42.9 us
    dot_general x16, matrix products, dot_tn(): lax.dot_general(left, right, (((0,), (0,)), ((), ())), preferred_element_...  38.8 us
    convert_element_type x23, other arithmetic, add_low(): return (first.astype(F32) + second.astype(F32)).astype(BF)  32.2 us
    pallas_call x4, Pallas kernels, attend(): pl.pallas_call(functools.partial(attend_kernel, 1024), grid=(pairs,), in_...  30.5 us
    ppermute x43, starting transfers between devices, swap_mp(): return lax.ppermute(part, 'mp', [(each, each ^ step) for each in range(MP)])  30.4 us
  transfers between devices with their start and end apart: 83, of which 20 were waited for; matrix products, arithmetic and copies ran while one was open for 30% of the time, Pallas kernels for 32%

profile of v10, /device:TPU:0, one launch (start us, length us, event | category | flops | bytes accessed | tf_op | source)
XLA Modules:
  0.0 618.4 jit_solution(38421974695898935)
XLA Ops:
  2.7 2.6 collective-permute-start.1
  17.2 2.7 collective-permute-start.6
  23.3 3.3 collective-permute-done.4
  27.5 9.2 %collective-permute-done.5 = bf16[2,1792]{1,0:T(2,128)(2,1)S(1)} collective-permute-done((bf16[2,1792]{1,0:T(2,128)(2,1)S(1)}, bf16[2,1792]{1,0:T(2,128)(2,1)S(1)}, u32[]{:S(2)}, u32[]{:S(2)}) %collective-permute-start.5) | collective-permute-done | bytes 7200 | tf_op jit(solution)/shard_map/ppermute | solution.py:368
  39.9 6.1 collective-permute-done.9
  61.4 2.9 collective-permute-start.17
  66.8 14.8 %collective-permute-done.14 = bf16[256,768]{1,0:T(8,128)(2,1)} collective-permute-done((bf16[256,768]{1,0:T(8,128)(2,1)}, bf16[256,768]{1,0:T(8,128)(2,1)}, u32[]{:S(2)}, u32[]{:S(2)}) %collective-permute-start.14) | collective-permute-done | bytes 393248 | tf_op jit(solution)/shard_map/ppermute | solution.py:368
  89.1 3.1 assemble_image.2
  92.3 11.0 %collective-permute-done.15 = bf16[512,768]{1,0:T(8,128)(2,1)} collective-permute-done((bf16[512,768]{1,0:T(8,128)(2,1)}, bf16[512,768]{1,0:T(8,128)(2,1)}, u32[]{:S(2)}, u32[]{:S(2)}) %collective-permute-start.15) | collective-permute-done | bytes 786464 | tf_op jit(solution)/shard_map/ppermute | solution.py:374
  104.8 3.1 pad_maximum_fusion.4.refs_4_
  116.1 3.8 add_convert_fusion.9.q_ref.k_ref.v_ref
  122.1 7.5 %attend.4 = (bf16[1024,256]{1,0:T(8,128)(2,1)S(1)}, f32[2,8,1024]{2,1,0:T(8,128)S(1)}) custom-call(bf16[1024,768]{1,0:T(8,128)(2,1)S(1)} %add_convert_fusion.9.q_ref.k_ref.v_ref, bf16[1024,768]{1,0:T(8,128)(2,1)S(1)} %add_convert_fusion.9.q_ref.k_ref.v_ref, bf16[1024,768]{1,0:T(8,128)(2,1)S(1)} %add_convert_fusion.9.q_ref.k_ref.v_ref), custom_call_target="tpu_custom_call" | custom-call | tf_op jit(solution)/shard_map/attend/pallas_call | solution.py:838
  139.7 3.0 add_convert_fusion.8.q_ref.k_ref.v_ref
  142.8 4.0 collective-permute-done.27
  149.9 8.0 %attend.5 = (bf16[1024,256]{1,0:T(8,128)(2,1)S(1)}, f32[2,8,1024]{2,1,0:T(8,128)S(1)}) custom-call(bf16[1024,768]{1,0:T(8,128)(2,1)S(1)} %add_convert_fusion.8.q_ref.k_ref.v_ref, bf16[1024,768]{1,0:T(8,128)(2,1)S(1)} %add_convert_fusion.8.q_ref.k_ref.v_ref, bf16[1024,768]{1,0:T(8,128)(2,1)S(1)} %add_convert_fusion.8.q_ref.k_ref.v_ref), custom_call_target="tpu_custom_call" | custom-call | tf_op jit(solution)/shard_map/attend/pallas_call | solution.py:838
  158.7 3.2 add_convert_fusion.7.q_ref.k_ref.v_ref
  161.9 7.5 %attend.6 = (bf16[1024,256]{1,0:T(8,128)(2,1)S(1)}, f32[2,8,1024]{2,1,0:T(8,128)S(1)}) custom-call(bf16[1024,768]{1,0:T(8,128)(2,1)S(1)} %add_convert_fusion.7.q_ref.k_ref.v_ref, bf16[1024,768]{1,0:T(8,128)(2,1)S(1)} %add_convert_fusion.7.q_ref.k_ref.v_ref, bf16[1024,768]{1,0:T(8,128)(2,1)S(1)} %add_convert_fusion.7.q_ref.k_ref.v_ref), custom_call_target="tpu_custom_call" | custom-call | tf_op jit(solution)/shard_map/attend/pallas_call | solution.py:838
  169.4 2.5 collective-permute-done.29
  172.0 4.8 pad_maximum_fusion.1.right_ref.refs_7_
  176.8 2.7 pad_maximum_fusion.right_ref.refs_6_
  189.9 3.2 add_convert_fusion.6.q_ref.k_ref.v_ref
  193.2 7.5 %attend.7 = (bf16[1024,256]{1,0:T(8,128)(2,1)S(1)}, f32[2,8,1024]{2,1,0:T(8,128)S(1)}) custom-call(bf16[1024,768]{1,0:T(8,128)(2,1)S(1)} %add_convert_fusion.6.q_ref.k_ref.v_ref, bf16[1024,768]{1,0:T(8,128)(2,1)S(1)} %add_convert_fusion.6.q_ref.k_ref.v_ref, bf16[1024,768]{1,0:T(8,128)(2,1)S(1)} %add_convert_fusion.6.q_ref.k_ref.v_ref), custom_call_target="tpu_custom_call" | custom-call | tf_op jit(solution)/shard_map/attend/pallas_call | solution.py:838
  210.5 6.9 %out_norm.1 = (f32[1024,1024]{1,0:T(8,128)}, f32[1024,1024]{1,0:T(8,128)}, bf16[1024,1024]{1,0:T(8,128)(2,1)}) custom-call(bf16[1024,256]{1,0:T(8,128)(2,1)S(1)} %copy-done.53, bf16[1024,256]{1,0:T(8,128)(2,1)S(1)} %copy-done.56, bf16[1024,256]{1,0:T(8,128)(2,1)S(1)} %copy-done.59, bf16[1024,256]{1,0:T(8,128)(2,1)S(1)} %copy-done.62, ...), custom_call_target="tpu_custom_call" | custom-call | tf_op jit(solution)/shard_map/out_norm/pallas_call | solution.py:744
  219.0 6.0 expand.5
  227.6 6.0 expand.4
  233.7 4.7 pad_maximum_fusion.3.refs_7_.right_ref
  238.5 2.9 pad_maximum_fusion.2.refs_6_.right_ref
  245.8 6.0 expand.7
  254.6 6.0 expand.6
  261.9 15.7 %down_output.1 = (bf16[1024,1024]{1,0:T(8,128)(2,1)S(1)}, f32[1024,1024]{1,0:T(8,128)}) custom-call(bf16[1024,1024]{1,0:T(8,128)(2,1)S(1)} %get-tuple-element.272.refs_0_, bf16[1024,1024]{1,0:T(8,128)(2,1)} %copy-done.36, bf16[1024,1024]{1,0:T(8,128)(2,1)} %copy-done.30, bf16[1024,1024]{1,0:T(8,128)(2,1)} %copy-done.28, ...), custom_call_target="tpu_custom_call" | custom-call | tf_op jit(solution)/shard_map/down_output/pallas_call | solution.py:744
  279.9 2.6 collective-permute-done.42
  284.8 3.7 convolution_convert_fusion.2
  288.5 3.7 convolution_convert_fusion.3
  302.1 2.9 multiply_reduce_fusion
  308.0 2.4 fusion.37
  310.4 2.6 add_convert_fusion.2
  315.7 2.7 add_convert_fusion.3
  321.1 4.8 slope_product.6
  327.3 5.0 slope_product.5
  333.7 5.0 slope_product.4
  347.0 5.0 slope_product.7
  353.3 3.7 convolution_convert_fusion
  357.0 3.7 convolution_convert_fusion.1
  369.6 20.4 %up_norm_back.1 = (f32[1024,1024]{1,0:T(8,128)}, bf16[1024,1024]{1,0:T(8,128)(2,1)S(1)}, f32[8,1024]{1,0:T(8,128)S(1)}) custom-call(bf16[1024,1024]{1,0:T(8,128)(2,1)S(1)} %copy-done.47, bf16[1024,1024]{1,0:T(8,128)(2,1)} %copy-done.43, bf16[1024,1024]{1,0:T(8,128)(2,1)} %copy-done.41, bf16[1024,1024]{1,0:T(8,128)(2,1)} %copy-done.48, ...), custom_call_target="tpu_custom_call" | custom-call | tf_op jit(solution)/shard_map/up_norm_back/pallas_call | solution.py:744
  390.1 2.4 fusion.40
  392.5 2.4 fusion.39
  408.9 2.5 add_convert_fusion
  414.0 2.5 add_convert_fusion.1
  422.0 13.7 %attend_back.4.refs_2_ = bf16[1024,768]{1,0:T(8,128)(2,1)S(1)} custom-call(bf16[1024,768]{1,0:T(8,128)(2,1)S(1)} %copy-done.3, bf16[1024,768]{1,0:T(8,128)(2,1)S(1)} %copy-done.3, bf16[1024,768]{1,0:T(8,128)(2,1)S(1)} %copy-done.3, bf16[1024,256]{1,0:T(8,128)(2,1)S(1)} %convolution_convert_fusion.15.g_ref, f32[2,8,1024]{2,1,0:T(8,128)S(1)} %get-tuple-element.324.lse_ref), custom_call_target="tpu_custom_call" | custom-call | tf_op jit(solution)/shard_map/attend_back/pallas_call | solution.py:858
  435.7 3.1 convolution_convert_fusion.7
  438.8 3.9 collective-permute-done.54
  458.1 14.1 %attend_back.5.refs_0_ = bf16[1024,768]{1,0:T(8,128)(2,1)S(1)} custom-call(bf16[1024,768]{1,0:T(8,128)(2,1)S(1)} %add_convert_fusion.9.q_ref.k_ref.v_ref, bf16[1024,768]{1,0:T(8,128)(2,1)S(1)} %add_convert_fusion.9.q_ref.k_ref.v_ref, bf16[1024,768]{1,0:T(8,128)(2,1)S(1)} %add_convert_fusion.9.q_ref.k_ref.v_ref, ...), custom_call_target="tpu_custom_call" | custom-call | tf_op jit(solution)/shard_map/attend_back/pallas_call | solution.py:858
  472.3 2.6 spread_image.2
  485.9 13.9 %attend_back.6.refs_3_ = bf16[1024,768]{1,0:T(8,128)(2,1)S(1)} custom-call(bf16[1024,768]{1,0:T(8,128)(2,1)S(1)} %copy-done.1, bf16[1024,768]{1,0:T(8,128)(2,1)S(1)} %copy-done.1, bf16[1024,768]{1,0:T(8,128)(2,1)S(1)} %copy-done.1, bf16[1024,256]{1,0:T(8,128)(2,1)S(1)} %convolution_convert_fusion.12.g_ref, f32[2,8,1024]{2,1,0:T(8,128)S(1)} %get-tuple-element.342.lse_ref), custom_call_target="tpu_custom_call" | custom-call | tf_op jit(solution)/shard_map/attend_back/pallas_call | solution.py:858
  499.8 3.1 convolution_convert_fusion.6
  507.7 3.0 multiply_subtract_fusion
  512.8 13.9 %attend_back.7.refs_1_ = bf16[1024,768]{1,0:T(8,128)(2,1)S(1)} custom-call(bf16[1024,768]{1,0:T(8,128)(2,1)S(1)} %add_convert_fusion.8.q_ref.k_ref.v_ref, bf16[1024,768]{1,0:T(8,128)(2,1)S(1)} %add_convert_fusion.8.q_ref.k_ref.v_ref, bf16[1024,768]{1,0:T(8,128)(2,1)S(1)} %add_convert_fusion.8.q_ref.k_ref.v_ref, bf16[1024,256]{1,0:T(8,128)(2,1)S(1)} %copy-done.64, ...), custom_call_target="tpu_custom_call" | custom-call | tf_op jit(solution)/shard_map/attend_back/pallas_call | solution.py:858
  535.8 9.3 %in_norm_back.3 = (bf16[512,1024]{1,0:T(8,128)(2,1)}, f32[8,1024]{1,0:T(8,128)S(1)}) custom-call(bf16[1024,768]{1,0:T(8,128)(2,1)S(1)} %copy-done.14, bf16[1024,768]{1,0:T(8,128)(2,1)S(1)} %attend_back.7.refs_1_, bf16[1024,768]{1,0:T(8,128)(2,1)S(1)} %copy-done.12, bf16[1024,768]{1,0:T(8,128)(2,1)} %copy-done.15, ...), custom_call_target="tpu_custom_call" | custom-call | tf_op jit(solution)/shard_map/in_norm_back/pallas_call | solution.py:744
  550.4 3.4 multiply_subtract_fusion.1
  564.5 8.8 %in_norm_back.2 = (bf16[512,1024]{1,0:T(8,128)(2,1)S(1)}, f32[8,1024]{1,0:T(8,128)S(1)}, f32[256,1024]{1,0:T(8,128)S(1)}) custom-call(bf16[1024,768]{1,0:T(8,128)(2,1)S(1)} %copy-done.14, bf16[1024,768]{1,0:T(8,128)(2,1)S(1)} %copy-done.17, bf16[1024,768]{1,0:T(8,128)(2,1)} %copy-done.11, bf16[1024,768]{1,0:T(8,128)(2,1)} %copy-done.15, ...), custom_call_target="tpu_custom_call" | custom-call | tf_op jit(solution)/shard_map/in_norm_back/pallas_call | solution.py:744
  589.2 2.6 collective-permute-start.81
  595.9 2.4 collective-permute-start.75
  600.1 5.4 collective-permute-done.75
  614.9 3.1 spread_image.3
  (710 shorter events, 260.0 us)
Async XLA Ops:
  11.4 16.1 %collective-permute-start.7 = (bf16[128,768]{1,0:T(8,128)(2,1)S(1)}, bf16[128,768]{1,0:T(8,128)(2,1)S(1)}, u32[]{:S(2)}, u32[]{:S(2)}) collective-permute-start(bf16[128,768]{1,0:T(8,128)(2,1)S(1)} %pad_maximum_fusion.35), channel_id=1, source_target_pairs={{0,8},{4,12},{8,0},{12,4},{16,24},{20,28},{24,16},{28,20},{1,9},{5... | collective-permute-start | bytes 589832 | tf_op jit(solution)/shard_map/ppermute | solution.py:368
  12.2 15.3 %collective-permute-start.8 = (bf16[128,512]{1,0:T(8,128)(2,1)S(1)}, bf16[128,512]{1,0:T(8,128)(2,1)S(1)}, u32[]{:S(2)}, u32[]{:S(2)}) collective-permute-start(bf16[128,512]{1,0:T(8,128)(2,1)S(1)} %copy.128), channel_id=1, source_target_pairs={{0,8},{4,12},{8,0},{12,4},{16,24},{20,28},{24,16},{28,20},{1,9},{5... | collective-permute-start | bytes 393224 | tf_op jit(solution)/shard_map/ppermute | solution.py:368
  17.2 19.5 %collective-permute-start.6 = (bf16[256,768]{1,0:T(8,128)(2,1)S(1)}, bf16[256,768]{1,0:T(8,128)(2,1)S(1)}, u32[]{:S(2)}, u32[]{:S(2)}) collective-permute-start(bf16[256,768]{1,0:T(8,128)(2,1)S(1)} %pad_maximum_fusion.29), channel_id=1, source_target_pairs={{0,16},{4,20},{8,24},{12,28},{16,0},{20,4},{24,8},{28,12},{1,17},{... | collective-permute-start | bytes 1179656 | tf_op jit(solution)/shard_map/ppermute | solution.py:368
  21.8 24.2 %collective-permute-start.11 = (bf16[2,256,1024]{2,1,0:T(8,128)(2,1)}, bf16[2,256,1024]{2,1,0:T(8,128)(2,1)}, u32[]{:S(2)}, u32[]{:S(2)}) collective-permute-start(bf16[2,256,1024]{2,1,0:T(8,128)(2,1)} %pad_maximum_fusion.6), channel_id=1, source_target_pairs={{0,2},{1,3},{2,0},{3,1},{4,6},{5,7},{6,4},{7,5},{8,10},{9,11},{10,... | collective-permute-start | bytes 3145736 | tf_op jit(solution)/shard_map/ppermute | solution.py:378
  49.4 32.1 %collective-permute-start.12 = (bf16[2,256,1024]{2,1,0:T(8,128)(2,1)}, bf16[2,256,1024]{2,1,0:T(8,128)(2,1)}, u32[]{:S(2)}, u32[]{:S(2)}) collective-permute-start(bf16[2,256,1024]{2,1,0:T(8,128)(2,1)} %pad_maximum_fusion.7), channel_id=1, source_target_pairs={{0,1},{1,0},{2,3},{3,2},{4,5},{5,4},{6,7},{7,6},{8,9},{9,8},{10,11... | collective-permute-start | bytes 3145736 | tf_op jit(solution)/shard_map/ppermute | solution.py:378
  51.9 14.9 %collective-permute-start.13 = (bf16[512,384]{1,0:T(8,128)(2,1)S(1)}, bf16[512,384]{1,0:T(8,128)(2,1)}, u32[]{:S(2)}, u32[]{:S(2)}) collective-permute-start(bf16[512,384]{1,0:T(8,128)(2,1)S(1)} %get-tuple-element.515), channel_id=1, source_target_pairs={{0,2},{1,3},{2,0},{3,1},{4,6},{5,7},{6,4},{7,5},{8,10},{9,11},{10,... | collective-permute-start | bytes 1179656 | tf_op jit(solution)/shard_map/ppermute | solution.py:378
  55.1 26.4 %collective-permute-start.14 = (bf16[256,768]{1,0:T(8,128)(2,1)}, bf16[256,768]{1,0:T(8,128)(2,1)}, u32[]{:S(2)}, u32[]{:S(2)}) collective-permute-start(bf16[256,768]{1,0:T(8,128)(2,1)} %pad_maximum_fusion.30), channel_id=1, source_target_pairs={{0,16},{4,20},{8,24},{12,28},{16,0},{20,4},{24,8},{28,12},{1,17},{... | collective-permute-start | bytes 1179656 | tf_op jit(solution)/shard_map/ppermute | solution.py:368
  61.4 30.9 %collective-permute-start.17 = (bf16[256,512]{1,0:T(8,128)(2,1)}, bf16[256,512]{1,0:T(8,128)(2,1)}, u32[]{:S(2)}, u32[]{:S(2)}) collective-permute-start(bf16[256,512]{1,0:T(8,128)(2,1)} %pad_maximum_fusion.31), channel_id=1, source_target_pairs={{0,16},{4,20},{8,24},{12,28},{16,0},{20,4},{24,8},{28,12},{1,17},{... | collective-permute-start | bytes 786440 | tf_op jit(solution)/shard_map/ppermute | solution.py:368
  66.2 26.0 %collective-permute-start.16 = (bf16[1024,384]{1,0:T(8,128)(2,1)}, bf16[1024,384]{1,0:T(8,128)(2,1)}, u32[]{:S(2)}, u32[]{:S(2)}) collective-permute-start(bf16[1024,384]{1,0:T(8,128)(2,1)} %pad_maximum_fusion.19), channel_id=1, source_target_pairs={{0,2},{1,3},{2,0},{3,1},{4,6},{5,7},{6,4},{7,5},{8,10},{9,11},{10,... | collective-permute-start | bytes 2359304 | tf_op jit(solution)/shard_map/ppermute | solution.py:378
  83.5 19.7 %collective-permute-start.15 = (bf16[512,768]{1,0:T(8,128)(2,1)}, bf16[512,768]{1,0:T(8,128)(2,1)}, u32[]{:S(2)}, u32[]{:S(2)}) collective-permute-start(bf16[512,768]{1,0:T(8,128)(2,1)} %pad_maximum_fusion.18), channel_id=1, source_target_pairs={{0,4},{4,0},{8,12},{12,8},{16,20},{20,16},{24,28},{28,24},{1,5},{5... | collective-permute-start | bytes 2359304 | tf_op jit(solution)/shard_map/ppermute | solution.py:374
  104.7 15.3 %collective-permute-start.19 = (bf16[1024,768]{1,0:T(8,128)(2,1)S(1)}, bf16[1024,768]{1,0:T(8,128)(2,1)}, u32[]{:S(2)}, u32[]{:S(2)}) collective-permute-start(bf16[1024,768]{1,0:T(8,128)(2,1)S(1)} %pad_maximum_fusion.5.refs_5_), channel_id=1, source_target_pairs={{0,1},{1,0},{2,3},{3,2},{4,5},{5,4},{6,7},{7,6},{8,9},{9,8},{10,11... | collective-permute-start | bytes 4718600 | tf_op jit(solution)/shard_map/ppermute | solution.py:378
  110.0 19.6 %collective-permute-start.20 = (bf16[2,512,128]{2,1,0:T(8,128)(2,1)}, bf16[2,512,128]{2,1,0:T(8,128)(2,1)}, u32[]{:S(2)}, u32[]{:S(2)}) collective-permute-start(bf16[2,512,128]{2,1,0:T(8,128)(2,1)} %pad_maximum_fusion.32), channel_id=1, source_target_pairs={{0,4},{4,0},{8,12},{12,8},{16,20},{20,16},{24,28},{28,24},{1,5},{5... | collective-permute-start | bytes 786440 | tf_op jit(solution)/shard_map/ppermute | solution.py:374
  113.3 16.3 %collective-permute-start.21 = (bf16[512,512]{1,0:T(8,128)(2,1)}, bf16[512,512]{1,0:T(8,128)(2,1)}, u32[]{:S(2)}, u32[]{:S(2)}) collective-permute-start(bf16[512,512]{1,0:T(8,128)(2,1)} %pad_maximum_fusion.23), channel_id=1, source_target_pairs={{0,2},{1,3},{2,0},{3,1},{4,6},{5,7},{6,4},{7,5},{8,10},{9,11},{10,... | collective-permute-start | bytes 1572872 | tf_op jit(solution)/shard_map/ppermute | solution.py:378
  115.6 14.6 %collective-permute-start.22 = (bf16[512,512]{1,0:T(8,128)(2,1)}, bf16[512,512]{1,0:T(8,128)(2,1)}, u32[]{:S(2)}, u32[]{:S(2)}) collective-permute-start(bf16[512,512]{1,0:T(8,128)(2,1)} %pad_maximum_fusion.26), channel_id=1, source_target_pairs={{0,4},{4,0},{8,12},{12,8},{16,20},{20,16},{24,28},{28,24},{1,5},{5... | collective-permute-start | bytes 1572872 | tf_op jit(solution)/shard_map/ppermute | solution.py:374
  131.4 40.6 %collective-permute-start.28 = (bf16[2,1024,128]{2,1,0:T(8,128)(2,1)S(1)}, bf16[2,1024,128]{2,1,0:T(8,128)(2,1)S(1)}, u32[]{:S(2)}, u32[]{:S(2)}) collective-permute-start(bf16[2,1024,128]{2,1,0:T(8,128)(2,1)S(1)} %pad_maximum_fusion.27), channel_id=1, source_target_pairs={{0,2},{1,3},{2,0},{3,1},{4,6},{5,7},{6,4},{7,5},{8,10},{9,11},{10,... | collective-permute-start | bytes 1572872 | tf_op jit(solution)/shard_map/ppermute | solution.py:378
  133.3 13.4 %collective-permute-start.27 = (bf16[256,512]{1,0:T(8,128)(2,1)S(1)}, bf16[256,512]{1,0:T(8,128)(2,1)S(1)}, u32[]{:S(2)}, u32[]{:S(2)}) collective-permute-start(bf16[256,512]{1,0:T(8,128)(2,1)S(1)} %pad_maximum_fusion.33), channel_id=1, source_target_pairs={{0,16},{4,20},{8,24},{12,28},{16,0},{20,4},{24,8},{28,12},{1,17},{... | collective-permute-start | bytes 786440 | tf_op jit(solution)/shard_map/ppermute | solution.py:368
  134.7 23.9 %collective-permute-start.26 = (bf16[1024,256]{1,0:T(8,128)(2,1)S(1)}, bf16[1024,256]{1,0:T(8,128)(2,1)S(1)}, u32[]{:S(2)}, u32[]{:S(2)}) collective-permute-start(bf16[1024,256]{1,0:T(8,128)(2,1)S(1)} %get-tuple-element.506), channel_id=1, source_target_pairs={{0,2},{1,3},{2,0},{3,1},{4,6},{5,7},{6,4},{7,5},{8,10},{9,11},{10,... | collective-permute-start | bytes 1572872 | tf_op jit(solution)/shard_map/ppermute | solution.py:378
  137.1 21.5 %collective-permute-start.25 = (bf16[256,1024]{1,0:T(8,128)(2,1)S(1)}, bf16[256,1024]{1,0:T(8,128)(2,1)S(1)}, u32[]{:S(2)}, u32[]{:S(2)}) collective-permute-start(bf16[256,1024]{1,0:T(8,128)(2,1)S(1)} %get-tuple-element.508), channel_id=1, source_target_pairs={{0,4},{4,0},{8,12},{12,8},{16,20},{20,16},{24,28},{28,24},{1,5},{5... | collective-permute-start | bytes 1572872 | tf_op jit(solution)/shard_map/ppermute | solution.py:374
  138.7 33.2 %collective-permute-start.31 = (bf16[1024,256]{1,0:T(8,128)(2,1)S(1)}, bf16[1024,256]{1,0:T(8,128)(2,1)S(1)}, u32[]{:S(2)}, u32[]{:S(2)}) collective-permute-start(bf16[1024,256]{1,0:T(8,128)(2,1)S(1)} %get-tuple-element.505), channel_id=1, source_target_pairs={{0,2},{1,3},{2,0},{3,1},{4,6},{5,7},{6,4},{7,5},{8,10},{9,11},{10,... | collective-permute-start | bytes 1572872 | tf_op jit(solution)/shard_map/ppermute | solution.py:378
  147.4 24.5 %collective-permute-start.30 = (bf16[256,1024]{1,0:T(8,128)(2,1)S(1)}, bf16[256,1024]{1,0:T(8,128)(2,1)S(1)}, u32[]{:S(2)}, u32[]{:S(2)}) collective-permute-start(bf16[256,1024]{1,0:T(8,128)(2,1)S(1)} %get-tuple-element.507), channel_id=1, source_target_pairs={{0,4},{4,0},{8,12},{12,8},{16,20},{20,16},{24,28},{28,24},{1,5},{5... | collective-permute-start | bytes 1572872 | tf_op jit(solution)/shard_map/ppermute | solution.py:374
  158.7 13.3 %collective-permute-start.29 = (bf16[256,512]{1,0:T(8,128)(2,1)S(1)}, bf16[256,512]{1,0:T(8,128)(2,1)S(1)}, u32[]{:S(2)}, u32[]{:S(2)}) collective-permute-start(bf16[256,512]{1,0:T(8,128)(2,1)S(1)} %pad_maximum_fusion.34), channel_id=1, source_target_pairs={{0,16},{4,20},{8,24},{12,28},{16,0},{20,4},{24,8},{28,12},{1,17},{... | collective-permute-start | bytes 786440 | tf_op jit(solution)/shard_map/ppermute | solution.py:368
  176.8 25.6 %collective-permute-start.33 = (bf16[1024,1024]{1,0:T(8,128)(2,1)}, bf16[1024,1024]{1,0:T(8,128)(2,1)}, u32[]{:S(2)}, u32[]{:S(2)}) collective-permute-start(bf16[1024,1024]{1,0:T(8,128)(2,1)} %pad_maximum_fusion.1.right_ref.refs_7_), channel_id=1, source_target_pairs={{0,1},{1,0},{2,3},{3,2},{4,5},{5,4},{6,7},{7,6},{8,9},{9,8},{10,11... | collective-permute-start | bytes 6291464 | tf_op jit(solution)/shard_map/ppermute | solution.py:378
  179.5 22.8 %collective-permute-start.32 = (bf16[1024,1024]{1,0:T(8,128)(2,1)}, bf16[1024,1024]{1,0:T(8,128)(2,1)}, u32[]{:S(2)}, u32[]{:S(2)}) collective-permute-start(bf16[1024,1024]{1,0:T(8,128)(2,1)} %pad_maximum_fusion.right_ref.refs_6_), channel_id=1, source_target_pairs={{0,1},{1,0},{2,3},{3,2},{4,5},{5,4},{6,7},{7,6},{8,9},{9,8},{10,11... | collective-permute-start | bytes 6291464 | tf_op jit(solution)/shard_map/ppermute | solution.py:378
  184.1 18.3 %collective-permute-start.36 = (bf16[2,1024,256]{2,1,0:T(8,128)(2,1)S(1)}, bf16[2,1024,256]{2,1,0:T(8,128)(2,1)S(1)}, u32[]{:S(2)}, u32[]{:S(2)}) collective-permute-start(bf16[2,1024,256]{2,1,0:T(8,128)(2,1)S(1)} %pad_maximum_fusion.9), channel_id=1, source_target_pairs={{0,1},{1,0},{2,3},{3,2},{4,5},{5,4},{6,7},{7,6},{8,9},{9,8},{10,11... | collective-permute-start | bytes 3145736 | tf_op jit(solution)/shard_map/ppermute | solution.py:378
  187.8 14.2 %collective-permute-start.35 = (bf16[512,512]{1,0:T(8,128)(2,1)S(1)}, bf16[512,512]{1,0:T(8,128)(2,1)S(1)}, u32[]{:S(2)}, u32[]{:S(2)}) collective-permute-start(bf16[512,512]{1,0:T(8,128)(2,1)S(1)} %pad_maximum_fusion.28), channel_id=1, source_target_pairs={{0,4},{4,0},{8,12},{12,8},{16,20},{20,16},{24,28},{28,24},{1,5},{5... | collective-permute-start | bytes 1572872 | tf_op jit(solution)/shard_map/ppermute | solution.py:374
  188.4 13.9 %collective-permute-start.34 = (bf16[512,512]{1,0:T(8,128)(2,1)S(1)}, bf16[512,512]{1,0:T(8,128)(2,1)S(1)}, u32[]{:S(2)}, u32[]{:S(2)}) collective-permute-start(bf16[512,512]{1,0:T(8,128)(2,1)S(1)} %constant_dynamic-update-slice_fusion), channel_id=1, source_target_pairs={{0,2},{1,3},{2,0},{3,1},{4,6},{5,7},{6,4},{7,5},{8,10},{9,11},{10,... | collective-permute-start | bytes 1572872 | tf_op jit(solution)/shard_map/ppermute | solution.py:378
  203.3 30.3 %collective-permute-start.38 = (bf16[1024,512]{1,0:T(8,128)(2,1)}, bf16[1024,512]{1,0:T(8,128)(2,1)}, u32[]{:S(2)}, u32[]{:S(2)}) collective-permute-start(bf16[1024,512]{1,0:T(8,128)(2,1)} %constant_dynamic-update-slice_fusion.3), channel_id=1, source_target_pairs={{0,2},{1,3},{2,0},{3,1},{4,6},{5,7},{6,4},{7,5},{8,10},{9,11},{10,... | collective-permute-start | bytes 3145736 | tf_op jit(solution)/shard_map/ppermute | solution.py:378
  206.0 27.6 %collective-permute-start.37 = (bf16[512,1024]{1,0:T(8,128)(2,1)}, bf16[512,1024]{1,0:T(8,128)(2,1)}, u32[]{:S(2)}, u32[]{:S(2)}) collective-permute-start(bf16[512,1024]{1,0:T(8,128)(2,1)} %pad_maximum_fusion.10), channel_id=1, source_target_pairs={{0,4},{4,0},{8,12},{12,8},{16,20},{20,16},{24,28},{28,24},{1,5},{5... | collective-permute-start | bytes 3145736 | tf_op jit(solution)/shard_map/ppermute | solution.py:374
  238.4 23.5 %collective-permute-start.40 = (bf16[1024,1024]{1,0:T(8,128)(2,1)}, bf16[1024,1024]{1,0:T(8,128)(2,1)}, u32[]{:S(2)}, u32[]{:S(2)}) collective-permute-start(bf16[1024,1024]{1,0:T(8,128)(2,1)} %pad_maximum_fusion.3.refs_7_.right_ref), channel_id=1, source_target_pairs={{0,1},{1,0},{2,3},{3,2},{4,5},{5,4},{6,7},{7,6},{8,9},{9,8},{10,11... | collective-permute-start | bytes 6291464 | tf_op jit(solution)/shard_map/ppermute | solution.py:378
  241.4 20.5 %collective-permute-start.39 = (bf16[1024,1024]{1,0:T(8,128)(2,1)}, bf16[1024,1024]{1,0:T(8,128)(2,1)}, u32[]{:S(2)}, u32[]{:S(2)}) collective-permute-start(bf16[1024,1024]{1,0:T(8,128)(2,1)} %pad_maximum_fusion.2.refs_6_.right_ref), channel_id=1, source_target_pairs={{0,1},{1,0},{2,3},{3,2},{4,5},{5,4},{6,7},{7,6},{8,9},{9,8},{10,11... | collective-permute-start | bytes 6291464 | tf_op jit(solution)/shard_map/ppermute | solution.py:378
  243.8 33.8 %collective-permute-start.41 = (bf16[2,256,1024]{2,1,0:T(8,128)(2,1)}, bf16[2,256,1024]{2,1,0:T(8,128)(2,1)}, u32[]{:S(2)}, u32[]{:S(2)}) collective-permute-start(bf16[2,256,1024]{2,1,0:T(8,128)(2,1)} %pad_maximum_fusion.11), channel_id=1, source_target_pairs={{0,2},{1,3},{2,0},{3,1},{4,6},{5,7},{6,4},{7,5},{8,10},{9,11},{10,... | collective-permute-start | bytes 3145736 | tf_op jit(solution)/shard_map/ppermute | solution.py:378
  292.2 18.2 %collective-permute-start.44 = (bf16[1024,1024]{1,0:T(8,128)(2,1)}, bf16[1024,1024]{1,0:T(8,128)(2,1)}, u32[]{:S(2)}, u32[]{:S(2)}) collective-permute-start(bf16[1024,1024]{1,0:T(8,128)(2,1)} %convolution_convert_fusion.2), channel_id=1, source_target_pairs={{0,1},{1,0},{2,3},{3,2},{4,5},{5,4},{6,7},{7,6},{8,9},{9,8},{10,11... | collective-permute-start | bytes 6291464 | tf_op jit(solution)/shard_map/ppermute | solution.py:378
  292.3 18.0 %collective-permute-start.43 = (bf16[1024,1024]{1,0:T(8,128)(2,1)}, bf16[1024,1024]{1,0:T(8,128)(2,1)}, u32[]{:S(2)}, u32[]{:S(2)}) collective-permute-start(bf16[1024,1024]{1,0:T(8,128)(2,1)} %convolution_convert_fusion.3), channel_id=1, source_target_pairs={{0,1},{1,0},{2,3},{3,2},{4,5},{5,4},{6,7},{7,6},{8,9},{9,8},{10,11... | collective-permute-start | bytes 6291464 | tf_op jit(solution)/shard_map/ppermute | solution.py:378
  314.1 31.3 %collective-permute-start.46 = (bf16[1024,256]{1,0:T(8,128)(2,1)}, bf16[1024,256]{1,0:T(8,128)(2,1)}, u32[]{:S(2)}, u32[]{:S(2)}) collective-permute-start(bf16[1024,256]{1,0:T(8,128)(2,1)} %get-tuple-element.477), channel_id=1, source_target_pairs={{0,2},{1,3},{2,0},{3,1},{4,6},{5,7},{6,4},{7,5},{8,10},{9,11},{10,... | collective-permute-start | bytes 1572872 | tf_op jit(solution)/shard_map/ppermute | solution.py:378
  320.2 25.3 %collective-permute-start.45 = (bf16[256,1024]{1,0:T(8,128)(2,1)}, bf16[256,1024]{1,0:T(8,128)(2,1)}, u32[]{:S(2)}, u32[]{:S(2)}) collective-permute-start(bf16[256,1024]{1,0:T(8,128)(2,1)} %get-tuple-element.479), channel_id=1, source_target_pairs={{0,4},{4,0},{8,12},{12,8},{16,20},{20,16},{24,28},{28,24},{1,5},{5... | collective-permute-start | bytes 1572872 | tf_op jit(solution)/shard_map/ppermute | solution.py:374
  338.7 22.0 %collective-permute-start.48 = (bf16[1024,256]{1,0:T(8,128)(2,1)}, bf16[1024,256]{1,0:T(8,128)(2,1)}, u32[]{:S(2)}, u32[]{:S(2)}) collective-permute-start(bf16[1024,256]{1,0:T(8,128)(2,1)} %get-tuple-element.476), channel_id=1, source_target_pairs={{0,2},{1,3},{2,0},{3,1},{4,6},{5,7},{6,4},{7,5},{8,10},{9,11},{10,... | collective-permute-start | bytes 1572872 | tf_op jit(solution)/shard_map/ppermute | solution.py:378
  339.2 21.5 %collective-permute-start.47 = (bf16[256,1024]{1,0:T(8,128)(2,1)}, bf16[256,1024]{1,0:T(8,128)(2,1)}, u32[]{:S(2)}, u32[]{:S(2)}) collective-permute-start(bf16[256,1024]{1,0:T(8,128)(2,1)} %get-tuple-element.478), channel_id=1, source_target_pairs={{0,4},{4,0},{8,12},{12,8},{16,20},{20,16},{24,28},{28,24},{1,5},{5... | collective-permute-start | bytes 1572872 | tf_op jit(solution)/shard_map/ppermute | solution.py:374
  341.3 53.6 %collective-permute-start.53 = (bf16[2,256,1024]{2,1,0:T(8,128)(2,1)}, bf16[2,256,1024]{2,1,0:T(8,128)(2,1)}, u32[]{:S(2)}, u32[]{:S(2)}) collective-permute-start(bf16[2,256,1024]{2,1,0:T(8,128)(2,1)} %bitcast.82), channel_id=1, source_target_pairs={{0,2},{1,3},{2,0},{3,1},{4,6},{5,7},{6,4},{7,5},{8,10},{9,11},{10,... | collective-permute-start | bytes 3145736 | tf_op jit(solution)/shard_map/ppermute | solution.py:378
  360.7 34.2 %collective-permute-start.50 = (bf16[1024,1024]{1,0:T(8,128)(2,1)}, bf16[1024,1024]{1,0:T(8,128)(2,1)}, u32[]{:S(2)}, u32[]{:S(2)}) collective-permute-start(bf16[1024,1024]{1,0:T(8,128)(2,1)} %convolution_convert_fusion), channel_id=1, source_target_pairs={{0,1},{1,0},{2,3},{3,2},{4,5},{5,4},{6,7},{7,6},{8,9},{9,8},{10,11... | collective-permute-start | bytes 6291464 | tf_op jit(solution)/shard_map/ppermute | solution.py:378
  360.8 34.2 %collective-permute-start.49 = (bf16[1024,1024]{1,0:T(8,128)(2,1)}, bf16[1024,1024]{1,0:T(8,128)(2,1)}, u32[]{:S(2)}, u32[]{:S(2)}) collective-permute-start(bf16[1024,1024]{1,0:T(8,128)(2,1)} %convolution_convert_fusion.1), channel_id=1, source_target_pairs={{0,1},{1,0},{2,3},{3,2},{4,5},{5,4},{6,7},{7,6},{8,9},{9,8},{10,11... | collective-permute-start | bytes 6291464 | tf_op jit(solution)/shard_map/ppermute | solution.py:378
  363.8 31.1 %collective-permute-start.52 = (bf16[512,512]{1,0:T(8,128)(2,1)}, bf16[512,512]{1,0:T(8,128)(2,1)}, u32[]{:S(2)}, u32[]{:S(2)}) collective-permute-start(bf16[512,512]{1,0:T(8,128)(2,1)} %slice.524), channel_id=1, source_target_pairs={{0,4},{4,0},{8,12},{12,8},{16,20},{20,16},{24,28},{28,24},{1,5},{5... | collective-permute-start | bytes 1572872 | tf_op jit(solution)/shard_map/ppermute | solution.py:374
  367.6 27.3 %collective-permute-start.51 = (bf16[512,512]{1,0:T(8,128)(2,1)}, bf16[512,512]{1,0:T(8,128)(2,1)}, u32[]{:S(2)}, u32[]{:S(2)}) collective-permute-start(bf16[512,512]{1,0:T(8,128)(2,1)} %slice.522), channel_id=1, source_target_pairs={{0,2},{1,3},{2,0},{3,1},{4,6},{5,7},{6,4},{7,5},{8,10},{9,11},{10,... | collective-permute-start | bytes 1572872 | tf_op jit(solution)/shard_map/ppermute | solution.py:378
  403.9 34.9 %collective-permute-start.58 = (bf16[2,256,1024]{2,1,0:T(8,128)(2,1)}, bf16[2,256,1024]{2,1,0:T(8,128)(2,1)}, u32[]{:S(2)}, u32[]{:S(2)}) collective-permute-start(bf16[2,256,1024]{2,1,0:T(8,128)(2,1)} %pad_maximum_fusion.14), channel_id=1, source_target_pairs={{0,1},{1,0},{2,3},{3,2},{4,5},{5,4},{6,7},{7,6},{8,9},{9,8},{10,11... | collective-permute-start | bytes 3145736 | tf_op jit(solution)/shard_map/ppermute | solution.py:378
  407.2 31.6 %collective-permute-start.57 = (bf16[256,1024]{1,0:T(8,128)(2,1)}, bf16[256,1024]{1,0:T(8,128)(2,1)}, u32[]{:S(2)}, u32[]{:S(2)}) collective-permute-start(bf16[256,1024]{1,0:T(8,128)(2,1)} %fusion.7), channel_id=1, source_target_pairs={{0,16},{4,20},{8,24},{12,28},{16,0},{20,4},{24,8},{28,12},{1,17},{... | collective-permute-start | bytes 1572872 | tf_op jit(solution)/shard_map/ppermute | solution.py:368
  408.7 30.1 %collective-permute-start.56 = (bf16[2,1024,256]{2,1,0:T(8,128)(2,1)}, bf16[2,1024,256]{2,1,0:T(8,128)(2,1)}, u32[]{:S(2)}, u32[]{:S(2)}) collective-permute-start(bf16[2,1024,256]{2,1,0:T(8,128)(2,1)} %pad_maximum_fusion.13), channel_id=1, source_target_pairs={{0,1},{1,0},{2,3},{3,2},{4,5},{5,4},{6,7},{7,6},{8,9},{9,8},{10,11... | collective-permute-start | bytes 3145736 | tf_op jit(solution)/shard_map/ppermute | solution.py:378
  412.5 26.2 %collective-permute-start.55 = (bf16[1024,512]{1,0:T(8,128)(2,1)}, bf16[1024,512]{1,0:T(8,128)(2,1)}, u32[]{:S(2)}, u32[]{:S(2)}) collective-permute-start(bf16[1024,512]{1,0:T(8,128)(2,1)} %slice.526), channel_id=1, source_target_pairs={{0,2},{1,3},{2,0},{3,1},{4,6},{5,7},{6,4},{7,5},{8,10},{9,11},{10,... | collective-permute-start | bytes 3145736 | tf_op jit(solution)/shard_map/ppermute | solution.py:378
  417.6 25.1 %collective-permute-start.54 = (bf16[512,1024]{1,0:T(8,128)(2,1)}, bf16[512,1024]{1,0:T(8,128)(2,1)}, u32[]{:S(2)}, u32[]{:S(2)}) collective-permute-start(bf16[512,1024]{1,0:T(8,128)(2,1)} %slice.525), channel_id=1, source_target_pairs={{0,4},{4,0},{8,12},{12,8},{16,20},{20,16},{24,28},{28,24},{1,5},{5... | collective-permute-start | bytes 3145736 | tf_op jit(solution)/shard_map/ppermute | solution.py:374
  444.7 32.1 %collective-permute-start.63 = (bf16[128,1024]{1,0:T(8,128)(2,1)}, bf16[128,1024]{1,0:T(8,128)(2,1)}, u32[]{:S(2)}, u32[]{:S(2)}) collective-permute-start(bf16[128,1024]{1,0:T(8,128)(2,1)} %slice.536), channel_id=1, source_target_pairs={{0,8},{4,12},{8,0},{12,4},{16,24},{20,28},{24,16},{28,20},{1,9},{5... | collective-permute-start | bytes 786440 | tf_op jit(solution)/shard_map/ppermute | solution.py:368
  446.6 31.6 %collective-permute-start.59 = (bf16[1024,768]{1,0:T(8,128)(2,1)}, bf16[1024,768]{1,0:T(8,128)(2,1)}, u32[]{:S(2)}, u32[]{:S(2)}) collective-permute-start(bf16[1024,768]{1,0:T(8,128)(2,1)} %convolution_convert_fusion.7), channel_id=1, source_target_pairs={{0,1},{1,0},{2,3},{3,2},{4,5},{5,4},{6,7},{7,6},{8,9},{9,8},{10,11... | collective-permute-start | bytes 4718600 | tf_op jit(solution)/shard_map/ppermute | solution.py:378
  449.0 27.8 %collective-permute-start.62 = (bf16[512,512]{1,0:T(8,128)(2,1)}, bf16[512,512]{1,0:T(8,128)(2,1)S(1)}, u32[]{:S(2)}, u32[]{:S(2)}) collective-permute-start(bf16[512,512]{1,0:T(8,128)(2,1)} %slice.535), channel_id=1, source_target_pairs={{0,4},{4,0},{8,12},{12,8},{16,20},{20,16},{24,28},{28,24},{1,5},{5... | collective-permute-start | bytes 1572872 | tf_op jit(solution)/shard_map/ppermute | solution.py:374
  452.5 24.3 %collective-permute-start.61 = (bf16[512,512]{1,0:T(8,128)(2,1)}, bf16[512,512]{1,0:T(8,128)(2,1)S(1)}, u32[]{:S(2)}, u32[]{:S(2)}) collective-permute-start(bf16[512,512]{1,0:T(8,128)(2,1)} %slice.533), channel_id=1, source_target_pairs={{0,2},{1,3},{2,0},{3,1},{4,6},{5,7},{6,4},{7,5},{8,10},{9,11},{10,... | collective-permute-start | bytes 1572872 | tf_op jit(solution)/shard_map/ppermute | solution.py:378
  456.3 21.8 %collective-permute-start.60 = (bf16[2,1024,128]{2,1,0:T(8,128)(2,1)}, bf16[2,1024,128]{2,1,0:T(8,128)(2,1)}, u32[]{:S(2)}, u32[]{:S(2)}) collective-permute-start(bf16[2,1024,128]{2,1,0:T(8,128)(2,1)} %slice.531), channel_id=1, source_target_pairs={{0,2},{1,3},{2,0},{3,1},{4,6},{5,7},{6,4},{7,5},{8,10},{9,11},{10,... | collective-permute-start | bytes 1572872 | tf_op jit(solution)/shard_map/ppermute | solution.py:378
  480.1 22.8 %collective-permute-start.65 = (bf16[1024,384]{1,0:T(8,128)(2,1)S(1)}, bf16[1024,384]{1,0:T(8,128)(2,1)S(1)}, u32[]{:S(2)}, u32[]{:S(2)}) collective-permute-start(bf16[1024,384]{1,0:T(8,128)(2,1)S(1)} %slice.539), channel_id=1, source_target_pairs={{0,2},{1,3},{2,0},{3,1},{4,6},{5,7},{6,4},{7,5},{8,10},{9,11},{10,... | collective-permute-start | bytes 2359304 | tf_op jit(solution)/shard_map/ppermute | solution.py:378
  483.6 19.2 %collective-permute-start.64 = (bf16[2,512,128]{2,1,0:T(8,128)(2,1)S(1)}, bf16[2,512,128]{2,1,0:T(8,128)(2,1)S(1)}, u32[]{:S(2)}, u32[]{:S(2)}) collective-permute-start(bf16[2,512,128]{2,1,0:T(8,128)(2,1)S(1)} %slice.538), channel_id=1, source_target_pairs={{0,4},{4,0},{8,12},{12,8},{16,20},{20,16},{24,28},{28,24},{1,5},{5... | collective-permute-start | bytes 786440 | tf_op jit(solution)/shard_map/ppermute | solution.py:374
  485.9 42.8 %collective-permute-start.68 = (bf16[256,1024]{1,0:T(8,128)(2,1)}, bf16[256,1024]{1,0:T(8,128)(2,1)}, u32[]{:S(2)}, u32[]{:S(2)}) collective-permute-start(bf16[256,1024]{1,0:T(8,128)(2,1)} %fusion.6), channel_id=1, source_target_pairs={{0,16},{4,20},{8,24},{12,28},{16,0},{20,4},{24,8},{28,12},{1,17},{... | collective-permute-start | bytes 1572872 | tf_op jit(solution)/shard_map/ppermute | solution.py:368
  503.8 24.9 %collective-permute-start.67 = (bf16[1024,768]{1,0:T(8,128)(2,1)}, bf16[1024,768]{1,0:T(8,128)(2,1)}, u32[]{:S(2)}, u32[]{:S(2)}) collective-permute-start(bf16[1024,768]{1,0:T(8,128)(2,1)} %convolution_convert_fusion.6), channel_id=1, source_target_pairs={{0,1},{1,0},{2,3},{3,2},{4,5},{5,4},{6,7},{7,6},{8,9},{9,8},{10,11... | collective-permute-start | bytes 4718600 | tf_op jit(solution)/shard_map/ppermute | solution.py:378
  510.9 17.7 %collective-permute-start.66 = (bf16[512,384]{1,0:T(8,128)(2,1)S(1)}, bf16[512,384]{1,0:T(8,128)(2,1)S(1)}, u32[]{:S(2)}, u32[]{:S(2)}) collective-permute-start(bf16[512,384]{1,0:T(8,128)(2,1)S(1)} %slice.541), channel_id=1, source_target_pairs={{0,4},{4,0},{8,12},{12,8},{16,20},{20,16},{24,28},{28,24},{1,5},{5... | collective-permute-start | bytes 1179656 | tf_op jit(solution)/shard_map/ppermute | solution.py:374
  529.9 17.6 %collective-permute-start.76 = (bf16[128,1024]{1,0:T(8,128)(2,1)S(1)}, bf16[128,1024]{1,0:T(8,128)(2,1)S(1)}, u32[]{:S(2)}, u32[]{:S(2)}) collective-permute-start(bf16[128,1024]{1,0:T(8,128)(2,1)S(1)} %slice.563), channel_id=1, source_target_pairs={{0,8},{4,12},{8,0},{12,4},{16,24},{20,28},{24,16},{28,20},{1,9},{5... | collective-permute-start | bytes 786440 | tf_op jit(solution)/shard_map/ppermute | solution.py:368
  534.8 19.7 %collective-permute-start.69 = (bf16[512,768]{1,0:T(8,128)(2,1)}, bf16[512,768]{1,0:T(8,128)(2,1)}, u32[]{:S(2)}, u32[]{:S(2)}) collective-permute-start(bf16[512,768]{1,0:T(8,128)(2,1)} %slice.546), channel_id=1, source_target_pairs={{0,4},{4,0},{8,12},{12,8},{16,20},{20,16},{24,28},{28,24},{1,5},{5... | collective-permute-start | bytes 2359304 | tf_op jit(solution)/shard_map/ppermute | solution.py:374
  545.1 31.8 %collective-permute-start.71 = (bf16[2,256,1024]{2,1,0:T(8,128)(2,1)}, bf16[2,256,1024]{2,1,0:T(8,128)(2,1)}, u32[]{:S(2)}, u32[]{:S(2)}) collective-permute-start(bf16[2,256,1024]{2,1,0:T(8,128)(2,1)} %bitcast.93), channel_id=1, source_target_pairs={{0,2},{1,3},{2,0},{3,1},{4,6},{5,7},{6,4},{7,5},{8,10},{9,11},{10,... | collective-permute-start | bytes 3145736 | tf_op jit(solution)/shard_map/ppermute | solution.py:378
  562.2 16.4 %collective-permute-start.70 = (bf16[512,384]{1,0:T(8,128)(2,1)}, bf16[512,384]{1,0:T(8,128)(2,1)}, u32[]{:S(2)}, u32[]{:S(2)}) collective-permute-start(bf16[512,384]{1,0:T(8,128)(2,1)} %slice.548), channel_id=1, source_target_pairs={{0,2},{1,3},{2,0},{3,1},{4,6},{5,7},{6,4},{7,5},{8,10},{9,11},{10,... | collective-permute-start | bytes 1179656 | tf_op jit(solution)/shard_map/ppermute | solution.py:378
  582.8 17.4 %collective-permute-start.73 = (bf16[128,1024]{1,0:T(8,128)(2,1)}, bf16[128,1024]{1,0:T(8,128)(2,1)S(1)}, u32[]{:S(2)}, u32[]{:S(2)}) collective-permute-start(bf16[128,1024]{1,0:T(8,128)(2,1)} %get-tuple-element.488), channel_id=1, source_target_pairs={{0,8},{4,12},{8,0},{12,4},{16,24},{20,28},{24,16},{28,20},{1,9},{5... | collective-permute-start | bytes 786440 | tf_op jit(solution)/shard_map/ppermute | solution.py:368
  583.2 16.9 %collective-permute-start.74 = (bf16[128,1024]{1,0:T(8,128)(2,1)}, bf16[128,1024]{1,0:T(8,128)(2,1)S(1)}, u32[]{:S(2)}, u32[]{:S(2)}) collective-permute-start(bf16[128,1024]{1,0:T(8,128)(2,1)} %get-tuple-element.487), channel_id=1, source_target_pairs={{0,16},{4,20},{8,24},{12,28},{16,0},{20,4},{24,8},{28,12},{1,17},{... | collective-permute-start | bytes 786440 | tf_op jit(solution)/shard_map/ppermute | solution.py:368
  598.7 14.9 %collective-permute-start.72 = (bf16[2,256,1024]{2,1,0:T(8,128)(2,1)}, bf16[2,256,1024]{2,1,0:T(8,128)(2,1)}, u32[]{:S(2)}, u32[]{:S(2)}) collective-permute-start(bf16[2,256,1024]{2,1,0:T(8,128)(2,1)} %pad_maximum_fusion.15), channel_id=1, source_target_pairs={{0,1},{1,0},{2,3},{3,2},{4,5},{5,4},{6,7},{7,6},{8,9},{9,8},{10,11... | collective-permute-start | bytes 3145736 | tf_op jit(solution)/shard_map/ppermute | solution.py:378
  (172 other events, 1097.8 us)

commit v11 on v9

--- a/solution.py
+++ b/solution.py
@@ -939,7 +939,10 @@
     up_shard = jnp.concatenate(
         [out_weight.T.astype(BF), up_weight.astype(BF).reshape(depth, -1)], 1
     )
-    down_shard = down_weight.transpose(2, 0, 1).astype(BF).reshape(depth, -1)
+    down_low = down_weight.transpose(2, 0, 1).astype(BF)
+    down_shards = [
+        down_low[:, at : at + half_units].reshape(depth, -1) for at in (0, half_units)
+    ]
     both = ("xy", "yx")
     small = Chain(small_steps, small_shard, vector_size)
     rows_qkv = Chain(rows_z_steps, qkv_shard)
@@ -979,23 +982,27 @@
         blended[core][half], log_total[core][half] = attend(heads[core][half])
 
     heads[0][0] = project(0, 0, get_qkv[0].own[0])
-    heads[0][0], down_shard = meet((heads[0][0], down_shard), *get_qkv)
+    heads[0][0], down_shards = meet((heads[0][0], down_shards), *get_qkv)
     w_qkv = [[each.own[0] for each in get_qkv], [each.result[0] for each in get_qkv]]
-    rows_down = Chain(rows_z_steps, down_shard)
+    rows_down = [Chain(rows_z_steps, each) for each in down_shards]
     forward_heads(0, 0)
-    blended[0][0], normed_one = meet((blended[0][0], normed_one), get_out, get_up, rows_down)
+    blended[0][0], normed_one = meet(
+        (blended[0][0], normed_one), get_out, get_up, *rows_down
+    )
     heads[0][1] = project(0, 1, w_qkv[0][1])
     forward_heads(0, 1)
-    blended[0][1], normed_one = meet((blended[0][1], normed_one), get_out, get_up)
+    blended[0][1], normed_one = meet(
+        (blended[0][1], normed_one), get_up, rows_down[0]
+    )
     heads[1][0] = project(1, 0, w_qkv[1][0])
     forward_heads(1, 0)
     blended[1][0], normed_one = meet(
-        (blended[1][0], normed_one), get_out, rows_down, get_up
-    )
-    get_down = Chain(gather_steps, jnp.split(rows_down.result, 2, 1), both)
+        (blended[1][0], normed_one), get_out, rows_down[1], get_up
+    )
+    get_down = Chain(gather_steps, [each.result for each in rows_down], both)
     heads[1][1] = project(1, 1, w_qkv[1][1])
     forward_heads(1, 1)
-    blended = meet(blended, get_up, get_down)
+    blended = meet(blended, get_up, get_down, get_out)
     w_out = [[each[0][half] for half in (0, 1)] for each in (get_out.own, get_out.result)]
     pairs = [(core, half) for core in cores for half in (0, 1)]
     branch_one, hidden, normed_two = row_call(

time: 622 us -> 603 us (0.969)
  waiting for transfers between devices: 104 us -> 87.7 us
  matrix products: 58.4 us -> 49.9 us
    unnamed x310 -> x351, local copies, waits for them, and re-layouts: 41.1 us -> 50.6 us
    dot_general x8, matrix products: 22 us -> 13.6 us  [dot_nn(): lax.dot_general(left, right, (((1,), (0,)), ((), ())), preferred_element_...]
    ppermute x43, waiting for transfers between devices: 25.8 us -> 18.4 us  [swap_mp(): return lax.ppermute(part, 'mp', [(each, each ^ step) for each in range(MP)])]
    concatenate x14 -> x13, other arithmetic: 28.6 us -> 22.3 us  [join(): return jnp.concatenate([rows, arrived], -2 if axis == 'y' else -1)]
    ppermute x18 -> x20, waiting for transfers between devices: 59.6 us -> 53.4 us  [swap_z(): lax.ppermute(part, 'dp', [(z * YS + y, (z ^ step) * YS + y) for z in rang...]
    ppermute x18 -> x20, starting transfers between devices: 25.4 us -> 28.7 us  [swap_z(): lax.ppermute(part, 'dp', [(z * YS + y, (z ^ step) * YS + y) for z in rang...]
  transfers between devices with their start and end apart: 79 -> 81, of which waited for: 21 -> 20; matrix products, arithmetic and copies ran while one was open for 25% -> 26% of each run, Pallas kernels for 33% -> 34%
where the time goes in v11:
time: 603 us; the launch traced here: 601 us
  Pallas kernels  211 us (35%)
  waiting for transfers between devices  87.7 us (15%)
  other arithmetic  86.3 us (14%)
  local copies, waits for them, and re-layouts  85.5 us (14%)
  starting transfers between devices  76.2 us (13%)
  matrix products  49.9 us (8%)
    pallas_call x5, Pallas kernels, row_call(): pl.pallas_call(functools.partial(kernel, len(lefts)), grid=(count,), in_s...  61 us
    pallas_call x4, Pallas kernels, attend_back(): pl.pallas_call(functools.partial(attend_back_kernel, 512), grid=(pairs,),...  56.6 us
    ppermute x20, waiting for transfers between devices, swap_z(): lax.ppermute(part, 'dp', [(z * YS + y, (z ^ step) * YS + y) for z in rang...  53.4 us
    unnamed x351, local copies, waits for them, and re-layouts  50.6 us
    pallas_call x4, Pallas kernels, attend(): pl.pallas_call(functools.partial(attend_kernel, 512), grid=(pairs,), in_s...  38.9 us
    dot_general x16, matrix products, dot_tn(): lax.dot_general(left, right, (((0,), (0,)), ((), ())), preferred_element_...  36.2 us
    ppermute x20, starting transfers between devices, swap_z(): lax.ppermute(part, 'dp', [(z * YS + y, (z ^ step) * YS + y) for z in rang...  28.7 us
    ppermute x43, starting transfers between devices, swap_mp(): return lax.ppermute(part, 'mp', [(each, each ^ step) for each in range(MP)])  28.6 us
  transfers between devices with their start and end apart: 81, of which 20 were waited for; matrix products, arithmetic and copies ran while one was open for 26% of the time, Pallas kernels for 34%

profile of v11, /device:TPU:0, one launch (start us, length us, event | category | flops | bytes accessed | tf_op | source)
XLA Modules:
  0.0 600.8 jit_solution(11961663176617695646)
XLA Ops:
  2.8 2.6 collective-permute-start.1
  11.2 4.2 collective-permute-done.3
  17.1 2.8 collective-permute-start.6
  25.1 4.7 collective-permute-done.4
  29.8 3.5 collective-permute-start.5
  33.3 3.9 collective-permute-done.5
  41.0 7.3 %collective-permute-done.8 = bf16[4,1792]{1,0:T(4,128)(2,1)S(1)} collective-permute-done((bf16[4,1792]{1,0:T(4,128)(2,1)S(1)}, bf16[4,1792]{1,0:T(4,128)(2,1)S(1)}, u32[]{:S(2)}, u32[]{:S(2)}) %collective-permute-start.8) | collective-permute-done | bytes 14368 | tf_op jit(solution)/shard_map/ppermute | solution.py:374
  58.1 5.8 collective-permute-done.12
  68.8 3.1 assemble_image.2
  71.9 25.0 %collective-permute-done.15 = bf16[256,1280]{1,0:T(8,128)(2,1)S(1)} collective-permute-done((bf16[256,1280]{1,0:T(8,128)(2,1)S(1)}, bf16[256,1280]{1,0:T(8,128)(2,1)S(1)}, u32[]{:S(2)}, u32[]{:S(2)}) %collective-permute-start.15) | collective-permute-done | bytes 655392 | tf_op jit(solution)/shard_map/ppermute | solution.py:368
  110.6 7.1 %attend.4 = (bf16[1024,256]{1,0:T(8,128)(2,1)S(1)}, f32[2,8,1024]{2,1,0:T(8,128)S(1)}) custom-call(bf16[1024,768]{1,0:T(8,128)(2,1)S(1)} %add_convert_fusion.9.q_ref.k_ref.v_ref, bf16[1024,768]{1,0:T(8,128)(2,1)S(1)} %add_convert_fusion.9.q_ref.k_ref.v_ref, bf16[1024,768]{1,0:T(8,128)(2,1)S(1)} %add_convert_fusion.9.q_ref.k_ref.v_ref), custom_call_target="tpu_custom_call" | custom-call | tf_op jit(solution)/shard_map/attend/pallas_call | solution.py:838
  117.7 4.1 collective-permute-done.20
  132.8 6.1 %collective-permute-done.25 = bf16[256,512]{1,0:T(8,128)(2,1)S(1)} collective-permute-done((bf16[256,512]{1,0:T(8,128)(2,1)S(1)}, bf16[256,512]{1,0:T(8,128)(2,1)S(1)}, u32[]{:S(2)}, u32[]{:S(2)}) %collective-permute-start.25) | collective-permute-done | bytes 262176 | tf_op jit(solution)/shard_map/ppermute | solution.py:368
  140.3 7.4 %attend.5 = (bf16[1024,256]{1,0:T(8,128)(2,1)S(1)}, f32[2,8,1024]{2,1,0:T(8,128)S(1)}) custom-call(bf16[1024,768]{1,0:T(8,128)(2,1)S(1)} %add_convert_fusion.8.q_ref.k_ref.v_ref, bf16[1024,768]{1,0:T(8,128)(2,1)S(1)} %add_convert_fusion.8.q_ref.k_ref.v_ref, bf16[1024,768]{1,0:T(8,128)(2,1)S(1)} %add_convert_fusion.8.q_ref.k_ref.v_ref), custom_call_target="tpu_custom_call" | custom-call | tf_op jit(solution)/shard_map/attend/pallas_call | solution.py:838
  149.1 3.2 add_convert_fusion.7.q_ref.k_ref.v_ref
  152.4 7.1 %attend.6 = (bf16[1024,256]{1,0:T(8,128)(2,1)S(1)}, f32[2,8,1024]{2,1,0:T(8,128)S(1)}) custom-call(bf16[1024,768]{1,0:T(8,128)(2,1)S(1)} %add_convert_fusion.7.q_ref.k_ref.v_ref, bf16[1024,768]{1,0:T(8,128)(2,1)S(1)} %add_convert_fusion.7.q_ref.k_ref.v_ref, bf16[1024,768]{1,0:T(8,128)(2,1)S(1)} %add_convert_fusion.7.q_ref.k_ref.v_ref), custom_call_target="tpu_custom_call" | custom-call | tf_op jit(solution)/shard_map/attend/pallas_call | solution.py:838
  159.5 2.4 collective-permute-done.27
  161.9 3.1 pad_maximum_fusion.1.right_ref.refs_7_
  165.1 2.7 pad_maximum_fusion.right_ref.refs_6_
  178.3 3.2 add_convert_fusion.6.q_ref.k_ref.v_ref
  181.5 17.3 %attend.7 = (bf16[1024,256]{1,0:T(8,128)(2,1)S(1)}, f32[2,8,1024]{2,1,0:T(8,128)S(1)}) custom-call(bf16[1024,768]{1,0:T(8,128)(2,1)S(1)} %add_convert_fusion.6.q_ref.k_ref.v_ref, bf16[1024,768]{1,0:T(8,128)(2,1)S(1)} %add_convert_fusion.6.q_ref.k_ref.v_ref, bf16[1024,768]{1,0:T(8,128)(2,1)S(1)} %add_convert_fusion.6.q_ref.k_ref.v_ref), custom_call_target="tpu_custom_call" | custom-call | tf_op jit(solution)/shard_map/attend/pallas_call | solution.py:838
  206.8 6.9 %out_norm.1 = (f32[1024,1024]{1,0:T(8,128)}, f32[1024,1024]{1,0:T(8,128)}, bf16[1024,1024]{1,0:T(8,128)(2,1)}) custom-call(bf16[1024,256]{1,0:T(8,128)(2,1)S(1)} %copy-done.54, bf16[1024,256]{1,0:T(8,128)(2,1)S(1)} %copy-done.57, bf16[1024,256]{1,0:T(8,128)(2,1)S(1)} %copy-done.60, bf16[1024,256]{1,0:T(8,128)(2,1)S(1)} %copy-done.63, ...), custom_call_target="tpu_custom_call" | custom-call | tf_op jit(solution)/shard_map/out_norm/pallas_call | solution.py:744
  215.3 6.0 expand.5
  223.9 6.0 expand.4
  230.0 4.7 pad_maximum_fusion.3.refs_7_.right_ref
  234.8 2.9 pad_maximum_fusion.2.refs_6_.right_ref
  242.3 6.0 expand.7
  251.0 6.0 expand.6
  258.3 15.7 %down_output.1 = (bf16[1024,1024]{1,0:T(8,128)(2,1)S(1)}, f32[1024,1024]{1,0:T(8,128)}) custom-call(bf16[1024,1024]{1,0:T(8,128)(2,1)S(1)} %get-tuple-element.268.refs_0_, bf16[1024,1024]{1,0:T(8,128)(2,1)} %copy-done.37, bf16[1024,1024]{1,0:T(8,128)(2,1)} %copy-done.31, bf16[1024,1024]{1,0:T(8,128)(2,1)} %copy-done.29, ...), custom_call_target="tpu_custom_call" | custom-call | tf_op jit(solution)/shard_map/down_output/pallas_call | solution.py:744
  276.4 2.6 collective-permute-done.40
  281.3 3.7 convolution_convert_fusion.2
  285.0 3.7 convolution_convert_fusion.3
  298.6 2.9 multiply_reduce_fusion
  302.1 2.4 fusion.37
  304.5 2.4 fusion.36
  306.9 2.6 add_convert_fusion.2
  311.9 2.7 add_convert_fusion.3
  317.9 4.8 slope_product.6
  324.1 5.0 slope_product.5
  330.5 5.0 slope_product.4
  343.8 5.0 slope_product.7
  350.1 3.7 convolution_convert_fusion
  353.8 3.8 convolution_convert_fusion.1
  366.6 20.3 %up_norm_back.1 = (f32[1024,1024]{1,0:T(8,128)}, bf16[1024,1024]{1,0:T(8,128)(2,1)S(1)}, f32[8,1024]{1,0:T(8,128)S(1)}) custom-call(bf16[1024,1024]{1,0:T(8,128)(2,1)S(1)} %copy-done.48, bf16[1024,1024]{1,0:T(8,128)(2,1)} %copy-done.44, bf16[1024,1024]{1,0:T(8,128)(2,1)} %copy-done.42, bf16[1024,1024]{1,0:T(8,128)(2,1)} %copy-done.49, ...), custom_call_target="tpu_custom_call" | custom-call | tf_op jit(solution)/shard_map/up_norm_back/pallas_call | solution.py:744
  387.0 2.4 fusion.39
  389.4 2.4 fusion.38
  404.0 2.6 add_convert_fusion
  407.4 2.6 add_convert_fusion.1
  413.3 13.9 %attend_back.4.refs_2_ = bf16[1024,768]{1,0:T(8,128)(2,1)S(1)} custom-call(bf16[1024,768]{1,0:T(8,128)(2,1)S(1)} %copy-done.3, bf16[1024,768]{1,0:T(8,128)(2,1)S(1)} %copy-done.3, bf16[1024,768]{1,0:T(8,128)(2,1)S(1)} %copy-done.3, bf16[1024,256]{1,0:T(8,128)(2,1)S(1)} %convolution_convert_fusion.15.g_ref, f32[2,8,1024]{2,1,0:T(8,128)S(1)} %get-tuple-element.320.lse_ref), custom_call_target="tpu_custom_call" | custom-call | tf_op jit(solution)/shard_map/attend_back/pallas_call | solution.py:858
  429.1 3.1 collective-permute-done.53
  432.2 3.0 collective-permute-done.52
  435.4 2.8 collective-permute-start.61
  442.7 14.1 %attend_back.5.refs_0_ = bf16[1024,768]{1,0:T(8,128)(2,1)S(1)} custom-call(bf16[1024,768]{1,0:T(8,128)(2,1)S(1)} %add_convert_fusion.9.q_ref.k_ref.v_ref, bf16[1024,768]{1,0:T(8,128)(2,1)S(1)} %add_convert_fusion.9.q_ref.k_ref.v_ref, bf16[1024,768]{1,0:T(8,128)(2,1)S(1)} %add_convert_fusion.9.q_ref.k_ref.v_ref, ...), custom_call_target="tpu_custom_call" | custom-call | tf_op jit(solution)/shard_map/attend_back/pallas_call | solution.py:858
  456.8 2.6 spread_image.2
  461.4 4.1 collective-permute-done.58
  470.9 14.3 %attend_back.6.refs_3_ = bf16[1024,768]{1,0:T(8,128)(2,1)S(1)} custom-call(bf16[1024,768]{1,0:T(8,128)(2,1)S(1)} %copy-done.1, bf16[1024,768]{1,0:T(8,128)(2,1)S(1)} %copy-done.1, bf16[1024,768]{1,0:T(8,128)(2,1)S(1)} %copy-done.1, bf16[1024,256]{1,0:T(8,128)(2,1)S(1)} %convolution_convert_fusion.12.g_ref, f32[2,8,1024]{2,1,0:T(8,128)S(1)} %get-tuple-element.338.lse_ref), custom_call_target="tpu_custom_call" | custom-call | tf_op jit(solution)/shard_map/attend_back/pallas_call | solution.py:858
  485.3 3.0 convolution_convert_fusion.6
  489.7 2.7 multiply_subtract_fusion
  494.6 14.3 %attend_back.7.refs_1_ = bf16[1024,768]{1,0:T(8,128)(2,1)S(1)} custom-call(bf16[1024,768]{1,0:T(8,128)(2,1)S(1)} %add_convert_fusion.8.q_ref.k_ref.v_ref, bf16[1024,768]{1,0:T(8,128)(2,1)S(1)} %add_convert_fusion.8.q_ref.k_ref.v_ref, bf16[1024,768]{1,0:T(8,128)(2,1)S(1)} %add_convert_fusion.8.q_ref.k_ref.v_ref, bf16[1024,256]{1,0:T(8,128)(2,1)S(1)} %copy-done.65, ...), custom_call_target="tpu_custom_call" | custom-call | tf_op jit(solution)/shard_map/attend_back/pallas_call | solution.py:858
  517.3 9.3 %in_norm_back.3 = (bf16[512,1024]{1,0:T(8,128)(2,1)}, f32[8,1024]{1,0:T(8,128)S(1)}) custom-call(bf16[1024,768]{1,0:T(8,128)(2,1)S(1)} %copy-done.14, bf16[1024,768]{1,0:T(8,128)(2,1)S(1)} %attend_back.7.refs_1_, bf16[1024,768]{1,0:T(8,128)(2,1)S(1)} %copy-done.12, bf16[1024,768]{1,0:T(8,128)(2,1)} %copy-done.15, ...), custom_call_target="tpu_custom_call" | custom-call | tf_op jit(solution)/shard_map/in_norm_back/pallas_call | solution.py:744
  531.5 3.4 multiply_subtract_fusion.1
  544.6 8.8 %in_norm_back.2 = (bf16[512,1024]{1,0:T(8,128)(2,1)S(1)}, f32[8,1024]{1,0:T(8,128)S(1)}, f32[256,1024]{1,0:T(8,128)S(1)}) custom-call(bf16[1024,768]{1,0:T(8,128)(2,1)S(1)} %copy-done.14, bf16[1024,768]{1,0:T(8,128)(2,1)S(1)} %copy-done.17, bf16[1024,768]{1,0:T(8,128)(2,1)} %copy-done.11, bf16[1024,768]{1,0:T(8,128)(2,1)} %copy-done.15, ...), custom_call_target="tpu_custom_call" | custom-call | tf_op jit(solution)/shard_map/in_norm_back/pallas_call | solution.py:744
  581.1 5.2 collective-permute-done.73
  597.4 3.1 spread_image.3
  (721 shorter events, 227.9 us)
Async XLA Ops:
  10.9 26.3 %collective-permute-start.7 = (bf16[128,1280]{1,0:T(8,128)(2,1)}, bf16[128,1280]{1,0:T(8,128)(2,1)S(1)}, u32[]{:S(2)}, u32[]{:S(2)}) collective-permute-start(bf16[128,1280]{1,0:T(8,128)(2,1)} %pad_maximum_fusion.31), channel_id=1, source_target_pairs={{0,8},{4,12},{8,0},{12,4},{16,24},{20,28},{24,16},{28,20},{1,9},{5... | collective-permute-start | bytes 983048 | tf_op jit(solution)/shard_map/ppermute | solution.py:368
  17.1 20.1 %collective-permute-start.6 = (bf16[256,768]{1,0:T(8,128)(2,1)}, bf16[256,768]{1,0:T(8,128)(2,1)}, u32[]{:S(2)}, u32[]{:S(2)}) collective-permute-start(bf16[256,768]{1,0:T(8,128)(2,1)} %pad_maximum_fusion.30), channel_id=1, source_target_pairs={{0,16},{4,20},{8,24},{12,28},{16,0},{20,4},{24,8},{28,12},{1,17},{... | collective-permute-start | bytes 1179656 | tf_op jit(solution)/shard_map/ppermute | solution.py:368
  21.9 27.1 %collective-permute-start.10 = (bf16[2,256,1024]{2,1,0:T(8,128)(2,1)}, bf16[2,256,1024]{2,1,0:T(8,128)(2,1)}, u32[]{:S(2)}, u32[]{:S(2)}) collective-permute-start(bf16[2,256,1024]{2,1,0:T(8,128)(2,1)} %pad_maximum_fusion.6), channel_id=1, source_target_pairs={{0,2},{1,3},{2,0},{3,1},{4,6},{5,7},{6,4},{7,5},{8,10},{9,11},{10,... | collective-permute-start | bytes 3145736 | tf_op jit(solution)/shard_map/ppermute | solution.py:378
  51.4 12.6 %collective-permute-start.11 = (bf16[2,256,1024]{2,1,0:T(8,128)(2,1)}, bf16[2,256,1024]{2,1,0:T(8,128)(2,1)}, u32[]{:S(2)}, u32[]{:S(2)}) collective-permute-start(bf16[2,256,1024]{2,1,0:T(8,128)(2,1)} %pad_maximum_fusion.7), channel_id=1, source_target_pairs={{0,1},{1,0},{2,3},{3,2},{4,5},{5,4},{6,7},{7,6},{8,9},{9,8},{10,11... | collective-permute-start | bytes 3145736 | tf_op jit(solution)/shard_map/ppermute | solution.py:378
  51.9 12.0 %collective-permute-start.12 = (bf16[512,384]{1,0:T(8,128)(2,1)S(1)}, bf16[512,384]{1,0:T(8,128)(2,1)S(1)}, u32[]{:S(2)}, u32[]{:S(2)}) collective-permute-start(bf16[512,384]{1,0:T(8,128)(2,1)S(1)} %get-tuple-element.513), channel_id=1, source_target_pairs={{0,2},{1,3},{2,0},{3,1},{4,6},{5,7},{6,4},{7,5},{8,10},{9,11},{10,... | collective-permute-start | bytes 1179656 | tf_op jit(solution)/shard_map/ppermute | solution.py:378
  57.4 39.6 %collective-permute-start.14 = (bf16[1024,384]{1,0:T(8,128)(2,1)S(1)}, bf16[1024,384]{1,0:T(8,128)(2,1)S(1)}, u32[]{:S(2)}, u32[]{:S(2)}) collective-permute-start(bf16[1024,384]{1,0:T(8,128)(2,1)S(1)} %pad_maximum_fusion.18), channel_id=1, source_target_pairs={{0,2},{1,3},{2,0},{3,1},{4,6},{5,7},{6,4},{7,5},{8,10},{9,11},{10,... | collective-permute-start | bytes 2359304 | tf_op jit(solution)/shard_map/ppermute | solution.py:378
  64.7 32.2 %collective-permute-start.13 = (bf16[512,768]{1,0:T(8,128)(2,1)S(1)}, bf16[512,768]{1,0:T(8,128)(2,1)S(1)}, u32[]{:S(2)}, u32[]{:S(2)}) collective-permute-start(bf16[512,768]{1,0:T(8,128)(2,1)S(1)} %pad_maximum_fusion.17), channel_id=1, source_target_pairs={{0,4},{4,0},{8,12},{12,8},{16,20},{20,16},{24,28},{28,24},{1,5},{5... | collective-permute-start | bytes 2359304 | tf_op jit(solution)/shard_map/ppermute | solution.py:374
  66.2 30.7 %collective-permute-start.15 = (bf16[256,1280]{1,0:T(8,128)(2,1)S(1)}, bf16[256,1280]{1,0:T(8,128)(2,1)S(1)}, u32[]{:S(2)}, u32[]{:S(2)}) collective-permute-start(bf16[256,1280]{1,0:T(8,128)(2,1)S(1)} %pad_maximum_fusion.19), channel_id=1, source_target_pairs={{0,16},{4,20},{8,24},{12,28},{16,0},{20,4},{24,8},{28,12},{1,17},{... | collective-permute-start | bytes 1966088 | tf_op jit(solution)/shard_map/ppermute | solution.py:368
  97.2 11.3 %collective-permute-start.17 = (bf16[1024,768]{1,0:T(8,128)(2,1)S(1)}, bf16[1024,768]{1,0:T(8,128)(2,1)}, u32[]{:S(2)}, u32[]{:S(2)}) collective-permute-start(bf16[1024,768]{1,0:T(8,128)(2,1)S(1)} %pad_maximum_fusion.5.refs_5_), channel_id=1, source_target_pairs={{0,1},{1,0},{2,3},{3,2},{4,5},{5,4},{6,7},{7,6},{8,9},{9,8},{10,11... | collective-permute-start | bytes 4718600 | tf_op jit(solution)/shard_map/ppermute | solution.py:378
  102.1 15.6 %collective-permute-start.18 = (bf16[2,512,128]{2,1,0:T(8,128)(2,1)}, bf16[2,512,128]{2,1,0:T(8,128)(2,1)}, u32[]{:S(2)}, u32[]{:S(2)}) collective-permute-start(bf16[2,512,128]{2,1,0:T(8,128)(2,1)} %pad_maximum_fusion.32), channel_id=1, source_target_pairs={{0,4},{4,0},{8,12},{12,8},{16,20},{20,16},{24,28},{28,24},{1,5},{5... | collective-permute-start | bytes 786440 | tf_op jit(solution)/shard_map/ppermute | solution.py:374
  103.8 14.0 %collective-permute-start.19 = (bf16[512,512]{1,0:T(8,128)(2,1)}, bf16[512,512]{1,0:T(8,128)(2,1)}, u32[]{:S(2)}, u32[]{:S(2)}) collective-permute-start(bf16[512,512]{1,0:T(8,128)(2,1)} %get-tuple-element.483), channel_id=1, source_target_pairs={{0,2},{1,3},{2,0},{3,1},{4,6},{5,7},{6,4},{7,5},{8,10},{9,11},{10,... | collective-permute-start | bytes 1572872 | tf_op jit(solution)/shard_map/ppermute | solution.py:378
  105.1 16.7 %collective-permute-start.20 = (bf16[512,512]{1,0:T(8,128)(2,1)}, bf16[512,512]{1,0:T(8,128)(2,1)}, u32[]{:S(2)}, u32[]{:S(2)}) collective-permute-start(bf16[512,512]{1,0:T(8,128)(2,1)} %get-tuple-element.482), channel_id=1, source_target_pairs={{0,4},{4,0},{8,12},{12,8},{16,20},{20,16},{24,28},{28,24},{1,5},{5... | collective-permute-start | bytes 1572872 | tf_op jit(solution)/shard_map/ppermute | solution.py:374
  108.5 13.4 %collective-permute-start.21 = (bf16[128,512]{1,0:T(8,128)(2,1)}, bf16[128,512]{1,0:T(8,128)(2,1)S(1)}, u32[]{:S(2)}, u32[]{:S(2)}) collective-permute-start(bf16[128,512]{1,0:T(8,128)(2,1)} %copy.177), channel_id=1, source_target_pairs={{0,8},{4,12},{8,0},{12,4},{16,24},{20,28},{24,16},{28,20},{1,9},{5... | collective-permute-start | bytes 393224 | tf_op jit(solution)/shard_map/ppermute | solution.py:368
  108.6 13.3 %collective-permute-start.22 = (bf16[128,512]{1,0:T(8,128)(2,1)}, bf16[128,512]{1,0:T(8,128)(2,1)S(1)}, u32[]{:S(2)}, u32[]{:S(2)}) collective-permute-start(bf16[128,512]{1,0:T(8,128)(2,1)} %copy.178), channel_id=1, source_target_pairs={{0,8},{4,12},{8,0},{12,4},{16,24},{20,28},{24,16},{28,20},{1,9},{5... | collective-permute-start | bytes 393224 | tf_op jit(solution)/shard_map/ppermute | solution.py:368
  123.0 38.9 %collective-permute-start.26 = (bf16[2,1024,128]{2,1,0:T(8,128)(2,1)S(1)}, bf16[2,1024,128]{2,1,0:T(8,128)(2,1)S(1)}, u32[]{:S(2)}, u32[]{:S(2)}) collective-permute-start(bf16[2,1024,128]{2,1,0:T(8,128)(2,1)S(1)} %pad_maximum_fusion.28), channel_id=1, source_target_pairs={{0,2},{1,3},{2,0},{3,1},{4,6},{5,7},{6,4},{7,5},{8,10},{9,11},{10,... | collective-permute-start | bytes 1572872 | tf_op jit(solution)/shard_map/ppermute | solution.py:378
  125.5 13.4 %collective-permute-start.25 = (bf16[256,512]{1,0:T(8,128)(2,1)S(1)}, bf16[256,512]{1,0:T(8,128)(2,1)S(1)}, u32[]{:S(2)}, u32[]{:S(2)}) collective-permute-start(bf16[256,512]{1,0:T(8,128)(2,1)S(1)} %pad_maximum_fusion.33), channel_id=1, source_target_pairs={{0,16},{4,20},{8,24},{12,28},{16,0},{20,4},{24,8},{28,12},{1,17},{... | collective-permute-start | bytes 786440 | tf_op jit(solution)/shard_map/ppermute | solution.py:368
  127.0 22.1 %collective-permute-start.24 = (bf16[1024,256]{1,0:T(8,128)(2,1)S(1)}, bf16[1024,256]{1,0:T(8,128)(2,1)S(1)}, u32[]{:S(2)}, u32[]{:S(2)}) collective-permute-start(bf16[1024,256]{1,0:T(8,128)(2,1)S(1)} %get-tuple-element.506), channel_id=1, source_target_pairs={{0,2},{1,3},{2,0},{3,1},{4,6},{5,7},{6,4},{7,5},{8,10},{9,11},{10,... | collective-permute-start | bytes 1572872 | tf_op jit(solution)/shard_map/ppermute | solution.py:378
  128.9 20.2 %collective-permute-start.23 = (bf16[256,1024]{1,0:T(8,128)(2,1)S(1)}, bf16[256,1024]{1,0:T(8,128)(2,1)S(1)}, u32[]{:S(2)}, u32[]{:S(2)}) collective-permute-start(bf16[256,1024]{1,0:T(8,128)(2,1)S(1)} %get-tuple-element.508), channel_id=1, source_target_pairs={{0,4},{4,0},{8,12},{12,8},{16,20},{20,16},{24,28},{28,24},{1,5},{5... | collective-permute-start | bytes 1572872 | tf_op jit(solution)/shard_map/ppermute | solution.py:374
  129.6 32.2 %collective-permute-start.29 = (bf16[1024,256]{1,0:T(8,128)(2,1)S(1)}, bf16[1024,256]{1,0:T(8,128)(2,1)S(1)}, u32[]{:S(2)}, u32[]{:S(2)}) collective-permute-start(bf16[1024,256]{1,0:T(8,128)(2,1)S(1)} %get-tuple-element.505), channel_id=1, source_target_pairs={{0,2},{1,3},{2,0},{3,1},{4,6},{5,7},{6,4},{7,5},{8,10},{9,11},{10,... | collective-permute-start | bytes 1572872 | tf_op jit(solution)/shard_map/ppermute | solution.py:378
  138.9 23.0 %collective-permute-start.28 = (bf16[256,1024]{1,0:T(8,128)(2,1)S(1)}, bf16[256,1024]{1,0:T(8,128)(2,1)S(1)}, u32[]{:S(2)}, u32[]{:S(2)}) collective-permute-start(bf16[256,1024]{1,0:T(8,128)(2,1)S(1)} %get-tuple-element.507), channel_id=1, source_target_pairs={{0,4},{4,0},{8,12},{12,8},{16,20},{20,16},{24,28},{28,24},{1,5},{5... | collective-permute-start | bytes 1572872 | tf_op jit(solution)/shard_map/ppermute | solution.py:374
  149.1 12.7 %collective-permute-start.27 = (bf16[256,512]{1,0:T(8,128)(2,1)S(1)}, bf16[256,512]{1,0:T(8,128)(2,1)S(1)}, u32[]{:S(2)}, u32[]{:S(2)}) collective-permute-start(bf16[256,512]{1,0:T(8,128)(2,1)S(1)} %pad_maximum_fusion.34), channel_id=1, source_target_pairs={{0,16},{4,20},{8,24},{12,28},{16,0},{20,4},{24,8},{28,12},{1,17},{... | collective-permute-start | bytes 786440 | tf_op jit(solution)/shard_map/ppermute | solution.py:368
  165.0 34.8 %collective-permute-start.31 = (bf16[1024,1024]{1,0:T(8,128)(2,1)}, bf16[1024,1024]{1,0:T(8,128)(2,1)}, u32[]{:S(2)}, u32[]{:S(2)}) collective-permute-start(bf16[1024,1024]{1,0:T(8,128)(2,1)} %pad_maximum_fusion.1.right_ref.refs_7_), channel_id=1, source_target_pairs={{0,1},{1,0},{2,3},{3,2},{4,5},{5,4},{6,7},{7,6},{8,9},{9,8},{10,11... | collective-permute-start | bytes 6291464 | tf_op jit(solution)/shard_map/ppermute | solution.py:378
  167.8 32.0 %collective-permute-start.30 = (bf16[1024,1024]{1,0:T(8,128)(2,1)}, bf16[1024,1024]{1,0:T(8,128)(2,1)}, u32[]{:S(2)}, u32[]{:S(2)}) collective-permute-start(bf16[1024,1024]{1,0:T(8,128)(2,1)} %pad_maximum_fusion.right_ref.refs_6_), channel_id=1, source_target_pairs={{0,1},{1,0},{2,3},{3,2},{4,5},{5,4},{6,7},{7,6},{8,9},{9,8},{10,11... | collective-permute-start | bytes 6291464 | tf_op jit(solution)/shard_map/ppermute | solution.py:378
  172.3 27.5 %collective-permute-start.34 = (bf16[2,1024,256]{2,1,0:T(8,128)(2,1)S(1)}, bf16[2,1024,256]{2,1,0:T(8,128)(2,1)S(1)}, u32[]{:S(2)}, u32[]{:S(2)}) collective-permute-start(bf16[2,1024,256]{2,1,0:T(8,128)(2,1)S(1)} %pad_maximum_fusion.8), channel_id=1, source_target_pairs={{0,1},{1,0},{2,3},{3,2},{4,5},{5,4},{6,7},{7,6},{8,9},{9,8},{10,11... | collective-permute-start | bytes 3145736 | tf_op jit(solution)/shard_map/ppermute | solution.py:378
  176.1 23.7 %collective-permute-start.33 = (bf16[512,512]{1,0:T(8,128)(2,1)S(1)}, bf16[512,512]{1,0:T(8,128)(2,1)S(1)}, u32[]{:S(2)}, u32[]{:S(2)}) collective-permute-start(bf16[512,512]{1,0:T(8,128)(2,1)S(1)} %pad_maximum_fusion.29), channel_id=1, source_target_pairs={{0,4},{4,0},{8,12},{12,8},{16,20},{20,16},{24,28},{28,24},{1,5},{5... | collective-permute-start | bytes 1572872 | tf_op jit(solution)/shard_map/ppermute | solution.py:374
  177.7 22.1 %collective-permute-start.32 = (bf16[512,512]{1,0:T(8,128)(2,1)S(1)}, bf16[512,512]{1,0:T(8,128)(2,1)S(1)}, u32[]{:S(2)}, u32[]{:S(2)}) collective-permute-start(bf16[512,512]{1,0:T(8,128)(2,1)S(1)} %constant_dynamic-update-slice_fusion), channel_id=1, source_target_pairs={{0,2},{1,3},{2,0},{3,1},{4,6},{5,7},{6,4},{7,5},{8,10},{9,11},{10,... | collective-permute-start | bytes 1572872 | tf_op jit(solution)/shard_map/ppermute | solution.py:378
  200.8 29.1 %collective-permute-start.36 = (bf16[1024,512]{1,0:T(8,128)(2,1)}, bf16[1024,512]{1,0:T(8,128)(2,1)}, u32[]{:S(2)}, u32[]{:S(2)}) collective-permute-start(bf16[1024,512]{1,0:T(8,128)(2,1)} %constant_dynamic-update-slice_fusion.3), channel_id=1, source_target_pairs={{0,2},{1,3},{2,0},{3,1},{4,6},{5,7},{6,4},{7,5},{8,10},{9,11},{10,... | collective-permute-start | bytes 3145736 | tf_op jit(solution)/shard_map/ppermute | solution.py:378
  203.5 26.4 %collective-permute-start.35 = (bf16[512,1024]{1,0:T(8,128)(2,1)}, bf16[512,1024]{1,0:T(8,128)(2,1)}, u32[]{:S(2)}, u32[]{:S(2)}) collective-permute-start(bf16[512,1024]{1,0:T(8,128)(2,1)} %pad_maximum_fusion.9), channel_id=1, source_target_pairs={{0,4},{4,0},{8,12},{12,8},{16,20},{20,16},{24,28},{28,24},{1,5},{5... | collective-permute-start | bytes 3145736 | tf_op jit(solution)/shard_map/ppermute | solution.py:374
  234.7 23.7 %collective-permute-start.38 = (bf16[1024,1024]{1,0:T(8,128)(2,1)}, bf16[1024,1024]{1,0:T(8,128)(2,1)}, u32[]{:S(2)}, u32[]{:S(2)}) collective-permute-start(bf16[1024,1024]{1,0:T(8,128)(2,1)} %pad_maximum_fusion.3.refs_7_.right_ref), channel_id=1, source_target_pairs={{0,1},{1,0},{2,3},{3,2},{4,5},{5,4},{6,7},{7,6},{8,9},{9,8},{10,11... | collective-permute-start | bytes 6291464 | tf_op jit(solution)/shard_map/ppermute | solution.py:378
  237.6 20.7 %collective-permute-start.37 = (bf16[1024,1024]{1,0:T(8,128)(2,1)}, bf16[1024,1024]{1,0:T(8,128)(2,1)}, u32[]{:S(2)}, u32[]{:S(2)}) collective-permute-start(bf16[1024,1024]{1,0:T(8,128)(2,1)} %pad_maximum_fusion.2.refs_6_.right_ref), channel_id=1, source_target_pairs={{0,1},{1,0},{2,3},{3,2},{4,5},{5,4},{6,7},{7,6},{8,9},{9,8},{10,11... | collective-permute-start | bytes 6291464 | tf_op jit(solution)/shard_map/ppermute | solution.py:378
  240.0 34.0 %collective-permute-start.39 = (bf16[2,256,1024]{2,1,0:T(8,128)(2,1)}, bf16[2,256,1024]{2,1,0:T(8,128)(2,1)}, u32[]{:S(2)}, u32[]{:S(2)}) collective-permute-start(bf16[2,256,1024]{2,1,0:T(8,128)(2,1)} %pad_maximum_fusion.10), channel_id=1, source_target_pairs={{0,2},{1,3},{2,0},{3,1},{4,6},{5,7},{6,4},{7,5},{8,10},{9,11},{10,... | collective-permute-start | bytes 3145736 | tf_op jit(solution)/shard_map/ppermute | solution.py:378
  288.7 18.2 %collective-permute-start.42 = (bf16[1024,1024]{1,0:T(8,128)(2,1)}, bf16[1024,1024]{1,0:T(8,128)(2,1)}, u32[]{:S(2)}, u32[]{:S(2)}) collective-permute-start(bf16[1024,1024]{1,0:T(8,128)(2,1)} %convolution_convert_fusion.2), channel_id=1, source_target_pairs={{0,1},{1,0},{2,3},{3,2},{4,5},{5,4},{6,7},{7,6},{8,9},{9,8},{10,11... | collective-permute-start | bytes 6291464 | tf_op jit(solution)/shard_map/ppermute | solution.py:378
  288.8 18.1 %collective-permute-start.41 = (bf16[1024,1024]{1,0:T(8,128)(2,1)}, bf16[1024,1024]{1,0:T(8,128)(2,1)}, u32[]{:S(2)}, u32[]{:S(2)}) collective-permute-start(bf16[1024,1024]{1,0:T(8,128)(2,1)} %convolution_convert_fusion.3), channel_id=1, source_target_pairs={{0,1},{1,0},{2,3},{3,2},{4,5},{5,4},{6,7},{7,6},{8,9},{9,8},{10,11... | collective-permute-start | bytes 6291464 | tf_op jit(solution)/shard_map/ppermute | solution.py:378
  310.6 31.6 %collective-permute-start.44 = (bf16[1024,256]{1,0:T(8,128)(2,1)}, bf16[1024,256]{1,0:T(8,128)(2,1)}, u32[]{:S(2)}, u32[]{:S(2)}) collective-permute-start(bf16[1024,256]{1,0:T(8,128)(2,1)} %get-tuple-element.473), channel_id=1, source_target_pairs={{0,2},{1,3},{2,0},{3,1},{4,6},{5,7},{6,4},{7,5},{8,10},{9,11},{10,... | collective-permute-start | bytes 1572872 | tf_op jit(solution)/shard_map/ppermute | solution.py:378
  316.4 25.7 %collective-permute-start.43 = (bf16[256,1024]{1,0:T(8,128)(2,1)}, bf16[256,1024]{1,0:T(8,128)(2,1)}, u32[]{:S(2)}, u32[]{:S(2)}) collective-permute-start(bf16[256,1024]{1,0:T(8,128)(2,1)} %get-tuple-element.475), channel_id=1, source_target_pairs={{0,4},{4,0},{8,12},{12,8},{16,20},{20,16},{24,28},{28,24},{1,5},{5... | collective-permute-start | bytes 1572872 | tf_op jit(solution)/shard_map/ppermute | solution.py:374
  335.5 22.0 %collective-permute-start.46 = (bf16[1024,256]{1,0:T(8,128)(2,1)}, bf16[1024,256]{1,0:T(8,128)(2,1)}, u32[]{:S(2)}, u32[]{:S(2)}) collective-permute-start(bf16[1024,256]{1,0:T(8,128)(2,1)} %get-tuple-element.472), channel_id=1, source_target_pairs={{0,2},{1,3},{2,0},{3,1},{4,6},{5,7},{6,4},{7,5},{8,10},{9,11},{10,... | collective-permute-start | bytes 1572872 | tf_op jit(solution)/shard_map/ppermute | solution.py:378
  336.1 21.5 %collective-permute-start.45 = (bf16[256,1024]{1,0:T(8,128)(2,1)}, bf16[256,1024]{1,0:T(8,128)(2,1)}, u32[]{:S(2)}, u32[]{:S(2)}) collective-permute-start(bf16[256,1024]{1,0:T(8,128)(2,1)} %get-tuple-element.474), channel_id=1, source_target_pairs={{0,4},{4,0},{8,12},{12,8},{16,20},{20,16},{24,28},{28,24},{1,5},{5... | collective-permute-start | bytes 1572872 | tf_op jit(solution)/shard_map/ppermute | solution.py:374
  338.1 53.7 %collective-permute-start.51 = (bf16[2,256,1024]{2,1,0:T(8,128)(2,1)}, bf16[2,256,1024]{2,1,0:T(8,128)(2,1)}, u32[]{:S(2)}, u32[]{:S(2)}) collective-permute-start(bf16[2,256,1024]{2,1,0:T(8,128)(2,1)} %bitcast.80), channel_id=1, source_target_pairs={{0,2},{1,3},{2,0},{3,1},{4,6},{5,7},{6,4},{7,5},{8,10},{9,11},{10,... | collective-permute-start | bytes 3145736 | tf_op jit(solution)/shard_map/ppermute | solution.py:378
  357.5 34.3 %collective-permute-start.48 = (bf16[1024,1024]{1,0:T(8,128)(2,1)}, bf16[1024,1024]{1,0:T(8,128)(2,1)}, u32[]{:S(2)}, u32[]{:S(2)}) collective-permute-start(bf16[1024,1024]{1,0:T(8,128)(2,1)} %convolution_convert_fusion), channel_id=1, source_target_pairs={{0,1},{1,0},{2,3},{3,2},{4,5},{5,4},{6,7},{7,6},{8,9},{9,8},{10,11... | collective-permute-start | bytes 6291464 | tf_op jit(solution)/shard_map/ppermute | solution.py:378
  357.6 34.3 %collective-permute-start.47 = (bf16[1024,1024]{1,0:T(8,128)(2,1)}, bf16[1024,1024]{1,0:T(8,128)(2,1)}, u32[]{:S(2)}, u32[]{:S(2)}) collective-permute-start(bf16[1024,1024]{1,0:T(8,128)(2,1)} %convolution_convert_fusion.1), channel_id=1, source_target_pairs={{0,1},{1,0},{2,3},{3,2},{4,5},{5,4},{6,7},{7,6},{8,9},{9,8},{10,11... | collective-permute-start | bytes 6291464 | tf_op jit(solution)/shard_map/ppermute | solution.py:378
  360.6 31.2 %collective-permute-start.50 = (bf16[512,512]{1,0:T(8,128)(2,1)}, bf16[512,512]{1,0:T(8,128)(2,1)}, u32[]{:S(2)}, u32[]{:S(2)}) collective-permute-start(bf16[512,512]{1,0:T(8,128)(2,1)} %slice.516), channel_id=1, source_target_pairs={{0,4},{4,0},{8,12},{12,8},{16,20},{20,16},{24,28},{28,24},{1,5},{5... | collective-permute-start | bytes 1572872 | tf_op jit(solution)/shard_map/ppermute | solution.py:374
  364.4 27.4 %collective-permute-start.49 = (bf16[512,512]{1,0:T(8,128)(2,1)}, bf16[512,512]{1,0:T(8,128)(2,1)}, u32[]{:S(2)}, u32[]{:S(2)}) collective-permute-start(bf16[512,512]{1,0:T(8,128)(2,1)} %slice.514), channel_id=1, source_target_pairs={{0,2},{1,3},{2,0},{3,1},{4,6},{5,7},{6,4},{7,5},{8,10},{9,11},{10,... | collective-permute-start | bytes 1572872 | tf_op jit(solution)/shard_map/ppermute | solution.py:378
  399.8 29.3 %collective-permute-start.56 = (bf16[2,256,1024]{2,1,0:T(8,128)(2,1)S(1)}, bf16[2,256,1024]{2,1,0:T(8,128)(2,1)S(1)}, u32[]{:S(2)}, u32[]{:S(2)}) collective-permute-start(bf16[2,256,1024]{2,1,0:T(8,128)(2,1)S(1)} %pad_maximum_fusion.13), channel_id=1, source_target_pairs={{0,1},{1,0},{2,3},{3,2},{4,5},{5,4},{6,7},{7,6},{8,9},{9,8},{10,11... | collective-permute-start | bytes 3145736 | tf_op jit(solution)/shard_map/ppermute | solution.py:378
  402.5 26.6 %collective-permute-start.55 = (bf16[256,1024]{1,0:T(8,128)(2,1)S(1)}, bf16[256,1024]{1,0:T(8,128)(2,1)S(1)}, u32[]{:S(2)}, u32[]{:S(2)}) collective-permute-start(bf16[256,1024]{1,0:T(8,128)(2,1)S(1)} %fusion.7), channel_id=1, source_target_pairs={{0,16},{4,20},{8,24},{12,28},{16,0},{20,4},{24,8},{28,12},{1,17},{... | collective-permute-start | bytes 1572872 | tf_op jit(solution)/shard_map/ppermute | solution.py:368
  403.8 25.3 %collective-permute-start.54 = (bf16[2,1024,256]{2,1,0:T(8,128)(2,1)S(1)}, bf16[2,1024,256]{2,1,0:T(8,128)(2,1)S(1)}, u32[]{:S(2)}, u32[]{:S(2)}) collective-permute-start(bf16[2,1024,256]{2,1,0:T(8,128)(2,1)S(1)} %pad_maximum_fusion.12), channel_id=1, source_target_pairs={{0,1},{1,0},{2,3},{3,2},{4,5},{5,4},{6,7},{7,6},{8,9},{9,8},{10,11... | collective-permute-start | bytes 3145736 | tf_op jit(solution)/shard_map/ppermute | solution.py:378
  406.6 25.6 %collective-permute-start.53 = (bf16[1024,512]{1,0:T(8,128)(2,1)S(1)}, bf16[1024,512]{1,0:T(8,128)(2,1)S(1)}, u32[]{:S(2)}, u32[]{:S(2)}) collective-permute-start(bf16[1024,512]{1,0:T(8,128)(2,1)S(1)} %slice.518), channel_id=1, source_target_pairs={{0,2},{1,3},{2,0},{3,1},{4,6},{5,7},{6,4},{7,5},{8,10},{9,11},{10,... | collective-permute-start | bytes 3145736 | tf_op jit(solution)/shard_map/ppermute | solution.py:378
  410.1 25.1 %collective-permute-start.52 = (bf16[512,1024]{1,0:T(8,128)(2,1)S(1)}, bf16[512,1024]{1,0:T(8,128)(2,1)S(1)}, u32[]{:S(2)}, u32[]{:S(2)}) collective-permute-start(bf16[512,1024]{1,0:T(8,128)(2,1)S(1)} %slice.517), channel_id=1, source_target_pairs={{0,4},{4,0},{8,12},{12,8},{16,20},{20,16},{24,28},{28,24},{1,5},{5... | collective-permute-start | bytes 3145736 | tf_op jit(solution)/shard_map/ppermute | solution.py:374
  435.4 25.9 %collective-permute-start.61 = (bf16[128,1024]{1,0:T(8,128)(2,1)S(1)}, bf16[128,1024]{1,0:T(8,128)(2,1)S(1)}, u32[]{:S(2)}, u32[]{:S(2)}) collective-permute-start(bf16[128,1024]{1,0:T(8,128)(2,1)S(1)} %slice.528), channel_id=1, source_target_pairs={{0,8},{4,12},{8,0},{12,4},{16,24},{20,28},{24,16},{28,20},{1,9},{5... | collective-permute-start | bytes 786440 | tf_op jit(solution)/shard_map/ppermute | solution.py:368
  438.2 27.3 %collective-permute-start.57 = (bf16[1024,768]{1,0:T(8,128)(2,1)S(1)}, bf16[1024,768]{1,0:T(8,128)(2,1)S(1)}, u32[]{:S(2)}, u32[]{:S(2)}) collective-permute-start(bf16[1024,768]{1,0:T(8,128)(2,1)S(1)} %convolution_convert_fusion.7), channel_id=1, source_target_pairs={{0,1},{1,0},{2,3},{3,2},{4,5},{5,4},{6,7},{7,6},{8,9},{9,8},{10,11... | collective-permute-start | bytes 4718600 | tf_op jit(solution)/shard_map/ppermute | solution.py:378
  438.6 22.7 %collective-permute-start.60 = (bf16[512,512]{1,0:T(8,128)(2,1)S(1)}, bf16[512,512]{1,0:T(8,128)(2,1)S(1)}, u32[]{:S(2)}, u32[]{:S(2)}) collective-permute-start(bf16[512,512]{1,0:T(8,128)(2,1)S(1)} %slice.527), channel_id=1, source_target_pairs={{0,4},{4,0},{8,12},{12,8},{16,20},{20,16},{24,28},{28,24},{1,5},{5... | collective-permute-start | bytes 1572872 | tf_op jit(solution)/shard_map/ppermute | solution.py:374
  440.1 21.2 %collective-permute-start.59 = (bf16[512,512]{1,0:T(8,128)(2,1)S(1)}, bf16[512,512]{1,0:T(8,128)(2,1)S(1)}, u32[]{:S(2)}, u32[]{:S(2)}) collective-permute-start(bf16[512,512]{1,0:T(8,128)(2,1)S(1)} %slice.525), channel_id=1, source_target_pairs={{0,2},{1,3},{2,0},{3,1},{4,6},{5,7},{6,4},{7,5},{8,10},{9,11},{10,... | collective-permute-start | bytes 1572872 | tf_op jit(solution)/shard_map/ppermute | solution.py:378
  441.0 24.5 %collective-permute-start.58 = (bf16[2,1024,128]{2,1,0:T(8,128)(2,1)S(1)}, bf16[2,1024,128]{2,1,0:T(8,128)(2,1)S(1)}, u32[]{:S(2)}, u32[]{:S(2)}) collective-permute-start(bf16[2,1024,128]{2,1,0:T(8,128)(2,1)S(1)} %slice.523), channel_id=1, source_target_pairs={{0,2},{1,3},{2,0},{3,1},{4,6},{5,7},{6,4},{7,5},{8,10},{9,11},{10,... | collective-permute-start | bytes 1572872 | tf_op jit(solution)/shard_map/ppermute | solution.py:378
  466.0 22.3 %collective-permute-start.63 = (bf16[1024,384]{1,0:T(8,128)(2,1)S(1)}, bf16[1024,384]{1,0:T(8,128)(2,1)S(1)}, u32[]{:S(2)}, u32[]{:S(2)}) collective-permute-start(bf16[1024,384]{1,0:T(8,128)(2,1)S(1)} %slice.531), channel_id=1, source_target_pairs={{0,2},{1,3},{2,0},{3,1},{4,6},{5,7},{6,4},{7,5},{8,10},{9,11},{10,... | collective-permute-start | bytes 2359304 | tf_op jit(solution)/shard_map/ppermute | solution.py:378
  467.8 20.5 %collective-permute-start.62 = (bf16[2,512,128]{2,1,0:T(8,128)(2,1)S(1)}, bf16[2,512,128]{2,1,0:T(8,128)(2,1)S(1)}, u32[]{:S(2)}, u32[]{:S(2)}) collective-permute-start(bf16[2,512,128]{2,1,0:T(8,128)(2,1)S(1)} %slice.530), channel_id=1, source_target_pairs={{0,4},{4,0},{8,12},{12,8},{16,20},{20,16},{24,28},{28,24},{1,5},{5... | collective-permute-start | bytes 786440 | tf_op jit(solution)/shard_map/ppermute | solution.py:374
  470.1 40.7 %collective-permute-start.66 = (bf16[256,1024]{1,0:T(8,128)(2,1)}, bf16[256,1024]{1,0:T(8,128)(2,1)}, u32[]{:S(2)}, u32[]{:S(2)}) collective-permute-start(bf16[256,1024]{1,0:T(8,128)(2,1)} %fusion.6), channel_id=1, source_target_pairs={{0,16},{4,20},{8,24},{12,28},{16,0},{20,4},{24,8},{28,12},{1,17},{... | collective-permute-start | bytes 1572872 | tf_op jit(solution)/shard_map/ppermute | solution.py:368
  488.3 22.5 %collective-permute-start.65 = (bf16[1024,768]{1,0:T(8,128)(2,1)}, bf16[1024,768]{1,0:T(8,128)(2,1)}, u32[]{:S(2)}, u32[]{:S(2)}) collective-permute-start(bf16[1024,768]{1,0:T(8,128)(2,1)} %convolution_convert_fusion.6), channel_id=1, source_target_pairs={{0,1},{1,0},{2,3},{3,2},{4,5},{5,4},{6,7},{7,6},{8,9},{9,8},{10,11... | collective-permute-start | bytes 4718600 | tf_op jit(solution)/shard_map/ppermute | solution.py:378
  492.7 18.1 %collective-permute-start.64 = (bf16[512,384]{1,0:T(8,128)(2,1)S(1)}, bf16[512,384]{1,0:T(8,128)(2,1)S(1)}, u32[]{:S(2)}, u32[]{:S(2)}) collective-permute-start(bf16[512,384]{1,0:T(8,128)(2,1)S(1)} %slice.533), channel_id=1, source_target_pairs={{0,4},{4,0},{8,12},{12,8},{16,20},{20,16},{24,28},{28,24},{1,5},{5... | collective-permute-start | bytes 1179656 | tf_op jit(solution)/shard_map/ppermute | solution.py:374
  512.1 16.5 %collective-permute-start.74 = (bf16[128,1024]{1,0:T(8,128)(2,1)S(1)}, bf16[128,1024]{1,0:T(8,128)(2,1)S(1)}, u32[]{:S(2)}, u32[]{:S(2)}) collective-permute-start(bf16[128,1024]{1,0:T(8,128)(2,1)S(1)} %slice.555), channel_id=1, source_target_pairs={{0,8},{4,12},{8,0},{12,4},{16,24},{20,28},{24,16},{28,20},{1,9},{5... | collective-permute-start | bytes 786440 | tf_op jit(solution)/shard_map/ppermute | solution.py:368
  516.2 18.8 %collective-permute-start.67 = (bf16[512,768]{1,0:T(8,128)(2,1)}, bf16[512,768]{1,0:T(8,128)(2,1)}, u32[]{:S(2)}, u32[]{:S(2)}) collective-permute-start(bf16[512,768]{1,0:T(8,128)(2,1)} %slice.538), channel_id=1, source_target_pairs={{0,4},{4,0},{8,12},{12,8},{16,20},{20,16},{24,28},{28,24},{1,5},{5... | collective-permute-start | bytes 2359304 | tf_op jit(solution)/shard_map/ppermute | solution.py:374
  526.6 30.5 %collective-permute-start.69 = (bf16[2,256,1024]{2,1,0:T(8,128)(2,1)}, bf16[2,256,1024]{2,1,0:T(8,128)(2,1)}, u32[]{:S(2)}, u32[]{:S(2)}) collective-permute-start(bf16[2,256,1024]{2,1,0:T(8,128)(2,1)} %bitcast.91), channel_id=1, source_target_pairs={{0,2},{1,3},{2,0},{3,1},{4,6},{5,7},{6,4},{7,5},{8,10},{9,11},{10,... | collective-permute-start | bytes 3145736 | tf_op jit(solution)/shard_map/ppermute | solution.py:378
  542.7 16.4 %collective-permute-start.68 = (bf16[512,384]{1,0:T(8,128)(2,1)}, bf16[512,384]{1,0:T(8,128)(2,1)}, u32[]{:S(2)}, u32[]{:S(2)}) collective-permute-start(bf16[512,384]{1,0:T(8,128)(2,1)} %slice.540), channel_id=1, source_target_pairs={{0,2},{1,3},{2,0},{3,1},{4,6},{5,7},{6,4},{7,5},{8,10},{9,11},{10,... | collective-permute-start | bytes 1179656 | tf_op jit(solution)/shard_map/ppermute | solution.py:378
  562.9 17.5 %collective-permute-start.71 = (bf16[128,1024]{1,0:T(8,128)(2,1)}, bf16[128,1024]{1,0:T(8,128)(2,1)S(1)}, u32[]{:S(2)}, u32[]{:S(2)}) collective-permute-start(bf16[128,1024]{1,0:T(8,128)(2,1)} %get-tuple-element.488), channel_id=1, source_target_pairs={{0,8},{4,12},{8,0},{12,4},{16,24},{20,28},{24,16},{28,20},{1,9},{5... | collective-permute-start | bytes 786440 | tf_op jit(solution)/shard_map/ppermute | solution.py:368
  563.5 16.9 %collective-permute-start.72 = (bf16[128,1024]{1,0:T(8,128)(2,1)}, bf16[128,1024]{1,0:T(8,128)(2,1)S(1)}, u32[]{:S(2)}, u32[]{:S(2)}) collective-permute-start(bf16[128,1024]{1,0:T(8,128)(2,1)} %get-tuple-element.487), channel_id=1, source_target_pairs={{0,16},{4,20},{8,24},{12,28},{16,0},{20,4},{24,8},{28,12},{1,17},{... | collective-permute-start | bytes 786440 | tf_op jit(solution)/shard_map/ppermute | solution.py:368
  579.0 17.1 %collective-permute-start.70 = (bf16[2,256,1024]{2,1,0:T(8,128)(2,1)}, bf16[2,256,1024]{2,1,0:T(8,128)(2,1)}, u32[]{:S(2)}, u32[]{:S(2)}) collective-permute-start(bf16[2,256,1024]{2,1,0:T(8,128)(2,1)} %pad_maximum_fusion.14), channel_id=1, source_target_pairs={{0,1},{1,0},{2,3},{3,2},{4,5},{5,4},{6,7},{7,6},{8,9},{9,8},{10,11... | collective-permute-start | bytes 3145736 | tf_op jit(solution)/shard_map/ppermute | solution.py:378
  (180 other events, 1138.5 us)
